TPU v7x, 32 devices: a whole 2x2x4 slice. The times are simulated.
32 devices in a mesh: ctx: 8 (over z, x), cls: 4 (over y, core).
Axes of the slice: x: 2, y: 2, z: 4, core: 2. Of those that a mesh axis runs over, the one named last changes fastest.
Arguments:
- tokens: bfloat16 [24576, 8192], P(('ctx', 'cls')), may hold values from -80 to 80
- doc_length: int32 [1], replicated, may hold values from 12288 to 24576
- queries: bfloat16 [64, 8192], P('cls', 'ctx'), may hold values from -0.046875 to 0.046875
- norm_gain: float32 [8192], P('ctx'), may hold values from 0.1 to 1.9
- head_weight: bfloat16 [8192, 4096], P('ctx', 'cls'), may hold values from -0.0625 to 0.0625
- head_bias: float32 [4096], P('cls'), may hold values from -20 to 20
- labels: int32 [4096], P('cls'), may hold values 0 or 1
Outputs:
- mean_loss: float32 [], replicated
- query_grad: float32 [64, 8192], P('cls', 'ctx')
- head_grad: float32 [8192, 4096], P('ctx', 'cls')
- bias_grad: float32 [4096], P('cls')
All inputs are finite; a program needn't handle non-finite values. No bound on the sum of `labels` on one device may be relied on, other than what follows from the above.
Results may differ from a plain program's by a relative error of at most 0.017.
Values may be sent and summed in bfloat16 or wider, within the bound.
No kernel may reach another device: no remote copies, remote signals or barrier semaphores. Data moves between devices by JAX's collectives and lax.ppermute only.
A program may use at most 64 MiB of HBM per device.

v0:
```python
import jax
import jax.numpy as jnp
from jax import lax
from jax.sharding import PartitionSpec as P


def shards(tokens, doc_length, queries, norm_gain, head_weight, head_bias, labels):
    context_count = lax.axis_size("ctx")
    class_count = lax.axis_size("cls")
    context_index = lax.axis_index("ctx")
    class_index = lax.axis_index("cls")
    token_count = tokens.shape[0]
    query_share = queries.shape[0]
    width_share = queries.shape[1]
    full_width = width_share * context_count

    def project_add(block_piece):
        return lax.dot_general(
            block_piece, tokens, (((1,), (1,)), ((), ())), preferred_element_type=jnp.float32
        )

    query_block = lax.all_gather(queries, "cls", axis=0, tiled=True)
    scores = project_add(lax.all_gather(query_block, "ctx", axis=1, tiled=True))
    offset = (context_index * class_count + class_index) * token_count
    position = offset + jnp.arange(token_count, dtype=jnp.int32)
    valid_mask = (position < doc_length[0])[None, :]
    local_peak = jnp.max(jnp.where(valid_mask, scores, -1e30), axis=1)
    peak = lax.pmax(local_peak, ("ctx", "cls"))
    weights = jnp.exp(jnp.where(valid_mask, scores - peak[:, None], -1e30))
    pooled_part = jnp.dot(weights.astype(jnp.bfloat16), tokens, preferred_element_type=jnp.float32)
    whole_sum = lax.psum(pooled_part, ("ctx", "cls"))
    pooled = lax.dynamic_slice(
        whole_sum,
        (class_index * query_share, context_index * width_share),
        (query_share, width_share),
    )
    scaled_b = (pooled * norm_gain[None, :]).astype(jnp.bfloat16)
    head_blocks = head_weight.reshape(width_share, query_share, -1)
    square_part = jnp.sum(pooled * pooled, axis=1)
    logit_part = jnp.einsum("hd,dha->ha", scaled_b, head_blocks, preferred_element_type=jnp.float32)
    squares, logit_raw = lax.psum((square_part, logit_part), "ctx")
    inverse_rms = lax.rsqrt(squares / full_width + 1e-05)
    logits = inverse_rms[:, None] * logit_raw + head_bias.reshape(query_share, -1)
    target = labels.reshape(query_share, -1).astype(jnp.float32)
    loss_part = jnp.sum(jax.nn.softplus(logits) - target * logits)
    mean_loss = lax.psum(loss_part, "cls") / (labels.shape[0] * class_count)
    logit_grad = jax.nn.sigmoid(logits) - target
    normed = pooled * inverse_rms[:, None] * norm_gain[None, :]
    head_grad = jnp.einsum("hd,ha->dha", normed, logit_grad).reshape(width_share, -1)
    normed_grad = (
        jnp.einsum("dha,ha->hd", head_blocks.astype(jnp.float32), logit_grad) * norm_gain[None, :]
    )
    unit_pooled = pooled * inverse_rms[:, None]
    inner_part = jnp.sum(unit_pooled * normed_grad, axis=1)
    inner_mean = lax.psum(inner_part, "ctx") / full_width
    pooled_grad = (inverse_rms[:, None] * (normed_grad - unit_pooled * inner_mean[:, None])).astype(
        jnp.bfloat16
    )
    grad_block = lax.all_gather(pooled_grad, "cls", axis=0, tiled=True)
    projected = project_add(lax.all_gather(grad_block, "ctx", axis=1, tiled=True))
    score_grad = (weights * projected).astype(jnp.bfloat16)
    query_part = jnp.dot(score_grad, tokens, preferred_element_type=jnp.float32)
    column_grad = lax.psum_scatter(query_part, "ctx", scatter_dimension=1, tiled=True)
    query_grad = lax.psum_scatter(column_grad, "cls", scatter_dimension=0, tiled=True)
    return (mean_loss, query_grad, head_grad, logit_grad.reshape(-1))


def solution(mesh):
    return jax.shard_map(
        shards,
        mesh=mesh,
        in_specs=(
            P(("ctx", "cls"), None),
            P(),
            P("cls", "ctx"),
            P("ctx"),
            P("ctx", "cls"),
            P("cls"),
            P("cls"),
        ),
        out_specs=(P(), P("cls", "ctx"), P("ctx", "cls"), P("cls")),
        check_vma=False,
    )
```

profile of v0, /device:TPU:0, one launch (start us, length us, event | category | flops | bytes accessed | tf_op | source)
XLA Modules:
  0.0 447.5 jit_solution(8108586227153220570)
XLA Ops:
  7.2 0.0 all-gather.3.cloned.1.call-start
  7.2 8.4 %all_gather.12 = bf16[64,1024]{1,0:T(8,128)(2,1)} all-gather(bf16[16,1024]{1,0:T(8,128)(2,1)} %param.9), channel_id=1, replica_groups=mesh['ctx'=8,'cls'=4] {'cls'}, dimensions={0}, use_global_device_ids=true | all-gather | bytes 163840 | tf_op jit(solution)/shard_map/all_gather | solution.py:22
  15.6 0.0 all-gather.3.cloned.1.call-update
  15.6 0.0 all-reduce.3.cloned.1.call-start
  16.3 40.1 %all-gather.3.cloned.1.call-done = bf16[64,8192]{1,0:T(8,128)(2,1)} async-done(((bf16[64,1024]{1,0:T(8,128)(2,1)}), bf16[64,8192]{1,0:T(8,128)(2,1)}) %all-gather.3.cloned.1.call-update) | async-done | bytes 1048592 | tf_op jit(solution)/shard_map/all_gather | solution.py:23
  56.4 8.9 %select_reduce_fusion = (f32[64]{0:T(128)S(1)}, f32[64,768]{1,0:T(8,128)S(1)}) fusion(pred[768]{0:T(1024)(128)(4,1)S(1)} %add_compare_fusion, bf16[64,8192]{1,0:T(8,128)(2,1)} %all-gather.3.cloned.1.call-done, bf16[768,8192]{1,0:T(8,128)(2,1)} %param.7), kind=kOutput, calls=%fused_computation.5 | convolution fusion | flops 805404608 | bytes 13829120 | tf_op jit(solution)/shard_map/dot_general | solution.py:18
  65.3 38.3 %pmax.7 = f32[64]{0:T(128)S(1)} all-reduce(f32[64]{0:T(128)S(1)} %get-tuple-element.16), channel_id=1, replica_groups=mesh['ctx'=8,'cls'=4] {'ctx','cls'}, use_global_device_ids=true, to_apply=%region_1.2 | all-reduce | flops 64 | bytes 512 | tf_op jit(solution)/shard_map/pmax | solution.py:28
  103.6 0.0 copy-start.2
  103.6 0.0 copy-start.1
  103.6 8.3 %fusion.3 = f32[64,8192]{1,0:T(8,128)} fusion(bf16[768,8192]{1,0:T(8,128)(2,1)} %param.7, f32[64,768]{1,0:T(8,128)S(1)} %get-tuple-element.17, f32[64]{0:T(128)S(1)} %pmax.7, pred[768]{0:T(1024)(128)(4,1)S(1)} %add_compare_fusion), kind=kOutput, calls=%fused_computation.7 | convolution fusion | flops 805453824 | bytes 14877696 | tf_op jit(solution)/shard_map/dot_general | solution.py:30
  111.9 0.0 copy-start
  111.9 0.0 all-reduce.3.cloned.1.call-update
  111.9 0.0 all-gather.5.cloned.1.call-start
  112.0 0.0 copy-done.2
  112.0 0.1 convert_element_type.22
  112.1 0.0 copy-done.1
  112.1 0.1 reshape.32
  112.1 2.9 copy.12
  115.0 131.4 %all-reduce.3.cloned.1.call-done = f32[64,8192]{1,0:T(8,128)} async-done(((f32[64,8192]{1,0:T(8,128)}), f32[64,8192]{1,0:T(8,128)}) %all-reduce.3.cloned.1.call-update) | async-done | bytes 2097168 | tf_op jit(solution)/shard_map/psum | solution.py:31
  246.4 0.0 copy-done
  246.4 1.0 multiply_reduce_fusion.1
  247.4 0.6 fusion.11
  248.0 20.7 %all-reduce = (f32[16,64]{1,0:T(8,128)S(1)}, f32[16]{0:T(128)S(1)}) all-reduce(f32[16,64]{1,0:T(8,128)S(1)} %bitcast.32, f32[16]{0:T(128)S(1)} %get-tuple-element.12), channel_id=1, replica_groups=mesh['ctx'=8,'cls'=4] {'ctx'}, use_global_device_ids=true, to_apply=%region_5.6 | all-reduce | flops 1040 | bytes 8320 | tf_op jit(solution)/shard_map/psum | solution.py:41
  268.7 0.7 divide_subtract_fusion
  269.4 0.4 fusion.18
  269.8 1.0 multiply_multiply_fusion
  270.8 17.1 %psum.39 = f32[16]{0:T(128)S(1)} all-reduce(f32[16]{0:T(128)S(1)} %get-tuple-element.11), channel_id=1, replica_groups=mesh['ctx'=8,'cls'=4] {'ctx'}, use_global_device_ids=true, to_apply=%region_9.10 | all-reduce | flops 16 | bytes 128 | tf_op jit(solution)/shard_map/psum | solution.py:55
  288.0 0.9 multiply_convert_fusion
  288.9 5.9 %all_gather.14 = bf16[64,1024]{1,0:T(8,128)(2,1)} all-gather(bf16[16,1024]{1,0:T(8,128)(2,1)S(1)} %multiply_convert_fusion), channel_id=1, replica_groups=mesh['ctx'=8,'cls'=4] {'cls'}, dimensions={0}, use_global_device_ids=true | all-gather | bytes 163840 | tf_op jit(solution)/shard_map/all_gather | solution.py:59
  294.8 0.0 all-gather.5.cloned.1.call-update
  294.8 0.2 reduce-scatter.3.cloned.1.call-start
  295.0 38.0 %all-gather.5.cloned.1.call-done = bf16[64,8192]{1,0:T(8,128)(2,1)} async-done(((bf16[64,1024]{1,0:T(8,128)(2,1)}), bf16[64,8192]{1,0:T(8,128)(2,1)}) %all-gather.5.cloned.1.call-update) | async-done | bytes 1048592 | tf_op jit(solution)/shard_map/all_gather | solution.py:60
  333.0 17.6 %fusion.1 = f32[64,8192]{1,0:T(8,128)} fusion(bf16[768,8192]{1,0:T(8,128)(2,1)} %param.7, bf16[64,8192]{1,0:T(8,128)(2,1)} %all-gather.5.cloned.1.call-done, f32[64,768]{1,0:T(8,128)S(1)} %get-tuple-element.17, f32[64]{0:T(128)S(1)} %pmax.7, pred[768]{0:T(1024)(128)(4,1)S(1)} %add_compare_fusion), kind=kOutput, calls=%fused_computation.3 | convolution fusion | flops 1610809344 | bytes 15926272 | tf_op jit(solution)/shard_map/dot_general | solution.py:62
  350.6 0.0 reduce-scatter.3.cloned.1.call-update
  350.6 0.0 reduce-scatter.5.cloned.1.call-start
  350.7 67.1 %reduce-scatter.3.cloned.1.call-done = f32[64,1024]{1,0:T(8,128)} async-done(((f32[64,8192]{1,0:T(8,128)}), f32[64,1024]{1,0:T(8,128)}) %reduce-scatter.3.cloned.1.call-update) | async-done | bytes 262160 | tf_op jit(solution)/shard_map/reduce_scatter | solution.py:63
  417.8 0.0 reduce-scatter.5.cloned.1.call-update
  417.8 6.3 %psum.38 = f32[]{:T(128)} all-reduce(f32[]{:T(128)} %get-tuple-element.15), channel_id=1, replica_groups=mesh['ctx'=8,'cls'=4] {'cls'}, use_global_device_ids=true, to_apply=%region_7.8 | all-reduce | flops 1 | bytes 8 | tf_op jit(solution)/shard_map/psum | solution.py:46
  424.1 0.7 reshape.34
  424.8 2.3 broadcast_multiply_fusion
  427.1 5.4 %copy.13 = f32[1024,1024]{1,0:T(8,128)} copy(f32[1024,1024]{0,1:T(8,128)} %bitcast.28) | data formatting | bytes 8388608
  433.1 6.7 %reduce-scatter.5.cloned.1.call-done = f32[16,1024]{1,0:T(8,128)} async-done(((f32[64,1024]{1,0:T(8,128)}), f32[16,1024]{1,0:T(8,128)}) %reduce-scatter.5.cloned.1.call-update) | async-done | bytes 65552 | tf_op jit(solution)/shard_map/reduce_scatter | solution.py:64
  (4 shorter events, 0.0 us)
Async XLA Ops:
  7.2 49.2 %all-gather.3.cloned.1.call-start = ((), (), s32[]{:S(2)}) async-start(), calls=%async_computation.2 | async-start | bytes 1179648 | tf_op jit(solution)/shard_map/all_gather | solution.py:23
  15.6 230.8 %all-reduce.3.cloned.1.call-start = ((), (), s32[]{:S(2)}) async-start(), calls=%async_computation.3 | async-start | bytes 4194304 | tf_op jit(solution)/shard_map/psum | solution.py:31
  103.6 8.4 %copy-start.2 = (s32[1024]{0:T(1024)S(1)}, s32[1024]{0:T(1024)}, u32[]{:S(2)}) copy-start(s32[1024]{0:T(1024)} %param.13) | copy-start | bytes 12292
  103.6 8.5 %copy-start.1 = (f32[1024]{0:T(1024)S(1)}, f32[1024]{0:T(1024)}, u32[]{:S(2)}) copy-start(f32[1024]{0:T(1024)} %param.12) | copy-start | bytes 12292
  111.9 134.5 %copy-start = (f32[1024]{0:T(1024)S(1)}, f32[1024]{0:T(1024)}, u32[]{:S(2)}) copy-start(f32[1024]{0:T(1024)} %param.10) | copy-start | bytes 12292
  111.9 221.1 %all-gather.5.cloned.1.call-start = ((), (), s32[]{:S(2)}) async-start(), calls=%async_computation.4 | async-start | bytes 1179648 | tf_op jit(solution)/shard_map/all_gather | solution.py:60
  294.8 123.0 %reduce-scatter.3.cloned.1.call-start = ((), (), s32[]{:S(2)}) async-start(), calls=%async_computation.5 | async-start | bytes 2359296 | tf_op jit(solution)/shard_map/reduce_scatter | solution.py:63
  350.6 89.3 %reduce-scatter.5.cloned.1.call-start = ((), (), s32[]{:S(2)}) async-start(), calls=%async_computation.6 | async-start | bytes 327680 | tf_op jit(solution)/shard_map/reduce_scatter | solution.py:64
Sparse Core Ops, SparseCore 0:
  15.7 40.6 all-gather.2
  112.0 134.3 all-reduce.2
  294.9 38.0 all-gather.4
  350.7 67.0 reduce-scatter.2
  420.8 19.0 reduce-scatter.4
where the time goes:
time: 448 us
  waiting for transfers between devices  283 us (63%)
  blocking collectives  96.6 us (22%)
  matrix products  35.9 us (8%)
  between operations  16.3 us (4%)
  local copies, waits for them, and re-layouts  9.02 us (2%)
  other arithmetic  5.97 us (1%)
    psum x1, waiting for transfers between devices, shards(): whole_sum = lax.psum(pooled_part, ('ctx', 'cls'))  131 us
    reduce_scatter x1, waiting for transfers between devices, shards(): lax.psum_scatter(query_part, 'ctx', scatter_dimension=1, tiled=True)  67.1 us
    all_gather x1, waiting for transfers between devices, shards(): scores = project_add(lax.all_gather(query_block, 'ctx', axis=1, tiled=True))  40.1 us
    pmax x1, blocking collectives, shards(): peak = lax.pmax(local_peak, ('ctx', 'cls'))  38.3 us
    all_gather x1, waiting for transfers between devices, shards(): lax.all_gather(grad_block, 'ctx', axis=1, tiled=True)  38 us
    psum x1, blocking collectives, shards(): squares, logit_raw = lax.psum((square_part, logit_part), 'ctx')  20.7 us
    dot_general x1, matrix products, shards(): query_part = jnp.dot(score_grad, tokens, preferred_element_type=jnp.float32)  17.6 us
    psum x1, blocking collectives, shards(): inner_mean = lax.psum(inner_part, 'ctx') / full_width  17.1 us
  transfers between devices with their start and end apart: 5, of which 5 were waited for; matrix products, arithmetic and copies ran while one was open for 3% of the time, Pallas kernels for 0%

commit v1 on v0

v1 whole, which is shorter than its diff:
```python
import functools

import jax
import jax.numpy as jnp
from jax import lax
from jax.experimental import pallas as pl
from jax.experimental.pallas import tpu as pltpu
from jax.sharding import PartitionSpec as P

F32 = jnp.float32
BF16 = jnp.bfloat16
LANES = 128
MASKED = -1e30
VMEM_LIMIT = 48 * 1024 * 1024


def bits(count):
    return [1 << b for b in reversed(range(count.bit_length() - 1))]


def swap(x, axis, bit):
    count = lax.axis_size(axis)
    return lax.ppermute(x, axis, [(i, i ^ bit) for i in range(count)])


def gather(block):
    held = block[None]
    for bit in bits(lax.axis_size("ctx")):
        held = jnp.concatenate([held, swap(held, "ctx", bit)], axis=0)
    for bit in bits(lax.axis_size("cls")):
        held = jnp.concatenate([held, swap(held, "cls", bit)], axis=1)
    return held


def relative_blocks(count):
    order = [0]
    for bit in bits(count):
        order = order + [o ^ bit for o in order]
    return order


def vmem_call(kernel, outs, name, scratch=(), any_args=(), smem_args=(), flops=0, count=0):
    def spec(i):
        if i in any_args:
            return pl.BlockSpec(memory_space=pl.ANY)
        if i in smem_args:
            return pl.BlockSpec(memory_space=pltpu.SMEM)
        return pl.BlockSpec(memory_space=pltpu.VMEM)

    return pl.pallas_call(
        kernel,
        out_shape=[jax.ShapeDtypeStruct(s, d) for s, d in outs],
        in_specs=[spec(i) for i in range(count)],
        out_specs=[pl.BlockSpec(memory_space=pltpu.VMEM)] * len(outs),
        scratch_shapes=list(scratch),
        compiler_params=pltpu.CompilerParams(vmem_limit_bytes=VMEM_LIMIT),
        name=name,
    )


def start_tokens(order_ref, tokens_ref, held, sems, width):
    copies = []
    for p in range(held.shape[0]):
        at = pl.multiple_of(order_ref[p] * width, LANES)
        copy = pltpu.make_async_copy(tokens_ref.at[:, pl.ds(at, width)], held.at[p], sems.at[p])
        copy.start()
        copies.append(copy)
    return copies


def project(copies, block_ref, held):
    total = None
    for p, copy in enumerate(copies):
        copy.wait()
        part = lax.dot_general(
            block_ref[p], held[p], (((1,), (1,)), ((), ())), preferred_element_type=F32
        )
        total = part if total is None else total + part
    return total


def spread(left, held, keep_ref, send_ref):
    half = keep_ref.shape[1]
    for p in range(held.shape[0]):
        part = jnp.dot(left, held[p], preferred_element_type=F32)
        keep_ref[p] = part[:half]
        send_ref[p] = part[half:].astype(send_ref.dtype)


def pool_kernel(order_ref, count_ref, q_ref, tokens_ref, keep_ref, send_ref, peak_ref, w_ref, held, sems):
    copies = start_tokens(order_ref, tokens_ref, held, sems, q_ref.shape[2])
    scores = project(copies, q_ref, held)
    valid = lax.broadcasted_iota(jnp.int32, scores.shape, 1) < count_ref[0]
    peak = jnp.max(jnp.where(valid, scores, MASKED), axis=1, keepdims=True)
    weights = jnp.where(valid, jnp.exp(scores - peak), 0.0)
    w_ref[...] = weights
    peak_ref[...] = jnp.broadcast_to(peak, peak_ref.shape)
    spread(weights.astype(BF16), held, keep_ref, send_ref)


def grad_kernel(order_ref, g_ref, tokens_ref, w_ref, peak_ref, top_ref, keep_ref, send_ref, held, sems):
    copies = start_tokens(order_ref, tokens_ref, held, sems, g_ref.shape[2])
    projected = project(copies, g_ref, held)
    weights = w_ref[...] * jnp.exp(peak_ref[:, :1] - top_ref[:, :1])
    spread((weights * projected).astype(BF16), held, keep_ref, send_ref)


def combine_peaks_kernel(axis, keep_ref, recv_ref, mine_ref, other_ref, *outs):
    mine, other = mine_ref[...], other_ref[...]
    top = jnp.maximum(mine, other)
    scale_mine = jnp.exp(mine - top)[:, :1]
    scale_other = jnp.exp(other - top)[:, :1]
    outs[-1][...] = top
    for p in range(keep_ref.shape[0]):
        total = keep_ref[p] * scale_mine + recv_ref[p].astype(F32) * scale_other
        store_half(axis, p, total, outs[:-1])


def combine_kernel(axis, keep_ref, recv_ref, *outs):
    for p in range(keep_ref.shape[0]):
        store_half(axis, p, keep_ref[p] + recv_ref[p].astype(F32), outs)


def store_half(axis, p, total, outs):
    keep_ref = outs[0]
    if len(outs) == 1:
        keep_ref[p] = total
    elif axis == "cls":
        half = keep_ref.shape[1]
        keep_ref[p] = total[:half]
        outs[1][p] = total[half:].astype(BF16)
    elif p < keep_ref.shape[0]:
        keep_ref[p] = total
    else:
        outs[1][p - keep_ref.shape[0]] = total.astype(BF16)


def scatter_sum(keep, send, peak):
    steps = [("ctx", b) for b in bits(lax.axis_size("ctx"))] + [("cls", b) for b in bits(lax.axis_size("cls"))]
    steps = steps[::-1]
    for i, (axis, bit) in enumerate(steps):
        recv = swap(send, axis, bit)
        blocks, rows, width = keep.shape
        following = steps[i + 1][0] if i + 1 < len(steps) else None
        if following is None:
            outs = [((blocks, rows, width), F32)]
        else:
            shape = (blocks, rows // 2, width) if following == "cls" else (blocks // 2, rows, width)
            outs = [(shape, F32), (shape, BF16)]
        if peak is None:
            out = vmem_call(functools.partial(combine_kernel, following), outs, "combine", count=2)(keep, recv)
        else:
            if axis == "cls":
                mine, other = peak[:rows], swap(peak[rows:], axis, bit)
            else:
                mine, other = peak, swap(peak, axis, bit)
            *out, peak = vmem_call(
                functools.partial(combine_peaks_kernel, following), outs + [(mine.shape, F32)], "combine_peaks", count=4
            )(keep, recv, mine, other)
        keep, send = out if following is not None else (out[0], None)
    return keep[0], peak


def head_mask(shape, attributes):
    row = lax.broadcasted_iota(jnp.int32, shape, 0)
    column = lax.broadcasted_iota(jnp.int32, shape, 1)
    return column // attributes == row


def head_sums_kernel(pooled_ref, gain_ref, weight_ref, sums_ref):
    pooled = pooled_ref[...]
    scaled_b = (pooled * gain_ref[...]).astype(BF16)
    product = jnp.dot(scaled_b, weight_ref[...], preferred_element_type=F32)
    mask = head_mask(product.shape, product.shape[1] // product.shape[0])
    squares = jnp.sum(pooled * pooled, axis=1, keepdims=True)
    sums_ref[0:1, :] = jnp.sum(jnp.where(mask, product, 0.0), axis=0, keepdims=True)
    sums_ref[1:2, :] = jnp.sum(jnp.where(mask, squares, 0.0), axis=0, keepdims=True)


def head_grads_kernel(
    full_width, sums_ref, pooled_ref, gain_ref, weight_ref, bias_ref, label_ref, bias_grad_ref, loss_ref, grad_ref, normed_ref
):
    pooled, gain = pooled_ref[...], gain_ref[...]
    heads, columns = pooled.shape[0], sums_ref.shape[1]
    mask = head_mask((heads, columns), columns // heads)
    inverse_flat = lax.rsqrt(sums_ref[1:2, :] / full_width + 1e-05)
    inverse_rms = jnp.max(jnp.where(mask, inverse_flat, 0.0), axis=1, keepdims=True)
    product = inverse_flat * sums_ref[0:1, :]
    logits = product + bias_ref[...]
    target = label_ref[...].astype(F32)
    loss = jnp.maximum(logits, 0.0) + jnp.log1p(jnp.exp(-jnp.abs(logits))) - target * logits
    loss_ref[...] = jnp.broadcast_to(jnp.sum(loss, axis=1, keepdims=True), loss_ref.shape)
    bias_grad = jax.nn.sigmoid(logits) - target
    bias_grad_ref[...] = bias_grad
    by_head = jnp.where(mask, bias_grad, 0.0)
    high = by_head.astype(BF16)
    low = (by_head - high.astype(F32)).astype(BF16)
    both = jnp.concatenate([high, low], axis=0)
    back = lax.dot_general(both, weight_ref[...], (((1,), (1,)), ((), ())), preferred_element_type=F32)
    normed_grad = (back[:heads] + back[heads:]) * gain
    inner = jnp.sum(by_head * product, axis=1, keepdims=True) / full_width
    unit = pooled * inverse_rms
    grad_ref[...] = (inverse_rms * (normed_grad - unit * inner)).astype(BF16)
    normed_ref[...] = unit * gain


def shards(tokens, doc_length, queries, norm_gain, head_weight, head_bias, labels):
    context_count = lax.axis_size("ctx")
    class_count = lax.axis_size("cls")
    context_index = lax.axis_index("ctx")
    class_index = lax.axis_index("cls")
    token_count = tokens.shape[0]
    rows, width = queries.shape
    full_width = width * context_count
    heads = rows * class_count
    columns = labels.shape[0]
    order = context_index ^ jnp.array(relative_blocks(context_count), jnp.int32)
    offset = (context_index * class_count + class_index) * token_count
    valid_count = jnp.clip(doc_length - offset, 0, token_count)
    half = ((context_count, heads // 2, width), F32), ((context_count, heads // 2, width), BF16)
    tokens_scratch = (pltpu.VMEM((context_count, token_count, width), BF16), pltpu.SemaphoreType.DMA((context_count,)))

    query_blocks = gather(queries)
    keep, send, own_peak, weights = vmem_call(
        pool_kernel,
        [*half, ((heads, LANES), F32), ((heads, token_count), F32)],
        "pool",
        tokens_scratch,
        any_args=(3,),
        smem_args=(0, 1),
        count=4,
    )(order, valid_count, query_blocks, tokens)
    pooled, peak = scatter_sum(keep, send, own_peak)
    top = peak
    for bit in bits(class_count):
        top = jnp.concatenate([top, swap(top, "cls", bit)], axis=0)

    gain = norm_gain[None, :]
    (sums,) = vmem_call(head_sums_kernel, [((2, columns), F32)], "head_sums", count=3)(pooled, gain, head_weight)
    for bit in bits(context_count):
        sums = sums + swap(sums, "ctx", bit)
    bias_grad, loss, pooled_grad, normed = vmem_call(
        functools.partial(head_grads_kernel, full_width),
        [((1, columns), F32), ((1, LANES), F32), ((rows, width), BF16), ((rows, width), F32)],
        "head_grads",
        count=6,
    )(sums, pooled, gain, head_weight, head_bias[None, :], labels[None, :])

    grad_blocks = gather(pooled_grad)
    keep, send = vmem_call(
        grad_kernel, half, "grad", tokens_scratch, any_args=(2,), smem_args=(0,), count=6
    )(order, grad_blocks, tokens, weights, own_peak, top)
    query_grad, _ = scatter_sum(keep, send, None)

    for bit in bits(class_count):
        loss = loss + swap(loss, "cls", bit)
    mean_loss = loss[0, 0] / (columns * class_count)
    bias_rows = bias_grad.reshape(rows, -1)
    head_grad = (normed.T[:, :, None] * bias_rows[None]).reshape(width, columns)
    return (mean_loss, query_grad, head_grad, bias_grad.reshape(-1))


def solution(mesh):
    return jax.shard_map(
        shards,
        mesh=mesh,
        in_specs=(
            P(("ctx", "cls"), None),
            P(),
            P("cls", "ctx"),
            P("ctx"),
            P("ctx", "cls"),
            P("cls"),
            P("cls"),
        ),
        out_specs=(P(), P("cls", "ctx"), P("ctx", "cls"), P("cls")),
        check_vma=False,
    )
```

time: 448 us -> 153 us (0.34)
  waiting for transfers between devices: 283 us -> 80.3 us
  blocking collectives: 96.6 us -> 0 us
  matrix products: 35.9 us -> 0 us
  starting transfers between devices: 0.39 us -> 32.6 us
  Pallas kernels: 0 us -> 23.9 us
  between operations: 16.3 us -> 2.71 us
    psum x1 -> x0, waiting for transfers between devices: 131 us -> none  [shards(): whole_sum = lax.psum(pooled_part, ('ctx', 'cls'))]
    ppermute x0 -> x32, waiting for transfers between devices: none -> 80.3 us  [swap(): return lax.ppermute(x, axis, [(i, i ^ bit) for i in range(count)])]
    all_gather x2 -> x0, waiting for transfers between devices: 78 us -> none  [the longest x1 40.1 us: shards(): scores = project_add(lax.all_gather(query_block, 'ctx', axis=1, tiled=True))]
    reduce_scatter x2 -> x0, waiting for transfers between devices: 73.9 us -> none  [the longest x1 67.1 us: shards(): lax.psum_scatter(query_part, 'ctx', scatter_dimension=1, tiled=True)]
    psum x3 -> x0, blocking collectives: 44.1 us -> none  [the longest x1 20.7 us: shards(): squares, logit_raw = lax.psum((square_part, logit_part), 'ctx')]
    pmax x1 -> x0, blocking collectives: 38.3 us -> none  [shards(): peak = lax.pmax(local_peak, ('ctx', 'cls'))]
    dot_general x5 -> x0, matrix products: 35.9 us -> none  [the longest x1 17.6 us: shards(): query_part = jnp.dot(score_grad, tokens, preferred_element_type=jnp.float32)]
    ppermute x0 -> x32, starting transfers between devices: none -> 32.6 us  [swap(): return lax.ppermute(x, axis, [(i, i ^ bit) for i in range(count)])]
  transfers between devices with their start and end apart: 5 -> 32, of which waited for: 5 -> 24; matrix products, arithmetic and copies ran while one was open for 3% -> 5% of each run, Pallas kernels for 0% -> 0%
where the time goes in v1:
time: 153 us; the launch traced here: 152 us
  waiting for transfers between devices  80.3 us (52%)
  starting transfers between devices  32.6 us (21%)
  Pallas kernels  23.9 us (16%)
  other arithmetic  7.15 us (5%)
  local copies, waits for them, and re-layouts  5.38 us (4%)
  between operations  2.71 us (2%)
    ppermute x32, waiting for transfers between devices, swap(): return lax.ppermute(x, axis, [(i, i ^ bit) for i in range(count)])  80.3 us
    ppermute x32, starting transfers between devices, swap(): return lax.ppermute(x, axis, [(i, i ^ bit) for i in range(count)])  32.6 us
    pallas_call x1, Pallas kernels, shards(): vmem_call(pool_kernel, [*half, ((heads, LANES), F32), ((heads, token_coun...  10.7 us
    pallas_call x1, Pallas kernels, shards(): vmem_call(grad_kernel, half, 'grad', tokens_scratch, any_args=(2,), smem_...  10.6 us
    unnamed x11, local copies, waits for them, and re-layouts  5.37 us
  transfers between devices with their start and end apart: 32, of which 24 were waited for; matrix products, arithmetic and copies ran while one was open for 5% of the time, Pallas kernels for 0%

profile of v1, /device:TPU:0, one launch (start us, length us, event | category | flops | bytes accessed | tf_op | source)
XLA Modules:
  0.0 152.0 jit_solution(4615111548484316490)
XLA Ops:
  0.6 4.1 %collective-permute-start = (bf16[1,16,1024]{2,1,0:T(8,128)(2,1)}, bf16[1,16,1024]{2,1,0:T(8,128)(2,1)S(1)}, u32[]{:S(2)}, u32[]{:S(2)}) collective-permute-start(bf16[1,16,1024]{2,1,0:T(8,128)(2,1)} %bitcast.27), channel_id=1, source_target_pairs={{0,16},{4,20},{8,24},{12,28},{16,0},{20,4},{24,8},{28,12},{1,17},{... | collective-permute-start | bytes 98312 | tf_op jit(solution)/shard_map/ppermute | solution.py:23
  4.7 2.5 %collective-permute-done = bf16[1,16,1024]{2,1,0:T(8,128)(2,1)S(1)} collective-permute-done((bf16[1,16,1024]{2,1,0:T(8,128)(2,1)}, bf16[1,16,1024]{2,1,0:T(8,128)(2,1)S(1)}, u32[]{:S(2)}, u32[]{:S(2)}) %collective-permute-start) | collective-permute-done | bytes 32800 | tf_op jit(solution)/shard_map/ppermute | solution.py:23
  7.2 0.8 pad_maximum_fusion.8
  8.0 1.6 %collective-permute-start.1 = (bf16[2,16,1024]{2,1,0:T(8,128)(2,1)S(1)}, bf16[2,16,1024]{2,1,0:T(8,128)(2,1)S(1)}, u32[]{:S(2)}, u32[]{:S(2)}) collective-permute-start(bf16[2,16,1024]{2,1,0:T(8,128)(2,1)S(1)} %pad_maximum_fusion.8), channel_id=1, source_target_pairs={{0,8},{4,12},{8,0},{12,4},{16,24},{20,28},{24,16},{28,20},{1,9},{5... | collective-permute-start | bytes 196616 | tf_op jit(solution)/shard_map/ppermute | solution.py:23
  9.5 2.7 %collective-permute-done.1 = bf16[2,16,1024]{2,1,0:T(8,128)(2,1)S(1)} collective-permute-done((bf16[2,16,1024]{2,1,0:T(8,128)(2,1)S(1)}, bf16[2,16,1024]{2,1,0:T(8,128)(2,1)S(1)}, u32[]{:S(2)}, u32[]{:S(2)}) %collective-permute-start.1) | collective-permute-done | bytes 65568 | tf_op jit(solution)/shard_map/ppermute | solution.py:23
  12.2 0.8 pad_maximum_fusion.6
  13.0 1.8 %collective-permute-start.2 = (bf16[4,16,1024]{2,1,0:T(8,128)(2,1)S(1)}, bf16[4,16,1024]{2,1,0:T(8,128)(2,1)S(1)}, u32[]{:S(2)}, u32[]{:S(2)}) collective-permute-start(bf16[4,16,1024]{2,1,0:T(8,128)(2,1)S(1)} %pad_maximum_fusion.6), channel_id=1, source_target_pairs={{0,4},{4,0},{8,12},{12,8},{16,20},{20,16},{24,28},{28,24},{1,5},{5... | collective-permute-start | bytes 393224 | tf_op jit(solution)/shard_map/ppermute | solution.py:23
  14.8 3.3 %collective-permute-done.2 = bf16[4,16,1024]{2,1,0:T(8,128)(2,1)S(1)} collective-permute-done((bf16[4,16,1024]{2,1,0:T(8,128)(2,1)S(1)}, bf16[4,16,1024]{2,1,0:T(8,128)(2,1)S(1)}, u32[]{:S(2)}, u32[]{:S(2)}) %collective-permute-start.2) | collective-permute-done | bytes 131104 | tf_op jit(solution)/shard_map/ppermute | solution.py:23
  18.0 0.8 pad_maximum_fusion.4
  18.8 1.8 %collective-permute-start.3 = (bf16[8,16,1024]{2,1,0:T(8,128)(2,1)S(1)}, bf16[8,16,1024]{2,1,0:T(8,128)(2,1)S(1)}, u32[]{:S(2)}, u32[]{:S(2)}) collective-permute-start(bf16[8,16,1024]{2,1,0:T(8,128)(2,1)S(1)} %pad_maximum_fusion.4), channel_id=1, source_target_pairs={{0,2},{1,3},{2,0},{3,1},{4,6},{5,7},{6,4},{7,5},{8,10},{9,11},{10,... | collective-permute-start | bytes 786440 | tf_op jit(solution)/shard_map/ppermute | solution.py:23
  20.6 4.6 %collective-permute-done.3 = bf16[8,16,1024]{2,1,0:T(8,128)(2,1)S(1)} collective-permute-done((bf16[8,16,1024]{2,1,0:T(8,128)(2,1)S(1)}, bf16[8,16,1024]{2,1,0:T(8,128)(2,1)S(1)}, u32[]{:S(2)}, u32[]{:S(2)}) %collective-permute-start.3) | collective-permute-done | bytes 262176 | tf_op jit(solution)/shard_map/ppermute | solution.py:23
  25.3 0.8 pad_maximum_fusion.2
  28.0 0.9 pad_maximum_fusion.q_ref
  28.9 10.7 %pool.1 = (f32[8,32,1024]{2,1,0:T(8,128)S(1)}, bf16[8,32,1024]{2,1,0:T(8,128)(2,1)S(1)}, f32[64,128]{1,0:T(8,128)S(1)}, f32[64,768]{1,0:T(8,128)S(1)}) custom-call(s32[8]{0:T(128)S(1)} %broadcast_xor_fusion.order_ref, s32[1]{0:T(128)S(6)} %min.6.count_ref, bf16[8,64,1024]{2,1,0:T(8,128)(2,1)S(1)} %pad_maximum_fusion.q_ref, bf16[768,8192]{1,0:T(8,128)(2,1)} %tokens_ref.3), custom_call_target="tpu_custom_call" | custom-call | tf_op jit(solution)/shard_map/pool/pallas_call | solution.py:224
  40.2 1.4 collective-permute-done.6.other_ref
  41.9 1.8 %collective-permute-start.7 = (bf16[8,16,1024]{2,1,0:T(8,128)(2,1)S(1)}, bf16[8,16,1024]{2,1,0:T(8,128)(2,1)S(1)}, u32[]{:S(2)}, u32[]{:S(2)}) collective-permute-start(bf16[8,16,1024]{2,1,0:T(8,128)(2,1)S(1)} %get-tuple-element.40), channel_id=1, source_target_pairs={{0,2},{1,3},{2,0},{3,1},{4,6},{5,7},{6,4},{7,5},{8,10},{9,11},{10,... | collective-permute-start | bytes 786440 | tf_op jit(solution)/shard_map/ppermute | solution.py:23
  44.0 6.5 %collective-permute-done.8.other_ref = f32[16,128]{1,0:T(8,128)S(1)} collective-permute-done((f32[16,128]{1,0:T(8,128)S(1)}, f32[16,128]{1,0:T(8,128)S(1)}, u32[]{:S(2)}, u32[]{:S(2)}) %collective-permute-start.8) | collective-permute-done | bytes 8224 | tf_op jit(solution)/shard_map/ppermute | solution.py:23
  50.7 1.8 %collective-permute-start.9 = (bf16[4,16,1024]{2,1,0:T(8,128)(2,1)S(1)}, bf16[4,16,1024]{2,1,0:T(8,128)(2,1)S(1)}, u32[]{:S(2)}, u32[]{:S(2)}) collective-permute-start(bf16[4,16,1024]{2,1,0:T(8,128)(2,1)S(1)} %get-tuple-element.43), channel_id=1, source_target_pairs={{0,4},{4,0},{8,12},{12,8},{16,20},{20,16},{24,28},{28,24},{1,5},{5... | collective-permute-start | bytes 393224 | tf_op jit(solution)/shard_map/ppermute | solution.py:23
  52.8 3.3 %collective-permute-done.10.other_ref = f32[16,128]{1,0:T(8,128)S(1)} collective-permute-done((f32[16,128]{1,0:T(8,128)S(1)}, f32[16,128]{1,0:T(8,128)S(1)}, u32[]{:S(2)}, u32[]{:S(2)}) %collective-permute-start.10) | collective-permute-done | bytes 8224 | tf_op jit(solution)/shard_map/ppermute | solution.py:23
  56.2 1.4 collective-permute-start.11
  58.3 3.0 %collective-permute-done.12.other_ref = f32[16,128]{1,0:T(8,128)S(1)} collective-permute-done((f32[16,128]{1,0:T(8,128)S(1)}, f32[16,128]{1,0:T(8,128)S(1)}, u32[]{:S(2)}, u32[]{:S(2)}) %collective-permute-start.12) | collective-permute-done | bytes 8224 | tf_op jit(solution)/shard_map/ppermute | solution.py:23
  61.4 2.9 %collective-permute-start.13 = (bf16[1,16,1024]{2,1,0:T(8,128)(2,1)S(1)}, bf16[1,16,1024]{2,1,0:T(8,128)(2,1)S(1)}, u32[]{:S(2)}, u32[]{:S(2)}) collective-permute-start(bf16[1,16,1024]{2,1,0:T(8,128)(2,1)S(1)} %get-tuple-element.49), channel_id=1, source_target_pairs={{0,16},{4,20},{8,24},{12,28},{16,0},{20,4},{24,8},{28,12},{1,17},{... | collective-permute-start | bytes 98312 | tf_op jit(solution)/shard_map/ppermute | solution.py:23
  64.4 4.5 %collective-permute-done.14.other_ref = f32[16,128]{1,0:T(8,128)S(1)} collective-permute-done((f32[16,128]{1,0:T(8,128)S(1)}, f32[16,128]{1,0:T(8,128)S(1)}, u32[]{:S(2)}, u32[]{:S(2)}) %collective-permute-start.14) | collective-permute-done | bytes 8224 | tf_op jit(solution)/shard_map/ppermute | solution.py:23
  69.9 4.1 %collective-permute-done.15 = f32[2,1024]{1,0:T(2,128)S(1)} collective-permute-done((f32[2,1024]{1,0:T(2,128)S(1)}, f32[2,1024]{1,0:T(2,128)S(1)}, u32[]{:S(2)}, u32[]{:S(2)}) %collective-permute-start.15) | collective-permute-done | bytes 8224 | tf_op jit(solution)/shard_map/ppermute | solution.py:23
  74.7 3.1 %collective-permute-done.16 = f32[2,1024]{1,0:T(2,128)S(1)} collective-permute-done((f32[2,1024]{1,0:T(2,128)S(1)}, f32[2,1024]{1,0:T(2,128)S(1)}, u32[]{:S(2)}, u32[]{:S(2)}) %collective-permute-start.16) | collective-permute-done | bytes 8224 | tf_op jit(solution)/shard_map/ppermute | solution.py:23
  77.7 1.5 collective-permute-start.17
  79.2 2.1 %collective-permute-done.17 = f32[2,1024]{1,0:T(2,128)S(1)} collective-permute-done((f32[2,1024]{1,0:T(2,128)S(1)}, f32[2,1024]{1,0:T(2,128)S(1)}, u32[]{:S(2)}, u32[]{:S(2)}) %collective-permute-start.17) | collective-permute-done | bytes 8224 | tf_op jit(solution)/shard_map/ppermute | solution.py:23
  81.4 0.7 head_grads.1
  82.5 4.8 %collective-permute-done.20 = bf16[1,16,1024]{2,1,0:T(8,128)(2,1)S(1)} collective-permute-done((bf16[1,16,1024]{2,1,0:T(8,128)(2,1)S(1)}, bf16[1,16,1024]{2,1,0:T(8,128)(2,1)S(1)}, u32[]{:S(2)}, u32[]{:S(2)}) %collective-permute-start.20) | collective-permute-done | bytes 32800 | tf_op jit(solution)/shard_map/ppermute | solution.py:23
  87.7 3.9 %collective-permute-done.21 = bf16[2,16,1024]{2,1,0:T(8,128)(2,1)S(1)} collective-permute-done((bf16[2,16,1024]{2,1,0:T(8,128)(2,1)S(1)}, bf16[2,16,1024]{2,1,0:T(8,128)(2,1)S(1)}, u32[]{:S(2)}, u32[]{:S(2)}) %collective-permute-start.21) | collective-permute-done | bytes 65568 | tf_op jit(solution)/shard_map/ppermute | solution.py:23
  91.7 1.5 collective-permute-start.22
  93.2 3.5 %collective-permute-done.22 = bf16[4,16,1024]{2,1,0:T(8,128)(2,1)S(1)} collective-permute-done((bf16[4,16,1024]{2,1,0:T(8,128)(2,1)S(1)}, bf16[4,16,1024]{2,1,0:T(8,128)(2,1)S(1)}, u32[]{:S(2)}, u32[]{:S(2)}) %collective-permute-start.22) | collective-permute-done | bytes 131104 | tf_op jit(solution)/shard_map/ppermute | solution.py:23
  96.7 1.6 %collective-permute-start.23 = (bf16[8,16,1024]{2,1,0:T(8,128)(2,1)S(1)}, bf16[8,16,1024]{2,1,0:T(8,128)(2,1)S(1)}, u32[]{:S(2)}, u32[]{:S(2)}) collective-permute-start(bf16[8,16,1024]{2,1,0:T(8,128)(2,1)S(1)} %pad_maximum_fusion.5), channel_id=1, source_target_pairs={{0,2},{1,3},{2,0},{3,1},{4,6},{5,7},{6,4},{7,5},{8,10},{9,11},{10,... | collective-permute-start | bytes 786440 | tf_op jit(solution)/shard_map/ppermute | solution.py:23
  98.3 4.9 %collective-permute-done.23 = bf16[8,16,1024]{2,1,0:T(8,128)(2,1)S(1)} collective-permute-done((bf16[8,16,1024]{2,1,0:T(8,128)(2,1)S(1)}, bf16[8,16,1024]{2,1,0:T(8,128)(2,1)S(1)}, u32[]{:S(2)}, u32[]{:S(2)}) %collective-permute-start.23) | collective-permute-done | bytes 262176 | tf_op jit(solution)/shard_map/ppermute | solution.py:23
  103.3 1.6 %collective-permute-start.25 = (f32[16,128]{1,0:T(8,128)S(1)}, f32[16,128]{1,0:T(8,128)S(1)}, u32[]{:S(2)}, u32[]{:S(2)}) collective-permute-start(f32[16,128]{1,0:T(8,128)S(1)} %get-tuple-element.55), channel_id=1, source_target_pairs={{0,2},{1,3},{2,0},{3,1},{4,6},{5,7},{6,4},{7,5},{8,10},{9,11},{10,... | collective-permute-start | bytes 24584 | tf_op jit(solution)/shard_map/ppermute | solution.py:23
  104.9 2.1 %collective-permute-done.25 = f32[16,128]{1,0:T(8,128)S(1)} collective-permute-done((f32[16,128]{1,0:T(8,128)S(1)}, f32[16,128]{1,0:T(8,128)S(1)}, u32[]{:S(2)}, u32[]{:S(2)}) %collective-permute-start.25) | collective-permute-done | bytes 8224 | tf_op jit(solution)/shard_map/ppermute | solution.py:23
  107.0 1.2 collective-permute-done.26
  108.3 10.6 %grad.1 = (f32[8,32,1024]{2,1,0:T(8,128)S(1)}, bf16[8,32,1024]{2,1,0:T(8,128)(2,1)S(1)}) custom-call(s32[8]{0:T(128)S(1)} %broadcast_xor_fusion.order_ref, bf16[8,64,1024]{2,1,0:T(8,128)(2,1)S(1)} %pad_maximum_fusion.1.g_ref, bf16[768,8192]{1,0:T(8,128)(2,1)} %tokens_ref.3, f32[64,768]{1,0:T(8,128)S(1)} %get-tuple-element.54.w_ref, ...), custom_call_target="tpu_custom_call" | custom-call | tf_op jit(solution)/shard_map/grad/pallas_call | solution.py:250
  119.1 1.7 %collective-permute-done.27.recv_ref = bf16[8,32,1024]{2,1,0:T(8,128)(2,1)S(1)} collective-permute-done((bf16[8,32,1024]{2,1,0:T(8,128)(2,1)S(1)}, bf16[8,32,1024]{2,1,0:T(8,128)(2,1)S(1)}, u32[]{:S(2)}, u32[]{:S(2)}) %collective-permute-start.27) | collective-permute-done | bytes 524320 | tf_op jit(solution)/shard_map/ppermute | solution.py:23
  121.0 1.6 %collective-permute-start.28 = (bf16[8,16,1024]{2,1,0:T(8,128)(2,1)S(1)}, bf16[8,16,1024]{2,1,0:T(8,128)(2,1)S(1)}, u32[]{:S(2)}, u32[]{:S(2)}) collective-permute-start(bf16[8,16,1024]{2,1,0:T(8,128)(2,1)S(1)} %get-tuple-element.59), channel_id=1, source_target_pairs={{0,2},{1,3},{2,0},{3,1},{4,6},{5,7},{6,4},{7,5},{8,10},{9,11},{10,... | collective-permute-start | bytes 786440 | tf_op jit(solution)/shard_map/ppermute | solution.py:23
  122.5 6.9 %collective-permute-done.28.recv_ref = bf16[8,16,1024]{2,1,0:T(8,128)(2,1)S(1)} collective-permute-done((bf16[8,16,1024]{2,1,0:T(8,128)(2,1)S(1)}, bf16[8,16,1024]{2,1,0:T(8,128)(2,1)S(1)}, u32[]{:S(2)}, u32[]{:S(2)}) %collective-permute-start.28) | collective-permute-done | bytes 262176 | tf_op jit(solution)/shard_map/ppermute | solution.py:23
  129.5 1.5 collective-permute-start.29
  131.0 3.5 %collective-permute-done.29.recv_ref = bf16[4,16,1024]{2,1,0:T(8,128)(2,1)S(1)} collective-permute-done((bf16[4,16,1024]{2,1,0:T(8,128)(2,1)S(1)}, bf16[4,16,1024]{2,1,0:T(8,128)(2,1)S(1)}, u32[]{:S(2)}, u32[]{:S(2)}) %collective-permute-start.29) | collective-permute-done | bytes 131104 | tf_op jit(solution)/shard_map/ppermute | solution.py:23
  134.9 3.9 %collective-permute-done.30.recv_ref = bf16[2,16,1024]{2,1,0:T(8,128)(2,1)S(1)} collective-permute-done((bf16[2,16,1024]{2,1,0:T(8,128)(2,1)S(1)}, bf16[2,16,1024]{2,1,0:T(8,128)(2,1)S(1)}, u32[]{:S(2)}, u32[]{:S(2)}) %collective-permute-start.30) | collective-permute-done | bytes 65568 | tf_op jit(solution)/shard_map/ppermute | solution.py:23
  139.0 1.6 %collective-permute-start.18 = (f32[1,128]{1,0:T(1,128)S(1)}, f32[1,128]{1,0:T(1,128)S(1)}, u32[]{:S(2)}, u32[]{:S(2)}) collective-permute-start(f32[1,128]{1,0:T(1,128)S(1)} %get-tuple-element.52), channel_id=1, source_target_pairs={{0,2},{1,3},{2,0},{3,1},{4,6},{5,7},{6,4},{7,5},{8,10},{9,11},{10,... | collective-permute-start | bytes 1544 | tf_op jit(solution)/shard_map/ppermute | solution.py:23
  140.5 2.0 %collective-permute-done.18 = f32[1,128]{1,0:T(1,128)S(1)} collective-permute-done((f32[1,128]{1,0:T(1,128)S(1)}, f32[1,128]{1,0:T(1,128)S(1)}, u32[]{:S(2)}, u32[]{:S(2)}) %collective-permute-start.18) | collective-permute-done | bytes 544 | tf_op jit(solution)/shard_map/ppermute | solution.py:23
  142.6 2.3 %bitcast_multiply_fusion = f32[1024,1024]{0,1:T(8,128)} fusion(f32[1024]{0:T(1024)S(1)} %bitcast.35, f32[1024,16]{0,1:T(8,128)S(1)} %bitcast.22), kind=kLoop, calls=%fused_computation | loop fusion | flops 1048576 | bytes 4263936 | tf_op jit(solution)/shard_map/mul | solution.py:259
  144.9 5.3 %copy.13 = f32[1024,1024]{1,0:T(8,128)} copy(f32[1024,1024]{0,1:T(8,128)} %bitcast_multiply_fusion) | data formatting | bytes 8388608
  (62 shorter events, 8.2 us)
Async XLA Ops:
  0.6 6.6 %collective-permute-start = (bf16[1,16,1024]{2,1,0:T(8,128)(2,1)}, bf16[1,16,1024]{2,1,0:T(8,128)(2,1)S(1)}, u32[]{:S(2)}, u32[]{:S(2)}) collective-permute-start(bf16[1,16,1024]{2,1,0:T(8,128)(2,1)} %bitcast.27), channel_id=1, source_target_pairs={{0,16},{4,20},{8,24},{12,28},{16,0},{20,4},{24,8},{28,12},{1,17},{... | collective-permute-start | bytes 98312 | tf_op jit(solution)/shard_map/ppermute | solution.py:23
  8.0 4.3 %collective-permute-start.1 = (bf16[2,16,1024]{2,1,0:T(8,128)(2,1)S(1)}, bf16[2,16,1024]{2,1,0:T(8,128)(2,1)S(1)}, u32[]{:S(2)}, u32[]{:S(2)}) collective-permute-start(bf16[2,16,1024]{2,1,0:T(8,128)(2,1)S(1)} %pad_maximum_fusion.8), channel_id=1, source_target_pairs={{0,8},{4,12},{8,0},{12,4},{16,24},{20,28},{24,16},{28,20},{1,9},{5... | collective-permute-start | bytes 196616 | tf_op jit(solution)/shard_map/ppermute | solution.py:23
  13.0 5.0 %collective-permute-start.2 = (bf16[4,16,1024]{2,1,0:T(8,128)(2,1)S(1)}, bf16[4,16,1024]{2,1,0:T(8,128)(2,1)S(1)}, u32[]{:S(2)}, u32[]{:S(2)}) collective-permute-start(bf16[4,16,1024]{2,1,0:T(8,128)(2,1)S(1)} %pad_maximum_fusion.6), channel_id=1, source_target_pairs={{0,4},{4,0},{8,12},{12,8},{16,20},{20,16},{24,28},{28,24},{1,5},{5... | collective-permute-start | bytes 393224 | tf_op jit(solution)/shard_map/ppermute | solution.py:23
  18.8 6.4 %collective-permute-start.3 = (bf16[8,16,1024]{2,1,0:T(8,128)(2,1)S(1)}, bf16[8,16,1024]{2,1,0:T(8,128)(2,1)S(1)}, u32[]{:S(2)}, u32[]{:S(2)}) collective-permute-start(bf16[8,16,1024]{2,1,0:T(8,128)(2,1)S(1)} %pad_maximum_fusion.4), channel_id=1, source_target_pairs={{0,2},{1,3},{2,0},{3,1},{4,6},{5,7},{6,4},{7,5},{8,10},{9,11},{10,... | collective-permute-start | bytes 786440 | tf_op jit(solution)/shard_map/ppermute | solution.py:23
  26.1 2.0 %collective-permute-start.4 = (bf16[8,32,1024]{2,1,0:T(8,128)(2,1)S(1)}, bf16[8,32,1024]{2,1,0:T(8,128)(2,1)S(1)}, u32[]{:S(2)}, u32[]{:S(2)}) collective-permute-start(bf16[8,32,1024]{2,1,0:T(8,128)(2,1)S(1)} %pad_maximum_fusion.2), channel_id=1, source_target_pairs={{0,1},{1,0},{2,3},{3,2},{4,5},{5,4},{6,7},{7,6},{8,9},{9,8},{10,11... | collective-permute-start | bytes 1572872 | tf_op jit(solution)/shard_map/ppermute | solution.py:23
  39.6 29.3 %copy-start = (bf16[1024,1024]{1,0:T(8,128)(2,1)S(1)}, bf16[1024,1024]{1,0:T(8,128)(2,1)}, u32[]{:S(2)}) copy-start(bf16[1024,1024]{1,0:T(8,128)(2,1)} %weight_ref.3) | copy-start | bytes 6291460
  39.6 29.3 %copy-start.1 = (f32[1024]{0:T(1024)S(1)}, f32[1024]{0:T(1024)}, u32[]{:S(2)}) copy-start(f32[1024]{0:T(1024)} %param.11) | copy-start | bytes 12292
  39.6 2.0 %collective-permute-start.5 = (bf16[8,32,1024]{2,1,0:T(8,128)(2,1)S(1)}, bf16[8,32,1024]{2,1,0:T(8,128)(2,1)S(1)}, u32[]{:S(2)}, u32[]{:S(2)}) collective-permute-start(bf16[8,32,1024]{2,1,0:T(8,128)(2,1)S(1)} %get-tuple-element.37), channel_id=1, source_target_pairs={{0,1},{1,0},{2,3},{3,2},{4,5},{5,4},{6,7},{7,6},{8,9},{9,8},{10,11... | collective-permute-start | bytes 1572872 | tf_op jit(solution)/shard_map/ppermute | solution.py:23
  39.9 1.8 %collective-permute-start.6 = (f32[32,128]{1,0:T(8,128)S(1)}, f32[32,128]{1,0:T(8,128)S(1)}, u32[]{:S(2)}, u32[]{:S(2)}) collective-permute-start(f32[32,128]{1,0:T(8,128)S(1)} %get-tuple-element.72), channel_id=1, source_target_pairs={{0,1},{1,0},{2,3},{3,2},{4,5},{5,4},{6,7},{7,6},{8,9},{9,8},{10,11... | collective-permute-start | bytes 49160 | tf_op jit(solution)/shard_map/ppermute | solution.py:23
  41.9 39.5 %copy-start.2 = (f32[1024]{0:T(1024)S(1)}, f32[1024]{0:T(1024)}, u32[]{:S(2)}) copy-start(f32[1024]{0:T(1024)} %param.13) | copy-start | bytes 12292
  41.9 39.5 %copy-start.3 = (s32[1024]{0:T(1024)S(1)}, s32[1024]{0:T(1024)}, u32[]{:S(2)}) copy-start(s32[1024]{0:T(1024)} %param.14) | copy-start | bytes 12292
  41.9 8.6 %collective-permute-start.7 = (bf16[8,16,1024]{2,1,0:T(8,128)(2,1)S(1)}, bf16[8,16,1024]{2,1,0:T(8,128)(2,1)S(1)}, u32[]{:S(2)}, u32[]{:S(2)}) collective-permute-start(bf16[8,16,1024]{2,1,0:T(8,128)(2,1)S(1)} %get-tuple-element.40), channel_id=1, source_target_pairs={{0,2},{1,3},{2,0},{3,1},{4,6},{5,7},{6,4},{7,5},{8,10},{9,11},{10,... | collective-permute-start | bytes 786440 | tf_op jit(solution)/shard_map/ppermute | solution.py:23
  43.7 6.8 %collective-permute-start.8 = (f32[16,128]{1,0:T(8,128)S(1)}, f32[16,128]{1,0:T(8,128)S(1)}, u32[]{:S(2)}, u32[]{:S(2)}) collective-permute-start(f32[16,128]{1,0:T(8,128)S(1)} %get-tuple-element.74), channel_id=1, source_target_pairs={{0,2},{1,3},{2,0},{3,1},{4,6},{5,7},{6,4},{7,5},{8,10},{9,11},{10,... | collective-permute-start | bytes 24584 | tf_op jit(solution)/shard_map/ppermute | solution.py:23
  50.7 5.4 %collective-permute-start.9 = (bf16[4,16,1024]{2,1,0:T(8,128)(2,1)S(1)}, bf16[4,16,1024]{2,1,0:T(8,128)(2,1)S(1)}, u32[]{:S(2)}, u32[]{:S(2)}) collective-permute-start(bf16[4,16,1024]{2,1,0:T(8,128)(2,1)S(1)} %get-tuple-element.43), channel_id=1, source_target_pairs={{0,4},{4,0},{8,12},{12,8},{16,20},{20,16},{24,28},{28,24},{1,5},{5... | collective-permute-start | bytes 393224 | tf_op jit(solution)/shard_map/ppermute | solution.py:23
  52.4 3.7 %collective-permute-start.10 = (f32[16,128]{1,0:T(8,128)S(1)}, f32[16,128]{1,0:T(8,128)S(1)}, u32[]{:S(2)}, u32[]{:S(2)}) collective-permute-start(f32[16,128]{1,0:T(8,128)S(1)} %get-tuple-element.44.mine_ref), channel_id=1, source_target_pairs={{0,4},{4,0},{8,12},{12,8},{16,20},{20,16},{24,28},{28,24},{1,5},{5... | collective-permute-start | bytes 24584 | tf_op jit(solution)/shard_map/ppermute | solution.py:23
  56.2 5.1 %collective-permute-start.11 = (bf16[2,16,1024]{2,1,0:T(8,128)(2,1)S(1)}, bf16[2,16,1024]{2,1,0:T(8,128)(2,1)S(1)}, u32[]{:S(2)}, u32[]{:S(2)}) collective-permute-start(bf16[2,16,1024]{2,1,0:T(8,128)(2,1)S(1)} %get-tuple-element.46), channel_id=1, source_target_pairs={{0,8},{4,12},{8,0},{12,4},{16,24},{20,28},{24,16},{28,20},{1,9},{5... | collective-permute-start | bytes 196616 | tf_op jit(solution)/shard_map/ppermute | solution.py:23
  57.6 3.7 %collective-permute-start.12 = (f32[16,128]{1,0:T(8,128)S(1)}, f32[16,128]{1,0:T(8,128)S(1)}, u32[]{:S(2)}, u32[]{:S(2)}) collective-permute-start(f32[16,128]{1,0:T(8,128)S(1)} %get-tuple-element.47.mine_ref), channel_id=1, source_target_pairs={{0,8},{4,12},{8,0},{12,4},{16,24},{20,28},{24,16},{28,20},{1,9},{5... | collective-permute-start | bytes 24584 | tf_op jit(solution)/shard_map/ppermute | solution.py:23
  61.4 7.4 %collective-permute-start.13 = (bf16[1,16,1024]{2,1,0:T(8,128)(2,1)S(1)}, bf16[1,16,1024]{2,1,0:T(8,128)(2,1)S(1)}, u32[]{:S(2)}, u32[]{:S(2)}) collective-permute-start(bf16[1,16,1024]{2,1,0:T(8,128)(2,1)S(1)} %get-tuple-element.49), channel_id=1, source_target_pairs={{0,16},{4,20},{8,24},{12,28},{16,0},{20,4},{24,8},{28,12},{1,17},{... | collective-permute-start | bytes 98312 | tf_op jit(solution)/shard_map/ppermute | solution.py:23
  64.3 4.5 %collective-permute-start.14 = (f32[16,128]{1,0:T(8,128)S(1)}, f32[16,128]{1,0:T(8,128)S(1)}, u32[]{:S(2)}, u32[]{:S(2)}) collective-permute-start(f32[16,128]{1,0:T(8,128)S(1)} %get-tuple-element.50.mine_ref), channel_id=1, source_target_pairs={{0,16},{4,20},{8,24},{12,28},{16,0},{20,4},{24,8},{28,12},{1,17},{... | collective-permute-start | bytes 24584 | tf_op jit(solution)/shard_map/ppermute | solution.py:23
  69.4 4.6 %collective-permute-start.15 = (f32[2,1024]{1,0:T(2,128)S(1)}, f32[2,1024]{1,0:T(2,128)S(1)}, u32[]{:S(2)}, u32[]{:S(2)}) collective-permute-start(f32[2,1024]{1,0:T(2,128)S(1)} %head_sums.1), channel_id=1, source_target_pairs={{0,16},{4,20},{8,24},{12,28},{16,0},{20,4},{24,8},{28,12},{1,17},{... | collective-permute-start | bytes 24584 | tf_op jit(solution)/shard_map/ppermute | solution.py:23
  74.0 3.8 %collective-permute-start.16 = (f32[2,1024]{1,0:T(2,128)S(1)}, f32[2,1024]{1,0:T(2,128)S(1)}, u32[]{:S(2)}, u32[]{:S(2)}) collective-permute-start(f32[2,1024]{1,0:T(2,128)S(1)} %add.19), channel_id=1, source_target_pairs={{0,8},{4,12},{8,0},{12,4},{16,24},{20,28},{24,16},{28,20},{1,9},{5... | collective-permute-start | bytes 24584 | tf_op jit(solution)/shard_map/ppermute | solution.py:23
  77.7 3.7 %collective-permute-start.17 = (f32[2,1024]{1,0:T(2,128)S(1)}, f32[2,1024]{1,0:T(2,128)S(1)}, u32[]{:S(2)}, u32[]{:S(2)}) collective-permute-start(f32[2,1024]{1,0:T(2,128)S(1)} %add.20), channel_id=1, source_target_pairs={{0,4},{4,0},{8,12},{12,8},{16,20},{20,16},{24,28},{28,24},{1,5},{5... | collective-permute-start | bytes 24584 | tf_op jit(solution)/shard_map/ppermute | solution.py:23
  82.1 5.2 %collective-permute-start.20 = (bf16[1,16,1024]{2,1,0:T(8,128)(2,1)S(1)}, bf16[1,16,1024]{2,1,0:T(8,128)(2,1)S(1)}, u32[]{:S(2)}, u32[]{:S(2)}) collective-permute-start(bf16[1,16,1024]{2,1,0:T(8,128)(2,1)S(1)} %bitcast.14), channel_id=1, source_target_pairs={{0,16},{4,20},{8,24},{12,28},{16,0},{20,4},{24,8},{28,12},{1,17},{... | collective-permute-start | bytes 98312 | tf_op jit(solution)/shard_map/ppermute | solution.py:23
  87.3 4.3 %collective-permute-start.21 = (bf16[2,16,1024]{2,1,0:T(8,128)(2,1)S(1)}, bf16[2,16,1024]{2,1,0:T(8,128)(2,1)S(1)}, u32[]{:S(2)}, u32[]{:S(2)}) collective-permute-start(bf16[2,16,1024]{2,1,0:T(8,128)(2,1)S(1)} %pad_maximum_fusion.9), channel_id=1, source_target_pairs={{0,8},{4,12},{8,0},{12,4},{16,24},{20,28},{24,16},{28,20},{1,9},{5... | collective-permute-start | bytes 196616 | tf_op jit(solution)/shard_map/ppermute | solution.py:23
  91.7 5.0 %collective-permute-start.22 = (bf16[4,16,1024]{2,1,0:T(8,128)(2,1)S(1)}, bf16[4,16,1024]{2,1,0:T(8,128)(2,1)S(1)}, u32[]{:S(2)}, u32[]{:S(2)}) collective-permute-start(bf16[4,16,1024]{2,1,0:T(8,128)(2,1)S(1)} %pad_maximum_fusion.7), channel_id=1, source_target_pairs={{0,4},{4,0},{8,12},{12,8},{16,20},{20,16},{24,28},{28,24},{1,5},{5... | collective-permute-start | bytes 393224 | tf_op jit(solution)/shard_map/ppermute | solution.py:23
  96.7 6.4 %collective-permute-start.23 = (bf16[8,16,1024]{2,1,0:T(8,128)(2,1)S(1)}, bf16[8,16,1024]{2,1,0:T(8,128)(2,1)S(1)}, u32[]{:S(2)}, u32[]{:S(2)}) collective-permute-start(bf16[8,16,1024]{2,1,0:T(8,128)(2,1)S(1)} %pad_maximum_fusion.5), channel_id=1, source_target_pairs={{0,2},{1,3},{2,0},{3,1},{4,6},{5,7},{6,4},{7,5},{8,10},{9,11},{10,... | collective-permute-start | bytes 786440 | tf_op jit(solution)/shard_map/ppermute | solution.py:23
  103.2 5.0 %collective-permute-start.24 = (bf16[8,32,1024]{2,1,0:T(8,128)(2,1)S(1)}, bf16[8,32,1024]{2,1,0:T(8,128)(2,1)S(1)}, u32[]{:S(2)}, u32[]{:S(2)}) collective-permute-start(bf16[8,32,1024]{2,1,0:T(8,128)(2,1)S(1)} %pad_maximum_fusion.3), channel_id=1, source_target_pairs={{0,1},{1,0},{2,3},{3,2},{4,5},{5,4},{6,7},{7,6},{8,9},{9,8},{10,11... | collective-permute-start | bytes 1572872 | tf_op jit(solution)/shard_map/ppermute | solution.py:23
  103.3 3.7 %collective-permute-start.25 = (f32[16,128]{1,0:T(8,128)S(1)}, f32[16,128]{1,0:T(8,128)S(1)}, u32[]{:S(2)}, u32[]{:S(2)}) collective-permute-start(f32[16,128]{1,0:T(8,128)S(1)} %get-tuple-element.55), channel_id=1, source_target_pairs={{0,2},{1,3},{2,0},{3,1},{4,6},{5,7},{6,4},{7,5},{8,10},{9,11},{10,... | collective-permute-start | bytes 24584 | tf_op jit(solution)/shard_map/ppermute | solution.py:23
  107.0 1.2 collective-permute-start.26
  118.9 23.7 %copy-start.4 = (f32[1,1024]{1,0:T(1,128)S(1)}, f32[1,1024]{1,0:T(1,128)}, u32[]{:S(2)}) copy-start(f32[1,1024]{1,0:T(1,128)} %get-tuple-element.67) | copy-start | bytes 12292
  118.9 2.0 %collective-permute-start.27 = (bf16[8,32,1024]{2,1,0:T(8,128)(2,1)S(1)}, bf16[8,32,1024]{2,1,0:T(8,128)(2,1)S(1)}, u32[]{:S(2)}, u32[]{:S(2)}) collective-permute-start(bf16[8,32,1024]{2,1,0:T(8,128)(2,1)S(1)} %get-tuple-element.57), channel_id=1, source_target_pairs={{0,1},{1,0},{2,3},{3,2},{4,5},{5,4},{6,7},{7,6},{8,9},{9,8},{10,11... | collective-permute-start | bytes 1572872 | tf_op jit(solution)/shard_map/ppermute | solution.py:23
  121.0 8.4 %collective-permute-start.28 = (bf16[8,16,1024]{2,1,0:T(8,128)(2,1)S(1)}, bf16[8,16,1024]{2,1,0:T(8,128)(2,1)S(1)}, u32[]{:S(2)}, u32[]{:S(2)}) collective-permute-start(bf16[8,16,1024]{2,1,0:T(8,128)(2,1)S(1)} %get-tuple-element.59), channel_id=1, source_target_pairs={{0,2},{1,3},{2,0},{3,1},{4,6},{5,7},{6,4},{7,5},{8,10},{9,11},{10,... | collective-permute-start | bytes 786440 | tf_op jit(solution)/shard_map/ppermute | solution.py:23
  129.5 5.0 %collective-permute-start.29 = (bf16[4,16,1024]{2,1,0:T(8,128)(2,1)S(1)}, bf16[4,16,1024]{2,1,0:T(8,128)(2,1)S(1)}, u32[]{:S(2)}, u32[]{:S(2)}) collective-permute-start(bf16[4,16,1024]{2,1,0:T(8,128)(2,1)S(1)} %get-tuple-element.61), channel_id=1, source_target_pairs={{0,4},{4,0},{8,12},{12,8},{16,20},{20,16},{24,28},{28,24},{1,5},{5... | collective-permute-start | bytes 393224 | tf_op jit(solution)/shard_map/ppermute | solution.py:23
  134.5 4.3 %collective-permute-start.30 = (bf16[2,16,1024]{2,1,0:T(8,128)(2,1)S(1)}, bf16[2,16,1024]{2,1,0:T(8,128)(2,1)S(1)}, u32[]{:S(2)}, u32[]{:S(2)}) collective-permute-start(bf16[2,16,1024]{2,1,0:T(8,128)(2,1)S(1)} %get-tuple-element.63), channel_id=1, source_target_pairs={{0,8},{4,12},{8,0},{12,4},{16,24},{20,28},{24,16},{28,20},{1,9},{5... | collective-permute-start | bytes 196616 | tf_op jit(solution)/shard_map/ppermute | solution.py:23
  138.9 11.4 %collective-permute-start.31 = (bf16[1,16,1024]{2,1,0:T(8,128)(2,1)S(1)}, bf16[1,16,1024]{2,1,0:T(8,128)(2,1)S(1)}, u32[]{:S(2)}, u32[]{:S(2)}) collective-permute-start(bf16[1,16,1024]{2,1,0:T(8,128)(2,1)S(1)} %get-tuple-element.65), channel_id=1, source_target_pairs={{0,16},{4,20},{8,24},{12,28},{16,0},{20,4},{24,8},{28,12},{1,17},{... | collective-permute-start | bytes 98312 | tf_op jit(solution)/shard_map/ppermute | solution.py:23
  139.0 3.6 %collective-permute-start.18 = (f32[1,128]{1,0:T(1,128)S(1)}, f32[1,128]{1,0:T(1,128)S(1)}, u32[]{:S(2)}, u32[]{:S(2)}) collective-permute-start(f32[1,128]{1,0:T(1,128)S(1)} %get-tuple-element.52), channel_id=1, source_target_pairs={{0,2},{1,3},{2,0},{3,1},{4,6},{5,7},{6,4},{7,5},{8,10},{9,11},{10,... | collective-permute-start | bytes 1544 | tf_op jit(solution)/shard_map/ppermute | solution.py:23
  142.6 7.6 %collective-permute-start.19 = (f32[1,128]{1,0:T(1,128)S(1)}, f32[1,128]{1,0:T(1,128)S(1)}, u32[]{:S(2)}, u32[]{:S(2)}) collective-permute-start(f32[1,128]{1,0:T(1,128)S(1)} %add.22), channel_id=1, source_target_pairs={{0,1},{1,0},{2,3},{3,2},{4,5},{5,4},{6,7},{7,6},{8,9},{9,8},{10,11... | collective-permute-start | bytes 1544 | tf_op jit(solution)/shard_map/ppermute | solution.py:23

commit v2 on v0

v2 whole, which is shorter than its diff:
```python
import functools

import jax
import jax.numpy as jnp
from jax import lax
from jax.experimental import pallas as pl
from jax.experimental.pallas import tpu as pltpu
from jax.sharding import PartitionSpec as P

F32 = jnp.float32
BF16 = jnp.bfloat16
LANES = 128
MASKED = -1e30
MIB = 1024 * 1024


def swap(x, ctx_bits, cls_bits):
    contexts, classes = lax.axis_size("ctx"), lax.axis_size("cls")
    pairs = [
        (c * classes + k, (c ^ ctx_bits) * classes + (k ^ cls_bits)) for c in range(contexts) for k in range(classes)
    ]
    return lax.ppermute(x, ("ctx", "cls"), pairs)


def far_steps():
    return [(2 * j, 0) for j in range(1, lax.axis_size("ctx") // 2)]


def near_steps():
    return [(i, 2 * k) for i in range(2) for k in range(lax.axis_size("cls") // 2) if i or k]


def relative_blocks(contexts):
    return [i ^ (2 * j) for i in range(2) for j in range(contexts // 2)]


def call(kernel, outs, name, args, scratch=(), any_args=(), smem_args=(), limit=16, cost=None):
    def spec(i):
        if i in any_args:
            return pl.BlockSpec(memory_space=pl.ANY)
        if i in smem_args:
            return pl.BlockSpec(memory_space=pltpu.SMEM)
        return pl.BlockSpec(memory_space=pltpu.VMEM)

    run = pl.pallas_call(
        kernel,
        out_shape=[jax.ShapeDtypeStruct(s, d) for s, d in outs],
        in_specs=[spec(i) for i in range(len(args))],
        out_specs=[pl.BlockSpec(memory_space=pltpu.VMEM)] * len(outs),
        scratch_shapes=list(scratch),
        compiler_params=pltpu.CompilerParams(vmem_limit_bytes=limit * MIB),
        cost_estimate=cost,
        name=name,
    )
    return list(run(*args))


def stack_kernel(axis, *refs):
    out_ref, at = refs[-1], 0
    for ref in refs[:-1]:
        size = ref.shape[axis]
        if axis == 0:
            out_ref[at : at + size] = ref[...]
        else:
            out_ref[:, at : at + size] = ref[...]
        at += size


def stack(parts, axis):
    shape = list(parts[0].shape)
    shape[axis] = sum(p.shape[axis] for p in parts)
    (out,) = call(functools.partial(stack_kernel, axis), [(tuple(shape), parts[0].dtype)], "stack", parts)
    return out


def near_kernel(*refs):
    out_ref, parts = refs[-1], refs[:-1]
    blocks, rows, _ = parts[0].shape
    across = len(parts) // 2
    for i in range(2):
        for k in range(across):
            out_ref[i * blocks : (i + 1) * blocks, k * rows : (k + 1) * rows] = parts[i * across + k][...]


def gather(block):
    block = block[None]
    held = stack([block] + [swap(block, *step) for step in far_steps()], 0)
    parts = [held] + [swap(held, *step) for step in near_steps()]
    blocks, rows, width = held.shape
    (held,) = call(near_kernel, [((2 * blocks, len(parts) // 2 * rows, width), held.dtype)], "near", parts)
    return held, swap(held, 0, 1)


def pieces(x):
    high = x.astype(BF16)
    rest = x - high.astype(F32)
    middle = rest.astype(BF16)
    return high, middle, (rest - middle.astype(F32)).astype(BF16)


def into_lanes(columns, rows):
    lane = lax.broadcasted_iota(jnp.int32, (rows, LANES), 1)
    out = jnp.zeros((rows, LANES), F32)
    for i, column in enumerate(columns):
        for j, piece in enumerate(pieces(column)):
            out = jnp.where(lane == 3 * i + j, piece.astype(F32), out)
    return out.astype(BF16)


def from_lanes(block, width, i):
    at = width + 3 * i
    block = block.astype(F32)
    return block[:, at : at + 1] + (block[:, at + 1 : at + 2] + block[:, at + 2 : at + 3])


def columns_of(context_ref, contexts, p, width):
    return pl.ds(pl.multiple_of((context_ref[0] ^ relative_blocks(contexts)[p]) * width, LANES), width)


def project(context_ref, own_ref, other_ref, tokens_ref, width):
    contexts = own_ref.shape[0]
    total = None
    for p in range(contexts):
        both = jnp.concatenate([own_ref[p], other_ref[p]], axis=0)[:, :width]
        block = tokens_ref[:, columns_of(context_ref, contexts, p, width)]
        part = lax.dot_general(block, both, (((1,), (1,)), ((), ())), preferred_element_type=F32)
        total = part if total is None else total + part
    return total.T


def spread(context_ref, left, tokens_ref, keep_ref, send_ref, extra):
    contexts, half, width = keep_ref.shape
    for p in range(contexts):
        block = tokens_ref[:, columns_of(context_ref, contexts, p, width)]
        part = jnp.dot(left, block, preferred_element_type=F32)
        keep_ref[p] = part[:half]
        send_ref[p, :, :width] = part[half:].astype(BF16)
        if extra is not None:
            send_ref[p, :, width:] = extra


def pool_kernel(context_ref, count_ref, own_ref, other_ref, tokens_ref, keep_ref, send_ref, peak_ref, w_ref):
    scores = project(context_ref, own_ref, other_ref, tokens_ref, keep_ref.shape[2])
    valid = lax.broadcasted_iota(jnp.int32, scores.shape, 1) < count_ref[0]
    peak = jnp.max(jnp.where(valid, scores, MASKED), axis=1, keepdims=True)
    weights = jnp.where(valid, jnp.exp(scores - peak), 0.0)
    w_ref[...] = weights
    peak_ref[...] = jnp.broadcast_to(peak, peak_ref.shape)
    half = keep_ref.shape[1]
    spread(context_ref, weights.astype(BF16), tokens_ref, keep_ref, send_ref, into_lanes([peak[half:]], half))


def grad_kernel(scale, context_ref, own_ref, other_ref, tokens_ref, w_ref, peak_ref, keep_ref, send_ref, loss_ref):
    width = keep_ref.shape[2]
    projected = project(context_ref, own_ref, other_ref, tokens_ref, width)
    own, other = own_ref[0], other_ref[0]
    top = jnp.concatenate([from_lanes(own, width, 0), from_lanes(other, width, 0)], axis=0)
    weights = w_ref[...] * jnp.exp(peak_ref[:, :1] - top)
    spread(context_ref, (weights * projected).astype(BF16), tokens_ref, keep_ref, send_ref, None)
    rows = loss_ref.shape[0] // 2
    each = own.shape[0] // rows
    sums = []
    for block in (own, other):
        column = from_lanes(block, width, 1)
        level = [column[i * each : i * each + 1] for i in range(rows)]
        while len(level) > 1:
            level = [a + b for a, b in zip(level[::2], level[1::2])]
        sums.append(level[0])
    loss_ref[...] = jnp.broadcast_to((sums[0] + sums[1]) * scale, loss_ref.shape)


def total_of(keep, peak, received, width):
    if peak is None:
        for block in received:
            keep = keep + block.astype(F32)
        return keep, None
    others = [from_lanes(block, width, 0) for block in received]
    top = peak
    for other in others:
        top = jnp.maximum(top, other)
    keep = keep * jnp.exp(peak - top)
    for block, other in zip(received, others):
        keep = keep + block[:, :width].astype(F32) * jnp.exp(other - top)
    return keep, top


def put(ref, p, total, top, width):
    ref[p, :, :width] = total.astype(BF16)
    if top is not None:
        ref[p, :, width:] = into_lanes([top], total.shape[0])


def core_kernel(peaks, across, *refs):
    keep_ref, recv_ref, *refs = refs
    peak = refs.pop(0)[: keep_ref.shape[1], :1] if peaks else None
    top_ref = refs.pop() if peaks else None
    width = keep_ref.shape[2]
    blocks, rows = refs[0].shape[:2]
    for i in range(2):
        for b in range(blocks):
            p = i * blocks + b
            total, top = total_of(keep_ref[p], peak, [recv_ref[p]], width)
            for k in range(across):
                part = total[k * rows : (k + 1) * rows]
                part_top = top[k * rows : (k + 1) * rows] if peaks else None
                if i == 0 and k == 0:
                    refs[0][b] = part
                else:
                    put(refs[i * across + k], b, part, part_top, width)
    if peaks:
        top_ref[...] = jnp.broadcast_to(top[:rows], top_ref.shape)


def near_sum_kernel(peaks, count, *refs):
    keep_ref, *refs = refs
    received, refs = refs[:count], list(refs[count:])
    peak = refs.pop(0)[:, :1] if peaks else None
    top_ref = refs.pop() if peaks else None
    width = keep_ref.shape[2]
    for p in range(keep_ref.shape[0]):
        total, top = total_of(keep_ref[p], peak, [ref[p] for ref in received], width)
        if p == 0:
            refs[0][0] = total
        else:
            put(refs[p], 0, total, top, width)
    if peaks:
        top_ref[...] = jnp.broadcast_to(top, top_ref.shape)


def scatter_sum(keep, send, peak):
    peaks = peak is not None
    contexts, half, width = keep.shape
    lanes = send.shape[2]
    near, far = near_steps(), far_steps()
    across = (len(near) + 1) // 2
    blocks, rows = contexts // 2, half // across
    top_out = [((rows, LANES), F32)] if peaks else []
    outs = [((blocks, rows, width), F32)] + [((blocks, rows, lanes), BF16)] * len(near) + top_out
    args = [keep, swap(send, 0, 1)] + ([peak] if peaks else [])
    out = call(functools.partial(core_kernel, peaks, across), outs, "core_sum", args)
    received = [swap(s, *step) for s, step in zip(out[1:], near)]
    outs = [((1, rows, width), F32)] + [((1, rows, lanes), BF16)] * len(far) + top_out
    args = [out[0], *received] + (out[-1:] if peaks else [])
    out = call(functools.partial(near_sum_kernel, peaks, len(received)), outs, "near_sum", args)
    received = [swap(s, *step) for s, step in zip(out[1:], far)]
    return [out[0], *received] + (out[-1:] if peaks else [])


def far_sum_kernel(*refs):
    keep_ref, *received, out_ref = refs
    out_ref[...] = total_of(keep_ref[0], None, [ref[0] for ref in received], keep_ref.shape[2])[0]


def head_mask(shape, attributes):
    row = lax.broadcasted_iota(jnp.int32, shape, 0)
    column = lax.broadcasted_iota(jnp.int32, shape, 1)
    return column // attributes == row


def head_sums_kernel(*refs):
    keep_ref, *received, peak_ref, gain_ref, weight_ref, sums_ref, pooled_ref, top_ref = refs
    pooled, top = total_of(keep_ref[0], peak_ref[:, :1], [ref[0] for ref in received], keep_ref.shape[2])
    pooled_ref[...] = pooled
    top_ref[...] = jnp.broadcast_to(top, top_ref.shape)
    scaled_b = (pooled * gain_ref[...]).astype(BF16)
    product = jnp.dot(scaled_b, weight_ref[...], preferred_element_type=F32)
    mask = head_mask(product.shape, product.shape[1] // product.shape[0])
    squares = jnp.sum(pooled * pooled, axis=1, keepdims=True)
    product_flat = jnp.sum(jnp.where(mask, product, 0.0), axis=0, keepdims=True)
    squares_flat = jnp.sum(jnp.where(mask, squares, 0.0), axis=0, keepdims=True)
    for p in range(sums_ref.shape[0]):
        sums_ref[p, 0:1, :] = product_flat
        sums_ref[p, 1:2, :] = squares_flat


def head_grads_kernel(
    full_width, sums_ref, pooled_ref, top_ref, gain_ref, weight_ref, bias_ref, label_ref, bias_grad_ref, grad_ref, normed_ref
):
    pooled, gain = pooled_ref[...], gain_ref[...]
    heads, width = pooled.shape
    columns = sums_ref.shape[2]
    sums = sums_ref[0]
    for p in range(1, sums_ref.shape[0]):
        sums = sums + sums_ref[p]
    mask = head_mask((heads, columns), columns // heads)
    inverse_flat = lax.rsqrt(sums[1:2] / full_width + 1e-05)
    inverse_rms = jnp.max(jnp.where(mask, inverse_flat, 0.0), axis=1, keepdims=True)
    product = inverse_flat * sums[0:1]
    logits = product + bias_ref[...]
    target = label_ref[...].astype(F32)
    losses = jnp.maximum(logits, 0.0) + jnp.log1p(jnp.exp(-jnp.abs(logits))) - target * logits
    loss = jnp.sum(losses, axis=1, keepdims=True)
    bias_grad = jax.nn.sigmoid(logits) - target
    bias_grad_ref[...] = bias_grad
    by_head = jnp.where(mask, bias_grad, 0.0)
    high = by_head.astype(BF16)
    low = (by_head - high.astype(F32)).astype(BF16)
    both = jnp.concatenate([high, low], axis=0)
    back = lax.dot_general(both, weight_ref[...], (((1,), (1,)), ((), ())), preferred_element_type=F32)
    normed_grad = (back[:heads] + back[heads:]) * gain
    inner = jnp.sum(by_head * product, axis=1, keepdims=True) / full_width
    unit = pooled * inverse_rms
    grad_ref[:, :width] = (inverse_rms * (normed_grad - unit * inner)).astype(BF16)
    grad_ref[:, width:] = into_lanes([top_ref[:, :1], jnp.broadcast_to(loss, (heads, 1))], heads)
    normed_ref[...] = unit * gain


def head_weight_grad_kernel(attributes, normed_ref, bias_grad_ref, out_ref):
    heads = normed_ref.shape[0]
    columns = out_ref.shape[1]
    parts = jnp.concatenate(pieces(normed_ref[...]), axis=0)
    row = lax.broadcasted_iota(jnp.int32, (3 * heads, columns), 0) % heads
    column = pl.program_id(0) * columns + lax.broadcasted_iota(jnp.int32, (3 * heads, columns), 1)
    ones = jnp.where(column // attributes == row, 1.0, 0.0).astype(BF16)
    normed = lax.dot_general(parts, ones, (((0,), (0,)), ((), ())), preferred_element_type=F32)
    out_ref[...] = normed * bias_grad_ref[...]


def head_weight_grad(normed, bias_grad):
    rows, width = normed.shape
    columns = bias_grad.shape[1]
    block = columns // 4
    return pl.pallas_call(
        functools.partial(head_weight_grad_kernel, columns // rows),
        out_shape=jax.ShapeDtypeStruct((width, columns), F32),
        grid=(columns // block,),
        in_specs=[
            pl.BlockSpec((rows, width), lambda i: (0, 0)),
            pl.BlockSpec((1, block), lambda i: (0, i)),
        ],
        out_specs=pl.BlockSpec((width, block), lambda i: (0, i)),
        compiler_params=pltpu.CompilerParams(vmem_limit_bytes=16 * MIB),
        cost_estimate=pl.CostEstimate(flops=6 * rows * width * columns, bytes_accessed=4 * width * columns, transcendentals=0),
        name="head_weight_grad",
    )(normed, bias_grad)


def shards(tokens, doc_length, queries, norm_gain, head_weight, head_bias, labels):
    contexts, classes = lax.axis_size("ctx"), lax.axis_size("cls")
    context_index, class_index = lax.axis_index("ctx"), lax.axis_index("cls")
    token_count = tokens.shape[0]
    rows, width = queries.shape
    full_width = width * contexts
    heads = rows * classes
    half = heads // 2
    columns = labels.shape[0]
    offset = (context_index * classes + class_index) * token_count
    valid_count = jnp.clip(doc_length - offset, 0, token_count)

    context = context_index.astype(jnp.int32)[None]
    own, other = gather(queries)
    keep, send, own_peak, weights = call(
        pool_kernel,
        [
            ((contexts, half, width), F32),
            ((contexts, half, width + LANES), BF16),
            ((heads, LANES), F32),
            ((heads, token_count), F32),
        ],
        "pool",
        [context, valid_count, own, other, tokens],
        smem_args=(0, 1),
        limit=32,
    )
    parts = scatter_sum(keep, send, own_peak)
    gain = norm_gain[None, :]
    sums, pooled, top = call(
        head_sums_kernel,
        [((contexts, 2, columns), F32), ((rows, width), F32), ((rows, LANES), F32)],
        "head_sums",
        [*parts, gain, head_weight],
    )
    sums = lax.all_to_all(sums, "ctx", 0, 0)
    bias_grad, pooled_grad, normed = call(
        functools.partial(head_grads_kernel, full_width),
        [((1, columns), F32), ((rows, width + LANES), BF16), ((rows, width), F32)],
        "head_grads",
        [sums, pooled, top, gain, head_weight, head_bias[None, :], labels[None, :]],
    )
    head_grad = head_weight_grad(normed, bias_grad)
    own, other = gather(pooled_grad)
    keep, send, loss = call(
        functools.partial(grad_kernel, 1.0 / (columns * classes)),
        [((contexts, half, width), F32), ((contexts, half, width), BF16), ((classes, LANES), F32)],
        "grad",
        [context, own, other, tokens, weights, own_peak],
        smem_args=(0,),
        limit=32,
    )
    (query_grad,) = call(far_sum_kernel, [((rows, width), F32)], "far_sum", scatter_sum(keep, send, None))
    return (loss[0, 0], query_grad, head_grad, bias_grad.reshape(-1))


def solution(mesh):
    return jax.shard_map(
        shards,
        mesh=mesh,
        in_specs=(
            P(("ctx", "cls"), None),
            P(),
            P("cls", "ctx"),
            P("ctx"),
            P("ctx", "cls"),
            P("cls"),
            P("cls"),
        ),
        out_specs=(P(), P("cls", "ctx"), P("ctx", "cls"), P("cls")),
        check_vma=False,
    )
```

time: 448 us -> 115 us (0.26)
  waiting for transfers between devices: 283 us -> 38.7 us
  blocking collectives: 96.6 us -> 11.3 us
  matrix products: 35.9 us -> 0 us
  starting transfers between devices: 0.39 us -> 33.9 us
  Pallas kernels: 0 us -> 23.9 us
  between operations: 16.3 us -> 1.42 us
  other arithmetic: 5.97 us -> 0 us
    psum x1 -> x0, waiting for transfers between devices: 131 us -> none  [shards(): whole_sum = lax.psum(pooled_part, ('ctx', 'cls'))]
    all_gather x2 -> x0, waiting for transfers between devices: 78 us -> none  [the longest x1 40.1 us: shards(): scores = project_add(lax.all_gather(query_block, 'ctx', axis=1, tiled=True))]
    reduce_scatter x2 -> x0, waiting for transfers between devices: 73.9 us -> none  [the longest x1 67.1 us: shards(): lax.psum_scatter(query_part, 'ctx', scatter_dimension=1, tiled=True)]
    psum x3 -> x0, blocking collectives: 44.1 us -> none  [the longest x1 20.7 us: shards(): squares, logit_raw = lax.psum((square_part, logit_part), 'ctx')]
    ppermute x0 -> x28, waiting for transfers between devices: none -> 38.7 us  [swap(): return lax.ppermute(x, ('ctx', 'cls'), pairs)]
    pmax x1 -> x0, blocking collectives: 38.3 us -> none  [shards(): peak = lax.pmax(local_peak, ('ctx', 'cls'))]
    dot_general x5 -> x0, matrix products: 35.9 us -> none  [the longest x1 17.6 us: shards(): query_part = jnp.dot(score_grad, tokens, preferred_element_type=jnp.float32)]
    ppermute x0 -> x28, starting transfers between devices: none -> 33.9 us  [swap(): return lax.ppermute(x, ('ctx', 'cls'), pairs)]
  transfers between devices with their start and end apart: 5 -> 28, of which waited for: 5 -> 23; matrix products, arithmetic and copies ran while one was open for 3% -> 0% of each run, Pallas kernels for 0% -> 3%
where the time goes in v2:
time: 115 us
  waiting for transfers between devices  38.7 us (34%)
  starting transfers between devices  33.9 us (29%)
  Pallas kernels  23.9 us (21%)
  blocking collectives  11.3 us (10%)
  local copies, waits for them, and re-layouts  5.87 us (5%)
  between operations  1.42 us (1%)
    ppermute x28, waiting for transfers between devices, swap(): return lax.ppermute(x, ('ctx', 'cls'), pairs)  38.7 us
    ppermute x28, starting transfers between devices, swap(): return lax.ppermute(x, ('ctx', 'cls'), pairs)  33.9 us
    pallas_call x13, Pallas kernels, call(): return list(run(*args))  20.9 us
    all_to_all x1, blocking collectives, shards(): sums = lax.all_to_all(sums, 'ctx', 0, 0)  11.3 us
    unnamed x16, local copies, waits for them, and re-layouts  5.36 us
    pallas_call x1, Pallas kernels, head_weight_grad(): pl.pallas_call(functools.partial(head_weight_grad_kernel, columns // rows...  2.95 us
  transfers between devices with their start and end apart: 28, of which 23 were waited for; matrix products, arithmetic and copies ran while one was open for 0% of the time, Pallas kernels for 3%

profile of v2, /device:TPU:0, one launch (start us, length us, event | category | flops | bytes accessed | tf_op | source)
XLA Modules:
  0.0 115.1 jit_solution(1544877915863154264)
XLA Ops:
  0.6 5.1 %collective-permute-start.2 = (bf16[1,16,1024]{2,1,0:T(8,128)(2,1)}, bf16[1,16,1024]{2,1,0:T(8,128)(2,1)S(1)}, u32[]{:S(2)}, u32[]{:S(2)}) collective-permute-start(bf16[1,16,1024]{2,1,0:T(8,128)(2,1)} %bitcast.13), channel_id=1, source_target_pairs={{0,24},{1,25},{2,26},{3,27},{4,28},{5,29},{6,30},{7,31},{8,16},{9,... | collective-permute-start | bytes 98312 | tf_op jit(solution)/shard_map/ppermute | solution.py:22
  5.7 0.6 collective-permute-start
  6.4 1.5 %collective-permute-done.2.refs_3_ = bf16[1,16,1024]{2,1,0:T(8,128)(2,1)S(1)} collective-permute-done((bf16[1,16,1024]{2,1,0:T(8,128)(2,1)}, bf16[1,16,1024]{2,1,0:T(8,128)(2,1)S(1)}, u32[]{:S(2)}, u32[]{:S(2)}) %collective-permute-start.2) | collective-permute-done | bytes 32800 | tf_op jit(solution)/shard_map/ppermute | solution.py:22
  7.8 2.9 %collective-permute-done.1.refs_2_ = bf16[1,16,1024]{2,1,0:T(8,128)(2,1)S(1)} collective-permute-done((bf16[1,16,1024]{2,1,0:T(8,128)(2,1)}, bf16[1,16,1024]{2,1,0:T(8,128)(2,1)S(1)}, u32[]{:S(2)}, u32[]{:S(2)}) %collective-permute-start.1) | collective-permute-done | bytes 32800 | tf_op jit(solution)/shard_map/ppermute | solution.py:22
  10.8 0.8 copy-done.3
  11.5 2.5 %collective-permute-start.5 = (bf16[4,16,1024]{2,1,0:T(8,128)(2,1)S(1)}, bf16[4,16,1024]{2,1,0:T(8,128)(2,1)S(1)}, u32[]{:S(2)}, u32[]{:S(2)}) collective-permute-start(bf16[4,16,1024]{2,1,0:T(8,128)(2,1)S(1)} %stack.2.refs_0_), channel_id=1, source_target_pairs={{0,6},{1,7},{2,4},{3,5},{4,2},{5,3},{6,0},{7,1},{8,14},{9,15},{10,... | collective-permute-start | bytes 393224 | tf_op jit(solution)/shard_map/ppermute | solution.py:22
  15.1 2.7 %collective-permute-done.5.refs_3_ = bf16[4,16,1024]{2,1,0:T(8,128)(2,1)S(1)} collective-permute-done((bf16[4,16,1024]{2,1,0:T(8,128)(2,1)S(1)}, bf16[4,16,1024]{2,1,0:T(8,128)(2,1)S(1)}, u32[]{:S(2)}, u32[]{:S(2)}) %collective-permute-start.5) | collective-permute-done | bytes 131104 | tf_op jit(solution)/shard_map/ppermute | solution.py:22
  17.8 1.4 %collective-permute-done.4.refs_2_ = bf16[4,16,1024]{2,1,0:T(8,128)(2,1)S(1)} collective-permute-done((bf16[4,16,1024]{2,1,0:T(8,128)(2,1)S(1)}, bf16[4,16,1024]{2,1,0:T(8,128)(2,1)S(1)}, u32[]{:S(2)}, u32[]{:S(2)}) %collective-permute-start.4) | collective-permute-done | bytes 131104 | tf_op jit(solution)/shard_map/ppermute | solution.py:22
  20.3 1.2 %collective-permute-done.6.other_ref = bf16[8,32,1024]{2,1,0:T(8,128)(2,1)S(1)} collective-permute-done((bf16[8,32,1024]{2,1,0:T(8,128)(2,1)S(1)}, bf16[8,32,1024]{2,1,0:T(8,128)(2,1)S(1)}, u32[]{:S(2)}, u32[]{:S(2)}) %collective-permute-start.6) | collective-permute-done | bytes 524320 | tf_op jit(solution)/shard_map/ppermute | solution.py:22
  21.6 4.6 %copy-done = bf16[768,8192]{1,0:T(8,128)(2,1)S(1)} copy-done((bf16[768,8192]{1,0:T(8,128)(2,1)S(1)}, bf16[768,8192]{1,0:T(8,128)(2,1)}, u32[]{:S(2)}) %copy-start) | copy-done | bytes 12582936
  26.2 8.8 %pool.1 = (f32[8,32,1024]{2,1,0:T(8,128)S(1)}, bf16[8,32,1152]{2,1,0:T(8,128)(2,1)S(1)}, f32[64,128]{1,0:T(8,128)S(1)}, f32[64,768]{1,0:T(8,128)S(1)}) custom-call(s32[1]{0:T(128)} %bitcast.context_ref, s32[1]{0:T(128)S(6)} %min.6.count_ref, bf16[8,32,1024]{2,1,0:T(8,128)(2,1)S(1)} %near.2.own_ref, ...), custom_call_target="tpu_custom_call" | custom-call | tf_op jit(solution)/shard_map/pool/pallas_call | solution.py:55
  35.2 1.9 %collective-permute-done.7.refs_1_ = bf16[8,32,1152]{2,1,0:T(8,128)(2,1)S(1)} collective-permute-done((bf16[8,32,1152]{2,1,0:T(8,128)(2,1)S(1)}, bf16[8,32,1152]{2,1,0:T(8,128)(2,1)S(1)}, u32[]{:S(2)}, u32[]{:S(2)}) %collective-permute-start.7) | collective-permute-done | bytes 589856 | tf_op jit(solution)/shard_map/ppermute | solution.py:22
  37.5 1.1 collective-permute-start.8
  38.7 1.5 %collective-permute-start.9 = (bf16[4,16,1152]{2,1,0:T(8,128)(2,1)S(1)}, bf16[4,16,1152]{2,1,0:T(8,128)(2,1)S(1)}, u32[]{:S(2)}, u32[]{:S(2)}) collective-permute-start(bf16[4,16,1152]{2,1,0:T(8,128)(2,1)S(1)} %get-tuple-element.40), channel_id=1, source_target_pairs={{0,4},{1,5},{2,6},{3,7},{4,0},{5,1},{6,2},{7,3},{8,12},{9,13},{10,... | collective-permute-start | bytes 442376 | tf_op jit(solution)/shard_map/ppermute | solution.py:22
  40.2 0.9 collective-permute-start.10
  41.1 2.4 %collective-permute-done.8.refs_1_ = bf16[4,16,1152]{2,1,0:T(8,128)(2,1)S(1)} collective-permute-done((bf16[4,16,1152]{2,1,0:T(8,128)(2,1)S(1)}, bf16[4,16,1152]{2,1,0:T(8,128)(2,1)S(1)}, u32[]{:S(2)}, u32[]{:S(2)}) %collective-permute-start.8) | collective-permute-done | bytes 147488 | tf_op jit(solution)/shard_map/ppermute | solution.py:22
  43.5 1.9 %collective-permute-done.9.refs_2_ = bf16[4,16,1152]{2,1,0:T(8,128)(2,1)S(1)} collective-permute-done((bf16[4,16,1152]{2,1,0:T(8,128)(2,1)S(1)}, bf16[4,16,1152]{2,1,0:T(8,128)(2,1)S(1)}, u32[]{:S(2)}, u32[]{:S(2)}) %collective-permute-start.9) | collective-permute-done | bytes 147488 | tf_op jit(solution)/shard_map/ppermute | solution.py:22
  45.4 2.4 %collective-permute-done.10.refs_3_ = bf16[4,16,1152]{2,1,0:T(8,128)(2,1)S(1)} collective-permute-done((bf16[4,16,1152]{2,1,0:T(8,128)(2,1)S(1)}, bf16[4,16,1152]{2,1,0:T(8,128)(2,1)S(1)}, u32[]{:S(2)}, u32[]{:S(2)}) %collective-permute-start.10) | collective-permute-done | bytes 147488 | tf_op jit(solution)/shard_map/ppermute | solution.py:22
  48.2 2.1 %collective-permute-start.12 = (bf16[1,16,1152]{2,1,0:T(8,128)(2,1)S(1)}, bf16[1,16,1152]{2,1,0:T(8,128)(2,1)S(1)}, u32[]{:S(2)}, u32[]{:S(2)}) collective-permute-start(bf16[1,16,1152]{2,1,0:T(8,128)(2,1)S(1)} %get-tuple-element.45), channel_id=1, source_target_pairs={{0,16},{1,17},{2,18},{3,19},{4,20},{5,21},{6,22},{7,23},{8,24},{9,... | collective-permute-start | bytes 110600 | tf_op jit(solution)/shard_map/ppermute | solution.py:22
  50.3 2.3 %collective-permute-start.13 = (bf16[1,16,1152]{2,1,0:T(8,128)(2,1)S(1)}, bf16[1,16,1152]{2,1,0:T(8,128)(2,1)S(1)}, u32[]{:S(2)}, u32[]{:S(2)}) collective-permute-start(bf16[1,16,1152]{2,1,0:T(8,128)(2,1)S(1)} %get-tuple-element.46), channel_id=1, source_target_pairs={{0,24},{1,25},{2,26},{3,27},{4,28},{5,29},{6,30},{7,31},{8,16},{9,... | collective-permute-start | bytes 110600 | tf_op jit(solution)/shard_map/ppermute | solution.py:22
  52.6 1.0 collective-permute-done.12.refs_2_
  53.6 2.5 %collective-permute-done.13.refs_3_ = bf16[1,16,1152]{2,1,0:T(8,128)(2,1)S(1)} collective-permute-done((bf16[1,16,1152]{2,1,0:T(8,128)(2,1)S(1)}, bf16[1,16,1152]{2,1,0:T(8,128)(2,1)S(1)}, u32[]{:S(2)}, u32[]{:S(2)}) %collective-permute-start.13) | collective-permute-done | bytes 36896 | tf_op jit(solution)/shard_map/ppermute | solution.py:22
  56.1 0.6 head_sums.1
  56.7 11.3 %all_to_all.5.sums_ref = f32[8,2,1024]{2,1,0:T(2,128)S(1)} all-to-all(f32[8,2,1024]{2,1,0:T(2,128)S(1)} %get-tuple-element.48), channel_id=1, replica_groups=mesh['ctx'=8,'cls'=4] {'ctx'}, dimensions={0} | all-to-all | bytes 131072 | tf_op jit(solution)/shard_map/all_to_all | solution.py:373
  68.0 1.2 %head_grads.1 = (f32[1,1024]{1,0:T(1,128)}, bf16[16,1152]{1,0:T(8,128)(2,1)S(1)}, f32[16,1024]{1,0:T(8,128)S(1)}) custom-call(f32[8,2,1024]{2,1,0:T(2,128)S(1)} %all_to_all.5.sums_ref, f32[16,1024]{1,0:T(8,128)S(1)} %get-tuple-element.49.pooled_ref, f32[16,128]{1,0:T(8,128)S(1)} %get-tuple-element.50.top_ref, f32[1,1024]{1,0:T(1,128)S(1)} %bitcast.18, ...), custom_call_target="tpu_custom_call" | custom-call | tf_op jit(solution)/shard_map/head_grads/pallas_call | solution.py:55
  69.7 1.1 collective-permute-start.15
  70.8 2.8 %collective-permute-start.14 = (bf16[1,16,1152]{2,1,0:T(8,128)(2,1)S(1)}, bf16[1,16,1152]{2,1,0:T(8,128)(2,1)S(1)}, u32[]{:S(2)}, u32[]{:S(2)}) collective-permute-start(bf16[1,16,1152]{2,1,0:T(8,128)(2,1)S(1)} %bitcast.11), channel_id=1, source_target_pairs={{0,8},{1,9},{2,10},{3,11},{4,12},{5,13},{6,14},{7,15},{8,0},{9,1},... | collective-permute-start | bytes 110600 | tf_op jit(solution)/shard_map/ppermute | solution.py:22
  73.6 1.4 %collective-permute-done.16.refs_3_ = bf16[1,16,1152]{2,1,0:T(8,128)(2,1)S(1)} collective-permute-done((bf16[1,16,1152]{2,1,0:T(8,128)(2,1)S(1)}, bf16[1,16,1152]{2,1,0:T(8,128)(2,1)S(1)}, u32[]{:S(2)}, u32[]{:S(2)}) %collective-permute-start.16) | collective-permute-done | bytes 36896 | tf_op jit(solution)/shard_map/ppermute | solution.py:22
  75.5 1.2 %collective-permute-start.19 = (bf16[4,16,1152]{2,1,0:T(8,128)(2,1)S(1)}, bf16[4,16,1152]{2,1,0:T(8,128)(2,1)S(1)}, u32[]{:S(2)}, u32[]{:S(2)}) collective-permute-start(bf16[4,16,1152]{2,1,0:T(8,128)(2,1)S(1)} %stack.3.refs_0_), channel_id=1, source_target_pairs={{0,6},{1,7},{2,4},{3,5},{4,2},{5,3},{6,0},{7,1},{8,14},{9,15},{10,... | collective-permute-start | bytes 442376 | tf_op jit(solution)/shard_map/ppermute | solution.py:22
  76.8 1.3 %collective-permute-start.18 = (bf16[4,16,1152]{2,1,0:T(8,128)(2,1)S(1)}, bf16[4,16,1152]{2,1,0:T(8,128)(2,1)S(1)}, u32[]{:S(2)}, u32[]{:S(2)}) collective-permute-start(bf16[4,16,1152]{2,1,0:T(8,128)(2,1)S(1)} %stack.3.refs_0_), channel_id=1, source_target_pairs={{0,4},{1,5},{2,6},{3,7},{4,0},{5,1},{6,2},{7,3},{8,12},{9,13},{10,... | collective-permute-start | bytes 442376 | tf_op jit(solution)/shard_map/ppermute | solution.py:22
  78.1 1.0 collective-permute-start.17
  79.1 2.6 %collective-permute-done.19.refs_3_ = bf16[4,16,1152]{2,1,0:T(8,128)(2,1)S(1)} collective-permute-done((bf16[4,16,1152]{2,1,0:T(8,128)(2,1)S(1)}, bf16[4,16,1152]{2,1,0:T(8,128)(2,1)S(1)}, u32[]{:S(2)}, u32[]{:S(2)}) %collective-permute-start.19) | collective-permute-done | bytes 147488 | tf_op jit(solution)/shard_map/ppermute | solution.py:22
  81.7 1.1 collective-permute-done.18.refs_2_
  83.4 2.0 %collective-permute-done.20.other_ref = bf16[8,32,1152]{2,1,0:T(8,128)(2,1)S(1)} collective-permute-done((bf16[8,32,1152]{2,1,0:T(8,128)(2,1)S(1)}, bf16[8,32,1152]{2,1,0:T(8,128)(2,1)S(1)}, u32[]{:S(2)}, u32[]{:S(2)}) %collective-permute-start.20) | collective-permute-done | bytes 589856 | tf_op jit(solution)/shard_map/ppermute | solution.py:22
  85.4 8.6 %grad.1 = (f32[8,32,1024]{2,1,0:T(8,128)S(1)}, bf16[8,32,1024]{2,1,0:T(8,128)(2,1)S(1)}, f32[4,128]{1,0:T(4,128)S(1)}) custom-call(s32[1]{0:T(128)} %bitcast.context_ref, bf16[8,32,1152]{2,1,0:T(8,128)(2,1)S(1)} %near.3.own_ref, bf16[8,32,1152]{2,1,0:T(8,128)(2,1)S(1)} %collective-permute-done.20.other_ref, bf16[768,8192]{1,0:T(8,128)(2,1)S(1)} %copy-done.1, ...), custom_call_target="tpu_custom_call" | custom-call | tf_op jit(solution)/shard_map/grad/pallas_call | solution.py:55
  94.2 1.8 %collective-permute-done.21.refs_1_ = bf16[8,32,1024]{2,1,0:T(8,128)(2,1)S(1)} collective-permute-done((bf16[8,32,1024]{2,1,0:T(8,128)(2,1)S(1)}, bf16[8,32,1024]{2,1,0:T(8,128)(2,1)S(1)}, u32[]{:S(2)}, u32[]{:S(2)}) %collective-permute-start.21) | collective-permute-done | bytes 524320 | tf_op jit(solution)/shard_map/ppermute | solution.py:22
  96.1 1.1 collective-permute-start.22
  97.2 0.7 collective-permute-start.23
  97.9 1.8 %collective-permute-start.24 = (bf16[4,16,1024]{2,1,0:T(8,128)(2,1)S(1)}, bf16[4,16,1024]{2,1,0:T(8,128)(2,1)S(1)}, u32[]{:S(2)}, u32[]{:S(2)}) collective-permute-start(bf16[4,16,1024]{2,1,0:T(8,128)(2,1)S(1)} %get-tuple-element.59), channel_id=1, source_target_pairs={{0,6},{1,7},{2,4},{3,5},{4,2},{5,3},{6,0},{7,1},{8,14},{9,15},{10,... | collective-permute-start | bytes 393224 | tf_op jit(solution)/shard_map/ppermute | solution.py:22
  99.6 2.1 %collective-permute-done.22.refs_1_ = bf16[4,16,1024]{2,1,0:T(8,128)(2,1)S(1)} collective-permute-done((bf16[4,16,1024]{2,1,0:T(8,128)(2,1)S(1)}, bf16[4,16,1024]{2,1,0:T(8,128)(2,1)S(1)}, u32[]{:S(2)}, u32[]{:S(2)}) %collective-permute-start.22) | collective-permute-done | bytes 131104 | tf_op jit(solution)/shard_map/ppermute | solution.py:22
  101.7 1.9 %collective-permute-done.23.refs_2_ = bf16[4,16,1024]{2,1,0:T(8,128)(2,1)S(1)} collective-permute-done((bf16[4,16,1024]{2,1,0:T(8,128)(2,1)S(1)}, bf16[4,16,1024]{2,1,0:T(8,128)(2,1)S(1)}, u32[]{:S(2)}, u32[]{:S(2)}) %collective-permute-start.23) | collective-permute-done | bytes 131104 | tf_op jit(solution)/shard_map/ppermute | solution.py:22
  103.5 2.1 %collective-permute-done.24.refs_3_ = bf16[4,16,1024]{2,1,0:T(8,128)(2,1)S(1)} collective-permute-done((bf16[4,16,1024]{2,1,0:T(8,128)(2,1)S(1)}, bf16[4,16,1024]{2,1,0:T(8,128)(2,1)S(1)}, u32[]{:S(2)}, u32[]{:S(2)}) %collective-permute-start.24) | collective-permute-done | bytes 131104 | tf_op jit(solution)/shard_map/ppermute | solution.py:22
  105.7 2.1 %collective-permute-start.25 = (bf16[1,16,1024]{2,1,0:T(8,128)(2,1)S(1)}, bf16[1,16,1024]{2,1,0:T(8,128)(2,1)S(1)}, u32[]{:S(2)}, u32[]{:S(2)}) collective-permute-start(bf16[1,16,1024]{2,1,0:T(8,128)(2,1)S(1)} %get-tuple-element.61), channel_id=1, source_target_pairs={{0,8},{1,9},{2,10},{3,11},{4,12},{5,13},{6,14},{7,15},{8,0},{9,1},... | collective-permute-start | bytes 98312 | tf_op jit(solution)/shard_map/ppermute | solution.py:22
  107.8 0.9 collective-permute-start.26
  108.7 1.5 %collective-permute-start.27 = (bf16[1,16,1024]{2,1,0:T(8,128)(2,1)S(1)}, bf16[1,16,1024]{2,1,0:T(8,128)(2,1)S(1)}, u32[]{:S(2)}, u32[]{:S(2)}) collective-permute-start(bf16[1,16,1024]{2,1,0:T(8,128)(2,1)S(1)} %get-tuple-element.63), channel_id=1, source_target_pairs={{0,24},{1,25},{2,26},{3,27},{4,28},{5,29},{6,30},{7,31},{8,16},{9,... | collective-permute-start | bytes 98312 | tf_op jit(solution)/shard_map/ppermute | solution.py:22
  110.3 3.0 %head_weight_grad.1 = f32[1024,1024]{1,0:T(8,128)} custom-call(f32[16,1024]{1,0:T(8,128)S(1)} %get-tuple-element.64.normed_ref, f32[1,1024]{1,0:T(1,128)S(1)} %copy-done.7), custom_call_target="tpu_custom_call" | custom-call | flops 100663296 | bytes 4194304 | tf_op jit(solution)/shard_map/head_weight_grad/pallas_call | solution.py:323
  113.7 0.7 collective-permute-done.27.refs_3_
  114.4 0.6 far_sum.1
  (40 shorter events, 5.1 us)
Async XLA Ops:
  0.6 7.2 %collective-permute-start.2 = (bf16[1,16,1024]{2,1,0:T(8,128)(2,1)}, bf16[1,16,1024]{2,1,0:T(8,128)(2,1)S(1)}, u32[]{:S(2)}, u32[]{:S(2)}) collective-permute-start(bf16[1,16,1024]{2,1,0:T(8,128)(2,1)} %bitcast.13), channel_id=1, source_target_pairs={{0,24},{1,25},{2,26},{3,27},{4,28},{5,29},{6,30},{7,31},{8,16},{9,... | collective-permute-start | bytes 98312 | tf_op jit(solution)/shard_map/ppermute | solution.py:22
  5.7 5.0 %collective-permute-start.1 = (bf16[1,16,1024]{2,1,0:T(8,128)(2,1)}, bf16[1,16,1024]{2,1,0:T(8,128)(2,1)S(1)}, u32[]{:S(2)}, u32[]{:S(2)}) collective-permute-start(bf16[1,16,1024]{2,1,0:T(8,128)(2,1)} %bitcast.14), channel_id=1, source_target_pairs={{0,16},{1,17},{2,18},{3,19},{4,20},{5,21},{6,22},{7,23},{8,24},{9,... | collective-permute-start | bytes 98312 | tf_op jit(solution)/shard_map/ppermute | solution.py:22
  5.7 5.0 %collective-permute-start = (bf16[1,16,1024]{2,1,0:T(8,128)(2,1)}, bf16[1,16,1024]{2,1,0:T(8,128)(2,1)S(1)}, u32[]{:S(2)}, u32[]{:S(2)}) collective-permute-start(bf16[1,16,1024]{2,1,0:T(8,128)(2,1)} %bitcast.15), channel_id=1, source_target_pairs={{0,8},{1,9},{2,10},{3,11},{4,12},{5,13},{6,14},{7,15},{8,0},{9,1},... | collective-permute-start | bytes 98312 | tf_op jit(solution)/shard_map/ppermute | solution.py:22
  10.8 0.8 copy-start.3
  11.5 6.3 %collective-permute-start.5 = (bf16[4,16,1024]{2,1,0:T(8,128)(2,1)S(1)}, bf16[4,16,1024]{2,1,0:T(8,128)(2,1)S(1)}, u32[]{:S(2)}, u32[]{:S(2)}) collective-permute-start(bf16[4,16,1024]{2,1,0:T(8,128)(2,1)S(1)} %stack.2.refs_0_), channel_id=1, source_target_pairs={{0,6},{1,7},{2,4},{3,5},{4,2},{5,3},{6,0},{7,1},{8,14},{9,15},{10,... | collective-permute-start | bytes 393224 | tf_op jit(solution)/shard_map/ppermute | solution.py:22
  14.1 5.1 %collective-permute-start.4 = (bf16[4,16,1024]{2,1,0:T(8,128)(2,1)S(1)}, bf16[4,16,1024]{2,1,0:T(8,128)(2,1)S(1)}, u32[]{:S(2)}, u32[]{:S(2)}) collective-permute-start(bf16[4,16,1024]{2,1,0:T(8,128)(2,1)S(1)} %stack.2.refs_0_), channel_id=1, source_target_pairs={{0,4},{1,5},{2,6},{3,7},{4,0},{5,1},{6,2},{7,3},{8,12},{9,13},{10,... | collective-permute-start | bytes 393224 | tf_op jit(solution)/shard_map/ppermute | solution.py:22
  14.6 5.0 %collective-permute-start.3 = (bf16[4,16,1024]{2,1,0:T(8,128)(2,1)S(1)}, bf16[4,16,1024]{2,1,0:T(8,128)(2,1)S(1)}, u32[]{:S(2)}, u32[]{:S(2)}) collective-permute-start(bf16[4,16,1024]{2,1,0:T(8,128)(2,1)S(1)} %stack.2.refs_0_), channel_id=1, source_target_pairs={{0,2},{1,3},{2,0},{3,1},{4,6},{5,7},{6,4},{7,5},{8,10},{9,11},{10,... | collective-permute-start | bytes 393224 | tf_op jit(solution)/shard_map/ppermute | solution.py:22
  19.6 2.0 %collective-permute-start.6 = (bf16[8,32,1024]{2,1,0:T(8,128)(2,1)S(1)}, bf16[8,32,1024]{2,1,0:T(8,128)(2,1)S(1)}, u32[]{:S(2)}, u32[]{:S(2)}) collective-permute-start(bf16[8,32,1024]{2,1,0:T(8,128)(2,1)S(1)} %near.2.own_ref), channel_id=1, source_target_pairs={{0,1},{1,0},{2,3},{3,2},{4,5},{5,4},{6,7},{7,6},{8,9},{9,8},{10,11... | collective-permute-start | bytes 1572872 | tf_op jit(solution)/shard_map/ppermute | solution.py:22
  21.6 4.6 %copy-start = (bf16[768,8192]{1,0:T(8,128)(2,1)S(1)}, bf16[768,8192]{1,0:T(8,128)(2,1)}, u32[]{:S(2)}) copy-start(bf16[768,8192]{1,0:T(8,128)(2,1)} %tokens_ref.3) | copy-start | bytes 37748740
  26.2 29.9 %copy-start.2 = (bf16[1024,1024]{1,0:T(8,128)(2,1)S(1)}, bf16[1024,1024]{1,0:T(8,128)(2,1)}, u32[]{:S(2)}) copy-start(bf16[1024,1024]{1,0:T(8,128)(2,1)} %weight_ref.1) | copy-start | bytes 6291460
  26.2 29.9 %copy-start.4 = (f32[1024]{0:T(1024)S(1)}, f32[1024]{0:T(1024)}, u32[]{:S(2)}) copy-start(f32[1024]{0:T(1024)} %param.10) | copy-start | bytes 12292
  26.2 59.2 %copy-start.1 = (bf16[768,8192]{1,0:T(8,128)(2,1)S(1)}, bf16[768,8192]{1,0:T(8,128)(2,1)}, u32[]{:S(2)}) copy-start(bf16[768,8192]{1,0:T(8,128)(2,1)} %tokens_ref.3) | copy-start | bytes 37748740
  35.0 33.0 %copy-start.5 = (f32[1024]{0:T(1024)S(1)}, f32[1024]{0:T(1024)}, u32[]{:S(2)}) copy-start(f32[1024]{0:T(1024)} %param.12) | copy-start | bytes 12292
  35.0 33.0 %copy-start.6 = (s32[1024]{0:T(1024)S(1)}, s32[1024]{0:T(1024)}, u32[]{:S(2)}) copy-start(s32[1024]{0:T(1024)} %param.13) | copy-start | bytes 12292
  35.0 2.1 %collective-permute-start.7 = (bf16[8,32,1152]{2,1,0:T(8,128)(2,1)S(1)}, bf16[8,32,1152]{2,1,0:T(8,128)(2,1)S(1)}, u32[]{:S(2)}, u32[]{:S(2)}) collective-permute-start(bf16[8,32,1152]{2,1,0:T(8,128)(2,1)S(1)} %get-tuple-element.36), channel_id=1, source_target_pairs={{0,1},{1,0},{2,3},{3,2},{4,5},{5,4},{6,7},{7,6},{8,9},{9,8},{10,11... | collective-permute-start | bytes 1769480 | tf_op jit(solution)/shard_map/ppermute | solution.py:22
  37.5 6.0 %collective-permute-start.8 = (bf16[4,16,1152]{2,1,0:T(8,128)(2,1)S(1)}, bf16[4,16,1152]{2,1,0:T(8,128)(2,1)S(1)}, u32[]{:S(2)}, u32[]{:S(2)}) collective-permute-start(bf16[4,16,1152]{2,1,0:T(8,128)(2,1)S(1)} %get-tuple-element.39), channel_id=1, source_target_pairs={{0,2},{1,3},{2,0},{3,1},{4,6},{5,7},{6,4},{7,5},{8,10},{9,11},{10,... | collective-permute-start | bytes 442376 | tf_op jit(solution)/shard_map/ppermute | solution.py:22
  38.7 6.7 %collective-permute-start.9 = (bf16[4,16,1152]{2,1,0:T(8,128)(2,1)S(1)}, bf16[4,16,1152]{2,1,0:T(8,128)(2,1)S(1)}, u32[]{:S(2)}, u32[]{:S(2)}) collective-permute-start(bf16[4,16,1152]{2,1,0:T(8,128)(2,1)S(1)} %get-tuple-element.40), channel_id=1, source_target_pairs={{0,4},{1,5},{2,6},{3,7},{4,0},{5,1},{6,2},{7,3},{8,12},{9,13},{10,... | collective-permute-start | bytes 442376 | tf_op jit(solution)/shard_map/ppermute | solution.py:22
  40.2 7.7 %collective-permute-start.10 = (bf16[4,16,1152]{2,1,0:T(8,128)(2,1)S(1)}, bf16[4,16,1152]{2,1,0:T(8,128)(2,1)S(1)}, u32[]{:S(2)}, u32[]{:S(2)}) collective-permute-start(bf16[4,16,1152]{2,1,0:T(8,128)(2,1)S(1)} %get-tuple-element.41), channel_id=1, source_target_pairs={{0,6},{1,7},{2,4},{3,5},{4,2},{5,3},{6,0},{7,1},{8,14},{9,15},{10,... | collective-permute-start | bytes 442376 | tf_op jit(solution)/shard_map/ppermute | solution.py:22
  48.2 4.5 %collective-permute-start.11 = (bf16[1,16,1152]{2,1,0:T(8,128)(2,1)S(1)}, bf16[1,16,1152]{2,1,0:T(8,128)(2,1)S(1)}, u32[]{:S(2)}, u32[]{:S(2)}) collective-permute-start(bf16[1,16,1152]{2,1,0:T(8,128)(2,1)S(1)} %get-tuple-element.44), channel_id=1, source_target_pairs={{0,8},{1,9},{2,10},{3,11},{4,12},{5,13},{6,14},{7,15},{8,0},{9,1},... | collective-permute-start | bytes 110600 | tf_op jit(solution)/shard_map/ppermute | solution.py:22
  48.2 5.4 %collective-permute-start.12 = (bf16[1,16,1152]{2,1,0:T(8,128)(2,1)S(1)}, bf16[1,16,1152]{2,1,0:T(8,128)(2,1)S(1)}, u32[]{:S(2)}, u32[]{:S(2)}) collective-permute-start(bf16[1,16,1152]{2,1,0:T(8,128)(2,1)S(1)} %get-tuple-element.45), channel_id=1, source_target_pairs={{0,16},{1,17},{2,18},{3,19},{4,20},{5,21},{6,22},{7,23},{8,24},{9,... | collective-permute-start | bytes 110600 | tf_op jit(solution)/shard_map/ppermute | solution.py:22
  50.3 5.8 %collective-permute-start.13 = (bf16[1,16,1152]{2,1,0:T(8,128)(2,1)S(1)}, bf16[1,16,1152]{2,1,0:T(8,128)(2,1)S(1)}, u32[]{:S(2)}, u32[]{:S(2)}) collective-permute-start(bf16[1,16,1152]{2,1,0:T(8,128)(2,1)S(1)} %get-tuple-element.46), channel_id=1, source_target_pairs={{0,24},{1,25},{2,26},{3,27},{4,28},{5,29},{6,30},{7,31},{8,16},{9,... | collective-permute-start | bytes 110600 | tf_op jit(solution)/shard_map/ppermute | solution.py:22
  69.2 5.8 %collective-permute-start.16 = (bf16[1,16,1152]{2,1,0:T(8,128)(2,1)S(1)}, bf16[1,16,1152]{2,1,0:T(8,128)(2,1)S(1)}, u32[]{:S(2)}, u32[]{:S(2)}) collective-permute-start(bf16[1,16,1152]{2,1,0:T(8,128)(2,1)S(1)} %bitcast.9), channel_id=1, source_target_pairs={{0,24},{1,25},{2,26},{3,27},{4,28},{5,29},{6,30},{7,31},{8,16},{9,... | collective-permute-start | bytes 110600 | tf_op jit(solution)/shard_map/ppermute | solution.py:22
  69.7 5.3 %collective-permute-start.15 = (bf16[1,16,1152]{2,1,0:T(8,128)(2,1)S(1)}, bf16[1,16,1152]{2,1,0:T(8,128)(2,1)S(1)}, u32[]{:S(2)}, u32[]{:S(2)}) collective-permute-start(bf16[1,16,1152]{2,1,0:T(8,128)(2,1)S(1)} %bitcast.10), channel_id=1, source_target_pairs={{0,16},{1,17},{2,18},{3,19},{4,20},{5,21},{6,22},{7,23},{8,24},{9,... | collective-permute-start | bytes 110600 | tf_op jit(solution)/shard_map/ppermute | solution.py:22
  70.8 4.8 %collective-permute-start.14 = (bf16[1,16,1152]{2,1,0:T(8,128)(2,1)S(1)}, bf16[1,16,1152]{2,1,0:T(8,128)(2,1)S(1)}, u32[]{:S(2)}, u32[]{:S(2)}) collective-permute-start(bf16[1,16,1152]{2,1,0:T(8,128)(2,1)S(1)} %bitcast.11), channel_id=1, source_target_pairs={{0,8},{1,9},{2,10},{3,11},{4,12},{5,13},{6,14},{7,15},{8,0},{9,1},... | collective-permute-start | bytes 110600 | tf_op jit(solution)/shard_map/ppermute | solution.py:22
  75.5 6.1 %collective-permute-start.19 = (bf16[4,16,1152]{2,1,0:T(8,128)(2,1)S(1)}, bf16[4,16,1152]{2,1,0:T(8,128)(2,1)S(1)}, u32[]{:S(2)}, u32[]{:S(2)}) collective-permute-start(bf16[4,16,1152]{2,1,0:T(8,128)(2,1)S(1)} %stack.3.refs_0_), channel_id=1, source_target_pairs={{0,6},{1,7},{2,4},{3,5},{4,2},{5,3},{6,0},{7,1},{8,14},{9,15},{10,... | collective-permute-start | bytes 442376 | tf_op jit(solution)/shard_map/ppermute | solution.py:22
  76.8 6.0 %collective-permute-start.18 = (bf16[4,16,1152]{2,1,0:T(8,128)(2,1)S(1)}, bf16[4,16,1152]{2,1,0:T(8,128)(2,1)S(1)}, u32[]{:S(2)}, u32[]{:S(2)}) collective-permute-start(bf16[4,16,1152]{2,1,0:T(8,128)(2,1)S(1)} %stack.3.refs_0_), channel_id=1, source_target_pairs={{0,4},{1,5},{2,6},{3,7},{4,0},{5,1},{6,2},{7,3},{8,12},{9,13},{10,... | collective-permute-start | bytes 442376 | tf_op jit(solution)/shard_map/ppermute | solution.py:22
  78.1 5.2 %collective-permute-start.17 = (bf16[4,16,1152]{2,1,0:T(8,128)(2,1)S(1)}, bf16[4,16,1152]{2,1,0:T(8,128)(2,1)S(1)}, u32[]{:S(2)}, u32[]{:S(2)}) collective-permute-start(bf16[4,16,1152]{2,1,0:T(8,128)(2,1)S(1)} %stack.3.refs_0_), channel_id=1, source_target_pairs={{0,2},{1,3},{2,0},{3,1},{4,6},{5,7},{6,4},{7,5},{8,10},{9,11},{10,... | collective-permute-start | bytes 442376 | tf_op jit(solution)/shard_map/ppermute | solution.py:22
  83.3 2.1 %collective-permute-start.20 = (bf16[8,32,1152]{2,1,0:T(8,128)(2,1)S(1)}, bf16[8,32,1152]{2,1,0:T(8,128)(2,1)S(1)}, u32[]{:S(2)}, u32[]{:S(2)}) collective-permute-start(bf16[8,32,1152]{2,1,0:T(8,128)(2,1)S(1)} %near.3.own_ref), channel_id=1, source_target_pairs={{0,1},{1,0},{2,3},{3,2},{4,5},{5,4},{6,7},{7,6},{8,9},{9,8},{10,11... | collective-permute-start | bytes 1769480 | tf_op jit(solution)/shard_map/ppermute | solution.py:22
  85.4 24.9 %copy-start.7 = (f32[1,1024]{1,0:T(1,128)S(1)}, f32[1,1024]{1,0:T(1,128)}, u32[]{:S(2)}) copy-start(f32[1,1024]{1,0:T(1,128)} %get-tuple-element.65.bias_grad_ref) | copy-start | bytes 12292
  94.0 2.0 %collective-permute-start.21 = (bf16[8,32,1024]{2,1,0:T(8,128)(2,1)S(1)}, bf16[8,32,1024]{2,1,0:T(8,128)(2,1)S(1)}, u32[]{:S(2)}, u32[]{:S(2)}) collective-permute-start(bf16[8,32,1024]{2,1,0:T(8,128)(2,1)S(1)} %get-tuple-element.55), channel_id=1, source_target_pairs={{0,1},{1,0},{2,3},{3,2},{4,5},{5,4},{6,7},{7,6},{8,9},{9,8},{10,11... | collective-permute-start | bytes 1572872 | tf_op jit(solution)/shard_map/ppermute | solution.py:22
  96.1 5.6 %collective-permute-start.22 = (bf16[4,16,1024]{2,1,0:T(8,128)(2,1)S(1)}, bf16[4,16,1024]{2,1,0:T(8,128)(2,1)S(1)}, u32[]{:S(2)}, u32[]{:S(2)}) collective-permute-start(bf16[4,16,1024]{2,1,0:T(8,128)(2,1)S(1)} %get-tuple-element.57), channel_id=1, source_target_pairs={{0,2},{1,3},{2,0},{3,1},{4,6},{5,7},{6,4},{7,5},{8,10},{9,11},{10,... | collective-permute-start | bytes 393224 | tf_op jit(solution)/shard_map/ppermute | solution.py:22
  97.2 6.4 %collective-permute-start.23 = (bf16[4,16,1024]{2,1,0:T(8,128)(2,1)S(1)}, bf16[4,16,1024]{2,1,0:T(8,128)(2,1)S(1)}, u32[]{:S(2)}, u32[]{:S(2)}) collective-permute-start(bf16[4,16,1024]{2,1,0:T(8,128)(2,1)S(1)} %get-tuple-element.58), channel_id=1, source_target_pairs={{0,4},{1,5},{2,6},{3,7},{4,0},{5,1},{6,2},{7,3},{8,12},{9,13},{10,... | collective-permute-start | bytes 393224 | tf_op jit(solution)/shard_map/ppermute | solution.py:22
  97.9 7.8 %collective-permute-start.24 = (bf16[4,16,1024]{2,1,0:T(8,128)(2,1)S(1)}, bf16[4,16,1024]{2,1,0:T(8,128)(2,1)S(1)}, u32[]{:S(2)}, u32[]{:S(2)}) collective-permute-start(bf16[4,16,1024]{2,1,0:T(8,128)(2,1)S(1)} %get-tuple-element.59), channel_id=1, source_target_pairs={{0,6},{1,7},{2,4},{3,5},{4,2},{5,3},{6,0},{7,1},{8,14},{9,15},{10,... | collective-permute-start | bytes 393224 | tf_op jit(solution)/shard_map/ppermute | solution.py:22
  105.7 8.0 %collective-permute-start.25 = (bf16[1,16,1024]{2,1,0:T(8,128)(2,1)S(1)}, bf16[1,16,1024]{2,1,0:T(8,128)(2,1)S(1)}, u32[]{:S(2)}, u32[]{:S(2)}) collective-permute-start(bf16[1,16,1024]{2,1,0:T(8,128)(2,1)S(1)} %get-tuple-element.61), channel_id=1, source_target_pairs={{0,8},{1,9},{2,10},{3,11},{4,12},{5,13},{6,14},{7,15},{8,0},{9,1},... | collective-permute-start | bytes 98312 | tf_op jit(solution)/shard_map/ppermute | solution.py:22
  107.8 5.9 %collective-permute-start.26 = (bf16[1,16,1024]{2,1,0:T(8,128)(2,1)S(1)}, bf16[1,16,1024]{2,1,0:T(8,128)(2,1)S(1)}, u32[]{:S(2)}, u32[]{:S(2)}) collective-permute-start(bf16[1,16,1024]{2,1,0:T(8,128)(2,1)S(1)} %get-tuple-element.62), channel_id=1, source_target_pairs={{0,16},{1,17},{2,18},{3,19},{4,20},{5,21},{6,22},{7,23},{8,24},{9,... | collective-permute-start | bytes 98312 | tf_op jit(solution)/shard_map/ppermute | solution.py:22
  108.7 5.7 %collective-permute-start.27 = (bf16[1,16,1024]{2,1,0:T(8,128)(2,1)S(1)}, bf16[1,16,1024]{2,1,0:T(8,128)(2,1)S(1)}, u32[]{:S(2)}, u32[]{:S(2)}) collective-permute-start(bf16[1,16,1024]{2,1,0:T(8,128)(2,1)S(1)} %get-tuple-element.63), channel_id=1, source_target_pairs={{0,24},{1,25},{2,26},{3,27},{4,28},{5,29},{6,30},{7,31},{8,16},{9,... | collective-permute-start | bytes 98312 | tf_op jit(solution)/shard_map/ppermute | solution.py:22

commit v3 on v2

--- a/solution.py
+++ b/solution.py
@@ -34,10 +34,10 @@
     return [i ^ (2 * j) for i in range(2) for j in range(contexts // 2)]
 
 
-def call(kernel, outs, name, args, scratch=(), any_args=(), smem_args=(), limit=16, cost=None):
+def call(kernel, outs, name, args, scratch=(), hbm_args=(), smem_args=(), limit=16, cost=None):
     def spec(i):
-        if i in any_args:
-            return pl.BlockSpec(memory_space=pl.ANY)
+        if i in hbm_args:
+            return pl.BlockSpec(memory_space=pltpu.HBM)
         if i in smem_args:
             return pl.BlockSpec(memory_space=pltpu.SMEM)
         return pl.BlockSpec(memory_space=pltpu.VMEM)
@@ -55,26 +55,14 @@
     return list(run(*args))
 
 
-def stack_kernel(axis, *refs):
-    out_ref, at = refs[-1], 0
-    for ref in refs[:-1]:
-        size = ref.shape[axis]
-        if axis == 0:
-            out_ref[at : at + size] = ref[...]
-        else:
-            out_ref[:, at : at + size] = ref[...]
-        at += size
-
-
-def stack(parts, axis):
-    shape = list(parts[0].shape)
-    shape[axis] = sum(p.shape[axis] for p in parts)
-    (out,) = call(functools.partial(stack_kernel, axis), [(tuple(shape), parts[0].dtype)], "stack", parts)
-    return out
-
-
-def near_kernel(*refs):
-    out_ref, parts = refs[-1], refs[:-1]
+def stack_kernel(*refs):
+    out_ref = refs[-1]
+    for at, ref in enumerate(refs[:-1]):
+        out_ref[at] = ref[...].reshape(out_ref.shape[1:])
+
+
+def near_kernel(count, *refs):
+    out_ref, parts = refs[-1], refs[:count]
     blocks, rows, _ = parts[0].shape
     across = len(parts) // 2
     for i in range(2):
@@ -82,12 +70,15 @@
             out_ref[i * blocks : (i + 1) * blocks, k * rows : (k + 1) * rows] = parts[i * across + k][...]
 
 
-def gather(block):
-    block = block[None]
-    held = stack([block] + [swap(block, *step) for step in far_steps()], 0)
+def gather(block, local=None, after=()):
+    far = [swap(block, *step) for step in far_steps()]
+    rows, width = block.shape
+    (held,) = call(
+        stack_kernel, [((len(far) + 1, rows, width), block.dtype)], "stack", [block if local is None else local, *far]
+    )
     parts = [held] + [swap(held, *step) for step in near_steps()]
-    blocks, rows, width = held.shape
-    (held,) = call(near_kernel, [((2 * blocks, len(parts) // 2 * rows, width), held.dtype)], "near", parts)
+    shape = (2 * held.shape[0], len(parts) // 2 * rows, width)
+    (held,) = call(functools.partial(near_kernel, len(parts)), [(shape, held.dtype)], "near", [*parts, *after])
     return held, swap(held, 0, 1)
 
 
@@ -111,6 +102,10 @@
     at = width + 3 * i
     block = block.astype(F32)
     return block[:, at : at + 1] + (block[:, at + 1 : at + 2] + block[:, at + 2 : at + 3])
+
+
+def first_kernel(tokens_ref, queries_ref, out_ref):
+    out_ref[...] = queries_ref[...]
 
 
 def columns_of(context_ref, contexts, p, width):
@@ -150,14 +145,14 @@
     spread(context_ref, weights.astype(BF16), tokens_ref, keep_ref, send_ref, into_lanes([peak[half:]], half))
 
 
-def grad_kernel(scale, context_ref, own_ref, other_ref, tokens_ref, w_ref, peak_ref, keep_ref, send_ref, loss_ref):
+def grad_kernel(scale, classes, context_ref, own_ref, other_ref, tokens_ref, w_ref, peak_ref, keep_ref, send_ref, loss_ref):
     width = keep_ref.shape[2]
     projected = project(context_ref, own_ref, other_ref, tokens_ref, width)
     own, other = own_ref[0], other_ref[0]
     top = jnp.concatenate([from_lanes(own, width, 0), from_lanes(other, width, 0)], axis=0)
     weights = w_ref[...] * jnp.exp(peak_ref[:, :1] - top)
     spread(context_ref, (weights * projected).astype(BF16), tokens_ref, keep_ref, send_ref, None)
-    rows = loss_ref.shape[0] // 2
+    rows = classes // 2
     each = own.shape[0] // rows
     sums = []
     for block in (own, other):
@@ -166,7 +161,7 @@
         while len(level) > 1:
             level = [a + b for a, b in zip(level[::2], level[1::2])]
         sums.append(level[0])
-    loss_ref[...] = jnp.broadcast_to((sums[0] + sums[1]) * scale, loss_ref.shape)
+    loss_ref[...] = (sums[0] + sums[1]) * scale
 
 
 def total_of(keep, peak, received, width):
@@ -268,20 +263,24 @@
     squares = jnp.sum(pooled * pooled, axis=1, keepdims=True)
     product_flat = jnp.sum(jnp.where(mask, product, 0.0), axis=0, keepdims=True)
     squares_flat = jnp.sum(jnp.where(mask, squares, 0.0), axis=0, keepdims=True)
-    for p in range(sums_ref.shape[0]):
-        sums_ref[p, 0:1, :] = product_flat
-        sums_ref[p, 1:2, :] = squares_flat
+    sums_ref[0:1, :] = product_flat
+    sums_ref[1:2, :] = squares_flat
+
+
+def tree_sum_kernel(*refs):
+    level = [ref[...] for ref in refs[:-1]]
+    while len(level) > 1:
+        level = [a + b for a, b in zip(level[::2], level[1::2])]
+    refs[-1][...] = level[0]
 
 
 def head_grads_kernel(
-    full_width, sums_ref, pooled_ref, top_ref, gain_ref, weight_ref, bias_ref, label_ref, bias_grad_ref, grad_ref, normed_ref
+    full_width, sums_ref, other_sums_ref, pooled_ref, top_ref, gain_ref, weight_ref, bias_ref, label_ref, bias_grad_ref, grad_ref, normed_ref
 ):
     pooled, gain = pooled_ref[...], gain_ref[...]
     heads, width = pooled.shape
-    columns = sums_ref.shape[2]
-    sums = sums_ref[0]
-    for p in range(1, sums_ref.shape[0]):
-        sums = sums + sums_ref[p]
+    columns = sums_ref.shape[1]
+    sums = sums_ref[...] + other_sums_ref[...]
     mask = head_mask((heads, columns), columns // heads)
     inverse_flat = lax.rsqrt(sums[1:2] / full_width + 1e-05)
     inverse_rms = jnp.max(jnp.where(mask, inverse_flat, 0.0), axis=1, keepdims=True)
@@ -305,7 +304,7 @@
     normed_ref[...] = unit * gain
 
 
-def head_weight_grad_kernel(attributes, normed_ref, bias_grad_ref, out_ref):
+def head_weight_grad_kernel(attributes, normed_ref, bias_grad_ref, out_ref, done_ref):
     heads = normed_ref.shape[0]
     columns = out_ref.shape[1]
     parts = jnp.concatenate(pieces(normed_ref[...]), axis=0)
@@ -314,6 +313,7 @@
     ones = jnp.where(column // attributes == row, 1.0, 0.0).astype(BF16)
     normed = lax.dot_general(parts, ones, (((0,), (0,)), ((), ())), preferred_element_type=F32)
     out_ref[...] = normed * bias_grad_ref[...]
+    done_ref[...] = jnp.zeros_like(done_ref)
 
 
 def head_weight_grad(normed, bias_grad):
@@ -322,13 +322,13 @@
     block = columns // 4
     return pl.pallas_call(
         functools.partial(head_weight_grad_kernel, columns // rows),
-        out_shape=jax.ShapeDtypeStruct((width, columns), F32),
+        out_shape=[jax.ShapeDtypeStruct((width, columns), F32), jax.ShapeDtypeStruct((8, LANES), F32)],
         grid=(columns // block,),
         in_specs=[
             pl.BlockSpec((rows, width), lambda i: (0, 0)),
             pl.BlockSpec((1, block), lambda i: (0, i)),
         ],
-        out_specs=pl.BlockSpec((width, block), lambda i: (0, i)),
+        out_specs=[pl.BlockSpec((width, block), lambda i: (0, i)), pl.BlockSpec((8, LANES), lambda i: (0, 0))],
         compiler_params=pltpu.CompilerParams(vmem_limit_bytes=16 * MIB),
         cost_estimate=pl.CostEstimate(flops=6 * rows * width * columns, bytes_accessed=4 * width * columns, transcendentals=0),
         name="head_weight_grad",
@@ -348,7 +348,15 @@
     valid_count = jnp.clip(doc_length - offset, 0, token_count)
 
     context = context_index.astype(jnp.int32)[None]
-    own, other = gather(queries)
+    (queries_here,) = call(
+        first_kernel,
+        [(queries.shape, BF16)],
+        "first",
+        [tokens, queries],
+        limit=32,
+        cost=pl.CostEstimate(flops=0, bytes_accessed=2 * token_count * full_width, transcendentals=0),
+    )
+    own, other = gather(queries, queries_here)
     keep, send, own_peak, weights = call(
         pool_kernel,
         [
@@ -366,29 +374,30 @@
     gain = norm_gain[None, :]
     sums, pooled, top = call(
         head_sums_kernel,
-        [((contexts, 2, columns), F32), ((rows, width), F32), ((rows, LANES), F32)],
+        [((2, columns), F32), ((rows, width), F32), ((rows, LANES), F32)],
         "head_sums",
         [*parts, gain, head_weight],
     )
-    sums = lax.all_to_all(sums, "ctx", 0, 0)
+    far_sums = [swap(sums, *step) for step in far_steps()]
+    (sums,) = call(tree_sum_kernel, [((2, columns), F32)], "tree_sum", [sums, *far_sums])
     bias_grad, pooled_grad, normed = call(
         functools.partial(head_grads_kernel, full_width),
         [((1, columns), F32), ((rows, width + LANES), BF16), ((rows, width), F32)],
         "head_grads",
-        [sums, pooled, top, gain, head_weight, head_bias[None, :], labels[None, :]],
-    )
-    head_grad = head_weight_grad(normed, bias_grad)
-    own, other = gather(pooled_grad)
+        [sums, swap(sums, 1, 0), pooled, top, gain, head_weight, head_bias[None, :], labels[None, :]],
+    )
+    head_grad, done = head_weight_grad(normed, bias_grad)
+    own, other = gather(pooled_grad, after=(done,))
     keep, send, loss = call(
-        functools.partial(grad_kernel, 1.0 / (columns * classes)),
-        [((contexts, half, width), F32), ((contexts, half, width), BF16), ((classes, LANES), F32)],
+        functools.partial(grad_kernel, 1.0 / (columns * classes), classes),
+        [((contexts, half, width), F32), ((contexts, half, width), BF16), ((1, 1), F32)],
         "grad",
         [context, own, other, tokens, weights, own_peak],
         smem_args=(0,),
         limit=32,
     )
     (query_grad,) = call(far_sum_kernel, [((rows, width), F32)], "far_sum", scatter_sum(keep, send, None))
-    return (loss[0, 0], query_grad, head_grad, bias_grad.reshape(-1))
+    return (loss.reshape(()), query_grad, head_grad, bias_grad.reshape(-1))
 
 
 def solution(mesh):

time: 115 us -> 116 us (level)
  blocking collectives: 11.3 us -> 0 us
  starting transfers between devices: 33.9 us -> 39.7 us
  local copies, waits for them, and re-layouts: 5.87 us -> 10.6 us
  waiting for transfers between devices: 38.7 us -> 40.5 us
    all_to_all x1 -> x0, blocking collectives: 11.3 us -> none  [shards(): sums = lax.all_to_all(sums, 'ctx', 0, 0)]
    ppermute x28 -> x32, starting transfers between devices: 33.9 us -> 39.7 us  [swap(): return lax.ppermute(x, ('ctx', 'cls'), pairs)]
    unnamed x16, local copies, waits for them, and re-layouts: 5.36 us -> 10.6 us
    ppermute x28 -> x32, waiting for transfers between devices: 38.7 us -> 40.5 us  [swap(): return lax.ppermute(x, ('ctx', 'cls'), pairs)]
    pallas_call x13 -> x15, Pallas kernels: 20.9 us -> 20.9 us  [call(): return list(run(*args))]
  transfers between devices with their start and end apart: 28 -> 32, of which waited for: 23 -> 26; matrix products, arithmetic and copies ran while one was open for 0% -> 0% of each run, Pallas kernels for 3% -> 3%
where the time goes in v3:
time: 116 us
  waiting for transfers between devices  40.5 us (35%)
  starting transfers between devices  39.7 us (34%)
  Pallas kernels  23.9 us (21%)
  local copies, waits for them, and re-layouts  10.6 us (9%)
  between operations  1.44 us (1%)
    ppermute x32, waiting for transfers between devices, swap(): return lax.ppermute(x, ('ctx', 'cls'), pairs)  40.5 us
    ppermute x32, starting transfers between devices, swap(): return lax.ppermute(x, ('ctx', 'cls'), pairs)  39.7 us
    pallas_call x15, Pallas kernels, call(): return list(run(*args))  20.9 us
    unnamed x16, local copies, waits for them, and re-layouts  10.6 us
    pallas_call x1, Pallas kernels, head_weight_grad(): pl.pallas_call(functools.partial(head_weight_grad_kernel, columns // rows...  2.95 us
  transfers between devices with their start and end apart: 32, of which 26 were waited for; matrix products, arithmetic and copies ran while one was open for 0% of the time, Pallas kernels for 3%

profile of v3, /device:TPU:0, one launch (start us, length us, event | category | flops | bytes accessed | tf_op | source)
XLA Modules:
  0.0 116.1 jit_solution(11030603447864704474)
XLA Ops:
  0.6 3.1 %collective-permute-start = (bf16[16,1024]{1,0:T(8,128)(2,1)}, bf16[16,1024]{1,0:T(8,128)(2,1)S(1)}, u32[]{:S(2)}, u32[]{:S(2)}) collective-permute-start(bf16[16,1024]{1,0:T(8,128)(2,1)} %queries_ref.1), channel_id=1, source_target_pairs={{0,8},{1,9},{2,10},{3,11},{4,12},{5,13},{6,14},{7,15},{8,0},{9,1},... | collective-permute-start | bytes 98312 | tf_op jit(solution)/shard_map/ppermute | solution.py:22
  3.7 2.5 %collective-permute-start.2 = (bf16[16,1024]{1,0:T(8,128)(2,1)}, bf16[16,1024]{1,0:T(8,128)(2,1)S(1)}, u32[]{:S(2)}, u32[]{:S(2)}) collective-permute-start(bf16[16,1024]{1,0:T(8,128)(2,1)} %queries_ref.1), channel_id=1, source_target_pairs={{0,24},{1,25},{2,26},{3,27},{4,28},{5,29},{6,30},{7,31},{8,16},{9,... | collective-permute-start | bytes 98312 | tf_op jit(solution)/shard_map/ppermute | solution.py:22
  6.3 4.6 %copy-done = bf16[768,8192]{1,0:T(8,128)(2,1)S(1)} copy-done((bf16[768,8192]{1,0:T(8,128)(2,1)S(1)}, bf16[768,8192]{1,0:T(8,128)(2,1)}, u32[]{:S(2)}) %copy-start) | copy-done | bytes 12582936
  10.9 0.8 copy-done.3
  11.7 2.5 %collective-permute-start.5 = (bf16[4,16,1024]{2,1,0:T(8,128)(2,1)S(1)}, bf16[4,16,1024]{2,1,0:T(8,128)(2,1)S(1)}, u32[]{:S(2)}, u32[]{:S(2)}) collective-permute-start(bf16[4,16,1024]{2,1,0:T(8,128)(2,1)S(1)} %stack.2.refs_0_), channel_id=1, source_target_pairs={{0,6},{1,7},{2,4},{3,5},{4,2},{5,3},{6,0},{7,1},{8,14},{9,15},{10,... | collective-permute-start | bytes 393224 | tf_op jit(solution)/shard_map/ppermute | solution.py:22
  15.2 3.6 %collective-permute-done.5.refs_3_ = bf16[4,16,1024]{2,1,0:T(8,128)(2,1)S(1)} collective-permute-done((bf16[4,16,1024]{2,1,0:T(8,128)(2,1)S(1)}, bf16[4,16,1024]{2,1,0:T(8,128)(2,1)S(1)}, u32[]{:S(2)}, u32[]{:S(2)}) %collective-permute-start.5) | collective-permute-done | bytes 131104 | tf_op jit(solution)/shard_map/ppermute | solution.py:22
  18.8 1.4 %collective-permute-done.4.refs_2_ = bf16[4,16,1024]{2,1,0:T(8,128)(2,1)S(1)} collective-permute-done((bf16[4,16,1024]{2,1,0:T(8,128)(2,1)S(1)}, bf16[4,16,1024]{2,1,0:T(8,128)(2,1)S(1)}, u32[]{:S(2)}, u32[]{:S(2)}) %collective-permute-start.4) | collective-permute-done | bytes 131104 | tf_op jit(solution)/shard_map/ppermute | solution.py:22
  21.0 1.2 %collective-permute-done.6.other_ref = bf16[8,32,1024]{2,1,0:T(8,128)(2,1)S(1)} collective-permute-done((bf16[8,32,1024]{2,1,0:T(8,128)(2,1)S(1)}, bf16[8,32,1024]{2,1,0:T(8,128)(2,1)S(1)}, u32[]{:S(2)}, u32[]{:S(2)}) %collective-permute-start.6) | collective-permute-done | bytes 524320 | tf_op jit(solution)/shard_map/ppermute | solution.py:22
  22.3 4.6 %copy-done.1 = bf16[768,8192]{1,0:T(8,128)(2,1)S(1)} copy-done((bf16[768,8192]{1,0:T(8,128)(2,1)S(1)}, bf16[768,8192]{1,0:T(8,128)(2,1)}, u32[]{:S(2)}) %copy-start.1) | copy-done | bytes 12582936
  26.9 8.8 %pool.1 = (f32[8,32,1024]{2,1,0:T(8,128)S(1)}, bf16[8,32,1152]{2,1,0:T(8,128)(2,1)S(1)}, f32[64,128]{1,0:T(8,128)S(1)}, f32[64,768]{1,0:T(8,128)S(1)}) custom-call(s32[1]{0:T(128)} %bitcast.context_ref, s32[1]{0:T(128)S(6)} %min.6.count_ref, bf16[8,32,1024]{2,1,0:T(8,128)(2,1)S(1)} %near.2.own_ref, ...), custom_call_target="tpu_custom_call" | custom-call | tf_op jit(solution)/shard_map/pool/pallas_call | solution.py:55
  35.9 1.9 %collective-permute-done.7.refs_1_ = bf16[8,32,1152]{2,1,0:T(8,128)(2,1)S(1)} collective-permute-done((bf16[8,32,1152]{2,1,0:T(8,128)(2,1)S(1)}, bf16[8,32,1152]{2,1,0:T(8,128)(2,1)S(1)}, u32[]{:S(2)}, u32[]{:S(2)}) %collective-permute-start.7) | collective-permute-done | bytes 589856 | tf_op jit(solution)/shard_map/ppermute | solution.py:22
  38.2 1.5 %collective-permute-start.8 = (bf16[4,16,1152]{2,1,0:T(8,128)(2,1)S(1)}, bf16[4,16,1152]{2,1,0:T(8,128)(2,1)S(1)}, u32[]{:S(2)}, u32[]{:S(2)}) collective-permute-start(bf16[4,16,1152]{2,1,0:T(8,128)(2,1)S(1)} %get-tuple-element.41), channel_id=1, source_target_pairs={{0,2},{1,3},{2,0},{3,1},{4,6},{5,7},{6,4},{7,5},{8,10},{9,11},{10,... | collective-permute-start | bytes 442376 | tf_op jit(solution)/shard_map/ppermute | solution.py:22
  39.7 1.5 %collective-permute-start.9 = (bf16[4,16,1152]{2,1,0:T(8,128)(2,1)S(1)}, bf16[4,16,1152]{2,1,0:T(8,128)(2,1)S(1)}, u32[]{:S(2)}, u32[]{:S(2)}) collective-permute-start(bf16[4,16,1152]{2,1,0:T(8,128)(2,1)S(1)} %get-tuple-element.42), channel_id=1, source_target_pairs={{0,4},{1,5},{2,6},{3,7},{4,0},{5,1},{6,2},{7,3},{8,12},{9,13},{10,... | collective-permute-start | bytes 442376 | tf_op jit(solution)/shard_map/ppermute | solution.py:22
  41.8 2.4 %collective-permute-done.8.refs_1_ = bf16[4,16,1152]{2,1,0:T(8,128)(2,1)S(1)} collective-permute-done((bf16[4,16,1152]{2,1,0:T(8,128)(2,1)S(1)}, bf16[4,16,1152]{2,1,0:T(8,128)(2,1)S(1)}, u32[]{:S(2)}, u32[]{:S(2)}) %collective-permute-start.8) | collective-permute-done | bytes 147488 | tf_op jit(solution)/shard_map/ppermute | solution.py:22
  44.2 2.2 %collective-permute-done.9.refs_2_ = bf16[4,16,1152]{2,1,0:T(8,128)(2,1)S(1)} collective-permute-done((bf16[4,16,1152]{2,1,0:T(8,128)(2,1)S(1)}, bf16[4,16,1152]{2,1,0:T(8,128)(2,1)S(1)}, u32[]{:S(2)}, u32[]{:S(2)}) %collective-permute-start.9) | collective-permute-done | bytes 147488 | tf_op jit(solution)/shard_map/ppermute | solution.py:22
  46.4 2.1 %collective-permute-done.10.refs_3_ = bf16[4,16,1152]{2,1,0:T(8,128)(2,1)S(1)} collective-permute-done((bf16[4,16,1152]{2,1,0:T(8,128)(2,1)S(1)}, bf16[4,16,1152]{2,1,0:T(8,128)(2,1)S(1)}, u32[]{:S(2)}, u32[]{:S(2)}) %collective-permute-start.10) | collective-permute-done | bytes 147488 | tf_op jit(solution)/shard_map/ppermute | solution.py:22
  48.8 1.6 %collective-permute-start.11 = (bf16[1,16,1152]{2,1,0:T(8,128)(2,1)S(1)}, bf16[1,16,1152]{2,1,0:T(8,128)(2,1)S(1)}, u32[]{:S(2)}, u32[]{:S(2)}) collective-permute-start(bf16[1,16,1152]{2,1,0:T(8,128)(2,1)S(1)} %get-tuple-element.46), channel_id=1, source_target_pairs={{0,8},{1,9},{2,10},{3,11},{4,12},{5,13},{6,14},{7,15},{8,0},{9,1},... | collective-permute-start | bytes 110600 | tf_op jit(solution)/shard_map/ppermute | solution.py:22
  50.4 1.7 %collective-permute-start.12 = (bf16[1,16,1152]{2,1,0:T(8,128)(2,1)S(1)}, bf16[1,16,1152]{2,1,0:T(8,128)(2,1)S(1)}, u32[]{:S(2)}, u32[]{:S(2)}) collective-permute-start(bf16[1,16,1152]{2,1,0:T(8,128)(2,1)S(1)} %get-tuple-element.47), channel_id=1, source_target_pairs={{0,16},{1,17},{2,18},{3,19},{4,20},{5,21},{6,22},{7,23},{8,24},{9,... | collective-permute-start | bytes 110600 | tf_op jit(solution)/shard_map/ppermute | solution.py:22
  52.1 1.2 %collective-permute-start.13 = (bf16[1,16,1152]{2,1,0:T(8,128)(2,1)S(1)}, bf16[1,16,1152]{2,1,0:T(8,128)(2,1)S(1)}, u32[]{:S(2)}, u32[]{:S(2)}) collective-permute-start(bf16[1,16,1152]{2,1,0:T(8,128)(2,1)S(1)} %get-tuple-element.48), channel_id=1, source_target_pairs={{0,24},{1,25},{2,26},{3,27},{4,28},{5,29},{6,30},{7,31},{8,16},{9,... | collective-permute-start | bytes 110600 | tf_op jit(solution)/shard_map/ppermute | solution.py:22
  53.3 2.7 %collective-permute-done.12.refs_2_ = bf16[1,16,1152]{2,1,0:T(8,128)(2,1)S(1)} collective-permute-done((bf16[1,16,1152]{2,1,0:T(8,128)(2,1)S(1)}, bf16[1,16,1152]{2,1,0:T(8,128)(2,1)S(1)}, u32[]{:S(2)}, u32[]{:S(2)}) %collective-permute-start.12) | collective-permute-done | bytes 36896 | tf_op jit(solution)/shard_map/ppermute | solution.py:22
  56.0 1.9 %collective-permute-done.13.refs_3_ = bf16[1,16,1152]{2,1,0:T(8,128)(2,1)S(1)} collective-permute-done((bf16[1,16,1152]{2,1,0:T(8,128)(2,1)S(1)}, bf16[1,16,1152]{2,1,0:T(8,128)(2,1)S(1)}, u32[]{:S(2)}, u32[]{:S(2)}) %collective-permute-start.13) | collective-permute-done | bytes 36896 | tf_op jit(solution)/shard_map/ppermute | solution.py:22
  58.5 1.2 %collective-permute-start.16 = (f32[2,1024]{1,0:T(2,128)S(1)}, f32[2,1024]{1,0:T(2,128)S(1)}, u32[]{:S(2)}, u32[]{:S(2)}) collective-permute-start(f32[2,1024]{1,0:T(2,128)S(1)} %get-tuple-element.50.refs_0_), channel_id=1, source_target_pairs={{0,24},{1,25},{2,26},{3,27},{4,28},{5,29},{6,30},{7,31},{8,16},{9,... | collective-permute-start | bytes 24584 | tf_op jit(solution)/shard_map/ppermute | solution.py:22
  59.7 3.2 %collective-permute-start.14 = (f32[2,1024]{1,0:T(2,128)S(1)}, f32[2,1024]{1,0:T(2,128)S(1)}, u32[]{:S(2)}, u32[]{:S(2)}) collective-permute-start(f32[2,1024]{1,0:T(2,128)S(1)} %get-tuple-element.50.refs_0_), channel_id=1, source_target_pairs={{0,8},{1,9},{2,10},{3,11},{4,12},{5,13},{6,14},{7,15},{8,0},{9,1},... | collective-permute-start | bytes 24584 | tf_op jit(solution)/shard_map/ppermute | solution.py:22
  63.0 1.1 collective-permute-done.16.refs_3_
  64.6 1.5 %collective-permute-start.17 = (f32[2,1024]{1,0:T(2,128)S(1)}, f32[2,1024]{1,0:T(2,128)S(1)}, u32[]{:S(2)}, u32[]{:S(2)}) collective-permute-start(f32[2,1024]{1,0:T(2,128)S(1)} %tree_sum.1.sums_ref), channel_id=1, source_target_pairs={{0,4},{1,5},{2,6},{3,7},{4,0},{5,1},{6,2},{7,3},{8,12},{9,13},{10,... | collective-permute-start | bytes 24584 | tf_op jit(solution)/shard_map/ppermute | solution.py:22
  66.1 2.2 %collective-permute-done.17.other_sums_ref = f32[2,1024]{1,0:T(2,128)S(1)} collective-permute-done((f32[2,1024]{1,0:T(2,128)S(1)}, f32[2,1024]{1,0:T(2,128)S(1)}, u32[]{:S(2)}, u32[]{:S(2)}) %collective-permute-start.17) | collective-permute-done | bytes 8224 | tf_op jit(solution)/shard_map/ppermute | solution.py:22
  68.3 1.2 %head_grads.1 = (f32[1,1024]{1,0:T(1,128)}, bf16[16,1152]{1,0:T(8,128)(2,1)S(1)}, f32[16,1024]{1,0:T(8,128)S(1)}) custom-call(f32[2,1024]{1,0:T(2,128)S(1)} %tree_sum.1.sums_ref, f32[2,1024]{1,0:T(2,128)S(1)} %collective-permute-done.17.other_sums_ref, f32[16,1024]{1,0:T(8,128)S(1)} %get-tuple-element.51.pooled_ref, ...), custom_call_target="tpu_custom_call" | custom-call | tf_op jit(solution)/shard_map/head_grads/pallas_call | solution.py:55
  69.5 2.4 %collective-permute-start.20 = (bf16[16,1152]{1,0:T(8,128)(2,1)S(1)}, bf16[16,1152]{1,0:T(8,128)(2,1)S(1)}, u32[]{:S(2)}, u32[]{:S(2)}) collective-permute-start(bf16[16,1152]{1,0:T(8,128)(2,1)S(1)} %get-tuple-element.53.refs_0_), channel_id=1, source_target_pairs={{0,24},{1,25},{2,26},{3,27},{4,28},{5,29},{6,30},{7,31},{8,16},{9,... | collective-permute-start | bytes 110600 | tf_op jit(solution)/shard_map/ppermute | solution.py:22
  71.9 1.1 collective-permute-start.19
  73.0 0.9 collective-permute-start.18
  73.9 1.4 %collective-permute-done.20.refs_3_ = bf16[16,1152]{1,0:T(8,128)(2,1)S(1)} collective-permute-done((bf16[16,1152]{1,0:T(8,128)(2,1)S(1)}, bf16[16,1152]{1,0:T(8,128)(2,1)S(1)}, u32[]{:S(2)}, u32[]{:S(2)}) %collective-permute-start.20) | collective-permute-done | bytes 36896 | tf_op jit(solution)/shard_map/ppermute | solution.py:22
  75.3 1.5 %collective-permute-done.19.refs_2_ = bf16[16,1152]{1,0:T(8,128)(2,1)S(1)} collective-permute-done((bf16[16,1152]{1,0:T(8,128)(2,1)S(1)}, bf16[16,1152]{1,0:T(8,128)(2,1)S(1)}, u32[]{:S(2)}, u32[]{:S(2)}) %collective-permute-start.19) | collective-permute-done | bytes 36896 | tf_op jit(solution)/shard_map/ppermute | solution.py:22
  77.2 2.4 %collective-permute-start.23 = (bf16[4,16,1152]{2,1,0:T(8,128)(2,1)S(1)}, bf16[4,16,1152]{2,1,0:T(8,128)(2,1)S(1)}, u32[]{:S(2)}, u32[]{:S(2)}) collective-permute-start(bf16[4,16,1152]{2,1,0:T(8,128)(2,1)S(1)} %stack.3.refs_0_), channel_id=1, source_target_pairs={{0,6},{1,7},{2,4},{3,5},{4,2},{5,3},{6,0},{7,1},{8,14},{9,15},{10,... | collective-permute-start | bytes 442376 | tf_op jit(solution)/shard_map/ppermute | solution.py:22
  81.4 3.0 %head_weight_grad.1 = (f32[1024,1024]{1,0:T(8,128)}, f32[8,128]{1,0:T(8,128)S(1)}) custom-call(f32[16,1024]{1,0:T(8,128)S(1)} %get-tuple-element.54.normed_ref, f32[1,1024]{1,0:T(1,128)S(1)} %copy-done.7), custom_call_target="tpu_custom_call" | custom-call | flops 100663296 | bytes 4194304 | tf_op jit(solution)/shard_map/head_weight_grad/pallas_call | solution.py:323
  85.4 2.0 %collective-permute-done.24.other_ref = bf16[8,32,1152]{2,1,0:T(8,128)(2,1)S(1)} collective-permute-done((bf16[8,32,1152]{2,1,0:T(8,128)(2,1)S(1)}, bf16[8,32,1152]{2,1,0:T(8,128)(2,1)S(1)}, u32[]{:S(2)}, u32[]{:S(2)}) %collective-permute-start.24) | collective-permute-done | bytes 589856 | tf_op jit(solution)/shard_map/ppermute | solution.py:22
  87.4 8.6 %grad.1 = (f32[8,32,1024]{2,1,0:T(8,128)S(1)}, bf16[8,32,1024]{2,1,0:T(8,128)(2,1)S(1)}, f32[1,1]{1,0:T(1,128)}) custom-call(s32[1]{0:T(128)} %bitcast.context_ref, bf16[8,32,1152]{2,1,0:T(8,128)(2,1)S(1)} %near.3.own_ref, bf16[8,32,1152]{2,1,0:T(8,128)(2,1)S(1)} %collective-permute-done.24.other_ref, bf16[768,8192]{1,0:T(8,128)(2,1)S(1)} %copy-done.1, ...), custom_call_target="tpu_custom_call" | custom-call | tf_op jit(solution)/shard_map/grad/pallas_call | solution.py:55
  96.2 1.8 %collective-permute-done.25.refs_1_ = bf16[8,32,1024]{2,1,0:T(8,128)(2,1)S(1)} collective-permute-done((bf16[8,32,1024]{2,1,0:T(8,128)(2,1)S(1)}, bf16[8,32,1024]{2,1,0:T(8,128)(2,1)S(1)}, u32[]{:S(2)}, u32[]{:S(2)}) %collective-permute-start.25) | collective-permute-done | bytes 524320 | tf_op jit(solution)/shard_map/ppermute | solution.py:22
  98.1 1.1 collective-permute-start.26
  99.2 1.5 %collective-permute-start.27 = (bf16[4,16,1024]{2,1,0:T(8,128)(2,1)S(1)}, bf16[4,16,1024]{2,1,0:T(8,128)(2,1)S(1)}, u32[]{:S(2)}, u32[]{:S(2)}) collective-permute-start(bf16[4,16,1024]{2,1,0:T(8,128)(2,1)S(1)} %get-tuple-element.63), channel_id=1, source_target_pairs={{0,4},{1,5},{2,6},{3,7},{4,0},{5,1},{6,2},{7,3},{8,12},{9,13},{10,... | collective-permute-start | bytes 393224 | tf_op jit(solution)/shard_map/ppermute | solution.py:22
  100.7 1.0 collective-permute-start.28
  101.6 2.1 %collective-permute-done.26.refs_1_ = bf16[4,16,1024]{2,1,0:T(8,128)(2,1)S(1)} collective-permute-done((bf16[4,16,1024]{2,1,0:T(8,128)(2,1)S(1)}, bf16[4,16,1024]{2,1,0:T(8,128)(2,1)S(1)}, u32[]{:S(2)}, u32[]{:S(2)}) %collective-permute-start.26) | collective-permute-done | bytes 131104 | tf_op jit(solution)/shard_map/ppermute | solution.py:22
  103.7 1.9 %collective-permute-done.27.refs_2_ = bf16[4,16,1024]{2,1,0:T(8,128)(2,1)S(1)} collective-permute-done((bf16[4,16,1024]{2,1,0:T(8,128)(2,1)S(1)}, bf16[4,16,1024]{2,1,0:T(8,128)(2,1)S(1)}, u32[]{:S(2)}, u32[]{:S(2)}) %collective-permute-start.27) | collective-permute-done | bytes 131104 | tf_op jit(solution)/shard_map/ppermute | solution.py:22
  105.6 2.1 %collective-permute-done.28.refs_3_ = bf16[4,16,1024]{2,1,0:T(8,128)(2,1)S(1)} collective-permute-done((bf16[4,16,1024]{2,1,0:T(8,128)(2,1)S(1)}, bf16[4,16,1024]{2,1,0:T(8,128)(2,1)S(1)}, u32[]{:S(2)}, u32[]{:S(2)}) %collective-permute-start.28) | collective-permute-done | bytes 131104 | tf_op jit(solution)/shard_map/ppermute | solution.py:22
  107.8 0.7 collective-permute-start.29
  108.5 1.3 %collective-permute-start.30 = (bf16[1,16,1024]{2,1,0:T(8,128)(2,1)S(1)}, bf16[1,16,1024]{2,1,0:T(8,128)(2,1)S(1)}, u32[]{:S(2)}, u32[]{:S(2)}) collective-permute-start(bf16[1,16,1024]{2,1,0:T(8,128)(2,1)S(1)} %get-tuple-element.67), channel_id=1, source_target_pairs={{0,16},{1,17},{2,18},{3,19},{4,20},{5,21},{6,22},{7,23},{8,24},{9,... | collective-permute-start | bytes 98312 | tf_op jit(solution)/shard_map/ppermute | solution.py:22
  109.8 2.4 %collective-permute-start.31 = (bf16[1,16,1024]{2,1,0:T(8,128)(2,1)S(1)}, bf16[1,16,1024]{2,1,0:T(8,128)(2,1)S(1)}, u32[]{:S(2)}, u32[]{:S(2)}) collective-permute-start(bf16[1,16,1024]{2,1,0:T(8,128)(2,1)S(1)} %get-tuple-element.68), channel_id=1, source_target_pairs={{0,24},{1,25},{2,26},{3,27},{4,28},{5,29},{6,30},{7,31},{8,16},{9,... | collective-permute-start | bytes 98312 | tf_op jit(solution)/shard_map/ppermute | solution.py:22
  112.2 1.3 %collective-permute-done.30.refs_2_ = bf16[1,16,1024]{2,1,0:T(8,128)(2,1)S(1)} collective-permute-done((bf16[1,16,1024]{2,1,0:T(8,128)(2,1)S(1)}, bf16[1,16,1024]{2,1,0:T(8,128)(2,1)S(1)}, u32[]{:S(2)}, u32[]{:S(2)}) %collective-permute-start.30) | collective-permute-done | bytes 32800 | tf_op jit(solution)/shard_map/ppermute | solution.py:22
  113.5 2.0 %collective-permute-done.31.refs_3_ = bf16[1,16,1024]{2,1,0:T(8,128)(2,1)S(1)} collective-permute-done((bf16[1,16,1024]{2,1,0:T(8,128)(2,1)S(1)}, bf16[1,16,1024]{2,1,0:T(8,128)(2,1)S(1)}, u32[]{:S(2)}, u32[]{:S(2)}) %collective-permute-start.31) | collective-permute-done | bytes 32800 | tf_op jit(solution)/shard_map/ppermute | solution.py:22
  (48 shorter events, 8.4 us)
Async XLA Ops:
  0.6 11.0 %collective-permute-start = (bf16[16,1024]{1,0:T(8,128)(2,1)}, bf16[16,1024]{1,0:T(8,128)(2,1)S(1)}, u32[]{:S(2)}, u32[]{:S(2)}) collective-permute-start(bf16[16,1024]{1,0:T(8,128)(2,1)} %queries_ref.1), channel_id=1, source_target_pairs={{0,8},{1,9},{2,10},{3,11},{4,12},{5,13},{6,14},{7,15},{8,0},{9,1},... | collective-permute-start | bytes 98312 | tf_op jit(solution)/shard_map/ppermute | solution.py:22
  3.7 7.9 %collective-permute-start.2 = (bf16[16,1024]{1,0:T(8,128)(2,1)}, bf16[16,1024]{1,0:T(8,128)(2,1)S(1)}, u32[]{:S(2)}, u32[]{:S(2)}) collective-permute-start(bf16[16,1024]{1,0:T(8,128)(2,1)} %queries_ref.1), channel_id=1, source_target_pairs={{0,24},{1,25},{2,26},{3,27},{4,28},{5,29},{6,30},{7,31},{8,16},{9,... | collective-permute-start | bytes 98312 | tf_op jit(solution)/shard_map/ppermute | solution.py:22
  6.2 5.5 %collective-permute-start.1 = (bf16[16,1024]{1,0:T(8,128)(2,1)}, bf16[16,1024]{1,0:T(8,128)(2,1)S(1)}, u32[]{:S(2)}, u32[]{:S(2)}) collective-permute-start(bf16[16,1024]{1,0:T(8,128)(2,1)} %queries_ref.1), channel_id=1, source_target_pairs={{0,16},{1,17},{2,18},{3,19},{4,20},{5,21},{6,22},{7,23},{8,24},{9,... | collective-permute-start | bytes 98312 | tf_op jit(solution)/shard_map/ppermute | solution.py:22
  6.3 4.6 %copy-start = (bf16[768,8192]{1,0:T(8,128)(2,1)S(1)}, bf16[768,8192]{1,0:T(8,128)(2,1)}, u32[]{:S(2)}) copy-start(bf16[768,8192]{1,0:T(8,128)(2,1)} %tokens_ref.5) | copy-start | bytes 37748740
  10.9 0.8 copy-start.3
  11.7 7.2 %collective-permute-start.5 = (bf16[4,16,1024]{2,1,0:T(8,128)(2,1)S(1)}, bf16[4,16,1024]{2,1,0:T(8,128)(2,1)S(1)}, u32[]{:S(2)}, u32[]{:S(2)}) collective-permute-start(bf16[4,16,1024]{2,1,0:T(8,128)(2,1)S(1)} %stack.2.refs_0_), channel_id=1, source_target_pairs={{0,6},{1,7},{2,4},{3,5},{4,2},{5,3},{6,0},{7,1},{8,14},{9,15},{10,... | collective-permute-start | bytes 393224 | tf_op jit(solution)/shard_map/ppermute | solution.py:22
  14.2 6.0 %collective-permute-start.4 = (bf16[4,16,1024]{2,1,0:T(8,128)(2,1)S(1)}, bf16[4,16,1024]{2,1,0:T(8,128)(2,1)S(1)}, u32[]{:S(2)}, u32[]{:S(2)}) collective-permute-start(bf16[4,16,1024]{2,1,0:T(8,128)(2,1)S(1)} %stack.2.refs_0_), channel_id=1, source_target_pairs={{0,4},{1,5},{2,6},{3,7},{4,0},{5,1},{6,2},{7,3},{8,12},{9,13},{10,... | collective-permute-start | bytes 393224 | tf_op jit(solution)/shard_map/ppermute | solution.py:22
  14.7 5.5 %collective-permute-start.3 = (bf16[4,16,1024]{2,1,0:T(8,128)(2,1)S(1)}, bf16[4,16,1024]{2,1,0:T(8,128)(2,1)S(1)}, u32[]{:S(2)}, u32[]{:S(2)}) collective-permute-start(bf16[4,16,1024]{2,1,0:T(8,128)(2,1)S(1)} %stack.2.refs_0_), channel_id=1, source_target_pairs={{0,2},{1,3},{2,0},{3,1},{4,6},{5,7},{6,4},{7,5},{8,10},{9,11},{10,... | collective-permute-start | bytes 393224 | tf_op jit(solution)/shard_map/ppermute | solution.py:22
  20.3 2.0 %collective-permute-start.6 = (bf16[8,32,1024]{2,1,0:T(8,128)(2,1)S(1)}, bf16[8,32,1024]{2,1,0:T(8,128)(2,1)S(1)}, u32[]{:S(2)}, u32[]{:S(2)}) collective-permute-start(bf16[8,32,1024]{2,1,0:T(8,128)(2,1)S(1)} %near.2.own_ref), channel_id=1, source_target_pairs={{0,1},{1,0},{2,3},{3,2},{4,5},{5,4},{6,7},{7,6},{8,9},{9,8},{10,11... | collective-permute-start | bytes 1572872 | tf_op jit(solution)/shard_map/ppermute | solution.py:22
  22.3 4.6 %copy-start.1 = (bf16[768,8192]{1,0:T(8,128)(2,1)S(1)}, bf16[768,8192]{1,0:T(8,128)(2,1)}, u32[]{:S(2)}) copy-start(bf16[768,8192]{1,0:T(8,128)(2,1)} %tokens_ref.5) | copy-start | bytes 37748740
  26.9 31.1 %copy-start.2 = (bf16[1024,1024]{1,0:T(8,128)(2,1)S(1)}, bf16[1024,1024]{1,0:T(8,128)(2,1)}, u32[]{:S(2)}) copy-start(bf16[1024,1024]{1,0:T(8,128)(2,1)} %weight_ref.1) | copy-start | bytes 6291460
  26.9 31.1 %copy-start.4 = (f32[1024]{0:T(1024)S(1)}, f32[1024]{0:T(1024)}, u32[]{:S(2)}) copy-start(f32[1024]{0:T(1024)} %param.10) | copy-start | bytes 12292
  35.7 32.6 %copy-start.5 = (f32[1024]{0:T(1024)S(1)}, f32[1024]{0:T(1024)}, u32[]{:S(2)}) copy-start(f32[1024]{0:T(1024)} %param.12) | copy-start | bytes 12292
  35.7 32.6 %copy-start.6 = (s32[1024]{0:T(1024)S(1)}, s32[1024]{0:T(1024)}, u32[]{:S(2)}) copy-start(s32[1024]{0:T(1024)} %param.13) | copy-start | bytes 12292
  35.7 2.1 %collective-permute-start.7 = (bf16[8,32,1152]{2,1,0:T(8,128)(2,1)S(1)}, bf16[8,32,1152]{2,1,0:T(8,128)(2,1)S(1)}, u32[]{:S(2)}, u32[]{:S(2)}) collective-permute-start(bf16[8,32,1152]{2,1,0:T(8,128)(2,1)S(1)} %get-tuple-element.38), channel_id=1, source_target_pairs={{0,1},{1,0},{2,3},{3,2},{4,5},{5,4},{6,7},{7,6},{8,9},{9,8},{10,11... | collective-permute-start | bytes 1769480 | tf_op jit(solution)/shard_map/ppermute | solution.py:22
  38.2 6.0 %collective-permute-start.8 = (bf16[4,16,1152]{2,1,0:T(8,128)(2,1)S(1)}, bf16[4,16,1152]{2,1,0:T(8,128)(2,1)S(1)}, u32[]{:S(2)}, u32[]{:S(2)}) collective-permute-start(bf16[4,16,1152]{2,1,0:T(8,128)(2,1)S(1)} %get-tuple-element.41), channel_id=1, source_target_pairs={{0,2},{1,3},{2,0},{3,1},{4,6},{5,7},{6,4},{7,5},{8,10},{9,11},{10,... | collective-permute-start | bytes 442376 | tf_op jit(solution)/shard_map/ppermute | solution.py:22
  39.7 6.7 %collective-permute-start.9 = (bf16[4,16,1152]{2,1,0:T(8,128)(2,1)S(1)}, bf16[4,16,1152]{2,1,0:T(8,128)(2,1)S(1)}, u32[]{:S(2)}, u32[]{:S(2)}) collective-permute-start(bf16[4,16,1152]{2,1,0:T(8,128)(2,1)S(1)} %get-tuple-element.42), channel_id=1, source_target_pairs={{0,4},{1,5},{2,6},{3,7},{4,0},{5,1},{6,2},{7,3},{8,12},{9,13},{10,... | collective-permute-start | bytes 442376 | tf_op jit(solution)/shard_map/ppermute | solution.py:22
  41.2 7.3 %collective-permute-start.10 = (bf16[4,16,1152]{2,1,0:T(8,128)(2,1)S(1)}, bf16[4,16,1152]{2,1,0:T(8,128)(2,1)S(1)}, u32[]{:S(2)}, u32[]{:S(2)}) collective-permute-start(bf16[4,16,1152]{2,1,0:T(8,128)(2,1)S(1)} %get-tuple-element.43), channel_id=1, source_target_pairs={{0,6},{1,7},{2,4},{3,5},{4,2},{5,3},{6,0},{7,1},{8,14},{9,15},{10,... | collective-permute-start | bytes 442376 | tf_op jit(solution)/shard_map/ppermute | solution.py:22
  48.8 4.5 %collective-permute-start.11 = (bf16[1,16,1152]{2,1,0:T(8,128)(2,1)S(1)}, bf16[1,16,1152]{2,1,0:T(8,128)(2,1)S(1)}, u32[]{:S(2)}, u32[]{:S(2)}) collective-permute-start(bf16[1,16,1152]{2,1,0:T(8,128)(2,1)S(1)} %get-tuple-element.46), channel_id=1, source_target_pairs={{0,8},{1,9},{2,10},{3,11},{4,12},{5,13},{6,14},{7,15},{8,0},{9,1},... | collective-permute-start | bytes 110600 | tf_op jit(solution)/shard_map/ppermute | solution.py:22
  50.4 5.6 %collective-permute-start.12 = (bf16[1,16,1152]{2,1,0:T(8,128)(2,1)S(1)}, bf16[1,16,1152]{2,1,0:T(8,128)(2,1)S(1)}, u32[]{:S(2)}, u32[]{:S(2)}) collective-permute-start(bf16[1,16,1152]{2,1,0:T(8,128)(2,1)S(1)} %get-tuple-element.47), channel_id=1, source_target_pairs={{0,16},{1,17},{2,18},{3,19},{4,20},{5,21},{6,22},{7,23},{8,24},{9,... | collective-permute-start | bytes 110600 | tf_op jit(solution)/shard_map/ppermute | solution.py:22
  52.1 5.8 %collective-permute-start.13 = (bf16[1,16,1152]{2,1,0:T(8,128)(2,1)S(1)}, bf16[1,16,1152]{2,1,0:T(8,128)(2,1)S(1)}, u32[]{:S(2)}, u32[]{:S(2)}) collective-permute-start(bf16[1,16,1152]{2,1,0:T(8,128)(2,1)S(1)} %get-tuple-element.48), channel_id=1, source_target_pairs={{0,24},{1,25},{2,26},{3,27},{4,28},{5,29},{6,30},{7,31},{8,16},{9,... | collective-permute-start | bytes 110600 | tf_op jit(solution)/shard_map/ppermute | solution.py:22
  58.5 5.5 %collective-permute-start.16 = (f32[2,1024]{1,0:T(2,128)S(1)}, f32[2,1024]{1,0:T(2,128)S(1)}, u32[]{:S(2)}, u32[]{:S(2)}) collective-permute-start(f32[2,1024]{1,0:T(2,128)S(1)} %get-tuple-element.50.refs_0_), channel_id=1, source_target_pairs={{0,24},{1,25},{2,26},{3,27},{4,28},{5,29},{6,30},{7,31},{8,16},{9,... | collective-permute-start | bytes 24584 | tf_op jit(solution)/shard_map/ppermute | solution.py:22
  59.7 4.5 %collective-permute-start.15 = (f32[2,1024]{1,0:T(2,128)S(1)}, f32[2,1024]{1,0:T(2,128)S(1)}, u32[]{:S(2)}, u32[]{:S(2)}) collective-permute-start(f32[2,1024]{1,0:T(2,128)S(1)} %get-tuple-element.50.refs_0_), channel_id=1, source_target_pairs={{0,16},{1,17},{2,18},{3,19},{4,20},{5,21},{6,22},{7,23},{8,24},{9,... | collective-permute-start | bytes 24584 | tf_op jit(solution)/shard_map/ppermute | solution.py:22
  59.7 4.9 %collective-permute-start.14 = (f32[2,1024]{1,0:T(2,128)S(1)}, f32[2,1024]{1,0:T(2,128)S(1)}, u32[]{:S(2)}, u32[]{:S(2)}) collective-permute-start(f32[2,1024]{1,0:T(2,128)S(1)} %get-tuple-element.50.refs_0_), channel_id=1, source_target_pairs={{0,8},{1,9},{2,10},{3,11},{4,12},{5,13},{6,14},{7,15},{8,0},{9,1},... | collective-permute-start | bytes 24584 | tf_op jit(solution)/shard_map/ppermute | solution.py:22
  64.6 3.7 %collective-permute-start.17 = (f32[2,1024]{1,0:T(2,128)S(1)}, f32[2,1024]{1,0:T(2,128)S(1)}, u32[]{:S(2)}, u32[]{:S(2)}) collective-permute-start(f32[2,1024]{1,0:T(2,128)S(1)} %tree_sum.1.sums_ref), channel_id=1, source_target_pairs={{0,4},{1,5},{2,6},{3,7},{4,0},{5,1},{6,2},{7,3},{8,12},{9,13},{10,... | collective-permute-start | bytes 24584 | tf_op jit(solution)/shard_map/ppermute | solution.py:22
  69.5 5.8 %collective-permute-start.20 = (bf16[16,1152]{1,0:T(8,128)(2,1)S(1)}, bf16[16,1152]{1,0:T(8,128)(2,1)S(1)}, u32[]{:S(2)}, u32[]{:S(2)}) collective-permute-start(bf16[16,1152]{1,0:T(8,128)(2,1)S(1)} %get-tuple-element.53.refs_0_), channel_id=1, source_target_pairs={{0,24},{1,25},{2,26},{3,27},{4,28},{5,29},{6,30},{7,31},{8,16},{9,... | collective-permute-start | bytes 110600 | tf_op jit(solution)/shard_map/ppermute | solution.py:22
  71.9 4.9 %collective-permute-start.19 = (bf16[16,1152]{1,0:T(8,128)(2,1)S(1)}, bf16[16,1152]{1,0:T(8,128)(2,1)S(1)}, u32[]{:S(2)}, u32[]{:S(2)}) collective-permute-start(bf16[16,1152]{1,0:T(8,128)(2,1)S(1)} %get-tuple-element.53.refs_0_), channel_id=1, source_target_pairs={{0,16},{1,17},{2,18},{3,19},{4,20},{5,21},{6,22},{7,23},{8,24},{9,... | collective-permute-start | bytes 110600 | tf_op jit(solution)/shard_map/ppermute | solution.py:22
  73.0 4.2 %collective-permute-start.18 = (bf16[16,1152]{1,0:T(8,128)(2,1)S(1)}, bf16[16,1152]{1,0:T(8,128)(2,1)S(1)}, u32[]{:S(2)}, u32[]{:S(2)}) collective-permute-start(bf16[16,1152]{1,0:T(8,128)(2,1)S(1)} %get-tuple-element.53.refs_0_), channel_id=1, source_target_pairs={{0,8},{1,9},{2,10},{3,11},{4,12},{5,13},{6,14},{7,15},{8,0},{9,1},... | collective-permute-start | bytes 110600 | tf_op jit(solution)/shard_map/ppermute | solution.py:22
  77.2 7.2 %collective-permute-start.23 = (bf16[4,16,1152]{2,1,0:T(8,128)(2,1)S(1)}, bf16[4,16,1152]{2,1,0:T(8,128)(2,1)S(1)}, u32[]{:S(2)}, u32[]{:S(2)}) collective-permute-start(bf16[4,16,1152]{2,1,0:T(8,128)(2,1)S(1)} %stack.3.refs_0_), channel_id=1, source_target_pairs={{0,6},{1,7},{2,4},{3,5},{4,2},{5,3},{6,0},{7,1},{8,14},{9,15},{10,... | collective-permute-start | bytes 442376 | tf_op jit(solution)/shard_map/ppermute | solution.py:22
  79.6 5.2 %collective-permute-start.22 = (bf16[4,16,1152]{2,1,0:T(8,128)(2,1)S(1)}, bf16[4,16,1152]{2,1,0:T(8,128)(2,1)S(1)}, u32[]{:S(2)}, u32[]{:S(2)}) collective-permute-start(bf16[4,16,1152]{2,1,0:T(8,128)(2,1)S(1)} %stack.3.refs_0_), channel_id=1, source_target_pairs={{0,4},{1,5},{2,6},{3,7},{4,0},{5,1},{6,2},{7,3},{8,12},{9,13},{10,... | collective-permute-start | bytes 442376 | tf_op jit(solution)/shard_map/ppermute | solution.py:22
  80.1 5.1 %collective-permute-start.21 = (bf16[4,16,1152]{2,1,0:T(8,128)(2,1)S(1)}, bf16[4,16,1152]{2,1,0:T(8,128)(2,1)S(1)}, u32[]{:S(2)}, u32[]{:S(2)}) collective-permute-start(bf16[4,16,1152]{2,1,0:T(8,128)(2,1)S(1)} %stack.3.refs_0_), channel_id=1, source_target_pairs={{0,2},{1,3},{2,0},{3,1},{4,6},{5,7},{6,4},{7,5},{8,10},{9,11},{10,... | collective-permute-start | bytes 442376 | tf_op jit(solution)/shard_map/ppermute | solution.py:22
  80.7 0.7 copy-start.7
  85.3 2.1 %collective-permute-start.24 = (bf16[8,32,1152]{2,1,0:T(8,128)(2,1)S(1)}, bf16[8,32,1152]{2,1,0:T(8,128)(2,1)S(1)}, u32[]{:S(2)}, u32[]{:S(2)}) collective-permute-start(bf16[8,32,1152]{2,1,0:T(8,128)(2,1)S(1)} %near.3.own_ref), channel_id=1, source_target_pairs={{0,1},{1,0},{2,3},{3,2},{4,5},{5,4},{6,7},{7,6},{8,9},{9,8},{10,11... | collective-permute-start | bytes 1769480 | tf_op jit(solution)/shard_map/ppermute | solution.py:22
  96.0 2.0 %collective-permute-start.25 = (bf16[8,32,1024]{2,1,0:T(8,128)(2,1)S(1)}, bf16[8,32,1024]{2,1,0:T(8,128)(2,1)S(1)}, u32[]{:S(2)}, u32[]{:S(2)}) collective-permute-start(bf16[8,32,1024]{2,1,0:T(8,128)(2,1)S(1)} %get-tuple-element.60), channel_id=1, source_target_pairs={{0,1},{1,0},{2,3},{3,2},{4,5},{5,4},{6,7},{7,6},{8,9},{9,8},{10,11... | collective-permute-start | bytes 1572872 | tf_op jit(solution)/shard_map/ppermute | solution.py:22
  98.1 5.6 %collective-permute-start.26 = (bf16[4,16,1024]{2,1,0:T(8,128)(2,1)S(1)}, bf16[4,16,1024]{2,1,0:T(8,128)(2,1)S(1)}, u32[]{:S(2)}, u32[]{:S(2)}) collective-permute-start(bf16[4,16,1024]{2,1,0:T(8,128)(2,1)S(1)} %get-tuple-element.62), channel_id=1, source_target_pairs={{0,2},{1,3},{2,0},{3,1},{4,6},{5,7},{6,4},{7,5},{8,10},{9,11},{10,... | collective-permute-start | bytes 393224 | tf_op jit(solution)/shard_map/ppermute | solution.py:22
  99.2 6.4 %collective-permute-start.27 = (bf16[4,16,1024]{2,1,0:T(8,128)(2,1)S(1)}, bf16[4,16,1024]{2,1,0:T(8,128)(2,1)S(1)}, u32[]{:S(2)}, u32[]{:S(2)}) collective-permute-start(bf16[4,16,1024]{2,1,0:T(8,128)(2,1)S(1)} %get-tuple-element.63), channel_id=1, source_target_pairs={{0,4},{1,5},{2,6},{3,7},{4,0},{5,1},{6,2},{7,3},{8,12},{9,13},{10,... | collective-permute-start | bytes 393224 | tf_op jit(solution)/shard_map/ppermute | solution.py:22
  100.7 7.0 %collective-permute-start.28 = (bf16[4,16,1024]{2,1,0:T(8,128)(2,1)S(1)}, bf16[4,16,1024]{2,1,0:T(8,128)(2,1)S(1)}, u32[]{:S(2)}, u32[]{:S(2)}) collective-permute-start(bf16[4,16,1024]{2,1,0:T(8,128)(2,1)S(1)} %get-tuple-element.64), channel_id=1, source_target_pairs={{0,6},{1,7},{2,4},{3,5},{4,2},{5,3},{6,0},{7,1},{8,14},{9,15},{10,... | collective-permute-start | bytes 393224 | tf_op jit(solution)/shard_map/ppermute | solution.py:22
  107.8 4.5 %collective-permute-start.29 = (bf16[1,16,1024]{2,1,0:T(8,128)(2,1)S(1)}, bf16[1,16,1024]{2,1,0:T(8,128)(2,1)S(1)}, u32[]{:S(2)}, u32[]{:S(2)}) collective-permute-start(bf16[1,16,1024]{2,1,0:T(8,128)(2,1)S(1)} %get-tuple-element.66), channel_id=1, source_target_pairs={{0,8},{1,9},{2,10},{3,11},{4,12},{5,13},{6,14},{7,15},{8,0},{9,1},... | collective-permute-start | bytes 98312 | tf_op jit(solution)/shard_map/ppermute | solution.py:22
  108.5 5.0 %collective-permute-start.30 = (bf16[1,16,1024]{2,1,0:T(8,128)(2,1)S(1)}, bf16[1,16,1024]{2,1,0:T(8,128)(2,1)S(1)}, u32[]{:S(2)}, u32[]{:S(2)}) collective-permute-start(bf16[1,16,1024]{2,1,0:T(8,128)(2,1)S(1)} %get-tuple-element.67), channel_id=1, source_target_pairs={{0,16},{1,17},{2,18},{3,19},{4,20},{5,21},{6,22},{7,23},{8,24},{9,... | collective-permute-start | bytes 98312 | tf_op jit(solution)/shard_map/ppermute | solution.py:22
  109.8 5.7 %collective-permute-start.31 = (bf16[1,16,1024]{2,1,0:T(8,128)(2,1)S(1)}, bf16[1,16,1024]{2,1,0:T(8,128)(2,1)S(1)}, u32[]{:S(2)}, u32[]{:S(2)}) collective-permute-start(bf16[1,16,1024]{2,1,0:T(8,128)(2,1)S(1)} %get-tuple-element.68), channel_id=1, source_target_pairs={{0,24},{1,25},{2,26},{3,27},{4,28},{5,29},{6,30},{7,31},{8,16},{9,... | collective-permute-start | bytes 98312 | tf_op jit(solution)/shard_map/ppermute | solution.py:22

commit v4 on v3

--- a/solution.py
+++ b/solution.py
@@ -23,11 +23,12 @@
 
 
 def far_steps():
-    return [(2 * j, 0) for j in range(1, lax.axis_size("ctx") // 2)]
+    return [(2 * j, 0) for j in reversed(range(1, lax.axis_size("ctx") // 2))]
 
 
 def near_steps():
-    return [(i, 2 * k) for i in range(2) for k in range(lax.axis_size("cls") // 2) if i or k]
+    steps = [(i, 2 * k) for i in range(2) for k in range(lax.axis_size("cls") // 2) if i or k]
+    return sorted(steps, key=lambda step: not (step[0] and step[1]))
 
 
 def relative_blocks(contexts):
@@ -61,24 +62,25 @@
         out_ref[at] = ref[...].reshape(out_ref.shape[1:])
 
 
-def near_kernel(count, *refs):
-    out_ref, parts = refs[-1], refs[:count]
-    blocks, rows, _ = parts[0].shape
-    across = len(parts) // 2
-    for i in range(2):
-        for k in range(across):
-            out_ref[i * blocks : (i + 1) * blocks, k * rows : (k + 1) * rows] = parts[i * across + k][...]
+def near_kernel(steps, *refs):
+    out_ref = refs[-1]
+    blocks, rows, _ = refs[0].shape
+    for (i, k), ref in zip(steps, refs):
+        at = k // 2 * rows
+        out_ref[i * blocks : (i + 1) * blocks, at : at + rows] = ref[...]
 
 
 def gather(block, local=None, after=()):
-    far = [swap(block, *step) for step in far_steps()]
+    far = [swap(block, *step) for step in far_steps()[::-1]]
     rows, width = block.shape
     (held,) = call(
         stack_kernel, [((len(far) + 1, rows, width), block.dtype)], "stack", [block if local is None else local, *far]
     )
-    parts = [held] + [swap(held, *step) for step in near_steps()]
+    steps = near_steps()[::-1]
+    parts = [held] + [swap(held, *step) for step in steps]
+    steps = [(0, 0)] + steps
     shape = (2 * held.shape[0], len(parts) // 2 * rows, width)
-    (held,) = call(functools.partial(near_kernel, len(parts)), [(shape, held.dtype)], "near", [*parts, *after])
+    (held,) = call(functools.partial(near_kernel, steps), [(shape, held.dtype)], "near", [*parts, *after])
     return held, swap(held, 0, 1)
 
 
@@ -104,32 +106,70 @@
     return block[:, at : at + 1] + (block[:, at + 1 : at + 2] + block[:, at + 2 : at + 3])
 
 
-def first_kernel(tokens_ref, queries_ref, out_ref):
-    out_ref[...] = queries_ref[...]
-
-
-def columns_of(context_ref, contexts, p, width):
-    return pl.ds(pl.multiple_of((context_ref[0] ^ relative_blocks(contexts)[p]) * width, LANES), width)
-
-
-def project(context_ref, own_ref, other_ref, tokens_ref, width):
+def load_kernel(tokens_ref, queries_ref, held_ref, own_ref, sems):
+    chunks = sems.shape[0] - 1
+    rows = held_ref.shape[0] // chunks
+    copies = [pltpu.make_async_copy(queries_ref, own_ref, sems.at[chunks])]
+    for i in range(chunks):
+        part = pl.ds(i * rows, rows)
+        copies.append(pltpu.make_async_copy(tokens_ref.at[part], held_ref.at[part], sems.at[i]))
+    for copy in copies:
+        copy.start()
+    for copy in copies:
+        copy.wait()
+
+
+def load(*arrays):
+    chunks = 8
+    return pl.pallas_call(
+        load_kernel,
+        out_shape=[pltpu.VMEM(x.shape, x.dtype) for x in arrays],
+        in_specs=[pl.BlockSpec(memory_space=pltpu.HBM)] * len(arrays),
+        out_specs=[pl.BlockSpec(memory_space=pltpu.VMEM)] * len(arrays),
+        scratch_shapes=[pltpu.SemaphoreType.DMA((chunks + 1,))],
+        compiler_params=pltpu.CompilerParams(vmem_limit_bytes=16 * MIB),
+        name="load",
+    )(*[pltpu.with_memory_space_constraint(x, pltpu.HBM) for x in arrays])
+
+
+def columns_of(context_ref, contexts, p, width, at=0, size=None):
+    start = pl.multiple_of((context_ref[0] ^ relative_blocks(contexts)[p]) * width, LANES)
+    return pl.ds(start + at, size or width)
+
+
+def project(context_ref, own_ref, other_ref, tokens_ref, width, tile=256):
+    contexts = own_ref.shape[0]
+    tiles = []
+    for at in range(0, tokens_ref.shape[0], tile):
+        total = None
+        for p in range(contexts):
+            both = jnp.concatenate([own_ref[p], other_ref[p]], axis=0)[:, :width]
+            block = tokens_ref[at : at + tile, columns_of(context_ref, contexts, p, width)]
+            part = lax.dot_general(block, both, (((1,), (1,)), ((), ())), preferred_element_type=F32)
+            total = part if total is None else total + part
+        tiles.append(total.T)
+    return jnp.concatenate(tiles, axis=1)
+
+
+def project_grad(context_ref, own_ref, other_ref, tokens_ref, width):
     contexts = own_ref.shape[0]
     total = None
     for p in range(contexts):
         both = jnp.concatenate([own_ref[p], other_ref[p]], axis=0)[:, :width]
         block = tokens_ref[:, columns_of(context_ref, contexts, p, width)]
-        part = lax.dot_general(block, both, (((1,), (1,)), ((), ())), preferred_element_type=F32)
+        part = lax.dot_general(both, block, (((1,), (1,)), ((), ())), preferred_element_type=F32)
         total = part if total is None else total + part
-    return total.T
-
-
-def spread(context_ref, left, tokens_ref, keep_ref, send_ref, extra):
+    return total
+
+
+def spread(context_ref, left, tokens_ref, keep_ref, send_ref, extra, tile):
     contexts, half, width = keep_ref.shape
     for p in range(contexts):
-        block = tokens_ref[:, columns_of(context_ref, contexts, p, width)]
-        part = jnp.dot(left, block, preferred_element_type=F32)
-        keep_ref[p] = part[:half]
-        send_ref[p, :, :width] = part[half:].astype(BF16)
+        for at in range(0, width, tile):
+            block = tokens_ref[:, columns_of(context_ref, contexts, p, width, at, tile)]
+            part = jnp.dot(left, block, preferred_element_type=F32)
+            keep_ref[p, :, at : at + tile] = part[:half]
+            send_ref[p, :, at : at + tile] = part[half:].astype(BF16)
         if extra is not None:
             send_ref[p, :, width:] = extra
 
@@ -142,16 +182,16 @@
     w_ref[...] = weights
     peak_ref[...] = jnp.broadcast_to(peak, peak_ref.shape)
     half = keep_ref.shape[1]
-    spread(context_ref, weights.astype(BF16), tokens_ref, keep_ref, send_ref, into_lanes([peak[half:]], half))
+    spread(context_ref, weights.astype(BF16), tokens_ref, keep_ref, send_ref, into_lanes([peak[half:]], half), 256)
 
 
 def grad_kernel(scale, classes, context_ref, own_ref, other_ref, tokens_ref, w_ref, peak_ref, keep_ref, send_ref, loss_ref):
     width = keep_ref.shape[2]
-    projected = project(context_ref, own_ref, other_ref, tokens_ref, width)
+    projected = project_grad(context_ref, own_ref, other_ref, tokens_ref, width)
     own, other = own_ref[0], other_ref[0]
     top = jnp.concatenate([from_lanes(own, width, 0), from_lanes(other, width, 0)], axis=0)
     weights = w_ref[...] * jnp.exp(peak_ref[:, :1] - top)
-    spread(context_ref, (weights * projected).astype(BF16), tokens_ref, keep_ref, send_ref, None)
+    spread(context_ref, (weights * projected).astype(BF16), tokens_ref, keep_ref, send_ref, None, width)
     rows = classes // 2
     each = own.shape[0] // rows
     sums = []
@@ -185,7 +225,7 @@
         ref[p, :, width:] = into_lanes([top], total.shape[0])
 
 
-def core_kernel(peaks, across, *refs):
+def core_kernel(peaks, steps, *refs):
     keep_ref, recv_ref, *refs = refs
     peak = refs.pop(0)[: keep_ref.shape[1], :1] if peaks else None
     top_ref = refs.pop() if peaks else None
@@ -195,18 +235,18 @@
         for b in range(blocks):
             p = i * blocks + b
             total, top = total_of(keep_ref[p], peak, [recv_ref[p]], width)
-            for k in range(across):
-                part = total[k * rows : (k + 1) * rows]
-                part_top = top[k * rows : (k + 1) * rows] if peaks else None
-                if i == 0 and k == 0:
-                    refs[0][b] = part
+            for ref, (_, k) in [(r, step) for r, step in zip(refs, steps) if step[0] == i]:
+                at = k // 2 * rows
+                part = total[at : at + rows]
+                if ref is refs[0]:
+                    ref[b] = part
                 else:
-                    put(refs[i * across + k], b, part, part_top, width)
+                    put(ref, b, part, top[at : at + rows] if peaks else None, width)
     if peaks:
         top_ref[...] = jnp.broadcast_to(top[:rows], top_ref.shape)
 
 
-def near_sum_kernel(peaks, count, *refs):
+def near_sum_kernel(peaks, count, steps, *refs):
     keep_ref, *refs = refs
     received, refs = refs[:count], list(refs[count:])
     peak = refs.pop(0)[:, :1] if peaks else None
@@ -217,7 +257,7 @@
         if p == 0:
             refs[0][0] = total
         else:
-            put(refs[p], 0, total, top, width)
+            put(refs[steps.index((2 * p, 0)) + 1], 0, total, top, width)
     if peaks:
         top_ref[...] = jnp.broadcast_to(top, top_ref.shape)
 
@@ -232,11 +272,11 @@
     top_out = [((rows, LANES), F32)] if peaks else []
     outs = [((blocks, rows, width), F32)] + [((blocks, rows, lanes), BF16)] * len(near) + top_out
     args = [keep, swap(send, 0, 1)] + ([peak] if peaks else [])
-    out = call(functools.partial(core_kernel, peaks, across), outs, "core_sum", args)
+    out = call(functools.partial(core_kernel, peaks, [(0, 0)] + near), outs, "core_sum", args)
     received = [swap(s, *step) for s, step in zip(out[1:], near)]
     outs = [((1, rows, width), F32)] + [((1, rows, lanes), BF16)] * len(far) + top_out
     args = [out[0], *received] + (out[-1:] if peaks else [])
-    out = call(functools.partial(near_sum_kernel, peaks, len(received)), outs, "near_sum", args)
+    out = call(functools.partial(near_sum_kernel, peaks, len(received), far), outs, "near_sum", args)
     received = [swap(s, *step) for s, step in zip(out[1:], far)]
     return [out[0], *received] + (out[-1:] if peaks else [])
 
@@ -348,14 +388,7 @@
     valid_count = jnp.clip(doc_length - offset, 0, token_count)
 
     context = context_index.astype(jnp.int32)[None]
-    (queries_here,) = call(
-        first_kernel,
-        [(queries.shape, BF16)],
-        "first",
-        [tokens, queries],
-        limit=32,
-        cost=pl.CostEstimate(flops=0, bytes_accessed=2 * token_count * full_width, transcendentals=0),
-    )
+    held, queries_here = load(tokens, queries)
     own, other = gather(queries, queries_here)
     keep, send, own_peak, weights = call(
         pool_kernel,
@@ -366,9 +399,9 @@
             ((heads, token_count), F32),
         ],
         "pool",
-        [context, valid_count, own, other, tokens],
+        [context, valid_count, own, other, held],
         smem_args=(0, 1),
-        limit=32,
+        limit=16,
     )
     parts = scatter_sum(keep, send, own_peak)
     gain = norm_gain[None, :]
@@ -378,7 +411,7 @@
         "head_sums",
         [*parts, gain, head_weight],
     )
-    far_sums = [swap(sums, *step) for step in far_steps()]
+    far_sums = [swap(sums, *step) for step in far_steps()[::-1]]
     (sums,) = call(tree_sum_kernel, [((2, columns), F32)], "tree_sum", [sums, *far_sums])
     bias_grad, pooled_grad, normed = call(
         functools.partial(head_grads_kernel, full_width),
@@ -392,9 +425,9 @@
         functools.partial(grad_kernel, 1.0 / (columns * classes), classes),
         [((contexts, half, width), F32), ((contexts, half, width), BF16), ((1, 1), F32)],
         "grad",
-        [context, own, other, tokens, weights, own_peak],
+        [context, own, other, held, weights, own_peak],
         smem_args=(0,),
-        limit=32,
+        limit=16,
     )
     (query_grad,) = call(far_sum_kernel, [((rows, width), F32)], "far_sum", scatter_sum(keep, send, None))
     return (loss.reshape(()), query_grad, head_grad, bias_grad.reshape(-1))

time: 116 us -> 116 us (level)
  Pallas kernels: 23.9 us -> 26.8 us
  waiting for transfers between devices: 40.5 us -> 38.2 us
    pallas_call x0 -> x1, Pallas kernels: none -> 4.72 us  [load(): pl.pallas_call(load_kernel, out_shape=[pltpu.VMEM(x.shape, x.dtype) for x...]
    ppermute x32, waiting for transfers between devices: 40.5 us -> 38.2 us  [swap(): return lax.ppermute(x, ('ctx', 'cls'), pairs)]
    pallas_call x15 -> x14, Pallas kernels: 20.9 us -> 19.2 us  [call(): return list(run(*args))]
  transfers between devices with their start and end apart: 32 -> 32, of which waited for: 26 -> 22; matrix products, arithmetic and copies ran while one was open for 0% -> 0% of each run, Pallas kernels for 3% -> 7%
where the time goes in v4:
time: 116 us
  starting transfers between devices  39.7 us (34%)
  waiting for transfers between devices  38.2 us (33%)
  Pallas kernels  26.8 us (23%)
  local copies, waits for them, and re-layouts  9.83 us (8%)
  between operations  1.46 us (1%)
    ppermute x32, starting transfers between devices, swap(): return lax.ppermute(x, ('ctx', 'cls'), pairs)  39.7 us
    ppermute x32, waiting for transfers between devices, swap(): return lax.ppermute(x, ('ctx', 'cls'), pairs)  38.2 us
    pallas_call x14, Pallas kernels, call(): return list(run(*args))  19.2 us
    unnamed x16, local copies, waits for them, and re-layouts  9.83 us
    pallas_call x1, Pallas kernels, load(): pl.pallas_call(load_kernel, out_shape=[pltpu.VMEM(x.shape, x.dtype) for x...  4.72 us
    pallas_call x1, Pallas kernels, head_weight_grad(): pl.pallas_call(functools.partial(head_weight_grad_kernel, columns // rows...  2.95 us
  transfers between devices with their start and end apart: 32, of which 22 were waited for; matrix products, arithmetic and copies ran while one was open for 0% of the time, Pallas kernels for 7%

profile of v4, /device:TPU:0, one launch (start us, length us, event | category | flops | bytes accessed | tf_op | source)
XLA Modules:
  0.0 116.1 jit_solution(912406912725475783)
XLA Ops:
  0.7 3.1 %collective-permute-start = (bf16[16,1024]{1,0:T(8,128)(2,1)}, bf16[16,1024]{1,0:T(8,128)(2,1)S(1)}, u32[]{:S(2)}, u32[]{:S(2)}) collective-permute-start(bf16[16,1024]{1,0:T(8,128)(2,1)} %queries_ref.1), channel_id=1, source_target_pairs={{0,8},{1,9},{2,10},{3,11},{4,12},{5,13},{6,14},{7,15},{8,0},{9,1},... | collective-permute-start | bytes 98312 | tf_op jit(solution)/shard_map/ppermute | solution.py:22
  3.7 2.5 %collective-permute-start.2 = (bf16[16,1024]{1,0:T(8,128)(2,1)}, bf16[16,1024]{1,0:T(8,128)(2,1)S(1)}, u32[]{:S(2)}, u32[]{:S(2)}) collective-permute-start(bf16[16,1024]{1,0:T(8,128)(2,1)} %queries_ref.1), channel_id=1, source_target_pairs={{0,24},{1,25},{2,26},{3,27},{4,28},{5,29},{6,30},{7,31},{8,16},{9,... | collective-permute-start | bytes 98312 | tf_op jit(solution)/shard_map/ppermute | solution.py:22
  6.3 4.7 %load.1 = (bf16[768,8192]{1,0:T(8,128)(2,1)S(1)}, bf16[16,1024]{1,0:T(8,128)(2,1)S(1)}) custom-call(bf16[768,8192]{1,0:T(8,128)(2,1)} %tokens_ref.1, bf16[16,1024]{1,0:T(8,128)(2,1)} %queries_ref.1), custom_call_target="tpu_custom_call" | custom-call | tf_op jit(solution)/shard_map/load/pallas_call | solution.py:124
  11.1 4.5 %copy-done = bf16[768,8192]{1,0:T(8,128)(2,1)} copy-done((bf16[768,8192]{1,0:T(8,128)(2,1)}, bf16[768,8192]{1,0:T(8,128)(2,1)S(1)}, u32[]{:S(2)}) %copy-start) | copy-done | bytes 12582936
  15.7 2.5 %collective-permute-start.5 = (bf16[4,16,1024]{2,1,0:T(8,128)(2,1)S(1)}, bf16[4,16,1024]{2,1,0:T(8,128)(2,1)S(1)}, u32[]{:S(2)}, u32[]{:S(2)}) collective-permute-start(bf16[4,16,1024]{2,1,0:T(8,128)(2,1)S(1)} %stack.2.refs_0_), channel_id=1, source_target_pairs={{0,6},{1,7},{2,4},{3,5},{4,2},{5,3},{6,0},{7,1},{8,14},{9,15},{10,... | collective-permute-start | bytes 393224 | tf_op jit(solution)/shard_map/ppermute | solution.py:22
  19.2 3.1 %collective-permute-done.5.refs_3_ = bf16[4,16,1024]{2,1,0:T(8,128)(2,1)S(1)} collective-permute-done((bf16[4,16,1024]{2,1,0:T(8,128)(2,1)S(1)}, bf16[4,16,1024]{2,1,0:T(8,128)(2,1)S(1)}, u32[]{:S(2)}, u32[]{:S(2)}) %collective-permute-start.5) | collective-permute-done | bytes 131104 | tf_op jit(solution)/shard_map/ppermute | solution.py:22
  22.3 1.8 %collective-permute-done.4.refs_2_ = bf16[4,16,1024]{2,1,0:T(8,128)(2,1)S(1)} collective-permute-done((bf16[4,16,1024]{2,1,0:T(8,128)(2,1)S(1)}, bf16[4,16,1024]{2,1,0:T(8,128)(2,1)S(1)}, u32[]{:S(2)}, u32[]{:S(2)}) %collective-permute-start.4) | collective-permute-done | bytes 131104 | tf_op jit(solution)/shard_map/ppermute | solution.py:22
  25.0 1.2 %collective-permute-done.6.other_ref = bf16[8,32,1024]{2,1,0:T(8,128)(2,1)S(1)} collective-permute-done((bf16[8,32,1024]{2,1,0:T(8,128)(2,1)S(1)}, bf16[8,32,1024]{2,1,0:T(8,128)(2,1)S(1)}, u32[]{:S(2)}, u32[]{:S(2)}) %collective-permute-start.6) | collective-permute-done | bytes 524320 | tf_op jit(solution)/shard_map/ppermute | solution.py:22
  26.2 4.6 %copy-done.1 = bf16[768,8192]{1,0:T(8,128)(2,1)S(1)} copy-done((bf16[768,8192]{1,0:T(8,128)(2,1)S(1)}, bf16[768,8192]{1,0:T(8,128)(2,1)}, u32[]{:S(2)}) %copy-start.1) | copy-done | bytes 12582936
  30.8 7.9 %pool.1 = (f32[8,32,1024]{2,1,0:T(8,128)S(1)}, bf16[8,32,1152]{2,1,0:T(8,128)(2,1)S(1)}, f32[64,128]{1,0:T(8,128)S(1)}, f32[64,768]{1,0:T(8,128)S(1)}) custom-call(s32[1]{0:T(128)} %bitcast.context_ref, s32[1]{0:T(128)S(6)} %min.6.count_ref, bf16[8,32,1024]{2,1,0:T(8,128)(2,1)S(1)} %near.2.own_ref, ...), custom_call_target="tpu_custom_call" | custom-call | tf_op jit(solution)/shard_map/pool/pallas_call | solution.py:56
  38.9 1.9 %collective-permute-done.7.refs_1_ = bf16[8,32,1152]{2,1,0:T(8,128)(2,1)S(1)} collective-permute-done((bf16[8,32,1152]{2,1,0:T(8,128)(2,1)S(1)}, bf16[8,32,1152]{2,1,0:T(8,128)(2,1)S(1)}, u32[]{:S(2)}, u32[]{:S(2)}) %collective-permute-start.7) | collective-permute-done | bytes 589856 | tf_op jit(solution)/shard_map/ppermute | solution.py:22
  41.2 1.7 %collective-permute-start.8 = (bf16[4,16,1152]{2,1,0:T(8,128)(2,1)S(1)}, bf16[4,16,1152]{2,1,0:T(8,128)(2,1)S(1)}, u32[]{:S(2)}, u32[]{:S(2)}) collective-permute-start(bf16[4,16,1152]{2,1,0:T(8,128)(2,1)S(1)} %get-tuple-element.45), channel_id=1, source_target_pairs={{0,6},{1,7},{2,4},{3,5},{4,2},{5,3},{6,0},{7,1},{8,14},{9,15},{10,... | collective-permute-start | bytes 442376 | tf_op jit(solution)/shard_map/ppermute | solution.py:22
  42.9 1.3 %collective-permute-start.9 = (bf16[4,16,1152]{2,1,0:T(8,128)(2,1)S(1)}, bf16[4,16,1152]{2,1,0:T(8,128)(2,1)S(1)}, u32[]{:S(2)}, u32[]{:S(2)}) collective-permute-start(bf16[4,16,1152]{2,1,0:T(8,128)(2,1)S(1)} %get-tuple-element.46), channel_id=1, source_target_pairs={{0,2},{1,3},{2,0},{3,1},{4,6},{5,7},{6,4},{7,5},{8,10},{9,11},{10,... | collective-permute-start | bytes 442376 | tf_op jit(solution)/shard_map/ppermute | solution.py:22
  44.8 4.1 %collective-permute-done.8.refs_1_ = bf16[4,16,1152]{2,1,0:T(8,128)(2,1)S(1)} collective-permute-done((bf16[4,16,1152]{2,1,0:T(8,128)(2,1)S(1)}, bf16[4,16,1152]{2,1,0:T(8,128)(2,1)S(1)}, u32[]{:S(2)}, u32[]{:S(2)}) %collective-permute-start.8) | collective-permute-done | bytes 147488 | tf_op jit(solution)/shard_map/ppermute | solution.py:22
  48.9 2.3 %collective-permute-done.9.refs_2_ = bf16[4,16,1152]{2,1,0:T(8,128)(2,1)S(1)} collective-permute-done((bf16[4,16,1152]{2,1,0:T(8,128)(2,1)S(1)}, bf16[4,16,1152]{2,1,0:T(8,128)(2,1)S(1)}, u32[]{:S(2)}, u32[]{:S(2)}) %collective-permute-start.9) | collective-permute-done | bytes 147488 | tf_op jit(solution)/shard_map/ppermute | solution.py:22
  51.6 2.7 %collective-permute-start.11 = (bf16[1,16,1152]{2,1,0:T(8,128)(2,1)S(1)}, bf16[1,16,1152]{2,1,0:T(8,128)(2,1)S(1)}, u32[]{:S(2)}, u32[]{:S(2)}) collective-permute-start(bf16[1,16,1152]{2,1,0:T(8,128)(2,1)S(1)} %get-tuple-element.50), channel_id=1, source_target_pairs={{0,24},{1,25},{2,26},{3,27},{4,28},{5,29},{6,30},{7,31},{8,16},{9,... | collective-permute-start | bytes 110600 | tf_op jit(solution)/shard_map/ppermute | solution.py:22
  54.6 1.4 %collective-permute-start.13 = (bf16[1,16,1152]{2,1,0:T(8,128)(2,1)S(1)}, bf16[1,16,1152]{2,1,0:T(8,128)(2,1)S(1)}, u32[]{:S(2)}, u32[]{:S(2)}) collective-permute-start(bf16[1,16,1152]{2,1,0:T(8,128)(2,1)S(1)} %get-tuple-element.52), channel_id=1, source_target_pairs={{0,8},{1,9},{2,10},{3,11},{4,12},{5,13},{6,14},{7,15},{8,0},{9,1},... | collective-permute-start | bytes 110600 | tf_op jit(solution)/shard_map/ppermute | solution.py:22
  56.0 1.5 %collective-permute-done.11.refs_1_ = bf16[1,16,1152]{2,1,0:T(8,128)(2,1)S(1)} collective-permute-done((bf16[1,16,1152]{2,1,0:T(8,128)(2,1)S(1)}, bf16[1,16,1152]{2,1,0:T(8,128)(2,1)S(1)}, u32[]{:S(2)}, u32[]{:S(2)}) %collective-permute-start.11) | collective-permute-done | bytes 36896 | tf_op jit(solution)/shard_map/ppermute | solution.py:22
  57.5 2.0 %collective-permute-done.12.refs_2_ = bf16[1,16,1152]{2,1,0:T(8,128)(2,1)S(1)} collective-permute-done((bf16[1,16,1152]{2,1,0:T(8,128)(2,1)S(1)}, bf16[1,16,1152]{2,1,0:T(8,128)(2,1)S(1)}, u32[]{:S(2)}, u32[]{:S(2)}) %collective-permute-start.12) | collective-permute-done | bytes 36896 | tf_op jit(solution)/shard_map/ppermute | solution.py:22
  60.1 2.2 %collective-permute-start.16 = (f32[2,1024]{1,0:T(2,128)S(1)}, f32[2,1024]{1,0:T(2,128)S(1)}, u32[]{:S(2)}, u32[]{:S(2)}) collective-permute-start(f32[2,1024]{1,0:T(2,128)S(1)} %get-tuple-element.54.refs_0_), channel_id=1, source_target_pairs={{0,24},{1,25},{2,26},{3,27},{4,28},{5,29},{6,30},{7,31},{8,16},{9,... | collective-permute-start | bytes 24584 | tf_op jit(solution)/shard_map/ppermute | solution.py:22
  62.2 2.3 %collective-permute-start.14 = (f32[2,1024]{1,0:T(2,128)S(1)}, f32[2,1024]{1,0:T(2,128)S(1)}, u32[]{:S(2)}, u32[]{:S(2)}) collective-permute-start(f32[2,1024]{1,0:T(2,128)S(1)} %get-tuple-element.54.refs_0_), channel_id=1, source_target_pairs={{0,8},{1,9},{2,10},{3,11},{4,12},{5,13},{6,14},{7,15},{8,0},{9,1},... | collective-permute-start | bytes 24584 | tf_op jit(solution)/shard_map/ppermute | solution.py:22
  64.5 1.1 collective-permute-done.16.refs_3_
  65.6 1.2 %collective-permute-done.15.refs_2_ = f32[2,1024]{1,0:T(2,128)S(1)} collective-permute-done((f32[2,1024]{1,0:T(2,128)S(1)}, f32[2,1024]{1,0:T(2,128)S(1)}, u32[]{:S(2)}, u32[]{:S(2)}) %collective-permute-start.15) | collective-permute-done | bytes 8224 | tf_op jit(solution)/shard_map/ppermute | solution.py:22
  66.8 1.6 %collective-permute-start.17 = (f32[2,1024]{1,0:T(2,128)S(1)}, f32[2,1024]{1,0:T(2,128)S(1)}, u32[]{:S(2)}, u32[]{:S(2)}) collective-permute-start(f32[2,1024]{1,0:T(2,128)S(1)} %tree_sum.1.sums_ref), channel_id=1, source_target_pairs={{0,4},{1,5},{2,6},{3,7},{4,0},{5,1},{6,2},{7,3},{8,12},{9,13},{10,... | collective-permute-start | bytes 24584 | tf_op jit(solution)/shard_map/ppermute | solution.py:22
  68.4 2.1 %collective-permute-done.17.other_sums_ref = f32[2,1024]{1,0:T(2,128)S(1)} collective-permute-done((f32[2,1024]{1,0:T(2,128)S(1)}, f32[2,1024]{1,0:T(2,128)S(1)}, u32[]{:S(2)}, u32[]{:S(2)}) %collective-permute-start.17) | collective-permute-done | bytes 8224 | tf_op jit(solution)/shard_map/ppermute | solution.py:22
  70.5 1.2 %head_grads.1 = (f32[1,1024]{1,0:T(1,128)}, bf16[16,1152]{1,0:T(8,128)(2,1)S(1)}, f32[16,1024]{1,0:T(8,128)S(1)}) custom-call(f32[2,1024]{1,0:T(2,128)S(1)} %tree_sum.1.sums_ref, f32[2,1024]{1,0:T(2,128)S(1)} %collective-permute-done.17.other_sums_ref, f32[16,1024]{1,0:T(8,128)S(1)} %get-tuple-element.55.pooled_ref, ...), custom_call_target="tpu_custom_call" | custom-call | tf_op jit(solution)/shard_map/head_grads/pallas_call | solution.py:56
  71.7 1.7 %collective-permute-start.20 = (bf16[16,1152]{1,0:T(8,128)(2,1)S(1)}, bf16[16,1152]{1,0:T(8,128)(2,1)S(1)}, u32[]{:S(2)}, u32[]{:S(2)}) collective-permute-start(bf16[16,1152]{1,0:T(8,128)(2,1)S(1)} %get-tuple-element.57.refs_0_), channel_id=1, source_target_pairs={{0,24},{1,25},{2,26},{3,27},{4,28},{5,29},{6,30},{7,31},{8,16},{9,... | collective-permute-start | bytes 110600 | tf_op jit(solution)/shard_map/ppermute | solution.py:22
  73.5 1.1 collective-permute-start.19
  74.5 1.6 %collective-permute-start.18 = (bf16[16,1152]{1,0:T(8,128)(2,1)S(1)}, bf16[16,1152]{1,0:T(8,128)(2,1)S(1)}, u32[]{:S(2)}, u32[]{:S(2)}) collective-permute-start(bf16[16,1152]{1,0:T(8,128)(2,1)S(1)} %get-tuple-element.57.refs_0_), channel_id=1, source_target_pairs={{0,8},{1,9},{2,10},{3,11},{4,12},{5,13},{6,14},{7,15},{8,0},{9,1},... | collective-permute-start | bytes 110600 | tf_op jit(solution)/shard_map/ppermute | solution.py:22
  76.1 1.4 %collective-permute-done.20.refs_3_ = bf16[16,1152]{1,0:T(8,128)(2,1)S(1)} collective-permute-done((bf16[16,1152]{1,0:T(8,128)(2,1)S(1)}, bf16[16,1152]{1,0:T(8,128)(2,1)S(1)}, u32[]{:S(2)}, u32[]{:S(2)}) %collective-permute-start.20) | collective-permute-done | bytes 36896 | tf_op jit(solution)/shard_map/ppermute | solution.py:22
  77.5 1.2 %collective-permute-done.19.refs_2_ = bf16[16,1152]{1,0:T(8,128)(2,1)S(1)} collective-permute-done((bf16[16,1152]{1,0:T(8,128)(2,1)S(1)}, bf16[16,1152]{1,0:T(8,128)(2,1)S(1)}, u32[]{:S(2)}, u32[]{:S(2)}) %collective-permute-start.19) | collective-permute-done | bytes 36896 | tf_op jit(solution)/shard_map/ppermute | solution.py:22
  78.7 1.7 %collective-permute-start.23 = (bf16[4,16,1152]{2,1,0:T(8,128)(2,1)S(1)}, bf16[4,16,1152]{2,1,0:T(8,128)(2,1)S(1)}, u32[]{:S(2)}, u32[]{:S(2)}) collective-permute-start(bf16[4,16,1152]{2,1,0:T(8,128)(2,1)S(1)} %stack.3.refs_0_), channel_id=1, source_target_pairs={{0,6},{1,7},{2,4},{3,5},{4,2},{5,3},{6,0},{7,1},{8,14},{9,15},{10,... | collective-permute-start | bytes 442376 | tf_op jit(solution)/shard_map/ppermute | solution.py:22
  80.4 1.3 %collective-permute-start.22 = (bf16[4,16,1152]{2,1,0:T(8,128)(2,1)S(1)}, bf16[4,16,1152]{2,1,0:T(8,128)(2,1)S(1)}, u32[]{:S(2)}, u32[]{:S(2)}) collective-permute-start(bf16[4,16,1152]{2,1,0:T(8,128)(2,1)S(1)} %stack.3.refs_0_), channel_id=1, source_target_pairs={{0,2},{1,3},{2,0},{3,1},{4,6},{5,7},{6,4},{7,5},{8,10},{9,11},{10,... | collective-permute-start | bytes 442376 | tf_op jit(solution)/shard_map/ppermute | solution.py:22
  82.3 0.7 copy-done.7
  83.0 3.0 %head_weight_grad.1 = (f32[1024,1024]{1,0:T(8,128)}, f32[8,128]{1,0:T(8,128)S(1)}) custom-call(f32[16,1024]{1,0:T(8,128)S(1)} %get-tuple-element.58.normed_ref, f32[1,1024]{1,0:T(1,128)S(1)} %copy-done.7), custom_call_target="tpu_custom_call" | custom-call | flops 100663296 | bytes 4194304 | tf_op jit(solution)/shard_map/head_weight_grad/pallas_call | solution.py:363
  87.0 2.0 %collective-permute-done.24.other_ref = bf16[8,32,1152]{2,1,0:T(8,128)(2,1)S(1)} collective-permute-done((bf16[8,32,1152]{2,1,0:T(8,128)(2,1)S(1)}, bf16[8,32,1152]{2,1,0:T(8,128)(2,1)S(1)}, u32[]{:S(2)}, u32[]{:S(2)}) %collective-permute-start.24) | collective-permute-done | bytes 589856 | tf_op jit(solution)/shard_map/ppermute | solution.py:22
  89.0 7.8 %grad.1 = (f32[8,32,1024]{2,1,0:T(8,128)S(1)}, bf16[8,32,1024]{2,1,0:T(8,128)(2,1)S(1)}, f32[1,1]{1,0:T(1,128)}) custom-call(s32[1]{0:T(128)} %bitcast.context_ref, bf16[8,32,1152]{2,1,0:T(8,128)(2,1)S(1)} %near.3.own_ref, bf16[8,32,1152]{2,1,0:T(8,128)(2,1)S(1)} %collective-permute-done.24.other_ref, bf16[768,8192]{1,0:T(8,128)(2,1)S(1)} %copy-done.2, ...), custom_call_target="tpu_custom_call" | custom-call | tf_op jit(solution)/shard_map/grad/pallas_call | solution.py:56
  97.0 1.8 %collective-permute-done.25.refs_1_ = bf16[8,32,1024]{2,1,0:T(8,128)(2,1)S(1)} collective-permute-done((bf16[8,32,1024]{2,1,0:T(8,128)(2,1)S(1)}, bf16[8,32,1024]{2,1,0:T(8,128)(2,1)S(1)}, u32[]{:S(2)}, u32[]{:S(2)}) %collective-permute-start.25) | collective-permute-done | bytes 524320 | tf_op jit(solution)/shard_map/ppermute | solution.py:22
  98.9 1.5 %collective-permute-start.26 = (bf16[4,16,1024]{2,1,0:T(8,128)(2,1)S(1)}, bf16[4,16,1024]{2,1,0:T(8,128)(2,1)S(1)}, u32[]{:S(2)}, u32[]{:S(2)}) collective-permute-start(bf16[4,16,1024]{2,1,0:T(8,128)(2,1)S(1)} %get-tuple-element.66), channel_id=1, source_target_pairs={{0,6},{1,7},{2,4},{3,5},{4,2},{5,3},{6,0},{7,1},{8,14},{9,15},{10,... | collective-permute-start | bytes 393224 | tf_op jit(solution)/shard_map/ppermute | solution.py:22
  100.3 1.1 collective-permute-start.27
  101.4 1.0 collective-permute-start.28
  102.4 3.8 %collective-permute-done.26.refs_1_ = bf16[4,16,1024]{2,1,0:T(8,128)(2,1)S(1)} collective-permute-done((bf16[4,16,1024]{2,1,0:T(8,128)(2,1)S(1)}, bf16[4,16,1024]{2,1,0:T(8,128)(2,1)S(1)}, u32[]{:S(2)}, u32[]{:S(2)}) %collective-permute-start.26) | collective-permute-done | bytes 131104 | tf_op jit(solution)/shard_map/ppermute | solution.py:22
  106.2 2.0 %collective-permute-done.27.refs_2_ = bf16[4,16,1024]{2,1,0:T(8,128)(2,1)S(1)} collective-permute-done((bf16[4,16,1024]{2,1,0:T(8,128)(2,1)S(1)}, bf16[4,16,1024]{2,1,0:T(8,128)(2,1)S(1)}, u32[]{:S(2)}, u32[]{:S(2)}) %collective-permute-start.27) | collective-permute-done | bytes 131104 | tf_op jit(solution)/shard_map/ppermute | solution.py:22
  108.3 2.3 %collective-permute-start.29 = (bf16[1,16,1024]{2,1,0:T(8,128)(2,1)S(1)}, bf16[1,16,1024]{2,1,0:T(8,128)(2,1)S(1)}, u32[]{:S(2)}, u32[]{:S(2)}) collective-permute-start(bf16[1,16,1024]{2,1,0:T(8,128)(2,1)S(1)} %get-tuple-element.70), channel_id=1, source_target_pairs={{0,24},{1,25},{2,26},{3,27},{4,28},{5,29},{6,30},{7,31},{8,16},{9,... | collective-permute-start | bytes 98312 | tf_op jit(solution)/shard_map/ppermute | solution.py:22
  111.2 1.6 %collective-permute-start.31 = (bf16[1,16,1024]{2,1,0:T(8,128)(2,1)S(1)}, bf16[1,16,1024]{2,1,0:T(8,128)(2,1)S(1)}, u32[]{:S(2)}, u32[]{:S(2)}) collective-permute-start(bf16[1,16,1024]{2,1,0:T(8,128)(2,1)S(1)} %get-tuple-element.72), channel_id=1, source_target_pairs={{0,8},{1,9},{2,10},{3,11},{4,12},{5,13},{6,14},{7,15},{8,0},{9,1},... | collective-permute-start | bytes 98312 | tf_op jit(solution)/shard_map/ppermute | solution.py:22
  112.7 1.3 %collective-permute-done.29.refs_1_ = bf16[1,16,1024]{2,1,0:T(8,128)(2,1)S(1)} collective-permute-done((bf16[1,16,1024]{2,1,0:T(8,128)(2,1)S(1)}, bf16[1,16,1024]{2,1,0:T(8,128)(2,1)S(1)}, u32[]{:S(2)}, u32[]{:S(2)}) %collective-permute-start.29) | collective-permute-done | bytes 32800 | tf_op jit(solution)/shard_map/ppermute | solution.py:22
  114.1 1.4 %collective-permute-done.30.refs_2_ = bf16[1,16,1024]{2,1,0:T(8,128)(2,1)S(1)} collective-permute-done((bf16[1,16,1024]{2,1,0:T(8,128)(2,1)S(1)}, bf16[1,16,1024]{2,1,0:T(8,128)(2,1)S(1)}, u32[]{:S(2)}, u32[]{:S(2)}) %collective-permute-start.30) | collective-permute-done | bytes 32800 | tf_op jit(solution)/shard_map/ppermute | solution.py:22
  115.5 0.6 far_sum.1
  (48 shorter events, 6.5 us)
Async XLA Ops:
  0.6 58.8 %copy-start.3 = (bf16[1024,1024]{1,0:T(8,128)(2,1)S(1)}, bf16[1024,1024]{1,0:T(8,128)(2,1)}, u32[]{:S(2)}) copy-start(bf16[1024,1024]{1,0:T(8,128)(2,1)} %weight_ref.1) | copy-start | bytes 6291460
  0.6 58.8 %copy-start.4 = (f32[1024]{0:T(1024)S(1)}, f32[1024]{0:T(1024)}, u32[]{:S(2)}) copy-start(f32[1024]{0:T(1024)} %param.10) | copy-start | bytes 12292
  0.7 15.0 %collective-permute-start = (bf16[16,1024]{1,0:T(8,128)(2,1)}, bf16[16,1024]{1,0:T(8,128)(2,1)S(1)}, u32[]{:S(2)}, u32[]{:S(2)}) collective-permute-start(bf16[16,1024]{1,0:T(8,128)(2,1)} %queries_ref.1), channel_id=1, source_target_pairs={{0,8},{1,9},{2,10},{3,11},{4,12},{5,13},{6,14},{7,15},{8,0},{9,1},... | collective-permute-start | bytes 98312 | tf_op jit(solution)/shard_map/ppermute | solution.py:22
  3.7 11.9 %collective-permute-start.2 = (bf16[16,1024]{1,0:T(8,128)(2,1)}, bf16[16,1024]{1,0:T(8,128)(2,1)S(1)}, u32[]{:S(2)}, u32[]{:S(2)}) collective-permute-start(bf16[16,1024]{1,0:T(8,128)(2,1)} %queries_ref.1), channel_id=1, source_target_pairs={{0,24},{1,25},{2,26},{3,27},{4,28},{5,29},{6,30},{7,31},{8,16},{9,... | collective-permute-start | bytes 98312 | tf_op jit(solution)/shard_map/ppermute | solution.py:22
  6.2 9.4 %collective-permute-start.1 = (bf16[16,1024]{1,0:T(8,128)(2,1)}, bf16[16,1024]{1,0:T(8,128)(2,1)S(1)}, u32[]{:S(2)}, u32[]{:S(2)}) collective-permute-start(bf16[16,1024]{1,0:T(8,128)(2,1)} %queries_ref.1), channel_id=1, source_target_pairs={{0,16},{1,17},{2,18},{3,19},{4,20},{5,21},{6,22},{7,23},{8,24},{9,... | collective-permute-start | bytes 98312 | tf_op jit(solution)/shard_map/ppermute | solution.py:22
  11.1 4.6 %copy-start = (bf16[768,8192]{1,0:T(8,128)(2,1)}, bf16[768,8192]{1,0:T(8,128)(2,1)S(1)}, u32[]{:S(2)}) copy-start(bf16[768,8192]{1,0:T(8,128)(2,1)S(1)} %get-tuple-element.40.tokens_ref) | copy-start | bytes 37748740
  15.6 54.9 %copy-start.5 = (f32[1024]{0:T(1024)S(1)}, f32[1024]{0:T(1024)}, u32[]{:S(2)}) copy-start(f32[1024]{0:T(1024)} %param.12) | copy-start | bytes 12292
  15.6 54.9 %copy-start.6 = (s32[1024]{0:T(1024)S(1)}, s32[1024]{0:T(1024)}, u32[]{:S(2)}) copy-start(s32[1024]{0:T(1024)} %param.13) | copy-start | bytes 12292
  15.7 6.6 %collective-permute-start.5 = (bf16[4,16,1024]{2,1,0:T(8,128)(2,1)S(1)}, bf16[4,16,1024]{2,1,0:T(8,128)(2,1)S(1)}, u32[]{:S(2)}, u32[]{:S(2)}) collective-permute-start(bf16[4,16,1024]{2,1,0:T(8,128)(2,1)S(1)} %stack.2.refs_0_), channel_id=1, source_target_pairs={{0,6},{1,7},{2,4},{3,5},{4,2},{5,3},{6,0},{7,1},{8,14},{9,15},{10,... | collective-permute-start | bytes 393224 | tf_op jit(solution)/shard_map/ppermute | solution.py:22
  18.2 5.9 %collective-permute-start.4 = (bf16[4,16,1024]{2,1,0:T(8,128)(2,1)S(1)}, bf16[4,16,1024]{2,1,0:T(8,128)(2,1)S(1)}, u32[]{:S(2)}, u32[]{:S(2)}) collective-permute-start(bf16[4,16,1024]{2,1,0:T(8,128)(2,1)S(1)} %stack.2.refs_0_), channel_id=1, source_target_pairs={{0,2},{1,3},{2,0},{3,1},{4,6},{5,7},{6,4},{7,5},{8,10},{9,11},{10,... | collective-permute-start | bytes 393224 | tf_op jit(solution)/shard_map/ppermute | solution.py:22
  18.7 5.5 %collective-permute-start.3 = (bf16[4,16,1024]{2,1,0:T(8,128)(2,1)S(1)}, bf16[4,16,1024]{2,1,0:T(8,128)(2,1)S(1)}, u32[]{:S(2)}, u32[]{:S(2)}) collective-permute-start(bf16[4,16,1024]{2,1,0:T(8,128)(2,1)S(1)} %stack.2.refs_0_), channel_id=1, source_target_pairs={{0,4},{1,5},{2,6},{3,7},{4,0},{5,1},{6,2},{7,3},{8,12},{9,13},{10,... | collective-permute-start | bytes 393224 | tf_op jit(solution)/shard_map/ppermute | solution.py:22
  24.2 2.0 %collective-permute-start.6 = (bf16[8,32,1024]{2,1,0:T(8,128)(2,1)S(1)}, bf16[8,32,1024]{2,1,0:T(8,128)(2,1)S(1)}, u32[]{:S(2)}, u32[]{:S(2)}) collective-permute-start(bf16[8,32,1024]{2,1,0:T(8,128)(2,1)S(1)} %near.2.own_ref), channel_id=1, source_target_pairs={{0,1},{1,0},{2,3},{3,2},{4,5},{5,4},{6,7},{7,6},{8,9},{9,8},{10,11... | collective-permute-start | bytes 1572872 | tf_op jit(solution)/shard_map/ppermute | solution.py:22
  26.2 4.6 %copy-start.1 = (bf16[768,8192]{1,0:T(8,128)(2,1)S(1)}, bf16[768,8192]{1,0:T(8,128)(2,1)}, u32[]{:S(2)}) copy-start(bf16[768,8192]{1,0:T(8,128)(2,1)} %copy-done) | copy-start | bytes 37748740
  30.8 58.2 %copy-start.2 = (bf16[768,8192]{1,0:T(8,128)(2,1)S(1)}, bf16[768,8192]{1,0:T(8,128)(2,1)}, u32[]{:S(2)}) copy-start(bf16[768,8192]{1,0:T(8,128)(2,1)} %copy-done) | copy-start | bytes 37748740
  38.7 2.1 %collective-permute-start.7 = (bf16[8,32,1152]{2,1,0:T(8,128)(2,1)S(1)}, bf16[8,32,1152]{2,1,0:T(8,128)(2,1)S(1)}, u32[]{:S(2)}, u32[]{:S(2)}) collective-permute-start(bf16[8,32,1152]{2,1,0:T(8,128)(2,1)S(1)} %get-tuple-element.42), channel_id=1, source_target_pairs={{0,1},{1,0},{2,3},{3,2},{4,5},{5,4},{6,7},{7,6},{8,9},{9,8},{10,11... | collective-permute-start | bytes 1769480 | tf_op jit(solution)/shard_map/ppermute | solution.py:22
  41.2 7.7 %collective-permute-start.8 = (bf16[4,16,1152]{2,1,0:T(8,128)(2,1)S(1)}, bf16[4,16,1152]{2,1,0:T(8,128)(2,1)S(1)}, u32[]{:S(2)}, u32[]{:S(2)}) collective-permute-start(bf16[4,16,1152]{2,1,0:T(8,128)(2,1)S(1)} %get-tuple-element.45), channel_id=1, source_target_pairs={{0,6},{1,7},{2,4},{3,5},{4,2},{5,3},{6,0},{7,1},{8,14},{9,15},{10,... | collective-permute-start | bytes 442376 | tf_op jit(solution)/shard_map/ppermute | solution.py:22
  42.9 8.3 %collective-permute-start.9 = (bf16[4,16,1152]{2,1,0:T(8,128)(2,1)S(1)}, bf16[4,16,1152]{2,1,0:T(8,128)(2,1)S(1)}, u32[]{:S(2)}, u32[]{:S(2)}) collective-permute-start(bf16[4,16,1152]{2,1,0:T(8,128)(2,1)S(1)} %get-tuple-element.46), channel_id=1, source_target_pairs={{0,2},{1,3},{2,0},{3,1},{4,6},{5,7},{6,4},{7,5},{8,10},{9,11},{10,... | collective-permute-start | bytes 442376 | tf_op jit(solution)/shard_map/ppermute | solution.py:22
  44.2 7.0 %collective-permute-start.10 = (bf16[4,16,1152]{2,1,0:T(8,128)(2,1)S(1)}, bf16[4,16,1152]{2,1,0:T(8,128)(2,1)S(1)}, u32[]{:S(2)}, u32[]{:S(2)}) collective-permute-start(bf16[4,16,1152]{2,1,0:T(8,128)(2,1)S(1)} %get-tuple-element.47), channel_id=1, source_target_pairs={{0,4},{1,5},{2,6},{3,7},{4,0},{5,1},{6,2},{7,3},{8,12},{9,13},{10,... | collective-permute-start | bytes 442376 | tf_op jit(solution)/shard_map/ppermute | solution.py:22
  51.6 5.9 %collective-permute-start.11 = (bf16[1,16,1152]{2,1,0:T(8,128)(2,1)S(1)}, bf16[1,16,1152]{2,1,0:T(8,128)(2,1)S(1)}, u32[]{:S(2)}, u32[]{:S(2)}) collective-permute-start(bf16[1,16,1152]{2,1,0:T(8,128)(2,1)S(1)} %get-tuple-element.50), channel_id=1, source_target_pairs={{0,24},{1,25},{2,26},{3,27},{4,28},{5,29},{6,30},{7,31},{8,16},{9,... | collective-permute-start | bytes 110600 | tf_op jit(solution)/shard_map/ppermute | solution.py:22
  54.3 5.2 %collective-permute-start.12 = (bf16[1,16,1152]{2,1,0:T(8,128)(2,1)S(1)}, bf16[1,16,1152]{2,1,0:T(8,128)(2,1)S(1)}, u32[]{:S(2)}, u32[]{:S(2)}) collective-permute-start(bf16[1,16,1152]{2,1,0:T(8,128)(2,1)S(1)} %get-tuple-element.51), channel_id=1, source_target_pairs={{0,16},{1,17},{2,18},{3,19},{4,20},{5,21},{6,22},{7,23},{8,24},{9,... | collective-permute-start | bytes 110600 | tf_op jit(solution)/shard_map/ppermute | solution.py:22
  54.6 4.8 %collective-permute-start.13 = (bf16[1,16,1152]{2,1,0:T(8,128)(2,1)S(1)}, bf16[1,16,1152]{2,1,0:T(8,128)(2,1)S(1)}, u32[]{:S(2)}, u32[]{:S(2)}) collective-permute-start(bf16[1,16,1152]{2,1,0:T(8,128)(2,1)S(1)} %get-tuple-element.52), channel_id=1, source_target_pairs={{0,8},{1,9},{2,10},{3,11},{4,12},{5,13},{6,14},{7,15},{8,0},{9,1},... | collective-permute-start | bytes 110600 | tf_op jit(solution)/shard_map/ppermute | solution.py:22
  60.1 5.5 %collective-permute-start.16 = (f32[2,1024]{1,0:T(2,128)S(1)}, f32[2,1024]{1,0:T(2,128)S(1)}, u32[]{:S(2)}, u32[]{:S(2)}) collective-permute-start(f32[2,1024]{1,0:T(2,128)S(1)} %get-tuple-element.54.refs_0_), channel_id=1, source_target_pairs={{0,24},{1,25},{2,26},{3,27},{4,28},{5,29},{6,30},{7,31},{8,16},{9,... | collective-permute-start | bytes 24584 | tf_op jit(solution)/shard_map/ppermute | solution.py:22
  62.2 4.5 %collective-permute-start.15 = (f32[2,1024]{1,0:T(2,128)S(1)}, f32[2,1024]{1,0:T(2,128)S(1)}, u32[]{:S(2)}, u32[]{:S(2)}) collective-permute-start(f32[2,1024]{1,0:T(2,128)S(1)} %get-tuple-element.54.refs_0_), channel_id=1, source_target_pairs={{0,16},{1,17},{2,18},{3,19},{4,20},{5,21},{6,22},{7,23},{8,24},{9,... | collective-permute-start | bytes 24584 | tf_op jit(solution)/shard_map/ppermute | solution.py:22
  62.2 4.5 %collective-permute-start.14 = (f32[2,1024]{1,0:T(2,128)S(1)}, f32[2,1024]{1,0:T(2,128)S(1)}, u32[]{:S(2)}, u32[]{:S(2)}) collective-permute-start(f32[2,1024]{1,0:T(2,128)S(1)} %get-tuple-element.54.refs_0_), channel_id=1, source_target_pairs={{0,8},{1,9},{2,10},{3,11},{4,12},{5,13},{6,14},{7,15},{8,0},{9,1},... | collective-permute-start | bytes 24584 | tf_op jit(solution)/shard_map/ppermute | solution.py:22
  66.8 3.7 %collective-permute-start.17 = (f32[2,1024]{1,0:T(2,128)S(1)}, f32[2,1024]{1,0:T(2,128)S(1)}, u32[]{:S(2)}, u32[]{:S(2)}) collective-permute-start(f32[2,1024]{1,0:T(2,128)S(1)} %tree_sum.1.sums_ref), channel_id=1, source_target_pairs={{0,4},{1,5},{2,6},{3,7},{4,0},{5,1},{6,2},{7,3},{8,12},{9,13},{10,... | collective-permute-start | bytes 24584 | tf_op jit(solution)/shard_map/ppermute | solution.py:22
  71.7 5.8 %collective-permute-start.20 = (bf16[16,1152]{1,0:T(8,128)(2,1)S(1)}, bf16[16,1152]{1,0:T(8,128)(2,1)S(1)}, u32[]{:S(2)}, u32[]{:S(2)}) collective-permute-start(bf16[16,1152]{1,0:T(8,128)(2,1)S(1)} %get-tuple-element.57.refs_0_), channel_id=1, source_target_pairs={{0,24},{1,25},{2,26},{3,27},{4,28},{5,29},{6,30},{7,31},{8,16},{9,... | collective-permute-start | bytes 110600 | tf_op jit(solution)/shard_map/ppermute | solution.py:22
  73.5 5.3 %collective-permute-start.19 = (bf16[16,1152]{1,0:T(8,128)(2,1)S(1)}, bf16[16,1152]{1,0:T(8,128)(2,1)S(1)}, u32[]{:S(2)}, u32[]{:S(2)}) collective-permute-start(bf16[16,1152]{1,0:T(8,128)(2,1)S(1)} %get-tuple-element.57.refs_0_), channel_id=1, source_target_pairs={{0,16},{1,17},{2,18},{3,19},{4,20},{5,21},{6,22},{7,23},{8,24},{9,... | collective-permute-start | bytes 110600 | tf_op jit(solution)/shard_map/ppermute | solution.py:22
  74.5 4.2 %collective-permute-start.18 = (bf16[16,1152]{1,0:T(8,128)(2,1)S(1)}, bf16[16,1152]{1,0:T(8,128)(2,1)S(1)}, u32[]{:S(2)}, u32[]{:S(2)}) collective-permute-start(bf16[16,1152]{1,0:T(8,128)(2,1)S(1)} %get-tuple-element.57.refs_0_), channel_id=1, source_target_pairs={{0,8},{1,9},{2,10},{3,11},{4,12},{5,13},{6,14},{7,15},{8,0},{9,1},... | collective-permute-start | bytes 110600 | tf_op jit(solution)/shard_map/ppermute | solution.py:22
  78.7 7.2 %collective-permute-start.23 = (bf16[4,16,1152]{2,1,0:T(8,128)(2,1)S(1)}, bf16[4,16,1152]{2,1,0:T(8,128)(2,1)S(1)}, u32[]{:S(2)}, u32[]{:S(2)}) collective-permute-start(bf16[4,16,1152]{2,1,0:T(8,128)(2,1)S(1)} %stack.3.refs_0_), channel_id=1, source_target_pairs={{0,6},{1,7},{2,4},{3,5},{4,2},{5,3},{6,0},{7,1},{8,14},{9,15},{10,... | collective-permute-start | bytes 442376 | tf_op jit(solution)/shard_map/ppermute | solution.py:22
  80.4 6.0 %collective-permute-start.22 = (bf16[4,16,1152]{2,1,0:T(8,128)(2,1)S(1)}, bf16[4,16,1152]{2,1,0:T(8,128)(2,1)S(1)}, u32[]{:S(2)}, u32[]{:S(2)}) collective-permute-start(bf16[4,16,1152]{2,1,0:T(8,128)(2,1)S(1)} %stack.3.refs_0_), channel_id=1, source_target_pairs={{0,2},{1,3},{2,0},{3,1},{4,6},{5,7},{6,4},{7,5},{8,10},{9,11},{10,... | collective-permute-start | bytes 442376 | tf_op jit(solution)/shard_map/ppermute | solution.py:22
  81.7 5.1 %collective-permute-start.21 = (bf16[4,16,1152]{2,1,0:T(8,128)(2,1)S(1)}, bf16[4,16,1152]{2,1,0:T(8,128)(2,1)S(1)}, u32[]{:S(2)}, u32[]{:S(2)}) collective-permute-start(bf16[4,16,1152]{2,1,0:T(8,128)(2,1)S(1)} %stack.3.refs_0_), channel_id=1, source_target_pairs={{0,4},{1,5},{2,6},{3,7},{4,0},{5,1},{6,2},{7,3},{8,12},{9,13},{10,... | collective-permute-start | bytes 442376 | tf_op jit(solution)/shard_map/ppermute | solution.py:22
  82.3 0.7 copy-start.7
  86.9 2.1 %collective-permute-start.24 = (bf16[8,32,1152]{2,1,0:T(8,128)(2,1)S(1)}, bf16[8,32,1152]{2,1,0:T(8,128)(2,1)S(1)}, u32[]{:S(2)}, u32[]{:S(2)}) collective-permute-start(bf16[8,32,1152]{2,1,0:T(8,128)(2,1)S(1)} %near.3.own_ref), channel_id=1, source_target_pairs={{0,1},{1,0},{2,3},{3,2},{4,5},{5,4},{6,7},{7,6},{8,9},{9,8},{10,11... | collective-permute-start | bytes 1769480 | tf_op jit(solution)/shard_map/ppermute | solution.py:22
  96.8 2.0 %collective-permute-start.25 = (bf16[8,32,1024]{2,1,0:T(8,128)(2,1)S(1)}, bf16[8,32,1024]{2,1,0:T(8,128)(2,1)S(1)}, u32[]{:S(2)}, u32[]{:S(2)}) collective-permute-start(bf16[8,32,1024]{2,1,0:T(8,128)(2,1)S(1)} %get-tuple-element.64), channel_id=1, source_target_pairs={{0,1},{1,0},{2,3},{3,2},{4,5},{5,4},{6,7},{7,6},{8,9},{9,8},{10,11... | collective-permute-start | bytes 1572872 | tf_op jit(solution)/shard_map/ppermute | solution.py:22
  98.9 7.3 %collective-permute-start.26 = (bf16[4,16,1024]{2,1,0:T(8,128)(2,1)S(1)}, bf16[4,16,1024]{2,1,0:T(8,128)(2,1)S(1)}, u32[]{:S(2)}, u32[]{:S(2)}) collective-permute-start(bf16[4,16,1024]{2,1,0:T(8,128)(2,1)S(1)} %get-tuple-element.66), channel_id=1, source_target_pairs={{0,6},{1,7},{2,4},{3,5},{4,2},{5,3},{6,0},{7,1},{8,14},{9,15},{10,... | collective-permute-start | bytes 393224 | tf_op jit(solution)/shard_map/ppermute | solution.py:22
  100.3 7.9 %collective-permute-start.27 = (bf16[4,16,1024]{2,1,0:T(8,128)(2,1)S(1)}, bf16[4,16,1024]{2,1,0:T(8,128)(2,1)S(1)}, u32[]{:S(2)}, u32[]{:S(2)}) collective-permute-start(bf16[4,16,1024]{2,1,0:T(8,128)(2,1)S(1)} %get-tuple-element.67), channel_id=1, source_target_pairs={{0,2},{1,3},{2,0},{3,1},{4,6},{5,7},{6,4},{7,5},{8,10},{9,11},{10,... | collective-permute-start | bytes 393224 | tf_op jit(solution)/shard_map/ppermute | solution.py:22
  101.4 6.8 %collective-permute-start.28 = (bf16[4,16,1024]{2,1,0:T(8,128)(2,1)S(1)}, bf16[4,16,1024]{2,1,0:T(8,128)(2,1)S(1)}, u32[]{:S(2)}, u32[]{:S(2)}) collective-permute-start(bf16[4,16,1024]{2,1,0:T(8,128)(2,1)S(1)} %get-tuple-element.68), channel_id=1, source_target_pairs={{0,4},{1,5},{2,6},{3,7},{4,0},{5,1},{6,2},{7,3},{8,12},{9,13},{10,... | collective-permute-start | bytes 393224 | tf_op jit(solution)/shard_map/ppermute | solution.py:22
  108.3 5.8 %collective-permute-start.29 = (bf16[1,16,1024]{2,1,0:T(8,128)(2,1)S(1)}, bf16[1,16,1024]{2,1,0:T(8,128)(2,1)S(1)}, u32[]{:S(2)}, u32[]{:S(2)}) collective-permute-start(bf16[1,16,1024]{2,1,0:T(8,128)(2,1)S(1)} %get-tuple-element.70), channel_id=1, source_target_pairs={{0,24},{1,25},{2,26},{3,27},{4,28},{5,29},{6,30},{7,31},{8,16},{9,... | collective-permute-start | bytes 98312 | tf_op jit(solution)/shard_map/ppermute | solution.py:22
  110.6 4.9 %collective-permute-start.30 = (bf16[1,16,1024]{2,1,0:T(8,128)(2,1)S(1)}, bf16[1,16,1024]{2,1,0:T(8,128)(2,1)S(1)}, u32[]{:S(2)}, u32[]{:S(2)}) collective-permute-start(bf16[1,16,1024]{2,1,0:T(8,128)(2,1)S(1)} %get-tuple-element.71), channel_id=1, source_target_pairs={{0,16},{1,17},{2,18},{3,19},{4,20},{5,21},{6,22},{7,23},{8,24},{9,... | collective-permute-start | bytes 98312 | tf_op jit(solution)/shard_map/ppermute | solution.py:22
  111.2 4.3 %collective-permute-start.31 = (bf16[1,16,1024]{2,1,0:T(8,128)(2,1)S(1)}, bf16[1,16,1024]{2,1,0:T(8,128)(2,1)S(1)}, u32[]{:S(2)}, u32[]{:S(2)}) collective-permute-start(bf16[1,16,1024]{2,1,0:T(8,128)(2,1)S(1)} %get-tuple-element.72), channel_id=1, source_target_pairs={{0,8},{1,9},{2,10},{3,11},{4,12},{5,13},{6,14},{7,15},{8,0},{9,1},... | collective-permute-start | bytes 98312 | tf_op jit(solution)/shard_map/ppermute | solution.py:22

commit v5 on v4

--- a/solution.py
+++ b/solution.py
@@ -132,41 +132,30 @@
     )(*[pltpu.with_memory_space_constraint(x, pltpu.HBM) for x in arrays])
 
 
-def columns_of(context_ref, contexts, p, width, at=0, size=None):
-    start = pl.multiple_of((context_ref[0] ^ relative_blocks(contexts)[p]) * width, LANES)
+def columns_of(contexts, p, width, at=0, size=None):
+    start = pl.multiple_of((lax.axis_index("ctx") ^ relative_blocks(contexts)[p]) * width, LANES)
     return pl.ds(start + at, size or width)
 
 
-def project(context_ref, own_ref, other_ref, tokens_ref, width, tile=256):
+def project(own_ref, other_ref, tokens_ref, width, tile=256):
     contexts = own_ref.shape[0]
     tiles = []
     for at in range(0, tokens_ref.shape[0], tile):
         total = None
         for p in range(contexts):
             both = jnp.concatenate([own_ref[p], other_ref[p]], axis=0)[:, :width]
-            block = tokens_ref[at : at + tile, columns_of(context_ref, contexts, p, width)]
-            part = lax.dot_general(block, both, (((1,), (1,)), ((), ())), preferred_element_type=F32)
+            block = tokens_ref[at : at + tile, columns_of(contexts, p, width)]
+            part = lax.dot_general(both, block, (((1,), (1,)), ((), ())), preferred_element_type=F32)
             total = part if total is None else total + part
-        tiles.append(total.T)
+        tiles.append(total)
     return jnp.concatenate(tiles, axis=1)
 
 
-def project_grad(context_ref, own_ref, other_ref, tokens_ref, width):
-    contexts = own_ref.shape[0]
-    total = None
-    for p in range(contexts):
-        both = jnp.concatenate([own_ref[p], other_ref[p]], axis=0)[:, :width]
-        block = tokens_ref[:, columns_of(context_ref, contexts, p, width)]
-        part = lax.dot_general(both, block, (((1,), (1,)), ((), ())), preferred_element_type=F32)
-        total = part if total is None else total + part
-    return total
-
-
-def spread(context_ref, left, tokens_ref, keep_ref, send_ref, extra, tile):
+def spread(left, tokens_ref, keep_ref, send_ref, extra, tile=256):
     contexts, half, width = keep_ref.shape
     for p in range(contexts):
         for at in range(0, width, tile):
-            block = tokens_ref[:, columns_of(context_ref, contexts, p, width, at, tile)]
+            block = tokens_ref[:, columns_of(contexts, p, width, at, tile)]
             part = jnp.dot(left, block, preferred_element_type=F32)
             keep_ref[p, :, at : at + tile] = part[:half]
             send_ref[p, :, at : at + tile] = part[half:].astype(BF16)
@@ -174,24 +163,25 @@
             send_ref[p, :, width:] = extra
 
 
-def pool_kernel(context_ref, count_ref, own_ref, other_ref, tokens_ref, keep_ref, send_ref, peak_ref, w_ref):
-    scores = project(context_ref, own_ref, other_ref, tokens_ref, keep_ref.shape[2])
-    valid = lax.broadcasted_iota(jnp.int32, scores.shape, 1) < count_ref[0]
+def pool_kernel(length_ref, own_ref, other_ref, tokens_ref, keep_ref, send_ref, peak_ref, w_ref):
+    scores = project(own_ref, other_ref, tokens_ref, keep_ref.shape[2])
+    shard = lax.axis_index("ctx") * lax.axis_size("cls") + lax.axis_index("cls")
+    valid = lax.broadcasted_iota(jnp.int32, scores.shape, 1) < length_ref[0] - shard * scores.shape[1]
     peak = jnp.max(jnp.where(valid, scores, MASKED), axis=1, keepdims=True)
     weights = jnp.where(valid, jnp.exp(scores - peak), 0.0)
     w_ref[...] = weights
     peak_ref[...] = jnp.broadcast_to(peak, peak_ref.shape)
     half = keep_ref.shape[1]
-    spread(context_ref, weights.astype(BF16), tokens_ref, keep_ref, send_ref, into_lanes([peak[half:]], half), 256)
-
-
-def grad_kernel(scale, classes, context_ref, own_ref, other_ref, tokens_ref, w_ref, peak_ref, keep_ref, send_ref, loss_ref):
+    spread(weights.astype(BF16), tokens_ref, keep_ref, send_ref, into_lanes([peak[half:]], half))
+
+
+def grad_kernel(scale, classes, own_ref, other_ref, tokens_ref, w_ref, peak_ref, keep_ref, send_ref, loss_ref):
     width = keep_ref.shape[2]
-    projected = project_grad(context_ref, own_ref, other_ref, tokens_ref, width)
+    projected = project(own_ref, other_ref, tokens_ref, width)
     own, other = own_ref[0], other_ref[0]
     top = jnp.concatenate([from_lanes(own, width, 0), from_lanes(other, width, 0)], axis=0)
     weights = w_ref[...] * jnp.exp(peak_ref[:, :1] - top)
-    spread(context_ref, (weights * projected).astype(BF16), tokens_ref, keep_ref, send_ref, None, width)
+    spread((weights * projected).astype(BF16), tokens_ref, keep_ref, send_ref, None)
     rows = classes // 2
     each = own.shape[0] // rows
     sums = []
@@ -315,7 +305,7 @@
 
 
 def head_grads_kernel(
-    full_width, sums_ref, other_sums_ref, pooled_ref, top_ref, gain_ref, weight_ref, bias_ref, label_ref, bias_grad_ref, grad_ref, normed_ref
+    full_width, sums_ref, other_sums_ref, pooled_ref, top_ref, gain_ref, weight_ref, bias_ref, label_ref, bias_grad_ref, copy_ref, grad_ref, normed_ref
 ):
     pooled, gain = pooled_ref[...], gain_ref[...]
     heads, width = pooled.shape
@@ -331,6 +321,7 @@
     loss = jnp.sum(losses, axis=1, keepdims=True)
     bias_grad = jax.nn.sigmoid(logits) - target
     bias_grad_ref[...] = bias_grad
+    copy_ref[...] = bias_grad
     by_head = jnp.where(mask, bias_grad, 0.0)
     high = by_head.astype(BF16)
     low = (by_head - high.astype(F32)).astype(BF16)
@@ -377,17 +368,12 @@
 
 def shards(tokens, doc_length, queries, norm_gain, head_weight, head_bias, labels):
     contexts, classes = lax.axis_size("ctx"), lax.axis_size("cls")
-    context_index, class_index = lax.axis_index("ctx"), lax.axis_index("cls")
     token_count = tokens.shape[0]
     rows, width = queries.shape
     full_width = width * contexts
     heads = rows * classes
     half = heads // 2
     columns = labels.shape[0]
-    offset = (context_index * classes + class_index) * token_count
-    valid_count = jnp.clip(doc_length - offset, 0, token_count)
-
-    context = context_index.astype(jnp.int32)[None]
     held, queries_here = load(tokens, queries)
     own, other = gather(queries, queries_here)
     keep, send, own_peak, weights = call(
@@ -399,8 +385,8 @@
             ((heads, token_count), F32),
         ],
         "pool",
-        [context, valid_count, own, other, held],
-        smem_args=(0, 1),
+        [doc_length, own, other, held],
+        smem_args=(0,),
         limit=16,
     )
     parts = scatter_sum(keep, send, own_peak)
@@ -413,20 +399,19 @@
     )
     far_sums = [swap(sums, *step) for step in far_steps()[::-1]]
     (sums,) = call(tree_sum_kernel, [((2, columns), F32)], "tree_sum", [sums, *far_sums])
-    bias_grad, pooled_grad, normed = call(
+    bias_grad, bias_grad_here, pooled_grad, normed = call(
         functools.partial(head_grads_kernel, full_width),
-        [((1, columns), F32), ((rows, width + LANES), BF16), ((rows, width), F32)],
+        [((1, columns), F32), ((1, columns), F32), ((rows, width + LANES), BF16), ((rows, width), F32)],
         "head_grads",
         [sums, swap(sums, 1, 0), pooled, top, gain, head_weight, head_bias[None, :], labels[None, :]],
     )
-    head_grad, done = head_weight_grad(normed, bias_grad)
+    head_grad, done = head_weight_grad(normed, bias_grad_here)
     own, other = gather(pooled_grad, after=(done,))
     keep, send, loss = call(
         functools.partial(grad_kernel, 1.0 / (columns * classes), classes),
         [((contexts, half, width), F32), ((contexts, half, width), BF16), ((1, 1), F32)],
         "grad",
-        [context, own, other, held, weights, own_peak],
-        smem_args=(0,),
+        [own, other, held, weights, own_peak],
         limit=16,
     )
     (query_grad,) = call(far_sum_kernel, [((rows, width), F32)], "far_sum", scatter_sum(keep, send, None))

time: 116 us -> 107 us (0.922)
  local copies, waits for them, and re-layouts: 9.83 us -> 0.02 us
    unnamed x16 -> x8, local copies, waits for them, and re-layouts: 9.83 us -> 0.02 us
  transfers between devices with their start and end apart: 32 -> 32, of which waited for: 22 -> 23; matrix products, arithmetic and copies ran while one was open for 0% -> 0% of each run, Pallas kernels for 7% -> 7%
where the time goes in v5:
time: 107 us
  starting transfers between devices  39.7 us (37%)
  waiting for transfers between devices  39 us (36%)
  Pallas kernels  27 us (25%)
  between operations  1.44 us (1%)
    ppermute x32, starting transfers between devices, swap(): return lax.ppermute(x, ('ctx', 'cls'), pairs)  39.7 us
    ppermute x32, waiting for transfers between devices, swap(): return lax.ppermute(x, ('ctx', 'cls'), pairs)  39 us
    pallas_call x14, Pallas kernels, call(): return list(run(*args))  19.4 us
    pallas_call x1, Pallas kernels, load(): pl.pallas_call(load_kernel, out_shape=[pltpu.VMEM(x.shape, x.dtype) for x...  4.72 us
    pallas_call x1, Pallas kernels, head_weight_grad(): pl.pallas_call(functools.partial(head_weight_grad_kernel, columns // rows...  2.95 us
  transfers between devices with their start and end apart: 32, of which 23 were waited for; matrix products, arithmetic and copies ran while one was open for 0% of the time, Pallas kernels for 7%

profile of v5, /device:TPU:0, one launch (start us, length us, event | category | flops | bytes accessed | tf_op | source)
XLA Modules:
  0.0 107.2 jit_solution(14929759556065319989)
XLA Ops:
  0.7 3.1 %collective-permute-start = (bf16[16,1024]{1,0:T(8,128)(2,1)}, bf16[16,1024]{1,0:T(8,128)(2,1)S(1)}, u32[]{:S(2)}, u32[]{:S(2)}) collective-permute-start(bf16[16,1024]{1,0:T(8,128)(2,1)} %queries_ref.1), channel_id=1, source_target_pairs={{0,8},{1,9},{2,10},{3,11},{4,12},{5,13},{6,14},{7,15},{8,0},{9,1},... | collective-permute-start | bytes 98312 | tf_op jit(solution)/shard_map/ppermute | solution.py:22
  3.7 2.5 %collective-permute-start.2 = (bf16[16,1024]{1,0:T(8,128)(2,1)}, bf16[16,1024]{1,0:T(8,128)(2,1)S(1)}, u32[]{:S(2)}, u32[]{:S(2)}) collective-permute-start(bf16[16,1024]{1,0:T(8,128)(2,1)} %queries_ref.1), channel_id=1, source_target_pairs={{0,24},{1,25},{2,26},{3,27},{4,28},{5,29},{6,30},{7,31},{8,16},{9,... | collective-permute-start | bytes 98312 | tf_op jit(solution)/shard_map/ppermute | solution.py:22
  6.3 4.7 %load.1 = (bf16[768,8192]{1,0:T(8,128)(2,1)S(1)}, bf16[16,1024]{1,0:T(8,128)(2,1)S(1)}) custom-call(bf16[768,8192]{1,0:T(8,128)(2,1)} %tokens_ref.1, bf16[16,1024]{1,0:T(8,128)(2,1)} %queries_ref.1), custom_call_target="tpu_custom_call" | custom-call | tf_op jit(solution)/shard_map/load/pallas_call | solution.py:124
  11.6 2.5 %collective-permute-start.5 = (bf16[4,16,1024]{2,1,0:T(8,128)(2,1)S(1)}, bf16[4,16,1024]{2,1,0:T(8,128)(2,1)S(1)}, u32[]{:S(2)}, u32[]{:S(2)}) collective-permute-start(bf16[4,16,1024]{2,1,0:T(8,128)(2,1)S(1)} %stack.2.refs_0_), channel_id=1, source_target_pairs={{0,6},{1,7},{2,4},{3,5},{4,2},{5,3},{6,0},{7,1},{8,14},{9,15},{10,... | collective-permute-start | bytes 393224 | tf_op jit(solution)/shard_map/ppermute | solution.py:22
  15.2 3.5 %collective-permute-done.5.refs_3_ = bf16[4,16,1024]{2,1,0:T(8,128)(2,1)S(1)} collective-permute-done((bf16[4,16,1024]{2,1,0:T(8,128)(2,1)S(1)}, bf16[4,16,1024]{2,1,0:T(8,128)(2,1)S(1)}, u32[]{:S(2)}, u32[]{:S(2)}) %collective-permute-start.5) | collective-permute-done | bytes 131104 | tf_op jit(solution)/shard_map/ppermute | solution.py:22
  18.7 0.9 collective-permute-done.4.refs_2_
  20.4 1.2 %collective-permute-done.6.other_ref = bf16[8,32,1024]{2,1,0:T(8,128)(2,1)S(1)} collective-permute-done((bf16[8,32,1024]{2,1,0:T(8,128)(2,1)S(1)}, bf16[8,32,1024]{2,1,0:T(8,128)(2,1)S(1)}, u32[]{:S(2)}, u32[]{:S(2)}) %collective-permute-start.6) | collective-permute-done | bytes 524320 | tf_op jit(solution)/shard_map/ppermute | solution.py:22
  21.7 8.1 %pool.1 = (f32[8,32,1024]{2,1,0:T(8,128)S(1)}, bf16[8,32,1152]{2,1,0:T(8,128)(2,1)S(1)}, f32[64,128]{1,0:T(8,128)S(1)}, f32[64,768]{1,0:T(8,128)S(1)}) custom-call(s32[1]{0:T(128)S(6)} %copy.11.length_ref, bf16[8,32,1024]{2,1,0:T(8,128)(2,1)S(1)} %near.2.own_ref, bf16[8,32,1024]{2,1,0:T(8,128)(2,1)S(1)} %collective-permute-done.6.other_ref, ...), custom_call_target="tpu_custom_call" | custom-call | tf_op jit(solution)/shard_map/pool/pallas_call | solution.py:56
  30.0 1.9 %collective-permute-done.7.refs_1_ = bf16[8,32,1152]{2,1,0:T(8,128)(2,1)S(1)} collective-permute-done((bf16[8,32,1152]{2,1,0:T(8,128)(2,1)S(1)}, bf16[8,32,1152]{2,1,0:T(8,128)(2,1)S(1)}, u32[]{:S(2)}, u32[]{:S(2)}) %collective-permute-start.7) | collective-permute-done | bytes 589856 | tf_op jit(solution)/shard_map/ppermute | solution.py:22
  32.3 1.7 %collective-permute-start.8 = (bf16[4,16,1152]{2,1,0:T(8,128)(2,1)S(1)}, bf16[4,16,1152]{2,1,0:T(8,128)(2,1)S(1)}, u32[]{:S(2)}, u32[]{:S(2)}) collective-permute-start(bf16[4,16,1152]{2,1,0:T(8,128)(2,1)S(1)} %get-tuple-element.46), channel_id=1, source_target_pairs={{0,6},{1,7},{2,4},{3,5},{4,2},{5,3},{6,0},{7,1},{8,14},{9,15},{10,... | collective-permute-start | bytes 442376 | tf_op jit(solution)/shard_map/ppermute | solution.py:22
  34.0 1.3 %collective-permute-start.9 = (bf16[4,16,1152]{2,1,0:T(8,128)(2,1)S(1)}, bf16[4,16,1152]{2,1,0:T(8,128)(2,1)S(1)}, u32[]{:S(2)}, u32[]{:S(2)}) collective-permute-start(bf16[4,16,1152]{2,1,0:T(8,128)(2,1)S(1)} %get-tuple-element.47), channel_id=1, source_target_pairs={{0,2},{1,3},{2,0},{3,1},{4,6},{5,7},{6,4},{7,5},{8,10},{9,11},{10,... | collective-permute-start | bytes 442376 | tf_op jit(solution)/shard_map/ppermute | solution.py:22
  35.8 4.1 %collective-permute-done.8.refs_1_ = bf16[4,16,1152]{2,1,0:T(8,128)(2,1)S(1)} collective-permute-done((bf16[4,16,1152]{2,1,0:T(8,128)(2,1)S(1)}, bf16[4,16,1152]{2,1,0:T(8,128)(2,1)S(1)}, u32[]{:S(2)}, u32[]{:S(2)}) %collective-permute-start.8) | collective-permute-done | bytes 147488 | tf_op jit(solution)/shard_map/ppermute | solution.py:22
  40.0 2.3 %collective-permute-done.9.refs_2_ = bf16[4,16,1152]{2,1,0:T(8,128)(2,1)S(1)} collective-permute-done((bf16[4,16,1152]{2,1,0:T(8,128)(2,1)S(1)}, bf16[4,16,1152]{2,1,0:T(8,128)(2,1)S(1)}, u32[]{:S(2)}, u32[]{:S(2)}) %collective-permute-start.9) | collective-permute-done | bytes 147488 | tf_op jit(solution)/shard_map/ppermute | solution.py:22
  42.7 2.7 %collective-permute-start.11 = (bf16[1,16,1152]{2,1,0:T(8,128)(2,1)S(1)}, bf16[1,16,1152]{2,1,0:T(8,128)(2,1)S(1)}, u32[]{:S(2)}, u32[]{:S(2)}) collective-permute-start(bf16[1,16,1152]{2,1,0:T(8,128)(2,1)S(1)} %get-tuple-element.51), channel_id=1, source_target_pairs={{0,24},{1,25},{2,26},{3,27},{4,28},{5,29},{6,30},{7,31},{8,16},{9,... | collective-permute-start | bytes 110600 | tf_op jit(solution)/shard_map/ppermute | solution.py:22
  45.7 1.4 %collective-permute-start.13 = (bf16[1,16,1152]{2,1,0:T(8,128)(2,1)S(1)}, bf16[1,16,1152]{2,1,0:T(8,128)(2,1)S(1)}, u32[]{:S(2)}, u32[]{:S(2)}) collective-permute-start(bf16[1,16,1152]{2,1,0:T(8,128)(2,1)S(1)} %get-tuple-element.53), channel_id=1, source_target_pairs={{0,8},{1,9},{2,10},{3,11},{4,12},{5,13},{6,14},{7,15},{8,0},{9,1},... | collective-permute-start | bytes 110600 | tf_op jit(solution)/shard_map/ppermute | solution.py:22
  47.1 1.5 %collective-permute-done.11.refs_1_ = bf16[1,16,1152]{2,1,0:T(8,128)(2,1)S(1)} collective-permute-done((bf16[1,16,1152]{2,1,0:T(8,128)(2,1)S(1)}, bf16[1,16,1152]{2,1,0:T(8,128)(2,1)S(1)}, u32[]{:S(2)}, u32[]{:S(2)}) %collective-permute-start.11) | collective-permute-done | bytes 36896 | tf_op jit(solution)/shard_map/ppermute | solution.py:22
  48.6 2.0 %collective-permute-done.12.refs_2_ = bf16[1,16,1152]{2,1,0:T(8,128)(2,1)S(1)} collective-permute-done((bf16[1,16,1152]{2,1,0:T(8,128)(2,1)S(1)}, bf16[1,16,1152]{2,1,0:T(8,128)(2,1)S(1)}, u32[]{:S(2)}, u32[]{:S(2)}) %collective-permute-start.12) | collective-permute-done | bytes 36896 | tf_op jit(solution)/shard_map/ppermute | solution.py:22
  50.5 0.6 head_sums.1
  51.2 2.2 %collective-permute-start.16 = (f32[2,1024]{1,0:T(2,128)S(1)}, f32[2,1024]{1,0:T(2,128)S(1)}, u32[]{:S(2)}, u32[]{:S(2)}) collective-permute-start(f32[2,1024]{1,0:T(2,128)S(1)} %get-tuple-element.55.refs_0_), channel_id=1, source_target_pairs={{0,24},{1,25},{2,26},{3,27},{4,28},{5,29},{6,30},{7,31},{8,16},{9,... | collective-permute-start | bytes 24584 | tf_op jit(solution)/shard_map/ppermute | solution.py:22
  53.3 2.3 %collective-permute-start.14 = (f32[2,1024]{1,0:T(2,128)S(1)}, f32[2,1024]{1,0:T(2,128)S(1)}, u32[]{:S(2)}, u32[]{:S(2)}) collective-permute-start(f32[2,1024]{1,0:T(2,128)S(1)} %get-tuple-element.55.refs_0_), channel_id=1, source_target_pairs={{0,8},{1,9},{2,10},{3,11},{4,12},{5,13},{6,14},{7,15},{8,0},{9,1},... | collective-permute-start | bytes 24584 | tf_op jit(solution)/shard_map/ppermute | solution.py:22
  55.6 1.1 collective-permute-done.16.refs_3_
  56.7 1.2 %collective-permute-done.15.refs_2_ = f32[2,1024]{1,0:T(2,128)S(1)} collective-permute-done((f32[2,1024]{1,0:T(2,128)S(1)}, f32[2,1024]{1,0:T(2,128)S(1)}, u32[]{:S(2)}, u32[]{:S(2)}) %collective-permute-start.15) | collective-permute-done | bytes 8224 | tf_op jit(solution)/shard_map/ppermute | solution.py:22
  57.9 1.6 %collective-permute-start.17 = (f32[2,1024]{1,0:T(2,128)S(1)}, f32[2,1024]{1,0:T(2,128)S(1)}, u32[]{:S(2)}, u32[]{:S(2)}) collective-permute-start(f32[2,1024]{1,0:T(2,128)S(1)} %tree_sum.1.sums_ref), channel_id=1, source_target_pairs={{0,4},{1,5},{2,6},{3,7},{4,0},{5,1},{6,2},{7,3},{8,12},{9,13},{10,... | collective-permute-start | bytes 24584 | tf_op jit(solution)/shard_map/ppermute | solution.py:22
  59.4 2.2 %collective-permute-done.17.other_sums_ref = f32[2,1024]{1,0:T(2,128)S(1)} collective-permute-done((f32[2,1024]{1,0:T(2,128)S(1)}, f32[2,1024]{1,0:T(2,128)S(1)}, u32[]{:S(2)}, u32[]{:S(2)}) %collective-permute-start.17) | collective-permute-done | bytes 8224 | tf_op jit(solution)/shard_map/ppermute | solution.py:22
  61.6 1.2 %head_grads.1 = (f32[1,1024]{1,0:T(1,128)}, f32[1,1024]{1,0:T(1,128)S(1)}, bf16[16,1152]{1,0:T(8,128)(2,1)S(1)}, f32[16,1024]{1,0:T(8,128)S(1)}) custom-call(f32[2,1024]{1,0:T(2,128)S(1)} %tree_sum.1.sums_ref, f32[2,1024]{1,0:T(2,128)S(1)} %collective-permute-done.17.other_sums_ref, f32[16,1024]{1,0:T(8,128)S(1)} %get-tuple-element.56.pooled_ref, ...), custom_call_target="tpu_custom_call" | custom-call | tf_op jit(solution)/shard_map/head_grads/pallas_call | solution.py:56
  62.8 1.7 %collective-permute-start.20 = (bf16[16,1152]{1,0:T(8,128)(2,1)S(1)}, bf16[16,1152]{1,0:T(8,128)(2,1)S(1)}, u32[]{:S(2)}, u32[]{:S(2)}) collective-permute-start(bf16[16,1152]{1,0:T(8,128)(2,1)S(1)} %get-tuple-element.58.refs_0_), channel_id=1, source_target_pairs={{0,24},{1,25},{2,26},{3,27},{4,28},{5,29},{6,30},{7,31},{8,16},{9,... | collective-permute-start | bytes 110600 | tf_op jit(solution)/shard_map/ppermute | solution.py:22
  64.5 1.1 collective-permute-start.19
  65.6 1.6 %collective-permute-start.18 = (bf16[16,1152]{1,0:T(8,128)(2,1)S(1)}, bf16[16,1152]{1,0:T(8,128)(2,1)S(1)}, u32[]{:S(2)}, u32[]{:S(2)}) collective-permute-start(bf16[16,1152]{1,0:T(8,128)(2,1)S(1)} %get-tuple-element.58.refs_0_), channel_id=1, source_target_pairs={{0,8},{1,9},{2,10},{3,11},{4,12},{5,13},{6,14},{7,15},{8,0},{9,1},... | collective-permute-start | bytes 110600 | tf_op jit(solution)/shard_map/ppermute | solution.py:22
  67.2 1.4 %collective-permute-done.20.refs_3_ = bf16[16,1152]{1,0:T(8,128)(2,1)S(1)} collective-permute-done((bf16[16,1152]{1,0:T(8,128)(2,1)S(1)}, bf16[16,1152]{1,0:T(8,128)(2,1)S(1)}, u32[]{:S(2)}, u32[]{:S(2)}) %collective-permute-start.20) | collective-permute-done | bytes 36896 | tf_op jit(solution)/shard_map/ppermute | solution.py:22
  68.6 1.2 %collective-permute-done.19.refs_2_ = bf16[16,1152]{1,0:T(8,128)(2,1)S(1)} collective-permute-done((bf16[16,1152]{1,0:T(8,128)(2,1)S(1)}, bf16[16,1152]{1,0:T(8,128)(2,1)S(1)}, u32[]{:S(2)}, u32[]{:S(2)}) %collective-permute-start.19) | collective-permute-done | bytes 36896 | tf_op jit(solution)/shard_map/ppermute | solution.py:22
  69.8 1.7 %collective-permute-start.23 = (bf16[4,16,1152]{2,1,0:T(8,128)(2,1)S(1)}, bf16[4,16,1152]{2,1,0:T(8,128)(2,1)S(1)}, u32[]{:S(2)}, u32[]{:S(2)}) collective-permute-start(bf16[4,16,1152]{2,1,0:T(8,128)(2,1)S(1)} %stack.3.refs_0_), channel_id=1, source_target_pairs={{0,6},{1,7},{2,4},{3,5},{4,2},{5,3},{6,0},{7,1},{8,14},{9,15},{10,... | collective-permute-start | bytes 442376 | tf_op jit(solution)/shard_map/ppermute | solution.py:22
  71.5 1.3 %collective-permute-start.22 = (bf16[4,16,1152]{2,1,0:T(8,128)(2,1)S(1)}, bf16[4,16,1152]{2,1,0:T(8,128)(2,1)S(1)}, u32[]{:S(2)}, u32[]{:S(2)}) collective-permute-start(bf16[4,16,1152]{2,1,0:T(8,128)(2,1)S(1)} %stack.3.refs_0_), channel_id=1, source_target_pairs={{0,2},{1,3},{2,0},{3,1},{4,6},{5,7},{6,4},{7,5},{8,10},{9,11},{10,... | collective-permute-start | bytes 442376 | tf_op jit(solution)/shard_map/ppermute | solution.py:22
  73.4 3.0 %head_weight_grad.1 = (f32[1024,1024]{1,0:T(8,128)}, f32[8,128]{1,0:T(8,128)S(1)}) custom-call(f32[16,1024]{1,0:T(8,128)S(1)} %get-tuple-element.59.normed_ref, f32[1,1024]{1,0:T(1,128)S(1)} %get-tuple-element.60.bias_grad_ref), custom_call_target="tpu_custom_call" | custom-call | flops 100663296 | bytes 4194304 | tf_op jit(solution)/shard_map/head_weight_grad/pallas_call | solution.py:354
  76.3 1.2 %collective-permute-done.22.refs_2_ = bf16[4,16,1152]{2,1,0:T(8,128)(2,1)S(1)} collective-permute-done((bf16[4,16,1152]{2,1,0:T(8,128)(2,1)S(1)}, bf16[4,16,1152]{2,1,0:T(8,128)(2,1)S(1)}, u32[]{:S(2)}, u32[]{:S(2)}) %collective-permute-start.22) | collective-permute-done | bytes 147488 | tf_op jit(solution)/shard_map/ppermute | solution.py:22
  78.1 2.0 %collective-permute-done.24.other_ref = bf16[8,32,1152]{2,1,0:T(8,128)(2,1)S(1)} collective-permute-done((bf16[8,32,1152]{2,1,0:T(8,128)(2,1)S(1)}, bf16[8,32,1152]{2,1,0:T(8,128)(2,1)S(1)}, u32[]{:S(2)}, u32[]{:S(2)}) %collective-permute-start.24) | collective-permute-done | bytes 589856 | tf_op jit(solution)/shard_map/ppermute | solution.py:22
  80.1 7.8 %grad.1 = (f32[8,32,1024]{2,1,0:T(8,128)S(1)}, bf16[8,32,1024]{2,1,0:T(8,128)(2,1)S(1)}, f32[1,1]{1,0:T(1,128)}) custom-call(bf16[8,32,1152]{2,1,0:T(8,128)(2,1)S(1)} %near.3.own_ref, bf16[8,32,1152]{2,1,0:T(8,128)(2,1)S(1)} %collective-permute-done.24.other_ref, bf16[768,8192]{1,0:T(8,128)(2,1)S(1)} %get-tuple-element.41.tokens_ref, ...), custom_call_target="tpu_custom_call" | custom-call | tf_op jit(solution)/shard_map/grad/pallas_call | solution.py:56
  88.1 1.8 %collective-permute-done.25.refs_1_ = bf16[8,32,1024]{2,1,0:T(8,128)(2,1)S(1)} collective-permute-done((bf16[8,32,1024]{2,1,0:T(8,128)(2,1)S(1)}, bf16[8,32,1024]{2,1,0:T(8,128)(2,1)S(1)}, u32[]{:S(2)}, u32[]{:S(2)}) %collective-permute-start.25) | collective-permute-done | bytes 524320 | tf_op jit(solution)/shard_map/ppermute | solution.py:22
  90.0 1.5 %collective-permute-start.26 = (bf16[4,16,1024]{2,1,0:T(8,128)(2,1)S(1)}, bf16[4,16,1024]{2,1,0:T(8,128)(2,1)S(1)}, u32[]{:S(2)}, u32[]{:S(2)}) collective-permute-start(bf16[4,16,1024]{2,1,0:T(8,128)(2,1)S(1)} %get-tuple-element.67), channel_id=1, source_target_pairs={{0,6},{1,7},{2,4},{3,5},{4,2},{5,3},{6,0},{7,1},{8,14},{9,15},{10,... | collective-permute-start | bytes 393224 | tf_op jit(solution)/shard_map/ppermute | solution.py:22
  91.4 1.1 %collective-permute-start.27 = (bf16[4,16,1024]{2,1,0:T(8,128)(2,1)S(1)}, bf16[4,16,1024]{2,1,0:T(8,128)(2,1)S(1)}, u32[]{:S(2)}, u32[]{:S(2)}) collective-permute-start(bf16[4,16,1024]{2,1,0:T(8,128)(2,1)S(1)} %get-tuple-element.68), channel_id=1, source_target_pairs={{0,2},{1,3},{2,0},{3,1},{4,6},{5,7},{6,4},{7,5},{8,10},{9,11},{10,... | collective-permute-start | bytes 393224 | tf_op jit(solution)/shard_map/ppermute | solution.py:22
  92.5 1.0 collective-permute-start.28
  93.5 3.8 %collective-permute-done.26.refs_1_ = bf16[4,16,1024]{2,1,0:T(8,128)(2,1)S(1)} collective-permute-done((bf16[4,16,1024]{2,1,0:T(8,128)(2,1)S(1)}, bf16[4,16,1024]{2,1,0:T(8,128)(2,1)S(1)}, u32[]{:S(2)}, u32[]{:S(2)}) %collective-permute-start.26) | collective-permute-done | bytes 131104 | tf_op jit(solution)/shard_map/ppermute | solution.py:22
  97.3 2.0 %collective-permute-done.27.refs_2_ = bf16[4,16,1024]{2,1,0:T(8,128)(2,1)S(1)} collective-permute-done((bf16[4,16,1024]{2,1,0:T(8,128)(2,1)S(1)}, bf16[4,16,1024]{2,1,0:T(8,128)(2,1)S(1)}, u32[]{:S(2)}, u32[]{:S(2)}) %collective-permute-start.27) | collective-permute-done | bytes 131104 | tf_op jit(solution)/shard_map/ppermute | solution.py:22
  99.4 2.3 %collective-permute-start.29 = (bf16[1,16,1024]{2,1,0:T(8,128)(2,1)S(1)}, bf16[1,16,1024]{2,1,0:T(8,128)(2,1)S(1)}, u32[]{:S(2)}, u32[]{:S(2)}) collective-permute-start(bf16[1,16,1024]{2,1,0:T(8,128)(2,1)S(1)} %get-tuple-element.71), channel_id=1, source_target_pairs={{0,24},{1,25},{2,26},{3,27},{4,28},{5,29},{6,30},{7,31},{8,16},{9,... | collective-permute-start | bytes 98312 | tf_op jit(solution)/shard_map/ppermute | solution.py:22
  101.7 0.6 collective-permute-start.30
  102.3 1.6 %collective-permute-start.31 = (bf16[1,16,1024]{2,1,0:T(8,128)(2,1)S(1)}, bf16[1,16,1024]{2,1,0:T(8,128)(2,1)S(1)}, u32[]{:S(2)}, u32[]{:S(2)}) collective-permute-start(bf16[1,16,1024]{2,1,0:T(8,128)(2,1)S(1)} %get-tuple-element.73), channel_id=1, source_target_pairs={{0,8},{1,9},{2,10},{3,11},{4,12},{5,13},{6,14},{7,15},{8,0},{9,1},... | collective-permute-start | bytes 98312 | tf_op jit(solution)/shard_map/ppermute | solution.py:22
  103.8 1.3 %collective-permute-done.29.refs_1_ = bf16[1,16,1024]{2,1,0:T(8,128)(2,1)S(1)} collective-permute-done((bf16[1,16,1024]{2,1,0:T(8,128)(2,1)S(1)}, bf16[1,16,1024]{2,1,0:T(8,128)(2,1)S(1)}, u32[]{:S(2)}, u32[]{:S(2)}) %collective-permute-start.29) | collective-permute-done | bytes 32800 | tf_op jit(solution)/shard_map/ppermute | solution.py:22
  105.2 1.4 %collective-permute-done.30.refs_2_ = bf16[1,16,1024]{2,1,0:T(8,128)(2,1)S(1)} collective-permute-done((bf16[1,16,1024]{2,1,0:T(8,128)(2,1)S(1)}, bf16[1,16,1024]{2,1,0:T(8,128)(2,1)S(1)}, u32[]{:S(2)}, u32[]{:S(2)}) %collective-permute-start.30) | collective-permute-done | bytes 32800 | tf_op jit(solution)/shard_map/ppermute | solution.py:22
  106.6 0.6 far_sum.1
  (40 shorter events, 5.2 us)
Async XLA Ops:
  0.6 49.9 %copy-start = (bf16[1024,1024]{1,0:T(8,128)(2,1)S(1)}, bf16[1024,1024]{1,0:T(8,128)(2,1)}, u32[]{:S(2)}) copy-start(bf16[1024,1024]{1,0:T(8,128)(2,1)} %weight_ref.1) | copy-start | bytes 6291460
  0.6 49.9 %copy-start.1 = (f32[1024]{0:T(1024)S(1)}, f32[1024]{0:T(1024)}, u32[]{:S(2)}) copy-start(f32[1024]{0:T(1024)} %param.10) | copy-start | bytes 12292
  0.7 10.4 %collective-permute-start = (bf16[16,1024]{1,0:T(8,128)(2,1)}, bf16[16,1024]{1,0:T(8,128)(2,1)S(1)}, u32[]{:S(2)}, u32[]{:S(2)}) collective-permute-start(bf16[16,1024]{1,0:T(8,128)(2,1)} %queries_ref.1), channel_id=1, source_target_pairs={{0,8},{1,9},{2,10},{3,11},{4,12},{5,13},{6,14},{7,15},{8,0},{9,1},... | collective-permute-start | bytes 98312 | tf_op jit(solution)/shard_map/ppermute | solution.py:22
  3.7 7.4 %collective-permute-start.2 = (bf16[16,1024]{1,0:T(8,128)(2,1)}, bf16[16,1024]{1,0:T(8,128)(2,1)S(1)}, u32[]{:S(2)}, u32[]{:S(2)}) collective-permute-start(bf16[16,1024]{1,0:T(8,128)(2,1)} %queries_ref.1), channel_id=1, source_target_pairs={{0,24},{1,25},{2,26},{3,27},{4,28},{5,29},{6,30},{7,31},{8,16},{9,... | collective-permute-start | bytes 98312 | tf_op jit(solution)/shard_map/ppermute | solution.py:22
  6.2 5.4 %collective-permute-start.1 = (bf16[16,1024]{1,0:T(8,128)(2,1)}, bf16[16,1024]{1,0:T(8,128)(2,1)S(1)}, u32[]{:S(2)}, u32[]{:S(2)}) collective-permute-start(bf16[16,1024]{1,0:T(8,128)(2,1)} %queries_ref.1), channel_id=1, source_target_pairs={{0,16},{1,17},{2,18},{3,19},{4,20},{5,21},{6,22},{7,23},{8,24},{9,... | collective-permute-start | bytes 98312 | tf_op jit(solution)/shard_map/ppermute | solution.py:22
  11.1 50.5 %copy-start.2 = (f32[1024]{0:T(1024)S(1)}, f32[1024]{0:T(1024)}, u32[]{:S(2)}) copy-start(f32[1024]{0:T(1024)} %param.12) | copy-start | bytes 12292
  11.1 50.5 %copy-start.3 = (s32[1024]{0:T(1024)S(1)}, s32[1024]{0:T(1024)}, u32[]{:S(2)}) copy-start(s32[1024]{0:T(1024)} %param.13) | copy-start | bytes 12292
  11.6 7.1 %collective-permute-start.5 = (bf16[4,16,1024]{2,1,0:T(8,128)(2,1)S(1)}, bf16[4,16,1024]{2,1,0:T(8,128)(2,1)S(1)}, u32[]{:S(2)}, u32[]{:S(2)}) collective-permute-start(bf16[4,16,1024]{2,1,0:T(8,128)(2,1)S(1)} %stack.2.refs_0_), channel_id=1, source_target_pairs={{0,6},{1,7},{2,4},{3,5},{4,2},{5,3},{6,0},{7,1},{8,14},{9,15},{10,... | collective-permute-start | bytes 393224 | tf_op jit(solution)/shard_map/ppermute | solution.py:22
  14.1 5.5 %collective-permute-start.4 = (bf16[4,16,1024]{2,1,0:T(8,128)(2,1)S(1)}, bf16[4,16,1024]{2,1,0:T(8,128)(2,1)S(1)}, u32[]{:S(2)}, u32[]{:S(2)}) collective-permute-start(bf16[4,16,1024]{2,1,0:T(8,128)(2,1)S(1)} %stack.2.refs_0_), channel_id=1, source_target_pairs={{0,2},{1,3},{2,0},{3,1},{4,6},{5,7},{6,4},{7,5},{8,10},{9,11},{10,... | collective-permute-start | bytes 393224 | tf_op jit(solution)/shard_map/ppermute | solution.py:22
  14.6 5.1 %collective-permute-start.3 = (bf16[4,16,1024]{2,1,0:T(8,128)(2,1)S(1)}, bf16[4,16,1024]{2,1,0:T(8,128)(2,1)S(1)}, u32[]{:S(2)}, u32[]{:S(2)}) collective-permute-start(bf16[4,16,1024]{2,1,0:T(8,128)(2,1)S(1)} %stack.2.refs_0_), channel_id=1, source_target_pairs={{0,4},{1,5},{2,6},{3,7},{4,0},{5,1},{6,2},{7,3},{8,12},{9,13},{10,... | collective-permute-start | bytes 393224 | tf_op jit(solution)/shard_map/ppermute | solution.py:22
  19.7 2.0 %collective-permute-start.6 = (bf16[8,32,1024]{2,1,0:T(8,128)(2,1)S(1)}, bf16[8,32,1024]{2,1,0:T(8,128)(2,1)S(1)}, u32[]{:S(2)}, u32[]{:S(2)}) collective-permute-start(bf16[8,32,1024]{2,1,0:T(8,128)(2,1)S(1)} %near.2.own_ref), channel_id=1, source_target_pairs={{0,1},{1,0},{2,3},{3,2},{4,5},{5,4},{6,7},{7,6},{8,9},{9,8},{10,11... | collective-permute-start | bytes 1572872 | tf_op jit(solution)/shard_map/ppermute | solution.py:22
  29.8 2.1 %collective-permute-start.7 = (bf16[8,32,1152]{2,1,0:T(8,128)(2,1)S(1)}, bf16[8,32,1152]{2,1,0:T(8,128)(2,1)S(1)}, u32[]{:S(2)}, u32[]{:S(2)}) collective-permute-start(bf16[8,32,1152]{2,1,0:T(8,128)(2,1)S(1)} %get-tuple-element.43), channel_id=1, source_target_pairs={{0,1},{1,0},{2,3},{3,2},{4,5},{5,4},{6,7},{7,6},{8,9},{9,8},{10,11... | collective-permute-start | bytes 1769480 | tf_op jit(solution)/shard_map/ppermute | solution.py:22
  32.3 7.7 %collective-permute-start.8 = (bf16[4,16,1152]{2,1,0:T(8,128)(2,1)S(1)}, bf16[4,16,1152]{2,1,0:T(8,128)(2,1)S(1)}, u32[]{:S(2)}, u32[]{:S(2)}) collective-permute-start(bf16[4,16,1152]{2,1,0:T(8,128)(2,1)S(1)} %get-tuple-element.46), channel_id=1, source_target_pairs={{0,6},{1,7},{2,4},{3,5},{4,2},{5,3},{6,0},{7,1},{8,14},{9,15},{10,... | collective-permute-start | bytes 442376 | tf_op jit(solution)/shard_map/ppermute | solution.py:22
  34.0 8.3 %collective-permute-start.9 = (bf16[4,16,1152]{2,1,0:T(8,128)(2,1)S(1)}, bf16[4,16,1152]{2,1,0:T(8,128)(2,1)S(1)}, u32[]{:S(2)}, u32[]{:S(2)}) collective-permute-start(bf16[4,16,1152]{2,1,0:T(8,128)(2,1)S(1)} %get-tuple-element.47), channel_id=1, source_target_pairs={{0,2},{1,3},{2,0},{3,1},{4,6},{5,7},{6,4},{7,5},{8,10},{9,11},{10,... | collective-permute-start | bytes 442376 | tf_op jit(solution)/shard_map/ppermute | solution.py:22
  35.3 7.0 %collective-permute-start.10 = (bf16[4,16,1152]{2,1,0:T(8,128)(2,1)S(1)}, bf16[4,16,1152]{2,1,0:T(8,128)(2,1)S(1)}, u32[]{:S(2)}, u32[]{:S(2)}) collective-permute-start(bf16[4,16,1152]{2,1,0:T(8,128)(2,1)S(1)} %get-tuple-element.48), channel_id=1, source_target_pairs={{0,4},{1,5},{2,6},{3,7},{4,0},{5,1},{6,2},{7,3},{8,12},{9,13},{10,... | collective-permute-start | bytes 442376 | tf_op jit(solution)/shard_map/ppermute | solution.py:22
  42.7 5.9 %collective-permute-start.11 = (bf16[1,16,1152]{2,1,0:T(8,128)(2,1)S(1)}, bf16[1,16,1152]{2,1,0:T(8,128)(2,1)S(1)}, u32[]{:S(2)}, u32[]{:S(2)}) collective-permute-start(bf16[1,16,1152]{2,1,0:T(8,128)(2,1)S(1)} %get-tuple-element.51), channel_id=1, source_target_pairs={{0,24},{1,25},{2,26},{3,27},{4,28},{5,29},{6,30},{7,31},{8,16},{9,... | collective-permute-start | bytes 110600 | tf_op jit(solution)/shard_map/ppermute | solution.py:22
  45.4 5.2 %collective-permute-start.12 = (bf16[1,16,1152]{2,1,0:T(8,128)(2,1)S(1)}, bf16[1,16,1152]{2,1,0:T(8,128)(2,1)S(1)}, u32[]{:S(2)}, u32[]{:S(2)}) collective-permute-start(bf16[1,16,1152]{2,1,0:T(8,128)(2,1)S(1)} %get-tuple-element.52), channel_id=1, source_target_pairs={{0,16},{1,17},{2,18},{3,19},{4,20},{5,21},{6,22},{7,23},{8,24},{9,... | collective-permute-start | bytes 110600 | tf_op jit(solution)/shard_map/ppermute | solution.py:22
  45.7 4.8 %collective-permute-start.13 = (bf16[1,16,1152]{2,1,0:T(8,128)(2,1)S(1)}, bf16[1,16,1152]{2,1,0:T(8,128)(2,1)S(1)}, u32[]{:S(2)}, u32[]{:S(2)}) collective-permute-start(bf16[1,16,1152]{2,1,0:T(8,128)(2,1)S(1)} %get-tuple-element.53), channel_id=1, source_target_pairs={{0,8},{1,9},{2,10},{3,11},{4,12},{5,13},{6,14},{7,15},{8,0},{9,1},... | collective-permute-start | bytes 110600 | tf_op jit(solution)/shard_map/ppermute | solution.py:22
  51.2 5.5 %collective-permute-start.16 = (f32[2,1024]{1,0:T(2,128)S(1)}, f32[2,1024]{1,0:T(2,128)S(1)}, u32[]{:S(2)}, u32[]{:S(2)}) collective-permute-start(f32[2,1024]{1,0:T(2,128)S(1)} %get-tuple-element.55.refs_0_), channel_id=1, source_target_pairs={{0,24},{1,25},{2,26},{3,27},{4,28},{5,29},{6,30},{7,31},{8,16},{9,... | collective-permute-start | bytes 24584 | tf_op jit(solution)/shard_map/ppermute | solution.py:22
  53.3 4.5 %collective-permute-start.15 = (f32[2,1024]{1,0:T(2,128)S(1)}, f32[2,1024]{1,0:T(2,128)S(1)}, u32[]{:S(2)}, u32[]{:S(2)}) collective-permute-start(f32[2,1024]{1,0:T(2,128)S(1)} %get-tuple-element.55.refs_0_), channel_id=1, source_target_pairs={{0,16},{1,17},{2,18},{3,19},{4,20},{5,21},{6,22},{7,23},{8,24},{9,... | collective-permute-start | bytes 24584 | tf_op jit(solution)/shard_map/ppermute | solution.py:22
  53.3 4.5 %collective-permute-start.14 = (f32[2,1024]{1,0:T(2,128)S(1)}, f32[2,1024]{1,0:T(2,128)S(1)}, u32[]{:S(2)}, u32[]{:S(2)}) collective-permute-start(f32[2,1024]{1,0:T(2,128)S(1)} %get-tuple-element.55.refs_0_), channel_id=1, source_target_pairs={{0,8},{1,9},{2,10},{3,11},{4,12},{5,13},{6,14},{7,15},{8,0},{9,1},... | collective-permute-start | bytes 24584 | tf_op jit(solution)/shard_map/ppermute | solution.py:22
  57.9 3.7 %collective-permute-start.17 = (f32[2,1024]{1,0:T(2,128)S(1)}, f32[2,1024]{1,0:T(2,128)S(1)}, u32[]{:S(2)}, u32[]{:S(2)}) collective-permute-start(f32[2,1024]{1,0:T(2,128)S(1)} %tree_sum.1.sums_ref), channel_id=1, source_target_pairs={{0,4},{1,5},{2,6},{3,7},{4,0},{5,1},{6,2},{7,3},{8,12},{9,13},{10,... | collective-permute-start | bytes 24584 | tf_op jit(solution)/shard_map/ppermute | solution.py:22
  62.8 5.8 %collective-permute-start.20 = (bf16[16,1152]{1,0:T(8,128)(2,1)S(1)}, bf16[16,1152]{1,0:T(8,128)(2,1)S(1)}, u32[]{:S(2)}, u32[]{:S(2)}) collective-permute-start(bf16[16,1152]{1,0:T(8,128)(2,1)S(1)} %get-tuple-element.58.refs_0_), channel_id=1, source_target_pairs={{0,24},{1,25},{2,26},{3,27},{4,28},{5,29},{6,30},{7,31},{8,16},{9,... | collective-permute-start | bytes 110600 | tf_op jit(solution)/shard_map/ppermute | solution.py:22
  64.5 5.3 %collective-permute-start.19 = (bf16[16,1152]{1,0:T(8,128)(2,1)S(1)}, bf16[16,1152]{1,0:T(8,128)(2,1)S(1)}, u32[]{:S(2)}, u32[]{:S(2)}) collective-permute-start(bf16[16,1152]{1,0:T(8,128)(2,1)S(1)} %get-tuple-element.58.refs_0_), channel_id=1, source_target_pairs={{0,16},{1,17},{2,18},{3,19},{4,20},{5,21},{6,22},{7,23},{8,24},{9,... | collective-permute-start | bytes 110600 | tf_op jit(solution)/shard_map/ppermute | solution.py:22
  65.6 4.2 %collective-permute-start.18 = (bf16[16,1152]{1,0:T(8,128)(2,1)S(1)}, bf16[16,1152]{1,0:T(8,128)(2,1)S(1)}, u32[]{:S(2)}, u32[]{:S(2)}) collective-permute-start(bf16[16,1152]{1,0:T(8,128)(2,1)S(1)} %get-tuple-element.58.refs_0_), channel_id=1, source_target_pairs={{0,8},{1,9},{2,10},{3,11},{4,12},{5,13},{6,14},{7,15},{8,0},{9,1},... | collective-permute-start | bytes 110600 | tf_op jit(solution)/shard_map/ppermute | solution.py:22
  69.8 6.5 %collective-permute-start.23 = (bf16[4,16,1152]{2,1,0:T(8,128)(2,1)S(1)}, bf16[4,16,1152]{2,1,0:T(8,128)(2,1)S(1)}, u32[]{:S(2)}, u32[]{:S(2)}) collective-permute-start(bf16[4,16,1152]{2,1,0:T(8,128)(2,1)S(1)} %stack.3.refs_0_), channel_id=1, source_target_pairs={{0,6},{1,7},{2,4},{3,5},{4,2},{5,3},{6,0},{7,1},{8,14},{9,15},{10,... | collective-permute-start | bytes 442376 | tf_op jit(solution)/shard_map/ppermute | solution.py:22
  71.5 6.0 %collective-permute-start.22 = (bf16[4,16,1152]{2,1,0:T(8,128)(2,1)S(1)}, bf16[4,16,1152]{2,1,0:T(8,128)(2,1)S(1)}, u32[]{:S(2)}, u32[]{:S(2)}) collective-permute-start(bf16[4,16,1152]{2,1,0:T(8,128)(2,1)S(1)} %stack.3.refs_0_), channel_id=1, source_target_pairs={{0,2},{1,3},{2,0},{3,1},{4,6},{5,7},{6,4},{7,5},{8,10},{9,11},{10,... | collective-permute-start | bytes 442376 | tf_op jit(solution)/shard_map/ppermute | solution.py:22
  72.8 5.1 %collective-permute-start.21 = (bf16[4,16,1152]{2,1,0:T(8,128)(2,1)S(1)}, bf16[4,16,1152]{2,1,0:T(8,128)(2,1)S(1)}, u32[]{:S(2)}, u32[]{:S(2)}) collective-permute-start(bf16[4,16,1152]{2,1,0:T(8,128)(2,1)S(1)} %stack.3.refs_0_), channel_id=1, source_target_pairs={{0,4},{1,5},{2,6},{3,7},{4,0},{5,1},{6,2},{7,3},{8,12},{9,13},{10,... | collective-permute-start | bytes 442376 | tf_op jit(solution)/shard_map/ppermute | solution.py:22
  78.0 2.1 %collective-permute-start.24 = (bf16[8,32,1152]{2,1,0:T(8,128)(2,1)S(1)}, bf16[8,32,1152]{2,1,0:T(8,128)(2,1)S(1)}, u32[]{:S(2)}, u32[]{:S(2)}) collective-permute-start(bf16[8,32,1152]{2,1,0:T(8,128)(2,1)S(1)} %near.3.own_ref), channel_id=1, source_target_pairs={{0,1},{1,0},{2,3},{3,2},{4,5},{5,4},{6,7},{7,6},{8,9},{9,8},{10,11... | collective-permute-start | bytes 1769480 | tf_op jit(solution)/shard_map/ppermute | solution.py:22
  87.9 2.0 %collective-permute-start.25 = (bf16[8,32,1024]{2,1,0:T(8,128)(2,1)S(1)}, bf16[8,32,1024]{2,1,0:T(8,128)(2,1)S(1)}, u32[]{:S(2)}, u32[]{:S(2)}) collective-permute-start(bf16[8,32,1024]{2,1,0:T(8,128)(2,1)S(1)} %get-tuple-element.65), channel_id=1, source_target_pairs={{0,1},{1,0},{2,3},{3,2},{4,5},{5,4},{6,7},{7,6},{8,9},{9,8},{10,11... | collective-permute-start | bytes 1572872 | tf_op jit(solution)/shard_map/ppermute | solution.py:22
  90.0 7.3 %collective-permute-start.26 = (bf16[4,16,1024]{2,1,0:T(8,128)(2,1)S(1)}, bf16[4,16,1024]{2,1,0:T(8,128)(2,1)S(1)}, u32[]{:S(2)}, u32[]{:S(2)}) collective-permute-start(bf16[4,16,1024]{2,1,0:T(8,128)(2,1)S(1)} %get-tuple-element.67), channel_id=1, source_target_pairs={{0,6},{1,7},{2,4},{3,5},{4,2},{5,3},{6,0},{7,1},{8,14},{9,15},{10,... | collective-permute-start | bytes 393224 | tf_op jit(solution)/shard_map/ppermute | solution.py:22
  91.4 7.9 %collective-permute-start.27 = (bf16[4,16,1024]{2,1,0:T(8,128)(2,1)S(1)}, bf16[4,16,1024]{2,1,0:T(8,128)(2,1)S(1)}, u32[]{:S(2)}, u32[]{:S(2)}) collective-permute-start(bf16[4,16,1024]{2,1,0:T(8,128)(2,1)S(1)} %get-tuple-element.68), channel_id=1, source_target_pairs={{0,2},{1,3},{2,0},{3,1},{4,6},{5,7},{6,4},{7,5},{8,10},{9,11},{10,... | collective-permute-start | bytes 393224 | tf_op jit(solution)/shard_map/ppermute | solution.py:22
  92.5 6.8 %collective-permute-start.28 = (bf16[4,16,1024]{2,1,0:T(8,128)(2,1)S(1)}, bf16[4,16,1024]{2,1,0:T(8,128)(2,1)S(1)}, u32[]{:S(2)}, u32[]{:S(2)}) collective-permute-start(bf16[4,16,1024]{2,1,0:T(8,128)(2,1)S(1)} %get-tuple-element.69), channel_id=1, source_target_pairs={{0,4},{1,5},{2,6},{3,7},{4,0},{5,1},{6,2},{7,3},{8,12},{9,13},{10,... | collective-permute-start | bytes 393224 | tf_op jit(solution)/shard_map/ppermute | solution.py:22
  99.4 5.8 %collective-permute-start.29 = (bf16[1,16,1024]{2,1,0:T(8,128)(2,1)S(1)}, bf16[1,16,1024]{2,1,0:T(8,128)(2,1)S(1)}, u32[]{:S(2)}, u32[]{:S(2)}) collective-permute-start(bf16[1,16,1024]{2,1,0:T(8,128)(2,1)S(1)} %get-tuple-element.71), channel_id=1, source_target_pairs={{0,24},{1,25},{2,26},{3,27},{4,28},{5,29},{6,30},{7,31},{8,16},{9,... | collective-permute-start | bytes 98312 | tf_op jit(solution)/shard_map/ppermute | solution.py:22
  101.7 4.9 %collective-permute-start.30 = (bf16[1,16,1024]{2,1,0:T(8,128)(2,1)S(1)}, bf16[1,16,1024]{2,1,0:T(8,128)(2,1)S(1)}, u32[]{:S(2)}, u32[]{:S(2)}) collective-permute-start(bf16[1,16,1024]{2,1,0:T(8,128)(2,1)S(1)} %get-tuple-element.72), channel_id=1, source_target_pairs={{0,16},{1,17},{2,18},{3,19},{4,20},{5,21},{6,22},{7,23},{8,24},{9,... | collective-permute-start | bytes 98312 | tf_op jit(solution)/shard_map/ppermute | solution.py:22
  102.3 4.3 %collective-permute-start.31 = (bf16[1,16,1024]{2,1,0:T(8,128)(2,1)S(1)}, bf16[1,16,1024]{2,1,0:T(8,128)(2,1)S(1)}, u32[]{:S(2)}, u32[]{:S(2)}) collective-permute-start(bf16[1,16,1024]{2,1,0:T(8,128)(2,1)S(1)} %get-tuple-element.73), channel_id=1, source_target_pairs={{0,8},{1,9},{2,10},{3,11},{4,12},{5,13},{6,14},{7,15},{8,0},{9,1},... | collective-permute-start | bytes 98312 | tf_op jit(solution)/shard_map/ppermute | solution.py:22

commit v6 on v5

v6 whole, which is shorter than its diff:
```python
import functools

import jax
import jax.numpy as jnp
from jax import lax
from jax.experimental import pallas as pl
from jax.experimental.pallas import tpu as pltpu
from jax.sharding import PartitionSpec as P

F32 = jnp.float32
BF16 = jnp.bfloat16
LANES = 128
MASKED = -1e30
MIB = 1024 * 1024


def swap(x, ctx_bits, cls_bits):
    contexts, classes = lax.axis_size("ctx"), lax.axis_size("cls")
    pairs = [
        (c * classes + k, (c ^ ctx_bits) * classes + (k ^ cls_bits)) for c in range(contexts) for k in range(classes)
    ]
    return lax.ppermute(x, ("ctx", "cls"), pairs)


def far_steps():
    return [(2 * j, 0) for j in reversed(range(1, lax.axis_size("ctx") // 2))]


def near_steps():
    steps = [(i, 2 * k) for i in range(2) for k in range(lax.axis_size("cls") // 2) if i or k]
    return sorted(steps, key=lambda step: not (step[0] and step[1]))


def call(kernel, outs, name, args, scratch=(), hbm_args=(), smem_args=(), limit=16, cost=None):
    def spec(i):
        if i in hbm_args:
            return pl.BlockSpec(memory_space=pltpu.HBM)
        if i in smem_args:
            return pl.BlockSpec(memory_space=pltpu.SMEM)
        return pl.BlockSpec(memory_space=pltpu.VMEM)

    run = pl.pallas_call(
        kernel,
        out_shape=[jax.ShapeDtypeStruct(s, d) for s, d in outs],
        in_specs=[spec(i) for i in range(len(args))],
        out_specs=[pl.BlockSpec(memory_space=pltpu.VMEM)] * len(outs),
        scratch_shapes=list(scratch),
        compiler_params=pltpu.CompilerParams(vmem_limit_bytes=limit * MIB),
        cost_estimate=cost,
        name=name,
    )
    return list(run(*args))


def stack_kernel(*refs):
    out_ref = refs[-1]
    for at, ref in enumerate(refs[:-1]):
        out_ref[at] = ref[...].reshape(out_ref.shape[1:])


def gather(block, local=None):
    far = [swap(block, *step) for step in far_steps()[::-1]]
    rows, width = block.shape
    (held,) = call(
        stack_kernel, [((len(far) + 1, rows, width), block.dtype)], "stack", [block if local is None else local, *far]
    )
    parts = {step: swap(held, *step) for step in near_steps()[::-1]}
    parts[0, 0] = held
    other = {step: swap(part, 0, 1) for step, part in parts.items()}
    steps = sorted(parts)
    return [[group[step] for group in (parts, other) for step in steps if step[0] == i] for i in range(2)]


def pieces(x):
    high = x.astype(BF16)
    rest = x - high.astype(F32)
    middle = rest.astype(BF16)
    return high, middle, (rest - middle.astype(F32)).astype(BF16)


def into_lanes(columns, rows):
    lane = lax.broadcasted_iota(jnp.int32, (rows, LANES), 1)
    out = jnp.zeros((rows, LANES), F32)
    for i, column in enumerate(columns):
        for j, piece in enumerate(pieces(column)):
            out = jnp.where(lane == 3 * i + j, piece.astype(F32), out)
    return out.astype(BF16)


def from_lanes(block, width, i):
    at = width + 3 * i
    block = block.astype(F32)
    return block[:, at : at + 1] + (block[:, at + 1 : at + 2] + block[:, at + 2 : at + 3])


def load_kernel(half, tokens_ref, *refs):
    count = (len(refs) - 2) // 2
    others, held_ref, copies_of, sems = refs[:count], refs[count], refs[count + 1 : -1], refs[-1]
    width = held_ref.shape[2]
    copies = [pltpu.make_async_copy(src, dst, sems.at[i]) for i, (src, dst) in enumerate(zip(others, copies_of))]
    for j in range(held_ref.shape[0]):
        start = pl.multiple_of((lax.axis_index("ctx") ^ half ^ (2 * j)) * width, LANES)
        copies.append(
            pltpu.make_async_copy(tokens_ref.at[:, pl.ds(start, width)], held_ref.at[j], sems.at[count + j])
        )
    for copy in copies:
        copy.start()
    for copy in copies:
        copy.wait()


def load(half, width, tokens, *others):
    rows, full_width = tokens.shape
    blocks = full_width // width // 2
    outs = [pltpu.VMEM((blocks, rows, width), tokens.dtype)] + [pltpu.VMEM(x.shape, x.dtype) for x in others]
    run = pl.pallas_call(
        functools.partial(load_kernel, half),
        out_shape=outs,
        in_specs=[pl.BlockSpec(memory_space=pltpu.HBM)] * (1 + len(others)),
        out_specs=[pl.BlockSpec(memory_space=pltpu.VMEM)] * len(outs),
        scratch_shapes=[pltpu.SemaphoreType.DMA((blocks + len(others),))],
        compiler_params=pltpu.CompilerParams(vmem_limit_bytes=16 * MIB),
        name="load",
    )
    return run(*[pltpu.with_memory_space_constraint(x, pltpu.HBM) for x in (tokens, *others)])


def project(parts, held_ref, tile=256):
    blocks, token_count, width = held_ref.shape
    tiles = []
    for at in range(0, token_count, tile):
        total = None
        for j in range(blocks):
            left = jnp.concatenate([ref[j] for ref in parts], axis=0)[:, :width]
            block = held_ref[j, at : at + tile, :]
            part = lax.dot_general(left, block, (((1,), (1,)), ((), ())), preferred_element_type=F32)
            total = part if total is None else total + part
        tiles.append(total)
    return jnp.concatenate(tiles, axis=1)


def spread(left, held_ref, keep_ref, send_ref, extra, tile=256):
    blocks, half, width = keep_ref.shape
    for j in range(blocks):
        for at in range(0, width, tile):
            part = jnp.dot(left, held_ref[j, :, at : at + tile], preferred_element_type=F32)
            keep_ref[j, :, at : at + tile] = part[:half]
            send_ref[j, :, at : at + tile] = part[half:].astype(BF16)
        if extra is not None:
            send_ref[j, :, width:] = extra


def project_kernel(count, *refs):
    refs[-1][...] = project(refs[:count], refs[count])


def peak_lanes(peak, half):
    return into_lanes([peak[half:, :1]], half)


def pool_kernel(count, length_ref, *refs):
    parts, refs = refs[:count], refs[count:]
    part_ref, held_ref, keep_ref, send_ref, peak_ref, w_ref, left_ref = refs
    scores = part_ref[...] + project(parts, held_ref)
    shard = lax.axis_index("ctx") * lax.axis_size("cls") + lax.axis_index("cls")
    valid = lax.broadcasted_iota(jnp.int32, scores.shape, 1) < length_ref[0] - shard * scores.shape[1]
    peak = jnp.max(jnp.where(valid, scores, MASKED), axis=1, keepdims=True)
    weights = jnp.where(valid, jnp.exp(scores - peak), 0.0)
    left = weights.astype(BF16)
    w_ref[...] = weights
    left_ref[...] = left
    peak_ref[...] = jnp.broadcast_to(peak, peak_ref.shape)
    spread(left, held_ref, keep_ref, send_ref, peak_lanes(peak, keep_ref.shape[1]))


def pool_rest_kernel(left_ref, peak_ref, held_ref, keep_ref, send_ref):
    spread(left_ref[...], held_ref, keep_ref, send_ref, peak_lanes(peak_ref[...], keep_ref.shape[1]))


def grad_kernel(scale, count, *refs):
    parts, refs = refs[:count], refs[count:]
    part_ref, held_ref, w_ref, peak_ref, keep_ref, send_ref, left_ref, loss_ref = refs
    width = held_ref.shape[2]
    projected = part_ref[...] + project(parts, held_ref)
    blocks = [ref[0] for ref in parts]
    top = jnp.concatenate([from_lanes(block, width, 0) for block in blocks], axis=0)
    weights = w_ref[...] * jnp.exp(peak_ref[:, :1] - top)
    left = (weights * projected).astype(BF16)
    left_ref[...] = left
    spread(left, held_ref, keep_ref, send_ref, None)
    loss_ref[...] = tree_sum([from_lanes(block, width, 1)[:1] for block in blocks]) * scale


def grad_rest_kernel(left_ref, held_ref, keep_ref, send_ref):
    spread(left_ref[...], held_ref, keep_ref, send_ref, None)


def total_of(keep, peak, received, width):
    if peak is None:
        for block in received:
            keep = keep + block.astype(F32)
        return keep, None
    others = [from_lanes(block, width, 0) for block in received]
    top = peak
    for other in others:
        top = jnp.maximum(top, other)
    keep = keep * jnp.exp(peak - top)
    for block, other in zip(received, others):
        keep = keep + block[:, :width].astype(F32) * jnp.exp(other - top)
    return keep, top


def put(ref, p, total, top, width):
    ref[p, :, :width] = total.astype(BF16)
    if top is not None:
        ref[p, :, width:] = into_lanes([top], total.shape[0])


def core_kernel(peaks, first, *refs):
    keep_ref, recv_ref, *refs = refs
    peak = refs.pop(0)[: keep_ref.shape[1], :1] if peaks else None
    refs = refs[1:] if first else refs
    top_ref = refs.pop() if peaks and first else None
    width = keep_ref.shape[2]
    rows = refs[0].shape[1]
    for j in range(keep_ref.shape[0]):
        total, top = total_of(keep_ref[j], peak, [recv_ref[j]], width)
        for k, ref in enumerate(refs):
            at = slice(k * rows, (k + 1) * rows)
            if first and k == 0:
                ref[j] = total[at]
            else:
                put(ref, j, total[at], top[at] if peaks else None, width)
    if peaks and first:
        top_ref[...] = jnp.broadcast_to(top[:rows], top_ref.shape)


def near_sum_kernel(peaks, count, steps, after, *refs):
    keep_ref, *refs = refs
    received, refs = refs[:count], refs[count:]
    peak = refs.pop(0)[:, :1] if peaks else None
    refs = refs[after:]
    top_ref = refs.pop() if peaks else None
    width = keep_ref.shape[2]
    for p in range(keep_ref.shape[0]):
        total, top = total_of(keep_ref[p], peak, [ref[p] for ref in received], width)
        if p == 0:
            refs[0][0] = total
        else:
            put(refs[steps.index((2 * p, 0)) + 1], 0, total, top, width)
    if peaks:
        top_ref[...] = jnp.broadcast_to(top, top_ref.shape)


def scatter_sum(halves, peak, after=()):
    peaks = peak is not None
    near, far = near_steps(), far_steps()
    across = (len(near) + 1) // 2
    blocks, half, width = halves[0][0].shape
    lanes = halves[0][1].shape[2]
    rows = half // across
    top_out = [((rows, LANES), F32)] if peaks else []
    parts = {}
    for i in reversed(range(2)):
        keep, send = halves[i]
        outs = [((blocks, rows, lanes), BF16)] * across
        if i == 0:
            outs = [((blocks, rows, width), F32)] + outs[1:] + top_out
        args = [keep, swap(send, 0, 1)] + ([peak] if peaks else [])
        if i == 0:
            args.append(parts[1, 0])
        out = call(functools.partial(core_kernel, peaks, i == 0), outs, "core_sum", args)
        parts.update({(i, 2 * k): out[k] for k in range(across)})
    received = [swap(parts[step], *step) for step in near]
    outs = [((1, rows, width), F32)] + [((1, rows, lanes), BF16)] * len(far) + top_out
    args = [parts[0, 0], *received] + (out[-1:] if peaks else []) + list(after)
    out = call(functools.partial(near_sum_kernel, peaks, len(received), far, len(after)), outs, "near_sum", args)
    received = [swap(x, *step) for x, step in zip(out[1:], far)]
    return [out[0], *received] + (out[-1:] if peaks else [])


def far_sum_kernel(*refs):
    keep_ref, *received, out_ref = refs
    out_ref[...] = total_of(keep_ref[0], None, [ref[0] for ref in received], keep_ref.shape[2])[0]


def head_mask(shape, attributes):
    row = lax.broadcasted_iota(jnp.int32, shape, 0)
    column = lax.broadcasted_iota(jnp.int32, shape, 1)
    return column // attributes == row


def head_sums_kernel(*refs):
    keep_ref, *received, peak_ref, gain_ref, weight_ref, sums_ref, pooled_ref, top_ref = refs
    pooled, top = total_of(keep_ref[0], peak_ref[:, :1], [ref[0] for ref in received], keep_ref.shape[2])
    pooled_ref[...] = pooled
    top_ref[...] = jnp.broadcast_to(top, top_ref.shape)
    scaled_b = (pooled * gain_ref[...]).astype(BF16)
    product = jnp.dot(scaled_b, weight_ref[...], preferred_element_type=F32)
    mask = head_mask(product.shape, product.shape[1] // product.shape[0])
    squares = jnp.sum(pooled * pooled, axis=1, keepdims=True)
    product_flat = jnp.sum(jnp.where(mask, product, 0.0), axis=0, keepdims=True)
    squares_flat = jnp.sum(jnp.where(mask, squares, 0.0), axis=0, keepdims=True)
    sums_ref[0:1, :] = product_flat
    sums_ref[1:2, :] = squares_flat


def tree_sum(level):
    while len(level) > 1:
        level = [a + b for a, b in zip(level[::2], level[1::2])]
    return level[0]


def head_grads_kernel(full_width, count, *refs):
    pooled_ref, top_ref, gain_ref, weight_ref, bias_ref, label_ref = refs[count : count + 6]
    bias_grad_ref, copy_ref, grad_ref, normed_ref = refs[count + 6 :]
    pooled, gain = pooled_ref[...], gain_ref[...]
    heads, width = pooled.shape
    columns = bias_ref.shape[1]
    sums = tree_sum([ref[...] for ref in refs[:count]])
    mask = head_mask((heads, columns), columns // heads)
    inverse_flat = lax.rsqrt(sums[1:2] / full_width + 1e-05)
    inverse_rms = jnp.max(jnp.where(mask, inverse_flat, 0.0), axis=1, keepdims=True)
    product = inverse_flat * sums[0:1]
    logits = product + bias_ref[...]
    target = label_ref[...].astype(F32)
    losses = jnp.maximum(logits, 0.0) + jnp.log1p(jnp.exp(-jnp.abs(logits))) - target * logits
    loss = jnp.sum(losses, axis=1, keepdims=True)
    bias_grad = jax.nn.sigmoid(logits) - target
    bias_grad_ref[...] = bias_grad
    copy_ref[...] = bias_grad
    by_head = jnp.where(mask, bias_grad, 0.0)
    high = by_head.astype(BF16)
    low = (by_head - high.astype(F32)).astype(BF16)
    both = jnp.concatenate([high, low], axis=0)
    back = lax.dot_general(both, weight_ref[...], (((1,), (1,)), ((), ())), preferred_element_type=F32)
    normed_grad = (back[:heads] + back[heads:]) * gain
    inner = jnp.sum(by_head * product, axis=1, keepdims=True) / full_width
    unit = pooled * inverse_rms
    grad_ref[:, :width] = (inverse_rms * (normed_grad - unit * inner)).astype(BF16)
    grad_ref[:, width:] = into_lanes([top_ref[:, :1], jnp.broadcast_to(loss, (heads, 1))], heads)
    normed_ref[...] = unit * gain


def head_weight_grad_kernel(attributes, normed_ref, bias_grad_ref, out_ref, done_ref):
    heads = normed_ref.shape[0]
    columns = out_ref.shape[1]
    parts = jnp.concatenate(pieces(normed_ref[...]), axis=0)
    row = lax.broadcasted_iota(jnp.int32, (3 * heads, columns), 0) % heads
    column = pl.program_id(0) * columns + lax.broadcasted_iota(jnp.int32, (3 * heads, columns), 1)
    ones = jnp.where(column // attributes == row, 1.0, 0.0).astype(BF16)
    normed = lax.dot_general(parts, ones, (((0,), (0,)), ((), ())), preferred_element_type=F32)
    out_ref[...] = normed * bias_grad_ref[...]
    done_ref[...] = jnp.zeros_like(done_ref)


def head_weight_grad(normed, bias_grad):
    rows, width = normed.shape
    columns = bias_grad.shape[1]
    block = columns // 4
    return pl.pallas_call(
        functools.partial(head_weight_grad_kernel, columns // rows),
        out_shape=[jax.ShapeDtypeStruct((width, columns), F32), jax.ShapeDtypeStruct((8, LANES), F32)],
        grid=(columns // block,),
        in_specs=[
            pl.BlockSpec((rows, width), lambda i: (0, 0)),
            pl.BlockSpec((1, block), lambda i: (0, i)),
        ],
        out_specs=[pl.BlockSpec((width, block), lambda i: (0, i)), pl.BlockSpec((8, LANES), lambda i: (0, 0))],
        compiler_params=pltpu.CompilerParams(vmem_limit_bytes=16 * MIB),
        cost_estimate=pl.CostEstimate(flops=6 * rows * width * columns, bytes_accessed=4 * width * columns, transcendentals=0),
        name="head_weight_grad",
    )(normed, bias_grad)


def shards(tokens, doc_length, queries, norm_gain, head_weight, head_bias, labels):
    contexts, classes = lax.axis_size("ctx"), lax.axis_size("cls")
    token_count = tokens.shape[0]
    rows, width = queries.shape
    full_width = width * contexts
    heads = rows * classes
    half = heads // 2
    columns = labels.shape[0]
    blocks = contexts // 2
    pair = [((blocks, half, width), F32), ((blocks, half, width + LANES), BF16)]
    product = ((heads, token_count), F32)
    cost = pl.CostEstimate(flops=256 * token_count * full_width, bytes_accessed=0, transcendentals=0)

    def project_half(parts, after=()):
        kernel = functools.partial(project_kernel, len(parts))
        return call(kernel, [product], "project", [*parts, held_a, *after], cost=cost)[0]

    held_a, queries_here = load(0, width, tokens, queries)
    held_b, gain = load(1, width, tokens, norm_gain[None, :])
    first, second = gather(queries, queries_here)
    part = project_half(first, [gain])
    keep_b, send_b, own_peak, weights, left = call(
        functools.partial(pool_kernel, classes),
        [*pair, ((heads, LANES), F32), product, ((heads, token_count), BF16)],
        "pool",
        [doc_length, *second, part, held_b],
        smem_args=(0,),
        cost=cost,
    )
    half_a = call(pool_rest_kernel, pair, "pool_rest", [left, own_peak, held_a], cost=cost)
    parts = scatter_sum([half_a, (keep_b, send_b)], own_peak)
    sums, pooled, top = call(
        head_sums_kernel,
        [((2, columns), F32), ((rows, width), F32), ((rows, LANES), F32)],
        "head_sums",
        [*parts, gain, head_weight],
    )
    all_sums = [sums] + [swap(sums, bits, 0) for bits in range(1, contexts)]
    bias_grad, bias_grad_here, pooled_grad, normed = call(
        functools.partial(head_grads_kernel, full_width, contexts),
        [((1, columns), F32), ((1, columns), F32), ((rows, width + LANES), BF16), ((rows, width), F32)],
        "head_grads",
        [*all_sums, pooled, top, gain, head_weight, head_bias[None, :], labels[None, :]],
    )
    head_grad, done = head_weight_grad(normed, bias_grad_here)
    first, second = gather(pooled_grad)
    part = project_half(first)
    pair = [((blocks, half, width), F32), ((blocks, half, width), BF16)]
    keep_b, send_b, left, loss = call(
        functools.partial(grad_kernel, 1.0 / (columns * classes), classes),
        [*pair, ((heads, token_count), BF16), ((1, 1), F32)],
        "grad",
        [*second, part, held_b, weights, own_peak],
        cost=cost,
    )
    half_a = call(grad_rest_kernel, pair, "grad_rest", [left, held_a], cost=cost)
    parts = scatter_sum([half_a, (keep_b, send_b)], None, after=(done,))
    (query_grad,) = call(far_sum_kernel, [((rows, width), F32)], "far_sum", parts)
    return (loss.reshape(()), query_grad, head_grad, bias_grad.reshape(-1))


def solution(mesh):
    return jax.shard_map(
        shards,
        mesh=mesh,
        in_specs=(
            P(("ctx", "cls"), None),
            P(),
            P("cls", "ctx"),
            P("ctx"),
            P("ctx", "cls"),
            P("cls"),
            P("cls"),
        ),
        out_specs=(P(), P("cls", "ctx"), P("ctx", "cls"), P("cls")),
        check_vma=False,
    )
```

time: 107 us -> 107 us (level)
  waiting for transfers between devices: 39 us -> 31.8 us
  starting transfers between devices: 39.7 us -> 46.7 us
    ppermute x32 -> x43, waiting for transfers between devices: 39 us -> 31.8 us  [swap(): return lax.ppermute(x, ('ctx', 'cls'), pairs)]
    ppermute x32 -> x43, starting transfers between devices: 39.7 us -> 46.7 us  [swap(): return lax.ppermute(x, ('ctx', 'cls'), pairs)]
    pallas_call x14 -> x17, Pallas kernels: 19.4 us -> 18.2 us  [call(): return list(run(*args))]
    pallas_call x1 -> x2, Pallas kernels: 4.72 us -> 5.82 us  [load(): run(*[pltpu.with_memory_space_constraint(x, pltpu.HBM) for x in (tokens,...]
  transfers between devices with their start and end apart: 32 -> 43, of which waited for: 23 -> 21; matrix products, arithmetic and copies ran while one was open for 0% -> 0% of each run, Pallas kernels for 7% -> 15%
where the time goes in v6:
time: 107 us
  starting transfers between devices  46.7 us (44%)
  waiting for transfers between devices  31.8 us (30%)
  Pallas kernels  27 us (25%)
  between operations  1.5 us (1%)
    ppermute x43, starting transfers between devices, swap(): return lax.ppermute(x, ('ctx', 'cls'), pairs)  46.7 us
    ppermute x43, waiting for transfers between devices, swap(): return lax.ppermute(x, ('ctx', 'cls'), pairs)  31.8 us
    pallas_call x17, Pallas kernels, call(): return list(run(*args))  18.2 us
    pallas_call x2, Pallas kernels, load(): run(*[pltpu.with_memory_space_constraint(x, pltpu.HBM) for x in (tokens,...  5.82 us
    pallas_call x1, Pallas kernels, head_weight_grad(): pl.pallas_call(functools.partial(head_weight_grad_kernel, columns // rows...  2.95 us
  transfers between devices with their start and end apart: 43, of which 21 were waited for; matrix products, arithmetic and copies ran while one was open for 0% of the time, Pallas kernels for 15%

profile of v6, /device:TPU:0, one launch (start us, length us, event | category | flops | bytes accessed | tf_op | source)
XLA Modules:
  0.0 107.0 jit_solution(13609863386524900694)
XLA Ops:
  0.6 3.1 %collective-permute-start = (bf16[16,1024]{1,0:T(8,128)(2,1)}, bf16[16,1024]{1,0:T(8,128)(2,1)S(1)}, u32[]{:S(2)}, u32[]{:S(2)}) collective-permute-start(bf16[16,1024]{1,0:T(8,128)(2,1)} %refs_0_.1), channel_id=1, source_target_pairs={{0,8},{1,9},{2,10},{3,11},{4,12},{5,13},{6,14},{7,15},{8,0},{9,1},... | collective-permute-start | bytes 98312 | tf_op jit(solution)/shard_map/ppermute | solution.py:22
  3.7 2.5 %collective-permute-start.2 = (bf16[16,1024]{1,0:T(8,128)(2,1)}, bf16[16,1024]{1,0:T(8,128)(2,1)S(1)}, u32[]{:S(2)}, u32[]{:S(2)}) collective-permute-start(bf16[16,1024]{1,0:T(8,128)(2,1)} %refs_0_.1), channel_id=1, source_target_pairs={{0,24},{1,25},{2,26},{3,27},{4,28},{5,29},{6,30},{7,31},{8,16},{9,... | collective-permute-start | bytes 98312 | tf_op jit(solution)/shard_map/ppermute | solution.py:22
  6.3 2.9 %load.2 = (bf16[4,768,1024]{2,1,0:T(8,128)(2,1)S(1)}, bf16[16,1024]{1,0:T(8,128)(2,1)S(1)}) custom-call(bf16[768,8192]{1,0:T(8,128)(2,1)} %tokens_ref.3, bf16[16,1024]{1,0:T(8,128)(2,1)} %refs_0_.1), custom_call_target="tpu_custom_call" | custom-call | tf_op jit(solution)/shard_map/load/pallas_call | solution.py:125
  9.2 0.9 collective-permute-done.2.refs_3_
  10.1 1.5 %collective-permute-done.1.refs_2_ = bf16[16,1024]{1,0:T(8,128)(2,1)S(1)} collective-permute-done((bf16[16,1024]{1,0:T(8,128)(2,1)}, bf16[16,1024]{1,0:T(8,128)(2,1)S(1)}, u32[]{:S(2)}, u32[]{:S(2)}) %collective-permute-start.1) | collective-permute-done | bytes 32800 | tf_op jit(solution)/shard_map/ppermute | solution.py:22
  11.6 1.6 %collective-permute-start.7 = (bf16[4,16,1024]{2,1,0:T(8,128)(2,1)S(1)}, bf16[4,16,1024]{2,1,0:T(8,128)(2,1)S(1)}, u32[]{:S(2)}, u32[]{:S(2)}) collective-permute-start(bf16[4,16,1024]{2,1,0:T(8,128)(2,1)S(1)} %stack.2.refs_0_), channel_id=1, source_target_pairs={{0,2},{1,3},{2,0},{3,1},{4,6},{5,7},{6,4},{7,5},{8,10},{9,11},{10,... | collective-permute-start | bytes 393224 | tf_op jit(solution)/shard_map/ppermute | solution.py:22
  13.2 1.4 %collective-permute-start.4 = (bf16[4,16,1024]{2,1,0:T(8,128)(2,1)S(1)}, bf16[4,16,1024]{2,1,0:T(8,128)(2,1)S(1)}, u32[]{:S(2)}, u32[]{:S(2)}) collective-permute-start(bf16[4,16,1024]{2,1,0:T(8,128)(2,1)S(1)} %stack.2.refs_0_), channel_id=1, source_target_pairs={{0,6},{1,7},{2,4},{3,5},{4,2},{5,3},{6,0},{7,1},{8,14},{9,15},{10,... | collective-permute-start | bytes 393224 | tf_op jit(solution)/shard_map/ppermute | solution.py:22
  15.1 2.6 %collective-permute-done.7.refs_1_ = bf16[4,16,1024]{2,1,0:T(8,128)(2,1)S(1)} collective-permute-done((bf16[4,16,1024]{2,1,0:T(8,128)(2,1)S(1)}, bf16[4,16,1024]{2,1,0:T(8,128)(2,1)S(1)}, u32[]{:S(2)}, u32[]{:S(2)}) %collective-permute-start.7) | collective-permute-done | bytes 131104 | tf_op jit(solution)/shard_map/ppermute | solution.py:22
  18.4 2.9 %load.3 = (bf16[4,768,1024]{2,1,0:T(8,128)(2,1)S(1)}, f32[1,1024]{1,0:T(1,128)S(1)}) custom-call(bf16[768,8192]{1,0:T(8,128)(2,1)} %tokens_ref.3, f32[1,1024]{1,0:T(1,128)} %bitcast.7), custom_call_target="tpu_custom_call" | custom-call | tf_op jit(solution)/shard_map/load/pallas_call | solution.py:125
  22.0 2.0 %project.2.refs_4_ = f32[64,768]{1,0:T(8,128)S(1)} custom-call(bf16[4,16,1024]{2,1,0:T(8,128)(2,1)S(1)} %stack.2.refs_0_, bf16[4,16,1024]{2,1,0:T(8,128)(2,1)S(1)} %collective-permute-done.7.refs_1_, bf16[4,16,1024]{2,1,0:T(8,128)(2,1)S(1)} %collective-permute-done.8.refs_2_, bf16[4,16,1024]{2,1,0:T(8,128)(2,1)S(1)} %collective-permute-done.9.refs_3_, ...), custom_call_target="tpu_custom_call" | custom-call | flops 1610612736 | tf_op jit(solution)/shard_map/project/pallas_call | solution.py:52
  24.1 4.2 %pool.1 = (f32[4,32,1024]{2,1,0:T(8,128)S(1)}, bf16[4,32,1152]{2,1,0:T(8,128)(2,1)S(1)}, f32[64,128]{1,0:T(8,128)S(1)}, f32[64,768]{1,0:T(8,128)S(1)}, bf16[64,768]{1,0:T(8,128)(2,1)S(1)}) custom-call(s32[1]{0:T(128)S(6)} %copy.11.length_ref, bf16[4,16,1024]{2,1,0:T(8,128)(2,1)S(1)} %collective-permute-done.3.refs_0_, ...), custom_call_target="tpu_custom_call" | custom-call | flops 1610612736 | tf_op jit(solution)/shard_map/pool/pallas_call | solution.py:52
  28.8 1.2 %pool_rest.1 = (f32[4,32,1024]{2,1,0:T(8,128)S(1)}, bf16[4,32,1152]{2,1,0:T(8,128)(2,1)S(1)}) custom-call(bf16[64,768]{1,0:T(8,128)(2,1)S(1)} %get-tuple-element.52.left_ref, f32[64,128]{1,0:T(8,128)S(1)} %get-tuple-element.53.peak_ref.refs_2_.refs_7_, bf16[4,768,1024]{2,1,0:T(8,128)(2,1)S(1)} %get-tuple-element.49.refs_4_.held_ref), custom_call_target="tpu_custom_call" | custom-call | flops 1610612736 | tf_op jit(solution)/shard_map/pool_rest/pallas_call | solution.py:52
  30.4 3.2 %collective-permute-start.12 = (bf16[4,16,1152]{2,1,0:T(8,128)(2,1)S(1)}, bf16[4,16,1152]{2,1,0:T(8,128)(2,1)S(1)}, u32[]{:S(2)}, u32[]{:S(2)}) collective-permute-start(bf16[4,16,1152]{2,1,0:T(8,128)(2,1)S(1)} %get-tuple-element.60), channel_id=1, source_target_pairs={{0,6},{1,7},{2,4},{3,5},{4,2},{5,3},{6,0},{7,1},{8,14},{9,15},{10,... | collective-permute-start | bytes 442376 | tf_op jit(solution)/shard_map/ppermute | solution.py:22
  34.6 3.7 %collective-permute-done.12.refs_1_ = bf16[4,16,1152]{2,1,0:T(8,128)(2,1)S(1)} collective-permute-done((bf16[4,16,1152]{2,1,0:T(8,128)(2,1)S(1)}, bf16[4,16,1152]{2,1,0:T(8,128)(2,1)S(1)}, u32[]{:S(2)}, u32[]{:S(2)}) %collective-permute-start.12) | collective-permute-done | bytes 147488 | tf_op jit(solution)/shard_map/ppermute | solution.py:22
  38.3 3.2 %collective-permute-done.14.refs_3_ = bf16[4,16,1152]{2,1,0:T(8,128)(2,1)S(1)} collective-permute-done((bf16[4,16,1152]{2,1,0:T(8,128)(2,1)S(1)}, bf16[4,16,1152]{2,1,0:T(8,128)(2,1)S(1)}, u32[]{:S(2)}, u32[]{:S(2)}) %collective-permute-start.14) | collective-permute-done | bytes 147488 | tf_op jit(solution)/shard_map/ppermute | solution.py:22
  41.8 1.8 %collective-permute-start.15 = (bf16[1,16,1152]{2,1,0:T(8,128)(2,1)S(1)}, bf16[1,16,1152]{2,1,0:T(8,128)(2,1)S(1)}, u32[]{:S(2)}, u32[]{:S(2)}) collective-permute-start(bf16[1,16,1152]{2,1,0:T(8,128)(2,1)S(1)} %get-tuple-element.64), channel_id=1, source_target_pairs={{0,24},{1,25},{2,26},{3,27},{4,28},{5,29},{6,30},{7,31},{8,16},{9,... | collective-permute-start | bytes 110600 | tf_op jit(solution)/shard_map/ppermute | solution.py:22
  43.7 2.6 %collective-permute-start.17 = (bf16[1,16,1152]{2,1,0:T(8,128)(2,1)S(1)}, bf16[1,16,1152]{2,1,0:T(8,128)(2,1)S(1)}, u32[]{:S(2)}, u32[]{:S(2)}) collective-permute-start(bf16[1,16,1152]{2,1,0:T(8,128)(2,1)S(1)} %get-tuple-element.66), channel_id=1, source_target_pairs={{0,8},{1,9},{2,10},{3,11},{4,12},{5,13},{6,14},{7,15},{8,0},{9,1},... | collective-permute-start | bytes 110600 | tf_op jit(solution)/shard_map/ppermute | solution.py:22
  46.3 1.4 %collective-permute-done.15.refs_1_ = bf16[1,16,1152]{2,1,0:T(8,128)(2,1)S(1)} collective-permute-done((bf16[1,16,1152]{2,1,0:T(8,128)(2,1)S(1)}, bf16[1,16,1152]{2,1,0:T(8,128)(2,1)S(1)}, u32[]{:S(2)}, u32[]{:S(2)}) %collective-permute-start.15) | collective-permute-done | bytes 36896 | tf_op jit(solution)/shard_map/ppermute | solution.py:22
  47.7 1.0 collective-permute-done.16.refs_2_
  49.3 2.9 %collective-permute-start.24 = (f32[2,1024]{1,0:T(2,128)S(1)}, f32[2,1024]{1,0:T(2,128)S(1)}, u32[]{:S(2)}, u32[]{:S(2)}) collective-permute-start(f32[2,1024]{1,0:T(2,128)S(1)} %get-tuple-element.68.refs_0_), channel_id=1, source_target_pairs={{0,28},{1,29},{2,30},{3,31},{4,24},{5,25},{6,26},{7,27},{8,20},{9,... | collective-permute-start | bytes 24584 | tf_op jit(solution)/shard_map/ppermute | solution.py:22
  52.2 1.9 %collective-permute-start.23 = (f32[2,1024]{1,0:T(2,128)S(1)}, f32[2,1024]{1,0:T(2,128)S(1)}, u32[]{:S(2)}, u32[]{:S(2)}) collective-permute-start(f32[2,1024]{1,0:T(2,128)S(1)} %get-tuple-element.68.refs_0_), channel_id=1, source_target_pairs={{0,24},{1,25},{2,26},{3,27},{4,28},{5,29},{6,30},{7,31},{8,16},{9,... | collective-permute-start | bytes 24584 | tf_op jit(solution)/shard_map/ppermute | solution.py:22
  54.1 2.9 %collective-permute-start.21 = (f32[2,1024]{1,0:T(2,128)S(1)}, f32[2,1024]{1,0:T(2,128)S(1)}, u32[]{:S(2)}, u32[]{:S(2)}) collective-permute-start(f32[2,1024]{1,0:T(2,128)S(1)} %get-tuple-element.68.refs_0_), channel_id=1, source_target_pairs={{0,16},{1,17},{2,18},{3,19},{4,20},{5,21},{6,22},{7,23},{8,24},{9,... | collective-permute-start | bytes 24584 | tf_op jit(solution)/shard_map/ppermute | solution.py:22
  57.7 2.3 %collective-permute-start.19 = (f32[2,1024]{1,0:T(2,128)S(1)}, f32[2,1024]{1,0:T(2,128)S(1)}, u32[]{:S(2)}, u32[]{:S(2)}) collective-permute-start(f32[2,1024]{1,0:T(2,128)S(1)} %get-tuple-element.68.refs_0_), channel_id=1, source_target_pairs={{0,8},{1,9},{2,10},{3,11},{4,12},{5,13},{6,14},{7,15},{8,0},{9,1},... | collective-permute-start | bytes 24584 | tf_op jit(solution)/shard_map/ppermute | solution.py:22
  60.5 1.0 collective-permute-done.20.refs_3_
  61.7 1.9 %collective-permute-done.18.refs_1_ = f32[2,1024]{1,0:T(2,128)S(1)} collective-permute-done((f32[2,1024]{1,0:T(2,128)S(1)}, f32[2,1024]{1,0:T(2,128)S(1)}, u32[]{:S(2)}, u32[]{:S(2)}) %collective-permute-start.18) | collective-permute-done | bytes 8224 | tf_op jit(solution)/shard_map/ppermute | solution.py:22
  63.7 1.2 %head_grads.1 = (f32[1,1024]{1,0:T(1,128)}, f32[1,1024]{1,0:T(1,128)S(1)}, bf16[16,1152]{1,0:T(8,128)(2,1)S(1)}, f32[16,1024]{1,0:T(8,128)S(1)}) custom-call(f32[2,1024]{1,0:T(2,128)S(1)} %get-tuple-element.68.refs_0_, f32[2,1024]{1,0:T(2,128)S(1)} %collective-permute-done.18.refs_1_, f32[2,1024]{1,0:T(2,128)S(1)} %collective-permute-done.19.refs_2_, ...), custom_call_target="tpu_custom_call" | custom-call | tf_op jit(solution)/shard_map/head_grads/pallas_call | solution.py:52
  64.9 1.9 %collective-permute-start.27 = (bf16[16,1152]{1,0:T(8,128)(2,1)S(1)}, bf16[16,1152]{1,0:T(8,128)(2,1)S(1)}, u32[]{:S(2)}, u32[]{:S(2)}) collective-permute-start(bf16[16,1152]{1,0:T(8,128)(2,1)S(1)} %get-tuple-element.71.refs_0_), channel_id=1, source_target_pairs={{0,24},{1,25},{2,26},{3,27},{4,28},{5,29},{6,30},{7,31},{8,16},{9,... | collective-permute-start | bytes 110600 | tf_op jit(solution)/shard_map/ppermute | solution.py:22
  66.8 2.5 %collective-permute-start.25 = (bf16[16,1152]{1,0:T(8,128)(2,1)S(1)}, bf16[16,1152]{1,0:T(8,128)(2,1)S(1)}, u32[]{:S(2)}, u32[]{:S(2)}) collective-permute-start(bf16[16,1152]{1,0:T(8,128)(2,1)S(1)} %get-tuple-element.71.refs_0_), channel_id=1, source_target_pairs={{0,8},{1,9},{2,10},{3,11},{4,12},{5,13},{6,14},{7,15},{8,0},{9,1},... | collective-permute-start | bytes 110600 | tf_op jit(solution)/shard_map/ppermute | solution.py:22
  69.3 1.4 %collective-permute-done.27.refs_3_ = bf16[16,1152]{1,0:T(8,128)(2,1)S(1)} collective-permute-done((bf16[16,1152]{1,0:T(8,128)(2,1)S(1)}, bf16[16,1152]{1,0:T(8,128)(2,1)S(1)}, u32[]{:S(2)}, u32[]{:S(2)}) %collective-permute-start.27) | collective-permute-done | bytes 36896 | tf_op jit(solution)/shard_map/ppermute | solution.py:22
  70.6 1.0 collective-permute-done.26.refs_2_
  71.6 1.6 %collective-permute-start.32 = (bf16[4,16,1152]{2,1,0:T(8,128)(2,1)S(1)}, bf16[4,16,1152]{2,1,0:T(8,128)(2,1)S(1)}, u32[]{:S(2)}, u32[]{:S(2)}) collective-permute-start(bf16[4,16,1152]{2,1,0:T(8,128)(2,1)S(1)} %stack.3.refs_0_), channel_id=1, source_target_pairs={{0,2},{1,3},{2,0},{3,1},{4,6},{5,7},{6,4},{7,5},{8,10},{9,11},{10,... | collective-permute-start | bytes 442376 | tf_op jit(solution)/shard_map/ppermute | solution.py:22
  73.7 1.5 %collective-permute-start.28 = (bf16[4,16,1152]{2,1,0:T(8,128)(2,1)S(1)}, bf16[4,16,1152]{2,1,0:T(8,128)(2,1)S(1)}, u32[]{:S(2)}, u32[]{:S(2)}) collective-permute-start(bf16[4,16,1152]{2,1,0:T(8,128)(2,1)S(1)} %stack.3.refs_0_), channel_id=1, source_target_pairs={{0,4},{1,5},{2,6},{3,7},{4,0},{5,1},{6,2},{7,3},{8,12},{9,13},{10,... | collective-permute-start | bytes 442376 | tf_op jit(solution)/shard_map/ppermute | solution.py:22
  75.2 1.6 %collective-permute-done.32.refs_1_ = bf16[4,16,1152]{2,1,0:T(8,128)(2,1)S(1)} collective-permute-done((bf16[4,16,1152]{2,1,0:T(8,128)(2,1)S(1)}, bf16[4,16,1152]{2,1,0:T(8,128)(2,1)S(1)}, u32[]{:S(2)}, u32[]{:S(2)}) %collective-permute-start.32) | collective-permute-done | bytes 147488 | tf_op jit(solution)/shard_map/ppermute | solution.py:22
  76.8 2.5 %collective-permute-done.29.refs_1_ = bf16[4,16,1152]{2,1,0:T(8,128)(2,1)S(1)} collective-permute-done((bf16[4,16,1152]{2,1,0:T(8,128)(2,1)S(1)}, bf16[4,16,1152]{2,1,0:T(8,128)(2,1)S(1)}, u32[]{:S(2)}, u32[]{:S(2)}) %collective-permute-start.29) | collective-permute-done | bytes 147488 | tf_op jit(solution)/shard_map/ppermute | solution.py:22
  79.9 2.0 %project.3.refs_4_ = f32[64,768]{1,0:T(8,128)S(1)} custom-call(bf16[4,16,1152]{2,1,0:T(8,128)(2,1)S(1)} %stack.3.refs_0_, bf16[4,16,1152]{2,1,0:T(8,128)(2,1)S(1)} %collective-permute-done.32.refs_1_, bf16[4,16,1152]{2,1,0:T(8,128)(2,1)S(1)} %collective-permute-done.33.refs_2_, bf16[4,16,1152]{2,1,0:T(8,128)(2,1)S(1)} %collective-permute-done.34.refs_3_, ...), custom_call_target="tpu_custom_call" | custom-call | flops 1610612736 | tf_op jit(solution)/shard_map/project/pallas_call | solution.py:52
  82.0 4.0 %grad.1 = (f32[4,32,1024]{2,1,0:T(8,128)S(1)}, bf16[4,32,1024]{2,1,0:T(8,128)(2,1)S(1)}, bf16[64,768]{1,0:T(8,128)(2,1)S(1)}, f32[1,1]{1,0:T(1,128)}) custom-call(bf16[4,16,1152]{2,1,0:T(8,128)(2,1)S(1)} %collective-permute-done.28.refs_0_, bf16[4,16,1152]{2,1,0:T(8,128)(2,1)S(1)} %collective-permute-done.29.refs_1_, ...), custom_call_target="tpu_custom_call" | custom-call | flops 1610612736 | tf_op jit(solution)/shard_map/grad/pallas_call | solution.py:52
  86.6 1.2 %grad_rest.1 = (f32[4,32,1024]{2,1,0:T(8,128)S(1)}, bf16[4,32,1024]{2,1,0:T(8,128)(2,1)S(1)}) custom-call(bf16[64,768]{1,0:T(8,128)(2,1)S(1)} %get-tuple-element.74.left_ref, bf16[4,768,1024]{2,1,0:T(8,128)(2,1)S(1)} %get-tuple-element.49.refs_4_.held_ref), custom_call_target="tpu_custom_call" | custom-call | flops 1610612736 | tf_op jit(solution)/shard_map/grad_rest/pallas_call | solution.py:52
  87.9 1.5 %collective-permute-done.35.refs_1_ = bf16[4,32,1024]{2,1,0:T(8,128)(2,1)S(1)} collective-permute-done((bf16[4,32,1024]{2,1,0:T(8,128)(2,1)S(1)}, bf16[4,32,1024]{2,1,0:T(8,128)(2,1)S(1)}, u32[]{:S(2)}, u32[]{:S(2)}) %collective-permute-start.35) | collective-permute-done | bytes 262176 | tf_op jit(solution)/shard_map/ppermute | solution.py:22
  89.4 1.6 %collective-permute-start.38 = (bf16[4,16,1024]{2,1,0:T(8,128)(2,1)S(1)}, bf16[4,16,1024]{2,1,0:T(8,128)(2,1)S(1)}, u32[]{:S(2)}, u32[]{:S(2)}) collective-permute-start(bf16[4,16,1024]{2,1,0:T(8,128)(2,1)S(1)} %get-tuple-element.82), channel_id=1, source_target_pairs={{0,2},{1,3},{2,0},{3,1},{4,6},{5,7},{6,4},{7,5},{8,10},{9,11},{10,... | collective-permute-start | bytes 393224 | tf_op jit(solution)/shard_map/ppermute | solution.py:22
  91.5 1.5 %collective-permute-start.39 = (bf16[4,16,1024]{2,1,0:T(8,128)(2,1)S(1)}, bf16[4,16,1024]{2,1,0:T(8,128)(2,1)S(1)}, u32[]{:S(2)}, u32[]{:S(2)}) collective-permute-start(bf16[4,16,1024]{2,1,0:T(8,128)(2,1)S(1)} %get-tuple-element.79.refs_2_), channel_id=1, source_target_pairs={{0,4},{1,5},{2,6},{3,7},{4,0},{5,1},{6,2},{7,3},{8,12},{9,13},{10,... | collective-permute-start | bytes 393224 | tf_op jit(solution)/shard_map/ppermute | solution.py:22
  93.0 3.0 %head_weight_grad.1 = (f32[1024,1024]{1,0:T(8,128)}, f32[8,128]{1,0:T(8,128)S(1)}) custom-call(f32[16,1024]{1,0:T(8,128)S(1)} %get-tuple-element.83.normed_ref, f32[1,1024]{1,0:T(1,128)S(1)} %get-tuple-element.84.bias_grad_ref), custom_call_target="tpu_custom_call" | custom-call | flops 100663296 | bytes 4194304 | tf_op jit(solution)/shard_map/head_weight_grad/pallas_call | solution.py:361
  95.9 1.4 %collective-permute-done.38.refs_2_ = bf16[4,16,1024]{2,1,0:T(8,128)(2,1)S(1)} collective-permute-done((bf16[4,16,1024]{2,1,0:T(8,128)(2,1)S(1)}, bf16[4,16,1024]{2,1,0:T(8,128)(2,1)S(1)}, u32[]{:S(2)}, u32[]{:S(2)}) %collective-permute-start.38) | collective-permute-done | bytes 131104 | tf_op jit(solution)/shard_map/ppermute | solution.py:22
  97.4 0.9 collective-permute-done.37.refs_1_
  99.1 2.0 %collective-permute-start.40 = (bf16[1,16,1024]{2,1,0:T(8,128)(2,1)S(1)}, bf16[1,16,1024]{2,1,0:T(8,128)(2,1)S(1)}, u32[]{:S(2)}, u32[]{:S(2)}) collective-permute-start(bf16[1,16,1024]{2,1,0:T(8,128)(2,1)S(1)} %get-tuple-element.87), channel_id=1, source_target_pairs={{0,24},{1,25},{2,26},{3,27},{4,28},{5,29},{6,30},{7,31},{8,16},{9,... | collective-permute-start | bytes 98312 | tf_op jit(solution)/shard_map/ppermute | solution.py:22
  101.2 1.1 %collective-permute-start.41 = (bf16[1,16,1024]{2,1,0:T(8,128)(2,1)S(1)}, bf16[1,16,1024]{2,1,0:T(8,128)(2,1)S(1)}, u32[]{:S(2)}, u32[]{:S(2)}) collective-permute-start(bf16[1,16,1024]{2,1,0:T(8,128)(2,1)S(1)} %get-tuple-element.88), channel_id=1, source_target_pairs={{0,16},{1,17},{2,18},{3,19},{4,20},{5,21},{6,22},{7,23},{8,24},{9,... | collective-permute-start | bytes 98312 | tf_op jit(solution)/shard_map/ppermute | solution.py:22
  102.3 1.3 %collective-permute-start.42 = (bf16[1,16,1024]{2,1,0:T(8,128)(2,1)S(1)}, bf16[1,16,1024]{2,1,0:T(8,128)(2,1)S(1)}, u32[]{:S(2)}, u32[]{:S(2)}) collective-permute-start(bf16[1,16,1024]{2,1,0:T(8,128)(2,1)S(1)} %get-tuple-element.89), channel_id=1, source_target_pairs={{0,8},{1,9},{2,10},{3,11},{4,12},{5,13},{6,14},{7,15},{8,0},{9,1},... | collective-permute-start | bytes 98312 | tf_op jit(solution)/shard_map/ppermute | solution.py:22
  103.6 1.7 %collective-permute-done.40.refs_1_ = bf16[1,16,1024]{2,1,0:T(8,128)(2,1)S(1)} collective-permute-done((bf16[1,16,1024]{2,1,0:T(8,128)(2,1)S(1)}, bf16[1,16,1024]{2,1,0:T(8,128)(2,1)S(1)}, u32[]{:S(2)}, u32[]{:S(2)}) %collective-permute-start.40) | collective-permute-done | bytes 32800 | tf_op jit(solution)/shard_map/ppermute | solution.py:22
  105.3 1.1 %collective-permute-done.41.refs_2_ = bf16[1,16,1024]{2,1,0:T(8,128)(2,1)S(1)} collective-permute-done((bf16[1,16,1024]{2,1,0:T(8,128)(2,1)S(1)}, bf16[1,16,1024]{2,1,0:T(8,128)(2,1)S(1)}, u32[]{:S(2)}, u32[]{:S(2)}) %collective-permute-start.41) | collective-permute-done | bytes 32800 | tf_op jit(solution)/shard_map/ppermute | solution.py:22
  (64 shorter events, 9.6 us)
Async XLA Ops:
  0.6 8.6 %collective-permute-start = (bf16[16,1024]{1,0:T(8,128)(2,1)}, bf16[16,1024]{1,0:T(8,128)(2,1)S(1)}, u32[]{:S(2)}, u32[]{:S(2)}) collective-permute-start(bf16[16,1024]{1,0:T(8,128)(2,1)} %refs_0_.1), channel_id=1, source_target_pairs={{0,8},{1,9},{2,10},{3,11},{4,12},{5,13},{6,14},{7,15},{8,0},{9,1},... | collective-permute-start | bytes 98312 | tf_op jit(solution)/shard_map/ppermute | solution.py:22
  3.7 6.4 %collective-permute-start.2 = (bf16[16,1024]{1,0:T(8,128)(2,1)}, bf16[16,1024]{1,0:T(8,128)(2,1)S(1)}, u32[]{:S(2)}, u32[]{:S(2)}) collective-permute-start(bf16[16,1024]{1,0:T(8,128)(2,1)} %refs_0_.1), channel_id=1, source_target_pairs={{0,24},{1,25},{2,26},{3,27},{4,28},{5,29},{6,30},{7,31},{8,16},{9,... | collective-permute-start | bytes 98312 | tf_op jit(solution)/shard_map/ppermute | solution.py:22
  6.2 5.4 %collective-permute-start.1 = (bf16[16,1024]{1,0:T(8,128)(2,1)}, bf16[16,1024]{1,0:T(8,128)(2,1)S(1)}, u32[]{:S(2)}, u32[]{:S(2)}) collective-permute-start(bf16[16,1024]{1,0:T(8,128)(2,1)} %refs_0_.1), channel_id=1, source_target_pairs={{0,16},{1,17},{2,18},{3,19},{4,20},{5,21},{6,22},{7,23},{8,24},{9,... | collective-permute-start | bytes 98312 | tf_op jit(solution)/shard_map/ppermute | solution.py:22
  11.6 6.2 %collective-permute-start.7 = (bf16[4,16,1024]{2,1,0:T(8,128)(2,1)S(1)}, bf16[4,16,1024]{2,1,0:T(8,128)(2,1)S(1)}, u32[]{:S(2)}, u32[]{:S(2)}) collective-permute-start(bf16[4,16,1024]{2,1,0:T(8,128)(2,1)S(1)} %stack.2.refs_0_), channel_id=1, source_target_pairs={{0,2},{1,3},{2,0},{3,1},{4,6},{5,7},{6,4},{7,5},{8,10},{9,11},{10,... | collective-permute-start | bytes 393224 | tf_op jit(solution)/shard_map/ppermute | solution.py:22
  13.2 8.2 %collective-permute-start.4 = (bf16[4,16,1024]{2,1,0:T(8,128)(2,1)S(1)}, bf16[4,16,1024]{2,1,0:T(8,128)(2,1)S(1)}, u32[]{:S(2)}, u32[]{:S(2)}) collective-permute-start(bf16[4,16,1024]{2,1,0:T(8,128)(2,1)S(1)} %stack.2.refs_0_), channel_id=1, source_target_pairs={{0,6},{1,7},{2,4},{3,5},{4,2},{5,3},{6,0},{7,1},{8,14},{9,15},{10,... | collective-permute-start | bytes 393224 | tf_op jit(solution)/shard_map/ppermute | solution.py:22
  14.6 7.3 %collective-permute-start.3 = (bf16[4,16,1024]{2,1,0:T(8,128)(2,1)S(1)}, bf16[4,16,1024]{2,1,0:T(8,128)(2,1)S(1)}, u32[]{:S(2)}, u32[]{:S(2)}) collective-permute-start(bf16[4,16,1024]{2,1,0:T(8,128)(2,1)S(1)} %stack.2.refs_0_), channel_id=1, source_target_pairs={{0,4},{1,5},{2,6},{3,7},{4,0},{5,1},{6,2},{7,3},{8,12},{9,13},{10,... | collective-permute-start | bytes 393224 | tf_op jit(solution)/shard_map/ppermute | solution.py:22
  15.1 6.9 %collective-permute-start.8 = (bf16[4,16,1024]{2,1,0:T(8,128)(2,1)S(1)}, bf16[4,16,1024]{2,1,0:T(8,128)(2,1)S(1)}, u32[]{:S(2)}, u32[]{:S(2)}) collective-permute-start(bf16[4,16,1024]{2,1,0:T(8,128)(2,1)S(1)} %stack.2.refs_0_), channel_id=1, source_target_pairs={{0,1},{1,0},{2,3},{3,2},{4,5},{5,4},{6,7},{7,6},{8,9},{9,8},{10,11... | collective-permute-start | bytes 393224 | tf_op jit(solution)/shard_map/ppermute | solution.py:22
  17.7 4.3 %collective-permute-start.9 = (bf16[4,16,1024]{2,1,0:T(8,128)(2,1)S(1)}, bf16[4,16,1024]{2,1,0:T(8,128)(2,1)S(1)}, u32[]{:S(2)}, u32[]{:S(2)}) collective-permute-start(bf16[4,16,1024]{2,1,0:T(8,128)(2,1)S(1)} %collective-permute-done.7.refs_1_), channel_id=1, source_target_pairs={{0,1},{1,0},{2,3},{3,2},{4,5},{5,4},{6,7},{7,6},{8,9},{9,8},{10,11... | collective-permute-start | bytes 393224 | tf_op jit(solution)/shard_map/ppermute | solution.py:22
  21.3 2.7 %collective-permute-start.6 = (bf16[4,16,1024]{2,1,0:T(8,128)(2,1)S(1)}, bf16[4,16,1024]{2,1,0:T(8,128)(2,1)S(1)}, u32[]{:S(2)}, u32[]{:S(2)}) collective-permute-start(bf16[4,16,1024]{2,1,0:T(8,128)(2,1)S(1)} %collective-permute-done.4.refs_1_), channel_id=1, source_target_pairs={{0,1},{1,0},{2,3},{3,2},{4,5},{5,4},{6,7},{7,6},{8,9},{9,8},{10,11... | collective-permute-start | bytes 393224 | tf_op jit(solution)/shard_map/ppermute | solution.py:22
  21.9 2.1 %collective-permute-start.5 = (bf16[4,16,1024]{2,1,0:T(8,128)(2,1)S(1)}, bf16[4,16,1024]{2,1,0:T(8,128)(2,1)S(1)}, u32[]{:S(2)}, u32[]{:S(2)}) collective-permute-start(bf16[4,16,1024]{2,1,0:T(8,128)(2,1)S(1)} %collective-permute-done.3.refs_0_), channel_id=1, source_target_pairs={{0,1},{1,0},{2,3},{3,2},{4,5},{5,4},{6,7},{7,6},{8,9},{9,8},{10,11... | collective-permute-start | bytes 393224 | tf_op jit(solution)/shard_map/ppermute | solution.py:22
  24.0 24.7 %copy-start = (bf16[1024,1024]{1,0:T(8,128)(2,1)S(1)}, bf16[1024,1024]{1,0:T(8,128)(2,1)}, u32[]{:S(2)}) copy-start(bf16[1024,1024]{1,0:T(8,128)(2,1)} %refs_11_.1) | copy-start | bytes 6291460
  28.2 35.4 %copy-start.1 = (f32[1024]{0:T(1024)S(1)}, f32[1024]{0:T(1024)}, u32[]{:S(2)}) copy-start(f32[1024]{0:T(1024)} %param.12) | copy-start | bytes 12292
  28.2 35.4 %copy-start.2 = (s32[1024]{0:T(1024)S(1)}, s32[1024]{0:T(1024)}, u32[]{:S(2)}) copy-start(s32[1024]{0:T(1024)} %param.13) | copy-start | bytes 12292
  28.3 1.8 %collective-permute-start.11 = (bf16[4,32,1152]{2,1,0:T(8,128)(2,1)S(1)}, bf16[4,32,1152]{2,1,0:T(8,128)(2,1)S(1)}, u32[]{:S(2)}, u32[]{:S(2)}) collective-permute-start(bf16[4,32,1152]{2,1,0:T(8,128)(2,1)S(1)} %get-tuple-element.57), channel_id=1, source_target_pairs={{0,1},{1,0},{2,3},{3,2},{4,5},{5,4},{6,7},{7,6},{8,9},{9,8},{10,11... | collective-permute-start | bytes 884744 | tf_op jit(solution)/shard_map/ppermute | solution.py:22
  30.0 4.2 %collective-permute-start.10 = (bf16[4,32,1152]{2,1,0:T(8,128)(2,1)S(1)}, bf16[4,32,1152]{2,1,0:T(8,128)(2,1)S(1)}, u32[]{:S(2)}, u32[]{:S(2)}) collective-permute-start(bf16[4,32,1152]{2,1,0:T(8,128)(2,1)S(1)} %get-tuple-element.55), channel_id=1, source_target_pairs={{0,1},{1,0},{2,3},{3,2},{4,5},{5,4},{6,7},{7,6},{8,9},{9,8},{10,11... | collective-permute-start | bytes 884744 | tf_op jit(solution)/shard_map/ppermute | solution.py:22
  30.4 7.9 %collective-permute-start.12 = (bf16[4,16,1152]{2,1,0:T(8,128)(2,1)S(1)}, bf16[4,16,1152]{2,1,0:T(8,128)(2,1)S(1)}, u32[]{:S(2)}, u32[]{:S(2)}) collective-permute-start(bf16[4,16,1152]{2,1,0:T(8,128)(2,1)S(1)} %get-tuple-element.60), channel_id=1, source_target_pairs={{0,6},{1,7},{2,4},{3,5},{4,2},{5,3},{6,0},{7,1},{8,14},{9,15},{10,... | collective-permute-start | bytes 442376 | tf_op jit(solution)/shard_map/ppermute | solution.py:22
  33.6 7.9 %collective-permute-start.14 = (bf16[4,16,1152]{2,1,0:T(8,128)(2,1)S(1)}, bf16[4,16,1152]{2,1,0:T(8,128)(2,1)S(1)}, u32[]{:S(2)}, u32[]{:S(2)}) collective-permute-start(bf16[4,16,1152]{2,1,0:T(8,128)(2,1)S(1)} %get-tuple-element.58.refs_3_), channel_id=1, source_target_pairs={{0,4},{1,5},{2,6},{3,7},{4,0},{5,1},{6,2},{7,3},{8,12},{9,13},{10,... | collective-permute-start | bytes 442376 | tf_op jit(solution)/shard_map/ppermute | solution.py:22
  34.4 7.1 %collective-permute-start.13 = (bf16[4,16,1152]{2,1,0:T(8,128)(2,1)S(1)}, bf16[4,16,1152]{2,1,0:T(8,128)(2,1)S(1)}, u32[]{:S(2)}, u32[]{:S(2)}) collective-permute-start(bf16[4,16,1152]{2,1,0:T(8,128)(2,1)S(1)} %get-tuple-element.61), channel_id=1, source_target_pairs={{0,2},{1,3},{2,0},{3,1},{4,6},{5,7},{6,4},{7,5},{8,10},{9,11},{10,... | collective-permute-start | bytes 442376 | tf_op jit(solution)/shard_map/ppermute | solution.py:22
  41.8 5.8 %collective-permute-start.15 = (bf16[1,16,1152]{2,1,0:T(8,128)(2,1)S(1)}, bf16[1,16,1152]{2,1,0:T(8,128)(2,1)S(1)}, u32[]{:S(2)}, u32[]{:S(2)}) collective-permute-start(bf16[1,16,1152]{2,1,0:T(8,128)(2,1)S(1)} %get-tuple-element.64), channel_id=1, source_target_pairs={{0,24},{1,25},{2,26},{3,27},{4,28},{5,29},{6,30},{7,31},{8,16},{9,... | collective-permute-start | bytes 110600 | tf_op jit(solution)/shard_map/ppermute | solution.py:22
  43.6 5.1 %collective-permute-start.16 = (bf16[1,16,1152]{2,1,0:T(8,128)(2,1)S(1)}, bf16[1,16,1152]{2,1,0:T(8,128)(2,1)S(1)}, u32[]{:S(2)}, u32[]{:S(2)}) collective-permute-start(bf16[1,16,1152]{2,1,0:T(8,128)(2,1)S(1)} %get-tuple-element.65), channel_id=1, source_target_pairs={{0,16},{1,17},{2,18},{3,19},{4,20},{5,21},{6,22},{7,23},{8,24},{9,... | collective-permute-start | bytes 110600 | tf_op jit(solution)/shard_map/ppermute | solution.py:22
  43.7 5.0 %collective-permute-start.17 = (bf16[1,16,1152]{2,1,0:T(8,128)(2,1)S(1)}, bf16[1,16,1152]{2,1,0:T(8,128)(2,1)S(1)}, u32[]{:S(2)}, u32[]{:S(2)}) collective-permute-start(bf16[1,16,1152]{2,1,0:T(8,128)(2,1)S(1)} %get-tuple-element.66), channel_id=1, source_target_pairs={{0,8},{1,9},{2,10},{3,11},{4,12},{5,13},{6,14},{7,15},{8,0},{9,1},... | collective-permute-start | bytes 110600 | tf_op jit(solution)/shard_map/ppermute | solution.py:22
  49.3 8.4 %collective-permute-start.24 = (f32[2,1024]{1,0:T(2,128)S(1)}, f32[2,1024]{1,0:T(2,128)S(1)}, u32[]{:S(2)}, u32[]{:S(2)}) collective-permute-start(f32[2,1024]{1,0:T(2,128)S(1)} %get-tuple-element.68.refs_0_), channel_id=1, source_target_pairs={{0,28},{1,29},{2,30},{3,31},{4,24},{5,25},{6,26},{7,27},{8,20},{9,... | collective-permute-start | bytes 24584 | tf_op jit(solution)/shard_map/ppermute | solution.py:22
  52.2 7.8 %collective-permute-start.23 = (f32[2,1024]{1,0:T(2,128)S(1)}, f32[2,1024]{1,0:T(2,128)S(1)}, u32[]{:S(2)}, u32[]{:S(2)}) collective-permute-start(f32[2,1024]{1,0:T(2,128)S(1)} %get-tuple-element.68.refs_0_), channel_id=1, source_target_pairs={{0,24},{1,25},{2,26},{3,27},{4,28},{5,29},{6,30},{7,31},{8,16},{9,... | collective-permute-start | bytes 24584 | tf_op jit(solution)/shard_map/ppermute | solution.py:22
  54.1 6.4 %collective-permute-start.22 = (f32[2,1024]{1,0:T(2,128)S(1)}, f32[2,1024]{1,0:T(2,128)S(1)}, u32[]{:S(2)}, u32[]{:S(2)}) collective-permute-start(f32[2,1024]{1,0:T(2,128)S(1)} %get-tuple-element.68.refs_0_), channel_id=1, source_target_pairs={{0,20},{1,21},{2,22},{3,23},{4,16},{5,17},{6,18},{7,19},{8,28},{9,... | collective-permute-start | bytes 24584 | tf_op jit(solution)/shard_map/ppermute | solution.py:22
  54.1 6.4 %collective-permute-start.21 = (f32[2,1024]{1,0:T(2,128)S(1)}, f32[2,1024]{1,0:T(2,128)S(1)}, u32[]{:S(2)}, u32[]{:S(2)}) collective-permute-start(f32[2,1024]{1,0:T(2,128)S(1)} %get-tuple-element.68.refs_0_), channel_id=1, source_target_pairs={{0,16},{1,17},{2,18},{3,19},{4,20},{5,21},{6,22},{7,23},{8,24},{9,... | collective-permute-start | bytes 24584 | tf_op jit(solution)/shard_map/ppermute | solution.py:22
  57.0 4.5 %collective-permute-start.20 = (f32[2,1024]{1,0:T(2,128)S(1)}, f32[2,1024]{1,0:T(2,128)S(1)}, u32[]{:S(2)}, u32[]{:S(2)}) collective-permute-start(f32[2,1024]{1,0:T(2,128)S(1)} %get-tuple-element.68.refs_0_), channel_id=1, source_target_pairs={{0,12},{1,13},{2,14},{3,15},{4,8},{5,9},{6,10},{7,11},{8,4},{9,5},... | collective-permute-start | bytes 24584 | tf_op jit(solution)/shard_map/ppermute | solution.py:22
  57.7 4.0 %collective-permute-start.19 = (f32[2,1024]{1,0:T(2,128)S(1)}, f32[2,1024]{1,0:T(2,128)S(1)}, u32[]{:S(2)}, u32[]{:S(2)}) collective-permute-start(f32[2,1024]{1,0:T(2,128)S(1)} %get-tuple-element.68.refs_0_), channel_id=1, source_target_pairs={{0,8},{1,9},{2,10},{3,11},{4,12},{5,13},{6,14},{7,15},{8,0},{9,1},... | collective-permute-start | bytes 24584 | tf_op jit(solution)/shard_map/ppermute | solution.py:22
  60.0 3.7 %collective-permute-start.18 = (f32[2,1024]{1,0:T(2,128)S(1)}, f32[2,1024]{1,0:T(2,128)S(1)}, u32[]{:S(2)}, u32[]{:S(2)}) collective-permute-start(f32[2,1024]{1,0:T(2,128)S(1)} %get-tuple-element.68.refs_0_), channel_id=1, source_target_pairs={{0,4},{1,5},{2,6},{3,7},{4,0},{5,1},{6,2},{7,3},{8,12},{9,13},{10,... | collective-permute-start | bytes 24584 | tf_op jit(solution)/shard_map/ppermute | solution.py:22
  64.9 5.8 %collective-permute-start.27 = (bf16[16,1152]{1,0:T(8,128)(2,1)S(1)}, bf16[16,1152]{1,0:T(8,128)(2,1)S(1)}, u32[]{:S(2)}, u32[]{:S(2)}) collective-permute-start(bf16[16,1152]{1,0:T(8,128)(2,1)S(1)} %get-tuple-element.71.refs_0_), channel_id=1, source_target_pairs={{0,24},{1,25},{2,26},{3,27},{4,28},{5,29},{6,30},{7,31},{8,16},{9,... | collective-permute-start | bytes 110600 | tf_op jit(solution)/shard_map/ppermute | solution.py:22
  66.8 4.9 %collective-permute-start.26 = (bf16[16,1152]{1,0:T(8,128)(2,1)S(1)}, bf16[16,1152]{1,0:T(8,128)(2,1)S(1)}, u32[]{:S(2)}, u32[]{:S(2)}) collective-permute-start(bf16[16,1152]{1,0:T(8,128)(2,1)S(1)} %get-tuple-element.71.refs_0_), channel_id=1, source_target_pairs={{0,16},{1,17},{2,18},{3,19},{4,20},{5,21},{6,22},{7,23},{8,24},{9,... | collective-permute-start | bytes 110600 | tf_op jit(solution)/shard_map/ppermute | solution.py:22
  66.8 4.9 %collective-permute-start.25 = (bf16[16,1152]{1,0:T(8,128)(2,1)S(1)}, bf16[16,1152]{1,0:T(8,128)(2,1)S(1)}, u32[]{:S(2)}, u32[]{:S(2)}) collective-permute-start(bf16[16,1152]{1,0:T(8,128)(2,1)S(1)} %get-tuple-element.71.refs_0_), channel_id=1, source_target_pairs={{0,8},{1,9},{2,10},{3,11},{4,12},{5,13},{6,14},{7,15},{8,0},{9,1},... | collective-permute-start | bytes 110600 | tf_op jit(solution)/shard_map/ppermute | solution.py:22
  71.6 5.2 %collective-permute-start.32 = (bf16[4,16,1152]{2,1,0:T(8,128)(2,1)S(1)}, bf16[4,16,1152]{2,1,0:T(8,128)(2,1)S(1)}, u32[]{:S(2)}, u32[]{:S(2)}) collective-permute-start(bf16[4,16,1152]{2,1,0:T(8,128)(2,1)S(1)} %stack.3.refs_0_), channel_id=1, source_target_pairs={{0,2},{1,3},{2,0},{3,1},{4,6},{5,7},{6,4},{7,5},{8,10},{9,11},{10,... | collective-permute-start | bytes 442376 | tf_op jit(solution)/shard_map/ppermute | solution.py:22
  73.3 6.0 %collective-permute-start.29 = (bf16[4,16,1152]{2,1,0:T(8,128)(2,1)S(1)}, bf16[4,16,1152]{2,1,0:T(8,128)(2,1)S(1)}, u32[]{:S(2)}, u32[]{:S(2)}) collective-permute-start(bf16[4,16,1152]{2,1,0:T(8,128)(2,1)S(1)} %stack.3.refs_0_), channel_id=1, source_target_pairs={{0,6},{1,7},{2,4},{3,5},{4,2},{5,3},{6,0},{7,1},{8,14},{9,15},{10,... | collective-permute-start | bytes 442376 | tf_op jit(solution)/shard_map/ppermute | solution.py:22
  73.7 6.2 %collective-permute-start.28 = (bf16[4,16,1152]{2,1,0:T(8,128)(2,1)S(1)}, bf16[4,16,1152]{2,1,0:T(8,128)(2,1)S(1)}, u32[]{:S(2)}, u32[]{:S(2)}) collective-permute-start(bf16[4,16,1152]{2,1,0:T(8,128)(2,1)S(1)} %stack.3.refs_0_), channel_id=1, source_target_pairs={{0,4},{1,5},{2,6},{3,7},{4,0},{5,1},{6,2},{7,3},{8,12},{9,13},{10,... | collective-permute-start | bytes 442376 | tf_op jit(solution)/shard_map/ppermute | solution.py:22
  75.2 4.7 %collective-permute-start.33 = (bf16[4,16,1152]{2,1,0:T(8,128)(2,1)S(1)}, bf16[4,16,1152]{2,1,0:T(8,128)(2,1)S(1)}, u32[]{:S(2)}, u32[]{:S(2)}) collective-permute-start(bf16[4,16,1152]{2,1,0:T(8,128)(2,1)S(1)} %stack.3.refs_0_), channel_id=1, source_target_pairs={{0,1},{1,0},{2,3},{3,2},{4,5},{5,4},{6,7},{7,6},{8,9},{9,8},{10,11... | collective-permute-start | bytes 442376 | tf_op jit(solution)/shard_map/ppermute | solution.py:22
  76.8 3.1 %collective-permute-start.34 = (bf16[4,16,1152]{2,1,0:T(8,128)(2,1)S(1)}, bf16[4,16,1152]{2,1,0:T(8,128)(2,1)S(1)}, u32[]{:S(2)}, u32[]{:S(2)}) collective-permute-start(bf16[4,16,1152]{2,1,0:T(8,128)(2,1)S(1)} %collective-permute-done.32.refs_1_), channel_id=1, source_target_pairs={{0,1},{1,0},{2,3},{3,2},{4,5},{5,4},{6,7},{7,6},{8,9},{9,8},{10,11... | collective-permute-start | bytes 442376 | tf_op jit(solution)/shard_map/ppermute | solution.py:22
  79.3 2.7 %collective-permute-start.31 = (bf16[4,16,1152]{2,1,0:T(8,128)(2,1)S(1)}, bf16[4,16,1152]{2,1,0:T(8,128)(2,1)S(1)}, u32[]{:S(2)}, u32[]{:S(2)}) collective-permute-start(bf16[4,16,1152]{2,1,0:T(8,128)(2,1)S(1)} %collective-permute-done.29.refs_1_), channel_id=1, source_target_pairs={{0,1},{1,0},{2,3},{3,2},{4,5},{5,4},{6,7},{7,6},{8,9},{9,8},{10,11... | collective-permute-start | bytes 442376 | tf_op jit(solution)/shard_map/ppermute | solution.py:22
  79.9 2.0 %collective-permute-start.30 = (bf16[4,16,1152]{2,1,0:T(8,128)(2,1)S(1)}, bf16[4,16,1152]{2,1,0:T(8,128)(2,1)S(1)}, u32[]{:S(2)}, u32[]{:S(2)}) collective-permute-start(bf16[4,16,1152]{2,1,0:T(8,128)(2,1)S(1)} %collective-permute-done.28.refs_0_), channel_id=1, source_target_pairs={{0,1},{1,0},{2,3},{3,2},{4,5},{5,4},{6,7},{7,6},{8,9},{9,8},{10,11... | collective-permute-start | bytes 442376 | tf_op jit(solution)/shard_map/ppermute | solution.py:22
  86.0 1.9 %collective-permute-start.36 = (bf16[4,32,1024]{2,1,0:T(8,128)(2,1)S(1)}, bf16[4,32,1024]{2,1,0:T(8,128)(2,1)S(1)}, u32[]{:S(2)}, u32[]{:S(2)}) collective-permute-start(bf16[4,32,1024]{2,1,0:T(8,128)(2,1)S(1)} %get-tuple-element.78), channel_id=1, source_target_pairs={{0,1},{1,0},{2,3},{3,2},{4,5},{5,4},{6,7},{7,6},{8,9},{9,8},{10,11... | collective-permute-start | bytes 786440 | tf_op jit(solution)/shard_map/ppermute | solution.py:22
  87.8 1.6 %collective-permute-start.35 = (bf16[4,32,1024]{2,1,0:T(8,128)(2,1)S(1)}, bf16[4,32,1024]{2,1,0:T(8,128)(2,1)S(1)}, u32[]{:S(2)}, u32[]{:S(2)}) collective-permute-start(bf16[4,32,1024]{2,1,0:T(8,128)(2,1)S(1)} %get-tuple-element.76), channel_id=1, source_target_pairs={{0,1},{1,0},{2,3},{3,2},{4,5},{5,4},{6,7},{7,6},{8,9},{9,8},{10,11... | collective-permute-start | bytes 786440 | tf_op jit(solution)/shard_map/ppermute | solution.py:22
  89.4 8.0 %collective-permute-start.38 = (bf16[4,16,1024]{2,1,0:T(8,128)(2,1)S(1)}, bf16[4,16,1024]{2,1,0:T(8,128)(2,1)S(1)}, u32[]{:S(2)}, u32[]{:S(2)}) collective-permute-start(bf16[4,16,1024]{2,1,0:T(8,128)(2,1)S(1)} %get-tuple-element.82), channel_id=1, source_target_pairs={{0,2},{1,3},{2,0},{3,1},{4,6},{5,7},{6,4},{7,5},{8,10},{9,11},{10,... | collective-permute-start | bytes 393224 | tf_op jit(solution)/shard_map/ppermute | solution.py:22
  91.0 7.3 %collective-permute-start.37 = (bf16[4,16,1024]{2,1,0:T(8,128)(2,1)S(1)}, bf16[4,16,1024]{2,1,0:T(8,128)(2,1)S(1)}, u32[]{:S(2)}, u32[]{:S(2)}) collective-permute-start(bf16[4,16,1024]{2,1,0:T(8,128)(2,1)S(1)} %get-tuple-element.81), channel_id=1, source_target_pairs={{0,6},{1,7},{2,4},{3,5},{4,2},{5,3},{6,0},{7,1},{8,14},{9,15},{10,... | collective-permute-start | bytes 393224 | tf_op jit(solution)/shard_map/ppermute | solution.py:22
  91.5 7.6 %collective-permute-start.39 = (bf16[4,16,1024]{2,1,0:T(8,128)(2,1)S(1)}, bf16[4,16,1024]{2,1,0:T(8,128)(2,1)S(1)}, u32[]{:S(2)}, u32[]{:S(2)}) collective-permute-start(bf16[4,16,1024]{2,1,0:T(8,128)(2,1)S(1)} %get-tuple-element.79.refs_2_), channel_id=1, source_target_pairs={{0,4},{1,5},{2,6},{3,7},{4,0},{5,1},{6,2},{7,3},{8,12},{9,13},{10,... | collective-permute-start | bytes 393224 | tf_op jit(solution)/shard_map/ppermute | solution.py:22
  99.1 6.1 %collective-permute-start.40 = (bf16[1,16,1024]{2,1,0:T(8,128)(2,1)S(1)}, bf16[1,16,1024]{2,1,0:T(8,128)(2,1)S(1)}, u32[]{:S(2)}, u32[]{:S(2)}) collective-permute-start(bf16[1,16,1024]{2,1,0:T(8,128)(2,1)S(1)} %get-tuple-element.87), channel_id=1, source_target_pairs={{0,24},{1,25},{2,26},{3,27},{4,28},{5,29},{6,30},{7,31},{8,16},{9,... | collective-permute-start | bytes 98312 | tf_op jit(solution)/shard_map/ppermute | solution.py:22
  101.2 5.2 %collective-permute-start.41 = (bf16[1,16,1024]{2,1,0:T(8,128)(2,1)S(1)}, bf16[1,16,1024]{2,1,0:T(8,128)(2,1)S(1)}, u32[]{:S(2)}, u32[]{:S(2)}) collective-permute-start(bf16[1,16,1024]{2,1,0:T(8,128)(2,1)S(1)} %get-tuple-element.88), channel_id=1, source_target_pairs={{0,16},{1,17},{2,18},{3,19},{4,20},{5,21},{6,22},{7,23},{8,24},{9,... | collective-permute-start | bytes 98312 | tf_op jit(solution)/shard_map/ppermute | solution.py:22
  102.3 4.1 %collective-permute-start.42 = (bf16[1,16,1024]{2,1,0:T(8,128)(2,1)S(1)}, bf16[1,16,1024]{2,1,0:T(8,128)(2,1)S(1)}, u32[]{:S(2)}, u32[]{:S(2)}) collective-permute-start(bf16[1,16,1024]{2,1,0:T(8,128)(2,1)S(1)} %get-tuple-element.89), channel_id=1, source_target_pairs={{0,8},{1,9},{2,10},{3,11},{4,12},{5,13},{6,14},{7,15},{8,0},{9,1},... | collective-permute-start | bytes 98312 | tf_op jit(solution)/shard_map/ppermute | solution.py:22

commit v7 on v6

--- a/solution.py
+++ b/solution.py
@@ -28,13 +28,11 @@
 
 def near_steps():
     steps = [(i, 2 * k) for i in range(2) for k in range(lax.axis_size("cls") // 2) if i or k]
-    return sorted(steps, key=lambda step: not (step[0] and step[1]))
-
-
-def call(kernel, outs, name, args, scratch=(), hbm_args=(), smem_args=(), limit=16, cost=None):
+    return sorted(steps, key=lambda step: (not (step[0] and step[1]), not step[0]))
+
+
+def call(kernel, outs, name, args, smem_args=(), aliases=None, limit=16, cost=None):
     def spec(i):
-        if i in hbm_args:
-            return pl.BlockSpec(memory_space=pltpu.HBM)
         if i in smem_args:
             return pl.BlockSpec(memory_space=pltpu.SMEM)
         return pl.BlockSpec(memory_space=pltpu.VMEM)
@@ -44,7 +42,7 @@
         out_shape=[jax.ShapeDtypeStruct(s, d) for s, d in outs],
         in_specs=[spec(i) for i in range(len(args))],
         out_specs=[pl.BlockSpec(memory_space=pltpu.VMEM)] * len(outs),
-        scratch_shapes=list(scratch),
+        input_output_aliases=aliases or {},
         compiler_params=pltpu.CompilerParams(vmem_limit_bytes=limit * MIB),
         cost_estimate=cost,
         name=name,
@@ -93,32 +91,32 @@
     return block[:, at : at + 1] + (block[:, at + 1 : at + 2] + block[:, at + 2 : at + 3])
 
 
-def load_kernel(half, tokens_ref, *refs):
-    count = (len(refs) - 2) // 2
-    others, held_ref, copies_of, sems = refs[:count], refs[count], refs[count + 1 : -1], refs[-1]
-    width = held_ref.shape[2]
+def load_kernel(tokens_ref, *refs):
+    count = (len(refs) - 3) // 2
+    others, halves, copies_of, sems = refs[:count], refs[count : count + 2], refs[count + 2 : -1], refs[-1]
+    blocks, _, width = halves[0].shape
     copies = [pltpu.make_async_copy(src, dst, sems.at[i]) for i, (src, dst) in enumerate(zip(others, copies_of))]
-    for j in range(held_ref.shape[0]):
-        start = pl.multiple_of((lax.axis_index("ctx") ^ half ^ (2 * j)) * width, LANES)
-        copies.append(
-            pltpu.make_async_copy(tokens_ref.at[:, pl.ds(start, width)], held_ref.at[j], sems.at[count + j])
-        )
+    for i in range(2):
+        for j in range(blocks):
+            start = pl.multiple_of((lax.axis_index("ctx") ^ i ^ (2 * j)) * width, LANES)
+            sem = sems.at[count + i * blocks + j]
+            copies.append(pltpu.make_async_copy(tokens_ref.at[:, pl.ds(start, width)], halves[i].at[j], sem))
     for copy in copies:
         copy.start()
     for copy in copies:
         copy.wait()
 
 
-def load(half, width, tokens, *others):
+def load(width, tokens, *others):
     rows, full_width = tokens.shape
     blocks = full_width // width // 2
-    outs = [pltpu.VMEM((blocks, rows, width), tokens.dtype)] + [pltpu.VMEM(x.shape, x.dtype) for x in others]
+    outs = [pltpu.VMEM((blocks, rows, width), tokens.dtype)] * 2 + [pltpu.VMEM(x.shape, x.dtype) for x in others]
     run = pl.pallas_call(
-        functools.partial(load_kernel, half),
+        load_kernel,
         out_shape=outs,
         in_specs=[pl.BlockSpec(memory_space=pltpu.HBM)] * (1 + len(others)),
         out_specs=[pl.BlockSpec(memory_space=pltpu.VMEM)] * len(outs),
-        scratch_shapes=[pltpu.SemaphoreType.DMA((blocks + len(others),))],
+        scratch_shapes=[pltpu.SemaphoreType.DMA((2 * blocks + len(others),))],
         compiler_params=pltpu.CompilerParams(vmem_limit_bytes=16 * MIB),
         name="load",
     )
@@ -195,64 +193,70 @@
     spread(left_ref[...], held_ref, keep_ref, send_ref, None)
 
 
-def total_of(keep, peak, received, width):
+def rescaling(peak, received, width):
     if peak is None:
-        for block in received:
-            keep = keep + block.astype(F32)
-        return keep, None
+        return None, None
     others = [from_lanes(block, width, 0) for block in received]
     top = peak
     for other in others:
         top = jnp.maximum(top, other)
-    keep = keep * jnp.exp(peak - top)
-    for block, other in zip(received, others):
-        keep = keep + block[:, :width].astype(F32) * jnp.exp(other - top)
-    return keep, top
-
-
-def put(ref, p, total, top, width):
-    ref[p, :, :width] = total.astype(BF16)
-    if top is not None:
-        ref[p, :, width:] = into_lanes([top], total.shape[0])
+    return top, [jnp.exp(p - top) for p in [peak, *others]]
+
+
+def total_of(keep, received, factors):
+    total = keep if factors is None else keep * factors[0]
+    for i, block in enumerate(received):
+        block = block[:, : keep.shape[1]].astype(F32)
+        total = total + (block if factors is None else block * factors[i + 1])
+    return total
+
+
+def put(ref, j, total, lanes):
+    width = total.shape[1]
+    ref[j, :, :width] = total.astype(BF16)
+    if lanes is not None:
+        ref[j, :, width:] = lanes
 
 
 def core_kernel(peaks, first, *refs):
     keep_ref, recv_ref, *refs = refs
     peak = refs.pop(0)[: keep_ref.shape[1], :1] if peaks else None
-    refs = refs[1:] if first else refs
+    refs = refs if first else refs[1:-1]
     top_ref = refs.pop() if peaks and first else None
     width = keep_ref.shape[2]
     rows = refs[0].shape[1]
+    top, factors = rescaling(peak, [recv_ref[0]], width)
+    lanes = into_lanes([top], top.shape[0]) if peaks else None
     for j in range(keep_ref.shape[0]):
-        total, top = total_of(keep_ref[j], peak, [recv_ref[j]], width)
+        total = total_of(keep_ref[j], [recv_ref[j]], factors)
         for k, ref in enumerate(refs):
             at = slice(k * rows, (k + 1) * rows)
             if first and k == 0:
                 ref[j] = total[at]
             else:
-                put(ref, j, total[at], top[at] if peaks else None, width)
+                put(ref, j, total[at], lanes[at] if peaks else None)
     if peaks and first:
         top_ref[...] = jnp.broadcast_to(top[:rows], top_ref.shape)
 
 
-def near_sum_kernel(peaks, count, steps, after, *refs):
+def near_sum_kernel(peaks, count, steps, *refs):
     keep_ref, *refs = refs
     received, refs = refs[:count], refs[count:]
     peak = refs.pop(0)[:, :1] if peaks else None
-    refs = refs[after:]
     top_ref = refs.pop() if peaks else None
-    width = keep_ref.shape[2]
+    top, factors = rescaling(peak, [ref[0] for ref in received], keep_ref.shape[2])
+    lanes = into_lanes([top], top.shape[0]) if peaks else None
     for p in range(keep_ref.shape[0]):
-        total, top = total_of(keep_ref[p], peak, [ref[p] for ref in received], width)
+        total = total_of(keep_ref[p], [ref[p] for ref in received], factors)
         if p == 0:
             refs[0][0] = total
         else:
-            put(refs[steps.index((2 * p, 0)) + 1], 0, total, top, width)
+            put(refs[steps.index((2 * p, 0)) + 1], 0, total, lanes)
     if peaks:
         top_ref[...] = jnp.broadcast_to(top, top_ref.shape)
 
 
-def scatter_sum(halves, peak, after=()):
+def scatter_sum(halves, peak):
     peaks = peak is not None
     near, far = near_steps(), far_steps()
     across = (len(near) + 1) // 2
@@ -260,28 +264,28 @@
     lanes = halves[0][1].shape[2]
     rows = half // across
     top_out = [((rows, LANES), F32)] if peaks else []
-    parts = {}
-    for i in reversed(range(2)):
-        keep, send = halves[i]
-        outs = [((blocks, rows, lanes), BF16)] * across
-        if i == 0:
-            outs = [((blocks, rows, width), F32)] + outs[1:] + top_out
-        args = [keep, swap(send, 0, 1)] + ([peak] if peaks else [])
-        if i == 0:
-            args.append(parts[1, 0])
-        out = call(functools.partial(core_kernel, peaks, i == 0), outs, "core_sum", args)
-        parts.update({(i, 2 * k): out[k] for k in range(across)})
+    part = ((blocks, rows, lanes), BF16)
+    (keep_a, send_a), (keep_b, send_b) = halves
+    args = [keep_b, swap(send_b, 0, 1)] + ([peak] if peaks else []) + [send_a]
+    outs = [part] * across + [((blocks, half, lanes), BF16)]
+    *parts_b, send_a = call(
+        functools.partial(core_kernel, peaks, False), outs, "core_sum", args, aliases={len(args) - 1: across}
+    )
+    args = [keep_a, swap(send_a, 0, 1)] + ([peak] if peaks else [])
+    outs = [((blocks, rows, width), F32)] + [part] * (across - 1) + top_out
+    out = call(functools.partial(core_kernel, peaks, True), outs, "core_sum", args)
+    parts = {(i, 2 * k): x for i, group in enumerate((out, parts_b)) for k, x in enumerate(group[:across])}
     received = [swap(parts[step], *step) for step in near]
     outs = [((1, rows, width), F32)] + [((1, rows, lanes), BF16)] * len(far) + top_out
-    args = [parts[0, 0], *received] + (out[-1:] if peaks else []) + list(after)
-    out = call(functools.partial(near_sum_kernel, peaks, len(received), far, len(after)), outs, "near_sum", args)
+    args = [parts[0, 0], *received] + (out[-1:] if peaks else [])
+    out = call(functools.partial(near_sum_kernel, peaks, len(received), far), outs, "near_sum", args)
     received = [swap(x, *step) for x, step in zip(out[1:], far)]
     return [out[0], *received] + (out[-1:] if peaks else [])
 
 
 def far_sum_kernel(*refs):
     keep_ref, *received, out_ref = refs
-    out_ref[...] = total_of(keep_ref[0], None, [ref[0] for ref in received], keep_ref.shape[2])[0]
+    out_ref[...] = total_of(keep_ref[0], [ref[0] for ref in received], None)
 
 
 def head_mask(shape, attributes):
@@ -292,7 +296,9 @@
 
 def head_sums_kernel(*refs):
     keep_ref, *received, peak_ref, gain_ref, weight_ref, sums_ref, pooled_ref, top_ref = refs
-    pooled, top = total_of(keep_ref[0], peak_ref[:, :1], [ref[0] for ref in received], keep_ref.shape[2])
+    received = [ref[0] for ref in received]
+    top, factors = rescaling(peak_ref[:, :1], received, keep_ref.shape[2])
+    pooled = total_of(keep_ref[0], received, factors)
     pooled_ref[...] = pooled
     top_ref[...] = jnp.broadcast_to(top, top_ref.shape)
     scaled_b = (pooled * gain_ref[...]).astype(BF16)
@@ -311,13 +317,17 @@
     return level[0]
 
 
-def head_grads_kernel(full_width, count, *refs):
-    pooled_ref, top_ref, gain_ref, weight_ref, bias_ref, label_ref = refs[count : count + 6]
-    bias_grad_ref, copy_ref, grad_ref, normed_ref = refs[count + 6 :]
+def tree_sum_kernel(*refs):
+    refs[-1][...] = tree_sum([ref[...] for ref in refs[:-1]])
+
+
+def head_grads_kernel(full_width, sums_ref, other_sums_ref, *refs):
+    pooled_ref, top_ref, gain_ref, weight_ref, bias_ref, label_ref, *refs = refs
+    bias_grad_ref, copy_ref, grad_ref, normed_ref = refs
     pooled, gain = pooled_ref[...], gain_ref[...]
     heads, width = pooled.shape
     columns = bias_ref.shape[1]
-    sums = tree_sum([ref[...] for ref in refs[:count]])
+    sums = sums_ref[...] + other_sums_ref[...]
     mask = head_mask((heads, columns), columns // heads)
     inverse_flat = lax.rsqrt(sums[1:2] / full_width + 1e-05)
     inverse_rms = jnp.max(jnp.where(mask, inverse_flat, 0.0), axis=1, keepdims=True)
@@ -342,7 +352,7 @@
     normed_ref[...] = unit * gain
 
 
-def head_weight_grad_kernel(attributes, normed_ref, bias_grad_ref, out_ref, done_ref):
+def head_weight_grad_kernel(attributes, normed_ref, bias_grad_ref, out_ref):
     heads = normed_ref.shape[0]
     columns = out_ref.shape[1]
     parts = jnp.concatenate(pieces(normed_ref[...]), axis=0)
@@ -351,7 +361,6 @@
     ones = jnp.where(column // attributes == row, 1.0, 0.0).astype(BF16)
     normed = lax.dot_general(parts, ones, (((0,), (0,)), ((), ())), preferred_element_type=F32)
     out_ref[...] = normed * bias_grad_ref[...]
-    done_ref[...] = jnp.zeros_like(done_ref)
 
 
 def head_weight_grad(normed, bias_grad):
@@ -360,15 +369,14 @@
     block = columns // 4
     return pl.pallas_call(
         functools.partial(head_weight_grad_kernel, columns // rows),
-        out_shape=[jax.ShapeDtypeStruct((width, columns), F32), jax.ShapeDtypeStruct((8, LANES), F32)],
+        out_shape=jax.ShapeDtypeStruct((width, columns), F32),
         grid=(columns // block,),
         in_specs=[
             pl.BlockSpec((rows, width), lambda i: (0, 0)),
             pl.BlockSpec((1, block), lambda i: (0, i)),
         ],
-        out_specs=[pl.BlockSpec((width, block), lambda i: (0, i)), pl.BlockSpec((8, LANES), lambda i: (0, 0))],
+        out_specs=pl.BlockSpec((width, block), lambda i: (0, i)),
         compiler_params=pltpu.CompilerParams(vmem_limit_bytes=16 * MIB),
-        cost_estimate=pl.CostEstimate(flops=6 * rows * width * columns, bytes_accessed=4 * width * columns, transcendentals=0),
         name="head_weight_grad",
     )(normed, bias_grad)
 
@@ -386,14 +394,12 @@
     product = ((heads, token_count), F32)
     cost = pl.CostEstimate(flops=256 * token_count * full_width, bytes_accessed=0, transcendentals=0)
 
-    def project_half(parts, after=()):
-        kernel = functools.partial(project_kernel, len(parts))
-        return call(kernel, [product], "project", [*parts, held_a, *after], cost=cost)[0]
-
-    held_a, queries_here = load(0, width, tokens, queries)
-    held_b, gain = load(1, width, tokens, norm_gain[None, :])
+    def project_half(parts):
+        return call(functools.partial(project_kernel, len(parts)), [product], "project", [*parts, held_a], cost=cost)[0]
+
+    held_a, held_b, queries_here, gain = load(width, tokens, queries, norm_gain[None, :])
     first, second = gather(queries, queries_here)
-    part = project_half(first, [gain])
+    part = project_half(first)
     keep_b, send_b, own_peak, weights, left = call(
         functools.partial(pool_kernel, classes),
         [*pair, ((heads, LANES), F32), product, ((heads, token_count), BF16)],
@@ -410,14 +416,15 @@
         "head_sums",
         [*parts, gain, head_weight],
     )
-    all_sums = [sums] + [swap(sums, bits, 0) for bits in range(1, contexts)]
+    far_sums = [swap(sums, *step) for step in far_steps()[::-1]]
+    (sums,) = call(tree_sum_kernel, [((2, columns), F32)], "tree_sum", [sums, *far_sums])
     bias_grad, bias_grad_here, pooled_grad, normed = call(
-        functools.partial(head_grads_kernel, full_width, contexts),
+        functools.partial(head_grads_kernel, full_width),
         [((1, columns), F32), ((1, columns), F32), ((rows, width + LANES), BF16), ((rows, width), F32)],
         "head_grads",
-        [*all_sums, pooled, top, gain, head_weight, head_bias[None, :], labels[None, :]],
-    )
-    head_grad, done = head_weight_grad(normed, bias_grad_here)
+        [sums, swap(sums, 1, 0), pooled, top, gain, head_weight, head_bias[None, :], labels[None, :]],
+    )
+    head_grad = head_weight_grad(normed, bias_grad_here)
     first, second = gather(pooled_grad)
     part = project_half(first)
     pair = [((blocks, half, width), F32), ((blocks, half, width), BF16)]
@@ -429,7 +436,7 @@
         cost=cost,
     )
     half_a = call(grad_rest_kernel, pair, "grad_rest", [left, held_a], cost=cost)
-    parts = scatter_sum([half_a, (keep_b, send_b)], None, after=(done,))
+    parts = scatter_sum([half_a, (keep_b, send_b)], None)
     (query_grad,) = call(far_sum_kernel, [((rows, width), F32)], "far_sum", parts)
     return (loss.reshape(()), query_grad, head_grad, bias_grad.reshape(-1))
 

time: 107 us -> 101 us (0.944)
  starting transfers between devices: 46.7 us -> 41.2 us
    ppermute x43 -> x40, starting transfers between devices: 46.7 us -> 41.2 us  [swap(): return lax.ppermute(x, ('ctx', 'cls'), pairs)]
    pallas_call x2 -> x1, Pallas kernels: 5.82 us -> 4.79 us  [load(): run(*[pltpu.with_memory_space_constraint(x, pltpu.HBM) for x in (tokens,...]
    ppermute x43 -> x40, waiting for transfers between devices: 31.8 us -> 31.7 us  [swap(): return lax.ppermute(x, ('ctx', 'cls'), pairs)]
    pallas_call x17 -> x18, Pallas kernels: 18.2 us -> 18.3 us  [call(): return list(run(*args))]
  transfers between devices with their start and end apart: 43 -> 40, of which waited for: 21 -> 20; matrix products, arithmetic and copies ran while one was open for 0% -> 0% of each run, Pallas kernels for 15% -> 14%
where the time goes in v7:
time: 101 us; the launch traced here: 100 us
  starting transfers between devices  41.2 us (41%)
  waiting for transfers between devices  31.7 us (31%)
  Pallas kernels  26 us (26%)
  between operations  1.5 us (1%)
    ppermute x40, starting transfers between devices, swap(): return lax.ppermute(x, ('ctx', 'cls'), pairs)  41.2 us
    ppermute x40, waiting for transfers between devices, swap(): return lax.ppermute(x, ('ctx', 'cls'), pairs)  31.7 us
    pallas_call x18, Pallas kernels, call(): return list(run(*args))  18.3 us
    pallas_call x1, Pallas kernels, load(): run(*[pltpu.with_memory_space_constraint(x, pltpu.HBM) for x in (tokens,...  4.79 us
    pallas_call x1, Pallas kernels, head_weight_grad(): pl.pallas_call(functools.partial(head_weight_grad_kernel, columns // rows...  2.94 us
  transfers between devices with their start and end apart: 40, of which 20 were waited for; matrix products, arithmetic and copies ran while one was open for 0% of the time, Pallas kernels for 14%

profile of v7, /device:TPU:0, one launch (start us, length us, event | category | flops | bytes accessed | tf_op | source)
XLA Modules:
  0.0 100.4 jit_solution(16797787000623635756)
XLA Ops:
  0.6 3.1 %collective-permute-start = (bf16[16,1024]{1,0:T(8,128)(2,1)}, bf16[16,1024]{1,0:T(8,128)(2,1)S(1)}, u32[]{:S(2)}, u32[]{:S(2)}) collective-permute-start(bf16[16,1024]{1,0:T(8,128)(2,1)} %refs_0_.1), channel_id=1, source_target_pairs={{0,8},{1,9},{2,10},{3,11},{4,12},{5,13},{6,14},{7,15},{8,0},{9,1},... | collective-permute-start | bytes 98312 | tf_op jit(solution)/shard_map/ppermute | solution.py:22
  3.7 2.5 %collective-permute-start.2 = (bf16[16,1024]{1,0:T(8,128)(2,1)}, bf16[16,1024]{1,0:T(8,128)(2,1)S(1)}, u32[]{:S(2)}, u32[]{:S(2)}) collective-permute-start(bf16[16,1024]{1,0:T(8,128)(2,1)} %refs_0_.1), channel_id=1, source_target_pairs={{0,24},{1,25},{2,26},{3,27},{4,28},{5,29},{6,30},{7,31},{8,16},{9,... | collective-permute-start | bytes 98312 | tf_op jit(solution)/shard_map/ppermute | solution.py:22
  6.3 4.8 %load.1 = (bf16[4,768,1024]{2,1,0:T(8,128)(2,1)S(1)}, bf16[4,768,1024]{2,1,0:T(8,128)(2,1)S(1)}, bf16[16,1024]{1,0:T(8,128)(2,1)S(1)}, f32[1,1024]{1,0:T(1,128)S(1)}) custom-call(bf16[768,8192]{1,0:T(8,128)(2,1)} %tokens_ref.1, bf16[16,1024]{1,0:T(8,128)(2,1)} %refs_0_.1, f32[1,1024]{1,0:T(1,128)} %bitcast.7), custom_call_target="tpu_custom_call" | custom-call | tf_op jit(solution)/shard_map/load/pallas_call | solution.py:123
  11.6 1.6 %collective-permute-start.7 = (bf16[4,16,1024]{2,1,0:T(8,128)(2,1)S(1)}, bf16[4,16,1024]{2,1,0:T(8,128)(2,1)S(1)}, u32[]{:S(2)}, u32[]{:S(2)}) collective-permute-start(bf16[4,16,1024]{2,1,0:T(8,128)(2,1)S(1)} %stack.2.refs_0_), channel_id=1, source_target_pairs={{0,2},{1,3},{2,0},{3,1},{4,6},{5,7},{6,4},{7,5},{8,10},{9,11},{10,... | collective-permute-start | bytes 393224 | tf_op jit(solution)/shard_map/ppermute | solution.py:22
  13.2 1.4 %collective-permute-start.4 = (bf16[4,16,1024]{2,1,0:T(8,128)(2,1)S(1)}, bf16[4,16,1024]{2,1,0:T(8,128)(2,1)S(1)}, u32[]{:S(2)}, u32[]{:S(2)}) collective-permute-start(bf16[4,16,1024]{2,1,0:T(8,128)(2,1)S(1)} %stack.2.refs_0_), channel_id=1, source_target_pairs={{0,6},{1,7},{2,4},{3,5},{4,2},{5,3},{6,0},{7,1},{8,14},{9,15},{10,... | collective-permute-start | bytes 393224 | tf_op jit(solution)/shard_map/ppermute | solution.py:22
  15.1 3.2 %collective-permute-done.7.refs_1_ = bf16[4,16,1024]{2,1,0:T(8,128)(2,1)S(1)} collective-permute-done((bf16[4,16,1024]{2,1,0:T(8,128)(2,1)S(1)}, bf16[4,16,1024]{2,1,0:T(8,128)(2,1)S(1)}, u32[]{:S(2)}, u32[]{:S(2)}) %collective-permute-start.7) | collective-permute-done | bytes 131104 | tf_op jit(solution)/shard_map/ppermute | solution.py:22
  20.0 2.0 %project.2.refs_4_ = f32[64,768]{1,0:T(8,128)S(1)} custom-call(bf16[4,16,1024]{2,1,0:T(8,128)(2,1)S(1)} %stack.2.refs_0_, bf16[4,16,1024]{2,1,0:T(8,128)(2,1)S(1)} %collective-permute-done.7.refs_1_, bf16[4,16,1024]{2,1,0:T(8,128)(2,1)S(1)} %collective-permute-done.8.refs_2_, bf16[4,16,1024]{2,1,0:T(8,128)(2,1)S(1)} %collective-permute-done.9.refs_3_, ...), custom_call_target="tpu_custom_call" | custom-call | flops 1610612736 | tf_op jit(solution)/shard_map/project/pallas_call | solution.py:50
  22.1 4.2 %pool.1 = (f32[4,32,1024]{2,1,0:T(8,128)S(1)}, bf16[4,32,1152]{2,1,0:T(8,128)(2,1)S(1)}, f32[64,128]{1,0:T(8,128)S(1)}, f32[64,768]{1,0:T(8,128)S(1)}, bf16[64,768]{1,0:T(8,128)(2,1)S(1)}) custom-call(s32[1]{0:T(128)S(6)} %copy.15.length_ref, bf16[4,16,1024]{2,1,0:T(8,128)(2,1)S(1)} %collective-permute-done.3.refs_0_, ...), custom_call_target="tpu_custom_call" | custom-call | flops 1610612736 | tf_op jit(solution)/shard_map/pool/pallas_call | solution.py:50
  26.8 1.2 %pool_rest.1 = (f32[4,32,1024]{2,1,0:T(8,128)S(1)}, bf16[4,32,1152]{2,1,0:T(8,128)(2,1)S(1)}) custom-call(bf16[64,768]{1,0:T(8,128)(2,1)S(1)} %get-tuple-element.51.left_ref, f32[64,128]{1,0:T(8,128)S(1)} %get-tuple-element.52.peak_ref.refs_2_.refs_7_, bf16[4,768,1024]{2,1,0:T(8,128)(2,1)S(1)} %get-tuple-element.49.refs_4_.held_ref), custom_call_target="tpu_custom_call" | custom-call | flops 1610612736 | tf_op jit(solution)/shard_map/pool_rest/pallas_call | solution.py:50
  28.8 2.4 %collective-permute-start.12 = (bf16[4,16,1152]{2,1,0:T(8,128)(2,1)S(1)}, bf16[4,16,1152]{2,1,0:T(8,128)(2,1)S(1)}, u32[]{:S(2)}, u32[]{:S(2)}) collective-permute-start(bf16[4,16,1152]{2,1,0:T(8,128)(2,1)S(1)} %get-tuple-element.59), channel_id=1, source_target_pairs={{0,6},{1,7},{2,4},{3,5},{4,2},{5,3},{6,0},{7,1},{8,14},{9,15},{10,... | collective-permute-start | bytes 442376 | tf_op jit(solution)/shard_map/ppermute | solution.py:22
  32.0 0.6 collective-permute-start.14
  32.7 3.7 %collective-permute-done.12.refs_1_ = bf16[4,16,1152]{2,1,0:T(8,128)(2,1)S(1)} collective-permute-done((bf16[4,16,1152]{2,1,0:T(8,128)(2,1)S(1)}, bf16[4,16,1152]{2,1,0:T(8,128)(2,1)S(1)}, u32[]{:S(2)}, u32[]{:S(2)}) %collective-permute-start.12) | collective-permute-done | bytes 147488 | tf_op jit(solution)/shard_map/ppermute | solution.py:22
  36.4 2.4 %collective-permute-done.13.refs_2_ = bf16[4,16,1152]{2,1,0:T(8,128)(2,1)S(1)} collective-permute-done((bf16[4,16,1152]{2,1,0:T(8,128)(2,1)S(1)}, bf16[4,16,1152]{2,1,0:T(8,128)(2,1)S(1)}, u32[]{:S(2)}, u32[]{:S(2)}) %collective-permute-start.13) | collective-permute-done | bytes 147488 | tf_op jit(solution)/shard_map/ppermute | solution.py:22
  39.1 2.7 %collective-permute-start.15 = (bf16[1,16,1152]{2,1,0:T(8,128)(2,1)S(1)}, bf16[1,16,1152]{2,1,0:T(8,128)(2,1)S(1)}, u32[]{:S(2)}, u32[]{:S(2)}) collective-permute-start(bf16[1,16,1152]{2,1,0:T(8,128)(2,1)S(1)} %get-tuple-element.64), channel_id=1, source_target_pairs={{0,24},{1,25},{2,26},{3,27},{4,28},{5,29},{6,30},{7,31},{8,16},{9,... | collective-permute-start | bytes 110600 | tf_op jit(solution)/shard_map/ppermute | solution.py:22
  42.2 1.4 %collective-permute-start.17 = (bf16[1,16,1152]{2,1,0:T(8,128)(2,1)S(1)}, bf16[1,16,1152]{2,1,0:T(8,128)(2,1)S(1)}, u32[]{:S(2)}, u32[]{:S(2)}) collective-permute-start(bf16[1,16,1152]{2,1,0:T(8,128)(2,1)S(1)} %get-tuple-element.66), channel_id=1, source_target_pairs={{0,8},{1,9},{2,10},{3,11},{4,12},{5,13},{6,14},{7,15},{8,0},{9,1},... | collective-permute-start | bytes 110600 | tf_op jit(solution)/shard_map/ppermute | solution.py:22
  43.6 1.8 %collective-permute-done.15.refs_1_ = bf16[1,16,1152]{2,1,0:T(8,128)(2,1)S(1)} collective-permute-done((bf16[1,16,1152]{2,1,0:T(8,128)(2,1)S(1)}, bf16[1,16,1152]{2,1,0:T(8,128)(2,1)S(1)}, u32[]{:S(2)}, u32[]{:S(2)}) %collective-permute-start.15) | collective-permute-done | bytes 36896 | tf_op jit(solution)/shard_map/ppermute | solution.py:22
  45.3 1.6 %collective-permute-done.16.refs_2_ = bf16[1,16,1152]{2,1,0:T(8,128)(2,1)S(1)} collective-permute-done((bf16[1,16,1152]{2,1,0:T(8,128)(2,1)S(1)}, bf16[1,16,1152]{2,1,0:T(8,128)(2,1)S(1)}, u32[]{:S(2)}, u32[]{:S(2)}) %collective-permute-start.16) | collective-permute-done | bytes 36896 | tf_op jit(solution)/shard_map/ppermute | solution.py:22
  47.0 0.6 head_sums.1
  47.6 1.9 %collective-permute-start.20 = (f32[2,1024]{1,0:T(2,128)S(1)}, f32[2,1024]{1,0:T(2,128)S(1)}, u32[]{:S(2)}, u32[]{:S(2)}) collective-permute-start(f32[2,1024]{1,0:T(2,128)S(1)} %get-tuple-element.69.refs_0_), channel_id=1, source_target_pairs={{0,24},{1,25},{2,26},{3,27},{4,28},{5,29},{6,30},{7,31},{8,16},{9,... | collective-permute-start | bytes 24584 | tf_op jit(solution)/shard_map/ppermute | solution.py:22
  49.7 2.4 %collective-permute-start.18 = (f32[2,1024]{1,0:T(2,128)S(1)}, f32[2,1024]{1,0:T(2,128)S(1)}, u32[]{:S(2)}, u32[]{:S(2)}) collective-permute-start(f32[2,1024]{1,0:T(2,128)S(1)} %get-tuple-element.69.refs_0_), channel_id=1, source_target_pairs={{0,8},{1,9},{2,10},{3,11},{4,12},{5,13},{6,14},{7,15},{8,0},{9,1},... | collective-permute-start | bytes 24584 | tf_op jit(solution)/shard_map/ppermute | solution.py:22
  52.1 1.1 %collective-permute-done.20.refs_3_ = f32[2,1024]{1,0:T(2,128)S(1)} collective-permute-done((f32[2,1024]{1,0:T(2,128)S(1)}, f32[2,1024]{1,0:T(2,128)S(1)}, u32[]{:S(2)}, u32[]{:S(2)}) %collective-permute-start.20) | collective-permute-done | bytes 8224 | tf_op jit(solution)/shard_map/ppermute | solution.py:22
  53.1 0.9 collective-permute-done.19.refs_2_
  54.1 1.6 %collective-permute-start.21 = (f32[2,1024]{1,0:T(2,128)S(1)}, f32[2,1024]{1,0:T(2,128)S(1)}, u32[]{:S(2)}, u32[]{:S(2)}) collective-permute-start(f32[2,1024]{1,0:T(2,128)S(1)} %tree_sum.1.sums_ref), channel_id=1, source_target_pairs={{0,4},{1,5},{2,6},{3,7},{4,0},{5,1},{6,2},{7,3},{8,12},{9,13},{10,... | collective-permute-start | bytes 24584 | tf_op jit(solution)/shard_map/ppermute | solution.py:22
  55.6 2.2 %collective-permute-done.21.other_sums_ref = f32[2,1024]{1,0:T(2,128)S(1)} collective-permute-done((f32[2,1024]{1,0:T(2,128)S(1)}, f32[2,1024]{1,0:T(2,128)S(1)}, u32[]{:S(2)}, u32[]{:S(2)}) %collective-permute-start.21) | collective-permute-done | bytes 8224 | tf_op jit(solution)/shard_map/ppermute | solution.py:22
  57.8 1.2 %head_grads.1 = (f32[1,1024]{1,0:T(1,128)}, f32[1,1024]{1,0:T(1,128)S(1)}, bf16[16,1152]{1,0:T(8,128)(2,1)S(1)}, f32[16,1024]{1,0:T(8,128)S(1)}) custom-call(f32[2,1024]{1,0:T(2,128)S(1)} %tree_sum.1.sums_ref, f32[2,1024]{1,0:T(2,128)S(1)} %collective-permute-done.21.other_sums_ref, f32[16,1024]{1,0:T(8,128)S(1)} %get-tuple-element.70.refs_0_, ...), custom_call_target="tpu_custom_call" | custom-call | tf_op jit(solution)/shard_map/head_grads/pallas_call | solution.py:50
  59.0 2.0 %collective-permute-start.24 = (bf16[16,1152]{1,0:T(8,128)(2,1)S(1)}, bf16[16,1152]{1,0:T(8,128)(2,1)S(1)}, u32[]{:S(2)}, u32[]{:S(2)}) collective-permute-start(bf16[16,1152]{1,0:T(8,128)(2,1)S(1)} %get-tuple-element.72.refs_0_), channel_id=1, source_target_pairs={{0,24},{1,25},{2,26},{3,27},{4,28},{5,29},{6,30},{7,31},{8,16},{9,... | collective-permute-start | bytes 110600 | tf_op jit(solution)/shard_map/ppermute | solution.py:22
  61.0 1.0 %collective-permute-start.23 = (bf16[16,1152]{1,0:T(8,128)(2,1)S(1)}, bf16[16,1152]{1,0:T(8,128)(2,1)S(1)}, u32[]{:S(2)}, u32[]{:S(2)}) collective-permute-start(bf16[16,1152]{1,0:T(8,128)(2,1)S(1)} %get-tuple-element.72.refs_0_), channel_id=1, source_target_pairs={{0,16},{1,17},{2,18},{3,19},{4,20},{5,21},{6,22},{7,23},{8,24},{9,... | collective-permute-start | bytes 110600 | tf_op jit(solution)/shard_map/ppermute | solution.py:22
  62.0 1.4 %collective-permute-start.22 = (bf16[16,1152]{1,0:T(8,128)(2,1)S(1)}, bf16[16,1152]{1,0:T(8,128)(2,1)S(1)}, u32[]{:S(2)}, u32[]{:S(2)}) collective-permute-start(bf16[16,1152]{1,0:T(8,128)(2,1)S(1)} %get-tuple-element.72.refs_0_), channel_id=1, source_target_pairs={{0,8},{1,9},{2,10},{3,11},{4,12},{5,13},{6,14},{7,15},{8,0},{9,1},... | collective-permute-start | bytes 110600 | tf_op jit(solution)/shard_map/ppermute | solution.py:22
  63.4 1.4 %collective-permute-done.24.refs_3_ = bf16[16,1152]{1,0:T(8,128)(2,1)S(1)} collective-permute-done((bf16[16,1152]{1,0:T(8,128)(2,1)S(1)}, bf16[16,1152]{1,0:T(8,128)(2,1)S(1)}, u32[]{:S(2)}, u32[]{:S(2)}) %collective-permute-start.24) | collective-permute-done | bytes 36896 | tf_op jit(solution)/shard_map/ppermute | solution.py:22
  64.8 1.6 %collective-permute-done.23.refs_2_ = bf16[16,1152]{1,0:T(8,128)(2,1)S(1)} collective-permute-done((bf16[16,1152]{1,0:T(8,128)(2,1)S(1)}, bf16[16,1152]{1,0:T(8,128)(2,1)S(1)}, u32[]{:S(2)}, u32[]{:S(2)}) %collective-permute-start.23) | collective-permute-done | bytes 36896 | tf_op jit(solution)/shard_map/ppermute | solution.py:22
  66.4 1.4 %collective-permute-start.29 = (bf16[4,16,1152]{2,1,0:T(8,128)(2,1)S(1)}, bf16[4,16,1152]{2,1,0:T(8,128)(2,1)S(1)}, u32[]{:S(2)}, u32[]{:S(2)}) collective-permute-start(bf16[4,16,1152]{2,1,0:T(8,128)(2,1)S(1)} %stack.3.refs_0_), channel_id=1, source_target_pairs={{0,2},{1,3},{2,0},{3,1},{4,6},{5,7},{6,4},{7,5},{8,10},{9,11},{10,... | collective-permute-start | bytes 442376 | tf_op jit(solution)/shard_map/ppermute | solution.py:22
  67.8 1.6 %collective-permute-start.26 = (bf16[4,16,1152]{2,1,0:T(8,128)(2,1)S(1)}, bf16[4,16,1152]{2,1,0:T(8,128)(2,1)S(1)}, u32[]{:S(2)}, u32[]{:S(2)}) collective-permute-start(bf16[4,16,1152]{2,1,0:T(8,128)(2,1)S(1)} %stack.3.refs_0_), channel_id=1, source_target_pairs={{0,6},{1,7},{2,4},{3,5},{4,2},{5,3},{6,0},{7,1},{8,14},{9,15},{10,... | collective-permute-start | bytes 442376 | tf_op jit(solution)/shard_map/ppermute | solution.py:22
  70.0 1.6 %collective-permute-done.29.refs_1_ = bf16[4,16,1152]{2,1,0:T(8,128)(2,1)S(1)} collective-permute-done((bf16[4,16,1152]{2,1,0:T(8,128)(2,1)S(1)}, bf16[4,16,1152]{2,1,0:T(8,128)(2,1)S(1)}, u32[]{:S(2)}, u32[]{:S(2)}) %collective-permute-start.29) | collective-permute-done | bytes 147488 | tf_op jit(solution)/shard_map/ppermute | solution.py:22
  71.6 2.2 %collective-permute-done.26.refs_1_ = bf16[4,16,1152]{2,1,0:T(8,128)(2,1)S(1)} collective-permute-done((bf16[4,16,1152]{2,1,0:T(8,128)(2,1)S(1)}, bf16[4,16,1152]{2,1,0:T(8,128)(2,1)S(1)}, u32[]{:S(2)}, u32[]{:S(2)}) %collective-permute-start.26) | collective-permute-done | bytes 147488 | tf_op jit(solution)/shard_map/ppermute | solution.py:22
  73.9 0.8 collective-permute-done.25.refs_0_
  74.7 2.0 %project.3.refs_4_ = f32[64,768]{1,0:T(8,128)S(1)} custom-call(bf16[4,16,1152]{2,1,0:T(8,128)(2,1)S(1)} %stack.3.refs_0_, bf16[4,16,1152]{2,1,0:T(8,128)(2,1)S(1)} %collective-permute-done.29.refs_1_, bf16[4,16,1152]{2,1,0:T(8,128)(2,1)S(1)} %collective-permute-done.30.refs_2_, bf16[4,16,1152]{2,1,0:T(8,128)(2,1)S(1)} %collective-permute-done.31.refs_3_, ...), custom_call_target="tpu_custom_call" | custom-call | flops 1610612736 | tf_op jit(solution)/shard_map/project/pallas_call | solution.py:50
  76.7 4.0 %grad.1 = (f32[4,32,1024]{2,1,0:T(8,128)S(1)}, bf16[4,32,1024]{2,1,0:T(8,128)(2,1)S(1)}, bf16[64,768]{1,0:T(8,128)(2,1)S(1)}, f32[1,1]{1,0:T(1,128)}) custom-call(bf16[4,16,1152]{2,1,0:T(8,128)(2,1)S(1)} %collective-permute-done.25.refs_0_, bf16[4,16,1152]{2,1,0:T(8,128)(2,1)S(1)} %collective-permute-done.26.refs_1_, ...), custom_call_target="tpu_custom_call" | custom-call | flops 1610612736 | tf_op jit(solution)/shard_map/grad/pallas_call | solution.py:50
  80.8 0.6 collective-permute-start.32
  81.3 1.2 %grad_rest.1 = (f32[4,32,1024]{2,1,0:T(8,128)S(1)}, bf16[4,32,1024]{2,1,0:T(8,128)(2,1)S(1)}) custom-call(bf16[64,768]{1,0:T(8,128)(2,1)S(1)} %get-tuple-element.75.left_ref, bf16[4,768,1024]{2,1,0:T(8,128)(2,1)S(1)} %get-tuple-element.49.refs_4_.held_ref), custom_call_target="tpu_custom_call" | custom-call | flops 1610612736 | tf_op jit(solution)/shard_map/grad_rest/pallas_call | solution.py:50
  83.0 2.3 %collective-permute-start.34 = (bf16[4,16,1024]{2,1,0:T(8,128)(2,1)S(1)}, bf16[4,16,1024]{2,1,0:T(8,128)(2,1)S(1)}, u32[]{:S(2)}, u32[]{:S(2)}) collective-permute-start(bf16[4,16,1024]{2,1,0:T(8,128)(2,1)S(1)} %get-tuple-element.82), channel_id=1, source_target_pairs={{0,6},{1,7},{2,4},{3,5},{4,2},{5,3},{6,0},{7,1},{8,14},{9,15},{10,... | collective-permute-start | bytes 393224 | tf_op jit(solution)/shard_map/ppermute | solution.py:22
  85.8 0.7 collective-permute-start.36
  86.6 3.6 %collective-permute-done.34.refs_1_ = bf16[4,16,1024]{2,1,0:T(8,128)(2,1)S(1)} collective-permute-done((bf16[4,16,1024]{2,1,0:T(8,128)(2,1)S(1)}, bf16[4,16,1024]{2,1,0:T(8,128)(2,1)S(1)}, u32[]{:S(2)}, u32[]{:S(2)}) %collective-permute-start.34) | collective-permute-done | bytes 131104 | tf_op jit(solution)/shard_map/ppermute | solution.py:22
  90.2 2.0 %collective-permute-done.35.refs_2_ = bf16[4,16,1024]{2,1,0:T(8,128)(2,1)S(1)} collective-permute-done((bf16[4,16,1024]{2,1,0:T(8,128)(2,1)S(1)}, bf16[4,16,1024]{2,1,0:T(8,128)(2,1)S(1)}, u32[]{:S(2)}, u32[]{:S(2)}) %collective-permute-start.35) | collective-permute-done | bytes 131104 | tf_op jit(solution)/shard_map/ppermute | solution.py:22
  92.4 2.2 %collective-permute-start.37 = (bf16[1,16,1024]{2,1,0:T(8,128)(2,1)S(1)}, bf16[1,16,1024]{2,1,0:T(8,128)(2,1)S(1)}, u32[]{:S(2)}, u32[]{:S(2)}) collective-permute-start(bf16[1,16,1024]{2,1,0:T(8,128)(2,1)S(1)} %get-tuple-element.86), channel_id=1, source_target_pairs={{0,24},{1,25},{2,26},{3,27},{4,28},{5,29},{6,30},{7,31},{8,16},{9,... | collective-permute-start | bytes 98312 | tf_op jit(solution)/shard_map/ppermute | solution.py:22
  94.6 0.6 collective-permute-start.38
  95.2 1.7 %collective-permute-start.39 = (bf16[1,16,1024]{2,1,0:T(8,128)(2,1)S(1)}, bf16[1,16,1024]{2,1,0:T(8,128)(2,1)S(1)}, u32[]{:S(2)}, u32[]{:S(2)}) collective-permute-start(bf16[1,16,1024]{2,1,0:T(8,128)(2,1)S(1)} %get-tuple-element.88), channel_id=1, source_target_pairs={{0,8},{1,9},{2,10},{3,11},{4,12},{5,13},{6,14},{7,15},{8,0},{9,1},... | collective-permute-start | bytes 98312 | tf_op jit(solution)/shard_map/ppermute | solution.py:22
  96.8 2.9 %head_weight_grad.1 = f32[1024,1024]{1,0:T(8,128)} custom-call(f32[16,1024]{1,0:T(8,128)S(1)} %get-tuple-element.89.normed_ref, f32[1,1024]{1,0:T(1,128)S(1)} %get-tuple-element.90.bias_grad_ref), custom_call_target="tpu_custom_call" | custom-call | tf_op jit(solution)/shard_map/head_weight_grad/pallas_call | solution.py:370
  99.8 0.6 far_sum.1
  (58 shorter events, 6.9 us)
Async XLA Ops:
  0.6 10.5 %collective-permute-start = (bf16[16,1024]{1,0:T(8,128)(2,1)}, bf16[16,1024]{1,0:T(8,128)(2,1)S(1)}, u32[]{:S(2)}, u32[]{:S(2)}) collective-permute-start(bf16[16,1024]{1,0:T(8,128)(2,1)} %refs_0_.1), channel_id=1, source_target_pairs={{0,8},{1,9},{2,10},{3,11},{4,12},{5,13},{6,14},{7,15},{8,0},{9,1},... | collective-permute-start | bytes 98312 | tf_op jit(solution)/shard_map/ppermute | solution.py:22
  3.7 7.4 %collective-permute-start.2 = (bf16[16,1024]{1,0:T(8,128)(2,1)}, bf16[16,1024]{1,0:T(8,128)(2,1)S(1)}, u32[]{:S(2)}, u32[]{:S(2)}) collective-permute-start(bf16[16,1024]{1,0:T(8,128)(2,1)} %refs_0_.1), channel_id=1, source_target_pairs={{0,24},{1,25},{2,26},{3,27},{4,28},{5,29},{6,30},{7,31},{8,16},{9,... | collective-permute-start | bytes 98312 | tf_op jit(solution)/shard_map/ppermute | solution.py:22
  6.2 5.4 %collective-permute-start.1 = (bf16[16,1024]{1,0:T(8,128)(2,1)}, bf16[16,1024]{1,0:T(8,128)(2,1)S(1)}, u32[]{:S(2)}, u32[]{:S(2)}) collective-permute-start(bf16[16,1024]{1,0:T(8,128)(2,1)} %refs_0_.1), channel_id=1, source_target_pairs={{0,16},{1,17},{2,18},{3,19},{4,20},{5,21},{6,22},{7,23},{8,24},{9,... | collective-permute-start | bytes 98312 | tf_op jit(solution)/shard_map/ppermute | solution.py:22
  11.6 6.8 %collective-permute-start.7 = (bf16[4,16,1024]{2,1,0:T(8,128)(2,1)S(1)}, bf16[4,16,1024]{2,1,0:T(8,128)(2,1)S(1)}, u32[]{:S(2)}, u32[]{:S(2)}) collective-permute-start(bf16[4,16,1024]{2,1,0:T(8,128)(2,1)S(1)} %stack.2.refs_0_), channel_id=1, source_target_pairs={{0,2},{1,3},{2,0},{3,1},{4,6},{5,7},{6,4},{7,5},{8,10},{9,11},{10,... | collective-permute-start | bytes 393224 | tf_op jit(solution)/shard_map/ppermute | solution.py:22
  13.2 6.3 %collective-permute-start.4 = (bf16[4,16,1024]{2,1,0:T(8,128)(2,1)S(1)}, bf16[4,16,1024]{2,1,0:T(8,128)(2,1)S(1)}, u32[]{:S(2)}, u32[]{:S(2)}) collective-permute-start(bf16[4,16,1024]{2,1,0:T(8,128)(2,1)S(1)} %stack.2.refs_0_), channel_id=1, source_target_pairs={{0,6},{1,7},{2,4},{3,5},{4,2},{5,3},{6,0},{7,1},{8,14},{9,15},{10,... | collective-permute-start | bytes 393224 | tf_op jit(solution)/shard_map/ppermute | solution.py:22
  14.6 5.4 %collective-permute-start.3 = (bf16[4,16,1024]{2,1,0:T(8,128)(2,1)S(1)}, bf16[4,16,1024]{2,1,0:T(8,128)(2,1)S(1)}, u32[]{:S(2)}, u32[]{:S(2)}) collective-permute-start(bf16[4,16,1024]{2,1,0:T(8,128)(2,1)S(1)} %stack.2.refs_0_), channel_id=1, source_target_pairs={{0,4},{1,5},{2,6},{3,7},{4,0},{5,1},{6,2},{7,3},{8,12},{9,13},{10,... | collective-permute-start | bytes 393224 | tf_op jit(solution)/shard_map/ppermute | solution.py:22
  15.1 4.9 %collective-permute-start.8 = (bf16[4,16,1024]{2,1,0:T(8,128)(2,1)S(1)}, bf16[4,16,1024]{2,1,0:T(8,128)(2,1)S(1)}, u32[]{:S(2)}, u32[]{:S(2)}) collective-permute-start(bf16[4,16,1024]{2,1,0:T(8,128)(2,1)S(1)} %stack.2.refs_0_), channel_id=1, source_target_pairs={{0,1},{1,0},{2,3},{3,2},{4,5},{5,4},{6,7},{7,6},{8,9},{9,8},{10,11... | collective-permute-start | bytes 393224 | tf_op jit(solution)/shard_map/ppermute | solution.py:22
  18.3 1.7 %collective-permute-start.9 = (bf16[4,16,1024]{2,1,0:T(8,128)(2,1)S(1)}, bf16[4,16,1024]{2,1,0:T(8,128)(2,1)S(1)}, u32[]{:S(2)}, u32[]{:S(2)}) collective-permute-start(bf16[4,16,1024]{2,1,0:T(8,128)(2,1)S(1)} %collective-permute-done.7.refs_1_), channel_id=1, source_target_pairs={{0,1},{1,0},{2,3},{3,2},{4,5},{5,4},{6,7},{7,6},{8,9},{9,8},{10,11... | collective-permute-start | bytes 393224 | tf_op jit(solution)/shard_map/ppermute | solution.py:22
  19.5 2.5 %collective-permute-start.6 = (bf16[4,16,1024]{2,1,0:T(8,128)(2,1)S(1)}, bf16[4,16,1024]{2,1,0:T(8,128)(2,1)S(1)}, u32[]{:S(2)}, u32[]{:S(2)}) collective-permute-start(bf16[4,16,1024]{2,1,0:T(8,128)(2,1)S(1)} %collective-permute-done.4.refs_1_), channel_id=1, source_target_pairs={{0,1},{1,0},{2,3},{3,2},{4,5},{5,4},{6,7},{7,6},{8,9},{9,8},{10,11... | collective-permute-start | bytes 393224 | tf_op jit(solution)/shard_map/ppermute | solution.py:22
  20.0 2.1 %collective-permute-start.5 = (bf16[4,16,1024]{2,1,0:T(8,128)(2,1)S(1)}, bf16[4,16,1024]{2,1,0:T(8,128)(2,1)S(1)}, u32[]{:S(2)}, u32[]{:S(2)}) collective-permute-start(bf16[4,16,1024]{2,1,0:T(8,128)(2,1)S(1)} %collective-permute-done.3.refs_0_), channel_id=1, source_target_pairs={{0,1},{1,0},{2,3},{3,2},{4,5},{5,4},{6,7},{7,6},{8,9},{9,8},{10,11... | collective-permute-start | bytes 393224 | tf_op jit(solution)/shard_map/ppermute | solution.py:22
  26.2 20.8 %copy-start = (bf16[1024,1024]{1,0:T(8,128)(2,1)S(1)}, bf16[1024,1024]{1,0:T(8,128)(2,1)}, u32[]{:S(2)}) copy-start(bf16[1024,1024]{1,0:T(8,128)(2,1)} %refs_3_.1) | copy-start | bytes 6291460
  26.2 31.6 %copy-start.1 = (f32[1024]{0:T(1024)S(1)}, f32[1024]{0:T(1024)}, u32[]{:S(2)}) copy-start(f32[1024]{0:T(1024)} %param.12) | copy-start | bytes 12292
  26.3 31.5 %copy-start.2 = (s32[1024]{0:T(1024)S(1)}, s32[1024]{0:T(1024)}, u32[]{:S(2)}) copy-start(s32[1024]{0:T(1024)} %param.13) | copy-start | bytes 12292
  26.3 1.8 %collective-permute-start.10 = (bf16[4,32,1152]{2,1,0:T(8,128)(2,1)S(1)}, bf16[4,32,1152]{2,1,0:T(8,128)(2,1)S(1)}, u32[]{:S(2)}, u32[]{:S(2)}) collective-permute-start(bf16[4,32,1152]{2,1,0:T(8,128)(2,1)S(1)} %get-tuple-element.55), channel_id=1, source_target_pairs={{0,1},{1,0},{2,3},{3,2},{4,5},{5,4},{6,7},{7,6},{8,9},{9,8},{10,11... | collective-permute-start | bytes 884744 | tf_op jit(solution)/shard_map/ppermute | solution.py:22
  28.4 3.4 %collective-permute-start.11 = (bf16[4,32,1152]{2,1,0:T(8,128)(2,1)S(1)}, bf16[4,32,1152]{2,1,0:T(8,128)(2,1)S(1)}, u32[]{:S(2)}, u32[]{:S(2)}) collective-permute-start(bf16[4,32,1152]{2,1,0:T(8,128)(2,1)S(1)} %get-tuple-element.57), channel_id=1, source_target_pairs={{0,1},{1,0},{2,3},{3,2},{4,5},{5,4},{6,7},{7,6},{8,9},{9,8},{10,11... | collective-permute-start | bytes 884744 | tf_op jit(solution)/shard_map/ppermute | solution.py:22
  28.8 7.6 %collective-permute-start.12 = (bf16[4,16,1152]{2,1,0:T(8,128)(2,1)S(1)}, bf16[4,16,1152]{2,1,0:T(8,128)(2,1)S(1)}, u32[]{:S(2)}, u32[]{:S(2)}) collective-permute-start(bf16[4,16,1152]{2,1,0:T(8,128)(2,1)S(1)} %get-tuple-element.59), channel_id=1, source_target_pairs={{0,6},{1,7},{2,4},{3,5},{4,2},{5,3},{6,0},{7,1},{8,14},{9,15},{10,... | collective-permute-start | bytes 442376 | tf_op jit(solution)/shard_map/ppermute | solution.py:22
  31.2 7.6 %collective-permute-start.13 = (bf16[4,16,1152]{2,1,0:T(8,128)(2,1)S(1)}, bf16[4,16,1152]{2,1,0:T(8,128)(2,1)S(1)}, u32[]{:S(2)}, u32[]{:S(2)}) collective-permute-start(bf16[4,16,1152]{2,1,0:T(8,128)(2,1)S(1)} %get-tuple-element.60), channel_id=1, source_target_pairs={{0,4},{1,5},{2,6},{3,7},{4,0},{5,1},{6,2},{7,3},{8,12},{9,13},{10,... | collective-permute-start | bytes 442376 | tf_op jit(solution)/shard_map/ppermute | solution.py:22
  32.0 6.7 %collective-permute-start.14 = (bf16[4,16,1152]{2,1,0:T(8,128)(2,1)S(1)}, bf16[4,16,1152]{2,1,0:T(8,128)(2,1)S(1)}, u32[]{:S(2)}, u32[]{:S(2)}) collective-permute-start(bf16[4,16,1152]{2,1,0:T(8,128)(2,1)S(1)} %get-tuple-element.61), channel_id=1, source_target_pairs={{0,2},{1,3},{2,0},{3,1},{4,6},{5,7},{6,4},{7,5},{8,10},{9,11},{10,... | collective-permute-start | bytes 442376 | tf_op jit(solution)/shard_map/ppermute | solution.py:22
  39.1 6.2 %collective-permute-start.15 = (bf16[1,16,1152]{2,1,0:T(8,128)(2,1)S(1)}, bf16[1,16,1152]{2,1,0:T(8,128)(2,1)S(1)}, u32[]{:S(2)}, u32[]{:S(2)}) collective-permute-start(bf16[1,16,1152]{2,1,0:T(8,128)(2,1)S(1)} %get-tuple-element.64), channel_id=1, source_target_pairs={{0,24},{1,25},{2,26},{3,27},{4,28},{5,29},{6,30},{7,31},{8,16},{9,... | collective-permute-start | bytes 110600 | tf_op jit(solution)/shard_map/ppermute | solution.py:22
  41.8 5.1 %collective-permute-start.16 = (bf16[1,16,1152]{2,1,0:T(8,128)(2,1)S(1)}, bf16[1,16,1152]{2,1,0:T(8,128)(2,1)S(1)}, u32[]{:S(2)}, u32[]{:S(2)}) collective-permute-start(bf16[1,16,1152]{2,1,0:T(8,128)(2,1)S(1)} %get-tuple-element.65), channel_id=1, source_target_pairs={{0,16},{1,17},{2,18},{3,19},{4,20},{5,21},{6,22},{7,23},{8,24},{9,... | collective-permute-start | bytes 110600 | tf_op jit(solution)/shard_map/ppermute | solution.py:22
  42.2 4.8 %collective-permute-start.17 = (bf16[1,16,1152]{2,1,0:T(8,128)(2,1)S(1)}, bf16[1,16,1152]{2,1,0:T(8,128)(2,1)S(1)}, u32[]{:S(2)}, u32[]{:S(2)}) collective-permute-start(bf16[1,16,1152]{2,1,0:T(8,128)(2,1)S(1)} %get-tuple-element.66), channel_id=1, source_target_pairs={{0,8},{1,9},{2,10},{3,11},{4,12},{5,13},{6,14},{7,15},{8,0},{9,1},... | collective-permute-start | bytes 110600 | tf_op jit(solution)/shard_map/ppermute | solution.py:22
  47.6 5.5 %collective-permute-start.20 = (f32[2,1024]{1,0:T(2,128)S(1)}, f32[2,1024]{1,0:T(2,128)S(1)}, u32[]{:S(2)}, u32[]{:S(2)}) collective-permute-start(f32[2,1024]{1,0:T(2,128)S(1)} %get-tuple-element.69.refs_0_), channel_id=1, source_target_pairs={{0,24},{1,25},{2,26},{3,27},{4,28},{5,29},{6,30},{7,31},{8,16},{9,... | collective-permute-start | bytes 24584 | tf_op jit(solution)/shard_map/ppermute | solution.py:22
  49.5 4.5 %collective-permute-start.19 = (f32[2,1024]{1,0:T(2,128)S(1)}, f32[2,1024]{1,0:T(2,128)S(1)}, u32[]{:S(2)}, u32[]{:S(2)}) collective-permute-start(f32[2,1024]{1,0:T(2,128)S(1)} %get-tuple-element.69.refs_0_), channel_id=1, source_target_pairs={{0,16},{1,17},{2,18},{3,19},{4,20},{5,21},{6,22},{7,23},{8,24},{9,... | collective-permute-start | bytes 24584 | tf_op jit(solution)/shard_map/ppermute | solution.py:22
  49.7 4.4 %collective-permute-start.18 = (f32[2,1024]{1,0:T(2,128)S(1)}, f32[2,1024]{1,0:T(2,128)S(1)}, u32[]{:S(2)}, u32[]{:S(2)}) collective-permute-start(f32[2,1024]{1,0:T(2,128)S(1)} %get-tuple-element.69.refs_0_), channel_id=1, source_target_pairs={{0,8},{1,9},{2,10},{3,11},{4,12},{5,13},{6,14},{7,15},{8,0},{9,1},... | collective-permute-start | bytes 24584 | tf_op jit(solution)/shard_map/ppermute | solution.py:22
  54.1 3.7 %collective-permute-start.21 = (f32[2,1024]{1,0:T(2,128)S(1)}, f32[2,1024]{1,0:T(2,128)S(1)}, u32[]{:S(2)}, u32[]{:S(2)}) collective-permute-start(f32[2,1024]{1,0:T(2,128)S(1)} %tree_sum.1.sums_ref), channel_id=1, source_target_pairs={{0,4},{1,5},{2,6},{3,7},{4,0},{5,1},{6,2},{7,3},{8,12},{9,13},{10,... | collective-permute-start | bytes 24584 | tf_op jit(solution)/shard_map/ppermute | solution.py:22
  59.0 5.8 %collective-permute-start.24 = (bf16[16,1152]{1,0:T(8,128)(2,1)S(1)}, bf16[16,1152]{1,0:T(8,128)(2,1)S(1)}, u32[]{:S(2)}, u32[]{:S(2)}) collective-permute-start(bf16[16,1152]{1,0:T(8,128)(2,1)S(1)} %get-tuple-element.72.refs_0_), channel_id=1, source_target_pairs={{0,24},{1,25},{2,26},{3,27},{4,28},{5,29},{6,30},{7,31},{8,16},{9,... | collective-permute-start | bytes 110600 | tf_op jit(solution)/shard_map/ppermute | solution.py:22
  61.0 5.3 %collective-permute-start.23 = (bf16[16,1152]{1,0:T(8,128)(2,1)S(1)}, bf16[16,1152]{1,0:T(8,128)(2,1)S(1)}, u32[]{:S(2)}, u32[]{:S(2)}) collective-permute-start(bf16[16,1152]{1,0:T(8,128)(2,1)S(1)} %get-tuple-element.72.refs_0_), channel_id=1, source_target_pairs={{0,16},{1,17},{2,18},{3,19},{4,20},{5,21},{6,22},{7,23},{8,24},{9,... | collective-permute-start | bytes 110600 | tf_op jit(solution)/shard_map/ppermute | solution.py:22
  62.0 4.3 %collective-permute-start.22 = (bf16[16,1152]{1,0:T(8,128)(2,1)S(1)}, bf16[16,1152]{1,0:T(8,128)(2,1)S(1)}, u32[]{:S(2)}, u32[]{:S(2)}) collective-permute-start(bf16[16,1152]{1,0:T(8,128)(2,1)S(1)} %get-tuple-element.72.refs_0_), channel_id=1, source_target_pairs={{0,8},{1,9},{2,10},{3,11},{4,12},{5,13},{6,14},{7,15},{8,0},{9,1},... | collective-permute-start | bytes 110600 | tf_op jit(solution)/shard_map/ppermute | solution.py:22
  66.4 5.2 %collective-permute-start.29 = (bf16[4,16,1152]{2,1,0:T(8,128)(2,1)S(1)}, bf16[4,16,1152]{2,1,0:T(8,128)(2,1)S(1)}, u32[]{:S(2)}, u32[]{:S(2)}) collective-permute-start(bf16[4,16,1152]{2,1,0:T(8,128)(2,1)S(1)} %stack.3.refs_0_), channel_id=1, source_target_pairs={{0,2},{1,3},{2,0},{3,1},{4,6},{5,7},{6,4},{7,5},{8,10},{9,11},{10,... | collective-permute-start | bytes 442376 | tf_op jit(solution)/shard_map/ppermute | solution.py:22
  67.8 6.0 %collective-permute-start.26 = (bf16[4,16,1152]{2,1,0:T(8,128)(2,1)S(1)}, bf16[4,16,1152]{2,1,0:T(8,128)(2,1)S(1)}, u32[]{:S(2)}, u32[]{:S(2)}) collective-permute-start(bf16[4,16,1152]{2,1,0:T(8,128)(2,1)S(1)} %stack.3.refs_0_), channel_id=1, source_target_pairs={{0,6},{1,7},{2,4},{3,5},{4,2},{5,3},{6,0},{7,1},{8,14},{9,15},{10,... | collective-permute-start | bytes 442376 | tf_op jit(solution)/shard_map/ppermute | solution.py:22
  69.4 5.2 %collective-permute-start.25 = (bf16[4,16,1152]{2,1,0:T(8,128)(2,1)S(1)}, bf16[4,16,1152]{2,1,0:T(8,128)(2,1)S(1)}, u32[]{:S(2)}, u32[]{:S(2)}) collective-permute-start(bf16[4,16,1152]{2,1,0:T(8,128)(2,1)S(1)} %stack.3.refs_0_), channel_id=1, source_target_pairs={{0,4},{1,5},{2,6},{3,7},{4,0},{5,1},{6,2},{7,3},{8,12},{9,13},{10,... | collective-permute-start | bytes 442376 | tf_op jit(solution)/shard_map/ppermute | solution.py:22
  70.0 4.7 %collective-permute-start.30 = (bf16[4,16,1152]{2,1,0:T(8,128)(2,1)S(1)}, bf16[4,16,1152]{2,1,0:T(8,128)(2,1)S(1)}, u32[]{:S(2)}, u32[]{:S(2)}) collective-permute-start(bf16[4,16,1152]{2,1,0:T(8,128)(2,1)S(1)} %stack.3.refs_0_), channel_id=1, source_target_pairs={{0,1},{1,0},{2,3},{3,2},{4,5},{5,4},{6,7},{7,6},{8,9},{9,8},{10,11... | collective-permute-start | bytes 442376 | tf_op jit(solution)/shard_map/ppermute | solution.py:22
  71.6 3.1 %collective-permute-start.31 = (bf16[4,16,1152]{2,1,0:T(8,128)(2,1)S(1)}, bf16[4,16,1152]{2,1,0:T(8,128)(2,1)S(1)}, u32[]{:S(2)}, u32[]{:S(2)}) collective-permute-start(bf16[4,16,1152]{2,1,0:T(8,128)(2,1)S(1)} %collective-permute-done.29.refs_1_), channel_id=1, source_target_pairs={{0,1},{1,0},{2,3},{3,2},{4,5},{5,4},{6,7},{7,6},{8,9},{9,8},{10,11... | collective-permute-start | bytes 442376 | tf_op jit(solution)/shard_map/ppermute | solution.py:22
  73.9 2.8 %collective-permute-start.28 = (bf16[4,16,1152]{2,1,0:T(8,128)(2,1)S(1)}, bf16[4,16,1152]{2,1,0:T(8,128)(2,1)S(1)}, u32[]{:S(2)}, u32[]{:S(2)}) collective-permute-start(bf16[4,16,1152]{2,1,0:T(8,128)(2,1)S(1)} %collective-permute-done.26.refs_1_), channel_id=1, source_target_pairs={{0,1},{1,0},{2,3},{3,2},{4,5},{5,4},{6,7},{7,6},{8,9},{9,8},{10,11... | collective-permute-start | bytes 442376 | tf_op jit(solution)/shard_map/ppermute | solution.py:22
  74.7 2.0 %collective-permute-start.27 = (bf16[4,16,1152]{2,1,0:T(8,128)(2,1)S(1)}, bf16[4,16,1152]{2,1,0:T(8,128)(2,1)S(1)}, u32[]{:S(2)}, u32[]{:S(2)}) collective-permute-start(bf16[4,16,1152]{2,1,0:T(8,128)(2,1)S(1)} %collective-permute-done.25.refs_0_), channel_id=1, source_target_pairs={{0,1},{1,0},{2,3},{3,2},{4,5},{5,4},{6,7},{7,6},{8,9},{9,8},{10,11... | collective-permute-start | bytes 442376 | tf_op jit(solution)/shard_map/ppermute | solution.py:22
  80.8 1.8 %collective-permute-start.32 = (bf16[4,32,1024]{2,1,0:T(8,128)(2,1)S(1)}, bf16[4,32,1024]{2,1,0:T(8,128)(2,1)S(1)}, u32[]{:S(2)}, u32[]{:S(2)}) collective-permute-start(bf16[4,32,1024]{2,1,0:T(8,128)(2,1)S(1)} %get-tuple-element.78), channel_id=1, source_target_pairs={{0,1},{1,0},{2,3},{3,2},{4,5},{5,4},{6,7},{7,6},{8,9},{9,8},{10,11... | collective-permute-start | bytes 786440 | tf_op jit(solution)/shard_map/ppermute | solution.py:22
  82.6 3.2 %collective-permute-start.33 = (bf16[4,32,1024]{2,1,0:T(8,128)(2,1)S(1)}, bf16[4,32,1024]{2,1,0:T(8,128)(2,1)S(1)}, u32[]{:S(2)}, u32[]{:S(2)}) collective-permute-start(bf16[4,32,1024]{2,1,0:T(8,128)(2,1)S(1)} %get-tuple-element.80), channel_id=1, source_target_pairs={{0,1},{1,0},{2,3},{3,2},{4,5},{5,4},{6,7},{7,6},{8,9},{9,8},{10,11... | collective-permute-start | bytes 786440 | tf_op jit(solution)/shard_map/ppermute | solution.py:22
  83.0 7.2 %collective-permute-start.34 = (bf16[4,16,1024]{2,1,0:T(8,128)(2,1)S(1)}, bf16[4,16,1024]{2,1,0:T(8,128)(2,1)S(1)}, u32[]{:S(2)}, u32[]{:S(2)}) collective-permute-start(bf16[4,16,1024]{2,1,0:T(8,128)(2,1)S(1)} %get-tuple-element.82), channel_id=1, source_target_pairs={{0,6},{1,7},{2,4},{3,5},{4,2},{5,3},{6,0},{7,1},{8,14},{9,15},{10,... | collective-permute-start | bytes 393224 | tf_op jit(solution)/shard_map/ppermute | solution.py:22
  85.3 6.9 %collective-permute-start.35 = (bf16[4,16,1024]{2,1,0:T(8,128)(2,1)S(1)}, bf16[4,16,1024]{2,1,0:T(8,128)(2,1)S(1)}, u32[]{:S(2)}, u32[]{:S(2)}) collective-permute-start(bf16[4,16,1024]{2,1,0:T(8,128)(2,1)S(1)} %get-tuple-element.83), channel_id=1, source_target_pairs={{0,4},{1,5},{2,6},{3,7},{4,0},{5,1},{6,2},{7,3},{8,12},{9,13},{10,... | collective-permute-start | bytes 393224 | tf_op jit(solution)/shard_map/ppermute | solution.py:22
  85.8 6.5 %collective-permute-start.36 = (bf16[4,16,1024]{2,1,0:T(8,128)(2,1)S(1)}, bf16[4,16,1024]{2,1,0:T(8,128)(2,1)S(1)}, u32[]{:S(2)}, u32[]{:S(2)}) collective-permute-start(bf16[4,16,1024]{2,1,0:T(8,128)(2,1)S(1)} %get-tuple-element.84), channel_id=1, source_target_pairs={{0,2},{1,3},{2,0},{3,1},{4,6},{5,7},{6,4},{7,5},{8,10},{9,11},{10,... | collective-permute-start | bytes 393224 | tf_op jit(solution)/shard_map/ppermute | solution.py:22
  92.4 7.4 %collective-permute-start.37 = (bf16[1,16,1024]{2,1,0:T(8,128)(2,1)S(1)}, bf16[1,16,1024]{2,1,0:T(8,128)(2,1)S(1)}, u32[]{:S(2)}, u32[]{:S(2)}) collective-permute-start(bf16[1,16,1024]{2,1,0:T(8,128)(2,1)S(1)} %get-tuple-element.86), channel_id=1, source_target_pairs={{0,24},{1,25},{2,26},{3,27},{4,28},{5,29},{6,30},{7,31},{8,16},{9,... | collective-permute-start | bytes 98312 | tf_op jit(solution)/shard_map/ppermute | solution.py:22
  94.6 5.2 %collective-permute-start.38 = (bf16[1,16,1024]{2,1,0:T(8,128)(2,1)S(1)}, bf16[1,16,1024]{2,1,0:T(8,128)(2,1)S(1)}, u32[]{:S(2)}, u32[]{:S(2)}) collective-permute-start(bf16[1,16,1024]{2,1,0:T(8,128)(2,1)S(1)} %get-tuple-element.87), channel_id=1, source_target_pairs={{0,16},{1,17},{2,18},{3,19},{4,20},{5,21},{6,22},{7,23},{8,24},{9,... | collective-permute-start | bytes 98312 | tf_op jit(solution)/shard_map/ppermute | solution.py:22
  95.2 4.6 %collective-permute-start.39 = (bf16[1,16,1024]{2,1,0:T(8,128)(2,1)S(1)}, bf16[1,16,1024]{2,1,0:T(8,128)(2,1)S(1)}, u32[]{:S(2)}, u32[]{:S(2)}) collective-permute-start(bf16[1,16,1024]{2,1,0:T(8,128)(2,1)S(1)} %get-tuple-element.88), channel_id=1, source_target_pairs={{0,8},{1,9},{2,10},{3,11},{4,12},{5,13},{6,14},{7,15},{8,0},{9,1},... | collective-permute-start | bytes 98312 | tf_op jit(solution)/shard_map/ppermute | solution.py:22

commit v8 on v7

--- a/solution.py
+++ b/solution.py
@@ -28,19 +28,14 @@
 
 def near_steps():
     steps = [(i, 2 * k) for i in range(2) for k in range(lax.axis_size("cls") // 2) if i or k]
-    return sorted(steps, key=lambda step: (not (step[0] and step[1]), not step[0]))
-
-
-def call(kernel, outs, name, args, smem_args=(), aliases=None, limit=16, cost=None):
-    def spec(i):
-        if i in smem_args:
-            return pl.BlockSpec(memory_space=pltpu.SMEM)
-        return pl.BlockSpec(memory_space=pltpu.VMEM)
-
+    return sorted(steps, key=lambda step: (not step[0], bool(step[1])))
+
+
+def call(kernel, outs, name, args, aliases=None, limit=16, cost=None):
     run = pl.pallas_call(
         kernel,
         out_shape=[jax.ShapeDtypeStruct(s, d) for s, d in outs],
-        in_specs=[spec(i) for i in range(len(args))],
+        in_specs=[pl.BlockSpec(memory_space=pltpu.VMEM)] * len(args),
         out_specs=[pl.BlockSpec(memory_space=pltpu.VMEM)] * len(outs),
         input_output_aliases=aliases or {},
         compiler_params=pltpu.CompilerParams(vmem_limit_bytes=limit * MIB),
@@ -56,13 +51,23 @@
         out_ref[at] = ref[...].reshape(out_ref.shape[1:])
 
 
-def gather(block, local=None):
+def hand_on_kernel(*refs):
+    del refs
+
+
+def hand_on(arrays, after):
+    outs = [(x.shape, x.dtype) for x in arrays]
+    return call(hand_on_kernel, outs, "hand_on", [*arrays, *after], aliases={i: i for i in range(len(arrays))})
+
+
+def gather(block, local=None, after=()):
     far = [swap(block, *step) for step in far_steps()[::-1]]
     rows, width = block.shape
     (held,) = call(
         stack_kernel, [((len(far) + 1, rows, width), block.dtype)], "stack", [block if local is None else local, *far]
     )
-    parts = {step: swap(held, *step) for step in near_steps()[::-1]}
+    steps = sorted(near_steps(), reverse=True)
+    parts = dict(zip(steps, hand_on([swap(held, *step) for step in steps], after)))
     parts[0, 0] = held
     other = {step: swap(part, 0, 1) for step, part in parts.items()}
     steps = sorted(parts)
@@ -91,36 +96,38 @@
     return block[:, at : at + 1] + (block[:, at + 1 : at + 2] + block[:, at + 2 : at + 3])
 
 
-def load_kernel(tokens_ref, *refs):
-    count = (len(refs) - 3) // 2
-    others, halves, copies_of, sems = refs[:count], refs[count : count + 2], refs[count + 2 : -1], refs[-1]
-    blocks, _, width = halves[0].shape
+def load_kernel(half, count, length_ref, tokens_ref, *refs):
+    others, held_ref, copies_of = refs[:count], refs[count], refs[count + 1 : 2 * count + 1]
+    length_out_ref, sems = refs[2 * count + 1 :]
+    blocks, _, width = held_ref.shape
     copies = [pltpu.make_async_copy(src, dst, sems.at[i]) for i, (src, dst) in enumerate(zip(others, copies_of))]
-    for i in range(2):
-        for j in range(blocks):
-            start = pl.multiple_of((lax.axis_index("ctx") ^ i ^ (2 * j)) * width, LANES)
-            sem = sems.at[count + i * blocks + j]
-            copies.append(pltpu.make_async_copy(tokens_ref.at[:, pl.ds(start, width)], halves[i].at[j], sem))
+    for j in range(blocks):
+        start = pl.multiple_of((lax.axis_index("ctx") ^ half ^ (2 * j)) * width, LANES)
+        copies.append(
+            pltpu.make_async_copy(tokens_ref.at[:, pl.ds(start, width)], held_ref.at[j], sems.at[count + j])
+        )
     for copy in copies:
         copy.start()
+    length_out_ref[...] = jnp.full(length_out_ref.shape, length_ref[0], jnp.int32)
     for copy in copies:
         copy.wait()
 
 
-def load(width, tokens, *others):
+def load(half, width, length, tokens, *others):
     rows, full_width = tokens.shape
     blocks = full_width // width // 2
-    outs = [pltpu.VMEM((blocks, rows, width), tokens.dtype)] * 2 + [pltpu.VMEM(x.shape, x.dtype) for x in others]
+    outs = [((blocks, rows, width), tokens.dtype)] + [(x.shape, x.dtype) for x in others] + [((1, LANES), jnp.int32)]
+    hbm = (tokens, *others)
     run = pl.pallas_call(
-        load_kernel,
-        out_shape=outs,
-        in_specs=[pl.BlockSpec(memory_space=pltpu.HBM)] * (1 + len(others)),
+        functools.partial(load_kernel, half, len(others)),
+        out_shape=[pltpu.VMEM(*out) for out in outs],
+        in_specs=[pl.BlockSpec(memory_space=pltpu.SMEM)] + [pl.BlockSpec(memory_space=pltpu.HBM)] * len(hbm),
         out_specs=[pl.BlockSpec(memory_space=pltpu.VMEM)] * len(outs),
-        scratch_shapes=[pltpu.SemaphoreType.DMA((2 * blocks + len(others),))],
+        scratch_shapes=[pltpu.SemaphoreType.DMA((blocks + len(others),))],
         compiler_params=pltpu.CompilerParams(vmem_limit_bytes=16 * MIB),
         name="load",
     )
-    return run(*[pltpu.with_memory_space_constraint(x, pltpu.HBM) for x in (tokens, *others)])
+    return run(length, *[pltpu.with_memory_space_constraint(x, pltpu.HBM) for x in hbm])
 
 
 def project(parts, held_ref, tile=256):
@@ -161,7 +168,7 @@
     part_ref, held_ref, keep_ref, send_ref, peak_ref, w_ref, left_ref = refs
     scores = part_ref[...] + project(parts, held_ref)
     shard = lax.axis_index("ctx") * lax.axis_size("cls") + lax.axis_index("cls")
-    valid = lax.broadcasted_iota(jnp.int32, scores.shape, 1) < length_ref[0] - shard * scores.shape[1]
+    valid = lax.broadcasted_iota(jnp.int32, scores.shape, 1) < length_ref[:, :1] - shard * scores.shape[1]
     peak = jnp.max(jnp.where(valid, scores, MASKED), axis=1, keepdims=True)
     weights = jnp.where(valid, jnp.exp(scores - peak), 0.0)
     left = weights.astype(BF16)
@@ -352,7 +359,7 @@
     normed_ref[...] = unit * gain
 
 
-def head_weight_grad_kernel(attributes, normed_ref, bias_grad_ref, out_ref):
+def head_weight_grad_kernel(attributes, normed_ref, bias_grad_ref, out_ref, done_ref):
     heads = normed_ref.shape[0]
     columns = out_ref.shape[1]
     parts = jnp.concatenate(pieces(normed_ref[...]), axis=0)
@@ -361,6 +368,7 @@
     ones = jnp.where(column // attributes == row, 1.0, 0.0).astype(BF16)
     normed = lax.dot_general(parts, ones, (((0,), (0,)), ((), ())), preferred_element_type=F32)
     out_ref[...] = normed * bias_grad_ref[...]
+    done_ref[...] = jnp.zeros_like(done_ref)
 
 
 def head_weight_grad(normed, bias_grad):
@@ -369,13 +377,13 @@
     block = columns // 4
     return pl.pallas_call(
         functools.partial(head_weight_grad_kernel, columns // rows),
-        out_shape=jax.ShapeDtypeStruct((width, columns), F32),
+        out_shape=[jax.ShapeDtypeStruct((width, columns), F32), jax.ShapeDtypeStruct((8, LANES), F32)],
         grid=(columns // block,),
         in_specs=[
             pl.BlockSpec((rows, width), lambda i: (0, 0)),
             pl.BlockSpec((1, block), lambda i: (0, i)),
         ],
-        out_specs=pl.BlockSpec((width, block), lambda i: (0, i)),
+        out_specs=[pl.BlockSpec((width, block), lambda i: (0, i)), pl.BlockSpec((8, LANES), lambda i: (0, 0))],
         compiler_params=pltpu.CompilerParams(vmem_limit_bytes=16 * MIB),
         name="head_weight_grad",
     )(normed, bias_grad)
@@ -397,15 +405,15 @@
     def project_half(parts):
         return call(functools.partial(project_kernel, len(parts)), [product], "project", [*parts, held_a], cost=cost)[0]
 
-    held_a, held_b, queries_here, gain = load(width, tokens, queries, norm_gain[None, :])
-    first, second = gather(queries, queries_here)
+    held_a, queries_here, length = load(0, width, doc_length, tokens, queries)
+    held_b, gain, _ = load(1, width, doc_length, tokens, norm_gain[None, :])
+    first, second = gather(queries, queries_here, after=(gain,))
     part = project_half(first)
     keep_b, send_b, own_peak, weights, left = call(
         functools.partial(pool_kernel, classes),
         [*pair, ((heads, LANES), F32), product, ((heads, token_count), BF16)],
         "pool",
-        [doc_length, *second, part, held_b],
-        smem_args=(0,),
+        [length, *second, part, held_b],
         cost=cost,
     )
     half_a = call(pool_rest_kernel, pair, "pool_rest", [left, own_peak, held_a], cost=cost)
@@ -424,8 +432,8 @@
         "head_grads",
         [sums, swap(sums, 1, 0), pooled, top, gain, head_weight, head_bias[None, :], labels[None, :]],
     )
-    head_grad = head_weight_grad(normed, bias_grad_here)
-    first, second = gather(pooled_grad)
+    head_grad, done = head_weight_grad(normed, bias_grad_here)
+    first, second = gather(pooled_grad, after=(done,))
     part = project_half(first)
     pair = [((blocks, half, width), F32), ((blocks, half, width), BF16)]
     keep_b, send_b, left, loss = call(

time: 101 us -> 105 us (1.040)
  waiting for transfers between devices: 31.7 us -> 34.2 us
  Pallas kernels: 26 us -> 27.5 us
    ppermute x40, waiting for transfers between devices: 31.7 us -> 34.2 us  [swap(): return lax.ppermute(x, ('ctx', 'cls'), pairs)]
    pallas_call x1 -> x2, Pallas kernels: 4.79 us -> 6.33 us  [load(): run(length, *[pltpu.with_memory_space_constraint(x, pltpu.HBM) for x in h...]
    pallas_call x18 -> x20, Pallas kernels: 18.3 us -> 18.2 us  [call(): return list(run(*args))]
  transfers between devices with their start and end apart: 40 -> 40, of which waited for: 20 -> 24; matrix products, arithmetic and copies ran while one was open for 0% -> 0% of each run, Pallas kernels for 14% -> 15%
where the time goes in v8:
time: 105 us; the launch traced here: 104 us
  starting transfers between devices  41.1 us (39%)
  waiting for transfers between devices  34.2 us (33%)
  Pallas kernels  27.5 us (26%)
  between operations  1.5 us (1%)
    ppermute x40, starting transfers between devices, swap(): return lax.ppermute(x, ('ctx', 'cls'), pairs)  41.1 us
    ppermute x40, waiting for transfers between devices, swap(): return lax.ppermute(x, ('ctx', 'cls'), pairs)  34.2 us
    pallas_call x20, Pallas kernels, call(): return list(run(*args))  18.2 us
    pallas_call x2, Pallas kernels, load(): run(length, *[pltpu.with_memory_space_constraint(x, pltpu.HBM) for x in h...  6.33 us
    pallas_call x1, Pallas kernels, head_weight_grad(): pl.pallas_call(functools.partial(head_weight_grad_kernel, columns // rows...  2.95 us
  transfers between devices with their start and end apart: 40, of which 24 were waited for; matrix products, arithmetic and copies ran while one was open for 0% of the time, Pallas kernels for 15%

profile of v8, /device:TPU:0, one launch (start us, length us, event | category | flops | bytes accessed | tf_op | source)
XLA Modules:
  0.0 104.4 jit_solution(4633984985425257418)
XLA Ops:
  0.6 3.1 %collective-permute-start = (bf16[16,1024]{1,0:T(8,128)(2,1)}, bf16[16,1024]{1,0:T(8,128)(2,1)S(1)}, u32[]{:S(2)}, u32[]{:S(2)}) collective-permute-start(bf16[16,1024]{1,0:T(8,128)(2,1)} %refs_0_.1), channel_id=1, source_target_pairs={{0,8},{1,9},{2,10},{3,11},{4,12},{5,13},{6,14},{7,15},{8,0},{9,1},... | collective-permute-start | bytes 98312 | tf_op jit(solution)/shard_map/ppermute | solution.py:22
  3.7 2.5 %collective-permute-start.2 = (bf16[16,1024]{1,0:T(8,128)(2,1)}, bf16[16,1024]{1,0:T(8,128)(2,1)S(1)}, u32[]{:S(2)}, u32[]{:S(2)}) collective-permute-start(bf16[16,1024]{1,0:T(8,128)(2,1)} %refs_0_.1), channel_id=1, source_target_pairs={{0,24},{1,25},{2,26},{3,27},{4,28},{5,29},{6,30},{7,31},{8,16},{9,... | collective-permute-start | bytes 98312 | tf_op jit(solution)/shard_map/ppermute | solution.py:22
  7.0 2.9 %load.2 = (bf16[4,768,1024]{2,1,0:T(8,128)(2,1)S(1)}, bf16[16,1024]{1,0:T(8,128)(2,1)S(1)}, s32[1,128]{1,0:T(1,128)S(1)}) custom-call(s32[1]{0:T(128)S(6)} %copy.27.length_ref, bf16[768,8192]{1,0:T(8,128)(2,1)} %tokens_ref.3, bf16[16,1024]{1,0:T(8,128)(2,1)} %refs_0_.1), custom_call_target="tpu_custom_call" | custom-call | tf_op jit(solution)/shard_map/load/pallas_call | solution.py:130
  10.1 1.5 %collective-permute-done.1.refs_2_ = bf16[16,1024]{1,0:T(8,128)(2,1)S(1)} collective-permute-done((bf16[16,1024]{1,0:T(8,128)(2,1)}, bf16[16,1024]{1,0:T(8,128)(2,1)S(1)}, u32[]{:S(2)}, u32[]{:S(2)}) %collective-permute-start.1) | collective-permute-done | bytes 32800 | tf_op jit(solution)/shard_map/ppermute | solution.py:22
  11.6 1.6 %collective-permute-start.5 = (bf16[4,16,1024]{2,1,0:T(8,128)(2,1)S(1)}, bf16[4,16,1024]{2,1,0:T(8,128)(2,1)S(1)}, u32[]{:S(2)}, u32[]{:S(2)}) collective-permute-start(bf16[4,16,1024]{2,1,0:T(8,128)(2,1)S(1)} %stack.2.refs_0_), channel_id=1, source_target_pairs={{0,2},{1,3},{2,0},{3,1},{4,6},{5,7},{6,4},{7,5},{8,10},{9,11},{10,... | collective-permute-start | bytes 393224 | tf_op jit(solution)/shard_map/ppermute | solution.py:22
  13.2 1.5 %collective-permute-start.4 = (bf16[4,16,1024]{2,1,0:T(8,128)(2,1)S(1)}, bf16[4,16,1024]{2,1,0:T(8,128)(2,1)S(1)}, u32[]{:S(2)}, u32[]{:S(2)}) collective-permute-start(bf16[4,16,1024]{2,1,0:T(8,128)(2,1)S(1)} %stack.2.refs_0_), channel_id=1, source_target_pairs={{0,4},{1,5},{2,6},{3,7},{4,0},{5,1},{6,2},{7,3},{8,12},{9,13},{10,... | collective-permute-start | bytes 393224 | tf_op jit(solution)/shard_map/ppermute | solution.py:22
  15.1 3.4 %load.3 = (bf16[4,768,1024]{2,1,0:T(8,128)(2,1)S(1)}, f32[1,1024]{1,0:T(1,128)S(1)}, s32[1,128]{1,0:T(1,128)}) custom-call(s32[1]{0:T(128)S(6)} %copy.27.length_ref, bf16[768,8192]{1,0:T(8,128)(2,1)} %tokens_ref.3, f32[1,1024]{1,0:T(1,128)} %bitcast.7), custom_call_target="tpu_custom_call" | custom-call | tf_op jit(solution)/shard_map/load/pallas_call | solution.py:130
  18.7 1.9 %collective-permute-done.3.refs_0_ = bf16[4,16,1024]{2,1,0:T(8,128)(2,1)S(1)} collective-permute-done((bf16[4,16,1024]{2,1,0:T(8,128)(2,1)S(1)}, bf16[4,16,1024]{2,1,0:T(8,128)(2,1)S(1)}, u32[]{:S(2)}, u32[]{:S(2)}) %collective-permute-start.3) | collective-permute-done | bytes 131104 | tf_op jit(solution)/shard_map/ppermute | solution.py:22
  21.9 2.0 %project.2.refs_4_ = f32[64,768]{1,0:T(8,128)S(1)} custom-call(bf16[4,16,1024]{2,1,0:T(8,128)(2,1)S(1)} %stack.2.refs_0_, bf16[4,16,1024]{2,1,0:T(8,128)(2,1)S(1)} %get-tuple-element.62.refs_1_, bf16[4,16,1024]{2,1,0:T(8,128)(2,1)S(1)} %collective-permute-done.8.refs_2_, bf16[4,16,1024]{2,1,0:T(8,128)(2,1)S(1)} %collective-permute-done.9.refs_3_, ...), custom_call_target="tpu_custom_call" | custom-call | flops 1610612736 | tf_op jit(solution)/shard_map/project/pallas_call | solution.py:45
  23.9 4.2 %pool.1 = (f32[4,32,1024]{2,1,0:T(8,128)S(1)}, bf16[4,32,1152]{2,1,0:T(8,128)(2,1)S(1)}, f32[64,128]{1,0:T(8,128)S(1)}, f32[64,768]{1,0:T(8,128)S(1)}, bf16[64,768]{1,0:T(8,128)(2,1)S(1)}) custom-call(s32[1,128]{1,0:T(1,128)S(1)} %get-tuple-element.57.length_ref, bf16[4,16,1024]{2,1,0:T(8,128)(2,1)S(1)} %get-tuple-element.60.refs_0_, ...), custom_call_target="tpu_custom_call" | custom-call | flops 1610612736 | tf_op jit(solution)/shard_map/pool/pallas_call | solution.py:45
  28.4 1.2 %pool_rest.1 = (f32[4,32,1024]{2,1,0:T(8,128)S(1)}, bf16[4,32,1152]{2,1,0:T(8,128)(2,1)S(1)}) custom-call(bf16[64,768]{1,0:T(8,128)(2,1)S(1)} %get-tuple-element.65.left_ref, f32[64,128]{1,0:T(8,128)S(1)} %get-tuple-element.66.peak_ref.refs_2_.refs_7_, bf16[4,768,1024]{2,1,0:T(8,128)(2,1)S(1)} %get-tuple-element.63.refs_4_.held_ref), custom_call_target="tpu_custom_call" | custom-call | flops 1610612736 | tf_op jit(solution)/shard_map/pool_rest/pallas_call | solution.py:45
  30.9 1.5 %collective-permute-start.13 = (bf16[4,16,1152]{2,1,0:T(8,128)(2,1)S(1)}, bf16[4,16,1152]{2,1,0:T(8,128)(2,1)S(1)}, u32[]{:S(2)}, u32[]{:S(2)}) collective-permute-start(bf16[4,16,1152]{2,1,0:T(8,128)(2,1)S(1)} %get-tuple-element.74), channel_id=1, source_target_pairs={{0,6},{1,7},{2,4},{3,5},{4,2},{5,3},{6,0},{7,1},{8,14},{9,15},{10,... | collective-permute-start | bytes 442376 | tf_op jit(solution)/shard_map/ppermute | solution.py:22
  32.7 1.5 %collective-permute-start.14 = (bf16[4,16,1152]{2,1,0:T(8,128)(2,1)S(1)}, bf16[4,16,1152]{2,1,0:T(8,128)(2,1)S(1)}, u32[]{:S(2)}, u32[]{:S(2)}) collective-permute-start(bf16[4,16,1152]{2,1,0:T(8,128)(2,1)S(1)} %get-tuple-element.75), channel_id=1, source_target_pairs={{0,2},{1,3},{2,0},{3,1},{4,6},{5,7},{6,4},{7,5},{8,10},{9,11},{10,... | collective-permute-start | bytes 442376 | tf_op jit(solution)/shard_map/ppermute | solution.py:22
  34.2 2.8 %collective-permute-done.12.refs_1_ = bf16[4,16,1152]{2,1,0:T(8,128)(2,1)S(1)} collective-permute-done((bf16[4,16,1152]{2,1,0:T(8,128)(2,1)S(1)}, bf16[4,16,1152]{2,1,0:T(8,128)(2,1)S(1)}, u32[]{:S(2)}, u32[]{:S(2)}) %collective-permute-start.12) | collective-permute-done | bytes 147488 | tf_op jit(solution)/shard_map/ppermute | solution.py:22
  37.0 2.8 %collective-permute-done.13.refs_2_ = bf16[4,16,1152]{2,1,0:T(8,128)(2,1)S(1)} collective-permute-done((bf16[4,16,1152]{2,1,0:T(8,128)(2,1)S(1)}, bf16[4,16,1152]{2,1,0:T(8,128)(2,1)S(1)}, u32[]{:S(2)}, u32[]{:S(2)}) %collective-permute-start.13) | collective-permute-done | bytes 147488 | tf_op jit(solution)/shard_map/ppermute | solution.py:22
  39.8 1.7 %collective-permute-done.14.refs_3_ = bf16[4,16,1152]{2,1,0:T(8,128)(2,1)S(1)} collective-permute-done((bf16[4,16,1152]{2,1,0:T(8,128)(2,1)S(1)}, bf16[4,16,1152]{2,1,0:T(8,128)(2,1)S(1)}, u32[]{:S(2)}, u32[]{:S(2)}) %collective-permute-start.14) | collective-permute-done | bytes 147488 | tf_op jit(solution)/shard_map/ppermute | solution.py:22
  41.8 1.8 %collective-permute-start.15 = (bf16[1,16,1152]{2,1,0:T(8,128)(2,1)S(1)}, bf16[1,16,1152]{2,1,0:T(8,128)(2,1)S(1)}, u32[]{:S(2)}, u32[]{:S(2)}) collective-permute-start(bf16[1,16,1152]{2,1,0:T(8,128)(2,1)S(1)} %get-tuple-element.78), channel_id=1, source_target_pairs={{0,24},{1,25},{2,26},{3,27},{4,28},{5,29},{6,30},{7,31},{8,16},{9,... | collective-permute-start | bytes 110600 | tf_op jit(solution)/shard_map/ppermute | solution.py:22
  44.0 2.3 %collective-permute-start.17 = (bf16[1,16,1152]{2,1,0:T(8,128)(2,1)S(1)}, bf16[1,16,1152]{2,1,0:T(8,128)(2,1)S(1)}, u32[]{:S(2)}, u32[]{:S(2)}) collective-permute-start(bf16[1,16,1152]{2,1,0:T(8,128)(2,1)S(1)} %get-tuple-element.80), channel_id=1, source_target_pairs={{0,8},{1,9},{2,10},{3,11},{4,12},{5,13},{6,14},{7,15},{8,0},{9,1},... | collective-permute-start | bytes 110600 | tf_op jit(solution)/shard_map/ppermute | solution.py:22
  46.3 1.6 %collective-permute-done.15.refs_1_ = bf16[1,16,1152]{2,1,0:T(8,128)(2,1)S(1)} collective-permute-done((bf16[1,16,1152]{2,1,0:T(8,128)(2,1)S(1)}, bf16[1,16,1152]{2,1,0:T(8,128)(2,1)S(1)}, u32[]{:S(2)}, u32[]{:S(2)}) %collective-permute-start.15) | collective-permute-done | bytes 36896 | tf_op jit(solution)/shard_map/ppermute | solution.py:22
  49.3 2.1 %collective-permute-start.20 = (f32[2,1024]{1,0:T(2,128)S(1)}, f32[2,1024]{1,0:T(2,128)S(1)}, u32[]{:S(2)}, u32[]{:S(2)}) collective-permute-start(f32[2,1024]{1,0:T(2,128)S(1)} %get-tuple-element.82.refs_0_), channel_id=1, source_target_pairs={{0,24},{1,25},{2,26},{3,27},{4,28},{5,29},{6,30},{7,31},{8,16},{9,... | collective-permute-start | bytes 24584 | tf_op jit(solution)/shard_map/ppermute | solution.py:22
  51.4 1.0 collective-permute-start.19
  52.4 1.4 %collective-permute-start.18 = (f32[2,1024]{1,0:T(2,128)S(1)}, f32[2,1024]{1,0:T(2,128)S(1)}, u32[]{:S(2)}, u32[]{:S(2)}) collective-permute-start(f32[2,1024]{1,0:T(2,128)S(1)} %get-tuple-element.82.refs_0_), channel_id=1, source_target_pairs={{0,8},{1,9},{2,10},{3,11},{4,12},{5,13},{6,14},{7,15},{8,0},{9,1},... | collective-permute-start | bytes 24584 | tf_op jit(solution)/shard_map/ppermute | solution.py:22
  53.8 1.1 %collective-permute-done.20.refs_3_ = f32[2,1024]{1,0:T(2,128)S(1)} collective-permute-done((f32[2,1024]{1,0:T(2,128)S(1)}, f32[2,1024]{1,0:T(2,128)S(1)}, u32[]{:S(2)}, u32[]{:S(2)}) %collective-permute-start.20) | collective-permute-done | bytes 8224 | tf_op jit(solution)/shard_map/ppermute | solution.py:22
  54.9 1.1 %collective-permute-done.19.refs_2_ = f32[2,1024]{1,0:T(2,128)S(1)} collective-permute-done((f32[2,1024]{1,0:T(2,128)S(1)}, f32[2,1024]{1,0:T(2,128)S(1)}, u32[]{:S(2)}, u32[]{:S(2)}) %collective-permute-start.19) | collective-permute-done | bytes 8224 | tf_op jit(solution)/shard_map/ppermute | solution.py:22
  56.1 1.5 %collective-permute-start.21 = (f32[2,1024]{1,0:T(2,128)S(1)}, f32[2,1024]{1,0:T(2,128)S(1)}, u32[]{:S(2)}, u32[]{:S(2)}) collective-permute-start(f32[2,1024]{1,0:T(2,128)S(1)} %tree_sum.1.sums_ref), channel_id=1, source_target_pairs={{0,4},{1,5},{2,6},{3,7},{4,0},{5,1},{6,2},{7,3},{8,12},{9,13},{10,... | collective-permute-start | bytes 24584 | tf_op jit(solution)/shard_map/ppermute | solution.py:22
  57.6 2.2 %collective-permute-done.21.other_sums_ref = f32[2,1024]{1,0:T(2,128)S(1)} collective-permute-done((f32[2,1024]{1,0:T(2,128)S(1)}, f32[2,1024]{1,0:T(2,128)S(1)}, u32[]{:S(2)}, u32[]{:S(2)}) %collective-permute-start.21) | collective-permute-done | bytes 8224 | tf_op jit(solution)/shard_map/ppermute | solution.py:22
  59.7 1.2 %head_grads.1 = (f32[1,1024]{1,0:T(1,128)}, f32[1,1024]{1,0:T(1,128)S(1)}, bf16[16,1152]{1,0:T(8,128)(2,1)S(1)}, f32[16,1024]{1,0:T(8,128)S(1)}) custom-call(f32[2,1024]{1,0:T(2,128)S(1)} %tree_sum.1.sums_ref, f32[2,1024]{1,0:T(2,128)S(1)} %collective-permute-done.21.other_sums_ref, f32[16,1024]{1,0:T(8,128)S(1)} %get-tuple-element.83.refs_0_, ...), custom_call_target="tpu_custom_call" | custom-call | tf_op jit(solution)/shard_map/head_grads/pallas_call | solution.py:45
  60.9 1.8 %collective-permute-start.24 = (bf16[16,1152]{1,0:T(8,128)(2,1)S(1)}, bf16[16,1152]{1,0:T(8,128)(2,1)S(1)}, u32[]{:S(2)}, u32[]{:S(2)}) collective-permute-start(bf16[16,1152]{1,0:T(8,128)(2,1)S(1)} %get-tuple-element.85.refs_0_), channel_id=1, source_target_pairs={{0,24},{1,25},{2,26},{3,27},{4,28},{5,29},{6,30},{7,31},{8,16},{9,... | collective-permute-start | bytes 110600 | tf_op jit(solution)/shard_map/ppermute | solution.py:22
  62.8 1.0 collective-permute-start.23
  63.8 1.5 %collective-permute-start.22 = (bf16[16,1152]{1,0:T(8,128)(2,1)S(1)}, bf16[16,1152]{1,0:T(8,128)(2,1)S(1)}, u32[]{:S(2)}, u32[]{:S(2)}) collective-permute-start(bf16[16,1152]{1,0:T(8,128)(2,1)S(1)} %get-tuple-element.85.refs_0_), channel_id=1, source_target_pairs={{0,8},{1,9},{2,10},{3,11},{4,12},{5,13},{6,14},{7,15},{8,0},{9,1},... | collective-permute-start | bytes 110600 | tf_op jit(solution)/shard_map/ppermute | solution.py:22
  65.3 1.4 %collective-permute-done.24.refs_3_ = bf16[16,1152]{1,0:T(8,128)(2,1)S(1)} collective-permute-done((bf16[16,1152]{1,0:T(8,128)(2,1)S(1)}, bf16[16,1152]{1,0:T(8,128)(2,1)S(1)}, u32[]{:S(2)}, u32[]{:S(2)}) %collective-permute-start.24) | collective-permute-done | bytes 36896 | tf_op jit(solution)/shard_map/ppermute | solution.py:22
  66.7 1.3 %collective-permute-done.23.refs_2_ = bf16[16,1152]{1,0:T(8,128)(2,1)S(1)} collective-permute-done((bf16[16,1152]{1,0:T(8,128)(2,1)S(1)}, bf16[16,1152]{1,0:T(8,128)(2,1)S(1)}, u32[]{:S(2)}, u32[]{:S(2)}) %collective-permute-start.23) | collective-permute-done | bytes 36896 | tf_op jit(solution)/shard_map/ppermute | solution.py:22
  68.0 1.3 %collective-permute-start.27 = (bf16[4,16,1152]{2,1,0:T(8,128)(2,1)S(1)}, bf16[4,16,1152]{2,1,0:T(8,128)(2,1)S(1)}, u32[]{:S(2)}, u32[]{:S(2)}) collective-permute-start(bf16[4,16,1152]{2,1,0:T(8,128)(2,1)S(1)} %stack.3.refs_0_), channel_id=1, source_target_pairs={{0,2},{1,3},{2,0},{3,1},{4,6},{5,7},{6,4},{7,5},{8,10},{9,11},{10,... | collective-permute-start | bytes 442376 | tf_op jit(solution)/shard_map/ppermute | solution.py:22
  70.1 1.5 %collective-permute-start.25 = (bf16[4,16,1152]{2,1,0:T(8,128)(2,1)S(1)}, bf16[4,16,1152]{2,1,0:T(8,128)(2,1)S(1)}, u32[]{:S(2)}, u32[]{:S(2)}) collective-permute-start(bf16[4,16,1152]{2,1,0:T(8,128)(2,1)S(1)} %stack.3.refs_0_), channel_id=1, source_target_pairs={{0,6},{1,7},{2,4},{3,5},{4,2},{5,3},{6,0},{7,1},{8,14},{9,15},{10,... | collective-permute-start | bytes 442376 | tf_op jit(solution)/shard_map/ppermute | solution.py:22
  71.6 3.0 %head_weight_grad.1 = (f32[1024,1024]{1,0:T(8,128)}, f32[8,128]{1,0:T(8,128)S(1)}) custom-call(f32[16,1024]{1,0:T(8,128)S(1)} %get-tuple-element.86.normed_ref, f32[1,1024]{1,0:T(1,128)S(1)} %get-tuple-element.87.bias_grad_ref), custom_call_target="tpu_custom_call" | custom-call | tf_op jit(solution)/shard_map/head_weight_grad/pallas_call | solution.py:378
  74.5 1.7 %collective-permute-done.25.refs_0_ = bf16[4,16,1152]{2,1,0:T(8,128)(2,1)S(1)} collective-permute-done((bf16[4,16,1152]{2,1,0:T(8,128)(2,1)S(1)}, bf16[4,16,1152]{2,1,0:T(8,128)(2,1)S(1)}, u32[]{:S(2)}, u32[]{:S(2)}) %collective-permute-start.25) | collective-permute-done | bytes 147488 | tf_op jit(solution)/shard_map/ppermute | solution.py:22
  77.7 2.0 %project.3.refs_4_ = f32[64,768]{1,0:T(8,128)S(1)} custom-call(bf16[4,16,1152]{2,1,0:T(8,128)(2,1)S(1)} %stack.3.refs_0_, bf16[4,16,1152]{2,1,0:T(8,128)(2,1)S(1)} %get-tuple-element.91.refs_1_, bf16[4,16,1152]{2,1,0:T(8,128)(2,1)S(1)} %collective-permute-done.30.refs_2_, bf16[4,16,1152]{2,1,0:T(8,128)(2,1)S(1)} %collective-permute-done.31.refs_3_, ...), custom_call_target="tpu_custom_call" | custom-call | flops 1610612736 | tf_op jit(solution)/shard_map/project/pallas_call | solution.py:45
  79.7 4.0 %grad.1 = (f32[4,32,1024]{2,1,0:T(8,128)S(1)}, bf16[4,32,1024]{2,1,0:T(8,128)(2,1)S(1)}, bf16[64,768]{1,0:T(8,128)(2,1)S(1)}, f32[1,1]{1,0:T(1,128)}) custom-call(bf16[4,16,1152]{2,1,0:T(8,128)(2,1)S(1)} %get-tuple-element.89.refs_0_, bf16[4,16,1152]{2,1,0:T(8,128)(2,1)S(1)} %get-tuple-element.90.refs_1_, ...), custom_call_target="tpu_custom_call" | custom-call | flops 1610612736 | tf_op jit(solution)/shard_map/grad/pallas_call | solution.py:45
  83.9 1.2 %grad_rest.1 = (f32[4,32,1024]{2,1,0:T(8,128)S(1)}, bf16[4,32,1024]{2,1,0:T(8,128)(2,1)S(1)}) custom-call(bf16[64,768]{1,0:T(8,128)(2,1)S(1)} %get-tuple-element.94.left_ref, bf16[4,768,1024]{2,1,0:T(8,128)(2,1)S(1)} %get-tuple-element.63.refs_4_.held_ref), custom_call_target="tpu_custom_call" | custom-call | flops 1610612736 | tf_op jit(solution)/shard_map/grad_rest/pallas_call | solution.py:45
  85.6 1.5 %collective-permute-start.34 = (bf16[4,16,1024]{2,1,0:T(8,128)(2,1)S(1)}, bf16[4,16,1024]{2,1,0:T(8,128)(2,1)S(1)}, u32[]{:S(2)}, u32[]{:S(2)}) collective-permute-start(bf16[4,16,1024]{2,1,0:T(8,128)(2,1)S(1)} %get-tuple-element.101), channel_id=1, source_target_pairs={{0,4},{1,5},{2,6},{3,7},{4,0},{5,1},{6,2},{7,3},{8,12},{9,13},{10,... | collective-permute-start | bytes 393224 | tf_op jit(solution)/shard_map/ppermute | solution.py:22
  87.1 1.3 %collective-permute-start.35 = (bf16[4,16,1024]{2,1,0:T(8,128)(2,1)S(1)}, bf16[4,16,1024]{2,1,0:T(8,128)(2,1)S(1)}, u32[]{:S(2)}, u32[]{:S(2)}) collective-permute-start(bf16[4,16,1024]{2,1,0:T(8,128)(2,1)S(1)} %get-tuple-element.102), channel_id=1, source_target_pairs={{0,6},{1,7},{2,4},{3,5},{4,2},{5,3},{6,0},{7,1},{8,14},{9,15},{10,... | collective-permute-start | bytes 393224 | tf_op jit(solution)/shard_map/ppermute | solution.py:22
  89.2 2.7 %collective-permute-done.34.refs_1_ = bf16[4,16,1024]{2,1,0:T(8,128)(2,1)S(1)} collective-permute-done((bf16[4,16,1024]{2,1,0:T(8,128)(2,1)S(1)}, bf16[4,16,1024]{2,1,0:T(8,128)(2,1)S(1)}, u32[]{:S(2)}, u32[]{:S(2)}) %collective-permute-start.34) | collective-permute-done | bytes 131104 | tf_op jit(solution)/shard_map/ppermute | solution.py:22
  92.0 3.1 %collective-permute-done.35.refs_2_ = bf16[4,16,1024]{2,1,0:T(8,128)(2,1)S(1)} collective-permute-done((bf16[4,16,1024]{2,1,0:T(8,128)(2,1)S(1)}, bf16[4,16,1024]{2,1,0:T(8,128)(2,1)S(1)}, u32[]{:S(2)}, u32[]{:S(2)}) %collective-permute-start.35) | collective-permute-done | bytes 131104 | tf_op jit(solution)/shard_map/ppermute | solution.py:22
  95.1 1.5 %collective-permute-done.36.refs_3_ = bf16[4,16,1024]{2,1,0:T(8,128)(2,1)S(1)} collective-permute-done((bf16[4,16,1024]{2,1,0:T(8,128)(2,1)S(1)}, bf16[4,16,1024]{2,1,0:T(8,128)(2,1)S(1)}, u32[]{:S(2)}, u32[]{:S(2)}) %collective-permute-start.36) | collective-permute-done | bytes 131104 | tf_op jit(solution)/shard_map/ppermute | solution.py:22
  96.6 2.2 %collective-permute-start.37 = (bf16[1,16,1024]{2,1,0:T(8,128)(2,1)S(1)}, bf16[1,16,1024]{2,1,0:T(8,128)(2,1)S(1)}, u32[]{:S(2)}, u32[]{:S(2)}) collective-permute-start(bf16[1,16,1024]{2,1,0:T(8,128)(2,1)S(1)} %get-tuple-element.105), channel_id=1, source_target_pairs={{0,24},{1,25},{2,26},{3,27},{4,28},{5,29},{6,30},{7,31},{8,16},{9,... | collective-permute-start | bytes 98312 | tf_op jit(solution)/shard_map/ppermute | solution.py:22
  99.4 1.6 %collective-permute-start.39 = (bf16[1,16,1024]{2,1,0:T(8,128)(2,1)S(1)}, bf16[1,16,1024]{2,1,0:T(8,128)(2,1)S(1)}, u32[]{:S(2)}, u32[]{:S(2)}) collective-permute-start(bf16[1,16,1024]{2,1,0:T(8,128)(2,1)S(1)} %get-tuple-element.107), channel_id=1, source_target_pairs={{0,8},{1,9},{2,10},{3,11},{4,12},{5,13},{6,14},{7,15},{8,0},{9,1},... | collective-permute-start | bytes 98312 | tf_op jit(solution)/shard_map/ppermute | solution.py:22
  101.1 1.3 %collective-permute-done.37.refs_1_ = bf16[1,16,1024]{2,1,0:T(8,128)(2,1)S(1)} collective-permute-done((bf16[1,16,1024]{2,1,0:T(8,128)(2,1)S(1)}, bf16[1,16,1024]{2,1,0:T(8,128)(2,1)S(1)}, u32[]{:S(2)}, u32[]{:S(2)}) %collective-permute-start.37) | collective-permute-done | bytes 32800 | tf_op jit(solution)/shard_map/ppermute | solution.py:22
  102.4 1.3 %collective-permute-done.38.refs_2_ = bf16[1,16,1024]{2,1,0:T(8,128)(2,1)S(1)} collective-permute-done((bf16[1,16,1024]{2,1,0:T(8,128)(2,1)S(1)}, bf16[1,16,1024]{2,1,0:T(8,128)(2,1)S(1)}, u32[]{:S(2)}, u32[]{:S(2)}) %collective-permute-start.38) | collective-permute-done | bytes 32800 | tf_op jit(solution)/shard_map/ppermute | solution.py:22
  (61 shorter events, 11.2 us)
Async XLA Ops:
  0.6 9.3 %collective-permute-start = (bf16[16,1024]{1,0:T(8,128)(2,1)}, bf16[16,1024]{1,0:T(8,128)(2,1)S(1)}, u32[]{:S(2)}, u32[]{:S(2)}) collective-permute-start(bf16[16,1024]{1,0:T(8,128)(2,1)} %refs_0_.1), channel_id=1, source_target_pairs={{0,8},{1,9},{2,10},{3,11},{4,12},{5,13},{6,14},{7,15},{8,0},{9,1},... | collective-permute-start | bytes 98312 | tf_op jit(solution)/shard_map/ppermute | solution.py:22
  3.7 6.4 %collective-permute-start.2 = (bf16[16,1024]{1,0:T(8,128)(2,1)}, bf16[16,1024]{1,0:T(8,128)(2,1)S(1)}, u32[]{:S(2)}, u32[]{:S(2)}) collective-permute-start(bf16[16,1024]{1,0:T(8,128)(2,1)} %refs_0_.1), channel_id=1, source_target_pairs={{0,24},{1,25},{2,26},{3,27},{4,28},{5,29},{6,30},{7,31},{8,16},{9,... | collective-permute-start | bytes 98312 | tf_op jit(solution)/shard_map/ppermute | solution.py:22
  6.2 5.4 %collective-permute-start.1 = (bf16[16,1024]{1,0:T(8,128)(2,1)}, bf16[16,1024]{1,0:T(8,128)(2,1)S(1)}, u32[]{:S(2)}, u32[]{:S(2)}) collective-permute-start(bf16[16,1024]{1,0:T(8,128)(2,1)} %refs_0_.1), channel_id=1, source_target_pairs={{0,16},{1,17},{2,18},{3,19},{4,20},{5,21},{6,22},{7,23},{8,24},{9,... | collective-permute-start | bytes 98312 | tf_op jit(solution)/shard_map/ppermute | solution.py:22
  11.6 7.1 %collective-permute-start.5 = (bf16[4,16,1024]{2,1,0:T(8,128)(2,1)S(1)}, bf16[4,16,1024]{2,1,0:T(8,128)(2,1)S(1)}, u32[]{:S(2)}, u32[]{:S(2)}) collective-permute-start(bf16[4,16,1024]{2,1,0:T(8,128)(2,1)S(1)} %stack.2.refs_0_), channel_id=1, source_target_pairs={{0,2},{1,3},{2,0},{3,1},{4,6},{5,7},{6,4},{7,5},{8,10},{9,11},{10,... | collective-permute-start | bytes 393224 | tf_op jit(solution)/shard_map/ppermute | solution.py:22
  13.2 5.5 %collective-permute-start.4 = (bf16[4,16,1024]{2,1,0:T(8,128)(2,1)S(1)}, bf16[4,16,1024]{2,1,0:T(8,128)(2,1)S(1)}, u32[]{:S(2)}, u32[]{:S(2)}) collective-permute-start(bf16[4,16,1024]{2,1,0:T(8,128)(2,1)S(1)} %stack.2.refs_0_), channel_id=1, source_target_pairs={{0,4},{1,5},{2,6},{3,7},{4,0},{5,1},{6,2},{7,3},{8,12},{9,13},{10,... | collective-permute-start | bytes 393224 | tf_op jit(solution)/shard_map/ppermute | solution.py:22
  14.7 5.9 %collective-permute-start.3 = (bf16[4,16,1024]{2,1,0:T(8,128)(2,1)S(1)}, bf16[4,16,1024]{2,1,0:T(8,128)(2,1)S(1)}, u32[]{:S(2)}, u32[]{:S(2)}) collective-permute-start(bf16[4,16,1024]{2,1,0:T(8,128)(2,1)S(1)} %stack.2.refs_0_), channel_id=1, source_target_pairs={{0,6},{1,7},{2,4},{3,5},{4,2},{5,3},{6,0},{7,1},{8,14},{9,15},{10,... | collective-permute-start | bytes 393224 | tf_op jit(solution)/shard_map/ppermute | solution.py:22
  18.6 2.5 %collective-permute-start.8 = (bf16[4,16,1024]{2,1,0:T(8,128)(2,1)S(1)}, bf16[4,16,1024]{2,1,0:T(8,128)(2,1)S(1)}, u32[]{:S(2)}, u32[]{:S(2)}) collective-permute-start(bf16[4,16,1024]{2,1,0:T(8,128)(2,1)S(1)} %stack.2.refs_0_), channel_id=1, source_target_pairs={{0,1},{1,0},{2,3},{3,2},{4,5},{5,4},{6,7},{7,6},{8,9},{9,8},{10,11... | collective-permute-start | bytes 393224 | tf_op jit(solution)/shard_map/ppermute | solution.py:22
  20.5 1.3 %collective-permute-start.9 = (bf16[4,16,1024]{2,1,0:T(8,128)(2,1)S(1)}, bf16[4,16,1024]{2,1,0:T(8,128)(2,1)S(1)}, u32[]{:S(2)}, u32[]{:S(2)}) collective-permute-start(bf16[4,16,1024]{2,1,0:T(8,128)(2,1)S(1)} %get-tuple-element.62.refs_1_), channel_id=1, source_target_pairs={{0,1},{1,0},{2,3},{3,2},{4,5},{5,4},{6,7},{7,6},{8,9},{9,8},{10,11... | collective-permute-start | bytes 393224 | tf_op jit(solution)/shard_map/ppermute | solution.py:22
  20.5 3.4 %collective-permute-start.6 = (bf16[4,16,1024]{2,1,0:T(8,128)(2,1)S(1)}, bf16[4,16,1024]{2,1,0:T(8,128)(2,1)S(1)}, u32[]{:S(2)}, u32[]{:S(2)}) collective-permute-start(bf16[4,16,1024]{2,1,0:T(8,128)(2,1)S(1)} %get-tuple-element.60.refs_0_), channel_id=1, source_target_pairs={{0,1},{1,0},{2,3},{3,2},{4,5},{5,4},{6,7},{7,6},{8,9},{9,8},{10,11... | collective-permute-start | bytes 393224 | tf_op jit(solution)/shard_map/ppermute | solution.py:22
  21.0 2.9 %collective-permute-start.7 = (bf16[4,16,1024]{2,1,0:T(8,128)(2,1)S(1)}, bf16[4,16,1024]{2,1,0:T(8,128)(2,1)S(1)}, u32[]{:S(2)}, u32[]{:S(2)}) collective-permute-start(bf16[4,16,1024]{2,1,0:T(8,128)(2,1)S(1)} %get-tuple-element.61.refs_1_), channel_id=1, source_target_pairs={{0,1},{1,0},{2,3},{3,2},{4,5},{5,4},{6,7},{7,6},{8,9},{9,8},{10,11... | collective-permute-start | bytes 393224 | tf_op jit(solution)/shard_map/ppermute | solution.py:22
  28.1 20.6 %copy-start = (bf16[1024,1024]{1,0:T(8,128)(2,1)S(1)}, bf16[1024,1024]{1,0:T(8,128)(2,1)}, u32[]{:S(2)}) copy-start(bf16[1024,1024]{1,0:T(8,128)(2,1)} %refs_3_.1) | copy-start | bytes 6291460
  28.1 31.6 %copy-start.1 = (f32[1024]{0:T(1024)S(1)}, f32[1024]{0:T(1024)}, u32[]{:S(2)}) copy-start(f32[1024]{0:T(1024)} %param.12) | copy-start | bytes 12292
  28.1 31.6 %copy-start.2 = (s32[1024]{0:T(1024)S(1)}, s32[1024]{0:T(1024)}, u32[]{:S(2)}) copy-start(s32[1024]{0:T(1024)} %param.13) | copy-start | bytes 12292
  28.1 1.6 %collective-permute-start.10 = (bf16[4,32,1152]{2,1,0:T(8,128)(2,1)S(1)}, bf16[4,32,1152]{2,1,0:T(8,128)(2,1)S(1)}, u32[]{:S(2)}, u32[]{:S(2)}) collective-permute-start(bf16[4,32,1152]{2,1,0:T(8,128)(2,1)S(1)} %get-tuple-element.69), channel_id=1, source_target_pairs={{0,1},{1,0},{2,3},{3,2},{4,5},{5,4},{6,7},{7,6},{8,9},{9,8},{10,11... | collective-permute-start | bytes 884744 | tf_op jit(solution)/shard_map/ppermute | solution.py:22
  30.1 2.3 %collective-permute-start.11 = (bf16[4,32,1152]{2,1,0:T(8,128)(2,1)S(1)}, bf16[4,32,1152]{2,1,0:T(8,128)(2,1)S(1)}, u32[]{:S(2)}, u32[]{:S(2)}) collective-permute-start(bf16[4,32,1152]{2,1,0:T(8,128)(2,1)S(1)} %get-tuple-element.71), channel_id=1, source_target_pairs={{0,1},{1,0},{2,3},{3,2},{4,5},{5,4},{6,7},{7,6},{8,9},{9,8},{10,11... | collective-permute-start | bytes 884744 | tf_op jit(solution)/shard_map/ppermute | solution.py:22
  30.3 6.7 %collective-permute-start.12 = (bf16[4,16,1152]{2,1,0:T(8,128)(2,1)S(1)}, bf16[4,16,1152]{2,1,0:T(8,128)(2,1)S(1)}, u32[]{:S(2)}, u32[]{:S(2)}) collective-permute-start(bf16[4,16,1152]{2,1,0:T(8,128)(2,1)S(1)} %get-tuple-element.73), channel_id=1, source_target_pairs={{0,4},{1,5},{2,6},{3,7},{4,0},{5,1},{6,2},{7,3},{8,12},{9,13},{10,... | collective-permute-start | bytes 442376 | tf_op jit(solution)/shard_map/ppermute | solution.py:22
  30.9 8.8 %collective-permute-start.13 = (bf16[4,16,1152]{2,1,0:T(8,128)(2,1)S(1)}, bf16[4,16,1152]{2,1,0:T(8,128)(2,1)S(1)}, u32[]{:S(2)}, u32[]{:S(2)}) collective-permute-start(bf16[4,16,1152]{2,1,0:T(8,128)(2,1)S(1)} %get-tuple-element.74), channel_id=1, source_target_pairs={{0,6},{1,7},{2,4},{3,5},{4,2},{5,3},{6,0},{7,1},{8,14},{9,15},{10,... | collective-permute-start | bytes 442376 | tf_op jit(solution)/shard_map/ppermute | solution.py:22
  32.7 8.8 %collective-permute-start.14 = (bf16[4,16,1152]{2,1,0:T(8,128)(2,1)S(1)}, bf16[4,16,1152]{2,1,0:T(8,128)(2,1)S(1)}, u32[]{:S(2)}, u32[]{:S(2)}) collective-permute-start(bf16[4,16,1152]{2,1,0:T(8,128)(2,1)S(1)} %get-tuple-element.75), channel_id=1, source_target_pairs={{0,2},{1,3},{2,0},{3,1},{4,6},{5,7},{6,4},{7,5},{8,10},{9,11},{10,... | collective-permute-start | bytes 442376 | tf_op jit(solution)/shard_map/ppermute | solution.py:22
  41.8 6.1 %collective-permute-start.15 = (bf16[1,16,1152]{2,1,0:T(8,128)(2,1)S(1)}, bf16[1,16,1152]{2,1,0:T(8,128)(2,1)S(1)}, u32[]{:S(2)}, u32[]{:S(2)}) collective-permute-start(bf16[1,16,1152]{2,1,0:T(8,128)(2,1)S(1)} %get-tuple-element.78), channel_id=1, source_target_pairs={{0,24},{1,25},{2,26},{3,27},{4,28},{5,29},{6,30},{7,31},{8,16},{9,... | collective-permute-start | bytes 110600 | tf_op jit(solution)/shard_map/ppermute | solution.py:22
  43.6 5.1 %collective-permute-start.16 = (bf16[1,16,1152]{2,1,0:T(8,128)(2,1)S(1)}, bf16[1,16,1152]{2,1,0:T(8,128)(2,1)S(1)}, u32[]{:S(2)}, u32[]{:S(2)}) collective-permute-start(bf16[1,16,1152]{2,1,0:T(8,128)(2,1)S(1)} %get-tuple-element.79), channel_id=1, source_target_pairs={{0,16},{1,17},{2,18},{3,19},{4,20},{5,21},{6,22},{7,23},{8,24},{9,... | collective-permute-start | bytes 110600 | tf_op jit(solution)/shard_map/ppermute | solution.py:22
  44.0 4.8 %collective-permute-start.17 = (bf16[1,16,1152]{2,1,0:T(8,128)(2,1)S(1)}, bf16[1,16,1152]{2,1,0:T(8,128)(2,1)S(1)}, u32[]{:S(2)}, u32[]{:S(2)}) collective-permute-start(bf16[1,16,1152]{2,1,0:T(8,128)(2,1)S(1)} %get-tuple-element.80), channel_id=1, source_target_pairs={{0,8},{1,9},{2,10},{3,11},{4,12},{5,13},{6,14},{7,15},{8,0},{9,1},... | collective-permute-start | bytes 110600 | tf_op jit(solution)/shard_map/ppermute | solution.py:22
  49.3 5.5 %collective-permute-start.20 = (f32[2,1024]{1,0:T(2,128)S(1)}, f32[2,1024]{1,0:T(2,128)S(1)}, u32[]{:S(2)}, u32[]{:S(2)}) collective-permute-start(f32[2,1024]{1,0:T(2,128)S(1)} %get-tuple-element.82.refs_0_), channel_id=1, source_target_pairs={{0,24},{1,25},{2,26},{3,27},{4,28},{5,29},{6,30},{7,31},{8,16},{9,... | collective-permute-start | bytes 24584 | tf_op jit(solution)/shard_map/ppermute | solution.py:22
  51.4 4.5 %collective-permute-start.19 = (f32[2,1024]{1,0:T(2,128)S(1)}, f32[2,1024]{1,0:T(2,128)S(1)}, u32[]{:S(2)}, u32[]{:S(2)}) collective-permute-start(f32[2,1024]{1,0:T(2,128)S(1)} %get-tuple-element.82.refs_0_), channel_id=1, source_target_pairs={{0,16},{1,17},{2,18},{3,19},{4,20},{5,21},{6,22},{7,23},{8,24},{9,... | collective-permute-start | bytes 24584 | tf_op jit(solution)/shard_map/ppermute | solution.py:22
  52.4 3.7 %collective-permute-start.18 = (f32[2,1024]{1,0:T(2,128)S(1)}, f32[2,1024]{1,0:T(2,128)S(1)}, u32[]{:S(2)}, u32[]{:S(2)}) collective-permute-start(f32[2,1024]{1,0:T(2,128)S(1)} %get-tuple-element.82.refs_0_), channel_id=1, source_target_pairs={{0,8},{1,9},{2,10},{3,11},{4,12},{5,13},{6,14},{7,15},{8,0},{9,1},... | collective-permute-start | bytes 24584 | tf_op jit(solution)/shard_map/ppermute | solution.py:22
  56.1 3.7 %collective-permute-start.21 = (f32[2,1024]{1,0:T(2,128)S(1)}, f32[2,1024]{1,0:T(2,128)S(1)}, u32[]{:S(2)}, u32[]{:S(2)}) collective-permute-start(f32[2,1024]{1,0:T(2,128)S(1)} %tree_sum.1.sums_ref), channel_id=1, source_target_pairs={{0,4},{1,5},{2,6},{3,7},{4,0},{5,1},{6,2},{7,3},{8,12},{9,13},{10,... | collective-permute-start | bytes 24584 | tf_op jit(solution)/shard_map/ppermute | solution.py:22
  60.9 5.8 %collective-permute-start.24 = (bf16[16,1152]{1,0:T(8,128)(2,1)S(1)}, bf16[16,1152]{1,0:T(8,128)(2,1)S(1)}, u32[]{:S(2)}, u32[]{:S(2)}) collective-permute-start(bf16[16,1152]{1,0:T(8,128)(2,1)S(1)} %get-tuple-element.85.refs_0_), channel_id=1, source_target_pairs={{0,24},{1,25},{2,26},{3,27},{4,28},{5,29},{6,30},{7,31},{8,16},{9,... | collective-permute-start | bytes 110600 | tf_op jit(solution)/shard_map/ppermute | solution.py:22
  62.8 5.3 %collective-permute-start.23 = (bf16[16,1152]{1,0:T(8,128)(2,1)S(1)}, bf16[16,1152]{1,0:T(8,128)(2,1)S(1)}, u32[]{:S(2)}, u32[]{:S(2)}) collective-permute-start(bf16[16,1152]{1,0:T(8,128)(2,1)S(1)} %get-tuple-element.85.refs_0_), channel_id=1, source_target_pairs={{0,16},{1,17},{2,18},{3,19},{4,20},{5,21},{6,22},{7,23},{8,24},{9,... | collective-permute-start | bytes 110600 | tf_op jit(solution)/shard_map/ppermute | solution.py:22
  63.8 4.2 %collective-permute-start.22 = (bf16[16,1152]{1,0:T(8,128)(2,1)S(1)}, bf16[16,1152]{1,0:T(8,128)(2,1)S(1)}, u32[]{:S(2)}, u32[]{:S(2)}) collective-permute-start(bf16[16,1152]{1,0:T(8,128)(2,1)S(1)} %get-tuple-element.85.refs_0_), channel_id=1, source_target_pairs={{0,8},{1,9},{2,10},{3,11},{4,12},{5,13},{6,14},{7,15},{8,0},{9,1},... | collective-permute-start | bytes 110600 | tf_op jit(solution)/shard_map/ppermute | solution.py:22
  68.0 6.5 %collective-permute-start.27 = (bf16[4,16,1152]{2,1,0:T(8,128)(2,1)S(1)}, bf16[4,16,1152]{2,1,0:T(8,128)(2,1)S(1)}, u32[]{:S(2)}, u32[]{:S(2)}) collective-permute-start(bf16[4,16,1152]{2,1,0:T(8,128)(2,1)S(1)} %stack.3.refs_0_), channel_id=1, source_target_pairs={{0,2},{1,3},{2,0},{3,1},{4,6},{5,7},{6,4},{7,5},{8,10},{9,11},{10,... | collective-permute-start | bytes 442376 | tf_op jit(solution)/shard_map/ppermute | solution.py:22
  69.4 5.2 %collective-permute-start.26 = (bf16[4,16,1152]{2,1,0:T(8,128)(2,1)S(1)}, bf16[4,16,1152]{2,1,0:T(8,128)(2,1)S(1)}, u32[]{:S(2)}, u32[]{:S(2)}) collective-permute-start(bf16[4,16,1152]{2,1,0:T(8,128)(2,1)S(1)} %stack.3.refs_0_), channel_id=1, source_target_pairs={{0,4},{1,5},{2,6},{3,7},{4,0},{5,1},{6,2},{7,3},{8,12},{9,13},{10,... | collective-permute-start | bytes 442376 | tf_op jit(solution)/shard_map/ppermute | solution.py:22
  70.1 6.2 %collective-permute-start.25 = (bf16[4,16,1152]{2,1,0:T(8,128)(2,1)S(1)}, bf16[4,16,1152]{2,1,0:T(8,128)(2,1)S(1)}, u32[]{:S(2)}, u32[]{:S(2)}) collective-permute-start(bf16[4,16,1152]{2,1,0:T(8,128)(2,1)S(1)} %stack.3.refs_0_), channel_id=1, source_target_pairs={{0,6},{1,7},{2,4},{3,5},{4,2},{5,3},{6,0},{7,1},{8,14},{9,15},{10,... | collective-permute-start | bytes 442376 | tf_op jit(solution)/shard_map/ppermute | solution.py:22
  74.5 2.3 %collective-permute-start.30 = (bf16[4,16,1152]{2,1,0:T(8,128)(2,1)S(1)}, bf16[4,16,1152]{2,1,0:T(8,128)(2,1)S(1)}, u32[]{:S(2)}, u32[]{:S(2)}) collective-permute-start(bf16[4,16,1152]{2,1,0:T(8,128)(2,1)S(1)} %stack.3.refs_0_), channel_id=1, source_target_pairs={{0,1},{1,0},{2,3},{3,2},{4,5},{5,4},{6,7},{7,6},{8,9},{9,8},{10,11... | collective-permute-start | bytes 442376 | tf_op jit(solution)/shard_map/ppermute | solution.py:22
  76.3 1.4 %collective-permute-start.31 = (bf16[4,16,1152]{2,1,0:T(8,128)(2,1)S(1)}, bf16[4,16,1152]{2,1,0:T(8,128)(2,1)S(1)}, u32[]{:S(2)}, u32[]{:S(2)}) collective-permute-start(bf16[4,16,1152]{2,1,0:T(8,128)(2,1)S(1)} %get-tuple-element.91.refs_1_), channel_id=1, source_target_pairs={{0,1},{1,0},{2,3},{3,2},{4,5},{5,4},{6,7},{7,6},{8,9},{9,8},{10,11... | collective-permute-start | bytes 442376 | tf_op jit(solution)/shard_map/ppermute | solution.py:22
  76.3 3.4 %collective-permute-start.28 = (bf16[4,16,1152]{2,1,0:T(8,128)(2,1)S(1)}, bf16[4,16,1152]{2,1,0:T(8,128)(2,1)S(1)}, u32[]{:S(2)}, u32[]{:S(2)}) collective-permute-start(bf16[4,16,1152]{2,1,0:T(8,128)(2,1)S(1)} %get-tuple-element.89.refs_0_), channel_id=1, source_target_pairs={{0,1},{1,0},{2,3},{3,2},{4,5},{5,4},{6,7},{7,6},{8,9},{9,8},{10,11... | collective-permute-start | bytes 442376 | tf_op jit(solution)/shard_map/ppermute | solution.py:22
  76.8 2.9 %collective-permute-start.29 = (bf16[4,16,1152]{2,1,0:T(8,128)(2,1)S(1)}, bf16[4,16,1152]{2,1,0:T(8,128)(2,1)S(1)}, u32[]{:S(2)}, u32[]{:S(2)}) collective-permute-start(bf16[4,16,1152]{2,1,0:T(8,128)(2,1)S(1)} %get-tuple-element.90.refs_1_), channel_id=1, source_target_pairs={{0,1},{1,0},{2,3},{3,2},{4,5},{5,4},{6,7},{7,6},{8,9},{9,8},{10,11... | collective-permute-start | bytes 442376 | tf_op jit(solution)/shard_map/ppermute | solution.py:22
  83.7 1.6 %collective-permute-start.32 = (bf16[4,32,1024]{2,1,0:T(8,128)(2,1)S(1)}, bf16[4,32,1024]{2,1,0:T(8,128)(2,1)S(1)}, u32[]{:S(2)}, u32[]{:S(2)}) collective-permute-start(bf16[4,32,1024]{2,1,0:T(8,128)(2,1)S(1)} %get-tuple-element.97), channel_id=1, source_target_pairs={{0,1},{1,0},{2,3},{3,2},{4,5},{5,4},{6,7},{7,6},{8,9},{9,8},{10,11... | collective-permute-start | bytes 786440 | tf_op jit(solution)/shard_map/ppermute | solution.py:22
  85.4 3.1 %collective-permute-start.33 = (bf16[4,32,1024]{2,1,0:T(8,128)(2,1)S(1)}, bf16[4,32,1024]{2,1,0:T(8,128)(2,1)S(1)}, u32[]{:S(2)}, u32[]{:S(2)}) collective-permute-start(bf16[4,32,1024]{2,1,0:T(8,128)(2,1)S(1)} %get-tuple-element.99), channel_id=1, source_target_pairs={{0,1},{1,0},{2,3},{3,2},{4,5},{5,4},{6,7},{7,6},{8,9},{9,8},{10,11... | collective-permute-start | bytes 786440 | tf_op jit(solution)/shard_map/ppermute | solution.py:22
  85.6 6.3 %collective-permute-start.34 = (bf16[4,16,1024]{2,1,0:T(8,128)(2,1)S(1)}, bf16[4,16,1024]{2,1,0:T(8,128)(2,1)S(1)}, u32[]{:S(2)}, u32[]{:S(2)}) collective-permute-start(bf16[4,16,1024]{2,1,0:T(8,128)(2,1)S(1)} %get-tuple-element.101), channel_id=1, source_target_pairs={{0,4},{1,5},{2,6},{3,7},{4,0},{5,1},{6,2},{7,3},{8,12},{9,13},{10,... | collective-permute-start | bytes 393224 | tf_op jit(solution)/shard_map/ppermute | solution.py:22
  87.1 8.0 %collective-permute-start.35 = (bf16[4,16,1024]{2,1,0:T(8,128)(2,1)S(1)}, bf16[4,16,1024]{2,1,0:T(8,128)(2,1)S(1)}, u32[]{:S(2)}, u32[]{:S(2)}) collective-permute-start(bf16[4,16,1024]{2,1,0:T(8,128)(2,1)S(1)} %get-tuple-element.102), channel_id=1, source_target_pairs={{0,6},{1,7},{2,4},{3,5},{4,2},{5,3},{6,0},{7,1},{8,14},{9,15},{10,... | collective-permute-start | bytes 393224 | tf_op jit(solution)/shard_map/ppermute | solution.py:22
  88.5 8.0 %collective-permute-start.36 = (bf16[4,16,1024]{2,1,0:T(8,128)(2,1)S(1)}, bf16[4,16,1024]{2,1,0:T(8,128)(2,1)S(1)}, u32[]{:S(2)}, u32[]{:S(2)}) collective-permute-start(bf16[4,16,1024]{2,1,0:T(8,128)(2,1)S(1)} %get-tuple-element.103), channel_id=1, source_target_pairs={{0,2},{1,3},{2,0},{3,1},{4,6},{5,7},{6,4},{7,5},{8,10},{9,11},{10,... | collective-permute-start | bytes 393224 | tf_op jit(solution)/shard_map/ppermute | solution.py:22
  96.6 5.8 %collective-permute-start.37 = (bf16[1,16,1024]{2,1,0:T(8,128)(2,1)S(1)}, bf16[1,16,1024]{2,1,0:T(8,128)(2,1)S(1)}, u32[]{:S(2)}, u32[]{:S(2)}) collective-permute-start(bf16[1,16,1024]{2,1,0:T(8,128)(2,1)S(1)} %get-tuple-element.105), channel_id=1, source_target_pairs={{0,24},{1,25},{2,26},{3,27},{4,28},{5,29},{6,30},{7,31},{8,16},{9,... | collective-permute-start | bytes 98312 | tf_op jit(solution)/shard_map/ppermute | solution.py:22
  98.8 4.9 %collective-permute-start.38 = (bf16[1,16,1024]{2,1,0:T(8,128)(2,1)S(1)}, bf16[1,16,1024]{2,1,0:T(8,128)(2,1)S(1)}, u32[]{:S(2)}, u32[]{:S(2)}) collective-permute-start(bf16[1,16,1024]{2,1,0:T(8,128)(2,1)S(1)} %get-tuple-element.106), channel_id=1, source_target_pairs={{0,16},{1,17},{2,18},{3,19},{4,20},{5,21},{6,22},{7,23},{8,24},{9,... | collective-permute-start | bytes 98312 | tf_op jit(solution)/shard_map/ppermute | solution.py:22
  99.4 4.3 %collective-permute-start.39 = (bf16[1,16,1024]{2,1,0:T(8,128)(2,1)S(1)}, bf16[1,16,1024]{2,1,0:T(8,128)(2,1)S(1)}, u32[]{:S(2)}, u32[]{:S(2)}) collective-permute-start(bf16[1,16,1024]{2,1,0:T(8,128)(2,1)S(1)} %get-tuple-element.107), channel_id=1, source_target_pairs={{0,8},{1,9},{2,10},{3,11},{4,12},{5,13},{6,14},{7,15},{8,0},{9,1},... | collective-permute-start | bytes 98312 | tf_op jit(solution)/shard_map/ppermute | solution.py:22

commit v9 on v7

--- a/solution.py
+++ b/solution.py
@@ -176,17 +176,16 @@
 
 
 def grad_kernel(scale, count, *refs):
-    parts, refs = refs[:count], refs[count:]
+    parts, notes, refs = refs[:count], refs[count : 2 * count], refs[2 * count :]
     part_ref, held_ref, w_ref, peak_ref, keep_ref, send_ref, left_ref, loss_ref = refs
-    width = held_ref.shape[2]
     projected = part_ref[...] + project(parts, held_ref)
-    blocks = [ref[0] for ref in parts]
-    top = jnp.concatenate([from_lanes(block, width, 0) for block in blocks], axis=0)
+    notes = [ref[...] for ref in notes]
+    top = jnp.concatenate([from_lanes(note, 0, 0) for note in notes], axis=0)
     weights = w_ref[...] * jnp.exp(peak_ref[:, :1] - top)
     left = (weights * projected).astype(BF16)
     left_ref[...] = left
     spread(left, held_ref, keep_ref, send_ref, None)
-    loss_ref[...] = tree_sum([from_lanes(block, width, 1)[:1] for block in blocks]) * scale
+    loss_ref[...] = tree_sum([from_lanes(note, 0, 1)[:1] for note in notes]) * scale
 
 
 def grad_rest_kernel(left_ref, held_ref, keep_ref, send_ref):
@@ -321,13 +320,14 @@
     refs[-1][...] = tree_sum([ref[...] for ref in refs[:-1]])
 
 
-def head_grads_kernel(full_width, sums_ref, other_sums_ref, *refs):
+def head_grads_kernel(full_width, count, *refs):
+    terms, refs = refs[:count], refs[count:]
     pooled_ref, top_ref, gain_ref, weight_ref, bias_ref, label_ref, *refs = refs
-    bias_grad_ref, copy_ref, grad_ref, normed_ref = refs
+    bias_grad_ref, copy_ref, grad_ref, note_ref, normed_ref = refs
     pooled, gain = pooled_ref[...], gain_ref[...]
     heads, width = pooled.shape
     columns = bias_ref.shape[1]
-    sums = sums_ref[...] + other_sums_ref[...]
+    sums = tree_sum([ref[...] for ref in terms])
     mask = head_mask((heads, columns), columns // heads)
     inverse_flat = lax.rsqrt(sums[1:2] / full_width + 1e-05)
     inverse_rms = jnp.max(jnp.where(mask, inverse_flat, 0.0), axis=1, keepdims=True)
@@ -347,8 +347,8 @@
     normed_grad = (back[:heads] + back[heads:]) * gain
     inner = jnp.sum(by_head * product, axis=1, keepdims=True) / full_width
     unit = pooled * inverse_rms
-    grad_ref[:, :width] = (inverse_rms * (normed_grad - unit * inner)).astype(BF16)
-    grad_ref[:, width:] = into_lanes([top_ref[:, :1], jnp.broadcast_to(loss, (heads, 1))], heads)
+    grad_ref[...] = (inverse_rms * (normed_grad - unit * inner)).astype(BF16)
+    note_ref[...] = into_lanes([top_ref[:, :1], jnp.broadcast_to(loss, (heads, 1))], heads)
     normed_ref[...] = unit * gain
 
 
@@ -416,23 +416,29 @@
         "head_sums",
         [*parts, gain, head_weight],
     )
-    far_sums = [swap(sums, *step) for step in far_steps()[::-1]]
-    (sums,) = call(tree_sum_kernel, [((2, columns), F32)], "tree_sum", [sums, *far_sums])
-    bias_grad, bias_grad_here, pooled_grad, normed = call(
-        functools.partial(head_grads_kernel, full_width),
-        [((1, columns), F32), ((1, columns), F32), ((rows, width + LANES), BF16), ((rows, width), F32)],
+    group = min(4, contexts)
+    terms = [sums] + [swap(sums, bits, 0) for bits in range(1, group)]
+    while group < contexts:
+        (sums,) = call(tree_sum_kernel, [((2, columns), F32)], "tree_sum", terms)
+        terms = [sums, swap(sums, group, 0)]
+        group *= 2
+    bias_grad, bias_grad_here, pooled_grad, note, normed = call(
+        functools.partial(head_grads_kernel, full_width, len(terms)),
+        [((1, columns), F32)] * 2 + [((rows, width), BF16), ((rows, LANES), BF16), ((rows, width), F32)],
         "head_grads",
-        [sums, swap(sums, 1, 0), pooled, top, gain, head_weight, head_bias[None, :], labels[None, :]],
+        [*terms, pooled, top, gain, head_weight, head_bias[None, :], labels[None, :]],
     )
     head_grad = head_weight_grad(normed, bias_grad_here)
     first, second = gather(pooled_grad)
     part = project_half(first)
+    notes = [note] + [swap(note, 0, bits) for bits in range(2, classes, 2)]
+    notes = notes + [swap(note, 0, 1) for note in notes]
     pair = [((blocks, half, width), F32), ((blocks, half, width), BF16)]
     keep_b, send_b, left, loss = call(
         functools.partial(grad_kernel, 1.0 / (columns * classes), classes),
         [*pair, ((heads, token_count), BF16), ((1, 1), F32)],
         "grad",
-        [*second, part, held_b, weights, own_peak],
+        [*second, *notes, part, held_b, weights, own_peak],
         cost=cost,
     )
     half_a = call(grad_rest_kernel, pair, "grad_rest", [left, held_a], cost=cost)

time: 101 us -> 105 us (1.040)
  waiting for transfers between devices: 31.7 us -> 34.1 us
  starting transfers between devices: 41.2 us -> 43.6 us
    ppermute x40 -> x43, waiting for transfers between devices: 31.7 us -> 34.1 us  [swap(): return lax.ppermute(x, ('ctx', 'cls'), pairs)]
    ppermute x40 -> x43, starting transfers between devices: 41.2 us -> 43.6 us  [swap(): return lax.ppermute(x, ('ctx', 'cls'), pairs)]
  transfers between devices with their start and end apart: 40 -> 43, of which waited for: 20 -> 19; matrix products, arithmetic and copies ran while one was open for 0% -> 0% of each run, Pallas kernels for 14% -> 14%
where the time goes in v9:
time: 105 us
  starting transfers between devices  43.6 us (42%)
  waiting for transfers between devices  34.1 us (32%)
  Pallas kernels  26 us (25%)
  between operations  1.51 us (1%)
    ppermute x43, starting transfers between devices, swap(): return lax.ppermute(x, ('ctx', 'cls'), pairs)  43.6 us
    ppermute x43, waiting for transfers between devices, swap(): return lax.ppermute(x, ('ctx', 'cls'), pairs)  34.1 us
    pallas_call x18, Pallas kernels, call(): return list(run(*args))  18.3 us
    pallas_call x1, Pallas kernels, load(): run(*[pltpu.with_memory_space_constraint(x, pltpu.HBM) for x in (tokens,...  4.79 us
    pallas_call x1, Pallas kernels, head_weight_grad(): pl.pallas_call(functools.partial(head_weight_grad_kernel, columns // rows...  2.95 us
  transfers between devices with their start and end apart: 43, of which 19 were waited for; matrix products, arithmetic and copies ran while one was open for 0% of the time, Pallas kernels for 14%

profile of v9, /device:TPU:0, one launch (start us, length us, event | category | flops | bytes accessed | tf_op | source)
XLA Modules:
  0.0 105.2 jit_solution(18413421890043924440)
XLA Ops:
  0.6 3.1 %collective-permute-start = (bf16[16,1024]{1,0:T(8,128)(2,1)}, bf16[16,1024]{1,0:T(8,128)(2,1)S(1)}, u32[]{:S(2)}, u32[]{:S(2)}) collective-permute-start(bf16[16,1024]{1,0:T(8,128)(2,1)} %refs_0_.1), channel_id=1, source_target_pairs={{0,8},{1,9},{2,10},{3,11},{4,12},{5,13},{6,14},{7,15},{8,0},{9,1},... | collective-permute-start | bytes 98312 | tf_op jit(solution)/shard_map/ppermute | solution.py:22
  3.7 2.5 %collective-permute-start.2 = (bf16[16,1024]{1,0:T(8,128)(2,1)}, bf16[16,1024]{1,0:T(8,128)(2,1)S(1)}, u32[]{:S(2)}, u32[]{:S(2)}) collective-permute-start(bf16[16,1024]{1,0:T(8,128)(2,1)} %refs_0_.1), channel_id=1, source_target_pairs={{0,24},{1,25},{2,26},{3,27},{4,28},{5,29},{6,30},{7,31},{8,16},{9,... | collective-permute-start | bytes 98312 | tf_op jit(solution)/shard_map/ppermute | solution.py:22
  6.3 4.8 %load.1 = (bf16[4,768,1024]{2,1,0:T(8,128)(2,1)S(1)}, bf16[4,768,1024]{2,1,0:T(8,128)(2,1)S(1)}, bf16[16,1024]{1,0:T(8,128)(2,1)S(1)}, f32[1,1024]{1,0:T(1,128)S(1)}) custom-call(bf16[768,8192]{1,0:T(8,128)(2,1)} %tokens_ref.1, bf16[16,1024]{1,0:T(8,128)(2,1)} %refs_0_.1, f32[1,1024]{1,0:T(1,128)} %bitcast.7), custom_call_target="tpu_custom_call" | custom-call | tf_op jit(solution)/shard_map/load/pallas_call | solution.py:123
  11.6 1.6 %collective-permute-start.7 = (bf16[4,16,1024]{2,1,0:T(8,128)(2,1)S(1)}, bf16[4,16,1024]{2,1,0:T(8,128)(2,1)S(1)}, u32[]{:S(2)}, u32[]{:S(2)}) collective-permute-start(bf16[4,16,1024]{2,1,0:T(8,128)(2,1)S(1)} %stack.2.refs_0_), channel_id=1, source_target_pairs={{0,2},{1,3},{2,0},{3,1},{4,6},{5,7},{6,4},{7,5},{8,10},{9,11},{10,... | collective-permute-start | bytes 393224 | tf_op jit(solution)/shard_map/ppermute | solution.py:22
  13.2 1.4 %collective-permute-start.4 = (bf16[4,16,1024]{2,1,0:T(8,128)(2,1)S(1)}, bf16[4,16,1024]{2,1,0:T(8,128)(2,1)S(1)}, u32[]{:S(2)}, u32[]{:S(2)}) collective-permute-start(bf16[4,16,1024]{2,1,0:T(8,128)(2,1)S(1)} %stack.2.refs_0_), channel_id=1, source_target_pairs={{0,6},{1,7},{2,4},{3,5},{4,2},{5,3},{6,0},{7,1},{8,14},{9,15},{10,... | collective-permute-start | bytes 393224 | tf_op jit(solution)/shard_map/ppermute | solution.py:22
  15.1 3.2 %collective-permute-done.7.refs_1_ = bf16[4,16,1024]{2,1,0:T(8,128)(2,1)S(1)} collective-permute-done((bf16[4,16,1024]{2,1,0:T(8,128)(2,1)S(1)}, bf16[4,16,1024]{2,1,0:T(8,128)(2,1)S(1)}, u32[]{:S(2)}, u32[]{:S(2)}) %collective-permute-start.7) | collective-permute-done | bytes 131104 | tf_op jit(solution)/shard_map/ppermute | solution.py:22
  20.0 2.0 %project.2.refs_4_ = f32[64,768]{1,0:T(8,128)S(1)} custom-call(bf16[4,16,1024]{2,1,0:T(8,128)(2,1)S(1)} %stack.2.refs_0_, bf16[4,16,1024]{2,1,0:T(8,128)(2,1)S(1)} %collective-permute-done.7.refs_1_, bf16[4,16,1024]{2,1,0:T(8,128)(2,1)S(1)} %collective-permute-done.8.refs_2_, bf16[4,16,1024]{2,1,0:T(8,128)(2,1)S(1)} %collective-permute-done.9.refs_3_, ...), custom_call_target="tpu_custom_call" | custom-call | flops 1610612736 | tf_op jit(solution)/shard_map/project/pallas_call | solution.py:50
  22.1 4.2 %pool.1 = (f32[4,32,1024]{2,1,0:T(8,128)S(1)}, bf16[4,32,1152]{2,1,0:T(8,128)(2,1)S(1)}, f32[64,128]{1,0:T(8,128)S(1)}, f32[64,768]{1,0:T(8,128)S(1)}, bf16[64,768]{1,0:T(8,128)(2,1)S(1)}) custom-call(s32[1]{0:T(128)S(6)} %copy.15.length_ref, bf16[4,16,1024]{2,1,0:T(8,128)(2,1)S(1)} %collective-permute-done.3.refs_0_, ...), custom_call_target="tpu_custom_call" | custom-call | flops 1610612736 | tf_op jit(solution)/shard_map/pool/pallas_call | solution.py:50
  26.3 0.6 collective-permute-start.10
  26.8 1.2 %pool_rest.1 = (f32[4,32,1024]{2,1,0:T(8,128)S(1)}, bf16[4,32,1152]{2,1,0:T(8,128)(2,1)S(1)}) custom-call(bf16[64,768]{1,0:T(8,128)(2,1)S(1)} %get-tuple-element.52.left_ref, f32[64,128]{1,0:T(8,128)S(1)} %get-tuple-element.53.peak_ref.refs_2_.refs_11_, bf16[4,768,1024]{2,1,0:T(8,128)(2,1)S(1)} %get-tuple-element.50.refs_4_.held_ref), custom_call_target="tpu_custom_call" | custom-call | flops 1610612736 | tf_op jit(solution)/shard_map/pool_rest/pallas_call | solution.py:50
  28.8 2.4 %collective-permute-start.12 = (bf16[4,16,1152]{2,1,0:T(8,128)(2,1)S(1)}, bf16[4,16,1152]{2,1,0:T(8,128)(2,1)S(1)}, u32[]{:S(2)}, u32[]{:S(2)}) collective-permute-start(bf16[4,16,1152]{2,1,0:T(8,128)(2,1)S(1)} %get-tuple-element.60), channel_id=1, source_target_pairs={{0,6},{1,7},{2,4},{3,5},{4,2},{5,3},{6,0},{7,1},{8,14},{9,15},{10,... | collective-permute-start | bytes 442376 | tf_op jit(solution)/shard_map/ppermute | solution.py:22
  32.0 0.6 collective-permute-start.14
  32.7 3.7 %collective-permute-done.12.refs_1_ = bf16[4,16,1152]{2,1,0:T(8,128)(2,1)S(1)} collective-permute-done((bf16[4,16,1152]{2,1,0:T(8,128)(2,1)S(1)}, bf16[4,16,1152]{2,1,0:T(8,128)(2,1)S(1)}, u32[]{:S(2)}, u32[]{:S(2)}) %collective-permute-start.12) | collective-permute-done | bytes 147488 | tf_op jit(solution)/shard_map/ppermute | solution.py:22
  36.4 2.4 %collective-permute-done.13.refs_2_ = bf16[4,16,1152]{2,1,0:T(8,128)(2,1)S(1)} collective-permute-done((bf16[4,16,1152]{2,1,0:T(8,128)(2,1)S(1)}, bf16[4,16,1152]{2,1,0:T(8,128)(2,1)S(1)}, u32[]{:S(2)}, u32[]{:S(2)}) %collective-permute-start.13) | collective-permute-done | bytes 147488 | tf_op jit(solution)/shard_map/ppermute | solution.py:22
  39.1 2.7 %collective-permute-start.15 = (bf16[1,16,1152]{2,1,0:T(8,128)(2,1)S(1)}, bf16[1,16,1152]{2,1,0:T(8,128)(2,1)S(1)}, u32[]{:S(2)}, u32[]{:S(2)}) collective-permute-start(bf16[1,16,1152]{2,1,0:T(8,128)(2,1)S(1)} %get-tuple-element.65), channel_id=1, source_target_pairs={{0,24},{1,25},{2,26},{3,27},{4,28},{5,29},{6,30},{7,31},{8,16},{9,... | collective-permute-start | bytes 110600 | tf_op jit(solution)/shard_map/ppermute | solution.py:22
  42.2 1.4 %collective-permute-start.17 = (bf16[1,16,1152]{2,1,0:T(8,128)(2,1)S(1)}, bf16[1,16,1152]{2,1,0:T(8,128)(2,1)S(1)}, u32[]{:S(2)}, u32[]{:S(2)}) collective-permute-start(bf16[1,16,1152]{2,1,0:T(8,128)(2,1)S(1)} %get-tuple-element.67), channel_id=1, source_target_pairs={{0,8},{1,9},{2,10},{3,11},{4,12},{5,13},{6,14},{7,15},{8,0},{9,1},... | collective-permute-start | bytes 110600 | tf_op jit(solution)/shard_map/ppermute | solution.py:22
  43.6 1.8 %collective-permute-done.15.refs_1_ = bf16[1,16,1152]{2,1,0:T(8,128)(2,1)S(1)} collective-permute-done((bf16[1,16,1152]{2,1,0:T(8,128)(2,1)S(1)}, bf16[1,16,1152]{2,1,0:T(8,128)(2,1)S(1)}, u32[]{:S(2)}, u32[]{:S(2)}) %collective-permute-start.15) | collective-permute-done | bytes 36896 | tf_op jit(solution)/shard_map/ppermute | solution.py:22
  45.3 1.6 %collective-permute-done.16.refs_2_ = bf16[1,16,1152]{2,1,0:T(8,128)(2,1)S(1)} collective-permute-done((bf16[1,16,1152]{2,1,0:T(8,128)(2,1)S(1)}, bf16[1,16,1152]{2,1,0:T(8,128)(2,1)S(1)}, u32[]{:S(2)}, u32[]{:S(2)}) %collective-permute-start.16) | collective-permute-done | bytes 36896 | tf_op jit(solution)/shard_map/ppermute | solution.py:22
  47.0 0.6 head_sums.1
  47.6 1.5 %collective-permute-start.20 = (f32[2,1024]{1,0:T(2,128)S(1)}, f32[2,1024]{1,0:T(2,128)S(1)}, u32[]{:S(2)}, u32[]{:S(2)}) collective-permute-start(f32[2,1024]{1,0:T(2,128)S(1)} %get-tuple-element.70.refs_0_), channel_id=1, source_target_pairs={{0,12},{1,13},{2,14},{3,15},{4,8},{5,9},{6,10},{7,11},{8,4},{9,5},... | collective-permute-start | bytes 24584 | tf_op jit(solution)/shard_map/ppermute | solution.py:22
  49.2 1.5 %collective-permute-start.19 = (f32[2,1024]{1,0:T(2,128)S(1)}, f32[2,1024]{1,0:T(2,128)S(1)}, u32[]{:S(2)}, u32[]{:S(2)}) collective-permute-start(f32[2,1024]{1,0:T(2,128)S(1)} %get-tuple-element.70.refs_0_), channel_id=1, source_target_pairs={{0,8},{1,9},{2,10},{3,11},{4,12},{5,13},{6,14},{7,15},{8,0},{9,1},... | collective-permute-start | bytes 24584 | tf_op jit(solution)/shard_map/ppermute | solution.py:22
  51.2 1.1 %collective-permute-done.20.refs_3_ = f32[2,1024]{1,0:T(2,128)S(1)} collective-permute-done((f32[2,1024]{1,0:T(2,128)S(1)}, f32[2,1024]{1,0:T(2,128)S(1)}, u32[]{:S(2)}, u32[]{:S(2)}) %collective-permute-start.20) | collective-permute-done | bytes 8224 | tf_op jit(solution)/shard_map/ppermute | solution.py:22
  52.2 0.6 collective-permute-done.19.refs_2_
  52.8 1.5 %collective-permute-done.18.refs_1_ = f32[2,1024]{1,0:T(2,128)S(1)} collective-permute-done((f32[2,1024]{1,0:T(2,128)S(1)}, f32[2,1024]{1,0:T(2,128)S(1)}, u32[]{:S(2)}, u32[]{:S(2)}) %collective-permute-start.18) | collective-permute-done | bytes 8224 | tf_op jit(solution)/shard_map/ppermute | solution.py:22
  54.3 1.7 %collective-permute-start.21 = (f32[2,1024]{1,0:T(2,128)S(1)}, f32[2,1024]{1,0:T(2,128)S(1)}, u32[]{:S(2)}, u32[]{:S(2)}) collective-permute-start(f32[2,1024]{1,0:T(2,128)S(1)} %tree_sum.1.refs_0_), channel_id=1, source_target_pairs={{0,16},{1,17},{2,18},{3,19},{4,20},{5,21},{6,22},{7,23},{8,24},{9,... | collective-permute-start | bytes 24584 | tf_op jit(solution)/shard_map/ppermute | solution.py:22
  56.0 2.9 %collective-permute-done.21.refs_1_ = f32[2,1024]{1,0:T(2,128)S(1)} collective-permute-done((f32[2,1024]{1,0:T(2,128)S(1)}, f32[2,1024]{1,0:T(2,128)S(1)}, u32[]{:S(2)}, u32[]{:S(2)}) %collective-permute-start.21) | collective-permute-done | bytes 8224 | tf_op jit(solution)/shard_map/ppermute | solution.py:22
  58.9 1.2 %head_grads.1 = (f32[1,1024]{1,0:T(1,128)}, f32[1,1024]{1,0:T(1,128)S(1)}, bf16[16,1024]{1,0:T(8,128)(2,1)S(1)}, bf16[16,128]{1,0:T(8,128)(2,1)S(1)}, f32[16,1024]{1,0:T(8,128)S(1)}) custom-call(f32[2,1024]{1,0:T(2,128)S(1)} %tree_sum.1.refs_0_, f32[2,1024]{1,0:T(2,128)S(1)} %collective-permute-done.21.refs_1_, f32[16,1024]{1,0:T(8,128)S(1)} %get-tuple-element.71.refs_2_, ...), custom_call_target="tpu_custom_call" | custom-call | tf_op jit(solution)/shard_map/head_grads/pallas_call | solution.py:50
  60.1 1.9 %collective-permute-start.24 = (bf16[16,1024]{1,0:T(8,128)(2,1)S(1)}, bf16[16,1024]{1,0:T(8,128)(2,1)S(1)}, u32[]{:S(2)}, u32[]{:S(2)}) collective-permute-start(bf16[16,1024]{1,0:T(8,128)(2,1)S(1)} %get-tuple-element.73.refs_0_), channel_id=1, source_target_pairs={{0,24},{1,25},{2,26},{3,27},{4,28},{5,29},{6,30},{7,31},{8,16},{9,... | collective-permute-start | bytes 98312 | tf_op jit(solution)/shard_map/ppermute | solution.py:22
  62.1 2.4 %collective-permute-start.22 = (bf16[16,1024]{1,0:T(8,128)(2,1)S(1)}, bf16[16,1024]{1,0:T(8,128)(2,1)S(1)}, u32[]{:S(2)}, u32[]{:S(2)}) collective-permute-start(bf16[16,1024]{1,0:T(8,128)(2,1)S(1)} %get-tuple-element.73.refs_0_), channel_id=1, source_target_pairs={{0,8},{1,9},{2,10},{3,11},{4,12},{5,13},{6,14},{7,15},{8,0},{9,1},... | collective-permute-start | bytes 98312 | tf_op jit(solution)/shard_map/ppermute | solution.py:22
  64.5 1.3 %collective-permute-done.24.refs_3_ = bf16[16,1024]{1,0:T(8,128)(2,1)S(1)} collective-permute-done((bf16[16,1024]{1,0:T(8,128)(2,1)S(1)}, bf16[16,1024]{1,0:T(8,128)(2,1)S(1)}, u32[]{:S(2)}, u32[]{:S(2)}) %collective-permute-start.24) | collective-permute-done | bytes 32800 | tf_op jit(solution)/shard_map/ppermute | solution.py:22
  65.8 1.1 %collective-permute-done.23.refs_2_ = bf16[16,1024]{1,0:T(8,128)(2,1)S(1)} collective-permute-done((bf16[16,1024]{1,0:T(8,128)(2,1)S(1)}, bf16[16,1024]{1,0:T(8,128)(2,1)S(1)}, u32[]{:S(2)}, u32[]{:S(2)}) %collective-permute-start.23) | collective-permute-done | bytes 32800 | tf_op jit(solution)/shard_map/ppermute | solution.py:22
  67.0 1.6 %collective-permute-start.32 = (bf16[4,16,1024]{2,1,0:T(8,128)(2,1)S(1)}, bf16[4,16,1024]{2,1,0:T(8,128)(2,1)S(1)}, u32[]{:S(2)}, u32[]{:S(2)}) collective-permute-start(bf16[4,16,1024]{2,1,0:T(8,128)(2,1)S(1)} %stack.3.refs_0_), channel_id=1, source_target_pairs={{0,2},{1,3},{2,0},{3,1},{4,6},{5,7},{6,4},{7,5},{8,10},{9,11},{10,... | collective-permute-start | bytes 393224 | tf_op jit(solution)/shard_map/ppermute | solution.py:22
  69.0 1.5 %collective-permute-start.25 = (bf16[4,16,1024]{2,1,0:T(8,128)(2,1)S(1)}, bf16[4,16,1024]{2,1,0:T(8,128)(2,1)S(1)}, u32[]{:S(2)}, u32[]{:S(2)}) collective-permute-start(bf16[4,16,1024]{2,1,0:T(8,128)(2,1)S(1)} %stack.3.refs_0_), channel_id=1, source_target_pairs={{0,4},{1,5},{2,6},{3,7},{4,0},{5,1},{6,2},{7,3},{8,12},{9,13},{10,... | collective-permute-start | bytes 393224 | tf_op jit(solution)/shard_map/ppermute | solution.py:22
  70.5 3.3 %collective-permute-done.32.refs_1_ = bf16[4,16,1024]{2,1,0:T(8,128)(2,1)S(1)} collective-permute-done((bf16[4,16,1024]{2,1,0:T(8,128)(2,1)S(1)}, bf16[4,16,1024]{2,1,0:T(8,128)(2,1)S(1)}, u32[]{:S(2)}, u32[]{:S(2)}) %collective-permute-start.32) | collective-permute-done | bytes 131104 | tf_op jit(solution)/shard_map/ppermute | solution.py:22
  73.8 2.6 %collective-permute-start.29 = (bf16[16,128]{1,0:T(8,128)(2,1)S(1)}, bf16[16,128]{1,0:T(8,128)(2,1)S(1)}, u32[]{:S(2)}, u32[]{:S(2)}) collective-permute-start(bf16[16,128]{1,0:T(8,128)(2,1)S(1)} %get-tuple-element.74.refs_4_), channel_id=1, source_target_pairs={{0,2},{1,3},{2,0},{3,1},{4,6},{5,7},{6,4},{7,5},{8,10},{9,11},{10,... | collective-permute-start | bytes 12296 | tf_op jit(solution)/shard_map/ppermute | solution.py:22
  76.4 1.6 %collective-permute-done.29.refs_5_ = bf16[16,128]{1,0:T(8,128)(2,1)S(1)} collective-permute-done((bf16[16,128]{1,0:T(8,128)(2,1)S(1)}, bf16[16,128]{1,0:T(8,128)(2,1)S(1)}, u32[]{:S(2)}, u32[]{:S(2)}) %collective-permute-start.29) | collective-permute-done | bytes 4128 | tf_op jit(solution)/shard_map/ppermute | solution.py:22
  79.0 2.0 %project.3.refs_8_ = f32[64,768]{1,0:T(8,128)S(1)} custom-call(bf16[4,16,1024]{2,1,0:T(8,128)(2,1)S(1)} %stack.3.refs_0_, bf16[4,16,1024]{2,1,0:T(8,128)(2,1)S(1)} %collective-permute-done.32.refs_1_, bf16[4,16,1024]{2,1,0:T(8,128)(2,1)S(1)} %collective-permute-done.33.refs_2_, bf16[4,16,1024]{2,1,0:T(8,128)(2,1)S(1)} %collective-permute-done.34.refs_3_, ...), custom_call_target="tpu_custom_call" | custom-call | flops 1610612736 | tf_op jit(solution)/shard_map/project/pallas_call | solution.py:50
  81.1 4.0 %grad.1 = (f32[4,32,1024]{2,1,0:T(8,128)S(1)}, bf16[4,32,1024]{2,1,0:T(8,128)(2,1)S(1)}, bf16[64,768]{1,0:T(8,128)(2,1)S(1)}, f32[1,1]{1,0:T(1,128)}) custom-call(bf16[4,16,1024]{2,1,0:T(8,128)(2,1)S(1)} %collective-permute-done.25.refs_0_, bf16[4,16,1024]{2,1,0:T(8,128)(2,1)S(1)} %collective-permute-done.26.refs_1_, ...), custom_call_target="tpu_custom_call" | custom-call | flops 1610612736 | tf_op jit(solution)/shard_map/grad/pallas_call | solution.py:50
  85.3 1.2 %grad_rest.1 = (f32[4,32,1024]{2,1,0:T(8,128)S(1)}, bf16[4,32,1024]{2,1,0:T(8,128)(2,1)S(1)}) custom-call(bf16[64,768]{1,0:T(8,128)(2,1)S(1)} %get-tuple-element.77.left_ref, bf16[4,768,1024]{2,1,0:T(8,128)(2,1)S(1)} %get-tuple-element.50.refs_4_.held_ref), custom_call_target="tpu_custom_call" | custom-call | flops 1610612736 | tf_op jit(solution)/shard_map/grad_rest/pallas_call | solution.py:50
  87.0 2.0 %collective-permute-start.37 = (bf16[4,16,1024]{2,1,0:T(8,128)(2,1)S(1)}, bf16[4,16,1024]{2,1,0:T(8,128)(2,1)S(1)}, u32[]{:S(2)}, u32[]{:S(2)}) collective-permute-start(bf16[4,16,1024]{2,1,0:T(8,128)(2,1)S(1)} %get-tuple-element.84), channel_id=1, source_target_pairs={{0,6},{1,7},{2,4},{3,5},{4,2},{5,3},{6,0},{7,1},{8,14},{9,15},{10,... | collective-permute-start | bytes 393224 | tf_op jit(solution)/shard_map/ppermute | solution.py:22
  89.0 1.5 %collective-permute-start.38 = (bf16[4,16,1024]{2,1,0:T(8,128)(2,1)S(1)}, bf16[4,16,1024]{2,1,0:T(8,128)(2,1)S(1)}, u32[]{:S(2)}, u32[]{:S(2)}) collective-permute-start(bf16[4,16,1024]{2,1,0:T(8,128)(2,1)S(1)} %get-tuple-element.85), channel_id=1, source_target_pairs={{0,4},{1,5},{2,6},{3,7},{4,0},{5,1},{6,2},{7,3},{8,12},{9,13},{10,... | collective-permute-start | bytes 393224 | tf_op jit(solution)/shard_map/ppermute | solution.py:22
  90.7 3.6 %collective-permute-done.37.refs_1_ = bf16[4,16,1024]{2,1,0:T(8,128)(2,1)S(1)} collective-permute-done((bf16[4,16,1024]{2,1,0:T(8,128)(2,1)S(1)}, bf16[4,16,1024]{2,1,0:T(8,128)(2,1)S(1)}, u32[]{:S(2)}, u32[]{:S(2)}) %collective-permute-start.37) | collective-permute-done | bytes 131104 | tf_op jit(solution)/shard_map/ppermute | solution.py:22
  94.3 2.8 %collective-permute-done.38.refs_2_ = bf16[4,16,1024]{2,1,0:T(8,128)(2,1)S(1)} collective-permute-done((bf16[4,16,1024]{2,1,0:T(8,128)(2,1)S(1)}, bf16[4,16,1024]{2,1,0:T(8,128)(2,1)S(1)}, u32[]{:S(2)}, u32[]{:S(2)}) %collective-permute-start.38) | collective-permute-done | bytes 131104 | tf_op jit(solution)/shard_map/ppermute | solution.py:22
  97.1 2.1 %collective-permute-start.40 = (bf16[1,16,1024]{2,1,0:T(8,128)(2,1)S(1)}, bf16[1,16,1024]{2,1,0:T(8,128)(2,1)S(1)}, u32[]{:S(2)}, u32[]{:S(2)}) collective-permute-start(bf16[1,16,1024]{2,1,0:T(8,128)(2,1)S(1)} %get-tuple-element.88), channel_id=1, source_target_pairs={{0,24},{1,25},{2,26},{3,27},{4,28},{5,29},{6,30},{7,31},{8,16},{9,... | collective-permute-start | bytes 98312 | tf_op jit(solution)/shard_map/ppermute | solution.py:22
  99.2 0.8 collective-permute-start.41
  100.0 1.6 %collective-permute-start.42 = (bf16[1,16,1024]{2,1,0:T(8,128)(2,1)S(1)}, bf16[1,16,1024]{2,1,0:T(8,128)(2,1)S(1)}, u32[]{:S(2)}, u32[]{:S(2)}) collective-permute-start(bf16[1,16,1024]{2,1,0:T(8,128)(2,1)S(1)} %get-tuple-element.90), channel_id=1, source_target_pairs={{0,8},{1,9},{2,10},{3,11},{4,12},{5,13},{6,14},{7,15},{8,0},{9,1},... | collective-permute-start | bytes 98312 | tf_op jit(solution)/shard_map/ppermute | solution.py:22
  101.6 2.9 %head_weight_grad.1 = f32[1024,1024]{1,0:T(8,128)} custom-call(f32[16,1024]{1,0:T(8,128)S(1)} %get-tuple-element.91.normed_ref, f32[1,1024]{1,0:T(1,128)S(1)} %get-tuple-element.92.bias_grad_ref), custom_call_target="tpu_custom_call" | custom-call | tf_op jit(solution)/shard_map/head_weight_grad/pallas_call | solution.py:370
  104.5 0.6 far_sum.1
  (64 shorter events, 7.4 us)
Async XLA Ops:
  0.6 10.5 %collective-permute-start = (bf16[16,1024]{1,0:T(8,128)(2,1)}, bf16[16,1024]{1,0:T(8,128)(2,1)S(1)}, u32[]{:S(2)}, u32[]{:S(2)}) collective-permute-start(bf16[16,1024]{1,0:T(8,128)(2,1)} %refs_0_.1), channel_id=1, source_target_pairs={{0,8},{1,9},{2,10},{3,11},{4,12},{5,13},{6,14},{7,15},{8,0},{9,1},... | collective-permute-start | bytes 98312 | tf_op jit(solution)/shard_map/ppermute | solution.py:22
  3.7 7.4 %collective-permute-start.2 = (bf16[16,1024]{1,0:T(8,128)(2,1)}, bf16[16,1024]{1,0:T(8,128)(2,1)S(1)}, u32[]{:S(2)}, u32[]{:S(2)}) collective-permute-start(bf16[16,1024]{1,0:T(8,128)(2,1)} %refs_0_.1), channel_id=1, source_target_pairs={{0,24},{1,25},{2,26},{3,27},{4,28},{5,29},{6,30},{7,31},{8,16},{9,... | collective-permute-start | bytes 98312 | tf_op jit(solution)/shard_map/ppermute | solution.py:22
  6.2 5.4 %collective-permute-start.1 = (bf16[16,1024]{1,0:T(8,128)(2,1)}, bf16[16,1024]{1,0:T(8,128)(2,1)S(1)}, u32[]{:S(2)}, u32[]{:S(2)}) collective-permute-start(bf16[16,1024]{1,0:T(8,128)(2,1)} %refs_0_.1), channel_id=1, source_target_pairs={{0,16},{1,17},{2,18},{3,19},{4,20},{5,21},{6,22},{7,23},{8,24},{9,... | collective-permute-start | bytes 98312 | tf_op jit(solution)/shard_map/ppermute | solution.py:22
  11.6 6.8 %collective-permute-start.7 = (bf16[4,16,1024]{2,1,0:T(8,128)(2,1)S(1)}, bf16[4,16,1024]{2,1,0:T(8,128)(2,1)S(1)}, u32[]{:S(2)}, u32[]{:S(2)}) collective-permute-start(bf16[4,16,1024]{2,1,0:T(8,128)(2,1)S(1)} %stack.2.refs_0_), channel_id=1, source_target_pairs={{0,2},{1,3},{2,0},{3,1},{4,6},{5,7},{6,4},{7,5},{8,10},{9,11},{10,... | collective-permute-start | bytes 393224 | tf_op jit(solution)/shard_map/ppermute | solution.py:22
  13.2 6.3 %collective-permute-start.4 = (bf16[4,16,1024]{2,1,0:T(8,128)(2,1)S(1)}, bf16[4,16,1024]{2,1,0:T(8,128)(2,1)S(1)}, u32[]{:S(2)}, u32[]{:S(2)}) collective-permute-start(bf16[4,16,1024]{2,1,0:T(8,128)(2,1)S(1)} %stack.2.refs_0_), channel_id=1, source_target_pairs={{0,6},{1,7},{2,4},{3,5},{4,2},{5,3},{6,0},{7,1},{8,14},{9,15},{10,... | collective-permute-start | bytes 393224 | tf_op jit(solution)/shard_map/ppermute | solution.py:22
  14.6 5.4 %collective-permute-start.3 = (bf16[4,16,1024]{2,1,0:T(8,128)(2,1)S(1)}, bf16[4,16,1024]{2,1,0:T(8,128)(2,1)S(1)}, u32[]{:S(2)}, u32[]{:S(2)}) collective-permute-start(bf16[4,16,1024]{2,1,0:T(8,128)(2,1)S(1)} %stack.2.refs_0_), channel_id=1, source_target_pairs={{0,4},{1,5},{2,6},{3,7},{4,0},{5,1},{6,2},{7,3},{8,12},{9,13},{10,... | collective-permute-start | bytes 393224 | tf_op jit(solution)/shard_map/ppermute | solution.py:22
  15.1 4.9 %collective-permute-start.8 = (bf16[4,16,1024]{2,1,0:T(8,128)(2,1)S(1)}, bf16[4,16,1024]{2,1,0:T(8,128)(2,1)S(1)}, u32[]{:S(2)}, u32[]{:S(2)}) collective-permute-start(bf16[4,16,1024]{2,1,0:T(8,128)(2,1)S(1)} %stack.2.refs_0_), channel_id=1, source_target_pairs={{0,1},{1,0},{2,3},{3,2},{4,5},{5,4},{6,7},{7,6},{8,9},{9,8},{10,11... | collective-permute-start | bytes 393224 | tf_op jit(solution)/shard_map/ppermute | solution.py:22
  18.3 1.7 %collective-permute-start.9 = (bf16[4,16,1024]{2,1,0:T(8,128)(2,1)S(1)}, bf16[4,16,1024]{2,1,0:T(8,128)(2,1)S(1)}, u32[]{:S(2)}, u32[]{:S(2)}) collective-permute-start(bf16[4,16,1024]{2,1,0:T(8,128)(2,1)S(1)} %collective-permute-done.7.refs_1_), channel_id=1, source_target_pairs={{0,1},{1,0},{2,3},{3,2},{4,5},{5,4},{6,7},{7,6},{8,9},{9,8},{10,11... | collective-permute-start | bytes 393224 | tf_op jit(solution)/shard_map/ppermute | solution.py:22
  19.5 2.5 %collective-permute-start.6 = (bf16[4,16,1024]{2,1,0:T(8,128)(2,1)S(1)}, bf16[4,16,1024]{2,1,0:T(8,128)(2,1)S(1)}, u32[]{:S(2)}, u32[]{:S(2)}) collective-permute-start(bf16[4,16,1024]{2,1,0:T(8,128)(2,1)S(1)} %collective-permute-done.4.refs_1_), channel_id=1, source_target_pairs={{0,1},{1,0},{2,3},{3,2},{4,5},{5,4},{6,7},{7,6},{8,9},{9,8},{10,11... | collective-permute-start | bytes 393224 | tf_op jit(solution)/shard_map/ppermute | solution.py:22
  20.0 2.1 %collective-permute-start.5 = (bf16[4,16,1024]{2,1,0:T(8,128)(2,1)S(1)}, bf16[4,16,1024]{2,1,0:T(8,128)(2,1)S(1)}, u32[]{:S(2)}, u32[]{:S(2)}) collective-permute-start(bf16[4,16,1024]{2,1,0:T(8,128)(2,1)S(1)} %collective-permute-done.3.refs_0_), channel_id=1, source_target_pairs={{0,1},{1,0},{2,3},{3,2},{4,5},{5,4},{6,7},{7,6},{8,9},{9,8},{10,11... | collective-permute-start | bytes 393224 | tf_op jit(solution)/shard_map/ppermute | solution.py:22
  26.2 20.8 %copy-start = (bf16[1024,1024]{1,0:T(8,128)(2,1)S(1)}, bf16[1024,1024]{1,0:T(8,128)(2,1)}, u32[]{:S(2)}) copy-start(bf16[1024,1024]{1,0:T(8,128)(2,1)} %refs_5_.1) | copy-start | bytes 6291460
  26.2 32.7 %copy-start.1 = (f32[1024]{0:T(1024)S(1)}, f32[1024]{0:T(1024)}, u32[]{:S(2)}) copy-start(f32[1024]{0:T(1024)} %param.12) | copy-start | bytes 12292
  26.3 32.7 %copy-start.2 = (s32[1024]{0:T(1024)S(1)}, s32[1024]{0:T(1024)}, u32[]{:S(2)}) copy-start(s32[1024]{0:T(1024)} %param.13) | copy-start | bytes 12292
  26.3 1.8 %collective-permute-start.10 = (bf16[4,32,1152]{2,1,0:T(8,128)(2,1)S(1)}, bf16[4,32,1152]{2,1,0:T(8,128)(2,1)S(1)}, u32[]{:S(2)}, u32[]{:S(2)}) collective-permute-start(bf16[4,32,1152]{2,1,0:T(8,128)(2,1)S(1)} %get-tuple-element.56), channel_id=1, source_target_pairs={{0,1},{1,0},{2,3},{3,2},{4,5},{5,4},{6,7},{7,6},{8,9},{9,8},{10,11... | collective-permute-start | bytes 884744 | tf_op jit(solution)/shard_map/ppermute | solution.py:22
  28.4 3.4 %collective-permute-start.11 = (bf16[4,32,1152]{2,1,0:T(8,128)(2,1)S(1)}, bf16[4,32,1152]{2,1,0:T(8,128)(2,1)S(1)}, u32[]{:S(2)}, u32[]{:S(2)}) collective-permute-start(bf16[4,32,1152]{2,1,0:T(8,128)(2,1)S(1)} %get-tuple-element.58), channel_id=1, source_target_pairs={{0,1},{1,0},{2,3},{3,2},{4,5},{5,4},{6,7},{7,6},{8,9},{9,8},{10,11... | collective-permute-start | bytes 884744 | tf_op jit(solution)/shard_map/ppermute | solution.py:22
  28.8 7.6 %collective-permute-start.12 = (bf16[4,16,1152]{2,1,0:T(8,128)(2,1)S(1)}, bf16[4,16,1152]{2,1,0:T(8,128)(2,1)S(1)}, u32[]{:S(2)}, u32[]{:S(2)}) collective-permute-start(bf16[4,16,1152]{2,1,0:T(8,128)(2,1)S(1)} %get-tuple-element.60), channel_id=1, source_target_pairs={{0,6},{1,7},{2,4},{3,5},{4,2},{5,3},{6,0},{7,1},{8,14},{9,15},{10,... | collective-permute-start | bytes 442376 | tf_op jit(solution)/shard_map/ppermute | solution.py:22
  31.2 7.6 %collective-permute-start.13 = (bf16[4,16,1152]{2,1,0:T(8,128)(2,1)S(1)}, bf16[4,16,1152]{2,1,0:T(8,128)(2,1)S(1)}, u32[]{:S(2)}, u32[]{:S(2)}) collective-permute-start(bf16[4,16,1152]{2,1,0:T(8,128)(2,1)S(1)} %get-tuple-element.61), channel_id=1, source_target_pairs={{0,4},{1,5},{2,6},{3,7},{4,0},{5,1},{6,2},{7,3},{8,12},{9,13},{10,... | collective-permute-start | bytes 442376 | tf_op jit(solution)/shard_map/ppermute | solution.py:22
  32.0 6.7 %collective-permute-start.14 = (bf16[4,16,1152]{2,1,0:T(8,128)(2,1)S(1)}, bf16[4,16,1152]{2,1,0:T(8,128)(2,1)S(1)}, u32[]{:S(2)}, u32[]{:S(2)}) collective-permute-start(bf16[4,16,1152]{2,1,0:T(8,128)(2,1)S(1)} %get-tuple-element.62), channel_id=1, source_target_pairs={{0,2},{1,3},{2,0},{3,1},{4,6},{5,7},{6,4},{7,5},{8,10},{9,11},{10,... | collective-permute-start | bytes 442376 | tf_op jit(solution)/shard_map/ppermute | solution.py:22
  39.1 6.2 %collective-permute-start.15 = (bf16[1,16,1152]{2,1,0:T(8,128)(2,1)S(1)}, bf16[1,16,1152]{2,1,0:T(8,128)(2,1)S(1)}, u32[]{:S(2)}, u32[]{:S(2)}) collective-permute-start(bf16[1,16,1152]{2,1,0:T(8,128)(2,1)S(1)} %get-tuple-element.65), channel_id=1, source_target_pairs={{0,24},{1,25},{2,26},{3,27},{4,28},{5,29},{6,30},{7,31},{8,16},{9,... | collective-permute-start | bytes 110600 | tf_op jit(solution)/shard_map/ppermute | solution.py:22
  41.8 5.1 %collective-permute-start.16 = (bf16[1,16,1152]{2,1,0:T(8,128)(2,1)S(1)}, bf16[1,16,1152]{2,1,0:T(8,128)(2,1)S(1)}, u32[]{:S(2)}, u32[]{:S(2)}) collective-permute-start(bf16[1,16,1152]{2,1,0:T(8,128)(2,1)S(1)} %get-tuple-element.66), channel_id=1, source_target_pairs={{0,16},{1,17},{2,18},{3,19},{4,20},{5,21},{6,22},{7,23},{8,24},{9,... | collective-permute-start | bytes 110600 | tf_op jit(solution)/shard_map/ppermute | solution.py:22
  42.2 4.8 %collective-permute-start.17 = (bf16[1,16,1152]{2,1,0:T(8,128)(2,1)S(1)}, bf16[1,16,1152]{2,1,0:T(8,128)(2,1)S(1)}, u32[]{:S(2)}, u32[]{:S(2)}) collective-permute-start(bf16[1,16,1152]{2,1,0:T(8,128)(2,1)S(1)} %get-tuple-element.67), channel_id=1, source_target_pairs={{0,8},{1,9},{2,10},{3,11},{4,12},{5,13},{6,14},{7,15},{8,0},{9,1},... | collective-permute-start | bytes 110600 | tf_op jit(solution)/shard_map/ppermute | solution.py:22
  47.6 4.6 %collective-permute-start.20 = (f32[2,1024]{1,0:T(2,128)S(1)}, f32[2,1024]{1,0:T(2,128)S(1)}, u32[]{:S(2)}, u32[]{:S(2)}) collective-permute-start(f32[2,1024]{1,0:T(2,128)S(1)} %get-tuple-element.70.refs_0_), channel_id=1, source_target_pairs={{0,12},{1,13},{2,14},{3,15},{4,8},{5,9},{6,10},{7,11},{8,4},{9,5},... | collective-permute-start | bytes 24584 | tf_op jit(solution)/shard_map/ppermute | solution.py:22
  49.2 3.7 %collective-permute-start.19 = (f32[2,1024]{1,0:T(2,128)S(1)}, f32[2,1024]{1,0:T(2,128)S(1)}, u32[]{:S(2)}, u32[]{:S(2)}) collective-permute-start(f32[2,1024]{1,0:T(2,128)S(1)} %get-tuple-element.70.refs_0_), channel_id=1, source_target_pairs={{0,8},{1,9},{2,10},{3,11},{4,12},{5,13},{6,14},{7,15},{8,0},{9,1},... | collective-permute-start | bytes 24584 | tf_op jit(solution)/shard_map/ppermute | solution.py:22
  50.6 3.7 %collective-permute-start.18 = (f32[2,1024]{1,0:T(2,128)S(1)}, f32[2,1024]{1,0:T(2,128)S(1)}, u32[]{:S(2)}, u32[]{:S(2)}) collective-permute-start(f32[2,1024]{1,0:T(2,128)S(1)} %get-tuple-element.70.refs_0_), channel_id=1, source_target_pairs={{0,4},{1,5},{2,6},{3,7},{4,0},{5,1},{6,2},{7,3},{8,12},{9,13},{10,... | collective-permute-start | bytes 24584 | tf_op jit(solution)/shard_map/ppermute | solution.py:22
  54.3 4.6 %collective-permute-start.21 = (f32[2,1024]{1,0:T(2,128)S(1)}, f32[2,1024]{1,0:T(2,128)S(1)}, u32[]{:S(2)}, u32[]{:S(2)}) collective-permute-start(f32[2,1024]{1,0:T(2,128)S(1)} %tree_sum.1.refs_0_), channel_id=1, source_target_pairs={{0,16},{1,17},{2,18},{3,19},{4,20},{5,21},{6,22},{7,23},{8,24},{9,... | collective-permute-start | bytes 24584 | tf_op jit(solution)/shard_map/ppermute | solution.py:22
  60.1 5.7 %collective-permute-start.24 = (bf16[16,1024]{1,0:T(8,128)(2,1)S(1)}, bf16[16,1024]{1,0:T(8,128)(2,1)S(1)}, u32[]{:S(2)}, u32[]{:S(2)}) collective-permute-start(bf16[16,1024]{1,0:T(8,128)(2,1)S(1)} %get-tuple-element.73.refs_0_), channel_id=1, source_target_pairs={{0,24},{1,25},{2,26},{3,27},{4,28},{5,29},{6,30},{7,31},{8,16},{9,... | collective-permute-start | bytes 98312 | tf_op jit(solution)/shard_map/ppermute | solution.py:22
  62.0 5.0 %collective-permute-start.23 = (bf16[16,1024]{1,0:T(8,128)(2,1)S(1)}, bf16[16,1024]{1,0:T(8,128)(2,1)S(1)}, u32[]{:S(2)}, u32[]{:S(2)}) collective-permute-start(bf16[16,1024]{1,0:T(8,128)(2,1)S(1)} %get-tuple-element.73.refs_0_), channel_id=1, source_target_pairs={{0,16},{1,17},{2,18},{3,19},{4,20},{5,21},{6,22},{7,23},{8,24},{9,... | collective-permute-start | bytes 98312 | tf_op jit(solution)/shard_map/ppermute | solution.py:22
  62.1 4.9 %collective-permute-start.22 = (bf16[16,1024]{1,0:T(8,128)(2,1)S(1)}, bf16[16,1024]{1,0:T(8,128)(2,1)S(1)}, u32[]{:S(2)}, u32[]{:S(2)}) collective-permute-start(bf16[16,1024]{1,0:T(8,128)(2,1)S(1)} %get-tuple-element.73.refs_0_), channel_id=1, source_target_pairs={{0,8},{1,9},{2,10},{3,11},{4,12},{5,13},{6,14},{7,15},{8,0},{9,1},... | collective-permute-start | bytes 98312 | tf_op jit(solution)/shard_map/ppermute | solution.py:22
  67.0 6.9 %collective-permute-start.32 = (bf16[4,16,1024]{2,1,0:T(8,128)(2,1)S(1)}, bf16[4,16,1024]{2,1,0:T(8,128)(2,1)S(1)}, u32[]{:S(2)}, u32[]{:S(2)}) collective-permute-start(bf16[4,16,1024]{2,1,0:T(8,128)(2,1)S(1)} %stack.3.refs_0_), channel_id=1, source_target_pairs={{0,2},{1,3},{2,0},{3,1},{4,6},{5,7},{6,4},{7,5},{8,10},{9,11},{10,... | collective-permute-start | bytes 393224 | tf_op jit(solution)/shard_map/ppermute | solution.py:22
  68.6 9.4 %collective-permute-start.33 = (bf16[4,16,1024]{2,1,0:T(8,128)(2,1)S(1)}, bf16[4,16,1024]{2,1,0:T(8,128)(2,1)S(1)}, u32[]{:S(2)}, u32[]{:S(2)}) collective-permute-start(bf16[4,16,1024]{2,1,0:T(8,128)(2,1)S(1)} %stack.3.refs_0_), channel_id=1, source_target_pairs={{0,1},{1,0},{2,3},{3,2},{4,5},{5,4},{6,7},{7,6},{8,9},{9,8},{10,11... | collective-permute-start | bytes 393224 | tf_op jit(solution)/shard_map/ppermute | solution.py:22
  68.6 9.9 %collective-permute-start.26 = (bf16[4,16,1024]{2,1,0:T(8,128)(2,1)S(1)}, bf16[4,16,1024]{2,1,0:T(8,128)(2,1)S(1)}, u32[]{:S(2)}, u32[]{:S(2)}) collective-permute-start(bf16[4,16,1024]{2,1,0:T(8,128)(2,1)S(1)} %stack.3.refs_0_), channel_id=1, source_target_pairs={{0,6},{1,7},{2,4},{3,5},{4,2},{5,3},{6,0},{7,1},{8,14},{9,15},{10,... | collective-permute-start | bytes 393224 | tf_op jit(solution)/shard_map/ppermute | solution.py:22
  69.0 9.5 %collective-permute-start.25 = (bf16[4,16,1024]{2,1,0:T(8,128)(2,1)S(1)}, bf16[4,16,1024]{2,1,0:T(8,128)(2,1)S(1)}, u32[]{:S(2)}, u32[]{:S(2)}) collective-permute-start(bf16[4,16,1024]{2,1,0:T(8,128)(2,1)S(1)} %stack.3.refs_0_), channel_id=1, source_target_pairs={{0,4},{1,5},{2,6},{3,7},{4,0},{5,1},{6,2},{7,3},{8,12},{9,13},{10,... | collective-permute-start | bytes 393224 | tf_op jit(solution)/shard_map/ppermute | solution.py:22
  73.8 5.2 %collective-permute-start.34 = (bf16[4,16,1024]{2,1,0:T(8,128)(2,1)S(1)}, bf16[4,16,1024]{2,1,0:T(8,128)(2,1)S(1)}, u32[]{:S(2)}, u32[]{:S(2)}) collective-permute-start(bf16[4,16,1024]{2,1,0:T(8,128)(2,1)S(1)} %collective-permute-done.32.refs_1_), channel_id=1, source_target_pairs={{0,1},{1,0},{2,3},{3,2},{4,5},{5,4},{6,7},{7,6},{8,9},{9,8},{10,11... | collective-permute-start | bytes 393224 | tf_op jit(solution)/shard_map/ppermute | solution.py:22
  73.8 4.1 %collective-permute-start.29 = (bf16[16,128]{1,0:T(8,128)(2,1)S(1)}, bf16[16,128]{1,0:T(8,128)(2,1)S(1)}, u32[]{:S(2)}, u32[]{:S(2)}) collective-permute-start(bf16[16,128]{1,0:T(8,128)(2,1)S(1)} %get-tuple-element.74.refs_4_), channel_id=1, source_target_pairs={{0,2},{1,3},{2,0},{3,1},{4,6},{5,7},{6,4},{7,5},{8,10},{9,11},{10,... | collective-permute-start | bytes 12296 | tf_op jit(solution)/shard_map/ppermute | solution.py:22
  78.0 3.1 %collective-permute-start.30 = (bf16[16,128]{1,0:T(8,128)(2,1)S(1)}, bf16[16,128]{1,0:T(8,128)(2,1)S(1)}, u32[]{:S(2)}, u32[]{:S(2)}) collective-permute-start(bf16[16,128]{1,0:T(8,128)(2,1)S(1)} %get-tuple-element.74.refs_4_), channel_id=1, source_target_pairs={{0,1},{1,0},{2,3},{3,2},{4,5},{5,4},{6,7},{7,6},{8,9},{9,8},{10,11... | collective-permute-start | bytes 12296 | tf_op jit(solution)/shard_map/ppermute | solution.py:22
  78.0 3.1 %collective-permute-start.31 = (bf16[16,128]{1,0:T(8,128)(2,1)S(1)}, bf16[16,128]{1,0:T(8,128)(2,1)S(1)}, u32[]{:S(2)}, u32[]{:S(2)}) collective-permute-start(bf16[16,128]{1,0:T(8,128)(2,1)S(1)} %collective-permute-done.29.refs_5_), channel_id=1, source_target_pairs={{0,1},{1,0},{2,3},{3,2},{4,5},{5,4},{6,7},{7,6},{8,9},{9,8},{10,11... | collective-permute-start | bytes 12296 | tf_op jit(solution)/shard_map/ppermute | solution.py:22
  78.5 2.6 %collective-permute-start.28 = (bf16[4,16,1024]{2,1,0:T(8,128)(2,1)S(1)}, bf16[4,16,1024]{2,1,0:T(8,128)(2,1)S(1)}, u32[]{:S(2)}, u32[]{:S(2)}) collective-permute-start(bf16[4,16,1024]{2,1,0:T(8,128)(2,1)S(1)} %collective-permute-done.26.refs_1_), channel_id=1, source_target_pairs={{0,1},{1,0},{2,3},{3,2},{4,5},{5,4},{6,7},{7,6},{8,9},{9,8},{10,11... | collective-permute-start | bytes 393224 | tf_op jit(solution)/shard_map/ppermute | solution.py:22
  78.6 2.5 %collective-permute-start.27 = (bf16[4,16,1024]{2,1,0:T(8,128)(2,1)S(1)}, bf16[4,16,1024]{2,1,0:T(8,128)(2,1)S(1)}, u32[]{:S(2)}, u32[]{:S(2)}) collective-permute-start(bf16[4,16,1024]{2,1,0:T(8,128)(2,1)S(1)} %collective-permute-done.25.refs_0_), channel_id=1, source_target_pairs={{0,1},{1,0},{2,3},{3,2},{4,5},{5,4},{6,7},{7,6},{8,9},{9,8},{10,11... | collective-permute-start | bytes 393224 | tf_op jit(solution)/shard_map/ppermute | solution.py:22
  85.1 1.6 %collective-permute-start.35 = (bf16[4,32,1024]{2,1,0:T(8,128)(2,1)S(1)}, bf16[4,32,1024]{2,1,0:T(8,128)(2,1)S(1)}, u32[]{:S(2)}, u32[]{:S(2)}) collective-permute-start(bf16[4,32,1024]{2,1,0:T(8,128)(2,1)S(1)} %get-tuple-element.80), channel_id=1, source_target_pairs={{0,1},{1,0},{2,3},{3,2},{4,5},{5,4},{6,7},{7,6},{8,9},{9,8},{10,11... | collective-permute-start | bytes 786440 | tf_op jit(solution)/shard_map/ppermute | solution.py:22
  86.8 3.8 %collective-permute-start.36 = (bf16[4,32,1024]{2,1,0:T(8,128)(2,1)S(1)}, bf16[4,32,1024]{2,1,0:T(8,128)(2,1)S(1)}, u32[]{:S(2)}, u32[]{:S(2)}) collective-permute-start(bf16[4,32,1024]{2,1,0:T(8,128)(2,1)S(1)} %get-tuple-element.82), channel_id=1, source_target_pairs={{0,1},{1,0},{2,3},{3,2},{4,5},{5,4},{6,7},{7,6},{8,9},{9,8},{10,11... | collective-permute-start | bytes 786440 | tf_op jit(solution)/shard_map/ppermute | solution.py:22
  87.0 7.2 %collective-permute-start.37 = (bf16[4,16,1024]{2,1,0:T(8,128)(2,1)S(1)}, bf16[4,16,1024]{2,1,0:T(8,128)(2,1)S(1)}, u32[]{:S(2)}, u32[]{:S(2)}) collective-permute-start(bf16[4,16,1024]{2,1,0:T(8,128)(2,1)S(1)} %get-tuple-element.84), channel_id=1, source_target_pairs={{0,6},{1,7},{2,4},{3,5},{4,2},{5,3},{6,0},{7,1},{8,14},{9,15},{10,... | collective-permute-start | bytes 393224 | tf_op jit(solution)/shard_map/ppermute | solution.py:22
  89.0 8.0 %collective-permute-start.38 = (bf16[4,16,1024]{2,1,0:T(8,128)(2,1)S(1)}, bf16[4,16,1024]{2,1,0:T(8,128)(2,1)S(1)}, u32[]{:S(2)}, u32[]{:S(2)}) collective-permute-start(bf16[4,16,1024]{2,1,0:T(8,128)(2,1)S(1)} %get-tuple-element.85), channel_id=1, source_target_pairs={{0,4},{1,5},{2,6},{3,7},{4,0},{5,1},{6,2},{7,3},{8,12},{9,13},{10,... | collective-permute-start | bytes 393224 | tf_op jit(solution)/shard_map/ppermute | solution.py:22
  90.6 6.5 %collective-permute-start.39 = (bf16[4,16,1024]{2,1,0:T(8,128)(2,1)S(1)}, bf16[4,16,1024]{2,1,0:T(8,128)(2,1)S(1)}, u32[]{:S(2)}, u32[]{:S(2)}) collective-permute-start(bf16[4,16,1024]{2,1,0:T(8,128)(2,1)S(1)} %get-tuple-element.86), channel_id=1, source_target_pairs={{0,2},{1,3},{2,0},{3,1},{4,6},{5,7},{6,4},{7,5},{8,10},{9,11},{10,... | collective-permute-start | bytes 393224 | tf_op jit(solution)/shard_map/ppermute | solution.py:22
  97.1 7.4 %collective-permute-start.40 = (bf16[1,16,1024]{2,1,0:T(8,128)(2,1)S(1)}, bf16[1,16,1024]{2,1,0:T(8,128)(2,1)S(1)}, u32[]{:S(2)}, u32[]{:S(2)}) collective-permute-start(bf16[1,16,1024]{2,1,0:T(8,128)(2,1)S(1)} %get-tuple-element.88), channel_id=1, source_target_pairs={{0,24},{1,25},{2,26},{3,27},{4,28},{5,29},{6,30},{7,31},{8,16},{9,... | collective-permute-start | bytes 98312 | tf_op jit(solution)/shard_map/ppermute | solution.py:22
  99.2 5.3 %collective-permute-start.41 = (bf16[1,16,1024]{2,1,0:T(8,128)(2,1)S(1)}, bf16[1,16,1024]{2,1,0:T(8,128)(2,1)S(1)}, u32[]{:S(2)}, u32[]{:S(2)}) collective-permute-start(bf16[1,16,1024]{2,1,0:T(8,128)(2,1)S(1)} %get-tuple-element.89), channel_id=1, source_target_pairs={{0,16},{1,17},{2,18},{3,19},{4,20},{5,21},{6,22},{7,23},{8,24},{9,... | collective-permute-start | bytes 98312 | tf_op jit(solution)/shard_map/ppermute | solution.py:22
  100.0 4.6 %collective-permute-start.42 = (bf16[1,16,1024]{2,1,0:T(8,128)(2,1)S(1)}, bf16[1,16,1024]{2,1,0:T(8,128)(2,1)S(1)}, u32[]{:S(2)}, u32[]{:S(2)}) collective-permute-start(bf16[1,16,1024]{2,1,0:T(8,128)(2,1)S(1)} %get-tuple-element.90), channel_id=1, source_target_pairs={{0,8},{1,9},{2,10},{3,11},{4,12},{5,13},{6,14},{7,15},{8,0},{9,1},... | collective-permute-start | bytes 98312 | tf_op jit(solution)/shard_map/ppermute | solution.py:22

commit v10 on v7

--- a/solution.py
+++ b/solution.py
@@ -158,7 +158,7 @@
 
 def pool_kernel(count, length_ref, *refs):
     parts, refs = refs[:count], refs[count:]
-    part_ref, held_ref, keep_ref, send_ref, peak_ref, w_ref, left_ref = refs
+    part_ref, held_ref, spread_ref, keep_ref, send_ref, peak_ref, w_ref, left_ref = refs
     scores = part_ref[...] + project(parts, held_ref)
     shard = lax.axis_index("ctx") * lax.axis_size("cls") + lax.axis_index("cls")
     valid = lax.broadcasted_iota(jnp.int32, scores.shape, 1) < length_ref[0] - shard * scores.shape[1]
@@ -168,7 +168,7 @@
     w_ref[...] = weights
     left_ref[...] = left
     peak_ref[...] = jnp.broadcast_to(peak, peak_ref.shape)
-    spread(left, held_ref, keep_ref, send_ref, peak_lanes(peak, keep_ref.shape[1]))
+    spread(left, spread_ref, keep_ref, send_ref, peak_lanes(peak, keep_ref.shape[1]))
 
 
 def pool_rest_kernel(left_ref, peak_ref, held_ref, keep_ref, send_ref):
@@ -177,7 +177,7 @@
 
 def grad_kernel(scale, count, *refs):
     parts, refs = refs[:count], refs[count:]
-    part_ref, held_ref, w_ref, peak_ref, keep_ref, send_ref, left_ref, loss_ref = refs
+    part_ref, held_ref, spread_ref, w_ref, peak_ref, keep_ref, send_ref, left_ref, loss_ref = refs
     width = held_ref.shape[2]
     projected = part_ref[...] + project(parts, held_ref)
     blocks = [ref[0] for ref in parts]
@@ -185,7 +185,7 @@
     weights = w_ref[...] * jnp.exp(peak_ref[:, :1] - top)
     left = (weights * projected).astype(BF16)
     left_ref[...] = left
-    spread(left, held_ref, keep_ref, send_ref, None)
+    spread(left, spread_ref, keep_ref, send_ref, None)
     loss_ref[...] = tree_sum([from_lanes(block, width, 1)[:1] for block in blocks]) * scale
 
 
@@ -395,16 +395,16 @@
     cost = pl.CostEstimate(flops=256 * token_count * full_width, bytes_accessed=0, transcendentals=0)
 
     def project_half(parts):
-        return call(functools.partial(project_kernel, len(parts)), [product], "project", [*parts, held_a], cost=cost)[0]
+        return call(functools.partial(project_kernel, len(parts)), [product], "project", [*parts, held_b], cost=cost)[0]
 
     held_a, held_b, queries_here, gain = load(width, tokens, queries, norm_gain[None, :])
     first, second = gather(queries, queries_here)
-    part = project_half(first)
+    part = project_half(second)
     keep_b, send_b, own_peak, weights, left = call(
         functools.partial(pool_kernel, classes),
         [*pair, ((heads, LANES), F32), product, ((heads, token_count), BF16)],
         "pool",
-        [doc_length, *second, part, held_b],
+        [doc_length, *first, part, held_a, held_b],
         smem_args=(0,),
         cost=cost,
     )
@@ -426,13 +426,13 @@
     )
     head_grad = head_weight_grad(normed, bias_grad_here)
     first, second = gather(pooled_grad)
-    part = project_half(first)
+    part = project_half(second)
     pair = [((blocks, half, width), F32), ((blocks, half, width), BF16)]
     keep_b, send_b, left, loss = call(
         functools.partial(grad_kernel, 1.0 / (columns * classes), classes),
         [*pair, ((heads, token_count), BF16), ((1, 1), F32)],
         "grad",
-        [*second, part, held_b, weights, own_peak],
+        [*first, part, held_a, held_b, weights, own_peak],
         cost=cost,
     )
     half_a = call(grad_rest_kernel, pair, "grad_rest", [left, held_a], cost=cost)

time: 101 us -> 101 us (level)
  transfers between devices with their start and end apart: 40 -> 40, of which waited for: 20 -> 21; matrix products, arithmetic and copies ran while one was open for 0% -> 0% of each run, Pallas kernels for 14% -> 14%
where the time goes in v10:
time: 101 us
  starting transfers between devices  41.7 us (41%)
  waiting for transfers between devices  31.7 us (31%)
  Pallas kernels  26 us (26%)
  between operations  1.48 us (1%)
    ppermute x40, starting transfers between devices, swap(): return lax.ppermute(x, ('ctx', 'cls'), pairs)  41.7 us
    ppermute x40, waiting for transfers between devices, swap(): return lax.ppermute(x, ('ctx', 'cls'), pairs)  31.7 us
    pallas_call x18, Pallas kernels, call(): return list(run(*args))  18.2 us
    pallas_call x1, Pallas kernels, load(): run(*[pltpu.with_memory_space_constraint(x, pltpu.HBM) for x in (tokens,...  4.79 us
    pallas_call x1, Pallas kernels, head_weight_grad(): pl.pallas_call(functools.partial(head_weight_grad_kernel, columns // rows...  2.95 us
  transfers between devices with their start and end apart: 40, of which 21 were waited for; matrix products, arithmetic and copies ran while one was open for 0% of the time, Pallas kernels for 14%

profile of v10, /device:TPU:0, one launch (start us, length us, event | category | flops | bytes accessed | tf_op | source)
XLA Modules:
  0.0 100.9 jit_solution(14873997215447419955)
XLA Ops:
  0.6 3.1 %collective-permute-start = (bf16[16,1024]{1,0:T(8,128)(2,1)}, bf16[16,1024]{1,0:T(8,128)(2,1)S(1)}, u32[]{:S(2)}, u32[]{:S(2)}) collective-permute-start(bf16[16,1024]{1,0:T(8,128)(2,1)} %refs_0_.1), channel_id=1, source_target_pairs={{0,8},{1,9},{2,10},{3,11},{4,12},{5,13},{6,14},{7,15},{8,0},{9,1},... | collective-permute-start | bytes 98312 | tf_op jit(solution)/shard_map/ppermute | solution.py:22
  3.7 2.5 %collective-permute-start.2 = (bf16[16,1024]{1,0:T(8,128)(2,1)}, bf16[16,1024]{1,0:T(8,128)(2,1)S(1)}, u32[]{:S(2)}, u32[]{:S(2)}) collective-permute-start(bf16[16,1024]{1,0:T(8,128)(2,1)} %refs_0_.1), channel_id=1, source_target_pairs={{0,24},{1,25},{2,26},{3,27},{4,28},{5,29},{6,30},{7,31},{8,16},{9,... | collective-permute-start | bytes 98312 | tf_op jit(solution)/shard_map/ppermute | solution.py:22
  6.3 4.8 %load.1 = (bf16[4,768,1024]{2,1,0:T(8,128)(2,1)S(1)}, bf16[4,768,1024]{2,1,0:T(8,128)(2,1)S(1)}, bf16[16,1024]{1,0:T(8,128)(2,1)S(1)}, f32[1,1024]{1,0:T(1,128)S(1)}) custom-call(bf16[768,8192]{1,0:T(8,128)(2,1)} %tokens_ref.1, bf16[16,1024]{1,0:T(8,128)(2,1)} %refs_0_.1, f32[1,1024]{1,0:T(1,128)} %bitcast.7), custom_call_target="tpu_custom_call" | custom-call | tf_op jit(solution)/shard_map/load/pallas_call | solution.py:123
  11.6 2.5 %collective-permute-start.7 = (bf16[4,16,1024]{2,1,0:T(8,128)(2,1)S(1)}, bf16[4,16,1024]{2,1,0:T(8,128)(2,1)S(1)}, u32[]{:S(2)}, u32[]{:S(2)}) collective-permute-start(bf16[4,16,1024]{2,1,0:T(8,128)(2,1)S(1)} %stack.2.refs_0_), channel_id=1, source_target_pairs={{0,6},{1,7},{2,4},{3,5},{4,2},{5,3},{6,0},{7,1},{8,14},{9,15},{10,... | collective-permute-start | bytes 393224 | tf_op jit(solution)/shard_map/ppermute | solution.py:22
  15.1 3.2 %collective-permute-done.7.refs_1_ = bf16[4,16,1024]{2,1,0:T(8,128)(2,1)S(1)} collective-permute-done((bf16[4,16,1024]{2,1,0:T(8,128)(2,1)S(1)}, bf16[4,16,1024]{2,1,0:T(8,128)(2,1)S(1)}, u32[]{:S(2)}, u32[]{:S(2)}) %collective-permute-start.7) | collective-permute-done | bytes 131104 | tf_op jit(solution)/shard_map/ppermute | solution.py:22
  18.3 1.3 %collective-permute-done.6.refs_0_ = bf16[4,16,1024]{2,1,0:T(8,128)(2,1)S(1)} collective-permute-done((bf16[4,16,1024]{2,1,0:T(8,128)(2,1)S(1)}, bf16[4,16,1024]{2,1,0:T(8,128)(2,1)S(1)}, u32[]{:S(2)}, u32[]{:S(2)}) %collective-permute-start.6) | collective-permute-done | bytes 131104 | tf_op jit(solution)/shard_map/ppermute | solution.py:22
  21.0 2.0 %project.2.refs_4_ = f32[64,768]{1,0:T(8,128)S(1)} custom-call(bf16[4,16,1024]{2,1,0:T(8,128)(2,1)S(1)} %collective-permute-done.6.refs_0_, bf16[4,16,1024]{2,1,0:T(8,128)(2,1)S(1)} %collective-permute-done.7.refs_1_, bf16[4,16,1024]{2,1,0:T(8,128)(2,1)S(1)} %collective-permute-done.8.refs_2_, bf16[4,16,1024]{2,1,0:T(8,128)(2,1)S(1)} %collective-permute-done.9.refs_3_, ...), custom_call_target="tpu_custom_call" | custom-call | flops 1610612736 | tf_op jit(solution)/shard_map/project/pallas_call | solution.py:50
  23.1 4.2 %pool.1 = (f32[4,32,1024]{2,1,0:T(8,128)S(1)}, bf16[4,32,1152]{2,1,0:T(8,128)(2,1)S(1)}, f32[64,128]{1,0:T(8,128)S(1)}, f32[64,768]{1,0:T(8,128)S(1)}, bf16[64,768]{1,0:T(8,128)(2,1)S(1)}) custom-call(s32[1]{0:T(128)S(6)} %copy.15.length_ref, bf16[4,16,1024]{2,1,0:T(8,128)(2,1)S(1)} %stack.2.refs_0_, ...), custom_call_target="tpu_custom_call" | custom-call | flops 1610612736 | tf_op jit(solution)/shard_map/pool/pallas_call | solution.py:50
  27.7 1.2 %pool_rest.1 = (f32[4,32,1024]{2,1,0:T(8,128)S(1)}, bf16[4,32,1152]{2,1,0:T(8,128)(2,1)S(1)}) custom-call(bf16[64,768]{1,0:T(8,128)(2,1)S(1)} %get-tuple-element.51.left_ref, f32[64,128]{1,0:T(8,128)S(1)} %get-tuple-element.52.peak_ref.refs_2_.refs_8_, bf16[4,768,1024]{2,1,0:T(8,128)(2,1)S(1)} %get-tuple-element.50.refs_5_.held_ref), custom_call_target="tpu_custom_call" | custom-call | flops 1610612736 | tf_op jit(solution)/shard_map/pool_rest/pallas_call | solution.py:50
  29.7 1.4 %collective-permute-start.12 = (bf16[4,16,1152]{2,1,0:T(8,128)(2,1)S(1)}, bf16[4,16,1152]{2,1,0:T(8,128)(2,1)S(1)}, u32[]{:S(2)}, u32[]{:S(2)}) collective-permute-start(bf16[4,16,1152]{2,1,0:T(8,128)(2,1)S(1)} %get-tuple-element.59), channel_id=1, source_target_pairs={{0,6},{1,7},{2,4},{3,5},{4,2},{5,3},{6,0},{7,1},{8,14},{9,15},{10,... | collective-permute-start | bytes 442376 | tf_op jit(solution)/shard_map/ppermute | solution.py:22
  32.0 1.6 %collective-permute-start.14 = (bf16[4,16,1152]{2,1,0:T(8,128)(2,1)S(1)}, bf16[4,16,1152]{2,1,0:T(8,128)(2,1)S(1)}, u32[]{:S(2)}, u32[]{:S(2)}) collective-permute-start(bf16[4,16,1152]{2,1,0:T(8,128)(2,1)S(1)} %get-tuple-element.61), channel_id=1, source_target_pairs={{0,2},{1,3},{2,0},{3,1},{4,6},{5,7},{6,4},{7,5},{8,10},{9,11},{10,... | collective-permute-start | bytes 442376 | tf_op jit(solution)/shard_map/ppermute | solution.py:22
  33.6 3.7 %collective-permute-done.12.refs_1_ = bf16[4,16,1152]{2,1,0:T(8,128)(2,1)S(1)} collective-permute-done((bf16[4,16,1152]{2,1,0:T(8,128)(2,1)S(1)}, bf16[4,16,1152]{2,1,0:T(8,128)(2,1)S(1)}, u32[]{:S(2)}, u32[]{:S(2)}) %collective-permute-start.12) | collective-permute-done | bytes 147488 | tf_op jit(solution)/shard_map/ppermute | solution.py:22
  37.3 1.4 %collective-permute-done.13.refs_2_ = bf16[4,16,1152]{2,1,0:T(8,128)(2,1)S(1)} collective-permute-done((bf16[4,16,1152]{2,1,0:T(8,128)(2,1)S(1)}, bf16[4,16,1152]{2,1,0:T(8,128)(2,1)S(1)}, u32[]{:S(2)}, u32[]{:S(2)}) %collective-permute-start.13) | collective-permute-done | bytes 147488 | tf_op jit(solution)/shard_map/ppermute | solution.py:22
  38.7 0.9 collective-permute-done.14.refs_3_
  40.0 2.7 %collective-permute-start.15 = (bf16[1,16,1152]{2,1,0:T(8,128)(2,1)S(1)}, bf16[1,16,1152]{2,1,0:T(8,128)(2,1)S(1)}, u32[]{:S(2)}, u32[]{:S(2)}) collective-permute-start(bf16[1,16,1152]{2,1,0:T(8,128)(2,1)S(1)} %get-tuple-element.64), channel_id=1, source_target_pairs={{0,24},{1,25},{2,26},{3,27},{4,28},{5,29},{6,30},{7,31},{8,16},{9,... | collective-permute-start | bytes 110600 | tf_op jit(solution)/shard_map/ppermute | solution.py:22
  43.0 1.4 %collective-permute-start.17 = (bf16[1,16,1152]{2,1,0:T(8,128)(2,1)S(1)}, bf16[1,16,1152]{2,1,0:T(8,128)(2,1)S(1)}, u32[]{:S(2)}, u32[]{:S(2)}) collective-permute-start(bf16[1,16,1152]{2,1,0:T(8,128)(2,1)S(1)} %get-tuple-element.66), channel_id=1, source_target_pairs={{0,8},{1,9},{2,10},{3,11},{4,12},{5,13},{6,14},{7,15},{8,0},{9,1},... | collective-permute-start | bytes 110600 | tf_op jit(solution)/shard_map/ppermute | solution.py:22
  44.4 1.4 %collective-permute-done.15.refs_1_ = bf16[1,16,1152]{2,1,0:T(8,128)(2,1)S(1)} collective-permute-done((bf16[1,16,1152]{2,1,0:T(8,128)(2,1)S(1)}, bf16[1,16,1152]{2,1,0:T(8,128)(2,1)S(1)}, u32[]{:S(2)}, u32[]{:S(2)}) %collective-permute-start.15) | collective-permute-done | bytes 36896 | tf_op jit(solution)/shard_map/ppermute | solution.py:22
  45.9 2.0 %collective-permute-done.16.refs_2_ = bf16[1,16,1152]{2,1,0:T(8,128)(2,1)S(1)} collective-permute-done((bf16[1,16,1152]{2,1,0:T(8,128)(2,1)S(1)}, bf16[1,16,1152]{2,1,0:T(8,128)(2,1)S(1)}, u32[]{:S(2)}, u32[]{:S(2)}) %collective-permute-start.16) | collective-permute-done | bytes 36896 | tf_op jit(solution)/shard_map/ppermute | solution.py:22
  47.9 0.6 head_sums.1
  48.5 2.2 %collective-permute-start.20 = (f32[2,1024]{1,0:T(2,128)S(1)}, f32[2,1024]{1,0:T(2,128)S(1)}, u32[]{:S(2)}, u32[]{:S(2)}) collective-permute-start(f32[2,1024]{1,0:T(2,128)S(1)} %get-tuple-element.69.refs_0_), channel_id=1, source_target_pairs={{0,24},{1,25},{2,26},{3,27},{4,28},{5,29},{6,30},{7,31},{8,16},{9,... | collective-permute-start | bytes 24584 | tf_op jit(solution)/shard_map/ppermute | solution.py:22
  50.7 2.3 %collective-permute-start.18 = (f32[2,1024]{1,0:T(2,128)S(1)}, f32[2,1024]{1,0:T(2,128)S(1)}, u32[]{:S(2)}, u32[]{:S(2)}) collective-permute-start(f32[2,1024]{1,0:T(2,128)S(1)} %get-tuple-element.69.refs_0_), channel_id=1, source_target_pairs={{0,8},{1,9},{2,10},{3,11},{4,12},{5,13},{6,14},{7,15},{8,0},{9,1},... | collective-permute-start | bytes 24584 | tf_op jit(solution)/shard_map/ppermute | solution.py:22
  52.9 1.1 %collective-permute-done.20.refs_3_ = f32[2,1024]{1,0:T(2,128)S(1)} collective-permute-done((f32[2,1024]{1,0:T(2,128)S(1)}, f32[2,1024]{1,0:T(2,128)S(1)}, u32[]{:S(2)}, u32[]{:S(2)}) %collective-permute-start.20) | collective-permute-done | bytes 8224 | tf_op jit(solution)/shard_map/ppermute | solution.py:22
  54.0 1.2 %collective-permute-done.19.refs_2_ = f32[2,1024]{1,0:T(2,128)S(1)} collective-permute-done((f32[2,1024]{1,0:T(2,128)S(1)}, f32[2,1024]{1,0:T(2,128)S(1)}, u32[]{:S(2)}, u32[]{:S(2)}) %collective-permute-start.19) | collective-permute-done | bytes 8224 | tf_op jit(solution)/shard_map/ppermute | solution.py:22
  55.2 1.6 %collective-permute-start.21 = (f32[2,1024]{1,0:T(2,128)S(1)}, f32[2,1024]{1,0:T(2,128)S(1)}, u32[]{:S(2)}, u32[]{:S(2)}) collective-permute-start(f32[2,1024]{1,0:T(2,128)S(1)} %tree_sum.1.sums_ref), channel_id=1, source_target_pairs={{0,4},{1,5},{2,6},{3,7},{4,0},{5,1},{6,2},{7,3},{8,12},{9,13},{10,... | collective-permute-start | bytes 24584 | tf_op jit(solution)/shard_map/ppermute | solution.py:22
  56.8 2.2 %collective-permute-done.21.other_sums_ref = f32[2,1024]{1,0:T(2,128)S(1)} collective-permute-done((f32[2,1024]{1,0:T(2,128)S(1)}, f32[2,1024]{1,0:T(2,128)S(1)}, u32[]{:S(2)}, u32[]{:S(2)}) %collective-permute-start.21) | collective-permute-done | bytes 8224 | tf_op jit(solution)/shard_map/ppermute | solution.py:22
  59.0 1.2 %head_grads.1 = (f32[1,1024]{1,0:T(1,128)}, f32[1,1024]{1,0:T(1,128)S(1)}, bf16[16,1152]{1,0:T(8,128)(2,1)S(1)}, f32[16,1024]{1,0:T(8,128)S(1)}) custom-call(f32[2,1024]{1,0:T(2,128)S(1)} %tree_sum.1.sums_ref, f32[2,1024]{1,0:T(2,128)S(1)} %collective-permute-done.21.other_sums_ref, f32[16,1024]{1,0:T(8,128)S(1)} %get-tuple-element.70.refs_0_, ...), custom_call_target="tpu_custom_call" | custom-call | tf_op jit(solution)/shard_map/head_grads/pallas_call | solution.py:50
  60.2 1.7 %collective-permute-start.24 = (bf16[16,1152]{1,0:T(8,128)(2,1)S(1)}, bf16[16,1152]{1,0:T(8,128)(2,1)S(1)}, u32[]{:S(2)}, u32[]{:S(2)}) collective-permute-start(bf16[16,1152]{1,0:T(8,128)(2,1)S(1)} %get-tuple-element.72.refs_0_), channel_id=1, source_target_pairs={{0,24},{1,25},{2,26},{3,27},{4,28},{5,29},{6,30},{7,31},{8,16},{9,... | collective-permute-start | bytes 110600 | tf_op jit(solution)/shard_map/ppermute | solution.py:22
  61.9 1.0 %collective-permute-start.23 = (bf16[16,1152]{1,0:T(8,128)(2,1)S(1)}, bf16[16,1152]{1,0:T(8,128)(2,1)S(1)}, u32[]{:S(2)}, u32[]{:S(2)}) collective-permute-start(bf16[16,1152]{1,0:T(8,128)(2,1)S(1)} %get-tuple-element.72.refs_0_), channel_id=1, source_target_pairs={{0,16},{1,17},{2,18},{3,19},{4,20},{5,21},{6,22},{7,23},{8,24},{9,... | collective-permute-start | bytes 110600 | tf_op jit(solution)/shard_map/ppermute | solution.py:22
  62.9 1.6 %collective-permute-start.22 = (bf16[16,1152]{1,0:T(8,128)(2,1)S(1)}, bf16[16,1152]{1,0:T(8,128)(2,1)S(1)}, u32[]{:S(2)}, u32[]{:S(2)}) collective-permute-start(bf16[16,1152]{1,0:T(8,128)(2,1)S(1)} %get-tuple-element.72.refs_0_), channel_id=1, source_target_pairs={{0,8},{1,9},{2,10},{3,11},{4,12},{5,13},{6,14},{7,15},{8,0},{9,1},... | collective-permute-start | bytes 110600 | tf_op jit(solution)/shard_map/ppermute | solution.py:22
  64.6 1.4 %collective-permute-done.24.refs_3_ = bf16[16,1152]{1,0:T(8,128)(2,1)S(1)} collective-permute-done((bf16[16,1152]{1,0:T(8,128)(2,1)S(1)}, bf16[16,1152]{1,0:T(8,128)(2,1)S(1)}, u32[]{:S(2)}, u32[]{:S(2)}) %collective-permute-start.24) | collective-permute-done | bytes 36896 | tf_op jit(solution)/shard_map/ppermute | solution.py:22
  65.9 1.2 %collective-permute-done.23.refs_2_ = bf16[16,1152]{1,0:T(8,128)(2,1)S(1)} collective-permute-done((bf16[16,1152]{1,0:T(8,128)(2,1)S(1)}, bf16[16,1152]{1,0:T(8,128)(2,1)S(1)}, u32[]{:S(2)}, u32[]{:S(2)}) %collective-permute-start.23) | collective-permute-done | bytes 36896 | tf_op jit(solution)/shard_map/ppermute | solution.py:22
  67.2 1.6 %collective-permute-start.29 = (bf16[4,16,1152]{2,1,0:T(8,128)(2,1)S(1)}, bf16[4,16,1152]{2,1,0:T(8,128)(2,1)S(1)}, u32[]{:S(2)}, u32[]{:S(2)}) collective-permute-start(bf16[4,16,1152]{2,1,0:T(8,128)(2,1)S(1)} %stack.3.refs_0_), channel_id=1, source_target_pairs={{0,6},{1,7},{2,4},{3,5},{4,2},{5,3},{6,0},{7,1},{8,14},{9,15},{10,... | collective-permute-start | bytes 442376 | tf_op jit(solution)/shard_map/ppermute | solution.py:22
  68.7 0.6 collective-permute-start.28
  69.3 1.4 %collective-permute-start.25 = (bf16[4,16,1152]{2,1,0:T(8,128)(2,1)S(1)}, bf16[4,16,1152]{2,1,0:T(8,128)(2,1)S(1)}, u32[]{:S(2)}, u32[]{:S(2)}) collective-permute-start(bf16[4,16,1152]{2,1,0:T(8,128)(2,1)S(1)} %stack.3.refs_0_), channel_id=1, source_target_pairs={{0,2},{1,3},{2,0},{3,1},{4,6},{5,7},{6,4},{7,5},{8,10},{9,11},{10,... | collective-permute-start | bytes 442376 | tf_op jit(solution)/shard_map/ppermute | solution.py:22
  70.7 2.6 %collective-permute-done.29.refs_1_ = bf16[4,16,1152]{2,1,0:T(8,128)(2,1)S(1)} collective-permute-done((bf16[4,16,1152]{2,1,0:T(8,128)(2,1)S(1)}, bf16[4,16,1152]{2,1,0:T(8,128)(2,1)S(1)}, u32[]{:S(2)}, u32[]{:S(2)}) %collective-permute-start.29) | collective-permute-done | bytes 147488 | tf_op jit(solution)/shard_map/ppermute | solution.py:22
  73.3 0.7 collective-permute-done.28.refs_0_
  75.4 2.0 %project.3.refs_4_ = f32[64,768]{1,0:T(8,128)S(1)} custom-call(bf16[4,16,1152]{2,1,0:T(8,128)(2,1)S(1)} %collective-permute-done.28.refs_0_, bf16[4,16,1152]{2,1,0:T(8,128)(2,1)S(1)} %collective-permute-done.29.refs_1_, bf16[4,16,1152]{2,1,0:T(8,128)(2,1)S(1)} %collective-permute-done.30.refs_2_, bf16[4,16,1152]{2,1,0:T(8,128)(2,1)S(1)} %collective-permute-done.31.refs_3_, ...), custom_call_target="tpu_custom_call" | custom-call | flops 1610612736 | tf_op jit(solution)/shard_map/project/pallas_call | solution.py:50
  77.4 4.0 %grad.1 = (f32[4,32,1024]{2,1,0:T(8,128)S(1)}, bf16[4,32,1024]{2,1,0:T(8,128)(2,1)S(1)}, bf16[64,768]{1,0:T(8,128)(2,1)S(1)}, f32[1,1]{1,0:T(1,128)}) custom-call(bf16[4,16,1152]{2,1,0:T(8,128)(2,1)S(1)} %stack.3.refs_0_, bf16[4,16,1152]{2,1,0:T(8,128)(2,1)S(1)} %collective-permute-done.25.refs_1_, bf16[4,16,1152]{2,1,0:T(8,128)(2,1)S(1)} %collective-permute-done.26.refs_2_, ...), custom_call_target="tpu_custom_call" | custom-call | flops 1610612736 | tf_op jit(solution)/shard_map/grad/pallas_call | solution.py:50
  81.7 1.2 %grad_rest.1 = (f32[4,32,1024]{2,1,0:T(8,128)S(1)}, bf16[4,32,1024]{2,1,0:T(8,128)(2,1)S(1)}) custom-call(bf16[64,768]{1,0:T(8,128)(2,1)S(1)} %get-tuple-element.75.left_ref, bf16[4,768,1024]{2,1,0:T(8,128)(2,1)S(1)} %get-tuple-element.50.refs_5_.held_ref), custom_call_target="tpu_custom_call" | custom-call | flops 1610612736 | tf_op jit(solution)/shard_map/grad_rest/pallas_call | solution.py:50
  83.4 2.3 %collective-permute-start.34 = (bf16[4,16,1024]{2,1,0:T(8,128)(2,1)S(1)}, bf16[4,16,1024]{2,1,0:T(8,128)(2,1)S(1)}, u32[]{:S(2)}, u32[]{:S(2)}) collective-permute-start(bf16[4,16,1024]{2,1,0:T(8,128)(2,1)S(1)} %get-tuple-element.82), channel_id=1, source_target_pairs={{0,6},{1,7},{2,4},{3,5},{4,2},{5,3},{6,0},{7,1},{8,14},{9,15},{10,... | collective-permute-start | bytes 393224 | tf_op jit(solution)/shard_map/ppermute | solution.py:22
  86.3 0.7 collective-permute-start.36
  87.0 3.6 %collective-permute-done.34.refs_1_ = bf16[4,16,1024]{2,1,0:T(8,128)(2,1)S(1)} collective-permute-done((bf16[4,16,1024]{2,1,0:T(8,128)(2,1)S(1)}, bf16[4,16,1024]{2,1,0:T(8,128)(2,1)S(1)}, u32[]{:S(2)}, u32[]{:S(2)}) %collective-permute-start.34) | collective-permute-done | bytes 131104 | tf_op jit(solution)/shard_map/ppermute | solution.py:22
  90.6 2.1 %collective-permute-done.35.refs_2_ = bf16[4,16,1024]{2,1,0:T(8,128)(2,1)S(1)} collective-permute-done((bf16[4,16,1024]{2,1,0:T(8,128)(2,1)S(1)}, bf16[4,16,1024]{2,1,0:T(8,128)(2,1)S(1)}, u32[]{:S(2)}, u32[]{:S(2)}) %collective-permute-start.35) | collective-permute-done | bytes 131104 | tf_op jit(solution)/shard_map/ppermute | solution.py:22
  92.9 2.3 %collective-permute-start.37 = (bf16[1,16,1024]{2,1,0:T(8,128)(2,1)S(1)}, bf16[1,16,1024]{2,1,0:T(8,128)(2,1)S(1)}, u32[]{:S(2)}, u32[]{:S(2)}) collective-permute-start(bf16[1,16,1024]{2,1,0:T(8,128)(2,1)S(1)} %get-tuple-element.86), channel_id=1, source_target_pairs={{0,24},{1,25},{2,26},{3,27},{4,28},{5,29},{6,30},{7,31},{8,16},{9,... | collective-permute-start | bytes 98312 | tf_op jit(solution)/shard_map/ppermute | solution.py:22
  95.1 0.6 collective-permute-start.38
  95.7 1.6 %collective-permute-start.39 = (bf16[1,16,1024]{2,1,0:T(8,128)(2,1)S(1)}, bf16[1,16,1024]{2,1,0:T(8,128)(2,1)S(1)}, u32[]{:S(2)}, u32[]{:S(2)}) collective-permute-start(bf16[1,16,1024]{2,1,0:T(8,128)(2,1)S(1)} %get-tuple-element.88), channel_id=1, source_target_pairs={{0,8},{1,9},{2,10},{3,11},{4,12},{5,13},{6,14},{7,15},{8,0},{9,1},... | collective-permute-start | bytes 98312 | tf_op jit(solution)/shard_map/ppermute | solution.py:22
  97.3 2.9 %head_weight_grad.1 = f32[1024,1024]{1,0:T(8,128)} custom-call(f32[16,1024]{1,0:T(8,128)S(1)} %get-tuple-element.89.normed_ref, f32[1,1024]{1,0:T(1,128)S(1)} %get-tuple-element.90.bias_grad_ref), custom_call_target="tpu_custom_call" | custom-call | tf_op jit(solution)/shard_map/head_weight_grad/pallas_call | solution.py:370
  100.3 0.6 far_sum.1
  (58 shorter events, 7.9 us)
Async XLA Ops:
  0.6 10.5 %collective-permute-start = (bf16[16,1024]{1,0:T(8,128)(2,1)}, bf16[16,1024]{1,0:T(8,128)(2,1)S(1)}, u32[]{:S(2)}, u32[]{:S(2)}) collective-permute-start(bf16[16,1024]{1,0:T(8,128)(2,1)} %refs_0_.1), channel_id=1, source_target_pairs={{0,8},{1,9},{2,10},{3,11},{4,12},{5,13},{6,14},{7,15},{8,0},{9,1},... | collective-permute-start | bytes 98312 | tf_op jit(solution)/shard_map/ppermute | solution.py:22
  3.7 7.4 %collective-permute-start.2 = (bf16[16,1024]{1,0:T(8,128)(2,1)}, bf16[16,1024]{1,0:T(8,128)(2,1)S(1)}, u32[]{:S(2)}, u32[]{:S(2)}) collective-permute-start(bf16[16,1024]{1,0:T(8,128)(2,1)} %refs_0_.1), channel_id=1, source_target_pairs={{0,24},{1,25},{2,26},{3,27},{4,28},{5,29},{6,30},{7,31},{8,16},{9,... | collective-permute-start | bytes 98312 | tf_op jit(solution)/shard_map/ppermute | solution.py:22
  6.2 5.4 %collective-permute-start.1 = (bf16[16,1024]{1,0:T(8,128)(2,1)}, bf16[16,1024]{1,0:T(8,128)(2,1)S(1)}, u32[]{:S(2)}, u32[]{:S(2)}) collective-permute-start(bf16[16,1024]{1,0:T(8,128)(2,1)} %refs_0_.1), channel_id=1, source_target_pairs={{0,16},{1,17},{2,18},{3,19},{4,20},{5,21},{6,22},{7,23},{8,24},{9,... | collective-permute-start | bytes 98312 | tf_op jit(solution)/shard_map/ppermute | solution.py:22
  11.6 6.7 %collective-permute-start.7 = (bf16[4,16,1024]{2,1,0:T(8,128)(2,1)S(1)}, bf16[4,16,1024]{2,1,0:T(8,128)(2,1)S(1)}, u32[]{:S(2)}, u32[]{:S(2)}) collective-permute-start(bf16[4,16,1024]{2,1,0:T(8,128)(2,1)S(1)} %stack.2.refs_0_), channel_id=1, source_target_pairs={{0,6},{1,7},{2,4},{3,5},{4,2},{5,3},{6,0},{7,1},{8,14},{9,15},{10,... | collective-permute-start | bytes 393224 | tf_op jit(solution)/shard_map/ppermute | solution.py:22
  14.1 5.6 %collective-permute-start.6 = (bf16[4,16,1024]{2,1,0:T(8,128)(2,1)S(1)}, bf16[4,16,1024]{2,1,0:T(8,128)(2,1)S(1)}, u32[]{:S(2)}, u32[]{:S(2)}) collective-permute-start(bf16[4,16,1024]{2,1,0:T(8,128)(2,1)S(1)} %stack.2.refs_0_), channel_id=1, source_target_pairs={{0,4},{1,5},{2,6},{3,7},{4,0},{5,1},{6,2},{7,3},{8,12},{9,13},{10,... | collective-permute-start | bytes 393224 | tf_op jit(solution)/shard_map/ppermute | solution.py:22
  14.6 6.3 %collective-permute-start.3 = (bf16[4,16,1024]{2,1,0:T(8,128)(2,1)S(1)}, bf16[4,16,1024]{2,1,0:T(8,128)(2,1)S(1)}, u32[]{:S(2)}, u32[]{:S(2)}) collective-permute-start(bf16[4,16,1024]{2,1,0:T(8,128)(2,1)S(1)} %stack.2.refs_0_), channel_id=1, source_target_pairs={{0,2},{1,3},{2,0},{3,1},{4,6},{5,7},{6,4},{7,5},{8,10},{9,11},{10,... | collective-permute-start | bytes 393224 | tf_op jit(solution)/shard_map/ppermute | solution.py:22
  18.3 2.7 %collective-permute-start.9 = (bf16[4,16,1024]{2,1,0:T(8,128)(2,1)S(1)}, bf16[4,16,1024]{2,1,0:T(8,128)(2,1)S(1)}, u32[]{:S(2)}, u32[]{:S(2)}) collective-permute-start(bf16[4,16,1024]{2,1,0:T(8,128)(2,1)S(1)} %collective-permute-done.7.refs_1_), channel_id=1, source_target_pairs={{0,1},{1,0},{2,3},{3,2},{4,5},{5,4},{6,7},{7,6},{8,9},{9,8},{10,11... | collective-permute-start | bytes 393224 | tf_op jit(solution)/shard_map/ppermute | solution.py:22
  19.7 1.3 %collective-permute-start.8 = (bf16[4,16,1024]{2,1,0:T(8,128)(2,1)S(1)}, bf16[4,16,1024]{2,1,0:T(8,128)(2,1)S(1)}, u32[]{:S(2)}, u32[]{:S(2)}) collective-permute-start(bf16[4,16,1024]{2,1,0:T(8,128)(2,1)S(1)} %collective-permute-done.6.refs_0_), channel_id=1, source_target_pairs={{0,1},{1,0},{2,3},{3,2},{4,5},{5,4},{6,7},{7,6},{8,9},{9,8},{10,11... | collective-permute-start | bytes 393224 | tf_op jit(solution)/shard_map/ppermute | solution.py:22
  20.3 2.7 %collective-permute-start.4 = (bf16[4,16,1024]{2,1,0:T(8,128)(2,1)S(1)}, bf16[4,16,1024]{2,1,0:T(8,128)(2,1)S(1)}, u32[]{:S(2)}, u32[]{:S(2)}) collective-permute-start(bf16[4,16,1024]{2,1,0:T(8,128)(2,1)S(1)} %stack.2.refs_0_), channel_id=1, source_target_pairs={{0,1},{1,0},{2,3},{3,2},{4,5},{5,4},{6,7},{7,6},{8,9},{9,8},{10,11... | collective-permute-start | bytes 393224 | tf_op jit(solution)/shard_map/ppermute | solution.py:22
  20.9 2.1 %collective-permute-start.5 = (bf16[4,16,1024]{2,1,0:T(8,128)(2,1)S(1)}, bf16[4,16,1024]{2,1,0:T(8,128)(2,1)S(1)}, u32[]{:S(2)}, u32[]{:S(2)}) collective-permute-start(bf16[4,16,1024]{2,1,0:T(8,128)(2,1)S(1)} %collective-permute-done.3.refs_1_), channel_id=1, source_target_pairs={{0,1},{1,0},{2,3},{3,2},{4,5},{5,4},{6,7},{7,6},{8,9},{9,8},{10,11... | collective-permute-start | bytes 393224 | tf_op jit(solution)/shard_map/ppermute | solution.py:22
  27.2 20.6 %copy-start = (bf16[1024,1024]{1,0:T(8,128)(2,1)S(1)}, bf16[1024,1024]{1,0:T(8,128)(2,1)}, u32[]{:S(2)}) copy-start(bf16[1024,1024]{1,0:T(8,128)(2,1)} %refs_3_.1) | copy-start | bytes 6291460
  27.2 31.7 %copy-start.1 = (f32[1024]{0:T(1024)S(1)}, f32[1024]{0:T(1024)}, u32[]{:S(2)}) copy-start(f32[1024]{0:T(1024)} %param.12) | copy-start | bytes 12292
  27.3 31.7 %copy-start.2 = (s32[1024]{0:T(1024)S(1)}, s32[1024]{0:T(1024)}, u32[]{:S(2)}) copy-start(s32[1024]{0:T(1024)} %param.13) | copy-start | bytes 12292
  27.3 1.7 %collective-permute-start.10 = (bf16[4,32,1152]{2,1,0:T(8,128)(2,1)S(1)}, bf16[4,32,1152]{2,1,0:T(8,128)(2,1)S(1)}, u32[]{:S(2)}, u32[]{:S(2)}) collective-permute-start(bf16[4,32,1152]{2,1,0:T(8,128)(2,1)S(1)} %get-tuple-element.55), channel_id=1, source_target_pairs={{0,1},{1,0},{2,3},{3,2},{4,5},{5,4},{6,7},{7,6},{8,9},{9,8},{10,11... | collective-permute-start | bytes 884744 | tf_op jit(solution)/shard_map/ppermute | solution.py:22
  29.3 2.4 %collective-permute-start.11 = (bf16[4,32,1152]{2,1,0:T(8,128)(2,1)S(1)}, bf16[4,32,1152]{2,1,0:T(8,128)(2,1)S(1)}, u32[]{:S(2)}, u32[]{:S(2)}) collective-permute-start(bf16[4,32,1152]{2,1,0:T(8,128)(2,1)S(1)} %get-tuple-element.57), channel_id=1, source_target_pairs={{0,1},{1,0},{2,3},{3,2},{4,5},{5,4},{6,7},{7,6},{8,9},{9,8},{10,11... | collective-permute-start | bytes 884744 | tf_op jit(solution)/shard_map/ppermute | solution.py:22
  29.7 7.6 %collective-permute-start.12 = (bf16[4,16,1152]{2,1,0:T(8,128)(2,1)S(1)}, bf16[4,16,1152]{2,1,0:T(8,128)(2,1)S(1)}, u32[]{:S(2)}, u32[]{:S(2)}) collective-permute-start(bf16[4,16,1152]{2,1,0:T(8,128)(2,1)S(1)} %get-tuple-element.59), channel_id=1, source_target_pairs={{0,6},{1,7},{2,4},{3,5},{4,2},{5,3},{6,0},{7,1},{8,14},{9,15},{10,... | collective-permute-start | bytes 442376 | tf_op jit(solution)/shard_map/ppermute | solution.py:22
  31.1 7.6 %collective-permute-start.13 = (bf16[4,16,1152]{2,1,0:T(8,128)(2,1)S(1)}, bf16[4,16,1152]{2,1,0:T(8,128)(2,1)S(1)}, u32[]{:S(2)}, u32[]{:S(2)}) collective-permute-start(bf16[4,16,1152]{2,1,0:T(8,128)(2,1)S(1)} %get-tuple-element.60), channel_id=1, source_target_pairs={{0,4},{1,5},{2,6},{3,7},{4,0},{5,1},{6,2},{7,3},{8,12},{9,13},{10,... | collective-permute-start | bytes 442376 | tf_op jit(solution)/shard_map/ppermute | solution.py:22
  32.0 7.7 %collective-permute-start.14 = (bf16[4,16,1152]{2,1,0:T(8,128)(2,1)S(1)}, bf16[4,16,1152]{2,1,0:T(8,128)(2,1)S(1)}, u32[]{:S(2)}, u32[]{:S(2)}) collective-permute-start(bf16[4,16,1152]{2,1,0:T(8,128)(2,1)S(1)} %get-tuple-element.61), channel_id=1, source_target_pairs={{0,2},{1,3},{2,0},{3,1},{4,6},{5,7},{6,4},{7,5},{8,10},{9,11},{10,... | collective-permute-start | bytes 442376 | tf_op jit(solution)/shard_map/ppermute | solution.py:22
  40.0 5.9 %collective-permute-start.15 = (bf16[1,16,1152]{2,1,0:T(8,128)(2,1)S(1)}, bf16[1,16,1152]{2,1,0:T(8,128)(2,1)S(1)}, u32[]{:S(2)}, u32[]{:S(2)}) collective-permute-start(bf16[1,16,1152]{2,1,0:T(8,128)(2,1)S(1)} %get-tuple-element.64), channel_id=1, source_target_pairs={{0,24},{1,25},{2,26},{3,27},{4,28},{5,29},{6,30},{7,31},{8,16},{9,... | collective-permute-start | bytes 110600 | tf_op jit(solution)/shard_map/ppermute | solution.py:22
  42.7 5.2 %collective-permute-start.16 = (bf16[1,16,1152]{2,1,0:T(8,128)(2,1)S(1)}, bf16[1,16,1152]{2,1,0:T(8,128)(2,1)S(1)}, u32[]{:S(2)}, u32[]{:S(2)}) collective-permute-start(bf16[1,16,1152]{2,1,0:T(8,128)(2,1)S(1)} %get-tuple-element.65), channel_id=1, source_target_pairs={{0,16},{1,17},{2,18},{3,19},{4,20},{5,21},{6,22},{7,23},{8,24},{9,... | collective-permute-start | bytes 110600 | tf_op jit(solution)/shard_map/ppermute | solution.py:22
  43.0 4.8 %collective-permute-start.17 = (bf16[1,16,1152]{2,1,0:T(8,128)(2,1)S(1)}, bf16[1,16,1152]{2,1,0:T(8,128)(2,1)S(1)}, u32[]{:S(2)}, u32[]{:S(2)}) collective-permute-start(bf16[1,16,1152]{2,1,0:T(8,128)(2,1)S(1)} %get-tuple-element.66), channel_id=1, source_target_pairs={{0,8},{1,9},{2,10},{3,11},{4,12},{5,13},{6,14},{7,15},{8,0},{9,1},... | collective-permute-start | bytes 110600 | tf_op jit(solution)/shard_map/ppermute | solution.py:22
  48.5 5.5 %collective-permute-start.20 = (f32[2,1024]{1,0:T(2,128)S(1)}, f32[2,1024]{1,0:T(2,128)S(1)}, u32[]{:S(2)}, u32[]{:S(2)}) collective-permute-start(f32[2,1024]{1,0:T(2,128)S(1)} %get-tuple-element.69.refs_0_), channel_id=1, source_target_pairs={{0,24},{1,25},{2,26},{3,27},{4,28},{5,29},{6,30},{7,31},{8,16},{9,... | collective-permute-start | bytes 24584 | tf_op jit(solution)/shard_map/ppermute | solution.py:22
  50.7 4.5 %collective-permute-start.19 = (f32[2,1024]{1,0:T(2,128)S(1)}, f32[2,1024]{1,0:T(2,128)S(1)}, u32[]{:S(2)}, u32[]{:S(2)}) collective-permute-start(f32[2,1024]{1,0:T(2,128)S(1)} %get-tuple-element.69.refs_0_), channel_id=1, source_target_pairs={{0,16},{1,17},{2,18},{3,19},{4,20},{5,21},{6,22},{7,23},{8,24},{9,... | collective-permute-start | bytes 24584 | tf_op jit(solution)/shard_map/ppermute | solution.py:22
  50.7 4.5 %collective-permute-start.18 = (f32[2,1024]{1,0:T(2,128)S(1)}, f32[2,1024]{1,0:T(2,128)S(1)}, u32[]{:S(2)}, u32[]{:S(2)}) collective-permute-start(f32[2,1024]{1,0:T(2,128)S(1)} %get-tuple-element.69.refs_0_), channel_id=1, source_target_pairs={{0,8},{1,9},{2,10},{3,11},{4,12},{5,13},{6,14},{7,15},{8,0},{9,1},... | collective-permute-start | bytes 24584 | tf_op jit(solution)/shard_map/ppermute | solution.py:22
  55.2 3.7 %collective-permute-start.21 = (f32[2,1024]{1,0:T(2,128)S(1)}, f32[2,1024]{1,0:T(2,128)S(1)}, u32[]{:S(2)}, u32[]{:S(2)}) collective-permute-start(f32[2,1024]{1,0:T(2,128)S(1)} %tree_sum.1.sums_ref), channel_id=1, source_target_pairs={{0,4},{1,5},{2,6},{3,7},{4,0},{5,1},{6,2},{7,3},{8,12},{9,13},{10,... | collective-permute-start | bytes 24584 | tf_op jit(solution)/shard_map/ppermute | solution.py:22
  60.2 5.8 %collective-permute-start.24 = (bf16[16,1152]{1,0:T(8,128)(2,1)S(1)}, bf16[16,1152]{1,0:T(8,128)(2,1)S(1)}, u32[]{:S(2)}, u32[]{:S(2)}) collective-permute-start(bf16[16,1152]{1,0:T(8,128)(2,1)S(1)} %get-tuple-element.72.refs_0_), channel_id=1, source_target_pairs={{0,24},{1,25},{2,26},{3,27},{4,28},{5,29},{6,30},{7,31},{8,16},{9,... | collective-permute-start | bytes 110600 | tf_op jit(solution)/shard_map/ppermute | solution.py:22
  61.9 5.3 %collective-permute-start.23 = (bf16[16,1152]{1,0:T(8,128)(2,1)S(1)}, bf16[16,1152]{1,0:T(8,128)(2,1)S(1)}, u32[]{:S(2)}, u32[]{:S(2)}) collective-permute-start(bf16[16,1152]{1,0:T(8,128)(2,1)S(1)} %get-tuple-element.72.refs_0_), channel_id=1, source_target_pairs={{0,16},{1,17},{2,18},{3,19},{4,20},{5,21},{6,22},{7,23},{8,24},{9,... | collective-permute-start | bytes 110600 | tf_op jit(solution)/shard_map/ppermute | solution.py:22
  62.9 4.2 %collective-permute-start.22 = (bf16[16,1152]{1,0:T(8,128)(2,1)S(1)}, bf16[16,1152]{1,0:T(8,128)(2,1)S(1)}, u32[]{:S(2)}, u32[]{:S(2)}) collective-permute-start(bf16[16,1152]{1,0:T(8,128)(2,1)S(1)} %get-tuple-element.72.refs_0_), channel_id=1, source_target_pairs={{0,8},{1,9},{2,10},{3,11},{4,12},{5,13},{6,14},{7,15},{8,0},{9,1},... | collective-permute-start | bytes 110600 | tf_op jit(solution)/shard_map/ppermute | solution.py:22
  67.2 6.1 %collective-permute-start.29 = (bf16[4,16,1152]{2,1,0:T(8,128)(2,1)S(1)}, bf16[4,16,1152]{2,1,0:T(8,128)(2,1)S(1)}, u32[]{:S(2)}, u32[]{:S(2)}) collective-permute-start(bf16[4,16,1152]{2,1,0:T(8,128)(2,1)S(1)} %stack.3.refs_0_), channel_id=1, source_target_pairs={{0,6},{1,7},{2,4},{3,5},{4,2},{5,3},{6,0},{7,1},{8,14},{9,15},{10,... | collective-permute-start | bytes 442376 | tf_op jit(solution)/shard_map/ppermute | solution.py:22
  68.7 5.3 %collective-permute-start.28 = (bf16[4,16,1152]{2,1,0:T(8,128)(2,1)S(1)}, bf16[4,16,1152]{2,1,0:T(8,128)(2,1)S(1)}, u32[]{:S(2)}, u32[]{:S(2)}) collective-permute-start(bf16[4,16,1152]{2,1,0:T(8,128)(2,1)S(1)} %stack.3.refs_0_), channel_id=1, source_target_pairs={{0,4},{1,5},{2,6},{3,7},{4,0},{5,1},{6,2},{7,3},{8,12},{9,13},{10,... | collective-permute-start | bytes 442376 | tf_op jit(solution)/shard_map/ppermute | solution.py:22
  69.3 5.5 %collective-permute-start.25 = (bf16[4,16,1152]{2,1,0:T(8,128)(2,1)S(1)}, bf16[4,16,1152]{2,1,0:T(8,128)(2,1)S(1)}, u32[]{:S(2)}, u32[]{:S(2)}) collective-permute-start(bf16[4,16,1152]{2,1,0:T(8,128)(2,1)S(1)} %stack.3.refs_0_), channel_id=1, source_target_pairs={{0,2},{1,3},{2,0},{3,1},{4,6},{5,7},{6,4},{7,5},{8,10},{9,11},{10,... | collective-permute-start | bytes 442376 | tf_op jit(solution)/shard_map/ppermute | solution.py:22
  73.3 1.5 %collective-permute-start.31 = (bf16[4,16,1152]{2,1,0:T(8,128)(2,1)S(1)}, bf16[4,16,1152]{2,1,0:T(8,128)(2,1)S(1)}, u32[]{:S(2)}, u32[]{:S(2)}) collective-permute-start(bf16[4,16,1152]{2,1,0:T(8,128)(2,1)S(1)} %collective-permute-done.29.refs_1_), channel_id=1, source_target_pairs={{0,1},{1,0},{2,3},{3,2},{4,5},{5,4},{6,7},{7,6},{8,9},{9,8},{10,11... | collective-permute-start | bytes 442376 | tf_op jit(solution)/shard_map/ppermute | solution.py:22
  74.0 1.4 %collective-permute-start.30 = (bf16[4,16,1152]{2,1,0:T(8,128)(2,1)S(1)}, bf16[4,16,1152]{2,1,0:T(8,128)(2,1)S(1)}, u32[]{:S(2)}, u32[]{:S(2)}) collective-permute-start(bf16[4,16,1152]{2,1,0:T(8,128)(2,1)S(1)} %collective-permute-done.28.refs_0_), channel_id=1, source_target_pairs={{0,1},{1,0},{2,3},{3,2},{4,5},{5,4},{6,7},{7,6},{8,9},{9,8},{10,11... | collective-permute-start | bytes 442376 | tf_op jit(solution)/shard_map/ppermute | solution.py:22
  74.0 3.4 %collective-permute-start.26 = (bf16[4,16,1152]{2,1,0:T(8,128)(2,1)S(1)}, bf16[4,16,1152]{2,1,0:T(8,128)(2,1)S(1)}, u32[]{:S(2)}, u32[]{:S(2)}) collective-permute-start(bf16[4,16,1152]{2,1,0:T(8,128)(2,1)S(1)} %stack.3.refs_0_), channel_id=1, source_target_pairs={{0,1},{1,0},{2,3},{3,2},{4,5},{5,4},{6,7},{7,6},{8,9},{9,8},{10,11... | collective-permute-start | bytes 442376 | tf_op jit(solution)/shard_map/ppermute | solution.py:22
  74.8 2.6 %collective-permute-start.27 = (bf16[4,16,1152]{2,1,0:T(8,128)(2,1)S(1)}, bf16[4,16,1152]{2,1,0:T(8,128)(2,1)S(1)}, u32[]{:S(2)}, u32[]{:S(2)}) collective-permute-start(bf16[4,16,1152]{2,1,0:T(8,128)(2,1)S(1)} %collective-permute-done.25.refs_1_), channel_id=1, source_target_pairs={{0,1},{1,0},{2,3},{3,2},{4,5},{5,4},{6,7},{7,6},{8,9},{9,8},{10,11... | collective-permute-start | bytes 442376 | tf_op jit(solution)/shard_map/ppermute | solution.py:22
  81.5 1.6 %collective-permute-start.32 = (bf16[4,32,1024]{2,1,0:T(8,128)(2,1)S(1)}, bf16[4,32,1024]{2,1,0:T(8,128)(2,1)S(1)}, u32[]{:S(2)}, u32[]{:S(2)}) collective-permute-start(bf16[4,32,1024]{2,1,0:T(8,128)(2,1)S(1)} %get-tuple-element.78), channel_id=1, source_target_pairs={{0,1},{1,0},{2,3},{3,2},{4,5},{5,4},{6,7},{7,6},{8,9},{9,8},{10,11... | collective-permute-start | bytes 786440 | tf_op jit(solution)/shard_map/ppermute | solution.py:22
  83.1 3.1 %collective-permute-start.33 = (bf16[4,32,1024]{2,1,0:T(8,128)(2,1)S(1)}, bf16[4,32,1024]{2,1,0:T(8,128)(2,1)S(1)}, u32[]{:S(2)}, u32[]{:S(2)}) collective-permute-start(bf16[4,32,1024]{2,1,0:T(8,128)(2,1)S(1)} %get-tuple-element.80), channel_id=1, source_target_pairs={{0,1},{1,0},{2,3},{3,2},{4,5},{5,4},{6,7},{7,6},{8,9},{9,8},{10,11... | collective-permute-start | bytes 786440 | tf_op jit(solution)/shard_map/ppermute | solution.py:22
  83.4 7.2 %collective-permute-start.34 = (bf16[4,16,1024]{2,1,0:T(8,128)(2,1)S(1)}, bf16[4,16,1024]{2,1,0:T(8,128)(2,1)S(1)}, u32[]{:S(2)}, u32[]{:S(2)}) collective-permute-start(bf16[4,16,1024]{2,1,0:T(8,128)(2,1)S(1)} %get-tuple-element.82), channel_id=1, source_target_pairs={{0,6},{1,7},{2,4},{3,5},{4,2},{5,3},{6,0},{7,1},{8,14},{9,15},{10,... | collective-permute-start | bytes 393224 | tf_op jit(solution)/shard_map/ppermute | solution.py:22
  85.7 7.0 %collective-permute-start.35 = (bf16[4,16,1024]{2,1,0:T(8,128)(2,1)S(1)}, bf16[4,16,1024]{2,1,0:T(8,128)(2,1)S(1)}, u32[]{:S(2)}, u32[]{:S(2)}) collective-permute-start(bf16[4,16,1024]{2,1,0:T(8,128)(2,1)S(1)} %get-tuple-element.83), channel_id=1, source_target_pairs={{0,4},{1,5},{2,6},{3,7},{4,0},{5,1},{6,2},{7,3},{8,12},{9,13},{10,... | collective-permute-start | bytes 393224 | tf_op jit(solution)/shard_map/ppermute | solution.py:22
  86.3 6.5 %collective-permute-start.36 = (bf16[4,16,1024]{2,1,0:T(8,128)(2,1)S(1)}, bf16[4,16,1024]{2,1,0:T(8,128)(2,1)S(1)}, u32[]{:S(2)}, u32[]{:S(2)}) collective-permute-start(bf16[4,16,1024]{2,1,0:T(8,128)(2,1)S(1)} %get-tuple-element.84), channel_id=1, source_target_pairs={{0,2},{1,3},{2,0},{3,1},{4,6},{5,7},{6,4},{7,5},{8,10},{9,11},{10,... | collective-permute-start | bytes 393224 | tf_op jit(solution)/shard_map/ppermute | solution.py:22
  92.9 7.4 %collective-permute-start.37 = (bf16[1,16,1024]{2,1,0:T(8,128)(2,1)S(1)}, bf16[1,16,1024]{2,1,0:T(8,128)(2,1)S(1)}, u32[]{:S(2)}, u32[]{:S(2)}) collective-permute-start(bf16[1,16,1024]{2,1,0:T(8,128)(2,1)S(1)} %get-tuple-element.86), channel_id=1, source_target_pairs={{0,24},{1,25},{2,26},{3,27},{4,28},{5,29},{6,30},{7,31},{8,16},{9,... | collective-permute-start | bytes 98312 | tf_op jit(solution)/shard_map/ppermute | solution.py:22
  95.1 5.1 %collective-permute-start.38 = (bf16[1,16,1024]{2,1,0:T(8,128)(2,1)S(1)}, bf16[1,16,1024]{2,1,0:T(8,128)(2,1)S(1)}, u32[]{:S(2)}, u32[]{:S(2)}) collective-permute-start(bf16[1,16,1024]{2,1,0:T(8,128)(2,1)S(1)} %get-tuple-element.87), channel_id=1, source_target_pairs={{0,16},{1,17},{2,18},{3,19},{4,20},{5,21},{6,22},{7,23},{8,24},{9,... | collective-permute-start | bytes 98312 | tf_op jit(solution)/shard_map/ppermute | solution.py:22
  95.7 4.6 %collective-permute-start.39 = (bf16[1,16,1024]{2,1,0:T(8,128)(2,1)S(1)}, bf16[1,16,1024]{2,1,0:T(8,128)(2,1)S(1)}, u32[]{:S(2)}, u32[]{:S(2)}) collective-permute-start(bf16[1,16,1024]{2,1,0:T(8,128)(2,1)S(1)} %get-tuple-element.88), channel_id=1, source_target_pairs={{0,8},{1,9},{2,10},{3,11},{4,12},{5,13},{6,14},{7,15},{8,0},{9,1},... | collective-permute-start | bytes 98312 | tf_op jit(solution)/shard_map/ppermute | solution.py:22

commit v11 on v10

--- a/solution.py
+++ b/solution.py
@@ -91,57 +91,87 @@
     return block[:, at : at + 1] + (block[:, at + 1 : at + 2] + block[:, at + 2 : at + 3])
 
 
-def load_kernel(tokens_ref, *refs):
-    count = (len(refs) - 3) // 2
-    others, halves, copies_of, sems = refs[:count], refs[count : count + 2], refs[count + 2 : -1], refs[-1]
-    blocks, _, width = halves[0].shape
-    copies = [pltpu.make_async_copy(src, dst, sems.at[i]) for i, (src, dst) in enumerate(zip(others, copies_of))]
-    for i in range(2):
-        for j in range(blocks):
-            start = pl.multiple_of((lax.axis_index("ctx") ^ i ^ (2 * j)) * width, LANES)
-            sem = sems.at[count + i * blocks + j]
-            copies.append(pltpu.make_async_copy(tokens_ref.at[:, pl.ds(start, width)], halves[i].at[j], sem))
+def token_copies(tokens_ref, held_ref, sems, half, first):
+    blocks, _, width = held_ref.shape
+    copies = []
+    for j in range(blocks):
+        start = pl.multiple_of((lax.axis_index("ctx") ^ half ^ (2 * (first + j))) * width, LANES)
+        copies.append(pltpu.make_async_copy(tokens_ref.at[:, pl.ds(start, width)], held_ref.at[j], sems.at[j]))
+    return copies
+
+
+def load_kernel(*refs):
+    tokens_ref, queries_ref, gain_ref, length_ref, a_ref, b_ref, here_ref, gain_here_ref, length_out_ref = refs[:9]
+    sems_a, sems_b, sems = refs[9:]
+    copies = [
+        pltpu.make_async_copy(queries_ref, here_ref, sems.at[0]),
+        pltpu.make_async_copy(gain_ref, gain_here_ref, sems.at[1]),
+        *token_copies(tokens_ref, a_ref, sems_a, 0, 0),
+        *token_copies(tokens_ref, b_ref, sems_b, 1, 0),
+    ]
     for copy in copies:
         copy.start()
+    length_out_ref[...] = jnp.full(length_out_ref.shape, length_ref[0], jnp.int32)
     for copy in copies:
         copy.wait()
 
 
-def load(width, tokens, *others):
+def in_vmem(kernel, outs, name, hbm_args, other_args, other_space, scratch):
+    specs = [pl.BlockSpec(memory_space=pltpu.HBM)] * len(hbm_args)
+    run = pl.pallas_call(
+        kernel,
+        out_shape=[pltpu.VMEM(*out) for out in outs],
+        in_specs=specs + [pl.BlockSpec(memory_space=other_space)] * len(other_args),
+        out_specs=[pl.BlockSpec(memory_space=pltpu.VMEM)] * len(outs),
+        scratch_shapes=scratch,
+        compiler_params=pltpu.CompilerParams(vmem_limit_bytes=16 * MIB),
+        name=name,
+    )
+    return run(*[pltpu.with_memory_space_constraint(x, pltpu.HBM) for x in hbm_args], *other_args)
+
+
+def load(width, tokens, queries, gain, length):
     rows, full_width = tokens.shape
     blocks = full_width // width // 2
-    outs = [pltpu.VMEM((blocks, rows, width), tokens.dtype)] * 2 + [pltpu.VMEM(x.shape, x.dtype) for x in others]
-    run = pl.pallas_call(
-        load_kernel,
-        out_shape=outs,
-        in_specs=[pl.BlockSpec(memory_space=pltpu.HBM)] * (1 + len(others)),
-        out_specs=[pl.BlockSpec(memory_space=pltpu.VMEM)] * len(outs),
-        scratch_shapes=[pltpu.SemaphoreType.DMA((2 * blocks + len(others),))],
-        compiler_params=pltpu.CompilerParams(vmem_limit_bytes=16 * MIB),
-        name="load",
-    )
-    return run(*[pltpu.with_memory_space_constraint(x, pltpu.HBM) for x in (tokens, *others)])
-
-
-def project(parts, held_ref, tile=256):
-    blocks, token_count, width = held_ref.shape
+    now = blocks - blocks // 2
+    outs = [((blocks, rows, width), BF16), ((now, rows, width), BF16), (queries.shape, BF16), (gain.shape, F32)]
+    dma = pltpu.SemaphoreType.DMA
+    scratch = [dma((blocks,)), dma((now,)), dma((2,))]
+    outs.append(((1, LANES), jnp.int32))
+    return in_vmem(load_kernel, outs, "load", [tokens, queries, gain], [length], pltpu.SMEM, scratch)
+
+
+def project_load_kernel(first, count, tokens_ref, *refs):
+    parts, (held_ref, out_ref, rest_ref, sems) = refs[:count], refs[count:]
+    copies = token_copies(tokens_ref, rest_ref, sems, 1, first)
+    for copy in copies:
+        copy.start()
+    out_ref[...] = project(parts, [held_ref])
+    for copy in copies:
+        copy.wait()
+
+
+def project(parts, held, tile=256):
+    blocks = [(ref, j) for ref in held for j in range(ref.shape[0])]
+    _, token_count, width = held[0].shape
     tiles = []
     for at in range(0, token_count, tile):
         total = None
-        for j in range(blocks):
-            left = jnp.concatenate([ref[j] for ref in parts], axis=0)[:, :width]
-            block = held_ref[j, at : at + tile, :]
+        for j, (ref, own) in enumerate(blocks):
+            left = jnp.concatenate([part[j] for part in parts], axis=0)[:, :width]
+            block = ref[own, at : at + tile, :]
             part = lax.dot_general(left, block, (((1,), (1,)), ((), ())), preferred_element_type=F32)
             total = part if total is None else total + part
         tiles.append(total)
     return jnp.concatenate(tiles, axis=1)
 
 
-def spread(left, held_ref, keep_ref, send_ref, extra, tile=256):
-    blocks, half, width = keep_ref.shape
-    for j in range(blocks):
+def spread(left, held, keep_ref, send_ref, extra, tile=256):
+    blocks = [(ref, j) for ref in held for j in range(ref.shape[0])]
+    _, half, width = keep_ref.shape
+    for j, (ref, own) in enumerate(blocks):
         for at in range(0, width, tile):
-            part = jnp.dot(left, held_ref[j, :, at : at + tile], preferred_element_type=F32)
+            part = jnp.dot(left, ref[own, :, at : at + tile], preferred_element_type=F32)
             keep_ref[j, :, at : at + tile] = part[:half]
             send_ref[j, :, at : at + tile] = part[half:].astype(BF16)
         if extra is not None:
@@ -149,7 +179,7 @@
 
 
 def project_kernel(count, *refs):
-    refs[-1][...] = project(refs[:count], refs[count])
+    refs[-1][...] = project(refs[:count], [refs[count]])
 
 
 def peak_lanes(peak, half):
@@ -157,40 +187,40 @@
 
 
 def pool_kernel(count, length_ref, *refs):
-    parts, refs = refs[:count], refs[count:]
-    part_ref, held_ref, spread_ref, keep_ref, send_ref, peak_ref, w_ref, left_ref = refs
-    scores = part_ref[...] + project(parts, held_ref)
+    parts, held, refs = refs[:count], refs[count : count + 2], refs[count + 2 :]
+    part_ref, keep_ref, send_ref, peak_ref, w_ref, left_ref = refs
+    scores = part_ref[...] + project(parts, held)
     shard = lax.axis_index("ctx") * lax.axis_size("cls") + lax.axis_index("cls")
-    valid = lax.broadcasted_iota(jnp.int32, scores.shape, 1) < length_ref[0] - shard * scores.shape[1]
+    valid = lax.broadcasted_iota(jnp.int32, scores.shape, 1) < length_ref[:, :1] - shard * scores.shape[1]
     peak = jnp.max(jnp.where(valid, scores, MASKED), axis=1, keepdims=True)
     weights = jnp.where(valid, jnp.exp(scores - peak), 0.0)
     left = weights.astype(BF16)
     w_ref[...] = weights
     left_ref[...] = left
     peak_ref[...] = jnp.broadcast_to(peak, peak_ref.shape)
-    spread(left, spread_ref, keep_ref, send_ref, peak_lanes(peak, keep_ref.shape[1]))
+    spread(left, held, keep_ref, send_ref, peak_lanes(peak, keep_ref.shape[1]))
 
 
 def pool_rest_kernel(left_ref, peak_ref, held_ref, keep_ref, send_ref):
-    spread(left_ref[...], held_ref, keep_ref, send_ref, peak_lanes(peak_ref[...], keep_ref.shape[1]))
+    spread(left_ref[...], [held_ref], keep_ref, send_ref, peak_lanes(peak_ref[...], keep_ref.shape[1]))
 
 
 def grad_kernel(scale, count, *refs):
-    parts, refs = refs[:count], refs[count:]
-    part_ref, held_ref, spread_ref, w_ref, peak_ref, keep_ref, send_ref, left_ref, loss_ref = refs
-    width = held_ref.shape[2]
-    projected = part_ref[...] + project(parts, held_ref)
+    parts, held, refs = refs[:count], refs[count : count + 2], refs[count + 2 :]
+    part_ref, w_ref, peak_ref, keep_ref, send_ref, left_ref, loss_ref = refs
+    width = held[0].shape[2]
+    projected = part_ref[...] + project(parts, held)
     blocks = [ref[0] for ref in parts]
     top = jnp.concatenate([from_lanes(block, width, 0) for block in blocks], axis=0)
     weights = w_ref[...] * jnp.exp(peak_ref[:, :1] - top)
     left = (weights * projected).astype(BF16)
     left_ref[...] = left
-    spread(left, spread_ref, keep_ref, send_ref, None)
+    spread(left, held, keep_ref, send_ref, None)
     loss_ref[...] = tree_sum([from_lanes(block, width, 1)[:1] for block in blocks]) * scale
 
 
 def grad_rest_kernel(left_ref, held_ref, keep_ref, send_ref):
-    spread(left_ref[...], held_ref, keep_ref, send_ref, None)
+    spread(left_ref[...], [held_ref], keep_ref, send_ref, None)
 
 
 def rescaling(peak, received, width):
@@ -394,18 +424,24 @@
     product = ((heads, token_count), F32)
     cost = pl.CostEstimate(flops=256 * token_count * full_width, bytes_accessed=0, transcendentals=0)
 
-    def project_half(parts):
-        return call(functools.partial(project_kernel, len(parts)), [product], "project", [*parts, held_b], cost=cost)[0]
-
-    held_a, held_b, queries_here, gain = load(width, tokens, queries, norm_gain[None, :])
+    held_a, held_b, queries_here, gain, length = load(width, tokens, queries, norm_gain[None, :], doc_length)
     first, second = gather(queries, queries_here)
-    part = project_half(second)
+    now = held_b.shape[0]
+    rest = (blocks - now, token_count, width)
+    part, held_c = in_vmem(
+        functools.partial(project_load_kernel, now, classes),
+        [product, (rest, BF16)],
+        "project_load",
+        [tokens],
+        [*first, held_a],
+        pltpu.VMEM,
+        [pltpu.SemaphoreType.DMA((blocks - now,))],
+    )
     keep_b, send_b, own_peak, weights, left = call(
         functools.partial(pool_kernel, classes),
         [*pair, ((heads, LANES), F32), product, ((heads, token_count), BF16)],
         "pool",
-        [doc_length, *first, part, held_a, held_b],
-        smem_args=(0,),
+        [length, *second, held_b, held_c, part],
         cost=cost,
     )
     half_a = call(pool_rest_kernel, pair, "pool_rest", [left, own_peak, held_a], cost=cost)
@@ -426,13 +462,15 @@
     )
     head_grad = head_weight_grad(normed, bias_grad_here)
     first, second = gather(pooled_grad)
-    part = project_half(second)
+    (part,) = call(
+        functools.partial(project_kernel, classes), [product], "project", [*first, held_a], cost=cost
+    )
     pair = [((blocks, half, width), F32), ((blocks, half, width), BF16)]
     keep_b, send_b, left, loss = call(
         functools.partial(grad_kernel, 1.0 / (columns * classes), classes),
         [*pair, ((heads, token_count), BF16), ((1, 1), F32)],
         "grad",
-        [*first, part, held_a, held_b, weights, own_peak],
+        [*second, held_b, held_c, part, weights, own_peak],
         cost=cost,
     )
     half_a = call(grad_rest_kernel, pair, "grad_rest", [left, held_a], cost=cost)

time: 101 us -> 102 us (level)
    pallas_call x1 -> x2, Pallas kernels: 4.79 us -> 7.63 us  [in_vmem(): run(*[pltpu.with_memory_space_constraint(x, pltpu.HBM) for x in hbm_args]...]
    pallas_call x18 -> x17, Pallas kernels: 18.2 us -> 16.2 us  [call(): return list(run(*args))]
  transfers between devices with their start and end apart: 40 -> 40, of which waited for: 21 -> 20; matrix products, arithmetic and copies ran while one was open for 0% -> 0% of each run, Pallas kernels for 14% -> 15%
where the time goes in v11:
time: 102 us
  starting transfers between devices  41.2 us (40%)
  waiting for transfers between devices  32.4 us (32%)
  Pallas kernels  26.8 us (26%)
  between operations  1.49 us (1%)
    ppermute x40, starting transfers between devices, swap(): return lax.ppermute(x, ('ctx', 'cls'), pairs)  41.2 us
    ppermute x40, waiting for transfers between devices, swap(): return lax.ppermute(x, ('ctx', 'cls'), pairs)  32.4 us
    pallas_call x17, Pallas kernels, call(): return list(run(*args))  16.2 us
    pallas_call x2, Pallas kernels, in_vmem(): run(*[pltpu.with_memory_space_constraint(x, pltpu.HBM) for x in hbm_args]...  7.63 us
    pallas_call x1, Pallas kernels, head_weight_grad(): pl.pallas_call(functools.partial(head_weight_grad_kernel, columns // rows...  2.95 us
  transfers between devices with their start and end apart: 40, of which 20 were waited for; matrix products, arithmetic and copies ran while one was open for 0% of the time, Pallas kernels for 15%

profile of v11, /device:TPU:0, one launch (start us, length us, event | category | flops | bytes accessed | tf_op | source)
XLA Modules:
  0.0 101.8 jit_solution(3818633447588420544)
XLA Ops:
  0.6 3.1 %collective-permute-start = (bf16[16,1024]{1,0:T(8,128)(2,1)}, bf16[16,1024]{1,0:T(8,128)(2,1)S(1)}, u32[]{:S(2)}, u32[]{:S(2)}) collective-permute-start(bf16[16,1024]{1,0:T(8,128)(2,1)} %refs_1_.1), channel_id=1, source_target_pairs={{0,8},{1,9},{2,10},{3,11},{4,12},{5,13},{6,14},{7,15},{8,0},{9,1},... | collective-permute-start | bytes 98312 | tf_op jit(solution)/shard_map/ppermute | solution.py:22
  3.7 2.5 %collective-permute-start.2 = (bf16[16,1024]{1,0:T(8,128)(2,1)}, bf16[16,1024]{1,0:T(8,128)(2,1)S(1)}, u32[]{:S(2)}, u32[]{:S(2)}) collective-permute-start(bf16[16,1024]{1,0:T(8,128)(2,1)} %refs_1_.1), channel_id=1, source_target_pairs={{0,24},{1,25},{2,26},{3,27},{4,28},{5,29},{6,30},{7,31},{8,16},{9,... | collective-permute-start | bytes 98312 | tf_op jit(solution)/shard_map/ppermute | solution.py:22
  7.0 3.9 %load.1 = (bf16[4,768,1024]{2,1,0:T(8,128)(2,1)S(1)}, bf16[2,768,1024]{2,1,0:T(8,128)(2,1)S(1)}, bf16[16,1024]{1,0:T(8,128)(2,1)S(1)}, f32[1,1024]{1,0:T(1,128)S(1)}, s32[1,128]{1,0:T(1,128)S(1)}) custom-call(bf16[768,8192]{1,0:T(8,128)(2,1)} %tokens_ref.1, bf16[16,1024]{1,0:T(8,128)(2,1)} %refs_1_.1, f32[1,1024]{1,0:T(1,128)} %bitcast.7, s32[1]{0:T(128)S(6)} %copy.15.refs_3_), custom_call_target="tpu_custom_call" | custom-call | tf_op jit(solution)/shard_map/load/pallas_call | solution.py:130
  10.9 0.7 collective-permute-done.1.refs_2_
  11.6 1.6 %collective-permute-start.7 = (bf16[4,16,1024]{2,1,0:T(8,128)(2,1)S(1)}, bf16[4,16,1024]{2,1,0:T(8,128)(2,1)S(1)}, u32[]{:S(2)}, u32[]{:S(2)}) collective-permute-start(bf16[4,16,1024]{2,1,0:T(8,128)(2,1)S(1)} %stack.2.refs_0_), channel_id=1, source_target_pairs={{0,2},{1,3},{2,0},{3,1},{4,6},{5,7},{6,4},{7,5},{8,10},{9,11},{10,... | collective-permute-start | bytes 393224 | tf_op jit(solution)/shard_map/ppermute | solution.py:22
  13.2 1.4 %collective-permute-start.4 = (bf16[4,16,1024]{2,1,0:T(8,128)(2,1)S(1)}, bf16[4,16,1024]{2,1,0:T(8,128)(2,1)S(1)}, u32[]{:S(2)}, u32[]{:S(2)}) collective-permute-start(bf16[4,16,1024]{2,1,0:T(8,128)(2,1)S(1)} %stack.2.refs_0_), channel_id=1, source_target_pairs={{0,6},{1,7},{2,4},{3,5},{4,2},{5,3},{6,0},{7,1},{8,14},{9,15},{10,... | collective-permute-start | bytes 393224 | tf_op jit(solution)/shard_map/ppermute | solution.py:22
  15.1 2.7 %collective-permute-done.7.refs_1_ = bf16[4,16,1024]{2,1,0:T(8,128)(2,1)S(1)} collective-permute-done((bf16[4,16,1024]{2,1,0:T(8,128)(2,1)S(1)}, bf16[4,16,1024]{2,1,0:T(8,128)(2,1)S(1)}, u32[]{:S(2)}, u32[]{:S(2)}) %collective-permute-start.7) | collective-permute-done | bytes 131104 | tf_op jit(solution)/shard_map/ppermute | solution.py:22
  17.9 1.3 %collective-permute-done.4.refs_1_ = bf16[4,16,1024]{2,1,0:T(8,128)(2,1)S(1)} collective-permute-done((bf16[4,16,1024]{2,1,0:T(8,128)(2,1)S(1)}, bf16[4,16,1024]{2,1,0:T(8,128)(2,1)S(1)}, u32[]{:S(2)}, u32[]{:S(2)}) %collective-permute-start.4) | collective-permute-done | bytes 131104 | tf_op jit(solution)/shard_map/ppermute | solution.py:22
  19.7 3.8 %project_load.1 = (f32[64,768]{1,0:T(8,128)S(1)}, bf16[2,768,1024]{2,1,0:T(8,128)(2,1)S(1)}) custom-call(bf16[768,8192]{1,0:T(8,128)(2,1)} %tokens_ref.1, bf16[4,16,1024]{2,1,0:T(8,128)(2,1)S(1)} %stack.2.refs_0_, bf16[4,16,1024]{2,1,0:T(8,128)(2,1)S(1)} %collective-permute-done.7.refs_1_, bf16[4,16,1024]{2,1,0:T(8,128)(2,1)S(1)} %collective-permute-done.8.refs_2_, ...), custom_call_target="tpu_custom_call" | custom-call | tf_op jit(solution)/shard_map/project_load/pallas_call | solution.py:130
  23.5 4.2 %pool.1 = (f32[4,32,1024]{2,1,0:T(8,128)S(1)}, bf16[4,32,1152]{2,1,0:T(8,128)(2,1)S(1)}, f32[64,128]{1,0:T(8,128)S(1)}, f32[64,768]{1,0:T(8,128)S(1)}, bf16[64,768]{1,0:T(8,128)(2,1)S(1)}) custom-call(s32[1,128]{1,0:T(1,128)S(1)} %get-tuple-element.51.length_ref, bf16[4,16,1024]{2,1,0:T(8,128)(2,1)S(1)} %collective-permute-done.3.refs_0_, ...), custom_call_target="tpu_custom_call" | custom-call | flops 1610612736 | tf_op jit(solution)/shard_map/pool/pallas_call | solution.py:50
  28.3 1.2 %pool_rest.1 = (f32[4,32,1024]{2,1,0:T(8,128)S(1)}, bf16[4,32,1152]{2,1,0:T(8,128)(2,1)S(1)}) custom-call(bf16[64,768]{1,0:T(8,128)(2,1)S(1)} %get-tuple-element.57.left_ref, f32[64,128]{1,0:T(8,128)S(1)} %get-tuple-element.58.peak_ref.refs_2_.refs_8_, bf16[4,768,1024]{2,1,0:T(8,128)(2,1)S(1)} %get-tuple-element.54.refs_4_.held_ref), custom_call_target="tpu_custom_call" | custom-call | flops 1610612736 | tf_op jit(solution)/shard_map/pool_rest/pallas_call | solution.py:50
  30.2 2.4 %collective-permute-start.12 = (bf16[4,16,1152]{2,1,0:T(8,128)(2,1)S(1)}, bf16[4,16,1152]{2,1,0:T(8,128)(2,1)S(1)}, u32[]{:S(2)}, u32[]{:S(2)}) collective-permute-start(bf16[4,16,1152]{2,1,0:T(8,128)(2,1)S(1)} %get-tuple-element.65), channel_id=1, source_target_pairs={{0,6},{1,7},{2,4},{3,5},{4,2},{5,3},{6,0},{7,1},{8,14},{9,15},{10,... | collective-permute-start | bytes 442376 | tf_op jit(solution)/shard_map/ppermute | solution.py:22
  33.4 0.7 collective-permute-start.14
  34.1 3.7 %collective-permute-done.12.refs_1_ = bf16[4,16,1152]{2,1,0:T(8,128)(2,1)S(1)} collective-permute-done((bf16[4,16,1152]{2,1,0:T(8,128)(2,1)S(1)}, bf16[4,16,1152]{2,1,0:T(8,128)(2,1)S(1)}, u32[]{:S(2)}, u32[]{:S(2)}) %collective-permute-start.12) | collective-permute-done | bytes 147488 | tf_op jit(solution)/shard_map/ppermute | solution.py:22
  37.8 2.3 %collective-permute-done.13.refs_2_ = bf16[4,16,1152]{2,1,0:T(8,128)(2,1)S(1)} collective-permute-done((bf16[4,16,1152]{2,1,0:T(8,128)(2,1)S(1)}, bf16[4,16,1152]{2,1,0:T(8,128)(2,1)S(1)}, u32[]{:S(2)}, u32[]{:S(2)}) %collective-permute-start.13) | collective-permute-done | bytes 147488 | tf_op jit(solution)/shard_map/ppermute | solution.py:22
  40.5 2.7 %collective-permute-start.15 = (bf16[1,16,1152]{2,1,0:T(8,128)(2,1)S(1)}, bf16[1,16,1152]{2,1,0:T(8,128)(2,1)S(1)}, u32[]{:S(2)}, u32[]{:S(2)}) collective-permute-start(bf16[1,16,1152]{2,1,0:T(8,128)(2,1)S(1)} %get-tuple-element.70), channel_id=1, source_target_pairs={{0,24},{1,25},{2,26},{3,27},{4,28},{5,29},{6,30},{7,31},{8,16},{9,... | collective-permute-start | bytes 110600 | tf_op jit(solution)/shard_map/ppermute | solution.py:22
  43.6 1.4 %collective-permute-start.17 = (bf16[1,16,1152]{2,1,0:T(8,128)(2,1)S(1)}, bf16[1,16,1152]{2,1,0:T(8,128)(2,1)S(1)}, u32[]{:S(2)}, u32[]{:S(2)}) collective-permute-start(bf16[1,16,1152]{2,1,0:T(8,128)(2,1)S(1)} %get-tuple-element.72), channel_id=1, source_target_pairs={{0,8},{1,9},{2,10},{3,11},{4,12},{5,13},{6,14},{7,15},{8,0},{9,1},... | collective-permute-start | bytes 110600 | tf_op jit(solution)/shard_map/ppermute | solution.py:22
  45.0 1.8 %collective-permute-done.15.refs_1_ = bf16[1,16,1152]{2,1,0:T(8,128)(2,1)S(1)} collective-permute-done((bf16[1,16,1152]{2,1,0:T(8,128)(2,1)S(1)}, bf16[1,16,1152]{2,1,0:T(8,128)(2,1)S(1)}, u32[]{:S(2)}, u32[]{:S(2)}) %collective-permute-start.15) | collective-permute-done | bytes 36896 | tf_op jit(solution)/shard_map/ppermute | solution.py:22
  46.8 1.6 %collective-permute-done.16.refs_2_ = bf16[1,16,1152]{2,1,0:T(8,128)(2,1)S(1)} collective-permute-done((bf16[1,16,1152]{2,1,0:T(8,128)(2,1)S(1)}, bf16[1,16,1152]{2,1,0:T(8,128)(2,1)S(1)}, u32[]{:S(2)}, u32[]{:S(2)}) %collective-permute-start.16) | collective-permute-done | bytes 36896 | tf_op jit(solution)/shard_map/ppermute | solution.py:22
  48.4 0.6 head_sums.1
  49.0 1.9 %collective-permute-start.20 = (f32[2,1024]{1,0:T(2,128)S(1)}, f32[2,1024]{1,0:T(2,128)S(1)}, u32[]{:S(2)}, u32[]{:S(2)}) collective-permute-start(f32[2,1024]{1,0:T(2,128)S(1)} %get-tuple-element.75.refs_0_), channel_id=1, source_target_pairs={{0,24},{1,25},{2,26},{3,27},{4,28},{5,29},{6,30},{7,31},{8,16},{9,... | collective-permute-start | bytes 24584 | tf_op jit(solution)/shard_map/ppermute | solution.py:22
  51.1 2.4 %collective-permute-start.18 = (f32[2,1024]{1,0:T(2,128)S(1)}, f32[2,1024]{1,0:T(2,128)S(1)}, u32[]{:S(2)}, u32[]{:S(2)}) collective-permute-start(f32[2,1024]{1,0:T(2,128)S(1)} %get-tuple-element.75.refs_0_), channel_id=1, source_target_pairs={{0,8},{1,9},{2,10},{3,11},{4,12},{5,13},{6,14},{7,15},{8,0},{9,1},... | collective-permute-start | bytes 24584 | tf_op jit(solution)/shard_map/ppermute | solution.py:22
  53.5 1.1 %collective-permute-done.20.refs_3_ = f32[2,1024]{1,0:T(2,128)S(1)} collective-permute-done((f32[2,1024]{1,0:T(2,128)S(1)}, f32[2,1024]{1,0:T(2,128)S(1)}, u32[]{:S(2)}, u32[]{:S(2)}) %collective-permute-start.20) | collective-permute-done | bytes 8224 | tf_op jit(solution)/shard_map/ppermute | solution.py:22
  54.5 0.9 collective-permute-done.19.refs_2_
  55.5 1.6 %collective-permute-start.21 = (f32[2,1024]{1,0:T(2,128)S(1)}, f32[2,1024]{1,0:T(2,128)S(1)}, u32[]{:S(2)}, u32[]{:S(2)}) collective-permute-start(f32[2,1024]{1,0:T(2,128)S(1)} %tree_sum.1.sums_ref), channel_id=1, source_target_pairs={{0,4},{1,5},{2,6},{3,7},{4,0},{5,1},{6,2},{7,3},{8,12},{9,13},{10,... | collective-permute-start | bytes 24584 | tf_op jit(solution)/shard_map/ppermute | solution.py:22
  57.0 2.1 %collective-permute-done.21.other_sums_ref = f32[2,1024]{1,0:T(2,128)S(1)} collective-permute-done((f32[2,1024]{1,0:T(2,128)S(1)}, f32[2,1024]{1,0:T(2,128)S(1)}, u32[]{:S(2)}, u32[]{:S(2)}) %collective-permute-start.21) | collective-permute-done | bytes 8224 | tf_op jit(solution)/shard_map/ppermute | solution.py:22
  59.2 1.2 %head_grads.1 = (f32[1,1024]{1,0:T(1,128)}, f32[1,1024]{1,0:T(1,128)S(1)}, bf16[16,1152]{1,0:T(8,128)(2,1)S(1)}, f32[16,1024]{1,0:T(8,128)S(1)}) custom-call(f32[2,1024]{1,0:T(2,128)S(1)} %tree_sum.1.sums_ref, f32[2,1024]{1,0:T(2,128)S(1)} %collective-permute-done.21.other_sums_ref, f32[16,1024]{1,0:T(8,128)S(1)} %get-tuple-element.76.refs_0_, ...), custom_call_target="tpu_custom_call" | custom-call | tf_op jit(solution)/shard_map/head_grads/pallas_call | solution.py:50
  60.4 2.0 %collective-permute-start.24 = (bf16[16,1152]{1,0:T(8,128)(2,1)S(1)}, bf16[16,1152]{1,0:T(8,128)(2,1)S(1)}, u32[]{:S(2)}, u32[]{:S(2)}) collective-permute-start(bf16[16,1152]{1,0:T(8,128)(2,1)S(1)} %get-tuple-element.78.refs_0_), channel_id=1, source_target_pairs={{0,24},{1,25},{2,26},{3,27},{4,28},{5,29},{6,30},{7,31},{8,16},{9,... | collective-permute-start | bytes 110600 | tf_op jit(solution)/shard_map/ppermute | solution.py:22
  62.4 1.0 %collective-permute-start.23 = (bf16[16,1152]{1,0:T(8,128)(2,1)S(1)}, bf16[16,1152]{1,0:T(8,128)(2,1)S(1)}, u32[]{:S(2)}, u32[]{:S(2)}) collective-permute-start(bf16[16,1152]{1,0:T(8,128)(2,1)S(1)} %get-tuple-element.78.refs_0_), channel_id=1, source_target_pairs={{0,16},{1,17},{2,18},{3,19},{4,20},{5,21},{6,22},{7,23},{8,24},{9,... | collective-permute-start | bytes 110600 | tf_op jit(solution)/shard_map/ppermute | solution.py:22
  63.5 1.3 %collective-permute-start.22 = (bf16[16,1152]{1,0:T(8,128)(2,1)S(1)}, bf16[16,1152]{1,0:T(8,128)(2,1)S(1)}, u32[]{:S(2)}, u32[]{:S(2)}) collective-permute-start(bf16[16,1152]{1,0:T(8,128)(2,1)S(1)} %get-tuple-element.78.refs_0_), channel_id=1, source_target_pairs={{0,8},{1,9},{2,10},{3,11},{4,12},{5,13},{6,14},{7,15},{8,0},{9,1},... | collective-permute-start | bytes 110600 | tf_op jit(solution)/shard_map/ppermute | solution.py:22
  64.8 1.4 %collective-permute-done.24.refs_3_ = bf16[16,1152]{1,0:T(8,128)(2,1)S(1)} collective-permute-done((bf16[16,1152]{1,0:T(8,128)(2,1)S(1)}, bf16[16,1152]{1,0:T(8,128)(2,1)S(1)}, u32[]{:S(2)}, u32[]{:S(2)}) %collective-permute-start.24) | collective-permute-done | bytes 36896 | tf_op jit(solution)/shard_map/ppermute | solution.py:22
  66.2 1.6 %collective-permute-done.23.refs_2_ = bf16[16,1152]{1,0:T(8,128)(2,1)S(1)} collective-permute-done((bf16[16,1152]{1,0:T(8,128)(2,1)S(1)}, bf16[16,1152]{1,0:T(8,128)(2,1)S(1)}, u32[]{:S(2)}, u32[]{:S(2)}) %collective-permute-start.23) | collective-permute-done | bytes 36896 | tf_op jit(solution)/shard_map/ppermute | solution.py:22
  67.8 1.4 %collective-permute-start.29 = (bf16[4,16,1152]{2,1,0:T(8,128)(2,1)S(1)}, bf16[4,16,1152]{2,1,0:T(8,128)(2,1)S(1)}, u32[]{:S(2)}, u32[]{:S(2)}) collective-permute-start(bf16[4,16,1152]{2,1,0:T(8,128)(2,1)S(1)} %stack.3.refs_0_), channel_id=1, source_target_pairs={{0,2},{1,3},{2,0},{3,1},{4,6},{5,7},{6,4},{7,5},{8,10},{9,11},{10,... | collective-permute-start | bytes 442376 | tf_op jit(solution)/shard_map/ppermute | solution.py:22
  69.2 1.6 %collective-permute-start.26 = (bf16[4,16,1152]{2,1,0:T(8,128)(2,1)S(1)}, bf16[4,16,1152]{2,1,0:T(8,128)(2,1)S(1)}, u32[]{:S(2)}, u32[]{:S(2)}) collective-permute-start(bf16[4,16,1152]{2,1,0:T(8,128)(2,1)S(1)} %stack.3.refs_0_), channel_id=1, source_target_pairs={{0,6},{1,7},{2,4},{3,5},{4,2},{5,3},{6,0},{7,1},{8,14},{9,15},{10,... | collective-permute-start | bytes 442376 | tf_op jit(solution)/shard_map/ppermute | solution.py:22
  71.4 1.6 %collective-permute-done.29.refs_1_ = bf16[4,16,1152]{2,1,0:T(8,128)(2,1)S(1)} collective-permute-done((bf16[4,16,1152]{2,1,0:T(8,128)(2,1)S(1)}, bf16[4,16,1152]{2,1,0:T(8,128)(2,1)S(1)}, u32[]{:S(2)}, u32[]{:S(2)}) %collective-permute-start.29) | collective-permute-done | bytes 147488 | tf_op jit(solution)/shard_map/ppermute | solution.py:22
  73.0 2.2 %collective-permute-done.26.refs_1_ = bf16[4,16,1152]{2,1,0:T(8,128)(2,1)S(1)} collective-permute-done((bf16[4,16,1152]{2,1,0:T(8,128)(2,1)S(1)}, bf16[4,16,1152]{2,1,0:T(8,128)(2,1)S(1)}, u32[]{:S(2)}, u32[]{:S(2)}) %collective-permute-start.26) | collective-permute-done | bytes 147488 | tf_op jit(solution)/shard_map/ppermute | solution.py:22
  75.3 0.8 collective-permute-done.25.refs_0_
  76.1 2.0 %project.1.refs_6_ = f32[64,768]{1,0:T(8,128)S(1)} custom-call(bf16[4,16,1152]{2,1,0:T(8,128)(2,1)S(1)} %stack.3.refs_0_, bf16[4,16,1152]{2,1,0:T(8,128)(2,1)S(1)} %collective-permute-done.29.refs_1_, bf16[4,16,1152]{2,1,0:T(8,128)(2,1)S(1)} %collective-permute-done.30.refs_2_, bf16[4,16,1152]{2,1,0:T(8,128)(2,1)S(1)} %collective-permute-done.31.refs_3_, ...), custom_call_target="tpu_custom_call" | custom-call | flops 1610612736 | tf_op jit(solution)/shard_map/project/pallas_call | solution.py:50
  78.1 4.0 %grad.1 = (f32[4,32,1024]{2,1,0:T(8,128)S(1)}, bf16[4,32,1024]{2,1,0:T(8,128)(2,1)S(1)}, bf16[64,768]{1,0:T(8,128)(2,1)S(1)}, f32[1,1]{1,0:T(1,128)}) custom-call(bf16[4,16,1152]{2,1,0:T(8,128)(2,1)S(1)} %collective-permute-done.25.refs_0_, bf16[4,16,1152]{2,1,0:T(8,128)(2,1)S(1)} %collective-permute-done.26.refs_1_, ...), custom_call_target="tpu_custom_call" | custom-call | flops 1610612736 | tf_op jit(solution)/shard_map/grad/pallas_call | solution.py:50
  82.7 1.2 %grad_rest.1 = (f32[4,32,1024]{2,1,0:T(8,128)S(1)}, bf16[4,32,1024]{2,1,0:T(8,128)(2,1)S(1)}) custom-call(bf16[64,768]{1,0:T(8,128)(2,1)S(1)} %get-tuple-element.81.left_ref, bf16[4,768,1024]{2,1,0:T(8,128)(2,1)S(1)} %get-tuple-element.54.refs_4_.held_ref), custom_call_target="tpu_custom_call" | custom-call | flops 1610612736 | tf_op jit(solution)/shard_map/grad_rest/pallas_call | solution.py:50
  84.4 2.3 %collective-permute-start.34 = (bf16[4,16,1024]{2,1,0:T(8,128)(2,1)S(1)}, bf16[4,16,1024]{2,1,0:T(8,128)(2,1)S(1)}, u32[]{:S(2)}, u32[]{:S(2)}) collective-permute-start(bf16[4,16,1024]{2,1,0:T(8,128)(2,1)S(1)} %get-tuple-element.88), channel_id=1, source_target_pairs={{0,6},{1,7},{2,4},{3,5},{4,2},{5,3},{6,0},{7,1},{8,14},{9,15},{10,... | collective-permute-start | bytes 393224 | tf_op jit(solution)/shard_map/ppermute | solution.py:22
  87.3 0.7 collective-permute-start.36
  88.0 3.6 %collective-permute-done.34.refs_1_ = bf16[4,16,1024]{2,1,0:T(8,128)(2,1)S(1)} collective-permute-done((bf16[4,16,1024]{2,1,0:T(8,128)(2,1)S(1)}, bf16[4,16,1024]{2,1,0:T(8,128)(2,1)S(1)}, u32[]{:S(2)}, u32[]{:S(2)}) %collective-permute-start.34) | collective-permute-done | bytes 131104 | tf_op jit(solution)/shard_map/ppermute | solution.py:22
  91.6 2.0 %collective-permute-done.35.refs_2_ = bf16[4,16,1024]{2,1,0:T(8,128)(2,1)S(1)} collective-permute-done((bf16[4,16,1024]{2,1,0:T(8,128)(2,1)S(1)}, bf16[4,16,1024]{2,1,0:T(8,128)(2,1)S(1)}, u32[]{:S(2)}, u32[]{:S(2)}) %collective-permute-start.35) | collective-permute-done | bytes 131104 | tf_op jit(solution)/shard_map/ppermute | solution.py:22
  93.8 2.2 %collective-permute-start.37 = (bf16[1,16,1024]{2,1,0:T(8,128)(2,1)S(1)}, bf16[1,16,1024]{2,1,0:T(8,128)(2,1)S(1)}, u32[]{:S(2)}, u32[]{:S(2)}) collective-permute-start(bf16[1,16,1024]{2,1,0:T(8,128)(2,1)S(1)} %get-tuple-element.92), channel_id=1, source_target_pairs={{0,24},{1,25},{2,26},{3,27},{4,28},{5,29},{6,30},{7,31},{8,16},{9,... | collective-permute-start | bytes 98312 | tf_op jit(solution)/shard_map/ppermute | solution.py:22
  96.5 1.7 %collective-permute-start.39 = (bf16[1,16,1024]{2,1,0:T(8,128)(2,1)S(1)}, bf16[1,16,1024]{2,1,0:T(8,128)(2,1)S(1)}, u32[]{:S(2)}, u32[]{:S(2)}) collective-permute-start(bf16[1,16,1024]{2,1,0:T(8,128)(2,1)S(1)} %get-tuple-element.94), channel_id=1, source_target_pairs={{0,8},{1,9},{2,10},{3,11},{4,12},{5,13},{6,14},{7,15},{8,0},{9,1},... | collective-permute-start | bytes 98312 | tf_op jit(solution)/shard_map/ppermute | solution.py:22
  98.2 2.9 %head_weight_grad.1 = f32[1024,1024]{1,0:T(8,128)} custom-call(f32[16,1024]{1,0:T(8,128)S(1)} %get-tuple-element.95.normed_ref, f32[1,1024]{1,0:T(1,128)S(1)} %get-tuple-element.96.bias_grad_ref), custom_call_target="tpu_custom_call" | custom-call | tf_op jit(solution)/shard_map/head_weight_grad/pallas_call | solution.py:400
  101.2 0.6 far_sum.1
  (58 shorter events, 7.3 us)
Async XLA Ops:
  0.6 10.2 %collective-permute-start = (bf16[16,1024]{1,0:T(8,128)(2,1)}, bf16[16,1024]{1,0:T(8,128)(2,1)S(1)}, u32[]{:S(2)}, u32[]{:S(2)}) collective-permute-start(bf16[16,1024]{1,0:T(8,128)(2,1)} %refs_1_.1), channel_id=1, source_target_pairs={{0,8},{1,9},{2,10},{3,11},{4,12},{5,13},{6,14},{7,15},{8,0},{9,1},... | collective-permute-start | bytes 98312 | tf_op jit(solution)/shard_map/ppermute | solution.py:22
  3.7 7.1 %collective-permute-start.2 = (bf16[16,1024]{1,0:T(8,128)(2,1)}, bf16[16,1024]{1,0:T(8,128)(2,1)S(1)}, u32[]{:S(2)}, u32[]{:S(2)}) collective-permute-start(bf16[16,1024]{1,0:T(8,128)(2,1)} %refs_1_.1), channel_id=1, source_target_pairs={{0,24},{1,25},{2,26},{3,27},{4,28},{5,29},{6,30},{7,31},{8,16},{9,... | collective-permute-start | bytes 98312 | tf_op jit(solution)/shard_map/ppermute | solution.py:22
  6.2 5.4 %collective-permute-start.1 = (bf16[16,1024]{1,0:T(8,128)(2,1)}, bf16[16,1024]{1,0:T(8,128)(2,1)S(1)}, u32[]{:S(2)}, u32[]{:S(2)}) collective-permute-start(bf16[16,1024]{1,0:T(8,128)(2,1)} %refs_1_.1), channel_id=1, source_target_pairs={{0,16},{1,17},{2,18},{3,19},{4,20},{5,21},{6,22},{7,23},{8,24},{9,... | collective-permute-start | bytes 98312 | tf_op jit(solution)/shard_map/ppermute | solution.py:22
  11.6 6.3 %collective-permute-start.7 = (bf16[4,16,1024]{2,1,0:T(8,128)(2,1)S(1)}, bf16[4,16,1024]{2,1,0:T(8,128)(2,1)S(1)}, u32[]{:S(2)}, u32[]{:S(2)}) collective-permute-start(bf16[4,16,1024]{2,1,0:T(8,128)(2,1)S(1)} %stack.2.refs_0_), channel_id=1, source_target_pairs={{0,2},{1,3},{2,0},{3,1},{4,6},{5,7},{6,4},{7,5},{8,10},{9,11},{10,... | collective-permute-start | bytes 393224 | tf_op jit(solution)/shard_map/ppermute | solution.py:22
  13.2 6.0 %collective-permute-start.4 = (bf16[4,16,1024]{2,1,0:T(8,128)(2,1)S(1)}, bf16[4,16,1024]{2,1,0:T(8,128)(2,1)S(1)}, u32[]{:S(2)}, u32[]{:S(2)}) collective-permute-start(bf16[4,16,1024]{2,1,0:T(8,128)(2,1)S(1)} %stack.2.refs_0_), channel_id=1, source_target_pairs={{0,6},{1,7},{2,4},{3,5},{4,2},{5,3},{6,0},{7,1},{8,14},{9,15},{10,... | collective-permute-start | bytes 393224 | tf_op jit(solution)/shard_map/ppermute | solution.py:22
  14.6 5.1 %collective-permute-start.3 = (bf16[4,16,1024]{2,1,0:T(8,128)(2,1)S(1)}, bf16[4,16,1024]{2,1,0:T(8,128)(2,1)S(1)}, u32[]{:S(2)}, u32[]{:S(2)}) collective-permute-start(bf16[4,16,1024]{2,1,0:T(8,128)(2,1)S(1)} %stack.2.refs_0_), channel_id=1, source_target_pairs={{0,4},{1,5},{2,6},{3,7},{4,0},{5,1},{6,2},{7,3},{8,12},{9,13},{10,... | collective-permute-start | bytes 393224 | tf_op jit(solution)/shard_map/ppermute | solution.py:22
  15.1 4.6 %collective-permute-start.8 = (bf16[4,16,1024]{2,1,0:T(8,128)(2,1)S(1)}, bf16[4,16,1024]{2,1,0:T(8,128)(2,1)S(1)}, u32[]{:S(2)}, u32[]{:S(2)}) collective-permute-start(bf16[4,16,1024]{2,1,0:T(8,128)(2,1)S(1)} %stack.2.refs_0_), channel_id=1, source_target_pairs={{0,1},{1,0},{2,3},{3,2},{4,5},{5,4},{6,7},{7,6},{8,9},{9,8},{10,11... | collective-permute-start | bytes 393224 | tf_op jit(solution)/shard_map/ppermute | solution.py:22
  17.9 1.9 %collective-permute-start.9 = (bf16[4,16,1024]{2,1,0:T(8,128)(2,1)S(1)}, bf16[4,16,1024]{2,1,0:T(8,128)(2,1)S(1)}, u32[]{:S(2)}, u32[]{:S(2)}) collective-permute-start(bf16[4,16,1024]{2,1,0:T(8,128)(2,1)S(1)} %collective-permute-done.7.refs_1_), channel_id=1, source_target_pairs={{0,1},{1,0},{2,3},{3,2},{4,5},{5,4},{6,7},{7,6},{8,9},{9,8},{10,11... | collective-permute-start | bytes 393224 | tf_op jit(solution)/shard_map/ppermute | solution.py:22
  19.2 4.3 %collective-permute-start.6 = (bf16[4,16,1024]{2,1,0:T(8,128)(2,1)S(1)}, bf16[4,16,1024]{2,1,0:T(8,128)(2,1)S(1)}, u32[]{:S(2)}, u32[]{:S(2)}) collective-permute-start(bf16[4,16,1024]{2,1,0:T(8,128)(2,1)S(1)} %collective-permute-done.4.refs_1_), channel_id=1, source_target_pairs={{0,1},{1,0},{2,3},{3,2},{4,5},{5,4},{6,7},{7,6},{8,9},{9,8},{10,11... | collective-permute-start | bytes 393224 | tf_op jit(solution)/shard_map/ppermute | solution.py:22
  19.7 3.8 %collective-permute-start.5 = (bf16[4,16,1024]{2,1,0:T(8,128)(2,1)S(1)}, bf16[4,16,1024]{2,1,0:T(8,128)(2,1)S(1)}, u32[]{:S(2)}, u32[]{:S(2)}) collective-permute-start(bf16[4,16,1024]{2,1,0:T(8,128)(2,1)S(1)} %collective-permute-done.3.refs_0_), channel_id=1, source_target_pairs={{0,1},{1,0},{2,3},{3,2},{4,5},{5,4},{6,7},{7,6},{8,9},{9,8},{10,11... | collective-permute-start | bytes 393224 | tf_op jit(solution)/shard_map/ppermute | solution.py:22
  27.7 1.8 %collective-permute-start.10 = (bf16[4,32,1152]{2,1,0:T(8,128)(2,1)S(1)}, bf16[4,32,1152]{2,1,0:T(8,128)(2,1)S(1)}, u32[]{:S(2)}, u32[]{:S(2)}) collective-permute-start(bf16[4,32,1152]{2,1,0:T(8,128)(2,1)S(1)} %get-tuple-element.61), channel_id=1, source_target_pairs={{0,1},{1,0},{2,3},{3,2},{4,5},{5,4},{6,7},{7,6},{8,9},{9,8},{10,11... | collective-permute-start | bytes 884744 | tf_op jit(solution)/shard_map/ppermute | solution.py:22
  28.3 20.1 %copy-start = (bf16[1024,1024]{1,0:T(8,128)(2,1)S(1)}, bf16[1024,1024]{1,0:T(8,128)(2,1)}, u32[]{:S(2)}) copy-start(bf16[1024,1024]{1,0:T(8,128)(2,1)} %refs_3_.2) | copy-start | bytes 6291460
  28.3 30.9 %copy-start.1 = (f32[1024]{0:T(1024)S(1)}, f32[1024]{0:T(1024)}, u32[]{:S(2)}) copy-start(f32[1024]{0:T(1024)} %param.12) | copy-start | bytes 12292
  28.3 30.9 %copy-start.2 = (s32[1024]{0:T(1024)S(1)}, s32[1024]{0:T(1024)}, u32[]{:S(2)}) copy-start(s32[1024]{0:T(1024)} %param.13) | copy-start | bytes 12292
  29.8 3.3 %collective-permute-start.11 = (bf16[4,32,1152]{2,1,0:T(8,128)(2,1)S(1)}, bf16[4,32,1152]{2,1,0:T(8,128)(2,1)S(1)}, u32[]{:S(2)}, u32[]{:S(2)}) collective-permute-start(bf16[4,32,1152]{2,1,0:T(8,128)(2,1)S(1)} %get-tuple-element.63), channel_id=1, source_target_pairs={{0,1},{1,0},{2,3},{3,2},{4,5},{5,4},{6,7},{7,6},{8,9},{9,8},{10,11... | collective-permute-start | bytes 884744 | tf_op jit(solution)/shard_map/ppermute | solution.py:22
  30.2 7.6 %collective-permute-start.12 = (bf16[4,16,1152]{2,1,0:T(8,128)(2,1)S(1)}, bf16[4,16,1152]{2,1,0:T(8,128)(2,1)S(1)}, u32[]{:S(2)}, u32[]{:S(2)}) collective-permute-start(bf16[4,16,1152]{2,1,0:T(8,128)(2,1)S(1)} %get-tuple-element.65), channel_id=1, source_target_pairs={{0,6},{1,7},{2,4},{3,5},{4,2},{5,3},{6,0},{7,1},{8,14},{9,15},{10,... | collective-permute-start | bytes 442376 | tf_op jit(solution)/shard_map/ppermute | solution.py:22
  32.6 7.6 %collective-permute-start.13 = (bf16[4,16,1152]{2,1,0:T(8,128)(2,1)S(1)}, bf16[4,16,1152]{2,1,0:T(8,128)(2,1)S(1)}, u32[]{:S(2)}, u32[]{:S(2)}) collective-permute-start(bf16[4,16,1152]{2,1,0:T(8,128)(2,1)S(1)} %get-tuple-element.66), channel_id=1, source_target_pairs={{0,4},{1,5},{2,6},{3,7},{4,0},{5,1},{6,2},{7,3},{8,12},{9,13},{10,... | collective-permute-start | bytes 442376 | tf_op jit(solution)/shard_map/ppermute | solution.py:22
  33.4 6.8 %collective-permute-start.14 = (bf16[4,16,1152]{2,1,0:T(8,128)(2,1)S(1)}, bf16[4,16,1152]{2,1,0:T(8,128)(2,1)S(1)}, u32[]{:S(2)}, u32[]{:S(2)}) collective-permute-start(bf16[4,16,1152]{2,1,0:T(8,128)(2,1)S(1)} %get-tuple-element.67), channel_id=1, source_target_pairs={{0,2},{1,3},{2,0},{3,1},{4,6},{5,7},{6,4},{7,5},{8,10},{9,11},{10,... | collective-permute-start | bytes 442376 | tf_op jit(solution)/shard_map/ppermute | solution.py:22
  40.5 6.2 %collective-permute-start.15 = (bf16[1,16,1152]{2,1,0:T(8,128)(2,1)S(1)}, bf16[1,16,1152]{2,1,0:T(8,128)(2,1)S(1)}, u32[]{:S(2)}, u32[]{:S(2)}) collective-permute-start(bf16[1,16,1152]{2,1,0:T(8,128)(2,1)S(1)} %get-tuple-element.70), channel_id=1, source_target_pairs={{0,24},{1,25},{2,26},{3,27},{4,28},{5,29},{6,30},{7,31},{8,16},{9,... | collective-permute-start | bytes 110600 | tf_op jit(solution)/shard_map/ppermute | solution.py:22
  43.3 5.1 %collective-permute-start.16 = (bf16[1,16,1152]{2,1,0:T(8,128)(2,1)S(1)}, bf16[1,16,1152]{2,1,0:T(8,128)(2,1)S(1)}, u32[]{:S(2)}, u32[]{:S(2)}) collective-permute-start(bf16[1,16,1152]{2,1,0:T(8,128)(2,1)S(1)} %get-tuple-element.71), channel_id=1, source_target_pairs={{0,16},{1,17},{2,18},{3,19},{4,20},{5,21},{6,22},{7,23},{8,24},{9,... | collective-permute-start | bytes 110600 | tf_op jit(solution)/shard_map/ppermute | solution.py:22
  43.6 4.8 %collective-permute-start.17 = (bf16[1,16,1152]{2,1,0:T(8,128)(2,1)S(1)}, bf16[1,16,1152]{2,1,0:T(8,128)(2,1)S(1)}, u32[]{:S(2)}, u32[]{:S(2)}) collective-permute-start(bf16[1,16,1152]{2,1,0:T(8,128)(2,1)S(1)} %get-tuple-element.72), channel_id=1, source_target_pairs={{0,8},{1,9},{2,10},{3,11},{4,12},{5,13},{6,14},{7,15},{8,0},{9,1},... | collective-permute-start | bytes 110600 | tf_op jit(solution)/shard_map/ppermute | solution.py:22
  49.0 5.5 %collective-permute-start.20 = (f32[2,1024]{1,0:T(2,128)S(1)}, f32[2,1024]{1,0:T(2,128)S(1)}, u32[]{:S(2)}, u32[]{:S(2)}) collective-permute-start(f32[2,1024]{1,0:T(2,128)S(1)} %get-tuple-element.75.refs_0_), channel_id=1, source_target_pairs={{0,24},{1,25},{2,26},{3,27},{4,28},{5,29},{6,30},{7,31},{8,16},{9,... | collective-permute-start | bytes 24584 | tf_op jit(solution)/shard_map/ppermute | solution.py:22
  50.9 4.6 %collective-permute-start.19 = (f32[2,1024]{1,0:T(2,128)S(1)}, f32[2,1024]{1,0:T(2,128)S(1)}, u32[]{:S(2)}, u32[]{:S(2)}) collective-permute-start(f32[2,1024]{1,0:T(2,128)S(1)} %get-tuple-element.75.refs_0_), channel_id=1, source_target_pairs={{0,16},{1,17},{2,18},{3,19},{4,20},{5,21},{6,22},{7,23},{8,24},{9,... | collective-permute-start | bytes 24584 | tf_op jit(solution)/shard_map/ppermute | solution.py:22
  51.1 4.4 %collective-permute-start.18 = (f32[2,1024]{1,0:T(2,128)S(1)}, f32[2,1024]{1,0:T(2,128)S(1)}, u32[]{:S(2)}, u32[]{:S(2)}) collective-permute-start(f32[2,1024]{1,0:T(2,128)S(1)} %get-tuple-element.75.refs_0_), channel_id=1, source_target_pairs={{0,8},{1,9},{2,10},{3,11},{4,12},{5,13},{6,14},{7,15},{8,0},{9,1},... | collective-permute-start | bytes 24584 | tf_op jit(solution)/shard_map/ppermute | solution.py:22
  55.5 3.7 %collective-permute-start.21 = (f32[2,1024]{1,0:T(2,128)S(1)}, f32[2,1024]{1,0:T(2,128)S(1)}, u32[]{:S(2)}, u32[]{:S(2)}) collective-permute-start(f32[2,1024]{1,0:T(2,128)S(1)} %tree_sum.1.sums_ref), channel_id=1, source_target_pairs={{0,4},{1,5},{2,6},{3,7},{4,0},{5,1},{6,2},{7,3},{8,12},{9,13},{10,... | collective-permute-start | bytes 24584 | tf_op jit(solution)/shard_map/ppermute | solution.py:22
  60.4 5.8 %collective-permute-start.24 = (bf16[16,1152]{1,0:T(8,128)(2,1)S(1)}, bf16[16,1152]{1,0:T(8,128)(2,1)S(1)}, u32[]{:S(2)}, u32[]{:S(2)}) collective-permute-start(bf16[16,1152]{1,0:T(8,128)(2,1)S(1)} %get-tuple-element.78.refs_0_), channel_id=1, source_target_pairs={{0,24},{1,25},{2,26},{3,27},{4,28},{5,29},{6,30},{7,31},{8,16},{9,... | collective-permute-start | bytes 110600 | tf_op jit(solution)/shard_map/ppermute | solution.py:22
  62.4 5.3 %collective-permute-start.23 = (bf16[16,1152]{1,0:T(8,128)(2,1)S(1)}, bf16[16,1152]{1,0:T(8,128)(2,1)S(1)}, u32[]{:S(2)}, u32[]{:S(2)}) collective-permute-start(bf16[16,1152]{1,0:T(8,128)(2,1)S(1)} %get-tuple-element.78.refs_0_), channel_id=1, source_target_pairs={{0,16},{1,17},{2,18},{3,19},{4,20},{5,21},{6,22},{7,23},{8,24},{9,... | collective-permute-start | bytes 110600 | tf_op jit(solution)/shard_map/ppermute | solution.py:22
  63.5 4.3 %collective-permute-start.22 = (bf16[16,1152]{1,0:T(8,128)(2,1)S(1)}, bf16[16,1152]{1,0:T(8,128)(2,1)S(1)}, u32[]{:S(2)}, u32[]{:S(2)}) collective-permute-start(bf16[16,1152]{1,0:T(8,128)(2,1)S(1)} %get-tuple-element.78.refs_0_), channel_id=1, source_target_pairs={{0,8},{1,9},{2,10},{3,11},{4,12},{5,13},{6,14},{7,15},{8,0},{9,1},... | collective-permute-start | bytes 110600 | tf_op jit(solution)/shard_map/ppermute | solution.py:22
  67.8 5.2 %collective-permute-start.29 = (bf16[4,16,1152]{2,1,0:T(8,128)(2,1)S(1)}, bf16[4,16,1152]{2,1,0:T(8,128)(2,1)S(1)}, u32[]{:S(2)}, u32[]{:S(2)}) collective-permute-start(bf16[4,16,1152]{2,1,0:T(8,128)(2,1)S(1)} %stack.3.refs_0_), channel_id=1, source_target_pairs={{0,2},{1,3},{2,0},{3,1},{4,6},{5,7},{6,4},{7,5},{8,10},{9,11},{10,... | collective-permute-start | bytes 442376 | tf_op jit(solution)/shard_map/ppermute | solution.py:22
  69.2 6.0 %collective-permute-start.26 = (bf16[4,16,1152]{2,1,0:T(8,128)(2,1)S(1)}, bf16[4,16,1152]{2,1,0:T(8,128)(2,1)S(1)}, u32[]{:S(2)}, u32[]{:S(2)}) collective-permute-start(bf16[4,16,1152]{2,1,0:T(8,128)(2,1)S(1)} %stack.3.refs_0_), channel_id=1, source_target_pairs={{0,6},{1,7},{2,4},{3,5},{4,2},{5,3},{6,0},{7,1},{8,14},{9,15},{10,... | collective-permute-start | bytes 442376 | tf_op jit(solution)/shard_map/ppermute | solution.py:22
  70.8 5.2 %collective-permute-start.25 = (bf16[4,16,1152]{2,1,0:T(8,128)(2,1)S(1)}, bf16[4,16,1152]{2,1,0:T(8,128)(2,1)S(1)}, u32[]{:S(2)}, u32[]{:S(2)}) collective-permute-start(bf16[4,16,1152]{2,1,0:T(8,128)(2,1)S(1)} %stack.3.refs_0_), channel_id=1, source_target_pairs={{0,4},{1,5},{2,6},{3,7},{4,0},{5,1},{6,2},{7,3},{8,12},{9,13},{10,... | collective-permute-start | bytes 442376 | tf_op jit(solution)/shard_map/ppermute | solution.py:22
  71.4 4.7 %collective-permute-start.30 = (bf16[4,16,1152]{2,1,0:T(8,128)(2,1)S(1)}, bf16[4,16,1152]{2,1,0:T(8,128)(2,1)S(1)}, u32[]{:S(2)}, u32[]{:S(2)}) collective-permute-start(bf16[4,16,1152]{2,1,0:T(8,128)(2,1)S(1)} %stack.3.refs_0_), channel_id=1, source_target_pairs={{0,1},{1,0},{2,3},{3,2},{4,5},{5,4},{6,7},{7,6},{8,9},{9,8},{10,11... | collective-permute-start | bytes 442376 | tf_op jit(solution)/shard_map/ppermute | solution.py:22
  73.0 3.1 %collective-permute-start.31 = (bf16[4,16,1152]{2,1,0:T(8,128)(2,1)S(1)}, bf16[4,16,1152]{2,1,0:T(8,128)(2,1)S(1)}, u32[]{:S(2)}, u32[]{:S(2)}) collective-permute-start(bf16[4,16,1152]{2,1,0:T(8,128)(2,1)S(1)} %collective-permute-done.29.refs_1_), channel_id=1, source_target_pairs={{0,1},{1,0},{2,3},{3,2},{4,5},{5,4},{6,7},{7,6},{8,9},{9,8},{10,11... | collective-permute-start | bytes 442376 | tf_op jit(solution)/shard_map/ppermute | solution.py:22
  75.3 2.8 %collective-permute-start.28 = (bf16[4,16,1152]{2,1,0:T(8,128)(2,1)S(1)}, bf16[4,16,1152]{2,1,0:T(8,128)(2,1)S(1)}, u32[]{:S(2)}, u32[]{:S(2)}) collective-permute-start(bf16[4,16,1152]{2,1,0:T(8,128)(2,1)S(1)} %collective-permute-done.26.refs_1_), channel_id=1, source_target_pairs={{0,1},{1,0},{2,3},{3,2},{4,5},{5,4},{6,7},{7,6},{8,9},{9,8},{10,11... | collective-permute-start | bytes 442376 | tf_op jit(solution)/shard_map/ppermute | solution.py:22
  76.1 2.0 %collective-permute-start.27 = (bf16[4,16,1152]{2,1,0:T(8,128)(2,1)S(1)}, bf16[4,16,1152]{2,1,0:T(8,128)(2,1)S(1)}, u32[]{:S(2)}, u32[]{:S(2)}) collective-permute-start(bf16[4,16,1152]{2,1,0:T(8,128)(2,1)S(1)} %collective-permute-done.25.refs_0_), channel_id=1, source_target_pairs={{0,1},{1,0},{2,3},{3,2},{4,5},{5,4},{6,7},{7,6},{8,9},{9,8},{10,11... | collective-permute-start | bytes 442376 | tf_op jit(solution)/shard_map/ppermute | solution.py:22
  82.2 1.8 %collective-permute-start.32 = (bf16[4,32,1024]{2,1,0:T(8,128)(2,1)S(1)}, bf16[4,32,1024]{2,1,0:T(8,128)(2,1)S(1)}, u32[]{:S(2)}, u32[]{:S(2)}) collective-permute-start(bf16[4,32,1024]{2,1,0:T(8,128)(2,1)S(1)} %get-tuple-element.84), channel_id=1, source_target_pairs={{0,1},{1,0},{2,3},{3,2},{4,5},{5,4},{6,7},{7,6},{8,9},{9,8},{10,11... | collective-permute-start | bytes 786440 | tf_op jit(solution)/shard_map/ppermute | solution.py:22
  84.0 3.2 %collective-permute-start.33 = (bf16[4,32,1024]{2,1,0:T(8,128)(2,1)S(1)}, bf16[4,32,1024]{2,1,0:T(8,128)(2,1)S(1)}, u32[]{:S(2)}, u32[]{:S(2)}) collective-permute-start(bf16[4,32,1024]{2,1,0:T(8,128)(2,1)S(1)} %get-tuple-element.86), channel_id=1, source_target_pairs={{0,1},{1,0},{2,3},{3,2},{4,5},{5,4},{6,7},{7,6},{8,9},{9,8},{10,11... | collective-permute-start | bytes 786440 | tf_op jit(solution)/shard_map/ppermute | solution.py:22
  84.4 7.2 %collective-permute-start.34 = (bf16[4,16,1024]{2,1,0:T(8,128)(2,1)S(1)}, bf16[4,16,1024]{2,1,0:T(8,128)(2,1)S(1)}, u32[]{:S(2)}, u32[]{:S(2)}) collective-permute-start(bf16[4,16,1024]{2,1,0:T(8,128)(2,1)S(1)} %get-tuple-element.88), channel_id=1, source_target_pairs={{0,6},{1,7},{2,4},{3,5},{4,2},{5,3},{6,0},{7,1},{8,14},{9,15},{10,... | collective-permute-start | bytes 393224 | tf_op jit(solution)/shard_map/ppermute | solution.py:22
  86.7 6.9 %collective-permute-start.35 = (bf16[4,16,1024]{2,1,0:T(8,128)(2,1)S(1)}, bf16[4,16,1024]{2,1,0:T(8,128)(2,1)S(1)}, u32[]{:S(2)}, u32[]{:S(2)}) collective-permute-start(bf16[4,16,1024]{2,1,0:T(8,128)(2,1)S(1)} %get-tuple-element.89), channel_id=1, source_target_pairs={{0,4},{1,5},{2,6},{3,7},{4,0},{5,1},{6,2},{7,3},{8,12},{9,13},{10,... | collective-permute-start | bytes 393224 | tf_op jit(solution)/shard_map/ppermute | solution.py:22
  87.3 6.4 %collective-permute-start.36 = (bf16[4,16,1024]{2,1,0:T(8,128)(2,1)S(1)}, bf16[4,16,1024]{2,1,0:T(8,128)(2,1)S(1)}, u32[]{:S(2)}, u32[]{:S(2)}) collective-permute-start(bf16[4,16,1024]{2,1,0:T(8,128)(2,1)S(1)} %get-tuple-element.90), channel_id=1, source_target_pairs={{0,2},{1,3},{2,0},{3,1},{4,6},{5,7},{6,4},{7,5},{8,10},{9,11},{10,... | collective-permute-start | bytes 393224 | tf_op jit(solution)/shard_map/ppermute | solution.py:22
  93.8 7.4 %collective-permute-start.37 = (bf16[1,16,1024]{2,1,0:T(8,128)(2,1)S(1)}, bf16[1,16,1024]{2,1,0:T(8,128)(2,1)S(1)}, u32[]{:S(2)}, u32[]{:S(2)}) collective-permute-start(bf16[1,16,1024]{2,1,0:T(8,128)(2,1)S(1)} %get-tuple-element.92), channel_id=1, source_target_pairs={{0,24},{1,25},{2,26},{3,27},{4,28},{5,29},{6,30},{7,31},{8,16},{9,... | collective-permute-start | bytes 98312 | tf_op jit(solution)/shard_map/ppermute | solution.py:22
  96.0 5.2 %collective-permute-start.38 = (bf16[1,16,1024]{2,1,0:T(8,128)(2,1)S(1)}, bf16[1,16,1024]{2,1,0:T(8,128)(2,1)S(1)}, u32[]{:S(2)}, u32[]{:S(2)}) collective-permute-start(bf16[1,16,1024]{2,1,0:T(8,128)(2,1)S(1)} %get-tuple-element.93), channel_id=1, source_target_pairs={{0,16},{1,17},{2,18},{3,19},{4,20},{5,21},{6,22},{7,23},{8,24},{9,... | collective-permute-start | bytes 98312 | tf_op jit(solution)/shard_map/ppermute | solution.py:22
  96.5 4.6 %collective-permute-start.39 = (bf16[1,16,1024]{2,1,0:T(8,128)(2,1)S(1)}, bf16[1,16,1024]{2,1,0:T(8,128)(2,1)S(1)}, u32[]{:S(2)}, u32[]{:S(2)}) collective-permute-start(bf16[1,16,1024]{2,1,0:T(8,128)(2,1)S(1)} %get-tuple-element.94), channel_id=1, source_target_pairs={{0,8},{1,9},{2,10},{3,11},{4,12},{5,13},{6,14},{7,15},{8,0},{9,1},... | collective-permute-start | bytes 98312 | tf_op jit(solution)/shard_map/ppermute | solution.py:22

commit v12 on v7

--- a/solution.py
+++ b/solution.py
@@ -123,27 +123,22 @@
     return run(*[pltpu.with_memory_space_constraint(x, pltpu.HBM) for x in (tokens, *others)])
 
 
-def project(parts, held_ref, tile=256):
-    blocks, token_count, width = held_ref.shape
-    tiles = []
-    for at in range(0, token_count, tile):
-        total = None
-        for j in range(blocks):
-            left = jnp.concatenate([ref[j] for ref in parts], axis=0)[:, :width]
-            block = held_ref[j, at : at + tile, :]
-            part = lax.dot_general(left, block, (((1,), (1,)), ((), ())), preferred_element_type=F32)
-            total = part if total is None else total + part
-        tiles.append(total)
-    return jnp.concatenate(tiles, axis=1)
-
-
-def spread(left, held_ref, keep_ref, send_ref, extra, tile=256):
+def project(parts, held_ref):
+    blocks, _, width = held_ref.shape
+    total = None
+    for j in range(blocks):
+        left = jnp.concatenate([ref[j] for ref in parts], axis=0)[:, :width]
+        part = lax.dot_general(left, held_ref[j], (((1,), (1,)), ((), ())), preferred_element_type=F32)
+        total = part if total is None else total + part
+    return total
+
+
+def spread(left, held_ref, keep_ref, send_ref, extra):
     blocks, half, width = keep_ref.shape
     for j in range(blocks):
-        for at in range(0, width, tile):
-            part = jnp.dot(left, held_ref[j, :, at : at + tile], preferred_element_type=F32)
-            keep_ref[j, :, at : at + tile] = part[:half]
-            send_ref[j, :, at : at + tile] = part[half:].astype(BF16)
+        part = jnp.dot(left, held_ref[j], preferred_element_type=F32)
+        keep_ref[j] = part[:half]
+        send_ref[j, :, :width] = part[half:].astype(BF16)
         if extra is not None:
             send_ref[j, :, width:] = extra
 

time: 101 us -> 101 us (level)
  transfers between devices with their start and end apart: 40 -> 40, of which waited for: 20 -> 20; matrix products, arithmetic and copies ran while one was open for 0% -> 0% of each run, Pallas kernels for 14% -> 15%
where the time goes in v12:
time: 101 us; the launch traced here: 100 us
  starting transfers between devices  41.2 us (41%)
  waiting for transfers between devices  31.7 us (31%)
  Pallas kernels  25.9 us (26%)
  between operations  1.5 us (1%)
    ppermute x40, starting transfers between devices, swap(): return lax.ppermute(x, ('ctx', 'cls'), pairs)  41.2 us
    ppermute x40, waiting for transfers between devices, swap(): return lax.ppermute(x, ('ctx', 'cls'), pairs)  31.7 us
    pallas_call x18, Pallas kernels, call(): return list(run(*args))  18.2 us
    pallas_call x1, Pallas kernels, load(): run(*[pltpu.with_memory_space_constraint(x, pltpu.HBM) for x in (tokens,...  4.79 us
    pallas_call x1, Pallas kernels, head_weight_grad(): pl.pallas_call(functools.partial(head_weight_grad_kernel, columns // rows...  2.95 us
  transfers between devices with their start and end apart: 40, of which 20 were waited for; matrix products, arithmetic and copies ran while one was open for 0% of the time, Pallas kernels for 15%

profile of v12, /device:TPU:0, one launch (start us, length us, event | category | flops | bytes accessed | tf_op | source)
XLA Modules:
  0.0 100.4 jit_solution(17517926098962358002)
XLA Ops:
  0.6 3.1 %collective-permute-start = (bf16[16,1024]{1,0:T(8,128)(2,1)}, bf16[16,1024]{1,0:T(8,128)(2,1)S(1)}, u32[]{:S(2)}, u32[]{:S(2)}) collective-permute-start(bf16[16,1024]{1,0:T(8,128)(2,1)} %refs_0_.1), channel_id=1, source_target_pairs={{0,8},{1,9},{2,10},{3,11},{4,12},{5,13},{6,14},{7,15},{8,0},{9,1},... | collective-permute-start | bytes 98312 | tf_op jit(solution)/shard_map/ppermute | solution.py:22
  3.7 2.5 %collective-permute-start.2 = (bf16[16,1024]{1,0:T(8,128)(2,1)}, bf16[16,1024]{1,0:T(8,128)(2,1)S(1)}, u32[]{:S(2)}, u32[]{:S(2)}) collective-permute-start(bf16[16,1024]{1,0:T(8,128)(2,1)} %refs_0_.1), channel_id=1, source_target_pairs={{0,24},{1,25},{2,26},{3,27},{4,28},{5,29},{6,30},{7,31},{8,16},{9,... | collective-permute-start | bytes 98312 | tf_op jit(solution)/shard_map/ppermute | solution.py:22
  6.3 4.8 %load.1 = (bf16[4,768,1024]{2,1,0:T(8,128)(2,1)S(1)}, bf16[4,768,1024]{2,1,0:T(8,128)(2,1)S(1)}, bf16[16,1024]{1,0:T(8,128)(2,1)S(1)}, f32[1,1024]{1,0:T(1,128)S(1)}) custom-call(bf16[768,8192]{1,0:T(8,128)(2,1)} %tokens_ref.1, bf16[16,1024]{1,0:T(8,128)(2,1)} %refs_0_.1, f32[1,1024]{1,0:T(1,128)} %bitcast.7), custom_call_target="tpu_custom_call" | custom-call | tf_op jit(solution)/shard_map/load/pallas_call | solution.py:123
  11.6 1.6 %collective-permute-start.7 = (bf16[4,16,1024]{2,1,0:T(8,128)(2,1)S(1)}, bf16[4,16,1024]{2,1,0:T(8,128)(2,1)S(1)}, u32[]{:S(2)}, u32[]{:S(2)}) collective-permute-start(bf16[4,16,1024]{2,1,0:T(8,128)(2,1)S(1)} %stack.2.refs_0_), channel_id=1, source_target_pairs={{0,2},{1,3},{2,0},{3,1},{4,6},{5,7},{6,4},{7,5},{8,10},{9,11},{10,... | collective-permute-start | bytes 393224 | tf_op jit(solution)/shard_map/ppermute | solution.py:22
  13.2 1.4 %collective-permute-start.4 = (bf16[4,16,1024]{2,1,0:T(8,128)(2,1)S(1)}, bf16[4,16,1024]{2,1,0:T(8,128)(2,1)S(1)}, u32[]{:S(2)}, u32[]{:S(2)}) collective-permute-start(bf16[4,16,1024]{2,1,0:T(8,128)(2,1)S(1)} %stack.2.refs_0_), channel_id=1, source_target_pairs={{0,6},{1,7},{2,4},{3,5},{4,2},{5,3},{6,0},{7,1},{8,14},{9,15},{10,... | collective-permute-start | bytes 393224 | tf_op jit(solution)/shard_map/ppermute | solution.py:22
  15.1 3.2 %collective-permute-done.7.refs_1_ = bf16[4,16,1024]{2,1,0:T(8,128)(2,1)S(1)} collective-permute-done((bf16[4,16,1024]{2,1,0:T(8,128)(2,1)S(1)}, bf16[4,16,1024]{2,1,0:T(8,128)(2,1)S(1)}, u32[]{:S(2)}, u32[]{:S(2)}) %collective-permute-start.7) | collective-permute-done | bytes 131104 | tf_op jit(solution)/shard_map/ppermute | solution.py:22
  20.0 2.0 %project.2.refs_4_ = f32[64,768]{1,0:T(8,128)S(1)} custom-call(bf16[4,16,1024]{2,1,0:T(8,128)(2,1)S(1)} %stack.2.refs_0_, bf16[4,16,1024]{2,1,0:T(8,128)(2,1)S(1)} %collective-permute-done.7.refs_1_, bf16[4,16,1024]{2,1,0:T(8,128)(2,1)S(1)} %collective-permute-done.8.refs_2_, bf16[4,16,1024]{2,1,0:T(8,128)(2,1)S(1)} %collective-permute-done.9.refs_3_, ...), custom_call_target="tpu_custom_call" | custom-call | flops 1610612736 | tf_op jit(solution)/shard_map/project/pallas_call | solution.py:50
  22.1 4.1 %pool.1 = (f32[4,32,1024]{2,1,0:T(8,128)S(1)}, bf16[4,32,1152]{2,1,0:T(8,128)(2,1)S(1)}, f32[64,128]{1,0:T(8,128)S(1)}, f32[64,768]{1,0:T(8,128)S(1)}, bf16[64,768]{1,0:T(8,128)(2,1)S(1)}) custom-call(s32[1]{0:T(128)S(6)} %copy.15.length_ref, bf16[4,16,1024]{2,1,0:T(8,128)(2,1)S(1)} %collective-permute-done.3.refs_0_, ...), custom_call_target="tpu_custom_call" | custom-call | flops 1610612736 | tf_op jit(solution)/shard_map/pool/pallas_call | solution.py:50
  26.7 1.2 %pool_rest.1 = (f32[4,32,1024]{2,1,0:T(8,128)S(1)}, bf16[4,32,1152]{2,1,0:T(8,128)(2,1)S(1)}) custom-call(bf16[64,768]{1,0:T(8,128)(2,1)S(1)} %get-tuple-element.51.left_ref, f32[64,128]{1,0:T(8,128)S(1)} %get-tuple-element.52.peak_ref.refs_2_.refs_7_, bf16[4,768,1024]{2,1,0:T(8,128)(2,1)S(1)} %get-tuple-element.49.refs_4_.held_ref), custom_call_target="tpu_custom_call" | custom-call | flops 1610612736 | tf_op jit(solution)/shard_map/pool_rest/pallas_call | solution.py:50
  28.7 2.4 %collective-permute-start.12 = (bf16[4,16,1152]{2,1,0:T(8,128)(2,1)S(1)}, bf16[4,16,1152]{2,1,0:T(8,128)(2,1)S(1)}, u32[]{:S(2)}, u32[]{:S(2)}) collective-permute-start(bf16[4,16,1152]{2,1,0:T(8,128)(2,1)S(1)} %get-tuple-element.59), channel_id=1, source_target_pairs={{0,6},{1,7},{2,4},{3,5},{4,2},{5,3},{6,0},{7,1},{8,14},{9,15},{10,... | collective-permute-start | bytes 442376 | tf_op jit(solution)/shard_map/ppermute | solution.py:22
  32.0 0.6 collective-permute-start.14
  32.6 3.7 %collective-permute-done.12.refs_1_ = bf16[4,16,1152]{2,1,0:T(8,128)(2,1)S(1)} collective-permute-done((bf16[4,16,1152]{2,1,0:T(8,128)(2,1)S(1)}, bf16[4,16,1152]{2,1,0:T(8,128)(2,1)S(1)}, u32[]{:S(2)}, u32[]{:S(2)}) %collective-permute-start.12) | collective-permute-done | bytes 147488 | tf_op jit(solution)/shard_map/ppermute | solution.py:22
  36.3 2.4 %collective-permute-done.13.refs_2_ = bf16[4,16,1152]{2,1,0:T(8,128)(2,1)S(1)} collective-permute-done((bf16[4,16,1152]{2,1,0:T(8,128)(2,1)S(1)}, bf16[4,16,1152]{2,1,0:T(8,128)(2,1)S(1)}, u32[]{:S(2)}, u32[]{:S(2)}) %collective-permute-start.13) | collective-permute-done | bytes 147488 | tf_op jit(solution)/shard_map/ppermute | solution.py:22
  39.0 2.7 %collective-permute-start.15 = (bf16[1,16,1152]{2,1,0:T(8,128)(2,1)S(1)}, bf16[1,16,1152]{2,1,0:T(8,128)(2,1)S(1)}, u32[]{:S(2)}, u32[]{:S(2)}) collective-permute-start(bf16[1,16,1152]{2,1,0:T(8,128)(2,1)S(1)} %get-tuple-element.64), channel_id=1, source_target_pairs={{0,24},{1,25},{2,26},{3,27},{4,28},{5,29},{6,30},{7,31},{8,16},{9,... | collective-permute-start | bytes 110600 | tf_op jit(solution)/shard_map/ppermute | solution.py:22
  42.1 1.4 %collective-permute-start.17 = (bf16[1,16,1152]{2,1,0:T(8,128)(2,1)S(1)}, bf16[1,16,1152]{2,1,0:T(8,128)(2,1)S(1)}, u32[]{:S(2)}, u32[]{:S(2)}) collective-permute-start(bf16[1,16,1152]{2,1,0:T(8,128)(2,1)S(1)} %get-tuple-element.66), channel_id=1, source_target_pairs={{0,8},{1,9},{2,10},{3,11},{4,12},{5,13},{6,14},{7,15},{8,0},{9,1},... | collective-permute-start | bytes 110600 | tf_op jit(solution)/shard_map/ppermute | solution.py:22
  43.5 1.7 %collective-permute-done.15.refs_1_ = bf16[1,16,1152]{2,1,0:T(8,128)(2,1)S(1)} collective-permute-done((bf16[1,16,1152]{2,1,0:T(8,128)(2,1)S(1)}, bf16[1,16,1152]{2,1,0:T(8,128)(2,1)S(1)}, u32[]{:S(2)}, u32[]{:S(2)}) %collective-permute-start.15) | collective-permute-done | bytes 36896 | tf_op jit(solution)/shard_map/ppermute | solution.py:22
  45.2 1.6 %collective-permute-done.16.refs_2_ = bf16[1,16,1152]{2,1,0:T(8,128)(2,1)S(1)} collective-permute-done((bf16[1,16,1152]{2,1,0:T(8,128)(2,1)S(1)}, bf16[1,16,1152]{2,1,0:T(8,128)(2,1)S(1)}, u32[]{:S(2)}, u32[]{:S(2)}) %collective-permute-start.16) | collective-permute-done | bytes 36896 | tf_op jit(solution)/shard_map/ppermute | solution.py:22
  46.9 0.6 head_sums.1
  47.5 1.9 %collective-permute-start.20 = (f32[2,1024]{1,0:T(2,128)S(1)}, f32[2,1024]{1,0:T(2,128)S(1)}, u32[]{:S(2)}, u32[]{:S(2)}) collective-permute-start(f32[2,1024]{1,0:T(2,128)S(1)} %get-tuple-element.69.refs_0_), channel_id=1, source_target_pairs={{0,24},{1,25},{2,26},{3,27},{4,28},{5,29},{6,30},{7,31},{8,16},{9,... | collective-permute-start | bytes 24584 | tf_op jit(solution)/shard_map/ppermute | solution.py:22
  49.6 2.4 %collective-permute-start.18 = (f32[2,1024]{1,0:T(2,128)S(1)}, f32[2,1024]{1,0:T(2,128)S(1)}, u32[]{:S(2)}, u32[]{:S(2)}) collective-permute-start(f32[2,1024]{1,0:T(2,128)S(1)} %get-tuple-element.69.refs_0_), channel_id=1, source_target_pairs={{0,8},{1,9},{2,10},{3,11},{4,12},{5,13},{6,14},{7,15},{8,0},{9,1},... | collective-permute-start | bytes 24584 | tf_op jit(solution)/shard_map/ppermute | solution.py:22
  52.0 1.1 %collective-permute-done.20.refs_3_ = f32[2,1024]{1,0:T(2,128)S(1)} collective-permute-done((f32[2,1024]{1,0:T(2,128)S(1)}, f32[2,1024]{1,0:T(2,128)S(1)}, u32[]{:S(2)}, u32[]{:S(2)}) %collective-permute-start.20) | collective-permute-done | bytes 8224 | tf_op jit(solution)/shard_map/ppermute | solution.py:22
  53.0 0.9 collective-permute-done.19.refs_2_
  54.0 1.6 %collective-permute-start.21 = (f32[2,1024]{1,0:T(2,128)S(1)}, f32[2,1024]{1,0:T(2,128)S(1)}, u32[]{:S(2)}, u32[]{:S(2)}) collective-permute-start(f32[2,1024]{1,0:T(2,128)S(1)} %tree_sum.1.sums_ref), channel_id=1, source_target_pairs={{0,4},{1,5},{2,6},{3,7},{4,0},{5,1},{6,2},{7,3},{8,12},{9,13},{10,... | collective-permute-start | bytes 24584 | tf_op jit(solution)/shard_map/ppermute | solution.py:22
  55.5 2.1 %collective-permute-done.21.other_sums_ref = f32[2,1024]{1,0:T(2,128)S(1)} collective-permute-done((f32[2,1024]{1,0:T(2,128)S(1)}, f32[2,1024]{1,0:T(2,128)S(1)}, u32[]{:S(2)}, u32[]{:S(2)}) %collective-permute-start.21) | collective-permute-done | bytes 8224 | tf_op jit(solution)/shard_map/ppermute | solution.py:22
  57.7 1.2 %head_grads.1 = (f32[1,1024]{1,0:T(1,128)}, f32[1,1024]{1,0:T(1,128)S(1)}, bf16[16,1152]{1,0:T(8,128)(2,1)S(1)}, f32[16,1024]{1,0:T(8,128)S(1)}) custom-call(f32[2,1024]{1,0:T(2,128)S(1)} %tree_sum.1.sums_ref, f32[2,1024]{1,0:T(2,128)S(1)} %collective-permute-done.21.other_sums_ref, f32[16,1024]{1,0:T(8,128)S(1)} %get-tuple-element.70.refs_0_, ...), custom_call_target="tpu_custom_call" | custom-call | tf_op jit(solution)/shard_map/head_grads/pallas_call | solution.py:50
  58.9 2.0 %collective-permute-start.24 = (bf16[16,1152]{1,0:T(8,128)(2,1)S(1)}, bf16[16,1152]{1,0:T(8,128)(2,1)S(1)}, u32[]{:S(2)}, u32[]{:S(2)}) collective-permute-start(bf16[16,1152]{1,0:T(8,128)(2,1)S(1)} %get-tuple-element.72.refs_0_), channel_id=1, source_target_pairs={{0,24},{1,25},{2,26},{3,27},{4,28},{5,29},{6,30},{7,31},{8,16},{9,... | collective-permute-start | bytes 110600 | tf_op jit(solution)/shard_map/ppermute | solution.py:22
  60.9 1.0 %collective-permute-start.23 = (bf16[16,1152]{1,0:T(8,128)(2,1)S(1)}, bf16[16,1152]{1,0:T(8,128)(2,1)S(1)}, u32[]{:S(2)}, u32[]{:S(2)}) collective-permute-start(bf16[16,1152]{1,0:T(8,128)(2,1)S(1)} %get-tuple-element.72.refs_0_), channel_id=1, source_target_pairs={{0,16},{1,17},{2,18},{3,19},{4,20},{5,21},{6,22},{7,23},{8,24},{9,... | collective-permute-start | bytes 110600 | tf_op jit(solution)/shard_map/ppermute | solution.py:22
  61.9 1.4 %collective-permute-start.22 = (bf16[16,1152]{1,0:T(8,128)(2,1)S(1)}, bf16[16,1152]{1,0:T(8,128)(2,1)S(1)}, u32[]{:S(2)}, u32[]{:S(2)}) collective-permute-start(bf16[16,1152]{1,0:T(8,128)(2,1)S(1)} %get-tuple-element.72.refs_0_), channel_id=1, source_target_pairs={{0,8},{1,9},{2,10},{3,11},{4,12},{5,13},{6,14},{7,15},{8,0},{9,1},... | collective-permute-start | bytes 110600 | tf_op jit(solution)/shard_map/ppermute | solution.py:22
  63.3 1.4 %collective-permute-done.24.refs_3_ = bf16[16,1152]{1,0:T(8,128)(2,1)S(1)} collective-permute-done((bf16[16,1152]{1,0:T(8,128)(2,1)S(1)}, bf16[16,1152]{1,0:T(8,128)(2,1)S(1)}, u32[]{:S(2)}, u32[]{:S(2)}) %collective-permute-start.24) | collective-permute-done | bytes 36896 | tf_op jit(solution)/shard_map/ppermute | solution.py:22
  64.7 1.6 %collective-permute-done.23.refs_2_ = bf16[16,1152]{1,0:T(8,128)(2,1)S(1)} collective-permute-done((bf16[16,1152]{1,0:T(8,128)(2,1)S(1)}, bf16[16,1152]{1,0:T(8,128)(2,1)S(1)}, u32[]{:S(2)}, u32[]{:S(2)}) %collective-permute-start.23) | collective-permute-done | bytes 36896 | tf_op jit(solution)/shard_map/ppermute | solution.py:22
  66.3 1.4 %collective-permute-start.29 = (bf16[4,16,1152]{2,1,0:T(8,128)(2,1)S(1)}, bf16[4,16,1152]{2,1,0:T(8,128)(2,1)S(1)}, u32[]{:S(2)}, u32[]{:S(2)}) collective-permute-start(bf16[4,16,1152]{2,1,0:T(8,128)(2,1)S(1)} %stack.3.refs_0_), channel_id=1, source_target_pairs={{0,2},{1,3},{2,0},{3,1},{4,6},{5,7},{6,4},{7,5},{8,10},{9,11},{10,... | collective-permute-start | bytes 442376 | tf_op jit(solution)/shard_map/ppermute | solution.py:22
  67.7 1.6 %collective-permute-start.26 = (bf16[4,16,1152]{2,1,0:T(8,128)(2,1)S(1)}, bf16[4,16,1152]{2,1,0:T(8,128)(2,1)S(1)}, u32[]{:S(2)}, u32[]{:S(2)}) collective-permute-start(bf16[4,16,1152]{2,1,0:T(8,128)(2,1)S(1)} %stack.3.refs_0_), channel_id=1, source_target_pairs={{0,6},{1,7},{2,4},{3,5},{4,2},{5,3},{6,0},{7,1},{8,14},{9,15},{10,... | collective-permute-start | bytes 442376 | tf_op jit(solution)/shard_map/ppermute | solution.py:22
  69.9 1.6 %collective-permute-done.29.refs_1_ = bf16[4,16,1152]{2,1,0:T(8,128)(2,1)S(1)} collective-permute-done((bf16[4,16,1152]{2,1,0:T(8,128)(2,1)S(1)}, bf16[4,16,1152]{2,1,0:T(8,128)(2,1)S(1)}, u32[]{:S(2)}, u32[]{:S(2)}) %collective-permute-start.29) | collective-permute-done | bytes 147488 | tf_op jit(solution)/shard_map/ppermute | solution.py:22
  71.5 2.2 %collective-permute-done.26.refs_1_ = bf16[4,16,1152]{2,1,0:T(8,128)(2,1)S(1)} collective-permute-done((bf16[4,16,1152]{2,1,0:T(8,128)(2,1)S(1)}, bf16[4,16,1152]{2,1,0:T(8,128)(2,1)S(1)}, u32[]{:S(2)}, u32[]{:S(2)}) %collective-permute-start.26) | collective-permute-done | bytes 147488 | tf_op jit(solution)/shard_map/ppermute | solution.py:22
  73.8 0.8 collective-permute-done.25.refs_0_
  74.6 2.0 %project.3.refs_4_ = f32[64,768]{1,0:T(8,128)S(1)} custom-call(bf16[4,16,1152]{2,1,0:T(8,128)(2,1)S(1)} %stack.3.refs_0_, bf16[4,16,1152]{2,1,0:T(8,128)(2,1)S(1)} %collective-permute-done.29.refs_1_, bf16[4,16,1152]{2,1,0:T(8,128)(2,1)S(1)} %collective-permute-done.30.refs_2_, bf16[4,16,1152]{2,1,0:T(8,128)(2,1)S(1)} %collective-permute-done.31.refs_3_, ...), custom_call_target="tpu_custom_call" | custom-call | flops 1610612736 | tf_op jit(solution)/shard_map/project/pallas_call | solution.py:50
  76.6 4.1 %grad.1 = (f32[4,32,1024]{2,1,0:T(8,128)S(1)}, bf16[4,32,1024]{2,1,0:T(8,128)(2,1)S(1)}, bf16[64,768]{1,0:T(8,128)(2,1)S(1)}, f32[1,1]{1,0:T(1,128)}) custom-call(bf16[4,16,1152]{2,1,0:T(8,128)(2,1)S(1)} %collective-permute-done.25.refs_0_, bf16[4,16,1152]{2,1,0:T(8,128)(2,1)S(1)} %collective-permute-done.26.refs_1_, ...), custom_call_target="tpu_custom_call" | custom-call | flops 1610612736 | tf_op jit(solution)/shard_map/grad/pallas_call | solution.py:50
  80.7 0.6 collective-permute-start.32
  81.3 1.2 %grad_rest.1 = (f32[4,32,1024]{2,1,0:T(8,128)S(1)}, bf16[4,32,1024]{2,1,0:T(8,128)(2,1)S(1)}) custom-call(bf16[64,768]{1,0:T(8,128)(2,1)S(1)} %get-tuple-element.75.left_ref, bf16[4,768,1024]{2,1,0:T(8,128)(2,1)S(1)} %get-tuple-element.49.refs_4_.held_ref), custom_call_target="tpu_custom_call" | custom-call | flops 1610612736 | tf_op jit(solution)/shard_map/grad_rest/pallas_call | solution.py:50
  82.9 2.3 %collective-permute-start.34 = (bf16[4,16,1024]{2,1,0:T(8,128)(2,1)S(1)}, bf16[4,16,1024]{2,1,0:T(8,128)(2,1)S(1)}, u32[]{:S(2)}, u32[]{:S(2)}) collective-permute-start(bf16[4,16,1024]{2,1,0:T(8,128)(2,1)S(1)} %get-tuple-element.82), channel_id=1, source_target_pairs={{0,6},{1,7},{2,4},{3,5},{4,2},{5,3},{6,0},{7,1},{8,14},{9,15},{10,... | collective-permute-start | bytes 393224 | tf_op jit(solution)/shard_map/ppermute | solution.py:22
  85.8 0.7 collective-permute-start.36
  86.5 3.6 %collective-permute-done.34.refs_1_ = bf16[4,16,1024]{2,1,0:T(8,128)(2,1)S(1)} collective-permute-done((bf16[4,16,1024]{2,1,0:T(8,128)(2,1)S(1)}, bf16[4,16,1024]{2,1,0:T(8,128)(2,1)S(1)}, u32[]{:S(2)}, u32[]{:S(2)}) %collective-permute-start.34) | collective-permute-done | bytes 131104 | tf_op jit(solution)/shard_map/ppermute | solution.py:22
  90.1 2.0 %collective-permute-done.35.refs_2_ = bf16[4,16,1024]{2,1,0:T(8,128)(2,1)S(1)} collective-permute-done((bf16[4,16,1024]{2,1,0:T(8,128)(2,1)S(1)}, bf16[4,16,1024]{2,1,0:T(8,128)(2,1)S(1)}, u32[]{:S(2)}, u32[]{:S(2)}) %collective-permute-start.35) | collective-permute-done | bytes 131104 | tf_op jit(solution)/shard_map/ppermute | solution.py:22
  92.3 2.2 %collective-permute-start.37 = (bf16[1,16,1024]{2,1,0:T(8,128)(2,1)S(1)}, bf16[1,16,1024]{2,1,0:T(8,128)(2,1)S(1)}, u32[]{:S(2)}, u32[]{:S(2)}) collective-permute-start(bf16[1,16,1024]{2,1,0:T(8,128)(2,1)S(1)} %get-tuple-element.86), channel_id=1, source_target_pairs={{0,24},{1,25},{2,26},{3,27},{4,28},{5,29},{6,30},{7,31},{8,16},{9,... | collective-permute-start | bytes 98312 | tf_op jit(solution)/shard_map/ppermute | solution.py:22
  94.5 0.6 collective-permute-start.38
  95.1 1.7 %collective-permute-start.39 = (bf16[1,16,1024]{2,1,0:T(8,128)(2,1)S(1)}, bf16[1,16,1024]{2,1,0:T(8,128)(2,1)S(1)}, u32[]{:S(2)}, u32[]{:S(2)}) collective-permute-start(bf16[1,16,1024]{2,1,0:T(8,128)(2,1)S(1)} %get-tuple-element.88), channel_id=1, source_target_pairs={{0,8},{1,9},{2,10},{3,11},{4,12},{5,13},{6,14},{7,15},{8,0},{9,1},... | collective-permute-start | bytes 98312 | tf_op jit(solution)/shard_map/ppermute | solution.py:22
  96.7 2.9 %head_weight_grad.1 = f32[1024,1024]{1,0:T(8,128)} custom-call(f32[16,1024]{1,0:T(8,128)S(1)} %get-tuple-element.89.normed_ref, f32[1,1024]{1,0:T(1,128)S(1)} %get-tuple-element.90.bias_grad_ref), custom_call_target="tpu_custom_call" | custom-call | tf_op jit(solution)/shard_map/head_weight_grad/pallas_call | solution.py:365
  99.7 0.6 far_sum.1
  (58 shorter events, 6.9 us)
Async XLA Ops:
  0.6 10.5 %collective-permute-start = (bf16[16,1024]{1,0:T(8,128)(2,1)}, bf16[16,1024]{1,0:T(8,128)(2,1)S(1)}, u32[]{:S(2)}, u32[]{:S(2)}) collective-permute-start(bf16[16,1024]{1,0:T(8,128)(2,1)} %refs_0_.1), channel_id=1, source_target_pairs={{0,8},{1,9},{2,10},{3,11},{4,12},{5,13},{6,14},{7,15},{8,0},{9,1},... | collective-permute-start | bytes 98312 | tf_op jit(solution)/shard_map/ppermute | solution.py:22
  3.7 7.4 %collective-permute-start.2 = (bf16[16,1024]{1,0:T(8,128)(2,1)}, bf16[16,1024]{1,0:T(8,128)(2,1)S(1)}, u32[]{:S(2)}, u32[]{:S(2)}) collective-permute-start(bf16[16,1024]{1,0:T(8,128)(2,1)} %refs_0_.1), channel_id=1, source_target_pairs={{0,24},{1,25},{2,26},{3,27},{4,28},{5,29},{6,30},{7,31},{8,16},{9,... | collective-permute-start | bytes 98312 | tf_op jit(solution)/shard_map/ppermute | solution.py:22
  6.2 5.4 %collective-permute-start.1 = (bf16[16,1024]{1,0:T(8,128)(2,1)}, bf16[16,1024]{1,0:T(8,128)(2,1)S(1)}, u32[]{:S(2)}, u32[]{:S(2)}) collective-permute-start(bf16[16,1024]{1,0:T(8,128)(2,1)} %refs_0_.1), channel_id=1, source_target_pairs={{0,16},{1,17},{2,18},{3,19},{4,20},{5,21},{6,22},{7,23},{8,24},{9,... | collective-permute-start | bytes 98312 | tf_op jit(solution)/shard_map/ppermute | solution.py:22
  11.6 6.8 %collective-permute-start.7 = (bf16[4,16,1024]{2,1,0:T(8,128)(2,1)S(1)}, bf16[4,16,1024]{2,1,0:T(8,128)(2,1)S(1)}, u32[]{:S(2)}, u32[]{:S(2)}) collective-permute-start(bf16[4,16,1024]{2,1,0:T(8,128)(2,1)S(1)} %stack.2.refs_0_), channel_id=1, source_target_pairs={{0,2},{1,3},{2,0},{3,1},{4,6},{5,7},{6,4},{7,5},{8,10},{9,11},{10,... | collective-permute-start | bytes 393224 | tf_op jit(solution)/shard_map/ppermute | solution.py:22
  13.2 6.3 %collective-permute-start.4 = (bf16[4,16,1024]{2,1,0:T(8,128)(2,1)S(1)}, bf16[4,16,1024]{2,1,0:T(8,128)(2,1)S(1)}, u32[]{:S(2)}, u32[]{:S(2)}) collective-permute-start(bf16[4,16,1024]{2,1,0:T(8,128)(2,1)S(1)} %stack.2.refs_0_), channel_id=1, source_target_pairs={{0,6},{1,7},{2,4},{3,5},{4,2},{5,3},{6,0},{7,1},{8,14},{9,15},{10,... | collective-permute-start | bytes 393224 | tf_op jit(solution)/shard_map/ppermute | solution.py:22
  14.6 5.4 %collective-permute-start.3 = (bf16[4,16,1024]{2,1,0:T(8,128)(2,1)S(1)}, bf16[4,16,1024]{2,1,0:T(8,128)(2,1)S(1)}, u32[]{:S(2)}, u32[]{:S(2)}) collective-permute-start(bf16[4,16,1024]{2,1,0:T(8,128)(2,1)S(1)} %stack.2.refs_0_), channel_id=1, source_target_pairs={{0,4},{1,5},{2,6},{3,7},{4,0},{5,1},{6,2},{7,3},{8,12},{9,13},{10,... | collective-permute-start | bytes 393224 | tf_op jit(solution)/shard_map/ppermute | solution.py:22
  15.1 4.9 %collective-permute-start.8 = (bf16[4,16,1024]{2,1,0:T(8,128)(2,1)S(1)}, bf16[4,16,1024]{2,1,0:T(8,128)(2,1)S(1)}, u32[]{:S(2)}, u32[]{:S(2)}) collective-permute-start(bf16[4,16,1024]{2,1,0:T(8,128)(2,1)S(1)} %stack.2.refs_0_), channel_id=1, source_target_pairs={{0,1},{1,0},{2,3},{3,2},{4,5},{5,4},{6,7},{7,6},{8,9},{9,8},{10,11... | collective-permute-start | bytes 393224 | tf_op jit(solution)/shard_map/ppermute | solution.py:22
  18.3 1.7 %collective-permute-start.9 = (bf16[4,16,1024]{2,1,0:T(8,128)(2,1)S(1)}, bf16[4,16,1024]{2,1,0:T(8,128)(2,1)S(1)}, u32[]{:S(2)}, u32[]{:S(2)}) collective-permute-start(bf16[4,16,1024]{2,1,0:T(8,128)(2,1)S(1)} %collective-permute-done.7.refs_1_), channel_id=1, source_target_pairs={{0,1},{1,0},{2,3},{3,2},{4,5},{5,4},{6,7},{7,6},{8,9},{9,8},{10,11... | collective-permute-start | bytes 393224 | tf_op jit(solution)/shard_map/ppermute | solution.py:22
  19.5 2.5 %collective-permute-start.6 = (bf16[4,16,1024]{2,1,0:T(8,128)(2,1)S(1)}, bf16[4,16,1024]{2,1,0:T(8,128)(2,1)S(1)}, u32[]{:S(2)}, u32[]{:S(2)}) collective-permute-start(bf16[4,16,1024]{2,1,0:T(8,128)(2,1)S(1)} %collective-permute-done.4.refs_1_), channel_id=1, source_target_pairs={{0,1},{1,0},{2,3},{3,2},{4,5},{5,4},{6,7},{7,6},{8,9},{9,8},{10,11... | collective-permute-start | bytes 393224 | tf_op jit(solution)/shard_map/ppermute | solution.py:22
  20.0 2.1 %collective-permute-start.5 = (bf16[4,16,1024]{2,1,0:T(8,128)(2,1)S(1)}, bf16[4,16,1024]{2,1,0:T(8,128)(2,1)S(1)}, u32[]{:S(2)}, u32[]{:S(2)}) collective-permute-start(bf16[4,16,1024]{2,1,0:T(8,128)(2,1)S(1)} %collective-permute-done.3.refs_0_), channel_id=1, source_target_pairs={{0,1},{1,0},{2,3},{3,2},{4,5},{5,4},{6,7},{7,6},{8,9},{9,8},{10,11... | collective-permute-start | bytes 393224 | tf_op jit(solution)/shard_map/ppermute | solution.py:22
  26.1 20.7 %copy-start = (bf16[1024,1024]{1,0:T(8,128)(2,1)S(1)}, bf16[1024,1024]{1,0:T(8,128)(2,1)}, u32[]{:S(2)}) copy-start(bf16[1024,1024]{1,0:T(8,128)(2,1)} %refs_3_.1) | copy-start | bytes 6291460
  26.1 31.5 %copy-start.1 = (f32[1024]{0:T(1024)S(1)}, f32[1024]{0:T(1024)}, u32[]{:S(2)}) copy-start(f32[1024]{0:T(1024)} %param.12) | copy-start | bytes 12292
  26.2 31.5 %copy-start.2 = (s32[1024]{0:T(1024)S(1)}, s32[1024]{0:T(1024)}, u32[]{:S(2)}) copy-start(s32[1024]{0:T(1024)} %param.13) | copy-start | bytes 12292
  26.2 1.8 %collective-permute-start.10 = (bf16[4,32,1152]{2,1,0:T(8,128)(2,1)S(1)}, bf16[4,32,1152]{2,1,0:T(8,128)(2,1)S(1)}, u32[]{:S(2)}, u32[]{:S(2)}) collective-permute-start(bf16[4,32,1152]{2,1,0:T(8,128)(2,1)S(1)} %get-tuple-element.55), channel_id=1, source_target_pairs={{0,1},{1,0},{2,3},{3,2},{4,5},{5,4},{6,7},{7,6},{8,9},{9,8},{10,11... | collective-permute-start | bytes 884744 | tf_op jit(solution)/shard_map/ppermute | solution.py:22
  28.3 3.4 %collective-permute-start.11 = (bf16[4,32,1152]{2,1,0:T(8,128)(2,1)S(1)}, bf16[4,32,1152]{2,1,0:T(8,128)(2,1)S(1)}, u32[]{:S(2)}, u32[]{:S(2)}) collective-permute-start(bf16[4,32,1152]{2,1,0:T(8,128)(2,1)S(1)} %get-tuple-element.57), channel_id=1, source_target_pairs={{0,1},{1,0},{2,3},{3,2},{4,5},{5,4},{6,7},{7,6},{8,9},{9,8},{10,11... | collective-permute-start | bytes 884744 | tf_op jit(solution)/shard_map/ppermute | solution.py:22
  28.7 7.6 %collective-permute-start.12 = (bf16[4,16,1152]{2,1,0:T(8,128)(2,1)S(1)}, bf16[4,16,1152]{2,1,0:T(8,128)(2,1)S(1)}, u32[]{:S(2)}, u32[]{:S(2)}) collective-permute-start(bf16[4,16,1152]{2,1,0:T(8,128)(2,1)S(1)} %get-tuple-element.59), channel_id=1, source_target_pairs={{0,6},{1,7},{2,4},{3,5},{4,2},{5,3},{6,0},{7,1},{8,14},{9,15},{10,... | collective-permute-start | bytes 442376 | tf_op jit(solution)/shard_map/ppermute | solution.py:22
  31.1 7.6 %collective-permute-start.13 = (bf16[4,16,1152]{2,1,0:T(8,128)(2,1)S(1)}, bf16[4,16,1152]{2,1,0:T(8,128)(2,1)S(1)}, u32[]{:S(2)}, u32[]{:S(2)}) collective-permute-start(bf16[4,16,1152]{2,1,0:T(8,128)(2,1)S(1)} %get-tuple-element.60), channel_id=1, source_target_pairs={{0,4},{1,5},{2,6},{3,7},{4,0},{5,1},{6,2},{7,3},{8,12},{9,13},{10,... | collective-permute-start | bytes 442376 | tf_op jit(solution)/shard_map/ppermute | solution.py:22
  32.0 6.7 %collective-permute-start.14 = (bf16[4,16,1152]{2,1,0:T(8,128)(2,1)S(1)}, bf16[4,16,1152]{2,1,0:T(8,128)(2,1)S(1)}, u32[]{:S(2)}, u32[]{:S(2)}) collective-permute-start(bf16[4,16,1152]{2,1,0:T(8,128)(2,1)S(1)} %get-tuple-element.61), channel_id=1, source_target_pairs={{0,2},{1,3},{2,0},{3,1},{4,6},{5,7},{6,4},{7,5},{8,10},{9,11},{10,... | collective-permute-start | bytes 442376 | tf_op jit(solution)/shard_map/ppermute | solution.py:22
  39.0 6.2 %collective-permute-start.15 = (bf16[1,16,1152]{2,1,0:T(8,128)(2,1)S(1)}, bf16[1,16,1152]{2,1,0:T(8,128)(2,1)S(1)}, u32[]{:S(2)}, u32[]{:S(2)}) collective-permute-start(bf16[1,16,1152]{2,1,0:T(8,128)(2,1)S(1)} %get-tuple-element.64), channel_id=1, source_target_pairs={{0,24},{1,25},{2,26},{3,27},{4,28},{5,29},{6,30},{7,31},{8,16},{9,... | collective-permute-start | bytes 110600 | tf_op jit(solution)/shard_map/ppermute | solution.py:22
  41.7 5.1 %collective-permute-start.16 = (bf16[1,16,1152]{2,1,0:T(8,128)(2,1)S(1)}, bf16[1,16,1152]{2,1,0:T(8,128)(2,1)S(1)}, u32[]{:S(2)}, u32[]{:S(2)}) collective-permute-start(bf16[1,16,1152]{2,1,0:T(8,128)(2,1)S(1)} %get-tuple-element.65), channel_id=1, source_target_pairs={{0,16},{1,17},{2,18},{3,19},{4,20},{5,21},{6,22},{7,23},{8,24},{9,... | collective-permute-start | bytes 110600 | tf_op jit(solution)/shard_map/ppermute | solution.py:22
  42.1 4.8 %collective-permute-start.17 = (bf16[1,16,1152]{2,1,0:T(8,128)(2,1)S(1)}, bf16[1,16,1152]{2,1,0:T(8,128)(2,1)S(1)}, u32[]{:S(2)}, u32[]{:S(2)}) collective-permute-start(bf16[1,16,1152]{2,1,0:T(8,128)(2,1)S(1)} %get-tuple-element.66), channel_id=1, source_target_pairs={{0,8},{1,9},{2,10},{3,11},{4,12},{5,13},{6,14},{7,15},{8,0},{9,1},... | collective-permute-start | bytes 110600 | tf_op jit(solution)/shard_map/ppermute | solution.py:22
  47.5 5.5 %collective-permute-start.20 = (f32[2,1024]{1,0:T(2,128)S(1)}, f32[2,1024]{1,0:T(2,128)S(1)}, u32[]{:S(2)}, u32[]{:S(2)}) collective-permute-start(f32[2,1024]{1,0:T(2,128)S(1)} %get-tuple-element.69.refs_0_), channel_id=1, source_target_pairs={{0,24},{1,25},{2,26},{3,27},{4,28},{5,29},{6,30},{7,31},{8,16},{9,... | collective-permute-start | bytes 24584 | tf_op jit(solution)/shard_map/ppermute | solution.py:22
  49.4 4.5 %collective-permute-start.19 = (f32[2,1024]{1,0:T(2,128)S(1)}, f32[2,1024]{1,0:T(2,128)S(1)}, u32[]{:S(2)}, u32[]{:S(2)}) collective-permute-start(f32[2,1024]{1,0:T(2,128)S(1)} %get-tuple-element.69.refs_0_), channel_id=1, source_target_pairs={{0,16},{1,17},{2,18},{3,19},{4,20},{5,21},{6,22},{7,23},{8,24},{9,... | collective-permute-start | bytes 24584 | tf_op jit(solution)/shard_map/ppermute | solution.py:22
  49.6 4.4 %collective-permute-start.18 = (f32[2,1024]{1,0:T(2,128)S(1)}, f32[2,1024]{1,0:T(2,128)S(1)}, u32[]{:S(2)}, u32[]{:S(2)}) collective-permute-start(f32[2,1024]{1,0:T(2,128)S(1)} %get-tuple-element.69.refs_0_), channel_id=1, source_target_pairs={{0,8},{1,9},{2,10},{3,11},{4,12},{5,13},{6,14},{7,15},{8,0},{9,1},... | collective-permute-start | bytes 24584 | tf_op jit(solution)/shard_map/ppermute | solution.py:22
  54.0 3.7 %collective-permute-start.21 = (f32[2,1024]{1,0:T(2,128)S(1)}, f32[2,1024]{1,0:T(2,128)S(1)}, u32[]{:S(2)}, u32[]{:S(2)}) collective-permute-start(f32[2,1024]{1,0:T(2,128)S(1)} %tree_sum.1.sums_ref), channel_id=1, source_target_pairs={{0,4},{1,5},{2,6},{3,7},{4,0},{5,1},{6,2},{7,3},{8,12},{9,13},{10,... | collective-permute-start | bytes 24584 | tf_op jit(solution)/shard_map/ppermute | solution.py:22
  58.9 5.8 %collective-permute-start.24 = (bf16[16,1152]{1,0:T(8,128)(2,1)S(1)}, bf16[16,1152]{1,0:T(8,128)(2,1)S(1)}, u32[]{:S(2)}, u32[]{:S(2)}) collective-permute-start(bf16[16,1152]{1,0:T(8,128)(2,1)S(1)} %get-tuple-element.72.refs_0_), channel_id=1, source_target_pairs={{0,24},{1,25},{2,26},{3,27},{4,28},{5,29},{6,30},{7,31},{8,16},{9,... | collective-permute-start | bytes 110600 | tf_op jit(solution)/shard_map/ppermute | solution.py:22
  60.9 5.3 %collective-permute-start.23 = (bf16[16,1152]{1,0:T(8,128)(2,1)S(1)}, bf16[16,1152]{1,0:T(8,128)(2,1)S(1)}, u32[]{:S(2)}, u32[]{:S(2)}) collective-permute-start(bf16[16,1152]{1,0:T(8,128)(2,1)S(1)} %get-tuple-element.72.refs_0_), channel_id=1, source_target_pairs={{0,16},{1,17},{2,18},{3,19},{4,20},{5,21},{6,22},{7,23},{8,24},{9,... | collective-permute-start | bytes 110600 | tf_op jit(solution)/shard_map/ppermute | solution.py:22
  61.9 4.3 %collective-permute-start.22 = (bf16[16,1152]{1,0:T(8,128)(2,1)S(1)}, bf16[16,1152]{1,0:T(8,128)(2,1)S(1)}, u32[]{:S(2)}, u32[]{:S(2)}) collective-permute-start(bf16[16,1152]{1,0:T(8,128)(2,1)S(1)} %get-tuple-element.72.refs_0_), channel_id=1, source_target_pairs={{0,8},{1,9},{2,10},{3,11},{4,12},{5,13},{6,14},{7,15},{8,0},{9,1},... | collective-permute-start | bytes 110600 | tf_op jit(solution)/shard_map/ppermute | solution.py:22
  66.3 5.2 %collective-permute-start.29 = (bf16[4,16,1152]{2,1,0:T(8,128)(2,1)S(1)}, bf16[4,16,1152]{2,1,0:T(8,128)(2,1)S(1)}, u32[]{:S(2)}, u32[]{:S(2)}) collective-permute-start(bf16[4,16,1152]{2,1,0:T(8,128)(2,1)S(1)} %stack.3.refs_0_), channel_id=1, source_target_pairs={{0,2},{1,3},{2,0},{3,1},{4,6},{5,7},{6,4},{7,5},{8,10},{9,11},{10,... | collective-permute-start | bytes 442376 | tf_op jit(solution)/shard_map/ppermute | solution.py:22
  67.7 6.0 %collective-permute-start.26 = (bf16[4,16,1152]{2,1,0:T(8,128)(2,1)S(1)}, bf16[4,16,1152]{2,1,0:T(8,128)(2,1)S(1)}, u32[]{:S(2)}, u32[]{:S(2)}) collective-permute-start(bf16[4,16,1152]{2,1,0:T(8,128)(2,1)S(1)} %stack.3.refs_0_), channel_id=1, source_target_pairs={{0,6},{1,7},{2,4},{3,5},{4,2},{5,3},{6,0},{7,1},{8,14},{9,15},{10,... | collective-permute-start | bytes 442376 | tf_op jit(solution)/shard_map/ppermute | solution.py:22
  69.3 5.2 %collective-permute-start.25 = (bf16[4,16,1152]{2,1,0:T(8,128)(2,1)S(1)}, bf16[4,16,1152]{2,1,0:T(8,128)(2,1)S(1)}, u32[]{:S(2)}, u32[]{:S(2)}) collective-permute-start(bf16[4,16,1152]{2,1,0:T(8,128)(2,1)S(1)} %stack.3.refs_0_), channel_id=1, source_target_pairs={{0,4},{1,5},{2,6},{3,7},{4,0},{5,1},{6,2},{7,3},{8,12},{9,13},{10,... | collective-permute-start | bytes 442376 | tf_op jit(solution)/shard_map/ppermute | solution.py:22
  69.9 4.7 %collective-permute-start.30 = (bf16[4,16,1152]{2,1,0:T(8,128)(2,1)S(1)}, bf16[4,16,1152]{2,1,0:T(8,128)(2,1)S(1)}, u32[]{:S(2)}, u32[]{:S(2)}) collective-permute-start(bf16[4,16,1152]{2,1,0:T(8,128)(2,1)S(1)} %stack.3.refs_0_), channel_id=1, source_target_pairs={{0,1},{1,0},{2,3},{3,2},{4,5},{5,4},{6,7},{7,6},{8,9},{9,8},{10,11... | collective-permute-start | bytes 442376 | tf_op jit(solution)/shard_map/ppermute | solution.py:22
  71.5 3.1 %collective-permute-start.31 = (bf16[4,16,1152]{2,1,0:T(8,128)(2,1)S(1)}, bf16[4,16,1152]{2,1,0:T(8,128)(2,1)S(1)}, u32[]{:S(2)}, u32[]{:S(2)}) collective-permute-start(bf16[4,16,1152]{2,1,0:T(8,128)(2,1)S(1)} %collective-permute-done.29.refs_1_), channel_id=1, source_target_pairs={{0,1},{1,0},{2,3},{3,2},{4,5},{5,4},{6,7},{7,6},{8,9},{9,8},{10,11... | collective-permute-start | bytes 442376 | tf_op jit(solution)/shard_map/ppermute | solution.py:22
  73.8 2.9 %collective-permute-start.28 = (bf16[4,16,1152]{2,1,0:T(8,128)(2,1)S(1)}, bf16[4,16,1152]{2,1,0:T(8,128)(2,1)S(1)}, u32[]{:S(2)}, u32[]{:S(2)}) collective-permute-start(bf16[4,16,1152]{2,1,0:T(8,128)(2,1)S(1)} %collective-permute-done.26.refs_1_), channel_id=1, source_target_pairs={{0,1},{1,0},{2,3},{3,2},{4,5},{5,4},{6,7},{7,6},{8,9},{9,8},{10,11... | collective-permute-start | bytes 442376 | tf_op jit(solution)/shard_map/ppermute | solution.py:22
  74.6 2.1 %collective-permute-start.27 = (bf16[4,16,1152]{2,1,0:T(8,128)(2,1)S(1)}, bf16[4,16,1152]{2,1,0:T(8,128)(2,1)S(1)}, u32[]{:S(2)}, u32[]{:S(2)}) collective-permute-start(bf16[4,16,1152]{2,1,0:T(8,128)(2,1)S(1)} %collective-permute-done.25.refs_0_), channel_id=1, source_target_pairs={{0,1},{1,0},{2,3},{3,2},{4,5},{5,4},{6,7},{7,6},{8,9},{9,8},{10,11... | collective-permute-start | bytes 442376 | tf_op jit(solution)/shard_map/ppermute | solution.py:22
  80.7 1.8 %collective-permute-start.32 = (bf16[4,32,1024]{2,1,0:T(8,128)(2,1)S(1)}, bf16[4,32,1024]{2,1,0:T(8,128)(2,1)S(1)}, u32[]{:S(2)}, u32[]{:S(2)}) collective-permute-start(bf16[4,32,1024]{2,1,0:T(8,128)(2,1)S(1)} %get-tuple-element.78), channel_id=1, source_target_pairs={{0,1},{1,0},{2,3},{3,2},{4,5},{5,4},{6,7},{7,6},{8,9},{9,8},{10,11... | collective-permute-start | bytes 786440 | tf_op jit(solution)/shard_map/ppermute | solution.py:22
  82.5 3.2 %collective-permute-start.33 = (bf16[4,32,1024]{2,1,0:T(8,128)(2,1)S(1)}, bf16[4,32,1024]{2,1,0:T(8,128)(2,1)S(1)}, u32[]{:S(2)}, u32[]{:S(2)}) collective-permute-start(bf16[4,32,1024]{2,1,0:T(8,128)(2,1)S(1)} %get-tuple-element.80), channel_id=1, source_target_pairs={{0,1},{1,0},{2,3},{3,2},{4,5},{5,4},{6,7},{7,6},{8,9},{9,8},{10,11... | collective-permute-start | bytes 786440 | tf_op jit(solution)/shard_map/ppermute | solution.py:22
  82.9 7.2 %collective-permute-start.34 = (bf16[4,16,1024]{2,1,0:T(8,128)(2,1)S(1)}, bf16[4,16,1024]{2,1,0:T(8,128)(2,1)S(1)}, u32[]{:S(2)}, u32[]{:S(2)}) collective-permute-start(bf16[4,16,1024]{2,1,0:T(8,128)(2,1)S(1)} %get-tuple-element.82), channel_id=1, source_target_pairs={{0,6},{1,7},{2,4},{3,5},{4,2},{5,3},{6,0},{7,1},{8,14},{9,15},{10,... | collective-permute-start | bytes 393224 | tf_op jit(solution)/shard_map/ppermute | solution.py:22
  85.2 6.9 %collective-permute-start.35 = (bf16[4,16,1024]{2,1,0:T(8,128)(2,1)S(1)}, bf16[4,16,1024]{2,1,0:T(8,128)(2,1)S(1)}, u32[]{:S(2)}, u32[]{:S(2)}) collective-permute-start(bf16[4,16,1024]{2,1,0:T(8,128)(2,1)S(1)} %get-tuple-element.83), channel_id=1, source_target_pairs={{0,4},{1,5},{2,6},{3,7},{4,0},{5,1},{6,2},{7,3},{8,12},{9,13},{10,... | collective-permute-start | bytes 393224 | tf_op jit(solution)/shard_map/ppermute | solution.py:22
  85.8 6.5 %collective-permute-start.36 = (bf16[4,16,1024]{2,1,0:T(8,128)(2,1)S(1)}, bf16[4,16,1024]{2,1,0:T(8,128)(2,1)S(1)}, u32[]{:S(2)}, u32[]{:S(2)}) collective-permute-start(bf16[4,16,1024]{2,1,0:T(8,128)(2,1)S(1)} %get-tuple-element.84), channel_id=1, source_target_pairs={{0,2},{1,3},{2,0},{3,1},{4,6},{5,7},{6,4},{7,5},{8,10},{9,11},{10,... | collective-permute-start | bytes 393224 | tf_op jit(solution)/shard_map/ppermute | solution.py:22
  92.3 7.4 %collective-permute-start.37 = (bf16[1,16,1024]{2,1,0:T(8,128)(2,1)S(1)}, bf16[1,16,1024]{2,1,0:T(8,128)(2,1)S(1)}, u32[]{:S(2)}, u32[]{:S(2)}) collective-permute-start(bf16[1,16,1024]{2,1,0:T(8,128)(2,1)S(1)} %get-tuple-element.86), channel_id=1, source_target_pairs={{0,24},{1,25},{2,26},{3,27},{4,28},{5,29},{6,30},{7,31},{8,16},{9,... | collective-permute-start | bytes 98312 | tf_op jit(solution)/shard_map/ppermute | solution.py:22
  94.5 5.2 %collective-permute-start.38 = (bf16[1,16,1024]{2,1,0:T(8,128)(2,1)S(1)}, bf16[1,16,1024]{2,1,0:T(8,128)(2,1)S(1)}, u32[]{:S(2)}, u32[]{:S(2)}) collective-permute-start(bf16[1,16,1024]{2,1,0:T(8,128)(2,1)S(1)} %get-tuple-element.87), channel_id=1, source_target_pairs={{0,16},{1,17},{2,18},{3,19},{4,20},{5,21},{6,22},{7,23},{8,24},{9,... | collective-permute-start | bytes 98312 | tf_op jit(solution)/shard_map/ppermute | solution.py:22
  95.1 4.6 %collective-permute-start.39 = (bf16[1,16,1024]{2,1,0:T(8,128)(2,1)S(1)}, bf16[1,16,1024]{2,1,0:T(8,128)(2,1)S(1)}, u32[]{:S(2)}, u32[]{:S(2)}) collective-permute-start(bf16[1,16,1024]{2,1,0:T(8,128)(2,1)S(1)} %get-tuple-element.88), channel_id=1, source_target_pairs={{0,8},{1,9},{2,10},{3,11},{4,12},{5,13},{6,14},{7,15},{8,0},{9,1},... | collective-permute-start | bytes 98312 | tf_op jit(solution)/shard_map/ppermute | solution.py:22

commit v13 on v12

--- a/solution.py
+++ b/solution.py
@@ -347,14 +347,18 @@
     normed_ref[...] = unit * gain
 
 
-def head_weight_grad_kernel(attributes, normed_ref, bias_grad_ref, out_ref):
+def head_weight_grad_kernel(attributes, normed_ref, bias_grad_ref, out_ref, parts_ref):
     heads = normed_ref.shape[0]
     columns = out_ref.shape[1]
-    parts = jnp.concatenate(pieces(normed_ref[...]), axis=0)
+
+    @pl.when(pl.program_id(0) == 0)
+    def _():
+        parts_ref[...] = jnp.concatenate([x.astype(F32) for x in pieces(normed_ref[...])], axis=0).T.astype(BF16)
+
     row = lax.broadcasted_iota(jnp.int32, (3 * heads, columns), 0) % heads
     column = pl.program_id(0) * columns + lax.broadcasted_iota(jnp.int32, (3 * heads, columns), 1)
     ones = jnp.where(column // attributes == row, 1.0, 0.0).astype(BF16)
-    normed = lax.dot_general(parts, ones, (((0,), (0,)), ((), ())), preferred_element_type=F32)
+    normed = jnp.dot(parts_ref[...], ones, preferred_element_type=F32)
     out_ref[...] = normed * bias_grad_ref[...]
 
 
@@ -371,6 +375,7 @@
             pl.BlockSpec((1, block), lambda i: (0, i)),
         ],
         out_specs=pl.BlockSpec((width, block), lambda i: (0, i)),
+        scratch_shapes=[pltpu.VMEM((width, 3 * rows), BF16)],
         compiler_params=pltpu.CompilerParams(vmem_limit_bytes=16 * MIB),
         name="head_weight_grad",
     )(normed, bias_grad)

time: 101 us -> 101 us (level)
  no operation moved by 1% of the time
where the time goes in v13:
time: 101 us; the launch traced here: 100 us
  starting transfers between devices  41.2 us (41%)
  waiting for transfers between devices  31.7 us (31%)
  Pallas kernels  26 us (26%)
  between operations  1.5 us (1%)
    ppermute x40, starting transfers between devices, swap(): return lax.ppermute(x, ('ctx', 'cls'), pairs)  41.2 us
    ppermute x40, waiting for transfers between devices, swap(): return lax.ppermute(x, ('ctx', 'cls'), pairs)  31.7 us
    pallas_call x18, Pallas kernels, call(): return list(run(*args))  18.2 us
    pallas_call x1, Pallas kernels, load(): run(*[pltpu.with_memory_space_constraint(x, pltpu.HBM) for x in (tokens,...  4.79 us
    pallas_call x1, Pallas kernels, head_weight_grad(): pl.pallas_call(functools.partial(head_weight_grad_kernel, columns // rows...  2.99 us
  transfers between devices with their start and end apart: 40, of which 20 were waited for; matrix products, arithmetic and copies ran while one was open for 0% of the time, Pallas kernels for 15%

profile of v13, /device:TPU:0, one launch (start us, length us, event | category | flops | bytes accessed | tf_op | source)
XLA Modules:
  0.0 100.4 jit_solution(8261408715354050204)
XLA Ops:
  0.6 3.1 %collective-permute-start = (bf16[16,1024]{1,0:T(8,128)(2,1)}, bf16[16,1024]{1,0:T(8,128)(2,1)S(1)}, u32[]{:S(2)}, u32[]{:S(2)}) collective-permute-start(bf16[16,1024]{1,0:T(8,128)(2,1)} %refs_0_.1), channel_id=1, source_target_pairs={{0,8},{1,9},{2,10},{3,11},{4,12},{5,13},{6,14},{7,15},{8,0},{9,1},... | collective-permute-start | bytes 98312 | tf_op jit(solution)/shard_map/ppermute | solution.py:22
  3.7 2.5 %collective-permute-start.2 = (bf16[16,1024]{1,0:T(8,128)(2,1)}, bf16[16,1024]{1,0:T(8,128)(2,1)S(1)}, u32[]{:S(2)}, u32[]{:S(2)}) collective-permute-start(bf16[16,1024]{1,0:T(8,128)(2,1)} %refs_0_.1), channel_id=1, source_target_pairs={{0,24},{1,25},{2,26},{3,27},{4,28},{5,29},{6,30},{7,31},{8,16},{9,... | collective-permute-start | bytes 98312 | tf_op jit(solution)/shard_map/ppermute | solution.py:22
  6.3 4.8 %load.1 = (bf16[4,768,1024]{2,1,0:T(8,128)(2,1)S(1)}, bf16[4,768,1024]{2,1,0:T(8,128)(2,1)S(1)}, bf16[16,1024]{1,0:T(8,128)(2,1)S(1)}, f32[1,1024]{1,0:T(1,128)S(1)}) custom-call(bf16[768,8192]{1,0:T(8,128)(2,1)} %tokens_ref.1, bf16[16,1024]{1,0:T(8,128)(2,1)} %refs_0_.1, f32[1,1024]{1,0:T(1,128)} %bitcast.7), custom_call_target="tpu_custom_call" | custom-call | tf_op jit(solution)/shard_map/load/pallas_call | solution.py:123
  11.6 1.6 %collective-permute-start.7 = (bf16[4,16,1024]{2,1,0:T(8,128)(2,1)S(1)}, bf16[4,16,1024]{2,1,0:T(8,128)(2,1)S(1)}, u32[]{:S(2)}, u32[]{:S(2)}) collective-permute-start(bf16[4,16,1024]{2,1,0:T(8,128)(2,1)S(1)} %stack.2.refs_0_), channel_id=1, source_target_pairs={{0,2},{1,3},{2,0},{3,1},{4,6},{5,7},{6,4},{7,5},{8,10},{9,11},{10,... | collective-permute-start | bytes 393224 | tf_op jit(solution)/shard_map/ppermute | solution.py:22
  13.2 1.4 %collective-permute-start.4 = (bf16[4,16,1024]{2,1,0:T(8,128)(2,1)S(1)}, bf16[4,16,1024]{2,1,0:T(8,128)(2,1)S(1)}, u32[]{:S(2)}, u32[]{:S(2)}) collective-permute-start(bf16[4,16,1024]{2,1,0:T(8,128)(2,1)S(1)} %stack.2.refs_0_), channel_id=1, source_target_pairs={{0,6},{1,7},{2,4},{3,5},{4,2},{5,3},{6,0},{7,1},{8,14},{9,15},{10,... | collective-permute-start | bytes 393224 | tf_op jit(solution)/shard_map/ppermute | solution.py:22
  15.1 3.2 %collective-permute-done.7.refs_1_ = bf16[4,16,1024]{2,1,0:T(8,128)(2,1)S(1)} collective-permute-done((bf16[4,16,1024]{2,1,0:T(8,128)(2,1)S(1)}, bf16[4,16,1024]{2,1,0:T(8,128)(2,1)S(1)}, u32[]{:S(2)}, u32[]{:S(2)}) %collective-permute-start.7) | collective-permute-done | bytes 131104 | tf_op jit(solution)/shard_map/ppermute | solution.py:22
  20.0 2.0 %project.2.refs_4_ = f32[64,768]{1,0:T(8,128)S(1)} custom-call(bf16[4,16,1024]{2,1,0:T(8,128)(2,1)S(1)} %stack.2.refs_0_, bf16[4,16,1024]{2,1,0:T(8,128)(2,1)S(1)} %collective-permute-done.7.refs_1_, bf16[4,16,1024]{2,1,0:T(8,128)(2,1)S(1)} %collective-permute-done.8.refs_2_, bf16[4,16,1024]{2,1,0:T(8,128)(2,1)S(1)} %collective-permute-done.9.refs_3_, ...), custom_call_target="tpu_custom_call" | custom-call | flops 1610612736 | tf_op jit(solution)/shard_map/project/pallas_call | solution.py:50
  22.1 4.1 %pool.1 = (f32[4,32,1024]{2,1,0:T(8,128)S(1)}, bf16[4,32,1152]{2,1,0:T(8,128)(2,1)S(1)}, f32[64,128]{1,0:T(8,128)S(1)}, f32[64,768]{1,0:T(8,128)S(1)}, bf16[64,768]{1,0:T(8,128)(2,1)S(1)}) custom-call(s32[1]{0:T(128)S(6)} %copy.15.length_ref, bf16[4,16,1024]{2,1,0:T(8,128)(2,1)S(1)} %collective-permute-done.3.refs_0_, ...), custom_call_target="tpu_custom_call" | custom-call | flops 1610612736 | tf_op jit(solution)/shard_map/pool/pallas_call | solution.py:50
  26.7 1.2 %pool_rest.1 = (f32[4,32,1024]{2,1,0:T(8,128)S(1)}, bf16[4,32,1152]{2,1,0:T(8,128)(2,1)S(1)}) custom-call(bf16[64,768]{1,0:T(8,128)(2,1)S(1)} %get-tuple-element.51.left_ref, f32[64,128]{1,0:T(8,128)S(1)} %get-tuple-element.52.peak_ref.refs_2_.refs_7_, bf16[4,768,1024]{2,1,0:T(8,128)(2,1)S(1)} %get-tuple-element.49.refs_4_.held_ref), custom_call_target="tpu_custom_call" | custom-call | flops 1610612736 | tf_op jit(solution)/shard_map/pool_rest/pallas_call | solution.py:50
  28.7 2.4 %collective-permute-start.12 = (bf16[4,16,1152]{2,1,0:T(8,128)(2,1)S(1)}, bf16[4,16,1152]{2,1,0:T(8,128)(2,1)S(1)}, u32[]{:S(2)}, u32[]{:S(2)}) collective-permute-start(bf16[4,16,1152]{2,1,0:T(8,128)(2,1)S(1)} %get-tuple-element.59), channel_id=1, source_target_pairs={{0,6},{1,7},{2,4},{3,5},{4,2},{5,3},{6,0},{7,1},{8,14},{9,15},{10,... | collective-permute-start | bytes 442376 | tf_op jit(solution)/shard_map/ppermute | solution.py:22
  32.0 0.6 collective-permute-start.14
  32.6 3.7 %collective-permute-done.12.refs_1_ = bf16[4,16,1152]{2,1,0:T(8,128)(2,1)S(1)} collective-permute-done((bf16[4,16,1152]{2,1,0:T(8,128)(2,1)S(1)}, bf16[4,16,1152]{2,1,0:T(8,128)(2,1)S(1)}, u32[]{:S(2)}, u32[]{:S(2)}) %collective-permute-start.12) | collective-permute-done | bytes 147488 | tf_op jit(solution)/shard_map/ppermute | solution.py:22
  36.3 2.4 %collective-permute-done.13.refs_2_ = bf16[4,16,1152]{2,1,0:T(8,128)(2,1)S(1)} collective-permute-done((bf16[4,16,1152]{2,1,0:T(8,128)(2,1)S(1)}, bf16[4,16,1152]{2,1,0:T(8,128)(2,1)S(1)}, u32[]{:S(2)}, u32[]{:S(2)}) %collective-permute-start.13) | collective-permute-done | bytes 147488 | tf_op jit(solution)/shard_map/ppermute | solution.py:22
  39.0 2.7 %collective-permute-start.15 = (bf16[1,16,1152]{2,1,0:T(8,128)(2,1)S(1)}, bf16[1,16,1152]{2,1,0:T(8,128)(2,1)S(1)}, u32[]{:S(2)}, u32[]{:S(2)}) collective-permute-start(bf16[1,16,1152]{2,1,0:T(8,128)(2,1)S(1)} %get-tuple-element.64), channel_id=1, source_target_pairs={{0,24},{1,25},{2,26},{3,27},{4,28},{5,29},{6,30},{7,31},{8,16},{9,... | collective-permute-start | bytes 110600 | tf_op jit(solution)/shard_map/ppermute | solution.py:22
  42.1 1.4 %collective-permute-start.17 = (bf16[1,16,1152]{2,1,0:T(8,128)(2,1)S(1)}, bf16[1,16,1152]{2,1,0:T(8,128)(2,1)S(1)}, u32[]{:S(2)}, u32[]{:S(2)}) collective-permute-start(bf16[1,16,1152]{2,1,0:T(8,128)(2,1)S(1)} %get-tuple-element.66), channel_id=1, source_target_pairs={{0,8},{1,9},{2,10},{3,11},{4,12},{5,13},{6,14},{7,15},{8,0},{9,1},... | collective-permute-start | bytes 110600 | tf_op jit(solution)/shard_map/ppermute | solution.py:22
  43.5 1.7 %collective-permute-done.15.refs_1_ = bf16[1,16,1152]{2,1,0:T(8,128)(2,1)S(1)} collective-permute-done((bf16[1,16,1152]{2,1,0:T(8,128)(2,1)S(1)}, bf16[1,16,1152]{2,1,0:T(8,128)(2,1)S(1)}, u32[]{:S(2)}, u32[]{:S(2)}) %collective-permute-start.15) | collective-permute-done | bytes 36896 | tf_op jit(solution)/shard_map/ppermute | solution.py:22
  45.2 1.6 %collective-permute-done.16.refs_2_ = bf16[1,16,1152]{2,1,0:T(8,128)(2,1)S(1)} collective-permute-done((bf16[1,16,1152]{2,1,0:T(8,128)(2,1)S(1)}, bf16[1,16,1152]{2,1,0:T(8,128)(2,1)S(1)}, u32[]{:S(2)}, u32[]{:S(2)}) %collective-permute-start.16) | collective-permute-done | bytes 36896 | tf_op jit(solution)/shard_map/ppermute | solution.py:22
  46.9 0.6 head_sums.1
  47.5 1.9 %collective-permute-start.20 = (f32[2,1024]{1,0:T(2,128)S(1)}, f32[2,1024]{1,0:T(2,128)S(1)}, u32[]{:S(2)}, u32[]{:S(2)}) collective-permute-start(f32[2,1024]{1,0:T(2,128)S(1)} %get-tuple-element.69.refs_0_), channel_id=1, source_target_pairs={{0,24},{1,25},{2,26},{3,27},{4,28},{5,29},{6,30},{7,31},{8,16},{9,... | collective-permute-start | bytes 24584 | tf_op jit(solution)/shard_map/ppermute | solution.py:22
  49.6 2.4 %collective-permute-start.18 = (f32[2,1024]{1,0:T(2,128)S(1)}, f32[2,1024]{1,0:T(2,128)S(1)}, u32[]{:S(2)}, u32[]{:S(2)}) collective-permute-start(f32[2,1024]{1,0:T(2,128)S(1)} %get-tuple-element.69.refs_0_), channel_id=1, source_target_pairs={{0,8},{1,9},{2,10},{3,11},{4,12},{5,13},{6,14},{7,15},{8,0},{9,1},... | collective-permute-start | bytes 24584 | tf_op jit(solution)/shard_map/ppermute | solution.py:22
  52.0 1.1 %collective-permute-done.20.refs_3_ = f32[2,1024]{1,0:T(2,128)S(1)} collective-permute-done((f32[2,1024]{1,0:T(2,128)S(1)}, f32[2,1024]{1,0:T(2,128)S(1)}, u32[]{:S(2)}, u32[]{:S(2)}) %collective-permute-start.20) | collective-permute-done | bytes 8224 | tf_op jit(solution)/shard_map/ppermute | solution.py:22
  53.0 0.9 collective-permute-done.19.refs_2_
  54.0 1.6 %collective-permute-start.21 = (f32[2,1024]{1,0:T(2,128)S(1)}, f32[2,1024]{1,0:T(2,128)S(1)}, u32[]{:S(2)}, u32[]{:S(2)}) collective-permute-start(f32[2,1024]{1,0:T(2,128)S(1)} %tree_sum.1.sums_ref), channel_id=1, source_target_pairs={{0,4},{1,5},{2,6},{3,7},{4,0},{5,1},{6,2},{7,3},{8,12},{9,13},{10,... | collective-permute-start | bytes 24584 | tf_op jit(solution)/shard_map/ppermute | solution.py:22
  55.5 2.1 %collective-permute-done.21.other_sums_ref = f32[2,1024]{1,0:T(2,128)S(1)} collective-permute-done((f32[2,1024]{1,0:T(2,128)S(1)}, f32[2,1024]{1,0:T(2,128)S(1)}, u32[]{:S(2)}, u32[]{:S(2)}) %collective-permute-start.21) | collective-permute-done | bytes 8224 | tf_op jit(solution)/shard_map/ppermute | solution.py:22
  57.7 1.2 %head_grads.1 = (f32[1,1024]{1,0:T(1,128)}, f32[1,1024]{1,0:T(1,128)S(1)}, bf16[16,1152]{1,0:T(8,128)(2,1)S(1)}, f32[16,1024]{1,0:T(8,128)S(1)}) custom-call(f32[2,1024]{1,0:T(2,128)S(1)} %tree_sum.1.sums_ref, f32[2,1024]{1,0:T(2,128)S(1)} %collective-permute-done.21.other_sums_ref, f32[16,1024]{1,0:T(8,128)S(1)} %get-tuple-element.70.refs_0_, ...), custom_call_target="tpu_custom_call" | custom-call | tf_op jit(solution)/shard_map/head_grads/pallas_call | solution.py:50
  58.9 2.0 %collective-permute-start.24 = (bf16[16,1152]{1,0:T(8,128)(2,1)S(1)}, bf16[16,1152]{1,0:T(8,128)(2,1)S(1)}, u32[]{:S(2)}, u32[]{:S(2)}) collective-permute-start(bf16[16,1152]{1,0:T(8,128)(2,1)S(1)} %get-tuple-element.72.refs_0_), channel_id=1, source_target_pairs={{0,24},{1,25},{2,26},{3,27},{4,28},{5,29},{6,30},{7,31},{8,16},{9,... | collective-permute-start | bytes 110600 | tf_op jit(solution)/shard_map/ppermute | solution.py:22
  60.9 1.0 %collective-permute-start.23 = (bf16[16,1152]{1,0:T(8,128)(2,1)S(1)}, bf16[16,1152]{1,0:T(8,128)(2,1)S(1)}, u32[]{:S(2)}, u32[]{:S(2)}) collective-permute-start(bf16[16,1152]{1,0:T(8,128)(2,1)S(1)} %get-tuple-element.72.refs_0_), channel_id=1, source_target_pairs={{0,16},{1,17},{2,18},{3,19},{4,20},{5,21},{6,22},{7,23},{8,24},{9,... | collective-permute-start | bytes 110600 | tf_op jit(solution)/shard_map/ppermute | solution.py:22
  61.9 1.4 %collective-permute-start.22 = (bf16[16,1152]{1,0:T(8,128)(2,1)S(1)}, bf16[16,1152]{1,0:T(8,128)(2,1)S(1)}, u32[]{:S(2)}, u32[]{:S(2)}) collective-permute-start(bf16[16,1152]{1,0:T(8,128)(2,1)S(1)} %get-tuple-element.72.refs_0_), channel_id=1, source_target_pairs={{0,8},{1,9},{2,10},{3,11},{4,12},{5,13},{6,14},{7,15},{8,0},{9,1},... | collective-permute-start | bytes 110600 | tf_op jit(solution)/shard_map/ppermute | solution.py:22
  63.3 1.4 %collective-permute-done.24.refs_3_ = bf16[16,1152]{1,0:T(8,128)(2,1)S(1)} collective-permute-done((bf16[16,1152]{1,0:T(8,128)(2,1)S(1)}, bf16[16,1152]{1,0:T(8,128)(2,1)S(1)}, u32[]{:S(2)}, u32[]{:S(2)}) %collective-permute-start.24) | collective-permute-done | bytes 36896 | tf_op jit(solution)/shard_map/ppermute | solution.py:22
  64.7 1.6 %collective-permute-done.23.refs_2_ = bf16[16,1152]{1,0:T(8,128)(2,1)S(1)} collective-permute-done((bf16[16,1152]{1,0:T(8,128)(2,1)S(1)}, bf16[16,1152]{1,0:T(8,128)(2,1)S(1)}, u32[]{:S(2)}, u32[]{:S(2)}) %collective-permute-start.23) | collective-permute-done | bytes 36896 | tf_op jit(solution)/shard_map/ppermute | solution.py:22
  66.3 1.4 %collective-permute-start.29 = (bf16[4,16,1152]{2,1,0:T(8,128)(2,1)S(1)}, bf16[4,16,1152]{2,1,0:T(8,128)(2,1)S(1)}, u32[]{:S(2)}, u32[]{:S(2)}) collective-permute-start(bf16[4,16,1152]{2,1,0:T(8,128)(2,1)S(1)} %stack.3.refs_0_), channel_id=1, source_target_pairs={{0,2},{1,3},{2,0},{3,1},{4,6},{5,7},{6,4},{7,5},{8,10},{9,11},{10,... | collective-permute-start | bytes 442376 | tf_op jit(solution)/shard_map/ppermute | solution.py:22
  67.7 1.6 %collective-permute-start.26 = (bf16[4,16,1152]{2,1,0:T(8,128)(2,1)S(1)}, bf16[4,16,1152]{2,1,0:T(8,128)(2,1)S(1)}, u32[]{:S(2)}, u32[]{:S(2)}) collective-permute-start(bf16[4,16,1152]{2,1,0:T(8,128)(2,1)S(1)} %stack.3.refs_0_), channel_id=1, source_target_pairs={{0,6},{1,7},{2,4},{3,5},{4,2},{5,3},{6,0},{7,1},{8,14},{9,15},{10,... | collective-permute-start | bytes 442376 | tf_op jit(solution)/shard_map/ppermute | solution.py:22
  69.9 1.6 %collective-permute-done.29.refs_1_ = bf16[4,16,1152]{2,1,0:T(8,128)(2,1)S(1)} collective-permute-done((bf16[4,16,1152]{2,1,0:T(8,128)(2,1)S(1)}, bf16[4,16,1152]{2,1,0:T(8,128)(2,1)S(1)}, u32[]{:S(2)}, u32[]{:S(2)}) %collective-permute-start.29) | collective-permute-done | bytes 147488 | tf_op jit(solution)/shard_map/ppermute | solution.py:22
  71.5 2.2 %collective-permute-done.26.refs_1_ = bf16[4,16,1152]{2,1,0:T(8,128)(2,1)S(1)} collective-permute-done((bf16[4,16,1152]{2,1,0:T(8,128)(2,1)S(1)}, bf16[4,16,1152]{2,1,0:T(8,128)(2,1)S(1)}, u32[]{:S(2)}, u32[]{:S(2)}) %collective-permute-start.26) | collective-permute-done | bytes 147488 | tf_op jit(solution)/shard_map/ppermute | solution.py:22
  73.8 0.8 collective-permute-done.25.refs_0_
  74.6 2.0 %project.3.refs_4_ = f32[64,768]{1,0:T(8,128)S(1)} custom-call(bf16[4,16,1152]{2,1,0:T(8,128)(2,1)S(1)} %stack.3.refs_0_, bf16[4,16,1152]{2,1,0:T(8,128)(2,1)S(1)} %collective-permute-done.29.refs_1_, bf16[4,16,1152]{2,1,0:T(8,128)(2,1)S(1)} %collective-permute-done.30.refs_2_, bf16[4,16,1152]{2,1,0:T(8,128)(2,1)S(1)} %collective-permute-done.31.refs_3_, ...), custom_call_target="tpu_custom_call" | custom-call | flops 1610612736 | tf_op jit(solution)/shard_map/project/pallas_call | solution.py:50
  76.6 4.1 %grad.1 = (f32[4,32,1024]{2,1,0:T(8,128)S(1)}, bf16[4,32,1024]{2,1,0:T(8,128)(2,1)S(1)}, bf16[64,768]{1,0:T(8,128)(2,1)S(1)}, f32[1,1]{1,0:T(1,128)}) custom-call(bf16[4,16,1152]{2,1,0:T(8,128)(2,1)S(1)} %collective-permute-done.25.refs_0_, bf16[4,16,1152]{2,1,0:T(8,128)(2,1)S(1)} %collective-permute-done.26.refs_1_, ...), custom_call_target="tpu_custom_call" | custom-call | flops 1610612736 | tf_op jit(solution)/shard_map/grad/pallas_call | solution.py:50
  80.7 0.6 collective-permute-start.32
  81.3 1.2 %grad_rest.1 = (f32[4,32,1024]{2,1,0:T(8,128)S(1)}, bf16[4,32,1024]{2,1,0:T(8,128)(2,1)S(1)}) custom-call(bf16[64,768]{1,0:T(8,128)(2,1)S(1)} %get-tuple-element.75.left_ref, bf16[4,768,1024]{2,1,0:T(8,128)(2,1)S(1)} %get-tuple-element.49.refs_4_.held_ref), custom_call_target="tpu_custom_call" | custom-call | flops 1610612736 | tf_op jit(solution)/shard_map/grad_rest/pallas_call | solution.py:50
  82.9 2.3 %collective-permute-start.34 = (bf16[4,16,1024]{2,1,0:T(8,128)(2,1)S(1)}, bf16[4,16,1024]{2,1,0:T(8,128)(2,1)S(1)}, u32[]{:S(2)}, u32[]{:S(2)}) collective-permute-start(bf16[4,16,1024]{2,1,0:T(8,128)(2,1)S(1)} %get-tuple-element.82), channel_id=1, source_target_pairs={{0,6},{1,7},{2,4},{3,5},{4,2},{5,3},{6,0},{7,1},{8,14},{9,15},{10,... | collective-permute-start | bytes 393224 | tf_op jit(solution)/shard_map/ppermute | solution.py:22
  85.8 0.7 collective-permute-start.36
  86.5 3.6 %collective-permute-done.34.refs_1_ = bf16[4,16,1024]{2,1,0:T(8,128)(2,1)S(1)} collective-permute-done((bf16[4,16,1024]{2,1,0:T(8,128)(2,1)S(1)}, bf16[4,16,1024]{2,1,0:T(8,128)(2,1)S(1)}, u32[]{:S(2)}, u32[]{:S(2)}) %collective-permute-start.34) | collective-permute-done | bytes 131104 | tf_op jit(solution)/shard_map/ppermute | solution.py:22
  90.1 2.0 %collective-permute-done.35.refs_2_ = bf16[4,16,1024]{2,1,0:T(8,128)(2,1)S(1)} collective-permute-done((bf16[4,16,1024]{2,1,0:T(8,128)(2,1)S(1)}, bf16[4,16,1024]{2,1,0:T(8,128)(2,1)S(1)}, u32[]{:S(2)}, u32[]{:S(2)}) %collective-permute-start.35) | collective-permute-done | bytes 131104 | tf_op jit(solution)/shard_map/ppermute | solution.py:22
  92.3 2.2 %collective-permute-start.37 = (bf16[1,16,1024]{2,1,0:T(8,128)(2,1)S(1)}, bf16[1,16,1024]{2,1,0:T(8,128)(2,1)S(1)}, u32[]{:S(2)}, u32[]{:S(2)}) collective-permute-start(bf16[1,16,1024]{2,1,0:T(8,128)(2,1)S(1)} %get-tuple-element.86), channel_id=1, source_target_pairs={{0,24},{1,25},{2,26},{3,27},{4,28},{5,29},{6,30},{7,31},{8,16},{9,... | collective-permute-start | bytes 98312 | tf_op jit(solution)/shard_map/ppermute | solution.py:22
  94.5 0.6 collective-permute-start.38
  95.1 1.7 %collective-permute-start.39 = (bf16[1,16,1024]{2,1,0:T(8,128)(2,1)S(1)}, bf16[1,16,1024]{2,1,0:T(8,128)(2,1)S(1)}, u32[]{:S(2)}, u32[]{:S(2)}) collective-permute-start(bf16[1,16,1024]{2,1,0:T(8,128)(2,1)S(1)} %get-tuple-element.88), channel_id=1, source_target_pairs={{0,8},{1,9},{2,10},{3,11},{4,12},{5,13},{6,14},{7,15},{8,0},{9,1},... | collective-permute-start | bytes 98312 | tf_op jit(solution)/shard_map/ppermute | solution.py:22
  96.7 3.0 %head_weight_grad.1 = f32[1024,1024]{1,0:T(8,128)} custom-call(f32[16,1024]{1,0:T(8,128)S(1)} %get-tuple-element.89.normed_ref, f32[1,1024]{1,0:T(1,128)S(1)} %get-tuple-element.90.bias_grad_ref), custom_call_target="tpu_custom_call" | custom-call | tf_op jit(solution)/shard_map/head_weight_grad/pallas_call | solution.py:369
  99.7 0.6 far_sum.1
  (58 shorter events, 6.9 us)
Async XLA Ops:
  0.6 10.5 %collective-permute-start = (bf16[16,1024]{1,0:T(8,128)(2,1)}, bf16[16,1024]{1,0:T(8,128)(2,1)S(1)}, u32[]{:S(2)}, u32[]{:S(2)}) collective-permute-start(bf16[16,1024]{1,0:T(8,128)(2,1)} %refs_0_.1), channel_id=1, source_target_pairs={{0,8},{1,9},{2,10},{3,11},{4,12},{5,13},{6,14},{7,15},{8,0},{9,1},... | collective-permute-start | bytes 98312 | tf_op jit(solution)/shard_map/ppermute | solution.py:22
  3.7 7.4 %collective-permute-start.2 = (bf16[16,1024]{1,0:T(8,128)(2,1)}, bf16[16,1024]{1,0:T(8,128)(2,1)S(1)}, u32[]{:S(2)}, u32[]{:S(2)}) collective-permute-start(bf16[16,1024]{1,0:T(8,128)(2,1)} %refs_0_.1), channel_id=1, source_target_pairs={{0,24},{1,25},{2,26},{3,27},{4,28},{5,29},{6,30},{7,31},{8,16},{9,... | collective-permute-start | bytes 98312 | tf_op jit(solution)/shard_map/ppermute | solution.py:22
  6.2 5.4 %collective-permute-start.1 = (bf16[16,1024]{1,0:T(8,128)(2,1)}, bf16[16,1024]{1,0:T(8,128)(2,1)S(1)}, u32[]{:S(2)}, u32[]{:S(2)}) collective-permute-start(bf16[16,1024]{1,0:T(8,128)(2,1)} %refs_0_.1), channel_id=1, source_target_pairs={{0,16},{1,17},{2,18},{3,19},{4,20},{5,21},{6,22},{7,23},{8,24},{9,... | collective-permute-start | bytes 98312 | tf_op jit(solution)/shard_map/ppermute | solution.py:22
  11.6 6.8 %collective-permute-start.7 = (bf16[4,16,1024]{2,1,0:T(8,128)(2,1)S(1)}, bf16[4,16,1024]{2,1,0:T(8,128)(2,1)S(1)}, u32[]{:S(2)}, u32[]{:S(2)}) collective-permute-start(bf16[4,16,1024]{2,1,0:T(8,128)(2,1)S(1)} %stack.2.refs_0_), channel_id=1, source_target_pairs={{0,2},{1,3},{2,0},{3,1},{4,6},{5,7},{6,4},{7,5},{8,10},{9,11},{10,... | collective-permute-start | bytes 393224 | tf_op jit(solution)/shard_map/ppermute | solution.py:22
  13.2 6.3 %collective-permute-start.4 = (bf16[4,16,1024]{2,1,0:T(8,128)(2,1)S(1)}, bf16[4,16,1024]{2,1,0:T(8,128)(2,1)S(1)}, u32[]{:S(2)}, u32[]{:S(2)}) collective-permute-start(bf16[4,16,1024]{2,1,0:T(8,128)(2,1)S(1)} %stack.2.refs_0_), channel_id=1, source_target_pairs={{0,6},{1,7},{2,4},{3,5},{4,2},{5,3},{6,0},{7,1},{8,14},{9,15},{10,... | collective-permute-start | bytes 393224 | tf_op jit(solution)/shard_map/ppermute | solution.py:22
  14.6 5.4 %collective-permute-start.3 = (bf16[4,16,1024]{2,1,0:T(8,128)(2,1)S(1)}, bf16[4,16,1024]{2,1,0:T(8,128)(2,1)S(1)}, u32[]{:S(2)}, u32[]{:S(2)}) collective-permute-start(bf16[4,16,1024]{2,1,0:T(8,128)(2,1)S(1)} %stack.2.refs_0_), channel_id=1, source_target_pairs={{0,4},{1,5},{2,6},{3,7},{4,0},{5,1},{6,2},{7,3},{8,12},{9,13},{10,... | collective-permute-start | bytes 393224 | tf_op jit(solution)/shard_map/ppermute | solution.py:22
  15.1 4.9 %collective-permute-start.8 = (bf16[4,16,1024]{2,1,0:T(8,128)(2,1)S(1)}, bf16[4,16,1024]{2,1,0:T(8,128)(2,1)S(1)}, u32[]{:S(2)}, u32[]{:S(2)}) collective-permute-start(bf16[4,16,1024]{2,1,0:T(8,128)(2,1)S(1)} %stack.2.refs_0_), channel_id=1, source_target_pairs={{0,1},{1,0},{2,3},{3,2},{4,5},{5,4},{6,7},{7,6},{8,9},{9,8},{10,11... | collective-permute-start | bytes 393224 | tf_op jit(solution)/shard_map/ppermute | solution.py:22
  18.3 1.7 %collective-permute-start.9 = (bf16[4,16,1024]{2,1,0:T(8,128)(2,1)S(1)}, bf16[4,16,1024]{2,1,0:T(8,128)(2,1)S(1)}, u32[]{:S(2)}, u32[]{:S(2)}) collective-permute-start(bf16[4,16,1024]{2,1,0:T(8,128)(2,1)S(1)} %collective-permute-done.7.refs_1_), channel_id=1, source_target_pairs={{0,1},{1,0},{2,3},{3,2},{4,5},{5,4},{6,7},{7,6},{8,9},{9,8},{10,11... | collective-permute-start | bytes 393224 | tf_op jit(solution)/shard_map/ppermute | solution.py:22
  19.5 2.5 %collective-permute-start.6 = (bf16[4,16,1024]{2,1,0:T(8,128)(2,1)S(1)}, bf16[4,16,1024]{2,1,0:T(8,128)(2,1)S(1)}, u32[]{:S(2)}, u32[]{:S(2)}) collective-permute-start(bf16[4,16,1024]{2,1,0:T(8,128)(2,1)S(1)} %collective-permute-done.4.refs_1_), channel_id=1, source_target_pairs={{0,1},{1,0},{2,3},{3,2},{4,5},{5,4},{6,7},{7,6},{8,9},{9,8},{10,11... | collective-permute-start | bytes 393224 | tf_op jit(solution)/shard_map/ppermute | solution.py:22
  20.0 2.1 %collective-permute-start.5 = (bf16[4,16,1024]{2,1,0:T(8,128)(2,1)S(1)}, bf16[4,16,1024]{2,1,0:T(8,128)(2,1)S(1)}, u32[]{:S(2)}, u32[]{:S(2)}) collective-permute-start(bf16[4,16,1024]{2,1,0:T(8,128)(2,1)S(1)} %collective-permute-done.3.refs_0_), channel_id=1, source_target_pairs={{0,1},{1,0},{2,3},{3,2},{4,5},{5,4},{6,7},{7,6},{8,9},{9,8},{10,11... | collective-permute-start | bytes 393224 | tf_op jit(solution)/shard_map/ppermute | solution.py:22
  26.1 20.7 %copy-start = (bf16[1024,1024]{1,0:T(8,128)(2,1)S(1)}, bf16[1024,1024]{1,0:T(8,128)(2,1)}, u32[]{:S(2)}) copy-start(bf16[1024,1024]{1,0:T(8,128)(2,1)} %refs_3_.1) | copy-start | bytes 6291460
  26.1 31.5 %copy-start.1 = (f32[1024]{0:T(1024)S(1)}, f32[1024]{0:T(1024)}, u32[]{:S(2)}) copy-start(f32[1024]{0:T(1024)} %param.12) | copy-start | bytes 12292
  26.2 31.5 %copy-start.2 = (s32[1024]{0:T(1024)S(1)}, s32[1024]{0:T(1024)}, u32[]{:S(2)}) copy-start(s32[1024]{0:T(1024)} %param.13) | copy-start | bytes 12292
  26.2 1.8 %collective-permute-start.10 = (bf16[4,32,1152]{2,1,0:T(8,128)(2,1)S(1)}, bf16[4,32,1152]{2,1,0:T(8,128)(2,1)S(1)}, u32[]{:S(2)}, u32[]{:S(2)}) collective-permute-start(bf16[4,32,1152]{2,1,0:T(8,128)(2,1)S(1)} %get-tuple-element.55), channel_id=1, source_target_pairs={{0,1},{1,0},{2,3},{3,2},{4,5},{5,4},{6,7},{7,6},{8,9},{9,8},{10,11... | collective-permute-start | bytes 884744 | tf_op jit(solution)/shard_map/ppermute | solution.py:22
  28.3 3.4 %collective-permute-start.11 = (bf16[4,32,1152]{2,1,0:T(8,128)(2,1)S(1)}, bf16[4,32,1152]{2,1,0:T(8,128)(2,1)S(1)}, u32[]{:S(2)}, u32[]{:S(2)}) collective-permute-start(bf16[4,32,1152]{2,1,0:T(8,128)(2,1)S(1)} %get-tuple-element.57), channel_id=1, source_target_pairs={{0,1},{1,0},{2,3},{3,2},{4,5},{5,4},{6,7},{7,6},{8,9},{9,8},{10,11... | collective-permute-start | bytes 884744 | tf_op jit(solution)/shard_map/ppermute | solution.py:22
  28.7 7.6 %collective-permute-start.12 = (bf16[4,16,1152]{2,1,0:T(8,128)(2,1)S(1)}, bf16[4,16,1152]{2,1,0:T(8,128)(2,1)S(1)}, u32[]{:S(2)}, u32[]{:S(2)}) collective-permute-start(bf16[4,16,1152]{2,1,0:T(8,128)(2,1)S(1)} %get-tuple-element.59), channel_id=1, source_target_pairs={{0,6},{1,7},{2,4},{3,5},{4,2},{5,3},{6,0},{7,1},{8,14},{9,15},{10,... | collective-permute-start | bytes 442376 | tf_op jit(solution)/shard_map/ppermute | solution.py:22
  31.1 7.6 %collective-permute-start.13 = (bf16[4,16,1152]{2,1,0:T(8,128)(2,1)S(1)}, bf16[4,16,1152]{2,1,0:T(8,128)(2,1)S(1)}, u32[]{:S(2)}, u32[]{:S(2)}) collective-permute-start(bf16[4,16,1152]{2,1,0:T(8,128)(2,1)S(1)} %get-tuple-element.60), channel_id=1, source_target_pairs={{0,4},{1,5},{2,6},{3,7},{4,0},{5,1},{6,2},{7,3},{8,12},{9,13},{10,... | collective-permute-start | bytes 442376 | tf_op jit(solution)/shard_map/ppermute | solution.py:22
  32.0 6.7 %collective-permute-start.14 = (bf16[4,16,1152]{2,1,0:T(8,128)(2,1)S(1)}, bf16[4,16,1152]{2,1,0:T(8,128)(2,1)S(1)}, u32[]{:S(2)}, u32[]{:S(2)}) collective-permute-start(bf16[4,16,1152]{2,1,0:T(8,128)(2,1)S(1)} %get-tuple-element.61), channel_id=1, source_target_pairs={{0,2},{1,3},{2,0},{3,1},{4,6},{5,7},{6,4},{7,5},{8,10},{9,11},{10,... | collective-permute-start | bytes 442376 | tf_op jit(solution)/shard_map/ppermute | solution.py:22
  39.0 6.2 %collective-permute-start.15 = (bf16[1,16,1152]{2,1,0:T(8,128)(2,1)S(1)}, bf16[1,16,1152]{2,1,0:T(8,128)(2,1)S(1)}, u32[]{:S(2)}, u32[]{:S(2)}) collective-permute-start(bf16[1,16,1152]{2,1,0:T(8,128)(2,1)S(1)} %get-tuple-element.64), channel_id=1, source_target_pairs={{0,24},{1,25},{2,26},{3,27},{4,28},{5,29},{6,30},{7,31},{8,16},{9,... | collective-permute-start | bytes 110600 | tf_op jit(solution)/shard_map/ppermute | solution.py:22
  41.7 5.1 %collective-permute-start.16 = (bf16[1,16,1152]{2,1,0:T(8,128)(2,1)S(1)}, bf16[1,16,1152]{2,1,0:T(8,128)(2,1)S(1)}, u32[]{:S(2)}, u32[]{:S(2)}) collective-permute-start(bf16[1,16,1152]{2,1,0:T(8,128)(2,1)S(1)} %get-tuple-element.65), channel_id=1, source_target_pairs={{0,16},{1,17},{2,18},{3,19},{4,20},{5,21},{6,22},{7,23},{8,24},{9,... | collective-permute-start | bytes 110600 | tf_op jit(solution)/shard_map/ppermute | solution.py:22
  42.1 4.8 %collective-permute-start.17 = (bf16[1,16,1152]{2,1,0:T(8,128)(2,1)S(1)}, bf16[1,16,1152]{2,1,0:T(8,128)(2,1)S(1)}, u32[]{:S(2)}, u32[]{:S(2)}) collective-permute-start(bf16[1,16,1152]{2,1,0:T(8,128)(2,1)S(1)} %get-tuple-element.66), channel_id=1, source_target_pairs={{0,8},{1,9},{2,10},{3,11},{4,12},{5,13},{6,14},{7,15},{8,0},{9,1},... | collective-permute-start | bytes 110600 | tf_op jit(solution)/shard_map/ppermute | solution.py:22
  47.5 5.5 %collective-permute-start.20 = (f32[2,1024]{1,0:T(2,128)S(1)}, f32[2,1024]{1,0:T(2,128)S(1)}, u32[]{:S(2)}, u32[]{:S(2)}) collective-permute-start(f32[2,1024]{1,0:T(2,128)S(1)} %get-tuple-element.69.refs_0_), channel_id=1, source_target_pairs={{0,24},{1,25},{2,26},{3,27},{4,28},{5,29},{6,30},{7,31},{8,16},{9,... | collective-permute-start | bytes 24584 | tf_op jit(solution)/shard_map/ppermute | solution.py:22
  49.4 4.5 %collective-permute-start.19 = (f32[2,1024]{1,0:T(2,128)S(1)}, f32[2,1024]{1,0:T(2,128)S(1)}, u32[]{:S(2)}, u32[]{:S(2)}) collective-permute-start(f32[2,1024]{1,0:T(2,128)S(1)} %get-tuple-element.69.refs_0_), channel_id=1, source_target_pairs={{0,16},{1,17},{2,18},{3,19},{4,20},{5,21},{6,22},{7,23},{8,24},{9,... | collective-permute-start | bytes 24584 | tf_op jit(solution)/shard_map/ppermute | solution.py:22
  49.6 4.4 %collective-permute-start.18 = (f32[2,1024]{1,0:T(2,128)S(1)}, f32[2,1024]{1,0:T(2,128)S(1)}, u32[]{:S(2)}, u32[]{:S(2)}) collective-permute-start(f32[2,1024]{1,0:T(2,128)S(1)} %get-tuple-element.69.refs_0_), channel_id=1, source_target_pairs={{0,8},{1,9},{2,10},{3,11},{4,12},{5,13},{6,14},{7,15},{8,0},{9,1},... | collective-permute-start | bytes 24584 | tf_op jit(solution)/shard_map/ppermute | solution.py:22
  54.0 3.7 %collective-permute-start.21 = (f32[2,1024]{1,0:T(2,128)S(1)}, f32[2,1024]{1,0:T(2,128)S(1)}, u32[]{:S(2)}, u32[]{:S(2)}) collective-permute-start(f32[2,1024]{1,0:T(2,128)S(1)} %tree_sum.1.sums_ref), channel_id=1, source_target_pairs={{0,4},{1,5},{2,6},{3,7},{4,0},{5,1},{6,2},{7,3},{8,12},{9,13},{10,... | collective-permute-start | bytes 24584 | tf_op jit(solution)/shard_map/ppermute | solution.py:22
  58.9 5.8 %collective-permute-start.24 = (bf16[16,1152]{1,0:T(8,128)(2,1)S(1)}, bf16[16,1152]{1,0:T(8,128)(2,1)S(1)}, u32[]{:S(2)}, u32[]{:S(2)}) collective-permute-start(bf16[16,1152]{1,0:T(8,128)(2,1)S(1)} %get-tuple-element.72.refs_0_), channel_id=1, source_target_pairs={{0,24},{1,25},{2,26},{3,27},{4,28},{5,29},{6,30},{7,31},{8,16},{9,... | collective-permute-start | bytes 110600 | tf_op jit(solution)/shard_map/ppermute | solution.py:22
  60.9 5.3 %collective-permute-start.23 = (bf16[16,1152]{1,0:T(8,128)(2,1)S(1)}, bf16[16,1152]{1,0:T(8,128)(2,1)S(1)}, u32[]{:S(2)}, u32[]{:S(2)}) collective-permute-start(bf16[16,1152]{1,0:T(8,128)(2,1)S(1)} %get-tuple-element.72.refs_0_), channel_id=1, source_target_pairs={{0,16},{1,17},{2,18},{3,19},{4,20},{5,21},{6,22},{7,23},{8,24},{9,... | collective-permute-start | bytes 110600 | tf_op jit(solution)/shard_map/ppermute | solution.py:22
  61.9 4.3 %collective-permute-start.22 = (bf16[16,1152]{1,0:T(8,128)(2,1)S(1)}, bf16[16,1152]{1,0:T(8,128)(2,1)S(1)}, u32[]{:S(2)}, u32[]{:S(2)}) collective-permute-start(bf16[16,1152]{1,0:T(8,128)(2,1)S(1)} %get-tuple-element.72.refs_0_), channel_id=1, source_target_pairs={{0,8},{1,9},{2,10},{3,11},{4,12},{5,13},{6,14},{7,15},{8,0},{9,1},... | collective-permute-start | bytes 110600 | tf_op jit(solution)/shard_map/ppermute | solution.py:22
  66.3 5.2 %collective-permute-start.29 = (bf16[4,16,1152]{2,1,0:T(8,128)(2,1)S(1)}, bf16[4,16,1152]{2,1,0:T(8,128)(2,1)S(1)}, u32[]{:S(2)}, u32[]{:S(2)}) collective-permute-start(bf16[4,16,1152]{2,1,0:T(8,128)(2,1)S(1)} %stack.3.refs_0_), channel_id=1, source_target_pairs={{0,2},{1,3},{2,0},{3,1},{4,6},{5,7},{6,4},{7,5},{8,10},{9,11},{10,... | collective-permute-start | bytes 442376 | tf_op jit(solution)/shard_map/ppermute | solution.py:22
  67.7 6.0 %collective-permute-start.26 = (bf16[4,16,1152]{2,1,0:T(8,128)(2,1)S(1)}, bf16[4,16,1152]{2,1,0:T(8,128)(2,1)S(1)}, u32[]{:S(2)}, u32[]{:S(2)}) collective-permute-start(bf16[4,16,1152]{2,1,0:T(8,128)(2,1)S(1)} %stack.3.refs_0_), channel_id=1, source_target_pairs={{0,6},{1,7},{2,4},{3,5},{4,2},{5,3},{6,0},{7,1},{8,14},{9,15},{10,... | collective-permute-start | bytes 442376 | tf_op jit(solution)/shard_map/ppermute | solution.py:22
  69.3 5.2 %collective-permute-start.25 = (bf16[4,16,1152]{2,1,0:T(8,128)(2,1)S(1)}, bf16[4,16,1152]{2,1,0:T(8,128)(2,1)S(1)}, u32[]{:S(2)}, u32[]{:S(2)}) collective-permute-start(bf16[4,16,1152]{2,1,0:T(8,128)(2,1)S(1)} %stack.3.refs_0_), channel_id=1, source_target_pairs={{0,4},{1,5},{2,6},{3,7},{4,0},{5,1},{6,2},{7,3},{8,12},{9,13},{10,... | collective-permute-start | bytes 442376 | tf_op jit(solution)/shard_map/ppermute | solution.py:22
  69.9 4.7 %collective-permute-start.30 = (bf16[4,16,1152]{2,1,0:T(8,128)(2,1)S(1)}, bf16[4,16,1152]{2,1,0:T(8,128)(2,1)S(1)}, u32[]{:S(2)}, u32[]{:S(2)}) collective-permute-start(bf16[4,16,1152]{2,1,0:T(8,128)(2,1)S(1)} %stack.3.refs_0_), channel_id=1, source_target_pairs={{0,1},{1,0},{2,3},{3,2},{4,5},{5,4},{6,7},{7,6},{8,9},{9,8},{10,11... | collective-permute-start | bytes 442376 | tf_op jit(solution)/shard_map/ppermute | solution.py:22
  71.5 3.1 %collective-permute-start.31 = (bf16[4,16,1152]{2,1,0:T(8,128)(2,1)S(1)}, bf16[4,16,1152]{2,1,0:T(8,128)(2,1)S(1)}, u32[]{:S(2)}, u32[]{:S(2)}) collective-permute-start(bf16[4,16,1152]{2,1,0:T(8,128)(2,1)S(1)} %collective-permute-done.29.refs_1_), channel_id=1, source_target_pairs={{0,1},{1,0},{2,3},{3,2},{4,5},{5,4},{6,7},{7,6},{8,9},{9,8},{10,11... | collective-permute-start | bytes 442376 | tf_op jit(solution)/shard_map/ppermute | solution.py:22
  73.8 2.9 %collective-permute-start.28 = (bf16[4,16,1152]{2,1,0:T(8,128)(2,1)S(1)}, bf16[4,16,1152]{2,1,0:T(8,128)(2,1)S(1)}, u32[]{:S(2)}, u32[]{:S(2)}) collective-permute-start(bf16[4,16,1152]{2,1,0:T(8,128)(2,1)S(1)} %collective-permute-done.26.refs_1_), channel_id=1, source_target_pairs={{0,1},{1,0},{2,3},{3,2},{4,5},{5,4},{6,7},{7,6},{8,9},{9,8},{10,11... | collective-permute-start | bytes 442376 | tf_op jit(solution)/shard_map/ppermute | solution.py:22
  74.6 2.1 %collective-permute-start.27 = (bf16[4,16,1152]{2,1,0:T(8,128)(2,1)S(1)}, bf16[4,16,1152]{2,1,0:T(8,128)(2,1)S(1)}, u32[]{:S(2)}, u32[]{:S(2)}) collective-permute-start(bf16[4,16,1152]{2,1,0:T(8,128)(2,1)S(1)} %collective-permute-done.25.refs_0_), channel_id=1, source_target_pairs={{0,1},{1,0},{2,3},{3,2},{4,5},{5,4},{6,7},{7,6},{8,9},{9,8},{10,11... | collective-permute-start | bytes 442376 | tf_op jit(solution)/shard_map/ppermute | solution.py:22
  80.7 1.8 %collective-permute-start.32 = (bf16[4,32,1024]{2,1,0:T(8,128)(2,1)S(1)}, bf16[4,32,1024]{2,1,0:T(8,128)(2,1)S(1)}, u32[]{:S(2)}, u32[]{:S(2)}) collective-permute-start(bf16[4,32,1024]{2,1,0:T(8,128)(2,1)S(1)} %get-tuple-element.78), channel_id=1, source_target_pairs={{0,1},{1,0},{2,3},{3,2},{4,5},{5,4},{6,7},{7,6},{8,9},{9,8},{10,11... | collective-permute-start | bytes 786440 | tf_op jit(solution)/shard_map/ppermute | solution.py:22
  82.5 3.2 %collective-permute-start.33 = (bf16[4,32,1024]{2,1,0:T(8,128)(2,1)S(1)}, bf16[4,32,1024]{2,1,0:T(8,128)(2,1)S(1)}, u32[]{:S(2)}, u32[]{:S(2)}) collective-permute-start(bf16[4,32,1024]{2,1,0:T(8,128)(2,1)S(1)} %get-tuple-element.80), channel_id=1, source_target_pairs={{0,1},{1,0},{2,3},{3,2},{4,5},{5,4},{6,7},{7,6},{8,9},{9,8},{10,11... | collective-permute-start | bytes 786440 | tf_op jit(solution)/shard_map/ppermute | solution.py:22
  82.9 7.2 %collective-permute-start.34 = (bf16[4,16,1024]{2,1,0:T(8,128)(2,1)S(1)}, bf16[4,16,1024]{2,1,0:T(8,128)(2,1)S(1)}, u32[]{:S(2)}, u32[]{:S(2)}) collective-permute-start(bf16[4,16,1024]{2,1,0:T(8,128)(2,1)S(1)} %get-tuple-element.82), channel_id=1, source_target_pairs={{0,6},{1,7},{2,4},{3,5},{4,2},{5,3},{6,0},{7,1},{8,14},{9,15},{10,... | collective-permute-start | bytes 393224 | tf_op jit(solution)/shard_map/ppermute | solution.py:22
  85.2 6.9 %collective-permute-start.35 = (bf16[4,16,1024]{2,1,0:T(8,128)(2,1)S(1)}, bf16[4,16,1024]{2,1,0:T(8,128)(2,1)S(1)}, u32[]{:S(2)}, u32[]{:S(2)}) collective-permute-start(bf16[4,16,1024]{2,1,0:T(8,128)(2,1)S(1)} %get-tuple-element.83), channel_id=1, source_target_pairs={{0,4},{1,5},{2,6},{3,7},{4,0},{5,1},{6,2},{7,3},{8,12},{9,13},{10,... | collective-permute-start | bytes 393224 | tf_op jit(solution)/shard_map/ppermute | solution.py:22
  85.8 6.5 %collective-permute-start.36 = (bf16[4,16,1024]{2,1,0:T(8,128)(2,1)S(1)}, bf16[4,16,1024]{2,1,0:T(8,128)(2,1)S(1)}, u32[]{:S(2)}, u32[]{:S(2)}) collective-permute-start(bf16[4,16,1024]{2,1,0:T(8,128)(2,1)S(1)} %get-tuple-element.84), channel_id=1, source_target_pairs={{0,2},{1,3},{2,0},{3,1},{4,6},{5,7},{6,4},{7,5},{8,10},{9,11},{10,... | collective-permute-start | bytes 393224 | tf_op jit(solution)/shard_map/ppermute | solution.py:22
  92.3 7.4 %collective-permute-start.37 = (bf16[1,16,1024]{2,1,0:T(8,128)(2,1)S(1)}, bf16[1,16,1024]{2,1,0:T(8,128)(2,1)S(1)}, u32[]{:S(2)}, u32[]{:S(2)}) collective-permute-start(bf16[1,16,1024]{2,1,0:T(8,128)(2,1)S(1)} %get-tuple-element.86), channel_id=1, source_target_pairs={{0,24},{1,25},{2,26},{3,27},{4,28},{5,29},{6,30},{7,31},{8,16},{9,... | collective-permute-start | bytes 98312 | tf_op jit(solution)/shard_map/ppermute | solution.py:22
  94.5 5.2 %collective-permute-start.38 = (bf16[1,16,1024]{2,1,0:T(8,128)(2,1)S(1)}, bf16[1,16,1024]{2,1,0:T(8,128)(2,1)S(1)}, u32[]{:S(2)}, u32[]{:S(2)}) collective-permute-start(bf16[1,16,1024]{2,1,0:T(8,128)(2,1)S(1)} %get-tuple-element.87), channel_id=1, source_target_pairs={{0,16},{1,17},{2,18},{3,19},{4,20},{5,21},{6,22},{7,23},{8,24},{9,... | collective-permute-start | bytes 98312 | tf_op jit(solution)/shard_map/ppermute | solution.py:22
  95.1 4.7 %collective-permute-start.39 = (bf16[1,16,1024]{2,1,0:T(8,128)(2,1)S(1)}, bf16[1,16,1024]{2,1,0:T(8,128)(2,1)S(1)}, u32[]{:S(2)}, u32[]{:S(2)}) collective-permute-start(bf16[1,16,1024]{2,1,0:T(8,128)(2,1)S(1)} %get-tuple-element.88), channel_id=1, source_target_pairs={{0,8},{1,9},{2,10},{3,11},{4,12},{5,13},{6,14},{7,15},{8,0},{9,1},... | collective-permute-start | bytes 98312 | tf_op jit(solution)/shard_map/ppermute | solution.py:22
